TPU v7x, 32 devices: a whole 2x2x4 slice. The times are simulated.
32 devices in a mesh: member: 2 (over y), fsdp: 4 (over z), tensor: 4 (over x, core).
Axes of the slice: x: 2, y: 2, z: 4, core: 2. Of those that a mesh axis runs over, the one named last changes fastest.
Arguments:
- tokens: bfloat16 [1024, 2560], P(('member', 'fsdp', 'tensor')), parts along dimension 0, may hold values from -6 to 6
- tile_weights: bfloat16 [768, 80, 128], P(('member', 'fsdp'), 'tensor'), parts along dimension 0, may hold values from -0.3125 to 0.3125
- cotangent: bfloat16 [1024, 10240], P(('member', 'fsdp', 'tensor')), parts along dimension 0, may hold values from -0.3125 to 0.3125
- tile_list: int32 [80, 3], P('tensor'), may hold values from 0 to 19, as said below
- tile_counts: int32 [80], P('tensor'), may hold values from 2 to 3
Outputs:
- activations: bfloat16 [1024, 10240], P(('member', 'fsdp', 'tensor')), parts along dimension 0
- tile_grads: float32 [768, 80, 128], P(('member', 'fsdp'), 'tensor'), parts along dimension 0
There are 2 independent parts, one for each index of `member`. A program takes and returns all parts, laid end to end along the dimension named above; an argument that names none is the same for every part. Nothing has to cross between parts.
Inputs may be any that keep to these rules, and one draw needn't show every extreme that they name: `tile_list`: each row holds 3 different tile rows.
All inputs are finite; a program needn't handle non-finite values.
Results may differ from a plain program's by a relative error of at most 0.0029.
Values may be sent and summed in bfloat16 or wider, within the bound.
No kernel may reach another device: no remote copies, remote signals or barrier semaphores. Data moves between devices by JAX's collectives and lax.ppermute only.
A program may use at most 64 MiB of HBM per device.

v0:
```python
import jax
import jax.numpy as jnp
from jax import lax
from jax.sharding import PartitionSpec as P

TILE = 128
SLOTS = 3


def gelu_tanh(value):
    return jax.nn.gelu(value, approximate=True)


def stack_inputs(gathered, tiles, counts):
    rows = gathered.shape[0]
    blocks = gathered.reshape(rows, gathered.shape[1] // TILE, TILE)
    chosen = jnp.take(blocks, tiles, axis=1)
    live = jnp.arange(SLOTS, dtype=jnp.int32)[None, :] < counts[:, None]
    picked = jnp.where(live[None, :, :, None], chosen, jnp.zeros((), chosen.dtype))
    return picked.reshape(rows, tiles.shape[0], SLOTS * TILE)


def body(tokens, tile_weights, cotangent, tile_list, tile_counts):
    gathered = lax.all_gather(tokens, "tensor", axis=0, tiled=True)
    group_rows = gathered.shape[0]
    stripes = tile_weights.shape[1]
    picked = stack_inputs(gathered, tile_list, tile_counts)
    stack = lax.all_gather(tile_weights, "fsdp", axis=0, tiled=True)
    pre = jnp.einsum("nsr,rsc->nsc", picked, stack, preferred_element_type=jnp.float32)
    act, backward = jax.vjp(gelu_tanh, pre)
    hidden = act.astype(jnp.bfloat16).reshape(group_rows, stripes * TILE)
    activations = lax.all_to_all(hidden, "tensor", split_axis=0, concat_axis=1, tiled=True)
    incoming = lax.all_to_all(cotangent, "tensor", split_axis=1, concat_axis=0, tiled=True)
    stack_again = lax.all_gather(tile_weights, "fsdp", axis=0, tiled=True)
    again = jnp.einsum("nsr,rsc->nsc", picked, stack_again, preferred_element_type=jnp.float32)
    unused, backward = jax.vjp(gelu_tanh, again)
    back_in = incoming.reshape(group_rows, stripes, TILE).astype(jnp.float32)
    slope = backward(back_in)[0].astype(jnp.bfloat16)
    term = jnp.einsum("nsr,nsc->rsc", picked, slope, preferred_element_type=jnp.float32)
    grads = lax.psum_scatter(term, "fsdp", scatter_dimension=0, tiled=True)
    return (activations, grads)


def solution(mesh):
    return jax.shard_map(
        body,
        mesh=mesh,
        in_specs=(
            P(("member", "fsdp", "tensor"), None),
            P(("member", "fsdp"), "tensor", None),
            P(("member", "fsdp", "tensor"), None),
            P("tensor", None),
            P("tensor"),
        ),
        out_specs=(P(("member", "fsdp", "tensor"), None), P(("member", "fsdp"), "tensor", None)),
        check_vma=False,
    )
```

profile of v0, /device:TPU:0, one launch (start us, length us, event | category | flops | bytes accessed | tf_op | source)
XLA Modules:
  0.0 160.9 jit_solution(6396229299867071771)
XLA Ops:
  7.2 0.0 all-gather.2.cloned.1.call-start
  7.2 0.7 all-gather.2.cloned.1.call-update
  7.9 2.0 %copy.64 = bf16[4,4,8,2560]{3,2,0,1:T(8,128)(2,1)} copy(bf16[4,4,8,2560]{3,2,1,0:T(8,128)(2,1)} %bitcast.33) | data formatting | bytes 1310720 | tf_op jit(solution)/shard_map/all_to_all | solution.py:33
  9.9 4.2 %all-to-all-start.1 = ((bf16[32,4,2560]{2,0,1:T(8,128)(2,1)}), bf16[32,4,2560]{2,0,1:T(8,128)(2,1)S(1)}, u32[]{:S(2)}, u32[]{:S(2)}) async-start(bf16[32,4,2560]{2,0,1:T(8,128)(2,1)} %bitcast.29), calls=%async_computation.1 | async-start | bytes 1310720 | tf_op jit(solution)/shard_map/all_to_all | solution.py:33
  14.1 0.1 iota_compare_fusion
  14.2 14.5 %all_gather.7 = bf16[128,2560]{1,0:T(8,128)(2,1)S(1)} all-gather(bf16[32,2560]{1,0:T(8,128)(2,1)S(1)} %copy-done.2), channel_id=1, replica_groups=mesh['member'=2,'fsdp'=4,'tensor'=4] {'tensor'}, dimensions={0}, use_global_device_ids=true | all-gather | bytes 819200 | tf_op jit(solution)/shard_map/all_gather | solution.py:24
  28.8 0.1 copy.39
  28.9 0.1 broadcast_in_dim.35
  29.0 0.1 broadcast_in_dim.38
  29.2 0.1 copy.41
  29.3 0.1 reshape.53
  29.4 0.3 copy.40
  29.7 0.3 copy.42
  30.0 0.9 gather_fusion
  31.0 2.3 %copy.43 = bf16[128,20,3,128]{0,3,2,1:T(8,128)(2,1)} copy(bf16[128,20,3,128]{3,0,2,1:T(8,128)(2,1)S(1)} %bitcast.30) | data formatting | bytes 3932160 | tf_op jit(solution)/shard_map/jit(_take)/gather | solution.py:17
  33.3 8.7 %fusion = bf16[128,20,384]{0,2,1:T(8,128)(2,1)} fusion(bf16[128,20,3,128]{0,3,2,1:T(8,128)(2,1)} %copy.43, pred[20,384]{1,0:T(8,128)(4,1)S(1)} %bitcast.38, pred[20,384]{1,0:T(8,128)(4,1)S(1)} %bitcast.37), kind=kLoop, calls=%fused_computation.3 | loop fusion | flops 1966080 | bytes 3947520 | tf_op jit(solution)/shard_map/jit(_where)/select_n | solution.py:19
  42.0 0.0 all-to-all-done.1
  42.0 0.1 convert_bitcast_fusion
  42.1 1.3 reshape.50
  43.5 12.4 %all-gather.2.cloned.1.call-done = bf16[384,20,128]{2,0,1:T(8,128)(2,1)} async-done(((bf16[96,20,128]{2,0,1:T(8,128)(2,1)}), bf16[384,20,128]{2,0,1:T(8,128)(2,1)}) %all-gather.2.cloned.1.call-update) | async-done | bytes 1966096 | tf_op jit(solution)/shard_map/all_gather | solution.py:28
  55.9 0.0 copy-done
  55.9 2.7 %multiply_convert_fusion = (bf16[128,20,128]{2,0,1:T(8,128)(2,1)S(1)}, f32[128,20,128]{2,0,1:T(8,128)S(1)}) fusion(bf16[128,20,384]{0,2,1:T(8,128)(2,1)S(1)} %copy-done, bf16[384,20,128]{2,0,1:T(8,128)(2,1)} %all-gather.2.cloned.1.call-done), kind=kOutput, calls=%fused_computation.15 | convolution fusion | flops 254607360 | bytes 5898240 | tf_op jit(solution)/shard_map/nsr,rsc->nsc/dot_general | solution.py:29
  58.5 0.0 copy-done.1
  58.5 3.2 %convolution_bitcast_fusion = f32[384,20,128]{0,2,1:T(8,128)} fusion(bf16[128,20,384]{0,2,1:T(8,128)(2,1)S(1)} %copy-done, f32[128,20,128]{2,0,1:T(8,128)S(1)} %get-tuple-element.11, f32[128,20,128]{2,1,0:T(8,128)S(1)} %copy-done.1), kind=kOutput, calls=%fused_computation.1 | convolution fusion | flops 258211840 | bytes 8519680 | tf_op jit(solution)/shard_map/nsr,nsc->rsc/dot_general | solution.py:39
  61.7 5.7 %copy.52 = f32[384,20,128]{2,1,0:T(8,128)} copy(f32[384,20,128]{0,2,1:T(8,128)} %convolution_bitcast_fusion) | data formatting | bytes 7864320 | tf_op jit(solution)/shard_map/nsr,nsc->rsc/transpose | solution.py:39
  67.4 0.0 reduce-scatter.2.cloned.1.call-update
  67.4 0.4 copy.45
  67.9 0.4 all_to_all.24
  68.3 12.8 %all_to_all.32 = bf16[4,32,2560]{2,1,0:T(8,128)(2,1)S(1)} all-to-all(bf16[4,32,2560]{2,1,0:T(8,128)(2,1)S(1)} %all_to_all.24), channel_id=1, replica_groups=mesh['member'=2,'fsdp'=4,'tensor'=4] {'tensor'}, dimensions={0} | all-to-all | bytes 1310720 | tf_op jit(solution)/shard_map/all_to_all | solution.py:32
  81.1 0.9 copy.58
  82.0 69.7 %reduce-scatter.2.cloned.1.call-done = f32[96,20,128]{2,1,0:T(8,128)} async-done(((f32[384,20,128]{2,1,0:T(8,128)}), f32[96,20,128]{2,1,0:T(8,128)}) %reduce-scatter.2.cloned.1.call-update) | async-done | bytes 983056 | tf_op jit(solution)/shard_map/reduce_scatter | solution.py:40
  151.7 2.4 %copy.53 = f32[96,20,128]{2,0,1:T(8,128)} copy(f32[96,20,128]{2,1,0:T(8,128)} %reduce-scatter.2.cloned.1.call-done) | data formatting | bytes 1966080
  (16 shorter events, 0.1 us)
Async XLA Ops:
  7.2 48.7 %all-gather.2.cloned.1.call-start = ((), (), s32[]{:S(2)}) async-start(), calls=%async_computation.3 | async-start | bytes 2457600 | tf_op jit(solution)/shard_map/all_gather | solution.py:28
  7.9 6.2 %copy-start.4 = (s32[20]{0:T(128)S(1)}, s32[20]{0:T(128)}, u32[]{:S(2)}) copy-start(s32[20]{0:T(128)} %param.9) | copy-start | bytes 244
  7.9 6.3 %copy-start.3 = (s32[20,3]{0,1:T(4,128)S(1)}, s32[20,3]{0,1:T(4,128)}, u32[]{:S(2)}) copy-start(s32[20,3]{0,1:T(4,128)} %param.8) | copy-start | bytes 724
  7.9 6.3 %copy-start.2 = (bf16[32,2560]{1,0:T(8,128)(2,1)S(1)}, bf16[32,2560]{1,0:T(8,128)(2,1)}, u32[]{:S(2)}) copy-start(bf16[32,2560]{1,0:T(8,128)(2,1)} %param.5) | copy-start | bytes 491524
  9.9 32.0 %all-to-all-start.1 = ((bf16[32,4,2560]{2,0,1:T(8,128)(2,1)}), bf16[32,4,2560]{2,0,1:T(8,128)(2,1)S(1)}, u32[]{:S(2)}, u32[]{:S(2)}) async-start(bf16[32,4,2560]{2,0,1:T(8,128)(2,1)} %bitcast.29), calls=%async_computation.1 | async-start | bytes 1310720 | tf_op jit(solution)/shard_map/all_to_all | solution.py:33
  14.1 137.6 %reduce-scatter.2.cloned.1.call-start = ((), (), s32[]{:S(2)}) async-start(), calls=%async_computation.4 | async-start | bytes 5898240 | tf_op jit(solution)/shard_map/reduce_scatter | solution.py:40
  42.1 13.8 %copy-start = (bf16[128,20,384]{0,2,1:T(8,128)(2,1)S(1)}, bf16[128,20,384]{0,2,1:T(8,128)(2,1)}, u32[]{:S(2)}) copy-start(bf16[128,20,384]{0,2,1:T(8,128)(2,1)} %fusion) | copy-start | bytes 5898244
  55.9 2.7 %copy-start.1 = (f32[128,20,128]{2,1,0:T(8,128)S(1)}, f32[128,20,128]{2,1,0:T(8,128)}, u32[]{:S(2)}) copy-start(f32[128,20,128]{2,1,0:T(8,128)} %reshape.50) | copy-start | bytes 3932164
Sparse Core Ops, SparseCore 0:
  9.6 46.2 all-gather.1
  67.6 84.0 reduce-scatter.1
where the time goes:
time: 161 us
  waiting for transfers between devices  82.8 us (51%)
  blocking collectives  27.3 us (17%)
  local copies, waits for them, and re-layouts  17.6 us (11%)
  between operations  14.2 us (9%)
  other arithmetic  8.89 us (6%)
  matrix products  5.82 us (4%)
  starting transfers between devices  4.25 us (3%)
    reduce_scatter x1, waiting for transfers between devices, body(): grads = lax.psum_scatter(term, 'fsdp', scatter_dimension=0, tiled=True)  69.7 us
    all_gather x1, blocking collectives, body(): gathered = lax.all_gather(tokens, 'tensor', axis=0, tiled=True)  14.5 us
    all_to_all x1, blocking collectives, body(): lax.all_to_all(hidden, 'tensor', split_axis=0, concat_axis=1, tiled=True)  12.8 us
    all_gather x1, waiting for transfers between devices, body(): stack = lax.all_gather(tile_weights, 'fsdp', axis=0, tiled=True)  12.4 us
    select_n x1, other arithmetic, stack_inputs(): jnp.where(live[None, :, :, None], chosen, jnp.zeros((), chosen.dtype))  8.68 us
    transpose x1, local copies, waits for them, and re-layouts, body(): jnp.einsum('nsr,nsc->rsc', picked, slope, preferred_element_type=jnp.floa...  5.72 us
    all_to_all x1, starting transfers between devices, body(): lax.all_to_all(cotangent, 'tensor', split_axis=1, concat_axis=0, tiled=True)  4.21 us
    gather x2, local copies, waits for them, and re-layouts, stack_inputs(): chosen = jnp.take(blocks, tiles, axis=1)  3.24 us
  transfers between devices with their start and end apart: 3, of which 2 were waited for; matrix products, arithmetic and copies ran while one was open for 11% of the time, Pallas kernels for 0%

commit v1 on v0

v1 whole, which is shorter than its diff:
```python
import functools

import jax
import jax.numpy as jnp
from jax import lax
from jax.experimental import pallas as pl
from jax.experimental.pallas import tpu as pltpu
from jax.sharding import PartitionSpec as P

TILE = 128
SLOTS = 3
PAIR = 2
ROOT = 0.7978845608028654
CUBIC = 0.044715


def gelu_and_derivative(v):
    square = v * v
    th = jnp.tanh(ROOT * (v + CUBIC * (square * v)))
    half = 0.5 * (1.0 + th)
    inner = ROOT * (1.0 + (3.0 * CUBIC) * square)
    return v * half, half + 0.5 * v * (1.0 - th * th) * inner


def stripe_kernel(tiles, counts, order, own, tokens, weights, cotangent, hidden, grads, mine):
    s = pl.program_id(0)
    blocks, rows = cotangent.shape[0], cotangent.shape[1]
    shards, shard_rows = weights.shape[0], weights.shape[2]
    picked = []
    for k in range(SLOTS):
        column = pl.multiple_of(tiles[s, k] * TILE, TILE)
        block = tokens[:, pl.ds(column, TILE)]
        picked.append(jnp.where(k < counts[s], block, jnp.zeros_like(block)))
    picked = jnp.concatenate(picked, axis=1)
    stack = jnp.concatenate([weights[f, 0] for f in range(shards)], axis=0)
    pre = jnp.dot(picked, stack, preferred_element_type=jnp.float32)
    act, slope = gelu_and_derivative(pre)
    back = jnp.concatenate([cotangent[order[b]] for b in range(blocks)], axis=0)
    slope = (back.astype(jnp.float32) * slope).astype(jnp.bfloat16)
    act = act.astype(jnp.bfloat16)
    for b in range(blocks):
        hidden[order[b]] = act[b * rows:(b + 1) * rows]
    term = lax.dot_general(picked, slope, (((0,), (0,)), ((), ())), preferred_element_type=jnp.float32)
    for f in range(shards):
        piece = term[f * shard_rows:(f + 1) * shard_rows]
        grads[f, 0] = piece.astype(jnp.bfloat16)

        @pl.when(own[0] == f)
        def _():
            mine[0] = piece


def stripe_call(tiles, counts, order, own, tokens, weights, cotangent):
    shards, stripes, shard_rows, _ = weights.shape
    blocks, rows, width = cotangent.shape
    return pl.pallas_call(
        stripe_kernel,
        out_shape=(
            jax.ShapeDtypeStruct(cotangent.shape, jnp.bfloat16),
            jax.ShapeDtypeStruct(weights.shape, jnp.bfloat16),
            jax.ShapeDtypeStruct(weights.shape[1:], jnp.float32),
        ),
        grid_spec=pltpu.PrefetchScalarGridSpec(
            num_scalar_prefetch=4,
            grid=(stripes,),
            in_specs=[
                pl.BlockSpec(tokens.shape, lambda s, *_: (0, 0)),
                pl.BlockSpec((shards, 1, shard_rows, TILE), lambda s, *_: (0, s, 0, 0)),
                pl.BlockSpec((blocks, rows, TILE), lambda s, *_: (0, 0, s)),
            ],
            out_specs=[
                pl.BlockSpec((blocks, rows, TILE), lambda s, *_: (0, 0, s)),
                pl.BlockSpec((shards, 1, shard_rows, TILE), lambda s, *_: (0, s, 0, 0)),
                pl.BlockSpec((1, shard_rows, TILE), lambda s, *_: (s, 0, 0)),
            ],
        ),
        compiler_params=pltpu.CompilerParams(vmem_limit_bytes=32 * 2**20),
        name="stripes",
    )(tiles, counts, order, own, tokens, weights, cotangent)


def body(fsdp, tensor, tokens, tile_weights, cotangent, tile_list, tile_counts):
    z, t = lax.axis_index("fsdp"), lax.axis_index("tensor")
    half = z % PAIR
    rows = tokens.shape[0]
    shard_rows, stripes = tile_weights.shape[0], tile_weights.shape[1]
    share = stripes // PAIR
    width = share * TILE
    blocks = PAIR * tensor
    groups = [[(p * PAIR + a) * tensor + b for a in range(PAIR) for b in range(tensor)] for p in range(fsdp // PAIR)]

    def swap(value, dz, dt):
        pairs = [(a * tensor + b, (a ^ dz) * tensor + (b ^ dt)) for a in range(fsdp) for b in range(tensor)]
        return lax.ppermute(value, ("fsdp", "tensor"), pairs)

    steps = [(0, 0), (1, 0)]
    gathered = jnp.concatenate([tokens, swap(tokens, 1, 0)], axis=0)
    bit = tensor // 2
    while bit:
        steps = steps + [(a, b ^ bit) for a, b in steps]
        gathered = jnp.concatenate([gathered, swap(gathered, 0, bit)], axis=0)
        bit //= 2
    order = jnp.stack([(half ^ a) * tensor + (t ^ b) for a, b in steps]).astype(jnp.int32)

    by_stripe = jnp.transpose(tile_weights, (1, 0, 2)).reshape(PAIR, share, shard_rows, TILE)
    outgoing = jnp.tile(by_stripe, (fsdp // PAIR, 1, 1, 1))
    weights = lax.all_to_all(outgoing, "fsdp", split_axis=0, concat_axis=0, tiled=True)

    away = cotangent.reshape(rows, tensor, PAIR, width).transpose(2, 1, 0, 3).reshape(blocks, rows, width)
    incoming = lax.all_to_all(away, ("fsdp", "tensor"), split_axis=0, concat_axis=0, axis_index_groups=groups, tiled=True)

    tiles = lax.dynamic_slice_in_dim(tile_list, half * share, share, 0)
    counts = lax.dynamic_slice_in_dim(tile_counts, half * share, share, 0)
    hidden, grads, mine = stripe_call(tiles, counts, order, z.reshape(1).astype(jnp.int32), gathered, weights, incoming)

    grads = lax.all_to_all(grads, "fsdp", split_axis=0, concat_axis=0, tiled=True)
    hidden = lax.all_to_all(hidden, ("fsdp", "tensor"), split_axis=0, concat_axis=0, axis_index_groups=groups, tiled=True)
    activations = hidden.reshape(PAIR, tensor, rows, width).transpose(2, 1, 0, 3).reshape(rows, cotangent.shape[1])

    here = (jnp.arange(fsdp) == z)[:, None, None, None]
    total = jnp.where(here, mine[None], grads.astype(jnp.float32))
    total = jnp.sum(total.reshape(fsdp // PAIR, PAIR, share, shard_rows, TILE), axis=0)
    return activations, total.reshape(stripes, shard_rows, TILE).transpose(1, 0, 2)


def solution(mesh):
    return jax.shard_map(
        functools.partial(body, mesh.shape["fsdp"], mesh.shape["tensor"]),
        mesh=mesh,
        in_specs=(
            P(("member", "fsdp", "tensor"), None),
            P(("member", "fsdp"), "tensor", None),
            P(("member", "fsdp", "tensor"), None),
            P("tensor", None),
            P("tensor"),
        ),
        out_specs=(P(("member", "fsdp", "tensor"), None), P(("member", "fsdp"), "tensor", None)),
        check_vma=False,
    )
```

time: 161 us -> 105 us (0.65)
  waiting for transfers between devices: 82.8 us -> 55.9 us
  blocking collectives: 27.3 us -> 13.3 us
  between operations: 14.2 us -> 0.77 us
  starting transfers between devices: 4.25 us -> 16.4 us
  local copies, waits for them, and re-layouts: 17.6 us -> 6.31 us
  Pallas kernels: 0 us -> 5.92 us
  matrix products: 5.82 us -> 0 us
  other arithmetic: 8.89 us -> 5.67 us
    reduce_scatter x1 -> x0, waiting for transfers between devices: 69.7 us -> none  [body(): grads = lax.psum_scatter(term, 'fsdp', scatter_dimension=0, tiled=True)]
    all_to_all x1 -> x3, waiting for transfers between devices: 0.01 us -> 39.9 us  [the longest x1 22.3 us: body(): lax.all_to_all(grads, 'fsdp', split_axis=0, concat_axis=0, tiled=True)]
    ppermute x0 -> x3, waiting for transfers between devices: none -> 16 us  [swap(): return lax.ppermute(value, ('fsdp', 'tensor'), pairs)]
    all_gather x1 -> x0, blocking collectives: 14.5 us -> none  [body(): gathered = lax.all_gather(tokens, 'tensor', axis=0, tiled=True)]
    all_gather x1 -> x0, waiting for transfers between devices: 12.4 us -> none  [body(): stack = lax.all_gather(tile_weights, 'fsdp', axis=0, tiled=True)]
    all_to_all x1 -> x3, starting transfers between devices: 4.21 us -> 12.7 us  [the longest x1 5.23 us: body(): lax.all_to_all(away, ('fsdp', 'tensor'), split_axis=0, concat_axis=0, axi...]
    select_n x2 -> x1, other arithmetic: 8.68 us -> 1.62 us  [body(): total = jnp.where(here, mine[None], grads.astype(jnp.float32))]
    pallas_call x0 -> x1, Pallas kernels: none -> 5.92 us  [stripe_call(): pl.pallas_call(stripe_kernel, out_shape=(jax.ShapeDtypeStruct(cotangent.s...]
  transfers between devices with their start and end apart: 3 -> 6, of which waited for: 2 -> 5; matrix products, arithmetic and copies ran while one was open for 11% -> 5% of each run, Pallas kernels for 0% -> 0%
where the time goes in v1:
time: 105 us; the launch traced here: 104 us
  waiting for transfers between devices  55.9 us (53%)
  starting transfers between devices  16.4 us (16%)
  blocking collectives  13.3 us (13%)
  local copies, waits for them, and re-layouts  6.31 us (6%)
  Pallas kernels  5.92 us (6%)
  other arithmetic  5.67 us (5%)
    all_to_all x1, waiting for transfers between devices, body(): lax.all_to_all(grads, 'fsdp', split_axis=0, concat_axis=0, tiled=True)  22.3 us
    all_to_all x1, waiting for transfers between devices, body(): lax.all_to_all(outgoing, 'fsdp', split_axis=0, concat_axis=0, tiled=True)  17.5 us
    ppermute x3, waiting for transfers between devices, swap(): return lax.ppermute(value, ('fsdp', 'tensor'), pairs)  16 us
    all_to_all x1, blocking collectives, body(): lax.all_to_all(hidden, ('fsdp', 'tensor'), split_axis=0, concat_axis=0, a...  13.3 us
    pallas_call x1, Pallas kernels, stripe_call(): pl.pallas_call(stripe_kernel, out_shape=(jax.ShapeDtypeStruct(cotangent.s...  5.92 us
    all_to_all x1, starting transfers between devices, body(): lax.all_to_all(away, ('fsdp', 'tensor'), split_axis=0, concat_axis=0, axi...  5.23 us
    all_to_all x1, starting transfers between devices, body(): lax.all_to_all(outgoing, 'fsdp', split_axis=0, concat_axis=0, tiled=True)  3.99 us
    ppermute x3, starting transfers between devices, swap(): return lax.ppermute(value, ('fsdp', 'tensor'), pairs)  3.62 us
  transfers between devices with their start and end apart: 6, of which 5 were waited for; matrix products, arithmetic and copies ran while one was open for 5% of the time, Pallas kernels for 0%

profile of v1, /device:TPU:0, one launch (start us, length us, event | category | flops | bytes accessed | tf_op | source)
XLA Modules:
  0.0 104.2 jit_solution(9288406761436413819)
XLA Ops:
  0.6 0.0 copy-start
  0.6 0.0 copy-start.2
  0.7 1.6 %reshape.35 = bf16[32,4,2,1280]{3,2,1,0:T(2,128)(2,1)S(1)} reshape(bf16[32,10240]{1,0:T(8,128)(2,1)} %param.7) | data formatting | bytes 1310720 | tf_op jit(solution)/shard_map/reshape | solution.py:109
  2.3 0.0 copy-start.4
  2.3 0.9 copy.8
  3.2 5.2 %all-to-all-start.1 = ((bf16[8,32,1280]{2,1,0:T(8,128)(2,1)}), bf16[8,32,1280]{2,1,0:T(8,128)(2,1)S(1)}, u32[]{:S(2)}, u32[]{:S(2)}) async-start(bf16[8,32,1280]{2,1,0:T(8,128)(2,1)} %bitcast.13), calls=%async_computation.1 | async-start | bytes 1310720 | tf_op jit(solution)/shard_map/all_to_all | solution.py:110
  8.4 0.0 copy-done.2
  8.4 2.0 %collective-permute-start = (bf16[32,2560]{1,0:T(8,128)(2,1)S(1)}, bf16[32,2560]{1,0:T(8,128)(2,1)S(1)}, u32[]{:S(2)}, u32[]{:S(2)}) collective-permute-start(bf16[32,2560]{1,0:T(8,128)(2,1)S(1)} %copy-done.2), channel_id=1, source_target_pairs={{0,4},{1,5},{2,6},{3,7},{4,0},{5,1},{6,2},{7,3},{8,12},{9,13},{10,... | collective-permute-start | bytes 491528 | tf_op jit(solution)/shard_map/ppermute | solution.py:94
  10.5 11.7 %collective-permute-done = bf16[32,2560]{1,0:T(8,128)(2,1)S(1)} collective-permute-done((bf16[32,2560]{1,0:T(8,128)(2,1)S(1)}, bf16[32,2560]{1,0:T(8,128)(2,1)S(1)}, u32[]{:S(2)}, u32[]{:S(2)}) %collective-permute-start) | collective-permute-done | bytes 163872 | tf_op jit(solution)/shard_map/ppermute | solution.py:94
  22.2 1.5 %collective-permute-start.1 = (bf16[64,2560]{1,0:T(8,128)(2,1)S(1)}, bf16[64,2560]{1,0:T(8,128)(2,1)S(1)}, u32[]{:S(2)}, u32[]{:S(2)}) collective-permute-start(bf16[64,2560]{1,0:T(8,128)(2,1)S(1)} %pad_maximum_fusion.2), channel_id=1, source_target_pairs={{0,2},{1,3},{2,0},{3,1},{4,6},{5,7},{6,4},{7,5},{8,10},{9,11},{10,... | collective-permute-start | bytes 983048 | tf_op jit(solution)/shard_map/ppermute | solution.py:94
  23.8 0.0 all-to-all-done.1.cotangent
  23.8 1.1 %tile.11 = bf16[2,2,10,96,128]{4,3,2,1,0:T(8,128)(2,1)} broadcast(bf16[2,10,96,128]{3,2,1,0:T(8,128)(2,1)S(1)} %bitcast.26), dimensions={1,2,3,4} | broadcast | bytes 1474560 | tf_op jit(solution)/shard_map/tile | solution.py:106
  24.9 4.0 %all-to-all-start = ((bf16[4,10,96,128]{3,2,1,0:T(8,128)(2,1)}), bf16[4,10,96,128]{3,2,1,0:T(8,128)(2,1)S(1)}, u32[]{:S(2)}, u32[]{:S(2)}) async-start(bf16[4,10,96,128]{3,2,1,0:T(8,128)(2,1)} %bitcast.11), calls=%async_computation | async-start | bytes 1966080 | tf_op jit(solution)/shard_map/all_to_all | solution.py:107
  28.9 2.7 %collective-permute-done.1 = bf16[64,2560]{1,0:T(8,128)(2,1)S(1)} collective-permute-done((bf16[64,2560]{1,0:T(8,128)(2,1)S(1)}, bf16[64,2560]{1,0:T(8,128)(2,1)S(1)}, u32[]{:S(2)}, u32[]{:S(2)}) %collective-permute-start.1) | collective-permute-done | bytes 327712 | tf_op jit(solution)/shard_map/ppermute | solution.py:94
  31.6 0.1 collective-permute-start.2
  31.7 0.1 constant_dynamic-slice_fusion
  31.8 0.1 copy.10.tiles
  31.9 0.1 dynamic_slice.7.counts
  32.0 0.3 copy-done.3
  32.3 0.1 stack.35.order
  32.4 1.5 %collective-permute-done.2 = bf16[128,2560]{1,0:T(8,128)(2,1)} collective-permute-done((bf16[128,2560]{1,0:T(8,128)(2,1)S(1)}, bf16[128,2560]{1,0:T(8,128)(2,1)}, u32[]{:S(2)}, u32[]{:S(2)}) %collective-permute-start.2) | collective-permute-done | bytes 655392 | tf_op jit(solution)/shard_map/ppermute | solution.py:94
  33.9 1.3 %pad_maximum_fusion.tokens = bf16[256,2560]{1,0:T(8,128)(2,1)S(1)} fusion(bf16[128,2560]{1,0:T(8,128)(2,1)} %collective-permute-done.2, bf16[64,2560]{1,0:T(8,128)(2,1)} %copy-done.3, bf16[32,2560]{1,0:T(8,128)(2,1)S(1)} %collective-permute-done, bf16[32,2560]{1,0:T(8,128)(2,1)S(1)} %copy-done.2), kind=kLoop, calls=%fused_computation.1 | loop fusion | flops 5242880 | bytes 2621440 | tf_op jit(solution)/shard_map/concatenate | solution.py:101
  35.2 17.5 %all-to-all-done.weights = bf16[4,10,96,128]{3,2,1,0:T(8,128)(2,1)S(1)} async-done(((bf16[4,10,96,128]{3,2,1,0:T(8,128)(2,1)}), bf16[4,10,96,128]{3,2,1,0:T(8,128)(2,1)S(1)}, u32[]{:S(2)}, u32[]{:S(2)}) %all-to-all-start) | async-done | bytes 983072 | tf_op jit(solution)/shard_map/all_to_all | solution.py:107
  52.7 5.9 %stripes.1 = (bf16[8,32,1280]{2,1,0:T(8,128)(2,1)S(1)}, bf16[4,10,96,128]{3,2,1,0:T(8,128)(2,1)S(1)}, f32[10,96,128]{2,1,0:T(8,128)S(1)}) custom-call(s32[10,3]{1,0:T(8,128)S(1)} %copy.10.tiles, s32[10]{0:T(128)S(1)} %dynamic_slice.7.counts, s32[8]{0:T(128)S(1)} %stack.35.order, s32[1]{0:T(128)} %bitcast.8.own, ...), custom_call_target="tpu_custom_call" | custom-call | tf_op jit(solution)/shard_map/stripes/pallas_call | solution.py:56
  58.6 0.0 copy-start.1
  58.6 13.3 %all_to_all.20 = bf16[8,32,1280]{2,1,0:T(8,128)(2,1)S(1)} all-to-all(bf16[8,32,1280]{2,1,0:T(8,128)(2,1)S(1)} %get-tuple-element.5), channel_id=1, replica_groups={{0,1,2,3,4,5,6,7},{8,9,10,11,12,13,14,15},{16,17,18,19,20,21,22,23},{24..., dimensions={0} | all-to-all | bytes 1310720 | tf_op jit(solution)/shard_map/all_to_all | solution.py:117
  71.9 3.5 %all-to-all-start.3 = ((bf16[4,10,96,128]{3,2,1,0:T(8,128)(2,1)}), bf16[4,10,96,128]{3,2,1,0:T(8,128)(2,1)S(1)}, u32[]{:S(2)}, u32[]{:S(2)}) async-start(bf16[4,10,96,128]{3,2,1,0:T(8,128)(2,1)} %copy-done.1), calls=%async_computation.3 | async-start | bytes 1966080 | tf_op jit(solution)/shard_map/all_to_all | solution.py:116
  75.5 0.7 copy.9
  76.1 1.3 %reshape.38 = bf16[32,10240]{1,0:T(8,128)(2,1)} reshape(bf16[32,4,2,1280]{3,2,1,0:T(2,128)(2,1)S(1)} %copy.9) | data formatting | bytes 1310720 | tf_op jit(solution)/shard_map/reshape | solution.py:118
  77.5 22.3 %all-to-all-done.3 = bf16[4,10,96,128]{3,2,1,0:T(8,128)(2,1)S(1)} async-done(((bf16[4,10,96,128]{3,2,1,0:T(8,128)(2,1)}), bf16[4,10,96,128]{3,2,1,0:T(8,128)(2,1)S(1)}, u32[]{:S(2)}, u32[]{:S(2)}) %all-to-all-start.3) | async-done | bytes 983072 | tf_op jit(solution)/shard_map/all_to_all | solution.py:116
  99.8 1.6 %convert_select_fusion = f32[4,10,96,128]{3,2,1,0:T(8,128)} fusion(bf16[4,10,96,128]{3,2,1,0:T(8,128)(2,1)S(1)} %all-to-all-done.3, f32[10,96,128]{2,1,0:T(8,128)S(1)} %get-tuple-element.6, pred[4]{0:T(512)(128)(4,1)S(1)} %iota_compare_fusion), kind=kLoop, calls=%fused_computation | loop fusion | flops 983040 | bytes 3440644 | tf_op jit(solution)/shard_map/jit(_where)/select_n | solution.py:121
  101.4 2.7 %reduce_sum.9 = f32[2,10,96,128]{3,2,1,0:T(8,128)} reduce(f32[2,2,10,96,128]{4,3,2,1,0:T(8,128)} %bitcast.23, f32[]{:T(128)} %constant.31.clone.1), dimensions={0}, to_apply=%region_0.1 | reduce | flops 245760 | bytes 2949124 | tf_op jit(solution)/shard_map/reduce_sum | solution.py:122
  (9 shorter events, 0.1 us)
Async XLA Ops:
  0.6 31.1 %copy-start = (s32[20,3]{0,1:T(4,128)S(1)}, s32[20,3]{0,1:T(4,128)}, u32[]{:S(2)}) copy-start(s32[20,3]{0,1:T(4,128)} %param.8) | copy-start | bytes 724
  0.6 7.8 %copy-start.2 = (bf16[32,2560]{1,0:T(8,128)(2,1)S(1)}, bf16[32,2560]{1,0:T(8,128)(2,1)}, u32[]{:S(2)}) copy-start(bf16[32,2560]{1,0:T(8,128)(2,1)} %param.5) | copy-start | bytes 491524
  2.3 21.5 %copy-start.4 = (bf16[96,20,128]{2,0,1:T(8,128)(2,1)S(1)}, bf16[96,20,128]{2,0,1:T(8,128)(2,1)}, u32[]{:S(2)}) copy-start(bf16[96,20,128]{2,0,1:T(8,128)(2,1)} %param.6) | copy-start | bytes 1474564
  3.2 20.5 %all-to-all-start.1 = ((bf16[8,32,1280]{2,1,0:T(8,128)(2,1)}), bf16[8,32,1280]{2,1,0:T(8,128)(2,1)S(1)}, u32[]{:S(2)}, u32[]{:S(2)}) async-start(bf16[8,32,1280]{2,1,0:T(8,128)(2,1)} %bitcast.13), calls=%async_computation.1 | async-start | bytes 1310720 | tf_op jit(solution)/shard_map/all_to_all | solution.py:110
  8.4 13.8 %collective-permute-start = (bf16[32,2560]{1,0:T(8,128)(2,1)S(1)}, bf16[32,2560]{1,0:T(8,128)(2,1)S(1)}, u32[]{:S(2)}, u32[]{:S(2)}) collective-permute-start(bf16[32,2560]{1,0:T(8,128)(2,1)S(1)} %copy-done.2), channel_id=1, source_target_pairs={{0,4},{1,5},{2,6},{3,7},{4,0},{5,1},{6,2},{7,3},{8,12},{9,13},{10,... | collective-permute-start | bytes 491528 | tf_op jit(solution)/shard_map/ppermute | solution.py:94
  22.2 9.3 %collective-permute-start.1 = (bf16[64,2560]{1,0:T(8,128)(2,1)S(1)}, bf16[64,2560]{1,0:T(8,128)(2,1)S(1)}, u32[]{:S(2)}, u32[]{:S(2)}) collective-permute-start(bf16[64,2560]{1,0:T(8,128)(2,1)S(1)} %pad_maximum_fusion.2), channel_id=1, source_target_pairs={{0,2},{1,3},{2,0},{3,1},{4,6},{5,7},{6,4},{7,5},{8,10},{9,11},{10,... | collective-permute-start | bytes 983048 | tf_op jit(solution)/shard_map/ppermute | solution.py:94
  24.9 7.0 %copy-start.5 = (s32[20]{0:T(128)S(1)}, s32[20]{0:T(128)}, u32[]{:S(2)}) copy-start(s32[20]{0:T(128)} %param.9) | copy-start | bytes 244
  24.9 27.8 %all-to-all-start = ((bf16[4,10,96,128]{3,2,1,0:T(8,128)(2,1)}), bf16[4,10,96,128]{3,2,1,0:T(8,128)(2,1)S(1)}, u32[]{:S(2)}, u32[]{:S(2)}) async-start(bf16[4,10,96,128]{3,2,1,0:T(8,128)(2,1)} %bitcast.11), calls=%async_computation | async-start | bytes 1966080 | tf_op jit(solution)/shard_map/all_to_all | solution.py:107
  31.6 0.7 copy-start.3
  31.6 2.3 %collective-permute-start.2 = (bf16[128,2560]{1,0:T(8,128)(2,1)S(1)}, bf16[128,2560]{1,0:T(8,128)(2,1)}, u32[]{:S(2)}, u32[]{:S(2)}) collective-permute-start(bf16[128,2560]{1,0:T(8,128)(2,1)S(1)} %pad_maximum_fusion.1), channel_id=1, source_target_pairs={{0,1},{1,0},{2,3},{3,2},{4,5},{5,4},{6,7},{7,6},{8,9},{9,8},{10,11... | collective-permute-start | bytes 1966088 | tf_op jit(solution)/shard_map/ppermute | solution.py:94
  58.6 13.3 %copy-start.1 = (bf16[4,10,96,128]{3,2,1,0:T(8,128)(2,1)}, bf16[4,10,96,128]{3,2,1,0:T(8,128)(2,1)S(1)}, u32[]{:S(2)}) copy-start(bf16[4,10,96,128]{3,2,1,0:T(8,128)(2,1)S(1)} %get-tuple-element.7) | copy-start | bytes 2949124
  71.9 27.9 %all-to-all-start.3 = ((bf16[4,10,96,128]{3,2,1,0:T(8,128)(2,1)}), bf16[4,10,96,128]{3,2,1,0:T(8,128)(2,1)S(1)}, u32[]{:S(2)}, u32[]{:S(2)}) async-start(bf16[4,10,96,128]{3,2,1,0:T(8,128)(2,1)} %copy-done.1), calls=%async_computation.3 | async-start | bytes 1966080 | tf_op jit(solution)/shard_map/all_to_all | solution.py:116

commit v2 on v1

v2 whole, which is shorter than its diff:
```python
import functools

import jax
import jax.numpy as jnp
from jax import lax
from jax.experimental import pallas as pl
from jax.experimental.pallas import tpu as pltpu
from jax.sharding import PartitionSpec as P

TILE = 128
SLOTS = 3
PAIR = 2
ROOT = 0.7978845608028654
CUBIC = 0.044715
ROOM = pltpu.CompilerParams(vmem_limit_bytes=32 * 2**20)
ANYWHERE = pl.BlockSpec(memory_space=pl.ANY)


def gelu_and_derivative(v):
    square = v * v
    th = jnp.tanh(ROOT * (v + CUBIC * (square * v)))
    half = 0.5 * (1.0 + th)
    inner = ROOT * (1.0 + (3.0 * CUBIC) * square)
    return v * half, half + 0.5 * v * (1.0 - th * th) * inner


def cut_kernel(starts, cotangent, *rest):
    pieces, sems = rest[:-1], rest[-1]
    width = pieces[0].shape[1]
    copies = []
    for b, piece in enumerate(pieces):
        column = pl.multiple_of(starts[b + 1] * TILE, TILE)
        copies.append(pltpu.make_async_copy(cotangent.at[:, pl.ds(column, width)], piece, sems.at[b]))
    for copy in copies:
        copy.start()
    for copy in copies:
        copy.wait()


def cut_call(starts, cotangent, blocks, width):
    return pl.pallas_call(
        cut_kernel,
        out_shape=[jax.ShapeDtypeStruct((cotangent.shape[0], width), cotangent.dtype)] * (blocks - 1),
        in_specs=[pl.BlockSpec(memory_space=pltpu.SMEM), ANYWHERE],
        out_specs=[ANYWHERE] * (blocks - 1),
        scratch_shapes=[pltpu.SemaphoreType.DMA((blocks - 1,))],
        compiler_params=ROOM,
        name="cut",
    )(starts, cotangent)


def join_kernel(starts, *rest):
    pieces, joined, sems = rest[:-2], rest[-2], rest[-1]
    width = pieces[0].shape[1]
    copies = []
    for b, piece in enumerate(pieces):
        column = pl.multiple_of(starts[b] * TILE, TILE)
        copies.append(pltpu.make_async_copy(piece, joined.at[:, pl.ds(column, width)], sems.at[b]))
    for copy in copies:
        copy.start()
    for copy in copies:
        copy.wait()


def join_call(starts, pieces):
    rows, width = pieces[0].shape
    return pl.pallas_call(
        join_kernel,
        out_shape=jax.ShapeDtypeStruct((rows, width * len(pieces)), pieces[0].dtype),
        in_specs=[pl.BlockSpec(memory_space=pltpu.SMEM)] + [ANYWHERE] * len(pieces),
        out_specs=ANYWHERE,
        scratch_shapes=[pltpu.SemaphoreType.DMA((len(pieces),))],
        compiler_params=ROOM,
        name="join",
    )(starts, *pieces)


def stripe_kernel(tiles, counts, starts, own, near, far, weights, *rest):
    s = pl.program_id(0)
    blocks = (len(rest) - 2) // 2
    back, (hidden, (grads, mine)) = rest[:blocks], (rest[blocks:2 * blocks], rest[2 * blocks:])
    rows = back[0].shape[0]
    shards, shard_rows = weights.shape[0], weights.shape[2]
    picked = []
    for k in range(SLOTS):
        column = pl.multiple_of(tiles[s, k] * TILE, TILE)
        block = jnp.concatenate([near[:, pl.ds(column, TILE)], far[:, pl.ds(column, TILE)]], axis=0)
        picked.append(jnp.where(k < counts[s], block, jnp.zeros_like(block)))
    picked = jnp.concatenate(picked, axis=1)
    stack = jnp.concatenate([weights[f, 0] for f in range(shards)], axis=0)
    pre = jnp.dot(picked, stack, preferred_element_type=jnp.float32)
    act, slope = gelu_and_derivative(pre)
    incoming = jnp.concatenate([block[...] for block in back], axis=0)
    slope = (incoming.astype(jnp.float32) * slope).astype(jnp.bfloat16)
    act = act.astype(jnp.bfloat16)
    for b in range(blocks):
        hidden[b][...] = act[b * rows:(b + 1) * rows]
    term = lax.dot_general(picked, slope, (((0,), (0,)), ((), ())), preferred_element_type=jnp.float32)
    for f in range(shards):
        piece = term[f * shard_rows:(f + 1) * shard_rows]
        grads[f, 0] = piece.astype(jnp.bfloat16)

        @pl.when(own[0] == f)
        def _():
            mine[0] = piece


def stripe_call(tiles, counts, starts, own, near, far, weights, cotangent, back):
    shards, stripes, shard_rows, _ = weights.shape
    rows, width = back[0].shape
    blocks = len(back) + 1
    strip = pl.BlockSpec((rows, TILE), lambda s, *_: (0, s))
    stack = pl.BlockSpec((shards, 1, shard_rows, TILE), lambda s, *_: (0, s, 0, 0))
    piece = jax.ShapeDtypeStruct((rows, width), jnp.bfloat16)
    return pl.pallas_call(
        stripe_kernel,
        out_shape=[piece] * blocks + [
            jax.ShapeDtypeStruct(weights.shape, jnp.bfloat16),
            jax.ShapeDtypeStruct(weights.shape[1:], jnp.float32),
        ],
        grid_spec=pltpu.PrefetchScalarGridSpec(
            num_scalar_prefetch=4,
            grid=(stripes,),
            in_specs=[
                pl.BlockSpec(near.shape, lambda s, *_: (0, 0)),
                pl.BlockSpec(far.shape, lambda s, *_: (0, 0)),
                stack,
                pl.BlockSpec((rows, TILE), lambda s, tiles, counts, starts, own: (0, starts[0] + s)),
            ] + [strip] * (blocks - 1),
            out_specs=[strip] * blocks + [stack, pl.BlockSpec((1, shard_rows, TILE), lambda s, *_: (s, 0, 0))],
        ),
        compiler_params=ROOM,
        name="stripes",
    )(tiles, counts, starts, own, near, far, weights, cotangent, *back)


def sum_kernel(own, grads, mine, total):
    shards = grads.shape[0]
    for a in range(PAIR):
        add = None
        for f in range(a, shards, PAIR):
            term = jnp.where(own[0] == f, mine[...], grads[f].astype(jnp.float32))
            add = term if add is None else add + term
        total[a] = add


def sum_call(own, grads, mine):
    shards, stripes, shard_rows, _ = grads.shape
    step = stripes // 2 if stripes % 2 == 0 else stripes
    return pl.pallas_call(
        sum_kernel,
        out_shape=jax.ShapeDtypeStruct((PAIR,) + mine.shape, jnp.float32),
        grid_spec=pltpu.PrefetchScalarGridSpec(
            num_scalar_prefetch=1,
            grid=(stripes // step,),
            in_specs=[
                pl.BlockSpec((shards, step, shard_rows, TILE), lambda s, *_: (0, s, 0, 0)),
                pl.BlockSpec((step, shard_rows, TILE), lambda s, *_: (s, 0, 0)),
            ],
            out_specs=pl.BlockSpec((PAIR, step, shard_rows, TILE), lambda s, *_: (0, s, 0, 0)),
        ),
        compiler_params=ROOM,
        name="sum",
    )(own, grads, mine)


def body(fsdp, tensor, tokens, tile_weights, cotangent, tile_list, tile_counts):
    z, t = lax.axis_index("fsdp"), lax.axis_index("tensor")
    half = z % PAIR
    shard_rows, stripes = tile_weights.shape[0], tile_weights.shape[1]
    share = stripes // PAIR
    width = share * TILE
    blocks = PAIR * tensor

    def swap(value, dz, dt):
        pairs = [(a * tensor + b, (a ^ dz) * tensor + (b ^ dt)) for a in range(fsdp) for b in range(tensor)]
        return lax.ppermute(value, ("fsdp", "tensor"), pairs)

    by_stripe = jnp.transpose(tile_weights, (1, 0, 2)).reshape(PAIR, share, shard_rows, TILE)
    outgoing = jnp.tile(by_stripe, (fsdp // PAIR, 1, 1, 1))
    weights = lax.all_to_all(outgoing, "fsdp", split_axis=0, concat_axis=0, tiled=True)

    steps = [(0, 0), (1, 0)]
    near = jnp.concatenate([tokens, swap(tokens, 1, 0)], axis=0)
    bit = tensor // 2
    while bit:
        steps = steps + [(a, b ^ bit) for a, b in steps]
        far = swap(near, 0, bit)
        if bit > 1:
            near = jnp.concatenate([near, far], axis=0)
        bit //= 2

    starts = jnp.stack([(t ^ b) * stripes + (half ^ a) * share for a, b in steps]).astype(jnp.int32)
    away = cut_call(starts, cotangent, blocks, width)
    back = [swap(piece, *step) for piece, step in zip(away, steps[1:])]

    tiles = lax.dynamic_slice_in_dim(tile_list, half * share, share, 0)
    counts = lax.dynamic_slice_in_dim(tile_counts, half * share, share, 0)
    own = z.reshape(1).astype(jnp.int32)
    *hidden, grads, mine = stripe_call(tiles, counts, starts, own, near, far, weights, cotangent, back)

    grads = lax.all_to_all(grads, "fsdp", split_axis=0, concat_axis=0, tiled=True)
    hidden = [hidden[0]] + [swap(piece, *step) for piece, step in zip(hidden[1:], steps[1:])]
    activations = join_call(starts, hidden)
    total = sum_call(own, grads, mine)
    return activations, total.reshape(stripes, shard_rows, TILE).transpose(1, 0, 2)


def solution(mesh):
    return jax.shard_map(
        functools.partial(body, mesh.shape["fsdp"], mesh.shape["tensor"]),
        mesh=mesh,
        in_specs=(
            P(("member", "fsdp", "tensor"), None),
            P(("member", "fsdp"), "tensor", None),
            P(("member", "fsdp", "tensor"), None),
            P("tensor", None),
            P("tensor"),
        ),
        out_specs=(P(("member", "fsdp", "tensor"), None), P(("member", "fsdp"), "tensor", None)),
        check_vma=False,
    )
```

time: 105 us -> 91.1 us (0.87)
  waiting for transfers between devices: 55.9 us -> 30.2 us
  starting transfers between devices: 16.4 us -> 30.4 us
  blocking collectives: 13.3 us -> 0 us
  local copies, waits for them, and re-layouts: 6.31 us -> 18 us
  other arithmetic: 5.67 us -> 0.02 us
  Pallas kernels: 5.92 us -> 11.2 us
    all_to_all x1, waiting for transfers between devices: 22.3 us -> 0.01 us  [body(): lax.all_to_all(grads, 'fsdp', split_axis=0, concat_axis=0, tiled=True)]
    ppermute x3 -> x17, starting transfers between devices: 3.62 us -> 21.2 us  [swap(): return lax.ppermute(value, ('fsdp', 'tensor'), pairs)]
    all_to_all x1, waiting for transfers between devices: 17.5 us -> 0.01 us  [body(): lax.all_to_all(outgoing, 'fsdp', split_axis=0, concat_axis=0, tiled=True)]
    unnamed x13 -> x69, local copies, waits for them, and re-layouts: 0.43 us -> 15.6 us
    ppermute x3 -> x17, waiting for transfers between devices: 16 us -> 30.2 us  [swap(): return lax.ppermute(value, ('fsdp', 'tensor'), pairs)]
    all_to_all x1 -> x0, blocking collectives: 13.3 us -> none  [body(): lax.all_to_all(hidden, ('fsdp', 'tensor'), split_axis=0, concat_axis=0, a...]
    pallas_call x1 -> x4, Pallas kernels: 5.92 us -> 11.2 us  [the longest x1 7.28 us: stripe_call(): pl.pallas_call(stripe_kernel, out_shape=[piece] * blocks + [jax.ShapeDtyp...]
    all_to_all x1 -> x0, starting transfers between devices: 5.23 us -> none  [body(): lax.all_to_all(away, ('fsdp', 'tensor'), split_axis=0, concat_axis=0, axi...]
  transfers between devices with their start and end apart: 6 -> 19, of which waited for: 5 -> 7; matrix products, arithmetic and copies ran while one was open for 5% -> 3% of each run, Pallas kernels for 0% -> 3%
where the time goes in v2:
time: 91.1 us; the launch traced here: 90.6 us
  starting transfers between devices  30.4 us (33%)
  waiting for transfers between devices  30.2 us (33%)
  local copies, waits for them, and re-layouts  18 us (20%)
  Pallas kernels  11.2 us (12%)
    ppermute x17, waiting for transfers between devices, swap(): return lax.ppermute(value, ('fsdp', 'tensor'), pairs)  30.2 us
    ppermute x17, starting transfers between devices, swap(): return lax.ppermute(value, ('fsdp', 'tensor'), pairs)  21.2 us
    unnamed x69, local copies, waits for them, and re-layouts  15.6 us
    pallas_call x1, Pallas kernels, stripe_call(): pl.pallas_call(stripe_kernel, out_shape=[piece] * blocks + [jax.ShapeDtyp...  7.28 us
    all_to_all x1, starting transfers between devices, body(): lax.all_to_all(grads, 'fsdp', split_axis=0, concat_axis=0, tiled=True)  5.2 us
    all_to_all x1, starting transfers between devices, body(): lax.all_to_all(outgoing, 'fsdp', split_axis=0, concat_axis=0, tiled=True)  3.99 us
    another operation x1, local copies, waits for them, and re-layouts, body(): outgoing = jnp.tile(by_stripe, (fsdp // PAIR, 1, 1, 1))  2.13 us
  transfers between devices with their start and end apart: 19, of which 7 were waited for; matrix products, arithmetic and copies ran while one was open for 3% of the time, Pallas kernels for 3%

profile of v2, /device:TPU:0, one launch (start us, length us, event | category | flops | bytes accessed | tf_op | source)
XLA Modules:
  0.0 90.6 jit_solution(3179644251334082643)
XLA Ops:
  0.6 3.1 %collective-permute-start = (bf16[32,2560]{1,0:T(8,128)(2,1)}, bf16[32,2560]{1,0:T(8,128)(2,1)S(1)}, u32[]{:S(2)}, u32[]{:S(2)}) collective-permute-start(bf16[32,2560]{1,0:T(8,128)(2,1)} %param.5), channel_id=1, source_target_pairs={{0,4},{1,5},{2,6},{3,7},{4,0},{5,1},{6,2},{7,3},{8,12},{9,13},{10,... | collective-permute-start | bytes 491528 | tf_op jit(solution)/shard_map/ppermute | solution.py:177
  3.7 2.1 %tile.11 = bf16[2,2,10,96,128]{4,3,2,1,0:T(8,128)(2,1)} broadcast(bf16[2,10,96,128]{3,2,1,0:T(8,128)(2,1)} %bitcast.17), dimensions={1,2,3,4} | broadcast | bytes 1474560 | tf_op jit(solution)/shard_map/tile | solution.py:180
  5.9 4.0 %all-to-all-start = ((bf16[4,10,96,128]{3,2,1,0:T(8,128)(2,1)}), bf16[4,10,96,128]{3,2,1,0:T(8,128)(2,1)S(1)}, u32[]{:S(2)}, u32[]{:S(2)}) async-start(bf16[4,10,96,128]{3,2,1,0:T(8,128)(2,1)} %bitcast.11), calls=%async_computation | async-start | bytes 1966080 | tf_op jit(solution)/shard_map/all_to_all | solution.py:181
  9.9 1.6 %collective-permute-start.1 = (bf16[64,2560]{1,0:T(8,128)(2,1)S(1)}, bf16[64,2560]{1,0:T(8,128)(2,1)S(1)}, u32[]{:S(2)}, u32[]{:S(2)}) collective-permute-start(bf16[64,2560]{1,0:T(8,128)(2,1)S(1)} %pad_maximum_fusion), channel_id=1, source_target_pairs={{0,2},{1,3},{2,0},{3,1},{4,6},{5,7},{6,4},{7,5},{8,10},{9,11},{10,... | collective-permute-start | bytes 983048 | tf_op jit(solution)/shard_map/ppermute | solution.py:177
  11.5 7.4 %collective-permute-done.1 = bf16[64,2560]{1,0:T(8,128)(2,1)S(1)} collective-permute-done((bf16[64,2560]{1,0:T(8,128)(2,1)S(1)}, bf16[64,2560]{1,0:T(8,128)(2,1)S(1)}, u32[]{:S(2)}, u32[]{:S(2)}) %collective-permute-start.1) | collective-permute-done | bytes 327712 | tf_op jit(solution)/shard_map/ppermute | solution.py:177
  19.1 1.3 %cut.1 = (bf16[32,1280]{1,0:T(8,128)(2,1)S(1)}, bf16[32,1280]{1,0:T(8,128)(2,1)}, bf16[32,1280]{1,0:T(8,128)(2,1)}, bf16[32,1280]{1,0:T(8,128)(2,1)}, bf16[32,12...) custom-call(s32[8]{0:T(128)S(1)} %stack.35.starts, bf16[32,10240]{1,0:T(8,128)(2,1)S(1)} %copy-done.1), custom_call_target="tpu_custom_call" | custom-call | tf_op jit(solution)/shard_map/cut/pallas_call | solution.py:41
  21.1 1.7 %collective-permute-start.3 = (bf16[32,1280]{1,0:T(8,128)(2,1)S(1)}, bf16[32,1280]{1,0:T(8,128)(2,1)S(1)}, u32[]{:S(2)}, u32[]{:S(2)}) collective-permute-start(bf16[32,1280]{1,0:T(8,128)(2,1)S(1)} %get-tuple-element.19), channel_id=1, source_target_pairs={{0,4},{1,5},{2,6},{3,7},{4,0},{5,1},{6,2},{7,3},{8,12},{9,13},{10,... | collective-permute-start | bytes 245768 | tf_op jit(solution)/shard_map/ppermute | solution.py:177
  22.8 1.5 %collective-permute-start.4 = (bf16[32,1280]{1,0:T(8,128)(2,1)}, bf16[32,1280]{1,0:T(8,128)(2,1)S(1)}, u32[]{:S(2)}, u32[]{:S(2)}) collective-permute-start(bf16[32,1280]{1,0:T(8,128)(2,1)} %get-tuple-element.20), channel_id=1, source_target_pairs={{0,2},{1,3},{2,0},{3,1},{4,6},{5,7},{6,4},{7,5},{8,10},{9,11},{10,... | collective-permute-start | bytes 245768 | tf_op jit(solution)/shard_map/ppermute | solution.py:177
  24.6 0.7 copy-done.32
  25.3 2.9 %collective-permute-done.3.rest_1_ = bf16[32,1280]{1,0:T(8,128)(2,1)S(1)} collective-permute-done((bf16[32,1280]{1,0:T(8,128)(2,1)S(1)}, bf16[32,1280]{1,0:T(8,128)(2,1)S(1)}, u32[]{:S(2)}, u32[]{:S(2)}) %collective-permute-start.3) | collective-permute-done | bytes 81952 | tf_op jit(solution)/shard_map/ppermute | solution.py:177
  28.2 0.6 copy-done.2
  28.8 3.7 %collective-permute-start.8 = (bf16[32,1280]{1,0:T(8,128)(2,1)S(1)}, bf16[32,1280]{1,0:T(8,128)(2,1)S(1)}, u32[]{:S(2)}, u32[]{:S(2)}) collective-permute-start(bf16[32,1280]{1,0:T(8,128)(2,1)S(1)} %get-tuple-element.24), channel_id=1, source_target_pairs={{0,3},{1,2},{2,1},{3,0},{4,7},{5,6},{6,5},{7,4},{8,11},{9,10},{10,... | collective-permute-start | bytes 245768 | tf_op jit(solution)/shard_map/ppermute | solution.py:177
  34.0 1.6 %collective-permute-done.7.rest_5_ = bf16[32,1280]{1,0:T(8,128)(2,1)S(1)} collective-permute-done((bf16[32,1280]{1,0:T(8,128)(2,1)}, bf16[32,1280]{1,0:T(8,128)(2,1)S(1)}, u32[]{:S(2)}, u32[]{:S(2)}) %collective-permute-start.7) | collective-permute-done | bytes 81952 | tf_op jit(solution)/shard_map/ppermute | solution.py:177
  36.8 1.5 %collective-permute-done.9.rest_7_ = bf16[32,1280]{1,0:T(8,128)(2,1)S(1)} collective-permute-done((bf16[32,1280]{1,0:T(8,128)(2,1)S(1)}, bf16[32,1280]{1,0:T(8,128)(2,1)S(1)}, u32[]{:S(2)}, u32[]{:S(2)}) %collective-permute-start.9) | collective-permute-done | bytes 81952 | tf_op jit(solution)/shard_map/ppermute | solution.py:177
  39.0 0.9 copy-done.3
  39.9 0.9 copy-done.5
  40.8 0.9 copy-done.7
  41.6 0.9 copy-done.11
  42.5 0.9 copy-done.13
  43.4 0.9 copy-done.15
  44.3 7.3 %stripes.1 = (bf16[32,1280]{1,0:T(8,128)(2,1)S(1)}, bf16[32,1280]{1,0:T(8,128)(2,1)S(1)}, bf16[32,1280]{1,0:T(8,128)(2,1)S(1)}, bf16[32,1280]{1,0:T(8,128)(2,1)S...) custom-call(s32[10,3]{1,0:T(8,128)S(1)} %copy.8.tiles, ...), custom_call_target="tpu_custom_call" | custom-call | tf_op jit(solution)/shard_map/stripes/pallas_call | solution.py:115
  56.7 5.2 %all-to-all-start.1 = ((bf16[4,10,96,128]{3,2,1,0:T(8,128)(2,1)}), bf16[4,10,96,128]{3,2,1,0:T(8,128)(2,1)S(1)}, u32[]{:S(2)}, u32[]{:S(2)}) async-start(bf16[4,10,96,128]{3,2,1,0:T(8,128)(2,1)} %get-tuple-element.34), calls=%async_computation.1 | async-start | bytes 1966080 | tf_op jit(solution)/shard_map/all_to_all | solution.py:202
  61.9 2.0 %collective-permute-start.10 = (bf16[32,1280]{1,0:T(8,128)(2,1)S(1)}, bf16[32,1280]{1,0:T(8,128)(2,1)S(1)}, u32[]{:S(2)}, u32[]{:S(2)}) collective-permute-start(bf16[32,1280]{1,0:T(8,128)(2,1)S(1)} %copy-done.30), channel_id=1, source_target_pairs={{0,4},{1,5},{2,6},{3,7},{4,0},{5,1},{6,2},{7,3},{8,12},{9,13},{10,... | collective-permute-start | bytes 245768 | tf_op jit(solution)/shard_map/ppermute | solution.py:177
  63.9 0.9 collective-permute-start.11
  64.8 0.7 collective-permute-start.12
  65.5 2.1 %collective-permute-start.14 = (bf16[32,1280]{1,0:T(8,128)(2,1)S(1)}, bf16[32,1280]{1,0:T(8,128)(2,1)S(1)}, u32[]{:S(2)}, u32[]{:S(2)}) collective-permute-start(bf16[32,1280]{1,0:T(8,128)(2,1)S(1)} %copy-done.21), channel_id=1, source_target_pairs={{0,5},{1,4},{2,7},{3,6},{4,1},{5,0},{6,3},{7,2},{8,13},{9,12},{10,... | collective-permute-start | bytes 245768 | tf_op jit(solution)/shard_map/ppermute | solution.py:177
  67.5 12.6 %collective-permute-done.10.rest_1_ = bf16[32,1280]{1,0:T(8,128)(2,1)S(1)} collective-permute-done((bf16[32,1280]{1,0:T(8,128)(2,1)S(1)}, bf16[32,1280]{1,0:T(8,128)(2,1)S(1)}, u32[]{:S(2)}, u32[]{:S(2)}) %collective-permute-start.10) | collective-permute-done | bytes 81952 | tf_op jit(solution)/shard_map/ppermute | solution.py:177
  80.2 3.7 %collective-permute-start.16 = (bf16[32,1280]{1,0:T(8,128)(2,1)S(1)}, bf16[32,1280]{1,0:T(8,128)(2,1)S(1)}, u32[]{:S(2)}, u32[]{:S(2)}) collective-permute-start(bf16[32,1280]{1,0:T(8,128)(2,1)S(1)} %copy-done.17), channel_id=1, source_target_pairs={{0,7},{1,6},{2,5},{3,4},{4,3},{5,2},{6,1},{7,0},{8,15},{9,14},{10,... | collective-permute-start | bytes 245768 | tf_op jit(solution)/shard_map/ppermute | solution.py:177
  83.8 1.0 %collective-permute-done.15.rest_6_ = bf16[32,1280]{1,0:T(8,128)(2,1)S(1)} collective-permute-done((bf16[32,1280]{1,0:T(8,128)(2,1)S(1)}, bf16[32,1280]{1,0:T(8,128)(2,1)S(1)}, u32[]{:S(2)}, u32[]{:S(2)}) %collective-permute-start.15) | collective-permute-done | bytes 81952 | tf_op jit(solution)/shard_map/ppermute | solution.py:177
  84.8 3.2 %collective-permute-done.16.rest_7_ = bf16[32,1280]{1,0:T(8,128)(2,1)S(1)} collective-permute-done((bf16[32,1280]{1,0:T(8,128)(2,1)S(1)}, bf16[32,1280]{1,0:T(8,128)(2,1)S(1)}, u32[]{:S(2)}, u32[]{:S(2)}) %collective-permute-start.16) | collective-permute-done | bytes 81952 | tf_op jit(solution)/shard_map/ppermute | solution.py:177
  88.0 1.4 %join.1 = bf16[32,10240]{1,0:T(8,128)(2,1)} custom-call(s32[8]{0:T(128)S(1)} %stack.35.starts, bf16[32,1280]{1,0:T(8,128)(2,1)S(1)} %copy-done.9, bf16[32,1280]{1,0:T(8,128)(2,1)S(1)} %collective-permute-done.10.rest_1_, bf16[32,1280]{1,0:T(8,128)(2,1)S(1)} %collective-permute-done.11.rest_2_, bf16[32,1280]{1,0:T(8,128)(2,1)S(1)} %collective-permute-done.12.rest_3_, ...), custom_call_target="tpu_custom_call" | custom-call | tf_op jit(solution)/shard_map/join/pallas_call | solution.py:67
  89.4 1.1 %sum.1 = f32[2,10,96,128]{3,2,1,0:T(8,128)} custom-call(s32[1]{0:T(128)} %bitcast.8.own, bf16[4,10,96,128]{3,2,1,0:T(8,128)(2,1)S(1)} %all-to-all-done.1.grads, f32[10,96,128]{2,1,0:T(8,128)S(1)} %get-tuple-element.35.mine), custom_call_target="tpu_custom_call" | custom-call | tf_op jit(solution)/shard_map/sum/pallas_call | solution.py:150
  (85 shorter events, 9.7 us)
Async XLA Ops:
  0.6 32.6 %copy-start = (s32[20,3]{0,1:T(4,128)S(1)}, s32[20,3]{0,1:T(4,128)}, u32[]{:S(2)}) copy-start(s32[20,3]{0,1:T(4,128)} %param.8) | copy-start | bytes 724
  0.6 9.2 %collective-permute-start = (bf16[32,2560]{1,0:T(8,128)(2,1)}, bf16[32,2560]{1,0:T(8,128)(2,1)S(1)}, u32[]{:S(2)}, u32[]{:S(2)}) collective-permute-start(bf16[32,2560]{1,0:T(8,128)(2,1)} %param.5), channel_id=1, source_target_pairs={{0,4},{1,5},{2,6},{3,7},{4,0},{5,1},{6,2},{7,3},{8,12},{9,13},{10,... | collective-permute-start | bytes 491528 | tf_op jit(solution)/shard_map/ppermute | solution.py:177
  5.9 4.0 %copy-start.31 = (bf16[32,2560]{1,0:T(8,128)(2,1)S(1)}, bf16[32,2560]{1,0:T(8,128)(2,1)}, u32[]{:S(2)}) copy-start(bf16[32,2560]{1,0:T(8,128)(2,1)} %param.5) | copy-start | bytes 491524
  5.9 33.1 %all-to-all-start = ((bf16[4,10,96,128]{3,2,1,0:T(8,128)(2,1)}), bf16[4,10,96,128]{3,2,1,0:T(8,128)(2,1)S(1)}, u32[]{:S(2)}, u32[]{:S(2)}) async-start(bf16[4,10,96,128]{3,2,1,0:T(8,128)(2,1)} %bitcast.11), calls=%async_computation | async-start | bytes 1966080 | tf_op jit(solution)/shard_map/all_to_all | solution.py:181
  9.9 9.2 %copy-start.1 = (bf16[32,10240]{1,0:T(8,128)(2,1)S(1)}, bf16[32,10240]{1,0:T(8,128)(2,1)}, u32[]{:S(2)}) copy-start(bf16[32,10240]{1,0:T(8,128)(2,1)} %rest_0_.1) | copy-start | bytes 1966084
  9.9 9.0 %collective-permute-start.1 = (bf16[64,2560]{1,0:T(8,128)(2,1)S(1)}, bf16[64,2560]{1,0:T(8,128)(2,1)S(1)}, u32[]{:S(2)}, u32[]{:S(2)}) collective-permute-start(bf16[64,2560]{1,0:T(8,128)(2,1)S(1)} %pad_maximum_fusion), channel_id=1, source_target_pairs={{0,2},{1,3},{2,0},{3,1},{4,6},{5,7},{6,4},{7,5},{8,10},{9,11},{10,... | collective-permute-start | bytes 983048 | tf_op jit(solution)/shard_map/ppermute | solution.py:177
  18.9 20.1 %collective-permute-start.2 = (bf16[128,2560]{1,0:T(8,128)(2,1)S(1)}, bf16[128,2560]{1,0:T(8,128)(2,1)S(1)}, u32[]{:S(2)}, u32[]{:S(2)}) collective-permute-start(bf16[128,2560]{1,0:T(8,128)(2,1)S(1)} %constant_dynamic-update-slice_fusion.near), channel_id=1, source_target_pairs={{0,1},{1,0},{2,3},{3,2},{4,5},{5,4},{6,7},{7,6},{8,9},{9,8},{10,11... | collective-permute-start | bytes 1966088 | tf_op jit(solution)/shard_map/ppermute | solution.py:177
  21.1 7.1 %collective-permute-start.3 = (bf16[32,1280]{1,0:T(8,128)(2,1)S(1)}, bf16[32,1280]{1,0:T(8,128)(2,1)S(1)}, u32[]{:S(2)}, u32[]{:S(2)}) collective-permute-start(bf16[32,1280]{1,0:T(8,128)(2,1)S(1)} %get-tuple-element.19), channel_id=1, source_target_pairs={{0,4},{1,5},{2,6},{3,7},{4,0},{5,1},{6,2},{7,3},{8,12},{9,13},{10,... | collective-permute-start | bytes 245768 | tf_op jit(solution)/shard_map/ppermute | solution.py:177
  22.8 5.4 %collective-permute-start.4 = (bf16[32,1280]{1,0:T(8,128)(2,1)}, bf16[32,1280]{1,0:T(8,128)(2,1)S(1)}, u32[]{:S(2)}, u32[]{:S(2)}) collective-permute-start(bf16[32,1280]{1,0:T(8,128)(2,1)} %get-tuple-element.20), channel_id=1, source_target_pairs={{0,2},{1,3},{2,0},{3,1},{4,6},{5,7},{6,4},{7,5},{8,10},{9,11},{10,... | collective-permute-start | bytes 245768 | tf_op jit(solution)/shard_map/ppermute | solution.py:177
  24.3 8.2 %collective-permute-start.5 = (bf16[32,1280]{1,0:T(8,128)(2,1)}, bf16[32,1280]{1,0:T(8,128)(2,1)S(1)}, u32[]{:S(2)}, u32[]{:S(2)}) collective-permute-start(bf16[32,1280]{1,0:T(8,128)(2,1)} %get-tuple-element.21), channel_id=1, source_target_pairs={{0,6},{1,7},{2,4},{3,5},{4,2},{5,3},{6,0},{7,1},{8,14},{9,15},{10,... | collective-permute-start | bytes 245768 | tf_op jit(solution)/shard_map/ppermute | solution.py:177
  24.6 8.8 %collective-permute-start.6 = (bf16[32,1280]{1,0:T(8,128)(2,1)}, bf16[32,1280]{1,0:T(8,128)(2,1)S(1)}, u32[]{:S(2)}, u32[]{:S(2)}) collective-permute-start(bf16[32,1280]{1,0:T(8,128)(2,1)} %get-tuple-element.22), channel_id=1, source_target_pairs={{0,1},{1,0},{2,3},{3,2},{4,5},{5,4},{6,7},{7,6},{8,9},{9,8},{10,11... | collective-permute-start | bytes 245768 | tf_op jit(solution)/shard_map/ppermute | solution.py:177
  28.2 7.3 %collective-permute-start.7 = (bf16[32,1280]{1,0:T(8,128)(2,1)}, bf16[32,1280]{1,0:T(8,128)(2,1)S(1)}, u32[]{:S(2)}, u32[]{:S(2)}) collective-permute-start(bf16[32,1280]{1,0:T(8,128)(2,1)} %copy-done.26), channel_id=1, source_target_pairs={{0,5},{1,4},{2,7},{3,6},{4,1},{5,0},{6,3},{7,2},{8,13},{9,12},{10,... | collective-permute-start | bytes 245768 | tf_op jit(solution)/shard_map/ppermute | solution.py:177
  28.8 7.3 %collective-permute-start.8 = (bf16[32,1280]{1,0:T(8,128)(2,1)S(1)}, bf16[32,1280]{1,0:T(8,128)(2,1)S(1)}, u32[]{:S(2)}, u32[]{:S(2)}) collective-permute-start(bf16[32,1280]{1,0:T(8,128)(2,1)S(1)} %get-tuple-element.24), channel_id=1, source_target_pairs={{0,3},{1,2},{2,1},{3,0},{4,7},{5,6},{6,5},{7,4},{8,11},{9,10},{10,... | collective-permute-start | bytes 245768 | tf_op jit(solution)/shard_map/ppermute | solution.py:177
  33.2 5.2 %collective-permute-start.9 = (bf16[32,1280]{1,0:T(8,128)(2,1)S(1)}, bf16[32,1280]{1,0:T(8,128)(2,1)S(1)}, u32[]{:S(2)}, u32[]{:S(2)}) collective-permute-start(bf16[32,1280]{1,0:T(8,128)(2,1)S(1)} %get-tuple-element.25), channel_id=1, source_target_pairs={{0,7},{1,6},{2,5},{3,4},{4,3},{5,2},{6,1},{7,0},{8,15},{9,14},{10,... | collective-permute-start | bytes 245768 | tf_op jit(solution)/shard_map/ppermute | solution.py:177
  39.0 0.9 copy-start.3
  42.5 0.9 copy-start.13
  56.6 5.3 %copy-start.30 = (bf16[32,1280]{1,0:T(8,128)(2,1)S(1)}, bf16[32,1280]{1,0:T(8,128)(2,1)}, u32[]{:S(2)}) copy-start(bf16[32,1280]{1,0:T(8,128)(2,1)} %copy-done.29) | copy-start | bytes 245764
  56.6 7.3 %copy-start.28 = (bf16[32,1280]{1,0:T(8,128)(2,1)S(1)}, bf16[32,1280]{1,0:T(8,128)(2,1)}, u32[]{:S(2)}) copy-start(bf16[32,1280]{1,0:T(8,128)(2,1)} %copy-done.27) | copy-start | bytes 245764
  56.6 8.1 %copy-start.25 = (bf16[32,1280]{1,0:T(8,128)(2,1)S(1)}, bf16[32,1280]{1,0:T(8,128)(2,1)}, u32[]{:S(2)}) copy-start(bf16[32,1280]{1,0:T(8,128)(2,1)} %copy-done.24) | copy-start | bytes 245764
  56.6 8.8 %copy-start.23 = (bf16[32,1280]{1,0:T(8,128)(2,1)S(1)}, bf16[32,1280]{1,0:T(8,128)(2,1)}, u32[]{:S(2)}) copy-start(bf16[32,1280]{1,0:T(8,128)(2,1)} %copy-done.22) | copy-start | bytes 245764
  56.6 8.8 %copy-start.21 = (bf16[32,1280]{1,0:T(8,128)(2,1)S(1)}, bf16[32,1280]{1,0:T(8,128)(2,1)}, u32[]{:S(2)}) copy-start(bf16[32,1280]{1,0:T(8,128)(2,1)} %copy-done.20) | copy-start | bytes 245764
  56.7 23.5 %copy-start.19 = (bf16[32,1280]{1,0:T(8,128)(2,1)S(1)}, bf16[32,1280]{1,0:T(8,128)(2,1)}, u32[]{:S(2)}) copy-start(bf16[32,1280]{1,0:T(8,128)(2,1)} %copy-done.18) | copy-start | bytes 245764
  56.7 23.5 %copy-start.17 = (bf16[32,1280]{1,0:T(8,128)(2,1)S(1)}, bf16[32,1280]{1,0:T(8,128)(2,1)}, u32[]{:S(2)}) copy-start(bf16[32,1280]{1,0:T(8,128)(2,1)} %copy-done.16) | copy-start | bytes 245764
  56.7 31.3 %copy-start.9 = (bf16[32,1280]{1,0:T(8,128)(2,1)S(1)}, bf16[32,1280]{1,0:T(8,128)(2,1)}, u32[]{:S(2)}) copy-start(bf16[32,1280]{1,0:T(8,128)(2,1)} %copy-done.8) | copy-start | bytes 245764
  56.7 32.7 %all-to-all-start.1 = ((bf16[4,10,96,128]{3,2,1,0:T(8,128)(2,1)}), bf16[4,10,96,128]{3,2,1,0:T(8,128)(2,1)S(1)}, u32[]{:S(2)}, u32[]{:S(2)}) async-start(bf16[4,10,96,128]{3,2,1,0:T(8,128)(2,1)} %get-tuple-element.34), calls=%async_computation.1 | async-start | bytes 1966080 | tf_op jit(solution)/shard_map/all_to_all | solution.py:202
  61.9 18.3 %collective-permute-start.10 = (bf16[32,1280]{1,0:T(8,128)(2,1)S(1)}, bf16[32,1280]{1,0:T(8,128)(2,1)S(1)}, u32[]{:S(2)}, u32[]{:S(2)}) collective-permute-start(bf16[32,1280]{1,0:T(8,128)(2,1)S(1)} %copy-done.30), channel_id=1, source_target_pairs={{0,4},{1,5},{2,6},{3,7},{4,0},{5,1},{6,2},{7,3},{8,12},{9,13},{10,... | collective-permute-start | bytes 245768 | tf_op jit(solution)/shard_map/ppermute | solution.py:177
  63.9 16.2 %collective-permute-start.11 = (bf16[32,1280]{1,0:T(8,128)(2,1)S(1)}, bf16[32,1280]{1,0:T(8,128)(2,1)S(1)}, u32[]{:S(2)}, u32[]{:S(2)}) collective-permute-start(bf16[32,1280]{1,0:T(8,128)(2,1)S(1)} %copy-done.28), channel_id=1, source_target_pairs={{0,2},{1,3},{2,0},{3,1},{4,6},{5,7},{6,4},{7,5},{8,10},{9,11},{10,... | collective-permute-start | bytes 245768 | tf_op jit(solution)/shard_map/ppermute | solution.py:177
  64.8 19.1 %collective-permute-start.12 = (bf16[32,1280]{1,0:T(8,128)(2,1)S(1)}, bf16[32,1280]{1,0:T(8,128)(2,1)S(1)}, u32[]{:S(2)}, u32[]{:S(2)}) collective-permute-start(bf16[32,1280]{1,0:T(8,128)(2,1)S(1)} %copy-done.25), channel_id=1, source_target_pairs={{0,6},{1,7},{2,4},{3,5},{4,2},{5,3},{6,0},{7,1},{8,14},{9,15},{10,... | collective-permute-start | bytes 245768 | tf_op jit(solution)/shard_map/ppermute | solution.py:177
  65.5 18.4 %collective-permute-start.13 = (bf16[32,1280]{1,0:T(8,128)(2,1)S(1)}, bf16[32,1280]{1,0:T(8,128)(2,1)S(1)}, u32[]{:S(2)}, u32[]{:S(2)}) collective-permute-start(bf16[32,1280]{1,0:T(8,128)(2,1)S(1)} %copy-done.23), channel_id=1, source_target_pairs={{0,1},{1,0},{2,3},{3,2},{4,5},{5,4},{6,7},{7,6},{8,9},{9,8},{10,11... | collective-permute-start | bytes 245768 | tf_op jit(solution)/shard_map/ppermute | solution.py:177
  65.5 18.4 %collective-permute-start.14 = (bf16[32,1280]{1,0:T(8,128)(2,1)S(1)}, bf16[32,1280]{1,0:T(8,128)(2,1)S(1)}, u32[]{:S(2)}, u32[]{:S(2)}) collective-permute-start(bf16[32,1280]{1,0:T(8,128)(2,1)S(1)} %copy-done.21), channel_id=1, source_target_pairs={{0,5},{1,4},{2,7},{3,6},{4,1},{5,0},{6,3},{7,2},{8,13},{9,12},{10,... | collective-permute-start | bytes 245768 | tf_op jit(solution)/shard_map/ppermute | solution.py:177
  80.2 4.7 %collective-permute-start.15 = (bf16[32,1280]{1,0:T(8,128)(2,1)S(1)}, bf16[32,1280]{1,0:T(8,128)(2,1)S(1)}, u32[]{:S(2)}, u32[]{:S(2)}) collective-permute-start(bf16[32,1280]{1,0:T(8,128)(2,1)S(1)} %copy-done.19), channel_id=1, source_target_pairs={{0,3},{1,2},{2,1},{3,0},{4,7},{5,6},{6,5},{7,4},{8,11},{9,10},{10,... | collective-permute-start | bytes 245768 | tf_op jit(solution)/shard_map/ppermute | solution.py:177
  80.2 7.8 %collective-permute-start.16 = (bf16[32,1280]{1,0:T(8,128)(2,1)S(1)}, bf16[32,1280]{1,0:T(8,128)(2,1)S(1)}, u32[]{:S(2)}, u32[]{:S(2)}) collective-permute-start(bf16[32,1280]{1,0:T(8,128)(2,1)S(1)} %copy-done.17), channel_id=1, source_target_pairs={{0,7},{1,6},{2,5},{3,4},{4,3},{5,2},{6,1},{7,0},{8,15},{9,14},{10,... | collective-permute-start | bytes 245768 | tf_op jit(solution)/shard_map/ppermute | solution.py:177
  (20 other events, 13.7 us)

commit v3 on v1

v3 whole, which is shorter than its diff:
```python
import functools

import jax
import jax.numpy as jnp
from jax import lax
from jax.experimental import pallas as pl
from jax.experimental.pallas import tpu as pltpu
from jax.sharding import PartitionSpec as P

TILE = 128
SLOTS = 3
PAIR = 2
DIRECT = 8
ROOT = 0.7978845608028654
CUBIC = 0.044715
ANYWHERE = pl.BlockSpec(memory_space=pl.ANY)


def room(mib):
    return pltpu.CompilerParams(vmem_limit_bytes=mib * 2**20)


def gelu_and_derivative(v):
    square = v * v
    th = jnp.tanh(ROOT * (v + CUBIC * (square * v)))
    half = 0.5 * (1.0 + th)
    inner = ROOT * (1.0 + (3.0 * CUBIC) * square)
    return v * half, half + 0.5 * v * (1.0 - th * th) * inner


def columns(block, tensor, width):
    return pl.ds(((block % tensor) * PAIR + block // tensor) * width, width)


def copy_all(copies):
    for copy in copies:
        copy.start()
    for copy in copies:
        copy.wait()


def cut_kernel(tensor, whole, pieces, sems):
    blocks, _, width = pieces.shape
    copy_all([pltpu.make_async_copy(whole.at[:, columns(b, tensor, width)], pieces.at[b], sems.at[b]) for b in range(blocks)])


def cut_call(tensor, whole):
    blocks = PAIR * tensor
    rows, width = whole.shape[0], whole.shape[1] // blocks
    return pl.pallas_call(
        functools.partial(cut_kernel, tensor),
        out_shape=jax.ShapeDtypeStruct((blocks, rows, width), whole.dtype),
        in_specs=[ANYWHERE],
        out_specs=ANYWHERE,
        scratch_shapes=[pltpu.SemaphoreType.DMA((blocks,))],
        compiler_params=room(1),
        name="cut",
    )(whole)


def join_kernel(tensor, pieces, whole, sems):
    blocks, _, width = pieces.shape
    copy_all([pltpu.make_async_copy(pieces.at[b], whole.at[:, columns(b, tensor, width)], sems.at[b]) for b in range(blocks)])


def join_call(tensor, pieces):
    blocks, rows, width = pieces.shape
    return pl.pallas_call(
        functools.partial(join_kernel, tensor),
        out_shape=jax.ShapeDtypeStruct((rows, blocks * width), pieces.dtype),
        in_specs=[ANYWHERE],
        out_specs=ANYWHERE,
        scratch_shapes=[pltpu.SemaphoreType.DMA((blocks,))],
        compiler_params=room(1),
        name="join",
    )(pieces)


def stripe_kernel(parts, step, tiles, counts, order, places, near, far, cotangent, *rest):
    weights, hidden, grads, (stack, term) = rest[:parts], rest[parts], rest[parts + 1:2 * parts + 1], rest[2 * parts + 1:]
    blocks, rows = cotangent.shape[0], cotangent.shape[1]
    size = weights[0].shape[1]
    spans = [pl.ds(pl.multiple_of(places[p], size), size) for p in range(parts)]
    for i in range(step):
        s = pl.program_id(0) * step + i
        cols = slice(i * TILE, (i + 1) * TILE)
        picked = []
        for k in range(SLOTS):
            column = pl.multiple_of(tiles[s, k] * TILE, TILE)
            block = jnp.concatenate([near[:, pl.ds(column, TILE)], far[:, pl.ds(column, TILE)]], axis=0)
            picked.append(jnp.where(k < counts[s], block, jnp.zeros_like(block)))
        picked = jnp.concatenate(picked, axis=1)
        for p in range(parts):
            stack[i, spans[p]] = weights[p][i]
        pre = jnp.dot(picked, stack[i], preferred_element_type=jnp.float32)
        act, slope = gelu_and_derivative(pre)
        back = jnp.concatenate([cotangent[order[b], :, cols] for b in range(blocks)], axis=0)
        slope = (back.astype(jnp.float32) * slope).astype(jnp.bfloat16)
        act = act.astype(jnp.bfloat16)
        for b in range(blocks):
            hidden[order[b], :, cols] = act[b * rows:(b + 1) * rows]
        term[i] = lax.dot_general(picked, slope, (((0,), (0,)), ((), ())), preferred_element_type=jnp.float32)
        for p in range(parts):
            grads[p][i] = term[i, spans[p]].astype(grads[p].dtype)


def stripe_call(tiles, counts, order, places, near, far, cotangent, weights):
    blocks, rows, width = cotangent.shape
    stripes, size, _ = weights[0].shape
    parts = len(weights)
    step = 2 if stripes % 2 == 0 else 1
    strip = pl.BlockSpec((blocks, rows, step * TILE), lambda s, *_: (0, 0, s))
    piece = pl.BlockSpec((step, size, TILE), lambda s, *_: (s, 0, 0))
    whole = pl.BlockSpec(near.shape, lambda s, *_: (0, 0))
    return pl.pallas_call(
        functools.partial(stripe_kernel, parts, step),
        out_shape=[jax.ShapeDtypeStruct(cotangent.shape, jnp.bfloat16)]
        + [jax.ShapeDtypeStruct(weights[0].shape, jnp.bfloat16 if p else jnp.float32) for p in range(parts)],
        grid_spec=pltpu.PrefetchScalarGridSpec(
            num_scalar_prefetch=4,
            grid=(stripes // step,),
            in_specs=[whole, whole, strip] + [piece] * parts,
            out_specs=[strip] + [piece] * parts,
            scratch_shapes=[
                pltpu.VMEM((step, SLOTS * TILE, TILE), jnp.bfloat16),
                pltpu.VMEM((step, SLOTS * TILE, TILE), jnp.float32),
            ],
        ),
        compiler_params=room(16),
        name="stripes",
    )(tiles, counts, order, places, near, far, cotangent, *weights)


def sum_kernel(half, *rest):
    grads, total = rest[:-1], rest[-1]
    for a in range(PAIR):

        @pl.when(pl.program_id(0) == a)
        def _():
            add = None
            for piece in grads[a::PAIR]:
                term = piece[...].astype(jnp.float32)
                add = term if add is None else add + term
            total[0] = add


def sum_call(half, grads):
    stripes, size, _ = grads[0].shape
    step = stripes // 2 if stripes % 2 == 0 else stripes
    chunks = stripes // step
    first = pl.BlockSpec((step, size, TILE), lambda a, c, half: (jnp.where(a == 0, c, chunks - 1), 0, 0))
    second = pl.BlockSpec((step, size, TILE), lambda a, c, half: (jnp.where(a == 0, 0, c), 0, 0))
    return pl.pallas_call(
        sum_kernel,
        out_shape=jax.ShapeDtypeStruct((PAIR, stripes, size, TILE), jnp.float32),
        grid_spec=pltpu.PrefetchScalarGridSpec(
            num_scalar_prefetch=1,
            grid=(PAIR, chunks),
            in_specs=[second if p % PAIR else first for p in range(len(grads))],
            out_specs=pl.BlockSpec((1, step, size, TILE), lambda a, c, half: (half[0] ^ a, c, 0, 0)),
        ),
        compiler_params=room(16),
        name="sum",
    )(half, *grads)


def body(fsdp, tensor, tokens, tile_weights, cotangent, tile_list, tile_counts):
    z, t = lax.axis_index("fsdp"), lax.axis_index("tensor")
    half = z % PAIR
    size, stripes = tile_weights.shape[0], tile_weights.shape[1]
    share = stripes // PAIR
    groups = [[(p * PAIR + a) * tensor + b for a in range(PAIR) for b in range(tensor)] for p in range(fsdp // PAIR)]
    direct = fsdp <= DIRECT

    def swap(value, dz, dt):
        pairs = [(a * tensor + b, (a ^ dz) * tensor + (b ^ dt)) for a in range(fsdp) for b in range(tensor)]
        return lax.ppermute(value, ("fsdp", "tensor"), pairs)

    def spread(value):
        return lax.all_to_all(value, ("fsdp", "tensor"), split_axis=0, concat_axis=0, axis_index_groups=groups, tiled=True)

    by_stripe = jnp.transpose(tile_weights, (1, 0, 2))
    if direct:
        same = lax.dynamic_slice_in_dim(by_stripe, half * share, share, 0)
        other = lax.dynamic_slice_in_dim(by_stripe, (1 - half) * share, share, 0)
        weights = [same] + [swap(other if k % PAIR else same, k, 0) for k in range(1, fsdp)]
        places = jnp.stack([(z ^ k) * size for k in range(fsdp)]).astype(jnp.int32)
    else:
        outgoing = jnp.tile(by_stripe.reshape(PAIR, share, size, TILE), (fsdp // PAIR, 1, 1, 1))
        arrived = lax.all_to_all(outgoing, "fsdp", split_axis=0, concat_axis=0, tiled=True)
        weights = [arrived.transpose(1, 0, 2, 3).reshape(share, fsdp * size, TILE)]
        places = jnp.zeros((1,), jnp.int32)

    steps = [(0, 0), (1, 0)]
    near = jnp.concatenate([tokens, swap(tokens, 1, 0)], axis=0)
    bit = tensor // 2
    while bit:
        steps = steps + [(a, b ^ bit) for a, b in steps]
        far = swap(near, 0, bit)
        if bit > 1:
            near = jnp.concatenate([near, far], axis=0)
        bit //= 2
    order = jnp.stack([(half ^ a) * tensor + (t ^ b) for a, b in steps]).astype(jnp.int32)

    incoming = spread(cut_call(tensor, cotangent))
    tiles = lax.dynamic_slice_in_dim(tile_list, half * share, share, 0)
    counts = lax.dynamic_slice_in_dim(tile_counts, half * share, share, 0)
    hidden, *grads = stripe_call(tiles, counts, order, places, near, far, incoming, weights)

    activations = join_call(tensor, spread(hidden))
    if direct:
        grads = [grads[0]] + [swap(grads[k], k, 0) for k in range(1, fsdp)]
        total = sum_call(half.reshape(1).astype(jnp.int32), grads)
    else:
        split = grads[0].reshape(share, fsdp, size, TILE).transpose(1, 0, 2, 3)
        mine = lax.dynamic_index_in_dim(split, z, 0)
        arrived = lax.all_to_all(split.astype(jnp.bfloat16), "fsdp", split_axis=0, concat_axis=0, tiled=True)
        here = (jnp.arange(fsdp) == z)[:, None, None, None]
        total = jnp.where(here, mine, arrived.astype(jnp.float32))
        total = jnp.sum(total.reshape(fsdp // PAIR, PAIR, share, size, TILE), axis=0)
    return activations, total.reshape(stripes, size, TILE).transpose(1, 0, 2)


def solution(mesh):
    return jax.shard_map(
        functools.partial(body, mesh.shape["fsdp"], mesh.shape["tensor"]),
        mesh=mesh,
        in_specs=(
            P(("member", "fsdp", "tensor"), None),
            P(("member", "fsdp"), "tensor", None),
            P(("member", "fsdp", "tensor"), None),
            P("tensor", None),
            P("tensor"),
        ),
        out_specs=(P(("member", "fsdp", "tensor"), None), P(("member", "fsdp"), "tensor", None)),
        check_vma=False,
    )
```

time: 105 us -> 93.3 us (0.89)
  blocking collectives: 13.3 us -> 0 us
  other arithmetic: 5.67 us -> 0.1 us
  starting transfers between devices: 16.4 us -> 21.3 us
  Pallas kernels: 5.92 us -> 8.88 us
  local copies, waits for them, and re-layouts: 6.31 us -> 4.97 us
    ppermute x3 -> x9, waiting for transfers between devices: 16 us -> 56.9 us  [swap(): return lax.ppermute(value, ('fsdp', 'tensor'), pairs)]
    all_to_all x3 -> x2, waiting for transfers between devices: 39.9 us -> 0.01 us  [spread(): lax.all_to_all(value, ('fsdp', 'tensor'), split_axis=0, concat_axis=0, ax...]
    all_to_all x1 -> x0, blocking collectives: 13.3 us -> none  [body(): lax.all_to_all(hidden, ('fsdp', 'tensor'), split_axis=0, concat_axis=0, a...]
    ppermute x3 -> x9, starting transfers between devices: 3.62 us -> 14 us  [swap(): return lax.ppermute(value, ('fsdp', 'tensor'), pairs)]
    all_to_all x3 -> x2, starting transfers between devices: 12.7 us -> 7.36 us  [spread(): lax.all_to_all(value, ('fsdp', 'tensor'), split_axis=0, concat_axis=0, ax...]
    reshape x3 -> x0, local copies, waits for them, and re-layouts: 3.88 us -> none  [the longest x2 2.55 us: body(): cotangent.reshape(rows, tensor, PAIR, width).transpose(2, 1, 0, 3)]
    unnamed x13 -> x25, local copies, waits for them, and re-layouts: 0.43 us -> 3.98 us
    pallas_call x1 -> x4, Pallas kernels: 5.92 us -> 8.88 us  [the longest x1 5.56 us: stripe_call(): pl.pallas_call(functools.partial(stripe_kernel, parts, step), out_shape=[...]
  transfers between devices with their start and end apart: 6 -> 11, of which waited for: 5 -> 6; matrix products, arithmetic and copies ran while one was open for 5% -> 1% of each run, Pallas kernels for 0% -> 3%
where the time goes in v3:
time: 93.3 us; the launch traced here: 92.9 us
  waiting for transfers between devices  56.9 us (61%)
  starting transfers between devices  21.3 us (23%)
  Pallas kernels  8.88 us (10%)
  local copies, waits for them, and re-layouts  4.97 us (5%)
    ppermute x9, waiting for transfers between devices, swap(): return lax.ppermute(value, ('fsdp', 'tensor'), pairs)  56.9 us
    ppermute x9, starting transfers between devices, swap(): return lax.ppermute(value, ('fsdp', 'tensor'), pairs)  14 us
    all_to_all x2, starting transfers between devices, spread(): lax.all_to_all(value, ('fsdp', 'tensor'), split_axis=0, concat_axis=0, ax...  7.36 us
    pallas_call x1, Pallas kernels, stripe_call(): pl.pallas_call(functools.partial(stripe_kernel, parts, step), out_shape=[...  5.56 us
    unnamed x25, local copies, waits for them, and re-layouts  3.98 us
  transfers between devices with their start and end apart: 11, of which 6 were waited for; matrix products, arithmetic and copies ran while one was open for 1% of the time, Pallas kernels for 3%

profile of v3, /device:TPU:0, one launch (start us, length us, event | category | flops | bytes accessed | tf_op | source)
XLA Modules:
  0.0 92.9 jit_solution(5911266134026206123)
XLA Ops:
  0.6 0.0 copy-start
  0.6 3.1 %collective-permute-start = (bf16[32,2560]{1,0:T(8,128)(2,1)}, bf16[32,2560]{1,0:T(8,128)(2,1)S(1)}, u32[]{:S(2)}, u32[]{:S(2)}) collective-permute-start(bf16[32,2560]{1,0:T(8,128)(2,1)} %param.5), channel_id=1, source_target_pairs={{0,4},{1,5},{2,6},{3,7},{4,0},{5,1},{6,2},{7,3},{8,12},{9,13},{10,... | collective-permute-start | bytes 491528 | tf_op jit(solution)/shard_map/ppermute | solution.py:177
  3.7 1.1 %copy-done.1 = bf16[32,10240]{1,0:T(8,128)(2,1)S(1)} copy-done((bf16[32,10240]{1,0:T(8,128)(2,1)S(1)}, bf16[32,10240]{1,0:T(8,128)(2,1)}, u32[]{:S(2)}) %copy-start.1) | copy-done | bytes 655384
  4.8 0.9 cut.1
  5.7 3.7 %all-to-all-start = ((bf16[8,32,1280]{2,1,0:T(8,128)(2,1)}), bf16[8,32,1280]{2,1,0:T(8,128)(2,1)S(1)}, u32[]{:S(2)}, u32[]{:S(2)}) async-start(bf16[8,32,1280]{2,1,0:T(8,128)(2,1)} %cut.1), calls=%async_computation | async-start | bytes 1310720 | tf_op jit(solution)/shard_map/all_to_all | solution.py:180
  9.5 2.0 %collective-permute-start.1 = (bf16[64,2560]{1,0:T(8,128)(2,1)S(1)}, bf16[64,2560]{1,0:T(8,128)(2,1)S(1)}, u32[]{:S(2)}, u32[]{:S(2)}) collective-permute-start(bf16[64,2560]{1,0:T(8,128)(2,1)S(1)} %pad_maximum_fusion), channel_id=1, source_target_pairs={{0,2},{1,3},{2,0},{3,1},{4,6},{5,7},{6,4},{7,5},{8,10},{9,11},{10,... | collective-permute-start | bytes 983048 | tf_op jit(solution)/shard_map/ppermute | solution.py:177
  11.5 15.1 %collective-permute-done.1 = bf16[64,2560]{1,0:T(8,128)(2,1)S(1)} collective-permute-done((bf16[64,2560]{1,0:T(8,128)(2,1)S(1)}, bf16[64,2560]{1,0:T(8,128)(2,1)S(1)}, u32[]{:S(2)}, u32[]{:S(2)}) %collective-permute-start.1) | collective-permute-done | bytes 327712 | tf_op jit(solution)/shard_map/ppermute | solution.py:177
  26.6 0.1 collective-permute-start.2
  26.7 0.7 dynamic-slice_bitcast_fusion
  27.5 3.5 %collective-permute-start.5 = (bf16[10,96,128]{2,1,0:T(8,128)(2,1)}, bf16[10,96,128]{2,1,0:T(8,128)(2,1)S(1)}, u32[]{:S(2)}, u32[]{:S(2)}) collective-permute-start(bf16[10,96,128]{2,1,0:T(8,128)(2,1)} %get-tuple-element.12), channel_id=1, source_target_pairs={{0,12},{1,13},{2,14},{3,15},{4,8},{5,9},{6,10},{7,11},{8,4},{9,5},... | collective-permute-start | bytes 737288 | tf_op jit(solution)/shard_map/ppermute | solution.py:177
  31.0 0.9 collective-permute-start.4
  31.9 0.7 copy-done.10
  32.5 0.1 dynamic_slice.13.counts
  32.6 0.1 constant_dynamic-slice_fusion
  32.7 0.1 copy.8.tiles
  32.8 0.1 stack.50.order
  32.9 0.1 pad_add_fusion.places
  32.9 5.4 %collective-permute-done.5.rest_3_ = bf16[10,96,128]{2,1,0:T(8,128)(2,1)S(1)} collective-permute-done((bf16[10,96,128]{2,1,0:T(8,128)(2,1)}, bf16[10,96,128]{2,1,0:T(8,128)(2,1)S(1)}, u32[]{:S(2)}, u32[]{:S(2)}) %collective-permute-start.5) | collective-permute-done | bytes 245792 | tf_op jit(solution)/shard_map/ppermute | solution.py:177
  38.3 5.9 %collective-permute-done.3.rest_1_ = bf16[10,96,128]{2,1,0:T(8,128)(2,1)S(1)} collective-permute-done((bf16[10,96,128]{2,1,0:T(8,128)(2,1)}, bf16[10,96,128]{2,1,0:T(8,128)(2,1)S(1)}, u32[]{:S(2)}, u32[]{:S(2)}) %collective-permute-start.3) | collective-permute-done | bytes 245792 | tf_op jit(solution)/shard_map/ppermute | solution.py:177
  44.2 8.5 %collective-permute-done.4.rest_2_ = bf16[10,96,128]{2,1,0:T(8,128)(2,1)S(1)} collective-permute-done((bf16[10,96,128]{2,1,0:T(8,128)(2,1)S(1)}, bf16[10,96,128]{2,1,0:T(8,128)(2,1)S(1)}, u32[]{:S(2)}, u32[]{:S(2)}) %collective-permute-start.4) | collective-permute-done | bytes 245792 | tf_op jit(solution)/shard_map/ppermute | solution.py:177
  52.7 5.6 %stripes.1 = (bf16[8,32,1280]{2,1,0:T(8,128)(2,1)}, f32[10,96,128]{2,1,0:T(8,128)S(1)}, bf16[10,96,128]{2,1,0:T(8,128)(2,1)S(1)}, bf16[10,96,128]{2,1,0:T(8,128)(2,1)S(1)}, bf16[10,96,128]{2,1,0:T(8,128)(2,1)S(1)}) custom-call(s32[10,3]{1,0:T(8,128)S(1)} %copy.8.tiles, s32[10]{0:T(128)S(1)} %dynamic_slice.13.counts, s32[8]{0:T(128)S(1)} %stack.50.order, ...), custom_call_target="tpu_custom_call" | custom-call | tf_op jit(solution)/shard_map/stripes/pallas_call | solution.py:115
  58.3 0.7 copy-done.2
  59.0 0.7 copy-done.4
  59.7 0.7 copy-done.6
  60.4 3.7 %all-to-all-start.1 = ((bf16[8,32,1280]{2,1,0:T(8,128)(2,1)}), bf16[8,32,1280]{2,1,0:T(8,128)(2,1)S(1)}, u32[]{:S(2)}, u32[]{:S(2)}) async-start(bf16[8,32,1280]{2,1,0:T(8,128)(2,1)} %get-tuple-element.7), calls=%async_computation.1 | async-start | bytes 1310720 | tf_op jit(solution)/shard_map/all_to_all | solution.py:180
  64.1 1.9 %collective-permute-start.6 = (bf16[10,96,128]{2,1,0:T(8,128)(2,1)S(1)}, bf16[10,96,128]{2,1,0:T(8,128)(2,1)S(1)}, u32[]{:S(2)}, u32[]{:S(2)}) collective-permute-start(bf16[10,96,128]{2,1,0:T(8,128)(2,1)S(1)} %copy-done.7), channel_id=1, source_target_pairs={{0,4},{1,5},{2,6},{3,7},{4,0},{5,1},{6,2},{7,3},{8,12},{9,13},{10,... | collective-permute-start | bytes 737288 | tf_op jit(solution)/shard_map/ppermute | solution.py:177
  66.0 1.2 %collective-permute-start.7 = (bf16[10,96,128]{2,1,0:T(8,128)(2,1)S(1)}, bf16[10,96,128]{2,1,0:T(8,128)(2,1)S(1)}, u32[]{:S(2)}, u32[]{:S(2)}) collective-permute-start(bf16[10,96,128]{2,1,0:T(8,128)(2,1)S(1)} %copy-done.5), channel_id=1, source_target_pairs={{0,8},{1,9},{2,10},{3,11},{4,12},{5,13},{6,14},{7,15},{8,0},{9,1},... | collective-permute-start | bytes 737288 | tf_op jit(solution)/shard_map/ppermute | solution.py:177
  67.2 1.3 %collective-permute-start.8 = (bf16[10,96,128]{2,1,0:T(8,128)(2,1)S(1)}, bf16[10,96,128]{2,1,0:T(8,128)(2,1)S(1)}, u32[]{:S(2)}, u32[]{:S(2)}) collective-permute-start(bf16[10,96,128]{2,1,0:T(8,128)(2,1)S(1)} %copy-done.3), channel_id=1, source_target_pairs={{0,12},{1,13},{2,14},{3,15},{4,8},{5,9},{6,10},{7,11},{8,4},{9,5},... | collective-permute-start | bytes 737288 | tf_op jit(solution)/shard_map/ppermute | solution.py:177
  68.5 16.4 %collective-permute-done.6.rest_1_ = bf16[10,96,128]{2,1,0:T(8,128)(2,1)S(1)} collective-permute-done((bf16[10,96,128]{2,1,0:T(8,128)(2,1)S(1)}, bf16[10,96,128]{2,1,0:T(8,128)(2,1)S(1)}, u32[]{:S(2)}, u32[]{:S(2)}) %collective-permute-start.6) | collective-permute-done | bytes 245792 | tf_op jit(solution)/shard_map/ppermute | solution.py:177
  85.0 5.5 %collective-permute-done.8.rest_3_ = bf16[10,96,128]{2,1,0:T(8,128)(2,1)S(1)} collective-permute-done((bf16[10,96,128]{2,1,0:T(8,128)(2,1)S(1)}, bf16[10,96,128]{2,1,0:T(8,128)(2,1)S(1)}, u32[]{:S(2)}, u32[]{:S(2)}) %collective-permute-start.8) | collective-permute-done | bytes 245792 | tf_op jit(solution)/shard_map/ppermute | solution.py:177
  90.5 1.5 %sum.1 = f32[2,10,96,128]{3,2,1,0:T(8,128)} custom-call(s32[1]{0:T(128)} %bitcast.14.half, f32[10,96,128]{2,1,0:T(8,128)S(1)} %get-tuple-element.8.rest_0_, bf16[10,96,128]{2,1,0:T(8,128)(2,1)S(1)} %collective-permute-done.6.rest_1_, bf16[10,96,128]{2,1,0:T(8,128)(2,1)S(1)} %collective-permute-done.7.rest_2_, ...), custom_call_target="tpu_custom_call" | custom-call | tf_op jit(solution)/shard_map/sum/pallas_call | solution.py:153
  92.0 0.9 join.1
  (26 shorter events, 0.1 us)
Async XLA Ops:
  0.6 32.0 %copy-start = (s32[20,3]{0,1:T(4,128)S(1)}, s32[20,3]{0,1:T(4,128)}, u32[]{:S(2)}) copy-start(s32[20,3]{0,1:T(4,128)} %param.8) | copy-start | bytes 724
  0.6 8.8 %collective-permute-start = (bf16[32,2560]{1,0:T(8,128)(2,1)}, bf16[32,2560]{1,0:T(8,128)(2,1)S(1)}, u32[]{:S(2)}, u32[]{:S(2)}) collective-permute-start(bf16[32,2560]{1,0:T(8,128)(2,1)} %param.5), channel_id=1, source_target_pairs={{0,4},{1,5},{2,6},{3,7},{4,0},{5,1},{6,2},{7,3},{8,12},{9,13},{10,... | collective-permute-start | bytes 491528 | tf_op jit(solution)/shard_map/ppermute | solution.py:177
  3.7 1.1 %copy-start.1 = (bf16[32,10240]{1,0:T(8,128)(2,1)S(1)}, bf16[32,10240]{1,0:T(8,128)(2,1)}, u32[]{:S(2)}) copy-start(bf16[32,10240]{1,0:T(8,128)(2,1)} %whole.1) | copy-start | bytes 1966084
  5.7 3.7 %copy-start.8 = (bf16[32,2560]{1,0:T(8,128)(2,1)S(1)}, bf16[32,2560]{1,0:T(8,128)(2,1)}, u32[]{:S(2)}) copy-start(bf16[32,2560]{1,0:T(8,128)(2,1)} %param.5) | copy-start | bytes 491524
  5.7 47.0 %all-to-all-start = ((bf16[8,32,1280]{2,1,0:T(8,128)(2,1)}), bf16[8,32,1280]{2,1,0:T(8,128)(2,1)S(1)}, u32[]{:S(2)}, u32[]{:S(2)}) async-start(bf16[8,32,1280]{2,1,0:T(8,128)(2,1)} %cut.1), calls=%async_computation | async-start | bytes 1310720 | tf_op jit(solution)/shard_map/all_to_all | solution.py:180
  9.5 17.2 %copy-start.9 = (bf16[96,20,128]{2,0,1:T(8,128)(2,1)S(1)}, bf16[96,20,128]{2,0,1:T(8,128)(2,1)}, u32[]{:S(2)}) copy-start(bf16[96,20,128]{2,0,1:T(8,128)(2,1)} %param.6) | copy-start | bytes 1474564
  9.5 17.1 %collective-permute-start.1 = (bf16[64,2560]{1,0:T(8,128)(2,1)S(1)}, bf16[64,2560]{1,0:T(8,128)(2,1)S(1)}, u32[]{:S(2)}, u32[]{:S(2)}) collective-permute-start(bf16[64,2560]{1,0:T(8,128)(2,1)S(1)} %pad_maximum_fusion), channel_id=1, source_target_pairs={{0,2},{1,3},{2,0},{3,1},{4,6},{5,7},{6,4},{7,5},{8,10},{9,11},{10,... | collective-permute-start | bytes 983048 | tf_op jit(solution)/shard_map/ppermute | solution.py:177
  26.6 26.1 %collective-permute-start.2 = (bf16[128,2560]{1,0:T(8,128)(2,1)S(1)}, bf16[128,2560]{1,0:T(8,128)(2,1)S(1)}, u32[]{:S(2)}, u32[]{:S(2)}) collective-permute-start(bf16[128,2560]{1,0:T(8,128)(2,1)S(1)} %constant_dynamic-update-slice_fusion.near), channel_id=1, source_target_pairs={{0,1},{1,0},{2,3},{3,2},{4,5},{5,4},{6,7},{7,6},{8,9},{9,8},{10,11... | collective-permute-start | bytes 1966088 | tf_op jit(solution)/shard_map/ppermute | solution.py:177
  27.5 10.9 %collective-permute-start.5 = (bf16[10,96,128]{2,1,0:T(8,128)(2,1)}, bf16[10,96,128]{2,1,0:T(8,128)(2,1)S(1)}, u32[]{:S(2)}, u32[]{:S(2)}) collective-permute-start(bf16[10,96,128]{2,1,0:T(8,128)(2,1)} %get-tuple-element.12), channel_id=1, source_target_pairs={{0,12},{1,13},{2,14},{3,15},{4,8},{5,9},{6,10},{7,11},{8,4},{9,5},... | collective-permute-start | bytes 737288 | tf_op jit(solution)/shard_map/ppermute | solution.py:177
  31.0 13.2 %collective-permute-start.3 = (bf16[10,96,128]{2,1,0:T(8,128)(2,1)}, bf16[10,96,128]{2,1,0:T(8,128)(2,1)S(1)}, u32[]{:S(2)}, u32[]{:S(2)}) collective-permute-start(bf16[10,96,128]{2,1,0:T(8,128)(2,1)} %get-tuple-element.12), channel_id=1, source_target_pairs={{0,4},{1,5},{2,6},{3,7},{4,0},{5,1},{6,2},{7,3},{8,12},{9,13},{10,... | collective-permute-start | bytes 737288 | tf_op jit(solution)/shard_map/ppermute | solution.py:177
  31.0 21.7 %collective-permute-start.4 = (bf16[10,96,128]{2,1,0:T(8,128)(2,1)S(1)}, bf16[10,96,128]{2,1,0:T(8,128)(2,1)S(1)}, u32[]{:S(2)}, u32[]{:S(2)}) collective-permute-start(bf16[10,96,128]{2,1,0:T(8,128)(2,1)S(1)} %get-tuple-element.13.rest_0_), channel_id=1, source_target_pairs={{0,8},{1,9},{2,10},{3,11},{4,12},{5,13},{6,14},{7,15},{8,0},{9,1},... | collective-permute-start | bytes 737288 | tf_op jit(solution)/shard_map/ppermute | solution.py:177
  31.9 0.7 copy-start.10
  58.3 0.7 copy-start.2
  59.0 0.7 copy-start.4
  59.7 0.7 copy-start.6
  60.4 3.7 %copy-start.7 = (bf16[10,96,128]{2,1,0:T(8,128)(2,1)S(1)}, bf16[10,96,128]{2,1,0:T(8,128)(2,1)}, u32[]{:S(2)}) copy-start(bf16[10,96,128]{2,1,0:T(8,128)(2,1)} %copy-done.6) | copy-start | bytes 737284
  60.4 5.6 %copy-start.5 = (bf16[10,96,128]{2,1,0:T(8,128)(2,1)S(1)}, bf16[10,96,128]{2,1,0:T(8,128)(2,1)}, u32[]{:S(2)}) copy-start(bf16[10,96,128]{2,1,0:T(8,128)(2,1)} %copy-done.4) | copy-start | bytes 737284
  60.4 6.8 %copy-start.3 = (bf16[10,96,128]{2,1,0:T(8,128)(2,1)S(1)}, bf16[10,96,128]{2,1,0:T(8,128)(2,1)}, u32[]{:S(2)}) copy-start(bf16[10,96,128]{2,1,0:T(8,128)(2,1)} %copy-done.2) | copy-start | bytes 737284
  60.4 31.6 %all-to-all-start.1 = ((bf16[8,32,1280]{2,1,0:T(8,128)(2,1)}), bf16[8,32,1280]{2,1,0:T(8,128)(2,1)S(1)}, u32[]{:S(2)}, u32[]{:S(2)}) async-start(bf16[8,32,1280]{2,1,0:T(8,128)(2,1)} %get-tuple-element.7), calls=%async_computation.1 | async-start | bytes 1310720 | tf_op jit(solution)/shard_map/all_to_all | solution.py:180
  64.1 20.9 %collective-permute-start.6 = (bf16[10,96,128]{2,1,0:T(8,128)(2,1)S(1)}, bf16[10,96,128]{2,1,0:T(8,128)(2,1)S(1)}, u32[]{:S(2)}, u32[]{:S(2)}) collective-permute-start(bf16[10,96,128]{2,1,0:T(8,128)(2,1)S(1)} %copy-done.7), channel_id=1, source_target_pairs={{0,4},{1,5},{2,6},{3,7},{4,0},{5,1},{6,2},{7,3},{8,12},{9,13},{10,... | collective-permute-start | bytes 737288 | tf_op jit(solution)/shard_map/ppermute | solution.py:177
  66.0 18.9 %collective-permute-start.7 = (bf16[10,96,128]{2,1,0:T(8,128)(2,1)S(1)}, bf16[10,96,128]{2,1,0:T(8,128)(2,1)S(1)}, u32[]{:S(2)}, u32[]{:S(2)}) collective-permute-start(bf16[10,96,128]{2,1,0:T(8,128)(2,1)S(1)} %copy-done.5), channel_id=1, source_target_pairs={{0,8},{1,9},{2,10},{3,11},{4,12},{5,13},{6,14},{7,15},{8,0},{9,1},... | collective-permute-start | bytes 737288 | tf_op jit(solution)/shard_map/ppermute | solution.py:177
  67.2 23.3 %collective-permute-start.8 = (bf16[10,96,128]{2,1,0:T(8,128)(2,1)S(1)}, bf16[10,96,128]{2,1,0:T(8,128)(2,1)S(1)}, u32[]{:S(2)}, u32[]{:S(2)}) collective-permute-start(bf16[10,96,128]{2,1,0:T(8,128)(2,1)S(1)} %copy-done.3), channel_id=1, source_target_pairs={{0,12},{1,13},{2,14},{3,15},{4,8},{5,9},{6,10},{7,11},{8,4},{9,5},... | collective-permute-start | bytes 737288 | tf_op jit(solution)/shard_map/ppermute | solution.py:177

commit v4 on v3

v4 whole, which is shorter than its diff:
```python
import functools

import jax
import jax.numpy as jnp
from jax import lax
from jax.experimental import pallas as pl
from jax.experimental.pallas import tpu as pltpu
from jax.sharding import PartitionSpec as P

TILE = 128
SLOTS = 3
PAIR = 2
DIRECT = 8
ROOT = 0.7978845608028654
CUBIC = 0.044715
ANYWHERE = pl.BlockSpec(memory_space=pl.ANY)


def room(mib):
    return pltpu.CompilerParams(vmem_limit_bytes=mib * 2**20)


def gelu_and_derivative(v):
    square = v * v
    th = jnp.tanh(ROOT * (v + CUBIC * (square * v)))
    half = 0.5 * (1.0 + th)
    inner = ROOT * (1.0 + (3.0 * CUBIC) * square)
    return v * half, half + 0.5 * v * (1.0 - th * th) * inner


def join_kernel(picks, starts, *rest):
    arrays, whole, sems = rest[:-2], rest[-2], rest[-1]
    width = whole.shape[1] // len(picks)
    copies = []
    for i, (array, index) in enumerate(picks):
        column = pl.multiple_of(starts[i] * TILE, TILE)
        copies.append(pltpu.make_async_copy(arrays[array].at[index], whole.at[:, pl.ds(column, width)], sems.at[i]))
    for copy in copies:
        copy.start()
    for copy in copies:
        copy.wait()


def join_call(starts, arrays, picks):
    _, rows, width = arrays[0].shape
    return pl.pallas_call(
        functools.partial(join_kernel, picks),
        out_shape=jax.ShapeDtypeStruct((rows, len(picks) * width), arrays[0].dtype),
        in_specs=[pl.BlockSpec(memory_space=pltpu.SMEM)] + [ANYWHERE] * len(arrays),
        out_specs=ANYWHERE,
        scratch_shapes=[pltpu.SemaphoreType.DMA((len(picks),))],
        compiler_params=room(1),
        name="join",
    )(starts, *arrays)


def stripe_kernel(step, parts, tiles, counts, places, near, far, back_home, back_away, weights, *rest):
    home, away, grads, term = rest[0], rest[1], rest[2:2 + parts], rest[2 + parts]
    blocks, rows = back_home.shape[0], back_home.shape[1]
    size = grads[0].shape[1]
    spans = [pl.ds(pl.multiple_of(places[p], size), size) for p in range(parts)]
    for i in range(step):
        s = pl.program_id(0) * step + i
        cols = slice(i * TILE, (i + 1) * TILE)
        picked = []
        for k in range(SLOTS):
            column = pl.multiple_of(tiles[s, k] * TILE, TILE)
            block = jnp.concatenate([near[:, pl.ds(column, TILE)], far[:, pl.ds(column, TILE)]], axis=0)
            picked.append(jnp.where(k < counts[s], block, jnp.zeros_like(block)))
        picked = jnp.concatenate(picked, axis=1)
        stack = jnp.concatenate([weights[f, i] for f in range(weights.shape[0])], axis=0)
        pre = jnp.dot(picked, stack, preferred_element_type=jnp.float32)
        act, slope = gelu_and_derivative(pre)
        back = jnp.concatenate([array[b, :, cols] for b in range(blocks) for array in (back_home, back_away)], axis=0)
        slope = (back.astype(jnp.float32) * slope).astype(jnp.bfloat16)
        act = act.astype(jnp.bfloat16)
        for b in range(blocks):
            home[b, :, cols] = act[(2 * b) * rows:(2 * b + 1) * rows]
            away[b, :, cols] = act[(2 * b + 1) * rows:(2 * b + 2) * rows]
        term[i] = lax.dot_general(picked, slope, (((0,), (0,)), ((), ())), preferred_element_type=jnp.float32)
        for p in range(parts):
            grads[p][i] = term[i, spans[p]].astype(grads[p].dtype)


def stripe_call(tiles, counts, places, near, far, back_home, back_away, weights):
    blocks, rows, width = back_home.shape
    shards, stripes, size, _ = weights.shape
    parts = places.shape[0]
    step = 2 if stripes % 2 == 0 else 1
    strip = pl.BlockSpec((blocks, rows, step * TILE), lambda s, *_: (0, 0, s))
    piece = pl.BlockSpec((step, SLOTS * TILE // parts, TILE), lambda s, *_: (s, 0, 0))
    whole = pl.BlockSpec(near.shape, lambda s, *_: (0, 0))
    term = (stripes, SLOTS * TILE // parts, TILE)
    return pl.pallas_call(
        functools.partial(stripe_kernel, step, parts),
        out_shape=[jax.ShapeDtypeStruct(back_home.shape, jnp.bfloat16)] * 2
        + [jax.ShapeDtypeStruct(term, jnp.bfloat16 if p else jnp.float32) for p in range(parts)],
        grid_spec=pltpu.PrefetchScalarGridSpec(
            num_scalar_prefetch=3,
            grid=(stripes // step,),
            in_specs=[whole, whole, strip, strip, pl.BlockSpec((shards, step, size, TILE), lambda s, *_: (0, s, 0, 0))],
            out_specs=[strip, strip] + [piece] * parts,
            scratch_shapes=[pltpu.VMEM((step, SLOTS * TILE, TILE), jnp.float32)],
        ),
        compiler_params=room(16),
        name="stripes",
    )(tiles, counts, places, near, far, back_home, back_away, weights)


def sum_kernel(half, *rest):
    grads, total = rest[:-1], rest[-1]
    for a in range(PAIR):

        @pl.when(pl.program_id(0) == a)
        def _():
            add = None
            for piece in grads[a::PAIR]:
                term = piece[...].astype(jnp.float32)
                add = term if add is None else add + term
            total[0] = add


def sum_call(half, grads):
    stripes, size, _ = grads[0].shape
    step = stripes // 2 if stripes % 2 == 0 else stripes
    chunks = stripes // step
    first = pl.BlockSpec((step, size, TILE), lambda a, c, half: (jnp.where(a == 0, c, chunks - 1), 0, 0))
    second = pl.BlockSpec((step, size, TILE), lambda a, c, half: (jnp.where(a == 0, 0, c), 0, 0))
    return pl.pallas_call(
        sum_kernel,
        out_shape=jax.ShapeDtypeStruct((PAIR, stripes, size, TILE), jnp.float32),
        grid_spec=pltpu.PrefetchScalarGridSpec(
            num_scalar_prefetch=1,
            grid=(PAIR, chunks),
            in_specs=[second if p % PAIR else first for p in range(len(grads))],
            out_specs=pl.BlockSpec((1, step, size, TILE), lambda a, c, half: (half[0] ^ a, c, 0, 0)),
        ),
        compiler_params=room(16),
        name="sum",
    )(half, *grads)


def body(fsdp, tensor, tokens, tile_weights, cotangent, tile_list, tile_counts):
    z, t = lax.axis_index("fsdp"), lax.axis_index("tensor")
    half = z % PAIR
    rows = tokens.shape[0]
    size, stripes = tile_weights.shape[0], tile_weights.shape[1]
    share = stripes // PAIR
    width = share * TILE
    direct = fsdp <= DIRECT
    bits = [1 << i for i in reversed(range((tensor - 1).bit_length()))]

    def swap(value, dz, dt):
        pairs = [(a * tensor + b, (a ^ dz) * tensor + (b ^ dt)) for a in range(fsdp) for b in range(tensor)]
        return lax.ppermute(value, ("fsdp", "tensor"), pairs)

    def halves(value, second):
        extent = value.shape[-1] // 2
        return [lax.dynamic_slice_in_dim(value, (second ^ a) * extent, extent, value.ndim - 1) for a in range(2)]

    by_stripe = jnp.transpose(tile_weights, (1, 0, 2))
    outgoing = jnp.tile(by_stripe.reshape(PAIR, share, size, TILE), (fsdp // PAIR, 1, 1, 1))
    weights = lax.all_to_all(outgoing, "fsdp", split_axis=0, concat_axis=0, tiled=True)
    if direct:
        places = jnp.stack([(z ^ k) * size for k in range(fsdp)]).astype(jnp.int32)
    else:
        weights = weights.transpose(1, 0, 2, 3).reshape(1, share, fsdp * size, TILE)
        places = jnp.zeros((1,), jnp.int32)

    order = [0]
    near = jnp.concatenate([tokens, swap(tokens, 1, 0)], axis=0)
    back = cotangent[None]
    for bit in bits:
        order = order + [b ^ bit for b in order]
        far = swap(near, 0, bit)
        if bit > 1:
            near = jnp.concatenate([near, far], axis=0)
        keep, send = halves(back, (t // bit) % 2)
        back = jnp.concatenate([keep, swap(send, 0, bit)], axis=0)
    back_home, send = halves(back, half)
    back_away = swap(send, 1, 0)

    tiles = lax.dynamic_slice_in_dim(tile_list, half * share, share, 0)
    counts = lax.dynamic_slice_in_dim(tile_counts, half * share, share, 0)
    home, away, *grads = stripe_call(tiles, counts, places, near, far, back_home, back_away, weights)

    arrays = [home, swap(away, 1, 0)]
    parts = [(0, range(len(order))), (1, range(len(order)))]
    origins = [(0, 0), (1, 0)]
    for bit in reversed(bits):
        count = len(parts[0][1]) // 2
        send = jnp.concatenate([arrays[a][span[count]:span[count] + count] for a, span in parts], axis=0)
        arrays.append(swap(send, 0, bit))
        parts = [(a, span[:count]) for a, span in parts] + [(len(arrays) - 1, range(i * count, (i + 1) * count)) for i in range(len(parts))]
        origins = origins + [(a, b ^ bit) for a, b in origins]
    starts = jnp.stack([(t ^ b) * stripes + (half ^ a) * share for a, b in origins]).astype(jnp.int32)
    activations = join_call(starts, arrays, [(a, span[0]) for a, span in parts])

    if direct:
        grads = [grads[0]] + [swap(grads[k], k, 0) for k in range(1, fsdp)]
        total = sum_call(half.reshape(1).astype(jnp.int32), grads)
    else:
        split = grads[0].reshape(share, fsdp, size, TILE).transpose(1, 0, 2, 3)
        mine = lax.dynamic_index_in_dim(split, z, 0)
        arrived = lax.all_to_all(split.astype(jnp.bfloat16), "fsdp", split_axis=0, concat_axis=0, tiled=True)
        here = (jnp.arange(fsdp) == z)[:, None, None, None]
        total = jnp.where(here, mine, arrived.astype(jnp.float32))
        total = jnp.sum(total.reshape(fsdp // PAIR, PAIR, share, size, TILE), axis=0)
    return activations, total.reshape(stripes, size, TILE).transpose(1, 0, 2)


def solution(mesh):
    return jax.shard_map(
        functools.partial(body, mesh.shape["fsdp"], mesh.shape["tensor"]),
        mesh=mesh,
        in_specs=(
            P(("member", "fsdp", "tensor"), None),
            P(("member", "fsdp"), "tensor", None),
            P(("member", "fsdp", "tensor"), None),
            P("tensor", None),
            P("tensor"),
        ),
        out_specs=(P(("member", "fsdp", "tensor"), None), P(("member", "fsdp"), "tensor", None)),
        check_vma=False,
    )
```

time: 93.3 us -> 83.5 us (0.89)
  the two profiles are of different devices: /device:TPU:0 before, /device:TPU:8 now
where the time goes in v4:
time: 83.5 us; the launch traced here: 83.3 us
  waiting for transfers between devices  49 us (59%)
  starting transfers between devices  16.9 us (20%)
  Pallas kernels  8.85 us (11%)
  local copies, waits for them, and re-layouts  6.35 us (8%)
  other arithmetic  1.27 us (2%)
  between operations  0.88 us (1%)
    ppermute x12, waiting for transfers between devices, swap(): return lax.ppermute(value, ('fsdp', 'tensor'), pairs)  49 us
    ppermute x12, starting transfers between devices, swap(): return lax.ppermute(value, ('fsdp', 'tensor'), pairs)  11.3 us
    pallas_call x1, Pallas kernels, stripe_call(): pl.pallas_call(functools.partial(stripe_kernel, step, parts), out_shape=[...  5.88 us
    all_to_all x1, starting transfers between devices, body(): lax.all_to_all(outgoing, 'fsdp', split_axis=0, concat_axis=0, tiled=True)  5.56 us
    unnamed x21, local copies, waits for them, and re-layouts  3.78 us
  transfers between devices with their start and end apart: 13, of which 8 were waited for; matrix products, arithmetic and copies ran while one was open for 5% of the time, Pallas kernels for 2%

profile of v4, /device:TPU:8, one launch (start us, length us, event | category | flops | bytes accessed | tf_op | source)
XLA Modules:
  0.0 83.3 jit_solution(3650005034192412299)
XLA Ops:
  0.8 1.2 %dynamic-slice_bitcast_fusion = (bf16[1,32,5120]{2,1,0:T(8,128)(2,1)S(1)}, bf16[1,32,5120]{2,1,0:T(8,128)(2,1)S(1)}) fusion(bf16[32,10240]{1,0:T(8,128)(2,1)} %param.7, s32[]{:T(128)S(6)} %select_n.47, s32[]{:T(128)S(6)} %select_n.46), kind=kLoop, calls=%fused_computation.15 | loop fusion | bytes 1310728 | tf_op jit(solution)/shard_map/dynamic_slice | solution.py:159
  2.0 1.9 %collective-permute-start.3 = (bf16[1,32,5120]{2,1,0:T(8,128)(2,1)S(1)}, bf16[1,32,5120]{2,1,0:T(8,128)(2,1)S(1)}, u32[]{:S(2)}, u32[]{:S(2)}) collective-permute-start(bf16[1,32,5120]{2,1,0:T(8,128)(2,1)S(1)} %get-tuple-element.18), channel_id=1, source_target_pairs={{0,2},{1,3},{2,0},{3,1},{4,6},{5,7},{6,4},{7,5},{8,10},{9,11},{10,... | collective-permute-start | bytes 983048 | tf_op jit(solution)/shard_map/ppermute | solution.py:155
  3.9 1.1 %tile.11 = bf16[2,2,10,96,128]{4,3,2,1,0:T(8,128)(2,1)} broadcast(bf16[2,10,96,128]{3,2,1,0:T(8,128)(2,1)S(1)} %bitcast.25), dimensions={1,2,3,4} | broadcast | bytes 1474560 | tf_op jit(solution)/shard_map/tile | solution.py:162
  5.0 5.6 %all-to-all-start = ((bf16[4,10,96,128]{3,2,1,0:T(8,128)(2,1)}), bf16[4,10,96,128]{3,2,1,0:T(8,128)(2,1)S(1)}, u32[]{:S(2)}, u32[]{:S(2)}) async-start(bf16[4,10,96,128]{3,2,1,0:T(8,128)(2,1)} %bitcast.16), calls=%async_computation | async-start | bytes 1966080 | tf_op jit(solution)/shard_map/all_to_all | solution.py:163
  10.6 0.6 collective-permute-start.1
  11.2 0.2 collective-permute-done.3
  11.6 7.4 %collective-permute-done.1 = bf16[64,2560]{1,0:T(8,128)(2,1)S(1)} collective-permute-done((bf16[64,2560]{1,0:T(8,128)(2,1)S(1)}, bf16[64,2560]{1,0:T(8,128)(2,1)S(1)}, u32[]{:S(2)}, u32[]{:S(2)}) %collective-permute-start.1) | collective-permute-done | bytes 327712 | tf_op jit(solution)/shard_map/ppermute | solution.py:155
  19.2 0.7 copy-done.7
  19.9 1.1 %fusion = (bf16[4,32,1280]{2,1,0:T(8,128)(2,1)S(1)}, bf16[4,32,1280]{2,1,0:T(8,128)(2,1)S(1)}) fusion(s32[]{:T(128)S(6)} %select_n.52, bf16[2,32,2560]{2,1,0:T(8,128)(2,1)S(1)} %get-tuple-element.17, bf16[2,32,2560]{2,1,0:T(8,128)(2,1)} %copy-done.7, s32[]{:T(128)S(6)} %select_n.51), kind=kLoop, calls=%fused_computation.8 | loop fusion | flops 1310720 | bytes 1310728 | tf_op jit(solution)/shard_map/concatenate | solution.py:179
  21.0 1.2 %collective-permute-start.5 = (bf16[4,32,1280]{2,1,0:T(8,128)(2,1)S(1)}, bf16[4,32,1280]{2,1,0:T(8,128)(2,1)S(1)}, u32[]{:S(2)}, u32[]{:S(2)}) collective-permute-start(bf16[4,32,1280]{2,1,0:T(8,128)(2,1)S(1)} %get-tuple-element.14), channel_id=1, source_target_pairs={{0,4},{1,5},{2,6},{3,7},{4,0},{5,1},{6,2},{7,3},{8,12},{9,13},{10,... | collective-permute-start | bytes 983048 | tf_op jit(solution)/shard_map/ppermute | solution.py:155
  22.2 0.7 copy-done.8
  22.8 0.1 dynamic_slice.25.counts
  23.0 0.1 copy.8.tiles
  23.1 0.1 pad_add_fusion.places
  23.1 11.3 %collective-permute-done.5.back_away = bf16[4,32,1280]{2,1,0:T(8,128)(2,1)S(1)} collective-permute-done((bf16[4,32,1280]{2,1,0:T(8,128)(2,1)S(1)}, bf16[4,32,1280]{2,1,0:T(8,128)(2,1)S(1)}, u32[]{:S(2)}, u32[]{:S(2)}) %collective-permute-start.5) | collective-permute-done | bytes 327712 | tf_op jit(solution)/shard_map/ppermute | solution.py:155
  34.4 0.7 copy-done.3
  35.1 1.0 %copy-done.4 = bf16[4,32,1280]{2,1,0:T(8,128)(2,1)S(1)} copy-done((bf16[4,32,1280]{2,1,0:T(8,128)(2,1)S(1)}, bf16[4,32,1280]{2,1,0:T(8,128)(2,1)}, u32[]{:S(2)}) %copy-start.4) | copy-done | bytes 327704
  36.1 5.9 %stripes.1 = (bf16[4,32,1280]{2,1,0:T(8,128)(2,1)S(1)}, bf16[4,32,1280]{2,1,0:T(8,128)(2,1)S(1)}, f32[10,96,128]{2,1,0:T(8,128)S(1)}, bf16[10,96,128]{2,1,0:T(8,...) custom-call(s32[10,3]{1,0:T(8,128)S(1)} %copy.8.tiles, s32[10]{0:T(128)S(1)} %dynamic_slice.25.counts, ...), custom_call_target="tpu_custom_call" | custom-call | tf_op jit(solution)/shard_map/stripes/pallas_call | solution.py:94
  42.0 2.5 %collective-permute-start.6 = (bf16[4,32,1280]{2,1,0:T(8,128)(2,1)S(1)}, bf16[4,32,1280]{2,1,0:T(8,128)(2,1)S(1)}, u32[]{:S(2)}, u32[]{:S(2)}) collective-permute-start(bf16[4,32,1280]{2,1,0:T(8,128)(2,1)S(1)} %get-tuple-element.9), channel_id=1, source_target_pairs={{0,4},{1,5},{2,6},{3,7},{4,0},{5,1},{6,2},{7,3},{8,12},{9,13},{10,... | collective-permute-start | bytes 983048 | tf_op jit(solution)/shard_map/ppermute | solution.py:155
  44.5 7.7 %collective-permute-done.6.rest_1_ = bf16[4,32,1280]{2,1,0:T(8,128)(2,1)S(1)} collective-permute-done((bf16[4,32,1280]{2,1,0:T(8,128)(2,1)S(1)}, bf16[4,32,1280]{2,1,0:T(8,128)(2,1)S(1)}, u32[]{:S(2)}, u32[]{:S(2)}) %collective-permute-start.6) | collective-permute-done | bytes 327712 | tf_op jit(solution)/shard_map/ppermute | solution.py:155
  52.3 0.6 copy-done.1
  52.9 1.0 %collective-permute-done.7.rest_2_ = bf16[4,32,1280]{2,1,0:T(8,128)(2,1)S(1)} collective-permute-done((bf16[4,32,1280]{2,1,0:T(8,128)(2,1)S(1)}, bf16[4,32,1280]{2,1,0:T(8,128)(2,1)S(1)}, u32[]{:S(2)}, u32[]{:S(2)}) %collective-permute-start.7) | collective-permute-done | bytes 327712 | tf_op jit(solution)/shard_map/ppermute | solution.py:155
  54.0 1.3 %collective-permute-start.8 = (bf16[4,32,1280]{2,1,0:T(8,128)(2,1)S(1)}, bf16[4,32,1280]{2,1,0:T(8,128)(2,1)S(1)}, u32[]{:S(2)}, u32[]{:S(2)}) collective-permute-start(bf16[4,32,1280]{2,1,0:T(8,128)(2,1)S(1)} %pad_maximum_fusion.2), channel_id=1, source_target_pairs={{0,2},{1,3},{2,0},{3,1},{4,6},{5,7},{6,4},{7,5},{8,10},{9,11},{10,... | collective-permute-start | bytes 983048 | tf_op jit(solution)/shard_map/ppermute | solution.py:155
  55.3 1.7 %collective-permute-start.9 = (bf16[10,96,128]{2,1,0:T(8,128)(2,1)}, bf16[10,96,128]{2,1,0:T(8,128)(2,1)S(1)}, u32[]{:S(2)}, u32[]{:S(2)}) collective-permute-start(bf16[10,96,128]{2,1,0:T(8,128)(2,1)} %get-tuple-element.11), channel_id=1, source_target_pairs={{0,4},{1,5},{2,6},{3,7},{4,0},{5,1},{6,2},{7,3},{8,12},{9,13},{10,... | collective-permute-start | bytes 737288 | tf_op jit(solution)/shard_map/ppermute | solution.py:155
  57.0 1.2 %collective-permute-start.10 = (bf16[10,96,128]{2,1,0:T(8,128)(2,1)}, bf16[10,96,128]{2,1,0:T(8,128)(2,1)S(1)}, u32[]{:S(2)}, u32[]{:S(2)}) collective-permute-start(bf16[10,96,128]{2,1,0:T(8,128)(2,1)} %get-tuple-element.12), channel_id=1, source_target_pairs={{0,8},{1,9},{2,10},{3,11},{4,12},{5,13},{6,14},{7,15},{8,0},{9,1},... | collective-permute-start | bytes 737288 | tf_op jit(solution)/shard_map/ppermute | solution.py:155
  58.3 0.5 collective-permute-start.11
  58.8 0.1 stack.50.starts
  58.9 8.2 %collective-permute-done.9.rest_1_ = bf16[10,96,128]{2,1,0:T(8,128)(2,1)S(1)} collective-permute-done((bf16[10,96,128]{2,1,0:T(8,128)(2,1)}, bf16[10,96,128]{2,1,0:T(8,128)(2,1)S(1)}, u32[]{:S(2)}, u32[]{:S(2)}) %collective-permute-start.9) | collective-permute-done | bytes 245792 | tf_op jit(solution)/shard_map/ppermute | solution.py:155
  67.1 8.4 %collective-permute-done.10.rest_2_ = bf16[10,96,128]{2,1,0:T(8,128)(2,1)S(1)} collective-permute-done((bf16[10,96,128]{2,1,0:T(8,128)(2,1)}, bf16[10,96,128]{2,1,0:T(8,128)(2,1)S(1)}, u32[]{:S(2)}, u32[]{:S(2)}) %collective-permute-start.10) | collective-permute-done | bytes 245792 | tf_op jit(solution)/shard_map/ppermute | solution.py:155
  75.5 4.8 %collective-permute-done.11.rest_3_ = bf16[10,96,128]{2,1,0:T(8,128)(2,1)S(1)} collective-permute-done((bf16[10,96,128]{2,1,0:T(8,128)(2,1)}, bf16[10,96,128]{2,1,0:T(8,128)(2,1)S(1)}, u32[]{:S(2)}, u32[]{:S(2)}) %collective-permute-start.11) | collective-permute-done | bytes 245792 | tf_op jit(solution)/shard_map/ppermute | solution.py:155
  80.3 1.5 %sum.1 = f32[2,10,96,128]{3,2,1,0:T(8,128)} custom-call(s32[1]{0:T(128)} %bitcast.17.half, f32[10,96,128]{2,1,0:T(8,128)S(1)} %get-tuple-element.10.rest_0_, bf16[10,96,128]{2,1,0:T(8,128)(2,1)S(1)} %collective-permute-done.9.rest_1_, bf16[10,96,128]{2,1,0:T(8,128)(2,1)S(1)} %collective-permute-done.10.rest_2_, ...), custom_call_target="tpu_custom_call" | custom-call | tf_op jit(solution)/shard_map/sum/pallas_call | solution.py:129
  81.8 1.4 %join.1 = bf16[32,10240]{1,0:T(8,128)(2,1)} custom-call(s32[8]{0:T(128)S(1)} %stack.50.starts, bf16[4,32,1280]{2,1,0:T(8,128)(2,1)S(1)} %get-tuple-element.8.rest_0_, bf16[4,32,1280]{2,1,0:T(8,128)(2,1)S(1)} %copy-done.2, bf16[4,32,1280]{2,1,0:T(8,128)(2,1)S(1)} %collective-permute-done.7.rest_2_, bf16[4,32,1280]{2,1,0:T(8,128)(2,1)S(1)} %collective-permute-done.8.rest_3_), custom_call_target="tpu_custom_call" | custom-call | tf_op jit(solution)/shard_map/join/pallas_call | solution.py:46
  (36 shorter events, 0.6 us)
Async XLA Ops:
  0.6 22.3 %copy-start = (s32[20,3]{0,1:T(4,128)S(1)}, s32[20,3]{0,1:T(4,128)}, u32[]{:S(2)}) copy-start(s32[20,3]{0,1:T(4,128)} %param.8) | copy-start | bytes 724
  0.6 9.9 %collective-permute-start = (bf16[32,2560]{1,0:T(8,128)(2,1)}, bf16[32,2560]{1,0:T(8,128)(2,1)S(1)}, u32[]{:S(2)}, u32[]{:S(2)}) collective-permute-start(bf16[32,2560]{1,0:T(8,128)(2,1)} %param.5), channel_id=1, source_target_pairs={{0,4},{1,5},{2,6},{3,7},{4,0},{5,1},{6,2},{7,3},{8,12},{9,13},{10,... | collective-permute-start | bytes 491528 | tf_op jit(solution)/shard_map/ppermute | solution.py:155
  0.8 3.1 %copy-start.6 = (bf16[96,20,128]{2,0,1:T(8,128)(2,1)S(1)}, bf16[96,20,128]{2,0,1:T(8,128)(2,1)}, u32[]{:S(2)}) copy-start(bf16[96,20,128]{2,0,1:T(8,128)(2,1)} %param.6) | copy-start | bytes 1474564
  2.0 9.5 %collective-permute-start.3 = (bf16[1,32,5120]{2,1,0:T(8,128)(2,1)S(1)}, bf16[1,32,5120]{2,1,0:T(8,128)(2,1)S(1)}, u32[]{:S(2)}, u32[]{:S(2)}) collective-permute-start(bf16[1,32,5120]{2,1,0:T(8,128)(2,1)S(1)} %get-tuple-element.18), channel_id=1, source_target_pairs={{0,2},{1,3},{2,0},{3,1},{4,6},{5,7},{6,4},{7,5},{8,10},{9,11},{10,... | collective-permute-start | bytes 983048 | tf_op jit(solution)/shard_map/ppermute | solution.py:155
  5.0 5.6 %copy-start.5 = (bf16[32,2560]{1,0:T(8,128)(2,1)S(1)}, bf16[32,2560]{1,0:T(8,128)(2,1)}, u32[]{:S(2)}) copy-start(bf16[32,2560]{1,0:T(8,128)(2,1)} %param.5) | copy-start | bytes 491524
  5.0 30.1 %all-to-all-start = ((bf16[4,10,96,128]{3,2,1,0:T(8,128)(2,1)}), bf16[4,10,96,128]{3,2,1,0:T(8,128)(2,1)S(1)}, u32[]{:S(2)}, u32[]{:S(2)}) async-start(bf16[4,10,96,128]{3,2,1,0:T(8,128)(2,1)} %bitcast.16), calls=%async_computation | async-start | bytes 1966080 | tf_op jit(solution)/shard_map/all_to_all | solution.py:163
  10.6 8.4 %collective-permute-start.1 = (bf16[64,2560]{1,0:T(8,128)(2,1)S(1)}, bf16[64,2560]{1,0:T(8,128)(2,1)S(1)}, u32[]{:S(2)}, u32[]{:S(2)}) collective-permute-start(bf16[64,2560]{1,0:T(8,128)(2,1)S(1)} %pad_maximum_fusion), channel_id=1, source_target_pairs={{0,2},{1,3},{2,0},{3,1},{4,6},{5,7},{6,4},{7,5},{8,10},{9,11},{10,... | collective-permute-start | bytes 983048 | tf_op jit(solution)/shard_map/ppermute | solution.py:155
  11.5 7.6 %collective-permute-start.4 = (bf16[2,32,2560]{2,1,0:T(8,128)(2,1)S(1)}, bf16[2,32,2560]{2,1,0:T(8,128)(2,1)S(1)}, u32[]{:S(2)}, u32[]{:S(2)}) collective-permute-start(bf16[2,32,2560]{2,1,0:T(8,128)(2,1)S(1)} %get-tuple-element.16), channel_id=1, source_target_pairs={{0,1},{1,0},{2,3},{3,2},{4,5},{5,4},{6,7},{7,6},{8,9},{9,8},{10,11... | collective-permute-start | bytes 983048 | tf_op jit(solution)/shard_map/ppermute | solution.py:155
  19.1 16.1 %collective-permute-start.2 = (bf16[128,2560]{1,0:T(8,128)(2,1)S(1)}, bf16[128,2560]{1,0:T(8,128)(2,1)S(1)}, u32[]{:S(2)}, u32[]{:S(2)}) collective-permute-start(bf16[128,2560]{1,0:T(8,128)(2,1)S(1)} %constant_dynamic-update-slice_fusion.near), channel_id=1, source_target_pairs={{0,1},{1,0},{2,3},{3,2},{4,5},{5,4},{6,7},{7,6},{8,9},{9,8},{10,11... | collective-permute-start | bytes 1966088 | tf_op jit(solution)/shard_map/ppermute | solution.py:155
  19.2 0.7 copy-start.7
  21.0 13.4 %collective-permute-start.5 = (bf16[4,32,1280]{2,1,0:T(8,128)(2,1)S(1)}, bf16[4,32,1280]{2,1,0:T(8,128)(2,1)S(1)}, u32[]{:S(2)}, u32[]{:S(2)}) collective-permute-start(bf16[4,32,1280]{2,1,0:T(8,128)(2,1)S(1)} %get-tuple-element.14), channel_id=1, source_target_pairs={{0,4},{1,5},{2,6},{3,7},{4,0},{5,1},{6,2},{7,3},{8,12},{9,13},{10,... | collective-permute-start | bytes 983048 | tf_op jit(solution)/shard_map/ppermute | solution.py:155
  22.2 0.7 copy-start.8
  34.4 0.7 copy-start.3
  35.1 1.0 %copy-start.4 = (bf16[4,32,1280]{2,1,0:T(8,128)(2,1)S(1)}, bf16[4,32,1280]{2,1,0:T(8,128)(2,1)}, u32[]{:S(2)}) copy-start(bf16[4,32,1280]{2,1,0:T(8,128)(2,1)} %copy-done.3) | copy-start | bytes 983044
  42.0 10.2 %collective-permute-start.6 = (bf16[4,32,1280]{2,1,0:T(8,128)(2,1)S(1)}, bf16[4,32,1280]{2,1,0:T(8,128)(2,1)S(1)}, u32[]{:S(2)}, u32[]{:S(2)}) collective-permute-start(bf16[4,32,1280]{2,1,0:T(8,128)(2,1)S(1)} %get-tuple-element.9), channel_id=1, source_target_pairs={{0,4},{1,5},{2,6},{3,7},{4,0},{5,1},{6,2},{7,3},{8,12},{9,13},{10,... | collective-permute-start | bytes 983048 | tf_op jit(solution)/shard_map/ppermute | solution.py:155
  52.1 0.7 copy-start.1
  52.2 1.7 %collective-permute-start.7 = (bf16[4,32,1280]{2,1,0:T(8,128)(2,1)S(1)}, bf16[4,32,1280]{2,1,0:T(8,128)(2,1)S(1)}, u32[]{:S(2)}, u32[]{:S(2)}) collective-permute-start(bf16[4,32,1280]{2,1,0:T(8,128)(2,1)S(1)} %pad_maximum_fusion.1), channel_id=1, source_target_pairs={{0,1},{1,0},{2,3},{3,2},{4,5},{5,4},{6,7},{7,6},{8,9},{9,8},{10,11... | collective-permute-start | bytes 983048 | tf_op jit(solution)/shard_map/ppermute | solution.py:155
  52.9 1.0 %slice-start = ((bf16[4,32,1280]{2,1,0:T(8,128)(2,1)}), bf16[1,32,1280]{2,1,0:T(8,128)(2,1)S(1)}, s32[]{:S(2)}) async-start(bf16[4,32,1280]{2,1,0:T(8,128)(2,1)} %copy-done.1), calls=%async_computation.1 | async-start | bytes 163840 | tf_op jit(solution)/shard_map/slice | solution.py:192
  54.0 27.9 %collective-permute-start.8 = (bf16[4,32,1280]{2,1,0:T(8,128)(2,1)S(1)}, bf16[4,32,1280]{2,1,0:T(8,128)(2,1)S(1)}, u32[]{:S(2)}, u32[]{:S(2)}) collective-permute-start(bf16[4,32,1280]{2,1,0:T(8,128)(2,1)S(1)} %pad_maximum_fusion.2), channel_id=1, source_target_pairs={{0,2},{1,3},{2,0},{3,1},{4,6},{5,7},{6,4},{7,5},{8,10},{9,11},{10,... | collective-permute-start | bytes 983048 | tf_op jit(solution)/shard_map/ppermute | solution.py:155
  55.3 11.8 %collective-permute-start.9 = (bf16[10,96,128]{2,1,0:T(8,128)(2,1)}, bf16[10,96,128]{2,1,0:T(8,128)(2,1)S(1)}, u32[]{:S(2)}, u32[]{:S(2)}) collective-permute-start(bf16[10,96,128]{2,1,0:T(8,128)(2,1)} %get-tuple-element.11), channel_id=1, source_target_pairs={{0,4},{1,5},{2,6},{3,7},{4,0},{5,1},{6,2},{7,3},{8,12},{9,13},{10,... | collective-permute-start | bytes 737288 | tf_op jit(solution)/shard_map/ppermute | solution.py:155
  57.0 18.5 %collective-permute-start.10 = (bf16[10,96,128]{2,1,0:T(8,128)(2,1)}, bf16[10,96,128]{2,1,0:T(8,128)(2,1)S(1)}, u32[]{:S(2)}, u32[]{:S(2)}) collective-permute-start(bf16[10,96,128]{2,1,0:T(8,128)(2,1)} %get-tuple-element.12), channel_id=1, source_target_pairs={{0,8},{1,9},{2,10},{3,11},{4,12},{5,13},{6,14},{7,15},{8,0},{9,1},... | collective-permute-start | bytes 737288 | tf_op jit(solution)/shard_map/ppermute | solution.py:155
  58.3 22.0 %collective-permute-start.11 = (bf16[10,96,128]{2,1,0:T(8,128)(2,1)}, bf16[10,96,128]{2,1,0:T(8,128)(2,1)S(1)}, u32[]{:S(2)}, u32[]{:S(2)}) collective-permute-start(bf16[10,96,128]{2,1,0:T(8,128)(2,1)} %get-tuple-element.13), channel_id=1, source_target_pairs={{0,12},{1,13},{2,14},{3,15},{4,8},{5,9},{6,10},{7,11},{8,4},{9,5},... | collective-permute-start | bytes 737288 | tf_op jit(solution)/shard_map/ppermute | solution.py:155
  80.3 1.5 %copy-start.2 = (bf16[4,32,1280]{2,1,0:T(8,128)(2,1)S(1)}, bf16[4,32,1280]{2,1,0:T(8,128)(2,1)}, u32[]{:S(2)}) copy-start(bf16[4,32,1280]{2,1,0:T(8,128)(2,1)} %copy-done.1) | copy-start | bytes 983044

commit v5 on v4

v5 whole, which is shorter than its diff:
```python
import functools

import jax
import jax.numpy as jnp
from jax import lax
from jax.experimental import pallas as pl
from jax.experimental.pallas import tpu as pltpu
from jax.sharding import PartitionSpec as P

TILE = 128
SLOTS = 3
PAIR = 2
DIRECT = 8
WEIGHT = 100 * 2**20
ROOT = 0.7978845608028654
CUBIC = 0.044715
ANYWHERE = pl.BlockSpec(memory_space=pl.ANY)


def room(mib):
    return pltpu.CompilerParams(vmem_limit_bytes=mib * 2**20)


def gelu_and_derivative(v):
    square = v * v
    th = jnp.tanh(ROOT * (v + CUBIC * (square * v)))
    half = 0.5 * (1.0 + th)
    inner = ROOT * (1.0 + (3.0 * CUBIC) * square)
    return v * half, half + 0.5 * v * (1.0 - th * th) * inner


def vmem(*arrays):
    return [pltpu.with_memory_space_constraint(array, pltpu.VMEM) for array in arrays]


def copy_all(copies):
    for copy in copies:
        copy.start()
    for copy in copies:
        copy.wait()


def cut_kernel(starts, whole, *rest):
    outs, sems = rest[:-1], rest[-1]
    count, _, width = outs[0].shape
    places = [(a, b, starts[a * count + b] * TILE) for a in range(PAIR) for b in range(count)]
    copy_all([
        pltpu.make_async_copy(whole.at[:, pl.ds(pl.multiple_of(column, TILE), width)], outs[a].at[b], sems.at[a * count + b])
        for a, b, column in places
    ])


def cut_call(starts, whole):
    count = starts.shape[0] // PAIR
    rows, width = whole.shape[0], whole.shape[1] // (PAIR * count)
    return pl.pallas_call(
        cut_kernel,
        out_shape=[jax.ShapeDtypeStruct((count, rows, width), whole.dtype)] * PAIR,
        in_specs=[pl.BlockSpec(memory_space=pltpu.SMEM), ANYWHERE],
        out_specs=[ANYWHERE] * PAIR,
        scratch_shapes=[pltpu.SemaphoreType.DMA((PAIR * count,))],
        compiler_params=room(1),
        name="cut",
    )(starts, whole)


def join_kernel(picks, starts, *rest):
    arrays, whole, sems = rest[:-2], rest[-2], rest[-1]
    width = whole.shape[1] // len(picks)
    copy_all([
        pltpu.make_async_copy(
            arrays[array].at[index], whole.at[:, pl.ds(pl.multiple_of(starts[i] * TILE, TILE), width)], sems.at[i]
        )
        for i, (array, index) in enumerate(picks)
    ])


def join_call(starts, arrays, picks):
    _, rows, width = arrays[0].shape
    return pl.pallas_call(
        functools.partial(join_kernel, picks),
        out_shape=jax.ShapeDtypeStruct((rows, len(picks) * width), arrays[0].dtype),
        in_specs=[pl.BlockSpec(memory_space=pltpu.SMEM)] + [ANYWHERE] * len(arrays),
        out_specs=ANYWHERE,
        scratch_shapes=[pltpu.SemaphoreType.DMA((len(picks),))],
        compiler_params=room(1),
        name="join",
    )(starts, *arrays)


def stripe_kernel(parts, picks, tiles, counts, places, near, far, weights, *rest):
    inputs = max(a for a, _ in picks) + 1
    arrays, (home, away), grads, term = rest[:inputs], rest[inputs:inputs + 2], rest[inputs + 2:-1], rest[-1]
    rows = arrays[0].shape[1]
    size = grads[0].shape[1]
    spans = [pl.ds(pl.multiple_of(places[p], size), size) for p in range(parts)]
    for s in range(weights.shape[1]):
        cols = slice(s * TILE, (s + 1) * TILE)
        picked = []
        for k in range(SLOTS):
            column = pl.multiple_of(tiles[s, k] * TILE, TILE)
            block = jnp.concatenate([near[:, pl.ds(column, TILE)], far[:, pl.ds(column, TILE)]], axis=0)
            picked.append(jnp.where(k < counts[s], block, jnp.zeros_like(block)))
        picked = jnp.concatenate(picked, axis=1)
        stack = jnp.concatenate([weights[f, s] for f in range(weights.shape[0])], axis=0)
        pre = jnp.dot(picked, stack, preferred_element_type=jnp.float32)
        act, slope = gelu_and_derivative(pre)
        back = jnp.concatenate([arrays[a][b, :, cols] for a, b in picks], axis=0)
        slope = (back.astype(jnp.float32) * slope).astype(jnp.bfloat16)
        act = act.astype(jnp.bfloat16)
        for b in range(len(picks) // 2):
            home[b, :, cols] = act[(2 * b) * rows:(2 * b + 1) * rows]
            away[b, :, cols] = act[(2 * b + 1) * rows:(2 * b + 2) * rows]
        term[s] = lax.dot_general(picked, slope, (((0,), (0,)), ((), ())), preferred_element_type=jnp.float32)
        for p in range(parts):
            grads[p][s] = term[s, spans[p]].astype(grads[p].dtype)


def stripe_call(tiles, counts, places, near, far, weights, arrays, picks):
    _, rows, width = arrays[0].shape
    stripes = weights.shape[1]
    parts = places.shape[0]
    blocks = len(picks)
    resident = pl.BlockSpec(memory_space=pltpu.VMEM)
    scalar = pl.BlockSpec(memory_space=pltpu.SMEM)
    term = (stripes, SLOTS * TILE // parts, TILE)
    return pl.pallas_call(
        functools.partial(stripe_kernel, parts, picks),
        out_shape=[pltpu.VMEM((blocks // 2, rows, width), jnp.bfloat16)] * 2
        + [pltpu.VMEM(term, jnp.bfloat16 if p else jnp.float32) for p in range(parts)],
        in_specs=[scalar] * 3 + [resident] * (3 + len(arrays)),
        out_specs=[resident] * (2 + parts),
        scratch_shapes=[pltpu.VMEM((stripes, SLOTS * TILE, TILE), jnp.float32)],
        compiler_params=room(24),
        name="stripes",
    )(tiles, counts, places, *vmem(near, far, weights, *arrays))


def sum_kernel(half, *rest):
    grads, total = rest[:-1], rest[-1]
    for a in range(PAIR):

        @pl.when(pl.program_id(0) == a)
        def _():
            add = None
            for piece in grads[a::PAIR]:
                term = piece[...].astype(jnp.float32)
                add = term if add is None else add + term
            total[0] = add


def sum_call(half, grads):
    stripes, size, _ = grads[0].shape
    step = stripes // 2 if stripes % 2 == 0 else stripes
    chunks = stripes // step
    first = pl.BlockSpec((step, size, TILE), lambda a, c, half: (jnp.where(a == 0, c, chunks - 1), 0, 0))
    second = pl.BlockSpec((step, size, TILE), lambda a, c, half: (jnp.where(a == 0, 0, c), 0, 0))
    return pl.pallas_call(
        sum_kernel,
        out_shape=jax.ShapeDtypeStruct((PAIR, stripes, size, TILE), jnp.float32),
        grid_spec=pltpu.PrefetchScalarGridSpec(
            num_scalar_prefetch=1,
            grid=(PAIR, chunks),
            in_specs=[second if p % PAIR else first for p in range(len(grads))],
            out_specs=pl.BlockSpec((1, step, size, TILE), lambda a, c, half: (half[0] ^ a, c, 0, 0)),
        ),
        compiler_params=room(16),
        cost_estimate=pl.CostEstimate(flops=0, bytes_accessed=WEIGHT, transcendentals=0),
        name="sum",
    )(half, *grads)


def body(fsdp, tensor, tokens, tile_weights, cotangent, tile_list, tile_counts):
    z, t = lax.axis_index("fsdp"), lax.axis_index("tensor")
    half = z % PAIR
    rows = tokens.shape[0]
    size, stripes = tile_weights.shape[0], tile_weights.shape[1]
    share = stripes // PAIR
    width = share * TILE
    direct = fsdp <= DIRECT
    bits = [1 << i for i in reversed(range((tensor - 1).bit_length()))]

    def swap(value, dz, dt):
        pairs = [(a * tensor + b, (a ^ dz) * tensor + (b ^ dt)) for a in range(fsdp) for b in range(tensor)]
        return lax.ppermute(value, ("fsdp", "tensor"), pairs)

    def exchange(arrays, spans, bit):
        count = len(spans[0][1]) // 2
        send = jnp.concatenate([arrays[a][span[count]:span[count] + count] for a, span in spans], axis=0)
        keep = [(a, span[:count]) for a, span in spans]
        new = [(len(arrays), range(i * count, (i + 1) * count)) for i in range(len(spans))]
        return arrays + [swap(send, 0, bit)], keep + new

    by_stripe = jnp.transpose(tile_weights, (1, 0, 2))
    outgoing = jnp.tile(by_stripe.reshape(PAIR, share, size, TILE), (fsdp // PAIR, 1, 1, 1))
    weights = lax.all_to_all(outgoing, "fsdp", split_axis=0, concat_axis=0, tiled=True)
    if direct:
        places = jnp.stack([(z ^ k) * size for k in range(fsdp)]).astype(jnp.int32)
    else:
        weights = weights.transpose(1, 0, 2, 3).reshape(1, share, fsdp * size, TILE)
        places = jnp.zeros((1,), jnp.int32)

    near = jnp.concatenate([tokens, swap(tokens, 1, 0)], axis=0)
    starts = jnp.stack([(t ^ b) * stripes + (half ^ a) * share for a in range(PAIR) for b in range(tensor)]).astype(jnp.int32)
    stay, leave = cut_call(starts, cotangent)
    arrays, spans = [stay, swap(leave, 1, 0)], [(0, range(tensor)), (1, range(tensor))]
    origins = [(0, 0), (1, 0)]
    for bit in bits:
        far = swap(near, 0, bit)
        if bit > 1:
            near = jnp.concatenate([near, far], axis=0)
        arrays, spans = exchange(arrays, spans, bit)
        origins = origins + [(a, b ^ bit) for a, b in origins]

    tiles = lax.dynamic_slice_in_dim(tile_list, half * share, share, 0)
    counts = lax.dynamic_slice_in_dim(tile_counts, half * share, share, 0)
    picks = [(a, span[0]) for a, span in spans]
    home, away, *grads = stripe_call(tiles, counts, places, near, far, weights, arrays, picks)

    arrays, spans = [home, swap(away, 1, 0)], [(0, range(tensor)), (1, range(tensor))]
    origins = [(0, 0), (1, 0)]
    for bit in reversed(bits):
        arrays, spans = exchange(arrays, spans, bit)
        origins = origins + [(a, b ^ bit) for a, b in origins]
    starts = jnp.stack([(t ^ b) * stripes + (half ^ a) * share for a, b in origins]).astype(jnp.int32)
    activations = join_call(starts, arrays, [(a, span[0]) for a, span in spans])

    if direct:
        grads = [grads[0]] + [swap(grads[k], k, 0) for k in range(1, fsdp)]
        total = sum_call(half.reshape(1).astype(jnp.int32), grads)
    else:
        split = grads[0].reshape(share, fsdp, size, TILE).transpose(1, 0, 2, 3)
        mine = lax.dynamic_index_in_dim(split, z, 0)
        arrived = lax.all_to_all(split.astype(jnp.bfloat16), "fsdp", split_axis=0, concat_axis=0, tiled=True)
        here = (jnp.arange(fsdp) == z)[:, None, None, None]
        total = jnp.where(here, mine, arrived.astype(jnp.float32))
        total = jnp.sum(total.reshape(fsdp // PAIR, PAIR, share, size, TILE), axis=0)
    return activations, total.reshape(stripes, size, TILE).transpose(1, 0, 2)


def solution(mesh):
    return jax.shard_map(
        functools.partial(body, mesh.shape["fsdp"], mesh.shape["tensor"]),
        mesh=mesh,
        in_specs=(
            P(("member", "fsdp", "tensor"), None),
            P(("member", "fsdp"), "tensor", None),
            P(("member", "fsdp", "tensor"), None),
            P("tensor", None),
            P("tensor"),
        ),
        out_specs=(P(("member", "fsdp", "tensor"), None), P(("member", "fsdp"), "tensor", None)),
        check_vma=False,
    )
```

time: 83.5 us -> 78.2 us (0.937)
  waiting for transfers between devices: 49 us -> 43.9 us
  starting transfers between devices: 16.9 us -> 19.2 us
  other arithmetic: 1.27 us -> 0.25 us
  Pallas kernels: 8.85 us -> 7.84 us
    ppermute x12, waiting for transfers between devices: 49 us -> 41.5 us  [swap(): return lax.ppermute(value, ('fsdp', 'tensor'), pairs)]
    ppermute x12, starting transfers between devices: 11.3 us -> 13.8 us  [swap(): return lax.ppermute(value, ('fsdp', 'tensor'), pairs)]
    all_to_all x1, waiting for transfers between devices: 0.01 us -> 2.43 us  [body(): lax.all_to_all(outgoing, 'fsdp', split_axis=0, concat_axis=0, tiled=True)]
    dynamic_slice x1 -> x0, local copies, waits for them, and re-layouts: 1.17 us -> none  [halves(): lax.dynamic_slice_in_dim(value, (second ^ a) * extent, extent, value.ndim...]
    concatenate x4, other arithmetic: 1.17 us -> 0.15 us  [exchange(): jnp.concatenate([arrays[a][span[count]:span[count] + count] for a, span i...]
    pallas_call x1 -> x2, Pallas kernels: 5.88 us -> 4.88 us  [the longest x1 4.03 us: stripe_call(): pl.pallas_call(functools.partial(stripe_kernel, parts, picks), out_shape=...]
    unnamed x21 -> x25, local copies, waits for them, and re-layouts: 3.78 us -> 4.19 us
  transfers between devices with their start and end apart: 13 -> 13, of which waited for: 8 -> 10; matrix products, arithmetic and copies ran while one was open for 5% -> 2% of each run, Pallas kernels for 2% -> 3%
where the time goes in v5:
time: 78.2 us; the launch traced here: 77.9 us
  waiting for transfers between devices  43.9 us (56%)
  starting transfers between devices  19.2 us (25%)
  Pallas kernels  7.84 us (10%)
  local copies, waits for them, and re-layouts  5.72 us (7%)
  between operations  0.89 us (1%)
    ppermute x12, waiting for transfers between devices, swap(): return lax.ppermute(value, ('fsdp', 'tensor'), pairs)  41.5 us
    ppermute x12, starting transfers between devices, swap(): return lax.ppermute(value, ('fsdp', 'tensor'), pairs)  13.8 us
    all_to_all x1, starting transfers between devices, body(): lax.all_to_all(outgoing, 'fsdp', split_axis=0, concat_axis=0, tiled=True)  5.45 us
    unnamed x25, local copies, waits for them, and re-layouts  4.19 us
    pallas_call x1, Pallas kernels, stripe_call(): pl.pallas_call(functools.partial(stripe_kernel, parts, picks), out_shape=...  4.03 us
    all_to_all x1, waiting for transfers between devices, body(): lax.all_to_all(outgoing, 'fsdp', split_axis=0, concat_axis=0, tiled=True)  2.43 us
  transfers between devices with their start and end apart: 13, of which 10 were waited for; matrix products, arithmetic and copies ran while one was open for 2% of the time, Pallas kernels for 3%

profile of v5, /device:TPU:8, one launch (start us, length us, event | category | flops | bytes accessed | tf_op | source)
XLA Modules:
  0.0 77.9 jit_solution(16934824791358948716)
XLA Ops:
  0.8 0.1 stack.67.starts
  0.8 1.1 %copy-done.5 = bf16[32,10240]{1,0:T(8,128)(2,1)S(1)} copy-done((bf16[32,10240]{1,0:T(8,128)(2,1)S(1)}, bf16[32,10240]{1,0:T(8,128)(2,1)}, u32[]{:S(2)}) %copy-start.5) | copy-done | bytes 655384
  1.9 0.8 %cut.1 = (bf16[4,32,1280]{2,1,0:T(8,128)(2,1)S(1)}, bf16[4,32,1280]{2,1,0:T(8,128)(2,1)S(1)}) custom-call(s32[8]{0:T(128)S(1)} %stack.67.starts, bf16[32,10240]{1,0:T(8,128)(2,1)S(1)} %copy-done.5), custom_call_target="tpu_custom_call" | custom-call | tf_op jit(solution)/shard_map/cut/pallas_call | solution.py:56
  2.8 2.0 %collective-permute-start.3 = (bf16[4,32,1280]{2,1,0:T(8,128)(2,1)S(1)}, bf16[4,32,1280]{2,1,0:T(8,128)(2,1)S(1)}, u32[]{:S(2)}, u32[]{:S(2)}) collective-permute-start(bf16[4,32,1280]{2,1,0:T(8,128)(2,1)S(1)} %get-tuple-element.11), channel_id=1, source_target_pairs={{0,4},{1,5},{2,6},{3,7},{4,0},{5,1},{6,2},{7,3},{8,12},{9,13},{10,... | collective-permute-start | bytes 983048 | tf_op jit(solution)/shard_map/ppermute | solution.py:185
  4.8 1.1 %tile.11 = bf16[2,2,10,96,128]{4,3,2,1,0:T(8,128)(2,1)} broadcast(bf16[2,10,96,128]{3,2,1,0:T(8,128)(2,1)S(1)} %bitcast.22), dimensions={1,2,3,4} | broadcast | bytes 1474560 | tf_op jit(solution)/shard_map/tile | solution.py:195
  5.9 5.4 %all-to-all-start = ((bf16[4,10,96,128]{3,2,1,0:T(8,128)(2,1)}), bf16[4,10,96,128]{3,2,1,0:T(8,128)(2,1)S(1)}, u32[]{:S(2)}, u32[]{:S(2)}) async-start(bf16[4,10,96,128]{3,2,1,0:T(8,128)(2,1)} %bitcast.20), calls=%async_computation | async-start | bytes 1966080 | tf_op jit(solution)/shard_map/all_to_all | solution.py:196
  11.5 1.6 %collective-permute-start.1 = (bf16[64,2560]{1,0:T(8,128)(2,1)S(1)}, bf16[64,2560]{1,0:T(8,128)(2,1)S(1)}, u32[]{:S(2)}, u32[]{:S(2)}) collective-permute-start(bf16[64,2560]{1,0:T(8,128)(2,1)S(1)} %pad_maximum_fusion), channel_id=1, source_target_pairs={{0,2},{1,3},{2,0},{3,1},{4,6},{5,7},{6,4},{7,5},{8,10},{9,11},{10,... | collective-permute-start | bytes 983048 | tf_op jit(solution)/shard_map/ppermute | solution.py:185
  13.1 2.0 %collective-permute-done.3.rest_1_ = bf16[4,32,1280]{2,1,0:T(8,128)(2,1)S(1)} collective-permute-done((bf16[4,32,1280]{2,1,0:T(8,128)(2,1)S(1)}, bf16[4,32,1280]{2,1,0:T(8,128)(2,1)S(1)}, u32[]{:S(2)}, u32[]{:S(2)}) %collective-permute-start.3) | collective-permute-done | bytes 327712 | tf_op jit(solution)/shard_map/ppermute | solution.py:185
  15.1 1.6 %collective-permute-start.4 = (bf16[4,32,1280]{2,1,0:T(8,128)(2,1)S(1)}, bf16[4,32,1280]{2,1,0:T(8,128)(2,1)S(1)}, u32[]{:S(2)}, u32[]{:S(2)}) collective-permute-start(bf16[4,32,1280]{2,1,0:T(8,128)(2,1)S(1)} %pad_maximum_fusion.1), channel_id=1, source_target_pairs={{0,2},{1,3},{2,0},{3,1},{4,6},{5,7},{6,4},{7,5},{8,10},{9,11},{10,... | collective-permute-start | bytes 983048 | tf_op jit(solution)/shard_map/ppermute | solution.py:185
  16.6 5.6 %collective-permute-done.1 = bf16[64,2560]{1,0:T(8,128)(2,1)S(1)} collective-permute-done((bf16[64,2560]{1,0:T(8,128)(2,1)S(1)}, bf16[64,2560]{1,0:T(8,128)(2,1)S(1)}, u32[]{:S(2)}, u32[]{:S(2)}) %collective-permute-start.1) | collective-permute-done | bytes 327712 | tf_op jit(solution)/shard_map/ppermute | solution.py:185
  22.3 4.6 %collective-permute-done.4.rest_2_ = bf16[4,32,1280]{2,1,0:T(8,128)(2,1)S(1)} collective-permute-done((bf16[4,32,1280]{2,1,0:T(8,128)(2,1)S(1)}, bf16[4,32,1280]{2,1,0:T(8,128)(2,1)S(1)}, u32[]{:S(2)}, u32[]{:S(2)}) %collective-permute-start.4) | collective-permute-done | bytes 327712 | tf_op jit(solution)/shard_map/ppermute | solution.py:185
  27.1 0.6 copy-done.10
  27.9 0.1 copy.8.tiles
  28.0 0.1 pad_add_fusion.places
  28.1 0.6 collective-permute-done.5.rest_3_
  28.7 0.7 copy-done.6
  29.4 2.4 %all-to-all-done.weights = bf16[4,10,96,128]{3,2,1,0:T(8,128)(2,1)S(1)} async-done(((bf16[4,10,96,128]{3,2,1,0:T(8,128)(2,1)}), bf16[4,10,96,128]{3,2,1,0:T(8,128)(2,1)S(1)}, u32[]{:S(2)}, u32[]{:S(2)}) %all-to-all-start) | async-done | bytes 983072 | tf_op jit(solution)/shard_map/all_to_all | solution.py:196
  31.9 1.0 %copy-done.7 = bf16[4,32,1280]{2,1,0:T(8,128)(2,1)S(1)} copy-done((bf16[4,32,1280]{2,1,0:T(8,128)(2,1)S(1)}, bf16[4,32,1280]{2,1,0:T(8,128)(2,1)}, u32[]{:S(2)}) %copy-start.7) | copy-done | bytes 327704
  32.9 4.0 %stripes.1 = (bf16[4,32,1280]{2,1,0:T(8,128)(2,1)S(1)}, bf16[4,32,1280]{2,1,0:T(8,128)(2,1)S(1)}, f32[10,96,128]{2,1,0:T(8,128)S(1)}, bf16[10,96,128]{2,1,0:T(8,...) custom-call(s32[10,3]{1,0:T(8,128)S(1)} %copy.8.tiles, s32[10]{0:T(128)S(1)} %dynamic_slice.7.counts, ...), custom_call_target="tpu_custom_call" | custom-call | tf_op jit(solution)/shard_map/stripes/pallas_call | solution.py:127
  36.9 3.3 %collective-permute-start.6 = (bf16[4,32,1280]{2,1,0:T(8,128)(2,1)S(1)}, bf16[4,32,1280]{2,1,0:T(8,128)(2,1)S(1)}, u32[]{:S(2)}, u32[]{:S(2)}) collective-permute-start(bf16[4,32,1280]{2,1,0:T(8,128)(2,1)S(1)} %get-tuple-element.13), channel_id=1, source_target_pairs={{0,4},{1,5},{2,6},{3,7},{4,0},{5,1},{6,2},{7,3},{8,12},{9,13},{10,... | collective-permute-start | bytes 983048 | tf_op jit(solution)/shard_map/ppermute | solution.py:185
  40.2 6.4 %collective-permute-done.6.rest_1_ = bf16[4,32,1280]{2,1,0:T(8,128)(2,1)S(1)} collective-permute-done((bf16[4,32,1280]{2,1,0:T(8,128)(2,1)S(1)}, bf16[4,32,1280]{2,1,0:T(8,128)(2,1)S(1)}, u32[]{:S(2)}, u32[]{:S(2)}) %collective-permute-start.6) | collective-permute-done | bytes 327712 | tf_op jit(solution)/shard_map/ppermute | solution.py:185
  46.7 0.6 copy-done.1
  47.3 1.0 %collective-permute-done.7.rest_2_ = bf16[4,32,1280]{2,1,0:T(8,128)(2,1)S(1)} collective-permute-done((bf16[4,32,1280]{2,1,0:T(8,128)(2,1)S(1)}, bf16[4,32,1280]{2,1,0:T(8,128)(2,1)S(1)}, u32[]{:S(2)}, u32[]{:S(2)}) %collective-permute-start.7) | collective-permute-done | bytes 327712 | tf_op jit(solution)/shard_map/ppermute | solution.py:185
  48.4 1.6 %collective-permute-start.8 = (bf16[4,32,1280]{2,1,0:T(8,128)(2,1)S(1)}, bf16[4,32,1280]{2,1,0:T(8,128)(2,1)S(1)}, u32[]{:S(2)}, u32[]{:S(2)}) collective-permute-start(bf16[4,32,1280]{2,1,0:T(8,128)(2,1)S(1)} %pad_maximum_fusion.4), channel_id=1, source_target_pairs={{0,2},{1,3},{2,0},{3,1},{4,6},{5,7},{6,4},{7,5},{8,10},{9,11},{10,... | collective-permute-start | bytes 983048 | tf_op jit(solution)/shard_map/ppermute | solution.py:185
  49.9 1.7 %collective-permute-start.9 = (bf16[10,96,128]{2,1,0:T(8,128)(2,1)}, bf16[10,96,128]{2,1,0:T(8,128)(2,1)S(1)}, u32[]{:S(2)}, u32[]{:S(2)}) collective-permute-start(bf16[10,96,128]{2,1,0:T(8,128)(2,1)} %get-tuple-element.15), channel_id=1, source_target_pairs={{0,4},{1,5},{2,6},{3,7},{4,0},{5,1},{6,2},{7,3},{8,12},{9,13},{10,... | collective-permute-start | bytes 737288 | tf_op jit(solution)/shard_map/ppermute | solution.py:185
  51.7 1.7 %collective-permute-start.11 = (bf16[10,96,128]{2,1,0:T(8,128)(2,1)}, bf16[10,96,128]{2,1,0:T(8,128)(2,1)S(1)}, u32[]{:S(2)}, u32[]{:S(2)}) collective-permute-start(bf16[10,96,128]{2,1,0:T(8,128)(2,1)} %get-tuple-element.17), channel_id=1, source_target_pairs={{0,12},{1,13},{2,14},{3,15},{4,8},{5,9},{6,10},{7,11},{8,4},{9,5},... | collective-permute-start | bytes 737288 | tf_op jit(solution)/shard_map/ppermute | solution.py:185
  53.4 0.1 stack.61.starts
  53.5 7.5 %collective-permute-done.9.rest_1_ = bf16[10,96,128]{2,1,0:T(8,128)(2,1)S(1)} collective-permute-done((bf16[10,96,128]{2,1,0:T(8,128)(2,1)}, bf16[10,96,128]{2,1,0:T(8,128)(2,1)S(1)}, u32[]{:S(2)}, u32[]{:S(2)}) %collective-permute-start.9) | collective-permute-done | bytes 245792 | tf_op jit(solution)/shard_map/ppermute | solution.py:185
  61.0 7.9 %collective-permute-done.10.rest_2_ = bf16[10,96,128]{2,1,0:T(8,128)(2,1)S(1)} collective-permute-done((bf16[10,96,128]{2,1,0:T(8,128)(2,1)}, bf16[10,96,128]{2,1,0:T(8,128)(2,1)S(1)}, u32[]{:S(2)}, u32[]{:S(2)}) %collective-permute-start.10) | collective-permute-done | bytes 245792 | tf_op jit(solution)/shard_map/ppermute | solution.py:185
  68.9 6.0 %collective-permute-done.11.rest_3_ = bf16[10,96,128]{2,1,0:T(8,128)(2,1)S(1)} collective-permute-done((bf16[10,96,128]{2,1,0:T(8,128)(2,1)}, bf16[10,96,128]{2,1,0:T(8,128)(2,1)S(1)}, u32[]{:S(2)}, u32[]{:S(2)}) %collective-permute-start.11) | collective-permute-done | bytes 245792 | tf_op jit(solution)/shard_map/ppermute | solution.py:185
  74.9 1.5 %sum.1 = f32[2,10,96,128]{3,2,1,0:T(8,128)} custom-call(s32[1]{0:T(128)} %bitcast.15.half, f32[10,96,128]{2,1,0:T(8,128)S(1)} %get-tuple-element.14.rest_0_, bf16[10,96,128]{2,1,0:T(8,128)(2,1)S(1)} %collective-permute-done.9.rest_1_, bf16[10,96,128]{2,1,0:T(8,128)(2,1)S(1)} %collective-permute-done.10.rest_2_, ...), custom_call_target="tpu_custom_call" | custom-call | bytes 104857600 | tf_op jit(solution)/shard_map/sum/pallas_call | solution.py:158
  76.4 1.4 %join.1 = bf16[32,10240]{1,0:T(8,128)(2,1)} custom-call(s32[8]{0:T(128)S(1)} %stack.61.starts, bf16[4,32,1280]{2,1,0:T(8,128)(2,1)S(1)} %get-tuple-element.12.rest_0_, bf16[4,32,1280]{2,1,0:T(8,128)(2,1)S(1)} %copy-done.2, bf16[4,32,1280]{2,1,0:T(8,128)(2,1)S(1)} %collective-permute-done.7.rest_2_, bf16[4,32,1280]{2,1,0:T(8,128)(2,1)S(1)} %collective-permute-done.8.rest_3_), custom_call_target="tpu_custom_call" | custom-call | tf_op jit(solution)/shard_map/join/pallas_call | solution.py:80
  (47 shorter events, 0.8 us)
Async XLA Ops:
  0.6 27.2 %copy-start = (s32[20,3]{0,1:T(4,128)S(1)}, s32[20,3]{0,1:T(4,128)}, u32[]{:S(2)}) copy-start(s32[20,3]{0,1:T(4,128)} %param.8) | copy-start | bytes 724
  0.6 10.8 %collective-permute-start = (bf16[32,2560]{1,0:T(8,128)(2,1)}, bf16[32,2560]{1,0:T(8,128)(2,1)S(1)}, u32[]{:S(2)}, u32[]{:S(2)}) collective-permute-start(bf16[32,2560]{1,0:T(8,128)(2,1)} %param.5), channel_id=1, source_target_pairs={{0,4},{1,5},{2,6},{3,7},{4,0},{5,1},{6,2},{7,3},{8,12},{9,13},{10,... | collective-permute-start | bytes 491528 | tf_op jit(solution)/shard_map/ppermute | solution.py:185
  0.8 1.1 %copy-start.5 = (bf16[32,10240]{1,0:T(8,128)(2,1)S(1)}, bf16[32,10240]{1,0:T(8,128)(2,1)}, u32[]{:S(2)}) copy-start(bf16[32,10240]{1,0:T(8,128)(2,1)} %whole.1) | copy-start | bytes 1966084
  1.9 2.9 %copy-start.9 = (bf16[96,20,128]{2,0,1:T(8,128)(2,1)S(1)}, bf16[96,20,128]{2,0,1:T(8,128)(2,1)}, u32[]{:S(2)}) copy-start(bf16[96,20,128]{2,0,1:T(8,128)(2,1)} %param.6) | copy-start | bytes 1474564
  2.8 12.2 %collective-permute-start.3 = (bf16[4,32,1280]{2,1,0:T(8,128)(2,1)S(1)}, bf16[4,32,1280]{2,1,0:T(8,128)(2,1)S(1)}, u32[]{:S(2)}, u32[]{:S(2)}) collective-permute-start(bf16[4,32,1280]{2,1,0:T(8,128)(2,1)S(1)} %get-tuple-element.11), channel_id=1, source_target_pairs={{0,4},{1,5},{2,6},{3,7},{4,0},{5,1},{6,2},{7,3},{8,12},{9,13},{10,... | collective-permute-start | bytes 983048 | tf_op jit(solution)/shard_map/ppermute | solution.py:185
  5.9 5.5 %copy-start.8 = (bf16[32,2560]{1,0:T(8,128)(2,1)S(1)}, bf16[32,2560]{1,0:T(8,128)(2,1)}, u32[]{:S(2)}) copy-start(bf16[32,2560]{1,0:T(8,128)(2,1)} %param.5) | copy-start | bytes 491524
  5.9 25.9 %all-to-all-start = ((bf16[4,10,96,128]{3,2,1,0:T(8,128)(2,1)}), bf16[4,10,96,128]{3,2,1,0:T(8,128)(2,1)S(1)}, u32[]{:S(2)}, u32[]{:S(2)}) async-start(bf16[4,10,96,128]{3,2,1,0:T(8,128)(2,1)} %bitcast.20), calls=%async_computation | async-start | bytes 1966080 | tf_op jit(solution)/shard_map/all_to_all | solution.py:196
  11.5 10.7 %collective-permute-start.1 = (bf16[64,2560]{1,0:T(8,128)(2,1)S(1)}, bf16[64,2560]{1,0:T(8,128)(2,1)S(1)}, u32[]{:S(2)}, u32[]{:S(2)}) collective-permute-start(bf16[64,2560]{1,0:T(8,128)(2,1)S(1)} %pad_maximum_fusion), channel_id=1, source_target_pairs={{0,2},{1,3},{2,0},{3,1},{4,6},{5,7},{6,4},{7,5},{8,10},{9,11},{10,... | collective-permute-start | bytes 983048 | tf_op jit(solution)/shard_map/ppermute | solution.py:185
  15.0 1.6 %copy-start.3 = (bf16[4,32,1280]{2,1,0:T(8,128)(2,1)}, bf16[4,32,1280]{2,1,0:T(8,128)(2,1)S(1)}, u32[]{:S(2)}) copy-start(bf16[4,32,1280]{2,1,0:T(8,128)(2,1)S(1)} %collective-permute-done.3.rest_1_) | copy-start | bytes 983044
  15.1 11.8 %collective-permute-start.4 = (bf16[4,32,1280]{2,1,0:T(8,128)(2,1)S(1)}, bf16[4,32,1280]{2,1,0:T(8,128)(2,1)S(1)}, u32[]{:S(2)}, u32[]{:S(2)}) collective-permute-start(bf16[4,32,1280]{2,1,0:T(8,128)(2,1)S(1)} %pad_maximum_fusion.1), channel_id=1, source_target_pairs={{0,2},{1,3},{2,0},{3,1},{4,6},{5,7},{6,4},{7,5},{8,10},{9,11},{10,... | collective-permute-start | bytes 983048 | tf_op jit(solution)/shard_map/ppermute | solution.py:185
  22.2 4.7 %slice-start.1 = ((bf16[4,32,1280]{2,1,0:T(8,128)(2,1)}), bf16[1,32,1280]{2,1,0:T(8,128)(2,1)S(1)}, s32[]{:S(2)}) async-start(bf16[4,32,1280]{2,1,0:T(8,128)(2,1)} %copy-done.3), calls=%async_computation.2 | async-start | bytes 163840 | tf_op jit(solution)/shard_map/slice | solution.py:189
  22.2 7.2 %collective-permute-start.2 = (bf16[128,2560]{1,0:T(8,128)(2,1)S(1)}, bf16[128,2560]{1,0:T(8,128)(2,1)}, u32[]{:S(2)}, u32[]{:S(2)}) collective-permute-start(bf16[128,2560]{1,0:T(8,128)(2,1)S(1)} %constant_dynamic-update-slice_fusion.near), channel_id=1, source_target_pairs={{0,1},{1,0},{2,3},{3,2},{4,5},{5,4},{6,7},{7,6},{8,9},{9,8},{10,11... | collective-permute-start | bytes 1966088 | tf_op jit(solution)/shard_map/ppermute | solution.py:185
  26.9 5.0 %copy-start.4 = (bf16[4,32,1280]{2,1,0:T(8,128)(2,1)S(1)}, bf16[4,32,1280]{2,1,0:T(8,128)(2,1)}, u32[]{:S(2)}) copy-start(bf16[4,32,1280]{2,1,0:T(8,128)(2,1)} %copy-done.3) | copy-start | bytes 983044
  27.0 1.7 %collective-permute-start.5 = (bf16[4,32,1280]{2,1,0:T(8,128)(2,1)S(1)}, bf16[4,32,1280]{2,1,0:T(8,128)(2,1)S(1)}, u32[]{:S(2)}, u32[]{:S(2)}) collective-permute-start(bf16[4,32,1280]{2,1,0:T(8,128)(2,1)S(1)} %pad_maximum_fusion.2), channel_id=1, source_target_pairs={{0,1},{1,0},{2,3},{3,2},{4,5},{5,4},{6,7},{7,6},{8,9},{9,8},{10,11... | collective-permute-start | bytes 983048 | tf_op jit(solution)/shard_map/ppermute | solution.py:185
  27.1 0.7 copy-start.10
  28.7 0.8 copy-start.6
  31.9 1.0 %copy-start.7 = (bf16[4,32,1280]{2,1,0:T(8,128)(2,1)S(1)}, bf16[4,32,1280]{2,1,0:T(8,128)(2,1)}, u32[]{:S(2)}) copy-start(bf16[4,32,1280]{2,1,0:T(8,128)(2,1)} %copy-done.6) | copy-start | bytes 983044
  36.9 9.6 %collective-permute-start.6 = (bf16[4,32,1280]{2,1,0:T(8,128)(2,1)S(1)}, bf16[4,32,1280]{2,1,0:T(8,128)(2,1)S(1)}, u32[]{:S(2)}, u32[]{:S(2)}) collective-permute-start(bf16[4,32,1280]{2,1,0:T(8,128)(2,1)S(1)} %get-tuple-element.13), channel_id=1, source_target_pairs={{0,4},{1,5},{2,6},{3,7},{4,0},{5,1},{6,2},{7,3},{8,12},{9,13},{10,... | collective-permute-start | bytes 983048 | tf_op jit(solution)/shard_map/ppermute | solution.py:185
  46.5 0.7 copy-start.1
  46.6 1.7 %collective-permute-start.7 = (bf16[4,32,1280]{2,1,0:T(8,128)(2,1)S(1)}, bf16[4,32,1280]{2,1,0:T(8,128)(2,1)S(1)}, u32[]{:S(2)}, u32[]{:S(2)}) collective-permute-start(bf16[4,32,1280]{2,1,0:T(8,128)(2,1)S(1)} %pad_maximum_fusion.3), channel_id=1, source_target_pairs={{0,1},{1,0},{2,3},{3,2},{4,5},{5,4},{6,7},{7,6},{8,9},{9,8},{10,11... | collective-permute-start | bytes 983048 | tf_op jit(solution)/shard_map/ppermute | solution.py:185
  47.3 1.0 %slice-start = ((bf16[4,32,1280]{2,1,0:T(8,128)(2,1)}), bf16[1,32,1280]{2,1,0:T(8,128)(2,1)S(1)}, s32[]{:S(2)}) async-start(bf16[4,32,1280]{2,1,0:T(8,128)(2,1)} %copy-done.1), calls=%async_computation.1 | async-start | bytes 163840 | tf_op jit(solution)/shard_map/slice | solution.py:189
  48.4 28.1 %collective-permute-start.8 = (bf16[4,32,1280]{2,1,0:T(8,128)(2,1)S(1)}, bf16[4,32,1280]{2,1,0:T(8,128)(2,1)S(1)}, u32[]{:S(2)}, u32[]{:S(2)}) collective-permute-start(bf16[4,32,1280]{2,1,0:T(8,128)(2,1)S(1)} %pad_maximum_fusion.4), channel_id=1, source_target_pairs={{0,2},{1,3},{2,0},{3,1},{4,6},{5,7},{6,4},{7,5},{8,10},{9,11},{10,... | collective-permute-start | bytes 983048 | tf_op jit(solution)/shard_map/ppermute | solution.py:185
  49.9 11.0 %collective-permute-start.9 = (bf16[10,96,128]{2,1,0:T(8,128)(2,1)}, bf16[10,96,128]{2,1,0:T(8,128)(2,1)S(1)}, u32[]{:S(2)}, u32[]{:S(2)}) collective-permute-start(bf16[10,96,128]{2,1,0:T(8,128)(2,1)} %get-tuple-element.15), channel_id=1, source_target_pairs={{0,4},{1,5},{2,6},{3,7},{4,0},{5,1},{6,2},{7,3},{8,12},{9,13},{10,... | collective-permute-start | bytes 737288 | tf_op jit(solution)/shard_map/ppermute | solution.py:185
  51.7 17.2 %collective-permute-start.10 = (bf16[10,96,128]{2,1,0:T(8,128)(2,1)}, bf16[10,96,128]{2,1,0:T(8,128)(2,1)S(1)}, u32[]{:S(2)}, u32[]{:S(2)}) collective-permute-start(bf16[10,96,128]{2,1,0:T(8,128)(2,1)} %get-tuple-element.16), channel_id=1, source_target_pairs={{0,8},{1,9},{2,10},{3,11},{4,12},{5,13},{6,14},{7,15},{8,0},{9,1},... | collective-permute-start | bytes 737288 | tf_op jit(solution)/shard_map/ppermute | solution.py:185
  51.7 23.2 %collective-permute-start.11 = (bf16[10,96,128]{2,1,0:T(8,128)(2,1)}, bf16[10,96,128]{2,1,0:T(8,128)(2,1)S(1)}, u32[]{:S(2)}, u32[]{:S(2)}) collective-permute-start(bf16[10,96,128]{2,1,0:T(8,128)(2,1)} %get-tuple-element.17), channel_id=1, source_target_pairs={{0,12},{1,13},{2,14},{3,15},{4,8},{5,9},{6,10},{7,11},{8,4},{9,5},... | collective-permute-start | bytes 737288 | tf_op jit(solution)/shard_map/ppermute | solution.py:185
  74.9 1.5 %copy-start.2 = (bf16[4,32,1280]{2,1,0:T(8,128)(2,1)S(1)}, bf16[4,32,1280]{2,1,0:T(8,128)(2,1)}, u32[]{:S(2)}) copy-start(bf16[4,32,1280]{2,1,0:T(8,128)(2,1)} %copy-done.1) | copy-start | bytes 983044

commit v6 on v5

--- a/solution.py
+++ b/solution.py
@@ -10,8 +10,7 @@
 TILE = 128
 SLOTS = 3
 PAIR = 2
-DIRECT = 8
-WEIGHT = 100 * 2**20
+ROWS = 16
 ROOT = 0.7978845608028654
 CUBIC = 0.044715
 ANYWHERE = pl.BlockSpec(memory_space=pl.ANY)
@@ -27,10 +26,6 @@
     half = 0.5 * (1.0 + th)
     inner = ROOT * (1.0 + (3.0 * CUBIC) * square)
     return v * half, half + 0.5 * v * (1.0 - th * th) * inner
-
-
-def vmem(*arrays):
-    return [pltpu.with_memory_space_constraint(array, pltpu.VMEM) for array in arrays]
 
 
 def copy_all(copies):
@@ -61,7 +56,7 @@
         scratch_shapes=[pltpu.SemaphoreType.DMA((PAIR * count,))],
         compiler_params=room(1),
         name="cut",
-    )(starts, whole)
+    )(starts, pltpu.with_memory_space_constraint(whole, pltpu.HBM))
 
 
 def join_kernel(picks, starts, *rest):
@@ -88,13 +83,12 @@
     )(starts, *arrays)
 
 
-def stripe_kernel(parts, picks, tiles, counts, places, near, far, weights, *rest):
-    inputs = max(a for a, _ in picks) + 1
-    arrays, (home, away), grads, term = rest[:inputs], rest[inputs:inputs + 2], rest[inputs + 2:-1], rest[-1]
+def stripe_kernel(picks, tiles, counts, own, near, far, weights, *rest):
+    arrays, (home, away, grads, mine, term) = rest[:-5], rest[-5:]
     rows = arrays[0].shape[1]
-    size = grads[0].shape[1]
-    spans = [pl.ds(pl.multiple_of(places[p], size), size) for p in range(parts)]
-    for s in range(weights.shape[1]):
+    shards, stripes, size, _ = weights.shape
+    span = pl.ds(pl.multiple_of(own[0] * size, size), size)
+    for s in range(stripes):
         cols = slice(s * TILE, (s + 1) * TILE)
         picked = []
         for k in range(SLOTS):
@@ -102,7 +96,7 @@
             block = jnp.concatenate([near[:, pl.ds(column, TILE)], far[:, pl.ds(column, TILE)]], axis=0)
             picked.append(jnp.where(k < counts[s], block, jnp.zeros_like(block)))
         picked = jnp.concatenate(picked, axis=1)
-        stack = jnp.concatenate([weights[f, s] for f in range(weights.shape[0])], axis=0)
+        stack = jnp.concatenate([weights[f, s] for f in range(shards)], axis=0)
         pre = jnp.dot(picked, stack, preferred_element_type=jnp.float32)
         act, slope = gelu_and_derivative(pre)
         back = jnp.concatenate([arrays[a][b, :, cols] for a, b in picks], axis=0)
@@ -112,62 +106,50 @@
             home[b, :, cols] = act[(2 * b) * rows:(2 * b + 1) * rows]
             away[b, :, cols] = act[(2 * b + 1) * rows:(2 * b + 2) * rows]
         term[s] = lax.dot_general(picked, slope, (((0,), (0,)), ((), ())), preferred_element_type=jnp.float32)
-        for p in range(parts):
-            grads[p][s] = term[s, spans[p]].astype(grads[p].dtype)
-
-
-def stripe_call(tiles, counts, places, near, far, weights, arrays, picks):
+        for f in range(shards):
+            grads[f, s] = term[s, f * size:(f + 1) * size].astype(grads.dtype)
+        mine[s] = term[s, span]
+
+
+def stripe_call(tiles, counts, own, near, far, weights, arrays, picks):
     _, rows, width = arrays[0].shape
     stripes = weights.shape[1]
-    parts = places.shape[0]
     blocks = len(picks)
     resident = pl.BlockSpec(memory_space=pltpu.VMEM)
     scalar = pl.BlockSpec(memory_space=pltpu.SMEM)
-    term = (stripes, SLOTS * TILE // parts, TILE)
-    return pl.pallas_call(
-        functools.partial(stripe_kernel, parts, picks),
-        out_shape=[pltpu.VMEM((blocks // 2, rows, width), jnp.bfloat16)] * 2
-        + [pltpu.VMEM(term, jnp.bfloat16 if p else jnp.float32) for p in range(parts)],
+    return pl.pallas_call(
+        functools.partial(stripe_kernel, picks),
+        out_shape=[jax.ShapeDtypeStruct((blocks // 2, rows, width), jnp.bfloat16)] * 2
+        + [jax.ShapeDtypeStruct(weights.shape, jnp.bfloat16), jax.ShapeDtypeStruct(weights.shape[1:], jnp.float32)],
         in_specs=[scalar] * 3 + [resident] * (3 + len(arrays)),
-        out_specs=[resident] * (2 + parts),
+        out_specs=[resident] * 4,
         scratch_shapes=[pltpu.VMEM((stripes, SLOTS * TILE, TILE), jnp.float32)],
-        compiler_params=room(24),
+        compiler_params=room(12),
         name="stripes",
-    )(tiles, counts, places, *vmem(near, far, weights, *arrays))
-
-
-def sum_kernel(half, *rest):
-    grads, total = rest[:-1], rest[-1]
-    for a in range(PAIR):
-
-        @pl.when(pl.program_id(0) == a)
-        def _():
-            add = None
-            for piece in grads[a::PAIR]:
-                term = piece[...].astype(jnp.float32)
-                add = term if add is None else add + term
-            total[0] = add
-
-
-def sum_call(half, grads):
-    stripes, size, _ = grads[0].shape
+    )(tiles, counts, own, near, far, weights, *arrays)
+
+
+def sum_kernel(own, grads, mine, total):
+    half = pl.program_id(0)
+    total[0] = sum(jnp.where(own[0] == p * PAIR + half, mine[...], grads[p].astype(jnp.float32)) for p in range(grads.shape[0]))
+
+
+def sum_call(own, grads, mine):
+    shards, stripes, size, _ = grads.shape
     step = stripes // 2 if stripes % 2 == 0 else stripes
-    chunks = stripes // step
-    first = pl.BlockSpec((step, size, TILE), lambda a, c, half: (jnp.where(a == 0, c, chunks - 1), 0, 0))
-    second = pl.BlockSpec((step, size, TILE), lambda a, c, half: (jnp.where(a == 0, 0, c), 0, 0))
+    by_half = pl.BlockSpec((shards // PAIR, None, step, size, TILE), lambda a, c, *_: (0, a, c, 0, 0))
     return pl.pallas_call(
         sum_kernel,
         out_shape=jax.ShapeDtypeStruct((PAIR, stripes, size, TILE), jnp.float32),
         grid_spec=pltpu.PrefetchScalarGridSpec(
             num_scalar_prefetch=1,
-            grid=(PAIR, chunks),
-            in_specs=[second if p % PAIR else first for p in range(len(grads))],
-            out_specs=pl.BlockSpec((1, step, size, TILE), lambda a, c, half: (half[0] ^ a, c, 0, 0)),
+            grid=(PAIR, stripes // step),
+            in_specs=[by_half, pl.BlockSpec((step, size, TILE), lambda a, c, *_: (c, 0, 0))],
+            out_specs=pl.BlockSpec((1, step, size, TILE), lambda a, c, *_: (a, c, 0, 0)),
         ),
-        compiler_params=room(16),
-        cost_estimate=pl.CostEstimate(flops=0, bytes_accessed=WEIGHT, transcendentals=0),
+        compiler_params=room(12),
         name="sum",
-    )(half, *grads)
+    )(own, grads.reshape(shards // PAIR, PAIR, stripes, size, TILE), mine)
 
 
 def body(fsdp, tensor, tokens, tile_weights, cotangent, tile_list, tile_counts):
@@ -177,7 +159,7 @@
     size, stripes = tile_weights.shape[0], tile_weights.shape[1]
     share = stripes // PAIR
     width = share * TILE
-    direct = fsdp <= DIRECT
+    whole_tiles = size % ROWS == 0
     bits = [1 << i for i in reversed(range((tensor - 1).bit_length()))]
 
     def swap(value, dz, dt):
@@ -194,11 +176,9 @@
     by_stripe = jnp.transpose(tile_weights, (1, 0, 2))
     outgoing = jnp.tile(by_stripe.reshape(PAIR, share, size, TILE), (fsdp // PAIR, 1, 1, 1))
     weights = lax.all_to_all(outgoing, "fsdp", split_axis=0, concat_axis=0, tiled=True)
-    if direct:
-        places = jnp.stack([(z ^ k) * size for k in range(fsdp)]).astype(jnp.int32)
-    else:
+    own = z.reshape(1).astype(jnp.int32)
+    if not whole_tiles:
         weights = weights.transpose(1, 0, 2, 3).reshape(1, share, fsdp * size, TILE)
-        places = jnp.zeros((1,), jnp.int32)
 
     near = jnp.concatenate([tokens, swap(tokens, 1, 0)], axis=0)
     starts = jnp.stack([(t ^ b) * stripes + (half ^ a) * share for a in range(PAIR) for b in range(tensor)]).astype(jnp.int32)
@@ -215,7 +195,13 @@
     tiles = lax.dynamic_slice_in_dim(tile_list, half * share, share, 0)
     counts = lax.dynamic_slice_in_dim(tile_counts, half * share, share, 0)
     picks = [(a, span[0]) for a, span in spans]
-    home, away, *grads = stripe_call(tiles, counts, places, near, far, weights, arrays, picks)
+    home, away, grads, mine = stripe_call(tiles, counts, own if whole_tiles else own * 0, near, far, weights, arrays, picks)
+
+    if not whole_tiles:
+        grads = grads.reshape(share, fsdp, size, TILE).transpose(1, 0, 2, 3)
+        mine = lax.dynamic_index_in_dim(mine.reshape(share, fsdp, size, TILE), z, 1, keepdims=False)
+    grads = lax.all_to_all(grads, "fsdp", split_axis=0, concat_axis=0, tiled=True)
+    total = sum_call(own, grads, mine)
 
     arrays, spans = [home, swap(away, 1, 0)], [(0, range(tensor)), (1, range(tensor))]
     origins = [(0, 0), (1, 0)]
@@ -225,16 +211,6 @@
     starts = jnp.stack([(t ^ b) * stripes + (half ^ a) * share for a, b in origins]).astype(jnp.int32)
     activations = join_call(starts, arrays, [(a, span[0]) for a, span in spans])
 
-    if direct:
-        grads = [grads[0]] + [swap(grads[k], k, 0) for k in range(1, fsdp)]
-        total = sum_call(half.reshape(1).astype(jnp.int32), grads)
-    else:
-        split = grads[0].reshape(share, fsdp, size, TILE).transpose(1, 0, 2, 3)
-        mine = lax.dynamic_index_in_dim(split, z, 0)
-        arrived = lax.all_to_all(split.astype(jnp.bfloat16), "fsdp", split_axis=0, concat_axis=0, tiled=True)
-        here = (jnp.arange(fsdp) == z)[:, None, None, None]
-        total = jnp.where(here, mine, arrived.astype(jnp.float32))
-        total = jnp.sum(total.reshape(fsdp // PAIR, PAIR, share, size, TILE), axis=0)
     return activations, total.reshape(stripes, size, TILE).transpose(1, 0, 2)
 
 

time: 78.2 us -> 74.2 us (0.949)
  the two profiles are of different devices: /device:TPU:8 before, /device:TPU:0 now
where the time goes in v6:
time: 74.2 us; the launch traced here: 73.8 us
  waiting for transfers between devices  41.6 us (56%)
  starting transfers between devices  17.1 us (23%)
  Pallas kernels  8.47 us (11%)
  local copies, waits for them, and re-layouts  5.56 us (7%)
  between operations  0.88 us (1%)
    ppermute x9, waiting for transfers between devices, swap(): return lax.ppermute(value, ('fsdp', 'tensor'), pairs)  36.2 us
    ppermute x9, starting transfers between devices, swap(): return lax.ppermute(value, ('fsdp', 'tensor'), pairs)  8.16 us
    all_to_all x1, waiting for transfers between devices, body(): lax.all_to_all(outgoing, 'fsdp', split_axis=0, concat_axis=0, tiled=True)  5.44 us
    all_to_all x1, starting transfers between devices, body(): lax.all_to_all(outgoing, 'fsdp', split_axis=0, concat_axis=0, tiled=True)  5.4 us
    unnamed x25, local copies, waits for them, and re-layouts  4.03 us
    pallas_call x1, Pallas kernels, stripe_call(): pl.pallas_call(functools.partial(stripe_kernel, picks), out_shape=[jax.Sh...  3.58 us
    all_to_all x1, starting transfers between devices, body(): lax.all_to_all(grads, 'fsdp', split_axis=0, concat_axis=0, tiled=True)  3.51 us
    pallas_call x1, Pallas kernels, cut_call(): pl.pallas_call(cut_kernel, out_shape=[jax.ShapeDtypeStruct((count, rows,...  1.79 us
  transfers between devices with their start and end apart: 11, of which 8 were waited for; matrix products, arithmetic and copies ran while one was open for 2% of the time, Pallas kernels for 4%

profile of v6, /device:TPU:0, one launch (start us, length us, event | category | flops | bytes accessed | tf_op | source)
XLA Modules:
  0.0 73.8 jit_solution(360159459127766589)
XLA Ops:
  0.7 3.1 %collective-permute-start = (bf16[32,2560]{1,0:T(8,128)(2,1)}, bf16[32,2560]{1,0:T(8,128)(2,1)S(1)}, u32[]{:S(2)}, u32[]{:S(2)}) collective-permute-start(bf16[32,2560]{1,0:T(8,128)(2,1)} %param.5), channel_id=1, source_target_pairs={{0,4},{1,5},{2,6},{3,7},{4,0},{5,1},{6,2},{7,3},{8,12},{9,13},{10,... | collective-permute-start | bytes 491528 | tf_op jit(solution)/shard_map/ppermute | solution.py:167
  3.7 0.1 stack.47.starts
  3.8 1.8 %cut.1 = (bf16[4,32,1280]{2,1,0:T(8,128)(2,1)S(1)}, bf16[4,32,1280]{2,1,0:T(8,128)(2,1)S(1)}) custom-call(s32[8]{0:T(128)S(1)} %stack.47.starts, bf16[32,10240]{1,0:T(8,128)(2,1)} %whole.1), custom_call_target="tpu_custom_call" | custom-call | tf_op jit(solution)/shard_map/cut/pallas_call | solution.py:51
  5.6 0.1 collective-permute-start.3
  5.7 1.1 %tile.11 = bf16[2,2,10,96,128]{4,3,2,1,0:T(8,128)(2,1)} broadcast(bf16[2,10,96,128]{3,2,1,0:T(8,128)(2,1)S(1)} %bitcast.20), dimensions={1,2,3,4} | broadcast | bytes 1474560 | tf_op jit(solution)/shard_map/tile | solution.py:177
  6.8 5.4 %all-to-all-start = ((bf16[4,10,96,128]{3,2,1,0:T(8,128)(2,1)}), bf16[4,10,96,128]{3,2,1,0:T(8,128)(2,1)S(1)}, u32[]{:S(2)}, u32[]{:S(2)}) async-start(bf16[4,10,96,128]{3,2,1,0:T(8,128)(2,1)} %bitcast.18), calls=%async_computation | async-start | bytes 1966080 | tf_op jit(solution)/shard_map/all_to_all | solution.py:178
  12.3 1.6 %collective-permute-start.1 = (bf16[64,2560]{1,0:T(8,128)(2,1)S(1)}, bf16[64,2560]{1,0:T(8,128)(2,1)S(1)}, u32[]{:S(2)}, u32[]{:S(2)}) collective-permute-start(bf16[64,2560]{1,0:T(8,128)(2,1)S(1)} %pad_maximum_fusion), channel_id=1, source_target_pairs={{0,2},{1,3},{2,0},{3,1},{4,6},{5,7},{6,4},{7,5},{8,10},{9,11},{10,... | collective-permute-start | bytes 983048 | tf_op jit(solution)/shard_map/ppermute | solution.py:167
  13.9 2.3 %collective-permute-done.3.rest_1_ = bf16[4,32,1280]{2,1,0:T(8,128)(2,1)S(1)} collective-permute-done((bf16[4,32,1280]{2,1,0:T(8,128)(2,1)S(1)}, bf16[4,32,1280]{2,1,0:T(8,128)(2,1)S(1)}, u32[]{:S(2)}, u32[]{:S(2)}) %collective-permute-start.3) | collective-permute-done | bytes 327712 | tf_op jit(solution)/shard_map/ppermute | solution.py:167
  16.3 1.6 %collective-permute-start.4 = (bf16[4,32,1280]{2,1,0:T(8,128)(2,1)S(1)}, bf16[4,32,1280]{2,1,0:T(8,128)(2,1)S(1)}, u32[]{:S(2)}, u32[]{:S(2)}) collective-permute-start(bf16[4,32,1280]{2,1,0:T(8,128)(2,1)S(1)} %pad_maximum_fusion.1), channel_id=1, source_target_pairs={{0,2},{1,3},{2,0},{3,1},{4,6},{5,7},{6,4},{7,5},{8,10},{9,11},{10,... | collective-permute-start | bytes 983048 | tf_op jit(solution)/shard_map/ppermute | solution.py:167
  17.9 5.1 %collective-permute-done.1 = bf16[64,2560]{1,0:T(8,128)(2,1)S(1)} collective-permute-done((bf16[64,2560]{1,0:T(8,128)(2,1)S(1)}, bf16[64,2560]{1,0:T(8,128)(2,1)S(1)}, u32[]{:S(2)}, u32[]{:S(2)}) %collective-permute-start.1) | collective-permute-done | bytes 327712 | tf_op jit(solution)/shard_map/ppermute | solution.py:167
  23.1 0.1 collective-permute-start.2
  23.2 4.9 %collective-permute-done.4.rest_2_ = bf16[4,32,1280]{2,1,0:T(8,128)(2,1)S(1)} collective-permute-done((bf16[4,32,1280]{2,1,0:T(8,128)(2,1)S(1)}, bf16[4,32,1280]{2,1,0:T(8,128)(2,1)S(1)}, u32[]{:S(2)}, u32[]{:S(2)}) %collective-permute-start.4) | collective-permute-done | bytes 327712 | tf_op jit(solution)/shard_map/ppermute | solution.py:167
  28.1 0.1 collective-permute-start.5
  28.2 0.6 copy-done.10
  28.9 0.1 dynamic_slice.7.counts
  28.9 0.1 constant_dynamic-slice_fusion
  29.0 0.1 copy.8.tiles
  29.1 0.7 collective-permute-done.5.rest_3_
  29.8 0.7 copy-done.6
  30.6 5.4 %all-to-all-done.weights = bf16[4,10,96,128]{3,2,1,0:T(8,128)(2,1)S(1)} async-done(((bf16[4,10,96,128]{3,2,1,0:T(8,128)(2,1)}), bf16[4,10,96,128]{3,2,1,0:T(8,128)(2,1)S(1)}, u32[]{:S(2)}, u32[]{:S(2)}) %all-to-all-start) | async-done | bytes 983072 | tf_op jit(solution)/shard_map/all_to_all | solution.py:178
  36.0 1.0 %copy-done.7 = bf16[4,32,1280]{2,1,0:T(8,128)(2,1)S(1)} copy-done((bf16[4,32,1280]{2,1,0:T(8,128)(2,1)S(1)}, bf16[4,32,1280]{2,1,0:T(8,128)(2,1)}, u32[]{:S(2)}) %copy-start.7) | copy-done | bytes 327704
  37.0 3.6 %stripes.1 = (bf16[4,32,1280]{2,1,0:T(8,128)(2,1)S(1)}, bf16[4,32,1280]{2,1,0:T(8,128)(2,1)}, bf16[4,10,96,128]{3,2,1,0:T(8,128)(2,1)S(1)}, f32[10,96,128]{2,1,0:T(8,128)S(1)}) custom-call(s32[10,3]{1,0:T(8,128)S(1)} %copy.8.tiles, s32[10]{0:T(128)S(1)} %dynamic_slice.7.counts, s32[1]{0:T(128)} %bitcast.8.own, ...), custom_call_target="tpu_custom_call" | custom-call | tf_op jit(solution)/shard_map/stripes/pallas_call | solution.py:120
  40.6 0.9 %copy-done.5 = bf16[4,10,96,128]{3,2,1,0:T(8,128)(2,1)} copy-done((bf16[4,10,96,128]{3,2,1,0:T(8,128)(2,1)}, bf16[4,10,96,128]{3,2,1,0:T(8,128)(2,1)S(1)}, u32[]{:S(2)}) %copy-start.5) | copy-done | bytes 983064
  41.5 3.5 %all-to-all-start.1 = ((bf16[4,10,96,128]{3,2,1,0:T(8,128)(2,1)}), bf16[4,10,96,128]{3,2,1,0:T(8,128)(2,1)S(1)}, u32[]{:S(2)}, u32[]{:S(2)}) async-start(bf16[4,10,96,128]{3,2,1,0:T(8,128)(2,1)} %copy-done.5), calls=%async_computation.1 | async-start | bytes 1966080 | tf_op jit(solution)/shard_map/all_to_all | solution.py:203
  45.1 14.0 %collective-permute-done.6.rest_1_ = bf16[4,32,1280]{2,1,0:T(8,128)(2,1)S(1)} collective-permute-done((bf16[4,32,1280]{2,1,0:T(8,128)(2,1)}, bf16[4,32,1280]{2,1,0:T(8,128)(2,1)S(1)}, u32[]{:S(2)}, u32[]{:S(2)}) %collective-permute-start.6) | collective-permute-done | bytes 327712 | tf_op jit(solution)/shard_map/ppermute | solution.py:167
  59.2 0.6 copy-done.1
  59.8 1.0 %collective-permute-done.7.rest_2_ = bf16[4,32,1280]{2,1,0:T(8,128)(2,1)S(1)} collective-permute-done((bf16[4,32,1280]{2,1,0:T(8,128)(2,1)S(1)}, bf16[4,32,1280]{2,1,0:T(8,128)(2,1)S(1)}, u32[]{:S(2)}, u32[]{:S(2)}) %collective-permute-start.7) | collective-permute-done | bytes 327712 | tf_op jit(solution)/shard_map/ppermute | solution.py:167
  60.9 1.5 %collective-permute-start.8 = (bf16[4,32,1280]{2,1,0:T(8,128)(2,1)S(1)}, bf16[4,32,1280]{2,1,0:T(8,128)(2,1)S(1)}, u32[]{:S(2)}, u32[]{:S(2)}) collective-permute-start(bf16[4,32,1280]{2,1,0:T(8,128)(2,1)S(1)} %pad_maximum_fusion.4), channel_id=1, source_target_pairs={{0,2},{1,3},{2,0},{3,1},{4,6},{5,7},{6,4},{7,5},{8,10},{9,11},{10,... | collective-permute-start | bytes 983048 | tf_op jit(solution)/shard_map/ppermute | solution.py:167
  62.4 0.1 stack.46.starts
  62.5 8.2 %collective-permute-done.8.rest_3_ = bf16[4,32,1280]{2,1,0:T(8,128)(2,1)S(1)} collective-permute-done((bf16[4,32,1280]{2,1,0:T(8,128)(2,1)S(1)}, bf16[4,32,1280]{2,1,0:T(8,128)(2,1)S(1)}, u32[]{:S(2)}, u32[]{:S(2)}) %collective-permute-start.8) | collective-permute-done | bytes 327712 | tf_op jit(solution)/shard_map/ppermute | solution.py:167
  70.7 1.4 %join.1 = bf16[32,10240]{1,0:T(8,128)(2,1)} custom-call(s32[8]{0:T(128)S(1)} %stack.46.starts, bf16[4,32,1280]{2,1,0:T(8,128)(2,1)S(1)} %get-tuple-element.10.rest_0_, bf16[4,32,1280]{2,1,0:T(8,128)(2,1)S(1)} %copy-done.2, bf16[4,32,1280]{2,1,0:T(8,128)(2,1)S(1)} %collective-permute-done.7.rest_2_, bf16[4,32,1280]{2,1,0:T(8,128)(2,1)S(1)} %collective-permute-done.8.rest_3_), custom_call_target="tpu_custom_call" | custom-call | tf_op jit(solution)/shard_map/join/pallas_call | solution.py:75
  72.1 1.7 %sum.1 = f32[2,10,96,128]{3,2,1,0:T(8,128)} custom-call(s32[1]{0:T(128)} %bitcast.8.own, bf16[2,2,10,96,128]{4,3,2,1,0:T(8,128)(2,1)S(1)} %bitcast.17, f32[10,96,128]{2,1,0:T(8,128)S(1)} %get-tuple-element.13.mine), custom_call_target="tpu_custom_call" | custom-call | tf_op jit(solution)/shard_map/sum/pallas_call | solution.py:141
  (42 shorter events, 0.4 us)
Async XLA Ops:
  0.6 28.3 %copy-start = (s32[20,3]{0,1:T(4,128)S(1)}, s32[20,3]{0,1:T(4,128)}, u32[]{:S(2)}) copy-start(s32[20,3]{0,1:T(4,128)} %param.8) | copy-start | bytes 724
  0.6 5.1 %copy-start.9 = (bf16[96,20,128]{2,0,1:T(8,128)(2,1)S(1)}, bf16[96,20,128]{2,0,1:T(8,128)(2,1)}, u32[]{:S(2)}) copy-start(bf16[96,20,128]{2,0,1:T(8,128)(2,1)} %param.6) | copy-start | bytes 1474564
  0.7 11.6 %collective-permute-start = (bf16[32,2560]{1,0:T(8,128)(2,1)}, bf16[32,2560]{1,0:T(8,128)(2,1)S(1)}, u32[]{:S(2)}, u32[]{:S(2)}) collective-permute-start(bf16[32,2560]{1,0:T(8,128)(2,1)} %param.5), channel_id=1, source_target_pairs={{0,4},{1,5},{2,6},{3,7},{4,0},{5,1},{6,2},{7,3},{8,12},{9,13},{10,... | collective-permute-start | bytes 491528 | tf_op jit(solution)/shard_map/ppermute | solution.py:167
  5.6 10.6 %collective-permute-start.3 = (bf16[4,32,1280]{2,1,0:T(8,128)(2,1)S(1)}, bf16[4,32,1280]{2,1,0:T(8,128)(2,1)S(1)}, u32[]{:S(2)}, u32[]{:S(2)}) collective-permute-start(bf16[4,32,1280]{2,1,0:T(8,128)(2,1)S(1)} %get-tuple-element.9), channel_id=1, source_target_pairs={{0,4},{1,5},{2,6},{3,7},{4,0},{5,1},{6,2},{7,3},{8,12},{9,13},{10,... | collective-permute-start | bytes 983048 | tf_op jit(solution)/shard_map/ppermute | solution.py:167
  6.8 5.4 %copy-start.8 = (bf16[32,2560]{1,0:T(8,128)(2,1)S(1)}, bf16[32,2560]{1,0:T(8,128)(2,1)}, u32[]{:S(2)}) copy-start(bf16[32,2560]{1,0:T(8,128)(2,1)} %param.5) | copy-start | bytes 491524
  6.8 29.2 %all-to-all-start = ((bf16[4,10,96,128]{3,2,1,0:T(8,128)(2,1)}), bf16[4,10,96,128]{3,2,1,0:T(8,128)(2,1)S(1)}, u32[]{:S(2)}, u32[]{:S(2)}) async-start(bf16[4,10,96,128]{3,2,1,0:T(8,128)(2,1)} %bitcast.18), calls=%async_computation | async-start | bytes 1966080 | tf_op jit(solution)/shard_map/all_to_all | solution.py:178
  12.3 10.7 %collective-permute-start.1 = (bf16[64,2560]{1,0:T(8,128)(2,1)S(1)}, bf16[64,2560]{1,0:T(8,128)(2,1)S(1)}, u32[]{:S(2)}, u32[]{:S(2)}) collective-permute-start(bf16[64,2560]{1,0:T(8,128)(2,1)S(1)} %pad_maximum_fusion), channel_id=1, source_target_pairs={{0,2},{1,3},{2,0},{3,1},{4,6},{5,7},{6,4},{7,5},{8,10},{9,11},{10,... | collective-permute-start | bytes 983048 | tf_op jit(solution)/shard_map/ppermute | solution.py:167
  16.2 1.7 %copy-start.3 = (bf16[4,32,1280]{2,1,0:T(8,128)(2,1)}, bf16[4,32,1280]{2,1,0:T(8,128)(2,1)S(1)}, u32[]{:S(2)}) copy-start(bf16[4,32,1280]{2,1,0:T(8,128)(2,1)S(1)} %collective-permute-done.3.rest_1_) | copy-start | bytes 983044
  16.3 11.7 %collective-permute-start.4 = (bf16[4,32,1280]{2,1,0:T(8,128)(2,1)S(1)}, bf16[4,32,1280]{2,1,0:T(8,128)(2,1)S(1)}, u32[]{:S(2)}, u32[]{:S(2)}) collective-permute-start(bf16[4,32,1280]{2,1,0:T(8,128)(2,1)S(1)} %pad_maximum_fusion.1), channel_id=1, source_target_pairs={{0,2},{1,3},{2,0},{3,1},{4,6},{5,7},{6,4},{7,5},{8,10},{9,11},{10,... | collective-permute-start | bytes 983048 | tf_op jit(solution)/shard_map/ppermute | solution.py:167
  23.1 5.0 %slice-start.1 = ((bf16[4,32,1280]{2,1,0:T(8,128)(2,1)}), bf16[1,32,1280]{2,1,0:T(8,128)(2,1)S(1)}, s32[]{:S(2)}) async-start(bf16[4,32,1280]{2,1,0:T(8,128)(2,1)} %copy-done.3), calls=%async_computation.3 | async-start | bytes 163840 | tf_op jit(solution)/shard_map/slice | solution.py:171
  23.1 7.5 %collective-permute-start.2 = (bf16[128,2560]{1,0:T(8,128)(2,1)S(1)}, bf16[128,2560]{1,0:T(8,128)(2,1)}, u32[]{:S(2)}, u32[]{:S(2)}) collective-permute-start(bf16[128,2560]{1,0:T(8,128)(2,1)S(1)} %constant_dynamic-update-slice_fusion.near), channel_id=1, source_target_pairs={{0,1},{1,0},{2,3},{3,2},{4,5},{5,4},{6,7},{7,6},{8,9},{9,8},{10,11... | collective-permute-start | bytes 1966088 | tf_op jit(solution)/shard_map/ppermute | solution.py:167
  28.1 7.9 %copy-start.4 = (bf16[4,32,1280]{2,1,0:T(8,128)(2,1)S(1)}, bf16[4,32,1280]{2,1,0:T(8,128)(2,1)}, u32[]{:S(2)}) copy-start(bf16[4,32,1280]{2,1,0:T(8,128)(2,1)} %copy-done.3) | copy-start | bytes 983044
  28.1 1.7 %collective-permute-start.5 = (bf16[4,32,1280]{2,1,0:T(8,128)(2,1)S(1)}, bf16[4,32,1280]{2,1,0:T(8,128)(2,1)S(1)}, u32[]{:S(2)}, u32[]{:S(2)}) collective-permute-start(bf16[4,32,1280]{2,1,0:T(8,128)(2,1)S(1)} %pad_maximum_fusion.2), channel_id=1, source_target_pairs={{0,1},{1,0},{2,3},{3,2},{4,5},{5,4},{6,7},{7,6},{8,9},{9,8},{10,11... | collective-permute-start | bytes 983048 | tf_op jit(solution)/shard_map/ppermute | solution.py:167
  28.2 0.7 copy-start.10
  29.8 0.7 copy-start.6
  36.0 1.0 %copy-start.7 = (bf16[4,32,1280]{2,1,0:T(8,128)(2,1)S(1)}, bf16[4,32,1280]{2,1,0:T(8,128)(2,1)}, u32[]{:S(2)}) copy-start(bf16[4,32,1280]{2,1,0:T(8,128)(2,1)} %copy-done.6) | copy-start | bytes 983044
  40.6 0.9 %copy-start.5 = (bf16[4,10,96,128]{3,2,1,0:T(8,128)(2,1)}, bf16[4,10,96,128]{3,2,1,0:T(8,128)(2,1)S(1)}, u32[]{:S(2)}) copy-start(bf16[4,10,96,128]{3,2,1,0:T(8,128)(2,1)S(1)} %get-tuple-element.12) | copy-start | bytes 2949124
  41.5 17.5 %collective-permute-start.6 = (bf16[4,32,1280]{2,1,0:T(8,128)(2,1)}, bf16[4,32,1280]{2,1,0:T(8,128)(2,1)S(1)}, u32[]{:S(2)}, u32[]{:S(2)}) collective-permute-start(bf16[4,32,1280]{2,1,0:T(8,128)(2,1)} %get-tuple-element.11), channel_id=1, source_target_pairs={{0,4},{1,5},{2,6},{3,7},{4,0},{5,1},{6,2},{7,3},{8,12},{9,13},{10,... | collective-permute-start | bytes 983048 | tf_op jit(solution)/shard_map/ppermute | solution.py:167
  41.5 30.6 %all-to-all-start.1 = ((bf16[4,10,96,128]{3,2,1,0:T(8,128)(2,1)}), bf16[4,10,96,128]{3,2,1,0:T(8,128)(2,1)S(1)}, u32[]{:S(2)}, u32[]{:S(2)}) async-start(bf16[4,10,96,128]{3,2,1,0:T(8,128)(2,1)} %copy-done.5), calls=%async_computation.1 | async-start | bytes 1966080 | tf_op jit(solution)/shard_map/all_to_all | solution.py:203
  59.0 0.7 copy-start.1
  59.1 1.7 %collective-permute-start.7 = (bf16[4,32,1280]{2,1,0:T(8,128)(2,1)S(1)}, bf16[4,32,1280]{2,1,0:T(8,128)(2,1)S(1)}, u32[]{:S(2)}, u32[]{:S(2)}) collective-permute-start(bf16[4,32,1280]{2,1,0:T(8,128)(2,1)S(1)} %pad_maximum_fusion.3), channel_id=1, source_target_pairs={{0,1},{1,0},{2,3},{3,2},{4,5},{5,4},{6,7},{7,6},{8,9},{9,8},{10,11... | collective-permute-start | bytes 983048 | tf_op jit(solution)/shard_map/ppermute | solution.py:167
  59.8 1.0 %slice-start = ((bf16[4,32,1280]{2,1,0:T(8,128)(2,1)}), bf16[1,32,1280]{2,1,0:T(8,128)(2,1)S(1)}, s32[]{:S(2)}) async-start(bf16[4,32,1280]{2,1,0:T(8,128)(2,1)} %copy-done.1), calls=%async_computation.2 | async-start | bytes 163840 | tf_op jit(solution)/shard_map/slice | solution.py:171
  60.8 9.9 %copy-start.2 = (bf16[4,32,1280]{2,1,0:T(8,128)(2,1)S(1)}, bf16[4,32,1280]{2,1,0:T(8,128)(2,1)}, u32[]{:S(2)}) copy-start(bf16[4,32,1280]{2,1,0:T(8,128)(2,1)} %copy-done.1) | copy-start | bytes 983044
  60.9 9.8 %collective-permute-start.8 = (bf16[4,32,1280]{2,1,0:T(8,128)(2,1)S(1)}, bf16[4,32,1280]{2,1,0:T(8,128)(2,1)S(1)}, u32[]{:S(2)}, u32[]{:S(2)}) collective-permute-start(bf16[4,32,1280]{2,1,0:T(8,128)(2,1)S(1)} %pad_maximum_fusion.4), channel_id=1, source_target_pairs={{0,2},{1,3},{2,0},{3,1},{4,6},{5,7},{6,4},{7,5},{8,10},{9,11},{10,... | collective-permute-start | bytes 983048 | tf_op jit(solution)/shard_map/ppermute | solution.py:167

commit v7 on v6

v7 whole, which is shorter than its diff:
```python
import functools

import jax
import jax.numpy as jnp
from jax import lax
from jax.experimental import pallas as pl
from jax.experimental.pallas import tpu as pltpu
from jax.sharding import PartitionSpec as P

TILE = 128
SLOTS = 3
PAIR = 2
ROWS = 16
ROOT = 0.7978845608028654
CUBIC = 0.044715
ANYWHERE = pl.BlockSpec(memory_space=pl.ANY)
RESIDENT = pl.BlockSpec(memory_space=pltpu.VMEM)
SCALAR = pl.BlockSpec(memory_space=pltpu.SMEM)


def room(mib):
    return pltpu.CompilerParams(vmem_limit_bytes=mib * 2**20)


def gelu_and_derivative(v):
    square = v * v
    th = jnp.tanh(ROOT * (v + CUBIC * (square * v)))
    half = 0.5 * (1.0 + th)
    inner = ROOT * (1.0 + (3.0 * CUBIC) * square)
    return v * half, half + 0.5 * v * (1.0 - th * th) * inner


def copy_all(pairs, sems):
    copies = [pltpu.make_async_copy(source, target, sems.at[i]) for i, (source, target) in enumerate(pairs)]
    for copy in copies:
        copy.start()
    for copy in copies:
        copy.wait()


def row_chunks(rows):
    step = ROWS if rows % ROWS == 0 else rows
    return [pl.ds(r, step) for r in range(0, rows, step)]


def cut_kernel(starts, whole, *rest):
    outs, sems = rest[:-1], rest[-1]
    count, rows, width = outs[0].shape
    pairs = []
    for a in reversed(range(PAIR)):
        for b in range(count):
            span = pl.ds(pl.multiple_of(starts[a * count + b] * TILE, TILE), width)
            pairs += [(whole.at[r, span], outs[a].at[b, r]) for r in row_chunks(rows)]
    copy_all(pairs, sems)


def cut_call(starts, whole):
    count = starts.shape[0] // PAIR
    rows, width = whole.shape[0], whole.shape[1] // (PAIR * count)
    return pl.pallas_call(
        cut_kernel,
        out_shape=[jax.ShapeDtypeStruct((count, rows, width), whole.dtype)] * PAIR,
        in_specs=[SCALAR, ANYWHERE],
        out_specs=[ANYWHERE] * PAIR,
        scratch_shapes=[pltpu.SemaphoreType.DMA((PAIR * count * len(row_chunks(rows)),))],
        compiler_params=room(1),
        name="cut",
    )(starts, pltpu.with_memory_space_constraint(whole, pltpu.HBM))


def join_kernel(refs, starts, *rest):
    arrays, whole, sems = rest[:-2], rest[-2], rest[-1]
    rows, width = whole.shape[0], whole.shape[1] // len(refs)
    pairs = []
    for i, (a, b) in enumerate(refs):
        span = pl.ds(pl.multiple_of(starts[i] * TILE, TILE), width)
        pairs += [(arrays[a].at[b, r], whole.at[r, span]) for r in row_chunks(rows)]
    copy_all(pairs, sems)


def join_call(starts, arrays, refs):
    _, rows, width = arrays[0].shape
    return pl.pallas_call(
        functools.partial(join_kernel, refs),
        out_shape=jax.ShapeDtypeStruct((rows, len(refs) * width), arrays[0].dtype),
        in_specs=[SCALAR] + [ANYWHERE] * len(arrays),
        out_specs=ANYWHERE,
        scratch_shapes=[pltpu.SemaphoreType.DMA((len(refs) * len(row_chunks(rows)),))],
        compiler_params=room(1),
        name="join",
    )(starts, *arrays)


def pick(tiles, counts, tokens, s):
    picked = []
    for k in range(SLOTS):
        column = pl.multiple_of(tiles[s, k] * TILE, TILE)
        block = jnp.concatenate([piece[:, pl.ds(column, TILE)] for piece in tokens], axis=0)
        picked.append(jnp.where(k < counts[s], block, jnp.zeros_like(block)))
    return jnp.concatenate(picked, axis=1)


def forward_kernel(pieces, refs, tiles, counts, *rest):
    tokens, weights, arrays, outs, slopes = rest[:pieces], rest[pieces], rest[pieces + 1:-5], rest[-5:-1], rest[-1]
    shards, stripes = weights.shape[0], weights.shape[1]
    rows = arrays[0].shape[1]
    part = outs[0].shape[0]
    for s in range(stripes):
        cols = slice(s * TILE, (s + 1) * TILE)
        stack = jnp.concatenate([weights[f, s] for f in range(shards)], axis=0)
        pre = jnp.dot(pick(tiles, counts, tokens, s), stack, preferred_element_type=jnp.float32)
        act, slope = gelu_and_derivative(pre)
        act = act.astype(jnp.bfloat16)
        for i in range(len(refs)):
            outs[(i % PAIR) * 2 + i // PAIR // part][i // PAIR % part, :, cols] = act[i * rows:(i + 1) * rows]
        back = jnp.concatenate([arrays[a][b, :, cols] for a, b in refs], axis=0)
        slopes[:, cols] = (back.astype(jnp.float32) * slope).astype(jnp.bfloat16)


def forward_call(tiles, counts, tokens, weights, arrays, refs):
    _, rows, width = arrays[0].shape
    blocks = len(refs)
    return pl.pallas_call(
        functools.partial(forward_kernel, len(tokens), refs),
        out_shape=[jax.ShapeDtypeStruct((blocks // PAIR // 2, rows, width), jnp.bfloat16)] * 4
        + [jax.ShapeDtypeStruct((blocks * rows, width), jnp.bfloat16)],
        in_specs=[SCALAR] * 2 + [RESIDENT] * (len(tokens) + 1 + len(arrays)),
        out_specs=[RESIDENT] * 5,
        compiler_params=room(12),
        name="forward",
    )(tiles, counts, *tokens, weights, *arrays)


def backward_kernel(pieces, tiles, counts, own, *rest):
    tokens, slopes, grads, mine, term, sent, sems = rest[:pieces], *rest[pieces:]
    shards, stripes, size, _ = grads.shape
    span = pl.ds(pl.multiple_of(own[0] * size, size), size)
    copies = []
    for s in range(stripes):
        picked = pick(tiles, counts, tokens, s)
        slope = slopes[:, s * TILE:(s + 1) * TILE]
        term[s] = lax.dot_general(picked, slope, (((0,), (0,)), ((), ())), preferred_element_type=jnp.float32)
        for f in range(shards):
            sent[s, f] = term[s, f * size:(f + 1) * size].astype(sent.dtype)
        copies.append(pltpu.make_async_copy(sent.at[s], grads.at[:, s], sems.at[s]))
        copies[-1].start()
        mine[s] = term[s, span]
    for copy in copies:
        copy.wait()


def backward_call(tiles, counts, own, tokens, slopes, shards):
    stripes, size = slopes.shape[1] // TILE, SLOTS * TILE // shards
    return pl.pallas_call(
        functools.partial(backward_kernel, len(tokens)),
        out_shape=[pltpu.HBM((shards, stripes, size, TILE), jnp.bfloat16), jax.ShapeDtypeStruct((stripes, size, TILE), jnp.float32)],
        in_specs=[SCALAR] * 3 + [RESIDENT] * (len(tokens) + 1),
        out_specs=[pl.BlockSpec(memory_space=pltpu.HBM), RESIDENT],
        scratch_shapes=[
            pltpu.VMEM((stripes, SLOTS * TILE, TILE), jnp.float32),
            pltpu.VMEM((stripes, shards, size, TILE), jnp.bfloat16),
            pltpu.SemaphoreType.DMA((stripes,)),
        ],
        compiler_params=room(12),
        name="backward",
    )(tiles, counts, own, *tokens, slopes)


def sum_kernel(own, grads, mine, total, held, sems):
    shards, stripes = grads.shape[0], grads.shape[1]
    step = 5 if stripes % 5 == 0 else stripes
    copies = []
    for a in range(PAIR):
        for c in range(0, stripes, step):
            held[a, c:c + step] = sum(
                jnp.where(own[0] == f, mine[c:c + step], grads[f, c:c + step].astype(jnp.float32)) for f in range(a, shards, PAIR)
            )
            span = pl.ds(c, step)
            copies.append(pltpu.make_async_copy(held.at[a, span], total.at[a, span], sems.at[len(copies)]))
            copies[-1].start()
    for copy in copies:
        copy.wait()


def sum_call(own, grads, mine):
    shape = (PAIR,) + mine.shape
    return pl.pallas_call(
        sum_kernel,
        out_shape=jax.ShapeDtypeStruct(shape, jnp.float32),
        in_specs=[SCALAR, RESIDENT, RESIDENT],
        out_specs=ANYWHERE,
        scratch_shapes=[pltpu.VMEM(shape, jnp.float32), pltpu.SemaphoreType.DMA((PAIR * mine.shape[0],))],
        compiler_params=room(12),
        name="sum",
    )(own, grads, mine)


def take(arrays, refs):
    runs = []
    for a, b in refs:
        if runs and runs[-1][0] == a and runs[-1][2] == b:
            runs[-1][2] = b + 1
        else:
            runs.append([a, b, b + 1])
    pieces = [arrays[a] if (low, high) == (0, arrays[a].shape[0]) else arrays[a][low:high] for a, low, high in runs]
    return pieces[0] if len(pieces) == 1 else jnp.concatenate(pieces, axis=0)


def body(fsdp, tensor, tokens, tile_weights, cotangent, tile_list, tile_counts):
    z, t = lax.axis_index("fsdp"), lax.axis_index("tensor")
    half = z % PAIR
    size, stripes = tile_weights.shape[0], tile_weights.shape[1]
    share = stripes // PAIR
    whole_tiles = size % ROWS == 0
    bits = [1 << i for i in reversed(range((tensor - 1).bit_length()))]

    def swap(value, dz, dt):
        pairs = [(a * tensor + b, (a ^ dz) * tensor + (b ^ dt)) for a in range(fsdp) for b in range(tensor)]
        return lax.ppermute(value, ("fsdp", "tensor"), pairs)

    def exchange(arrays, groups, steps):
        for bit in steps:
            count = len(groups[0]) // 2
            arrays = arrays + [swap(take(arrays, [ref for group in groups for ref in group[count:]]), 0, bit)]
            new = [[(len(arrays) - 1, i * count + j) for j in range(count)] for i in range(len(groups))]
            groups = [group[:count] for group in groups] + new
        return arrays, [group[0] for group in groups]

    def interleave(home, away):
        shifted = [(a + len(home[0]), b) for a, b in away[1]]
        return home[0] + away[0], [ref for two in zip(home[1], shifted) for ref in two]

    by_stripe = jnp.transpose(tile_weights, (1, 0, 2))
    outgoing = jnp.tile(by_stripe.reshape(PAIR, share, size, TILE), (fsdp // PAIR, 1, 1, 1))
    weights = lax.all_to_all(outgoing, "fsdp", split_axis=0, concat_axis=0, tiled=True)
    own = z.reshape(1).astype(jnp.int32)
    if not whole_tiles:
        weights = weights.transpose(1, 0, 2, 3).reshape(1, share, fsdp * size, TILE)

    pieces, order = [jnp.concatenate([tokens, swap(tokens, 1, 0)], axis=0)], [0]
    for bit in bits:
        pieces = pieces + [swap(piece, 0, bit) for piece in pieces]
        order = order + [b ^ bit for b in order]

    starts = jnp.stack([(t ^ b) * stripes + (half ^ a) * share for a in range(PAIR) for b in range(tensor)]).astype(jnp.int32)
    stay, leave = cut_call(starts, cotangent)
    all_blocks = [[(0, b) for b in range(tensor)]]
    arrays, refs = interleave(exchange([stay], all_blocks, bits), exchange([swap(leave, 1, 0)], all_blocks, bits))

    tiles = lax.dynamic_slice_in_dim(tile_list, half * share, share, 0)
    counts = lax.dynamic_slice_in_dim(tile_counts, half * share, share, 0)
    home_near, home_far, away_near, away_far, slopes = forward_call(tiles, counts, pieces, weights, arrays, refs)

    part = tensor // 2
    two_arrays = [[(i // part, i % part) for i in range(tensor)]]
    steps = list(reversed(bits))
    arrays, refs = interleave(
        exchange([home_near, home_far], two_arrays, steps), exchange([swap(away_near, 1, 0), swap(away_far, 1, 0)], two_arrays, steps)
    )
    origins = [0]
    for bit in steps:
        origins = origins + [b ^ bit for b in origins]
    starts = jnp.stack([(t ^ b) * stripes + (half ^ a) * share for b in origins for a in range(PAIR)]).astype(jnp.int32)
    activations = join_call(starts, arrays, refs)

    if whole_tiles:
        grads, mine = backward_call(tiles, counts, own, pieces, slopes, fsdp)
    else:
        grads, mine = backward_call(tiles, counts, own * 0, pieces, slopes, 1)
        grads = grads.reshape(share, fsdp, size, TILE).transpose(1, 0, 2, 3)
        mine = lax.dynamic_index_in_dim(mine.reshape(share, fsdp, size, TILE), z, 1, keepdims=False)
    total = sum_call(own, lax.all_to_all(grads, "fsdp", split_axis=0, concat_axis=0, tiled=True), mine)
    return activations, total.reshape(stripes, size, TILE).transpose(1, 0, 2)


def solution(mesh):
    return jax.shard_map(
        functools.partial(body, mesh.shape["fsdp"], mesh.shape["tensor"]),
        mesh=mesh,
        in_specs=(
            P(("member", "fsdp", "tensor"), None),
            P(("member", "fsdp"), "tensor", None),
            P(("member", "fsdp", "tensor"), None),
            P("tensor", None),
            P("tensor"),
        ),
        out_specs=(P(("member", "fsdp", "tensor"), None), P(("member", "fsdp"), "tensor", None)),
        check_vma=False,
    )
```

time: 74.2 us -> 91.7 us (1.24)
  waiting for transfers between devices: 41.6 us -> 48.6 us
  starting transfers between devices: 17.1 us -> 23.7 us
  local copies, waits for them, and re-layouts: 5.56 us -> 7.78 us
  other arithmetic: 0.18 us -> 1.4 us
    ppermute x9 -> x15, waiting for transfers between devices: 36.2 us -> 48.6 us  [swap(): return lax.ppermute(value, ('fsdp', 'tensor'), pairs)]
    all_to_all x1, waiting for transfers between devices: 5.44 us -> 0.01 us  [body(): lax.all_to_all(outgoing, 'fsdp', split_axis=0, concat_axis=0, tiled=True)]
    ppermute x9 -> x15, starting transfers between devices: 8.16 us -> 13.3 us  [swap(): return lax.ppermute(value, ('fsdp', 'tensor'), pairs)]
    concatenate x5 -> x4, other arithmetic: 0.18 us -> 1.4 us  [take(): return pieces[0] if len(pieces) == 1 else jnp.concatenate(pieces, axis=0)]
    all_to_all x1, starting transfers between devices: 5.4 us -> 6.45 us  [body(): lax.all_to_all(outgoing, 'fsdp', split_axis=0, concat_axis=0, tiled=True)]
    another operation x1, local copies, waits for them, and re-layouts: 1.1 us -> 2.13 us  [body(): jnp.tile(by_stripe.reshape(PAIR, share, size, TILE), (fsdp // PAIR, 1, 1,...]
    pallas_call x3 -> x4, Pallas kernels: 6.68 us -> 7.15 us  [the longest x1 2.26 us: backward_call(): pl.pallas_call(functools.partial(backward_kernel, len(tokens)), out_shape...]
    unnamed x25 -> x36, local copies, waits for them, and re-layouts: 4.03 us -> 4.39 us
  transfers between devices with their start and end apart: 11 -> 17, of which waited for: 8 -> 7; matrix products, arithmetic and copies ran while one was open for 2% -> 2% of each run, Pallas kernels for 4% -> 4%
where the time goes in v7:
time: 91.7 us; the launch traced here: 91.2 us
  waiting for transfers between devices  48.6 us (53%)
  starting transfers between devices  23.7 us (26%)
  Pallas kernels  8.91 us (10%)
  local copies, waits for them, and re-layouts  7.78 us (8%)
  other arithmetic  1.4 us (2%)
    ppermute x15, waiting for transfers between devices, swap(): return lax.ppermute(value, ('fsdp', 'tensor'), pairs)  48.6 us
    ppermute x15, starting transfers between devices, swap(): return lax.ppermute(value, ('fsdp', 'tensor'), pairs)  13.3 us
    all_to_all x1, starting transfers between devices, body(): lax.all_to_all(outgoing, 'fsdp', split_axis=0, concat_axis=0, tiled=True)  6.45 us
    unnamed x36, local copies, waits for them, and re-layouts  4.39 us
    all_to_all x1, starting transfers between devices, body(): lax.all_to_all(grads, 'fsdp', split_axis=0, concat_axis=0, tiled=True)  3.87 us
    pallas_call x1, Pallas kernels, backward_call(): pl.pallas_call(functools.partial(backward_kernel, len(tokens)), out_shape...  2.26 us
    pallas_call x1, Pallas kernels, forward_call(): pl.pallas_call(functools.partial(forward_kernel, len(tokens), refs), out_...  2.24 us
    another operation x1, local copies, waits for them, and re-layouts, body(): jnp.tile(by_stripe.reshape(PAIR, share, size, TILE), (fsdp // PAIR, 1, 1,...  2.13 us
  transfers between devices with their start and end apart: 17, of which 7 were waited for; matrix products, arithmetic and copies ran while one was open for 2% of the time, Pallas kernels for 4%

profile of v7, /device:TPU:0, one launch (start us, length us, event | category | flops | bytes accessed | tf_op | source)
XLA Modules:
  0.0 91.2 jit_solution(15233037811107663872)
XLA Ops:
  0.6 2.1 %tile.11 = bf16[2,2,10,96,128]{4,3,2,1,0:T(8,128)(2,1)} broadcast(bf16[2,10,96,128]{3,2,1,0:T(8,128)(2,1)} %bitcast.17), dimensions={1,2,3,4} | broadcast | bytes 1474560 | tf_op jit(solution)/shard_map/tile | solution.py:234
  2.8 6.4 %all-to-all-start = ((bf16[4,10,96,128]{3,2,1,0:T(8,128)(2,1)}), bf16[4,10,96,128]{3,2,1,0:T(8,128)(2,1)S(1)}, u32[]{:S(2)}, u32[]{:S(2)}) async-start(bf16[4,10,96,128]{3,2,1,0:T(8,128)(2,1)} %bitcast.10), calls=%async_computation | async-start | bytes 1966080 | tf_op jit(solution)/shard_map/all_to_all | solution.py:235
  9.2 2.0 %collective-permute-start = (bf16[32,2560]{1,0:T(8,128)(2,1)S(1)}, bf16[32,2560]{1,0:T(8,128)(2,1)S(1)}, u32[]{:S(2)}, u32[]{:S(2)}) collective-permute-start(bf16[32,2560]{1,0:T(8,128)(2,1)S(1)} %copy-done.15), channel_id=1, source_target_pairs={{0,4},{1,5},{2,6},{3,7},{4,0},{5,1},{6,2},{7,3},{8,12},{9,13},{10,... | collective-permute-start | bytes 491528 | tf_op jit(solution)/shard_map/ppermute | solution.py:219
  11.3 1.8 %cut.1 = (bf16[4,32,1280]{2,1,0:T(8,128)(2,1)S(1)}, bf16[4,32,1280]{2,1,0:T(8,128)(2,1)S(1)}) custom-call(s32[8]{0:T(128)S(1)} %stack.47.starts, bf16[32,10240]{1,0:T(8,128)(2,1)} %whole.1), custom_call_target="tpu_custom_call" | custom-call | tf_op jit(solution)/shard_map/cut/pallas_call | solution.py:60
  13.1 1.6 %collective-permute-start.4 = (bf16[2,32,1280]{2,1,0:T(8,128)(2,1)S(1)}, bf16[2,32,1280]{2,1,0:T(8,128)(2,1)S(1)}, u32[]{:S(2)}, u32[]{:S(2)}) collective-permute-start(bf16[2,32,1280]{2,1,0:T(8,128)(2,1)S(1)} %slice.30), channel_id=1, source_target_pairs={{0,2},{1,3},{2,0},{3,1},{4,6},{5,7},{6,4},{7,5},{8,10},{9,11},{10,... | collective-permute-start | bytes 491528 | tf_op jit(solution)/shard_map/ppermute | solution.py:219
  14.7 15.2 %collective-permute-done = bf16[32,2560]{1,0:T(8,128)(2,1)S(1)} collective-permute-done((bf16[32,2560]{1,0:T(8,128)(2,1)S(1)}, bf16[32,2560]{1,0:T(8,128)(2,1)S(1)}, u32[]{:S(2)}, u32[]{:S(2)}) %collective-permute-start) | collective-permute-done | bytes 163872 | tf_op jit(solution)/shard_map/ppermute | solution.py:219
  29.9 1.6 %collective-permute-start.1 = (bf16[64,2560]{1,0:T(8,128)(2,1)S(1)}, bf16[64,2560]{1,0:T(8,128)(2,1)S(1)}, u32[]{:S(2)}, u32[]{:S(2)}) collective-permute-start(bf16[64,2560]{1,0:T(8,128)(2,1)S(1)} %constant_dynamic-update-slice_fusion.rest_0_), channel_id=1, source_target_pairs={{0,2},{1,3},{2,0},{3,1},{4,6},{5,7},{6,4},{7,5},{8,10},{9,11},{10,... | collective-permute-start | bytes 983048 | tf_op jit(solution)/shard_map/ppermute | solution.py:219
  31.5 0.7 copy-done.5
  32.2 5.8 %collective-permute-done.6.rest_8_ = bf16[4,32,1280]{2,1,0:T(8,128)(2,1)S(1)} collective-permute-done((bf16[4,32,1280]{2,1,0:T(8,128)(2,1)S(1)}, bf16[4,32,1280]{2,1,0:T(8,128)(2,1)S(1)}, u32[]{:S(2)}, u32[]{:S(2)}) %collective-permute-start.6) | collective-permute-done | bytes 327712 | tf_op jit(solution)/shard_map/ppermute | solution.py:219
  37.9 1.6 %collective-permute-start.7 = (bf16[2,32,1280]{2,1,0:T(8,128)(2,1)S(1)}, bf16[2,32,1280]{2,1,0:T(8,128)(2,1)S(1)}, u32[]{:S(2)}, u32[]{:S(2)}) collective-permute-start(bf16[2,32,1280]{2,1,0:T(8,128)(2,1)S(1)} %slice.41), channel_id=1, source_target_pairs={{0,2},{1,3},{2,0},{3,1},{4,6},{5,7},{6,4},{7,5},{8,10},{9,11},{10,... | collective-permute-start | bytes 491528 | tf_op jit(solution)/shard_map/ppermute | solution.py:219
  39.5 0.7 pad_maximum_fusion
  40.2 0.6 collective-permute-start.3
  40.8 2.5 %collective-permute-done.7.rest_9_ = bf16[2,32,1280]{2,1,0:T(8,128)(2,1)S(1)} collective-permute-done((bf16[2,32,1280]{2,1,0:T(8,128)(2,1)S(1)}, bf16[2,32,1280]{2,1,0:T(8,128)(2,1)S(1)}, u32[]{:S(2)}, u32[]{:S(2)}) %collective-permute-start.7) | collective-permute-done | bytes 163872 | tf_op jit(solution)/shard_map/ppermute | solution.py:219
  43.3 0.7 pad_maximum_fusion.1
  44.0 0.7 copy-done.16
  44.9 0.7 copy-done.9
  45.8 0.9 copy-done.10
  46.7 2.2 %forward.1 = (bf16[2,32,1280]{2,1,0:T(8,128)(2,1)S(1)}, bf16[2,32,1280]{2,1,0:T(8,128)(2,1)S(1)}, bf16[2,32,1280]{2,1,0:T(8,128)(2,1)S(1)}, bf16[2,32,1280]{2,1,0:T(8,128)(2,1)S(1)}, bf16[256,1280]{1,0:T(8,128)(2,1)S(1)}) custom-call(s32[10,3]{1,0:T(8,128)S(1)} %copy.8.tiles, s32[10]{0:T(128)S(1)} %dynamic_slice.7.counts, ...), custom_call_target="tpu_custom_call" | custom-call | tf_op jit(solution)/shard_map/forward/pallas_call | solution.py:123
  48.9 0.7 copy-done.7
  49.6 2.3 %backward.1 = (bf16[4,10,96,128]{3,2,1,0:T(8,128)(2,1)}, f32[10,96,128]{2,1,0:T(8,128)S(1)}) custom-call(s32[10,3]{1,0:T(8,128)S(1)} %copy.8.tiles, s32[10]{0:T(128)S(1)} %dynamic_slice.7.counts, s32[1]{0:T(128)} %bitcast.11.own, bf16[64,2560]{1,0:T(8,128)(2,1)S(1)} %constant_dynamic-update-slice_fusion.rest_0_, ...), custom_call_target="tpu_custom_call" | custom-call | tf_op jit(solution)/shard_map/backward/pallas_call | solution.py:154
  51.9 3.9 %all-to-all-start.1 = ((bf16[4,10,96,128]{3,2,1,0:T(8,128)(2,1)}), bf16[4,10,96,128]{3,2,1,0:T(8,128)(2,1)S(1)}, u32[]{:S(2)}, u32[]{:S(2)}) async-start(bf16[4,10,96,128]{3,2,1,0:T(8,128)(2,1)} %get-tuple-element.18), calls=%async_computation.1 | async-start | bytes 1966080 | tf_op jit(solution)/shard_map/all_to_all | solution.py:272
  55.8 2.0 %collective-permute-start.12 = (bf16[2,32,1280]{2,1,0:T(8,128)(2,1)S(1)}, bf16[2,32,1280]{2,1,0:T(8,128)(2,1)S(1)}, u32[]{:S(2)}, u32[]{:S(2)}) collective-permute-start(bf16[2,32,1280]{2,1,0:T(8,128)(2,1)S(1)} %copy-done.14), channel_id=1, source_target_pairs={{0,4},{1,5},{2,6},{3,7},{4,0},{5,1},{6,2},{7,3},{8,12},{9,13},{10,... | collective-permute-start | bytes 491528 | tf_op jit(solution)/shard_map/ppermute | solution.py:219
  57.8 0.9 collective-permute-start.11
  58.7 17.6 %collective-permute-done.12.rest_5_ = bf16[2,32,1280]{2,1,0:T(8,128)(2,1)S(1)} collective-permute-done((bf16[2,32,1280]{2,1,0:T(8,128)(2,1)S(1)}, bf16[2,32,1280]{2,1,0:T(8,128)(2,1)S(1)}, u32[]{:S(2)}, u32[]{:S(2)}) %collective-permute-start.12) | collective-permute-done | bytes 163872 | tf_op jit(solution)/shard_map/ppermute | solution.py:219
  76.4 1.6 %collective-permute-start.10 = (bf16[2,32,1280]{2,1,0:T(8,128)(2,1)S(1)}, bf16[2,32,1280]{2,1,0:T(8,128)(2,1)S(1)}, u32[]{:S(2)}, u32[]{:S(2)}) collective-permute-start(bf16[2,32,1280]{2,1,0:T(8,128)(2,1)S(1)} %pad_maximum_fusion.2), channel_id=1, source_target_pairs={{0,2},{1,3},{2,0},{3,1},{4,6},{5,7},{6,4},{7,5},{8,10},{9,11},{10,... | collective-permute-start | bytes 491528 | tf_op jit(solution)/shard_map/ppermute | solution.py:219
  78.0 3.6 %collective-permute-done.11.rest_4_ = bf16[2,32,1280]{2,1,0:T(8,128)(2,1)S(1)} collective-permute-done((bf16[2,32,1280]{2,1,0:T(8,128)(2,1)S(1)}, bf16[2,32,1280]{2,1,0:T(8,128)(2,1)S(1)}, u32[]{:S(2)}, u32[]{:S(2)}) %collective-permute-start.11) | collective-permute-done | bytes 163872 | tf_op jit(solution)/shard_map/ppermute | solution.py:219
  81.5 0.7 copy-done.3
  82.2 0.9 slice-done.1
  83.1 1.6 %collective-permute-start.14 = (bf16[2,32,1280]{2,1,0:T(8,128)(2,1)S(1)}, bf16[2,32,1280]{2,1,0:T(8,128)(2,1)S(1)}, u32[]{:S(2)}, u32[]{:S(2)}) collective-permute-start(bf16[2,32,1280]{2,1,0:T(8,128)(2,1)S(1)} %pad_maximum_fusion.3), channel_id=1, source_target_pairs={{0,2},{1,3},{2,0},{3,1},{4,6},{5,7},{6,4},{7,5},{8,10},{9,11},{10,... | collective-permute-start | bytes 491528 | tf_op jit(solution)/shard_map/ppermute | solution.py:219
  84.8 3.7 %collective-permute-done.14.rest_7_ = bf16[2,32,1280]{2,1,0:T(8,128)(2,1)S(1)} collective-permute-done((bf16[2,32,1280]{2,1,0:T(8,128)(2,1)S(1)}, bf16[2,32,1280]{2,1,0:T(8,128)(2,1)S(1)}, u32[]{:S(2)}, u32[]{:S(2)}) %collective-permute-start.14) | collective-permute-done | bytes 163872 | tf_op jit(solution)/shard_map/ppermute | solution.py:219
  88.5 1.5 %join.1 = bf16[32,10240]{1,0:T(8,128)(2,1)} custom-call(s32[8]{0:T(128)S(1)} %stack.46.starts, bf16[2,32,1280]{2,1,0:T(8,128)(2,1)S(1)} %get-tuple-element.13.rest_0_, bf16[2,32,1280]{2,1,0:T(8,128)(2,1)S(1)} %copy-done.8, bf16[2,32,1280]{2,1,0:T(8,128)(2,1)S(1)} %collective-permute-done.9.rest_2_, bf16[2,32,1280]{2,1,0:T(8,128)(2,1)S(1)} %collective-permute-done.10.rest_3_, ...), custom_call_target="tpu_custom_call" | custom-call | tf_op jit(solution)/shard_map/join/pallas_call | solution.py:83
  90.0 1.2 %sum.1 = f32[2,10,96,128]{3,2,1,0:T(8,128)} custom-call(s32[1]{0:T(128)} %bitcast.11.own, bf16[4,10,96,128]{3,2,1,0:T(8,128)(2,1)S(1)} %all-to-all-done.1.grads, f32[10,96,128]{2,1,0:T(8,128)S(1)} %get-tuple-element.19.mine), custom_call_target="tpu_custom_call" | custom-call | tf_op jit(solution)/shard_map/sum/pallas_call | solution.py:187
  (66 shorter events, 0.8 us)
Async XLA Ops:
  0.6 44.1 %copy-start = (s32[20,3]{0,1:T(4,128)S(1)}, s32[20,3]{0,1:T(4,128)}, u32[]{:S(2)}) copy-start(s32[20,3]{0,1:T(4,128)} %param.8) | copy-start | bytes 724
  2.8 6.5 %copy-start.15 = (bf16[32,2560]{1,0:T(8,128)(2,1)S(1)}, bf16[32,2560]{1,0:T(8,128)(2,1)}, u32[]{:S(2)}) copy-start(bf16[32,2560]{1,0:T(8,128)(2,1)} %param.5) | copy-start | bytes 491524
  2.8 43.0 %all-to-all-start = ((bf16[4,10,96,128]{3,2,1,0:T(8,128)(2,1)}), bf16[4,10,96,128]{3,2,1,0:T(8,128)(2,1)S(1)}, u32[]{:S(2)}, u32[]{:S(2)}) async-start(bf16[4,10,96,128]{3,2,1,0:T(8,128)(2,1)} %bitcast.10), calls=%async_computation | async-start | bytes 1966080 | tf_op jit(solution)/shard_map/all_to_all | solution.py:235
  9.2 20.7 %collective-permute-start = (bf16[32,2560]{1,0:T(8,128)(2,1)S(1)}, bf16[32,2560]{1,0:T(8,128)(2,1)S(1)}, u32[]{:S(2)}, u32[]{:S(2)}) collective-permute-start(bf16[32,2560]{1,0:T(8,128)(2,1)S(1)} %copy-done.15), channel_id=1, source_target_pairs={{0,4},{1,5},{2,6},{3,7},{4,0},{5,1},{6,2},{7,3},{8,12},{9,13},{10,... | collective-permute-start | bytes 491528 | tf_op jit(solution)/shard_map/ppermute | solution.py:219
  13.1 18.3 %collective-permute-start.4 = (bf16[2,32,1280]{2,1,0:T(8,128)(2,1)S(1)}, bf16[2,32,1280]{2,1,0:T(8,128)(2,1)S(1)}, u32[]{:S(2)}, u32[]{:S(2)}) collective-permute-start(bf16[2,32,1280]{2,1,0:T(8,128)(2,1)S(1)} %slice.30), channel_id=1, source_target_pairs={{0,2},{1,3},{2,0},{3,1},{4,6},{5,7},{6,4},{7,5},{8,10},{9,11},{10,... | collective-permute-start | bytes 491528 | tf_op jit(solution)/shard_map/ppermute | solution.py:219
  14.7 23.2 %collective-permute-start.6 = (bf16[4,32,1280]{2,1,0:T(8,128)(2,1)S(1)}, bf16[4,32,1280]{2,1,0:T(8,128)(2,1)S(1)}, u32[]{:S(2)}, u32[]{:S(2)}) collective-permute-start(bf16[4,32,1280]{2,1,0:T(8,128)(2,1)S(1)} %get-tuple-element.12), channel_id=1, source_target_pairs={{0,4},{1,5},{2,6},{3,7},{4,0},{5,1},{6,2},{7,3},{8,12},{9,13},{10,... | collective-permute-start | bytes 983048 | tf_op jit(solution)/shard_map/ppermute | solution.py:219
  29.9 10.3 %collective-permute-start.1 = (bf16[64,2560]{1,0:T(8,128)(2,1)S(1)}, bf16[64,2560]{1,0:T(8,128)(2,1)S(1)}, u32[]{:S(2)}, u32[]{:S(2)}) collective-permute-start(bf16[64,2560]{1,0:T(8,128)(2,1)S(1)} %constant_dynamic-update-slice_fusion.rest_0_), channel_id=1, source_target_pairs={{0,2},{1,3},{2,0},{3,1},{4,6},{5,7},{6,4},{7,5},{8,10},{9,11},{10,... | collective-permute-start | bytes 983048 | tf_op jit(solution)/shard_map/ppermute | solution.py:219
  31.5 14.1 %collective-permute-start.2 = (bf16[64,2560]{1,0:T(8,128)(2,1)S(1)}, bf16[64,2560]{1,0:T(8,128)(2,1)S(1)}, u32[]{:S(2)}, u32[]{:S(2)}) collective-permute-start(bf16[64,2560]{1,0:T(8,128)(2,1)S(1)} %constant_dynamic-update-slice_fusion.rest_0_), channel_id=1, source_target_pairs={{0,1},{1,0},{2,3},{3,2},{4,5},{5,4},{6,7},{7,6},{8,9},{9,8},{10,11... | collective-permute-start | bytes 983048 | tf_op jit(solution)/shard_map/ppermute | solution.py:219
  37.9 2.3 %copy-start.1 = (bf16[4,32,1280]{2,1,0:T(8,128)(2,1)}, bf16[4,32,1280]{2,1,0:T(8,128)(2,1)S(1)}, u32[]{:S(2)}) copy-start(bf16[4,32,1280]{2,1,0:T(8,128)(2,1)S(1)} %collective-permute-done.6.rest_8_) | copy-start | bytes 983044
  37.9 1.6 %slice-start.2 = ((bf16[2,32,1280]{2,1,0:T(8,128)(2,1)}), bf16[1,32,1280]{2,1,0:T(8,128)(2,1)S(1)}, s32[]{:S(2)}) async-start(bf16[2,32,1280]{2,1,0:T(8,128)(2,1)} %copy-done.5), calls=%async_computation.4 | async-start | bytes 163840 | tf_op jit(solution)/shard_map/slice | solution.py:205
  37.9 5.4 %collective-permute-start.7 = (bf16[2,32,1280]{2,1,0:T(8,128)(2,1)S(1)}, bf16[2,32,1280]{2,1,0:T(8,128)(2,1)S(1)}, u32[]{:S(2)}, u32[]{:S(2)}) collective-permute-start(bf16[2,32,1280]{2,1,0:T(8,128)(2,1)S(1)} %slice.41), channel_id=1, source_target_pairs={{0,2},{1,3},{2,0},{3,1},{4,6},{5,7},{6,4},{7,5},{8,10},{9,11},{10,... | collective-permute-start | bytes 491528 | tf_op jit(solution)/shard_map/ppermute | solution.py:219
  40.2 4.7 %collective-permute-start.5 = (bf16[2,32,1280]{2,1,0:T(8,128)(2,1)}, bf16[2,32,1280]{2,1,0:T(8,128)(2,1)S(1)}, u32[]{:S(2)}, u32[]{:S(2)}) collective-permute-start(bf16[2,32,1280]{2,1,0:T(8,128)(2,1)} %pad_maximum_fusion), channel_id=1, source_target_pairs={{0,1},{1,0},{2,3},{3,2},{4,5},{5,4},{6,7},{7,6},{8,9},{9,8},{10,11... | collective-permute-start | bytes 491528 | tf_op jit(solution)/shard_map/ppermute | solution.py:219
  40.2 5.6 %copy-start.6 = (bf16[2,32,1280]{2,1,0:T(8,128)(2,1)S(1)}, bf16[2,32,1280]{2,1,0:T(8,128)(2,1)}, u32[]{:S(2)}) copy-start(bf16[2,32,1280]{2,1,0:T(8,128)(2,1)} %copy-done.5) | copy-start | bytes 491524
  40.2 3.1 %slice-start = ((bf16[4,32,1280]{2,1,0:T(8,128)(2,1)}), bf16[1,32,1280]{2,1,0:T(8,128)(2,1)S(1)}, s32[]{:S(2)}) async-start(bf16[4,32,1280]{2,1,0:T(8,128)(2,1)} %copy-done.1), calls=%async_computation.2 | async-start | bytes 163840 | tf_op jit(solution)/shard_map/slice | solution.py:205
  40.2 5.6 %copy-start.2 = (bf16[4,32,1280]{2,1,0:T(8,128)(2,1)S(1)}, bf16[4,32,1280]{2,1,0:T(8,128)(2,1)}, u32[]{:S(2)}) copy-start(bf16[4,32,1280]{2,1,0:T(8,128)(2,1)} %copy-done.1) | copy-start | bytes 983044
  40.2 5.5 %collective-permute-start.3 = (bf16[64,2560]{1,0:T(8,128)(2,1)S(1)}, bf16[64,2560]{1,0:T(8,128)(2,1)S(1)}, u32[]{:S(2)}, u32[]{:S(2)}) collective-permute-start(bf16[64,2560]{1,0:T(8,128)(2,1)S(1)} %collective-permute-done.1.rest_1_), channel_id=1, source_target_pairs={{0,1},{1,0},{2,3},{3,2},{4,5},{5,4},{6,7},{7,6},{8,9},{9,8},{10,11... | collective-permute-start | bytes 983048 | tf_op jit(solution)/shard_map/ppermute | solution.py:219
  44.0 1.7 %collective-permute-start.8 = (bf16[2,32,1280]{2,1,0:T(8,128)(2,1)}, bf16[2,32,1280]{2,1,0:T(8,128)(2,1)}, u32[]{:S(2)}, u32[]{:S(2)}) collective-permute-start(bf16[2,32,1280]{2,1,0:T(8,128)(2,1)} %pad_maximum_fusion.1), channel_id=1, source_target_pairs={{0,1},{1,0},{2,3},{3,2},{4,5},{5,4},{6,7},{7,6},{8,9},{9,8},{10,11... | collective-permute-start | bytes 491528 | tf_op jit(solution)/shard_map/ppermute | solution.py:219
  45.8 0.9 %copy-start.10 = (bf16[2,32,1280]{2,1,0:T(8,128)(2,1)S(1)}, bf16[2,32,1280]{2,1,0:T(8,128)(2,1)}, u32[]{:S(2)}) copy-start(bf16[2,32,1280]{2,1,0:T(8,128)(2,1)} %copy-done.9) | copy-start | bytes 491524
  49.6 2.3 %copy-start.11 = (bf16[2,32,1280]{2,1,0:T(8,128)(2,1)}, bf16[2,32,1280]{2,1,0:T(8,128)(2,1)S(1)}, u32[]{:S(2)}) copy-start(bf16[2,32,1280]{2,1,0:T(8,128)(2,1)S(1)} %get-tuple-element.15) | copy-start | bytes 491524
  49.6 2.3 %copy-start.13 = (bf16[2,32,1280]{2,1,0:T(8,128)(2,1)}, bf16[2,32,1280]{2,1,0:T(8,128)(2,1)S(1)}, u32[]{:S(2)}) copy-start(bf16[2,32,1280]{2,1,0:T(8,128)(2,1)S(1)} %get-tuple-element.16) | copy-start | bytes 491524
  51.9 3.9 %copy-start.14 = (bf16[2,32,1280]{2,1,0:T(8,128)(2,1)S(1)}, bf16[2,32,1280]{2,1,0:T(8,128)(2,1)}, u32[]{:S(2)}) copy-start(bf16[2,32,1280]{2,1,0:T(8,128)(2,1)} %copy-done.13) | copy-start | bytes 491524
  51.9 5.9 %copy-start.8 = (bf16[2,32,1280]{2,1,0:T(8,128)(2,1)S(1)}, bf16[2,32,1280]{2,1,0:T(8,128)(2,1)}, u32[]{:S(2)}) copy-start(bf16[2,32,1280]{2,1,0:T(8,128)(2,1)} %copy-done.7) | copy-start | bytes 491524
  51.9 38.1 %all-to-all-start.1 = ((bf16[4,10,96,128]{3,2,1,0:T(8,128)(2,1)}), bf16[4,10,96,128]{3,2,1,0:T(8,128)(2,1)S(1)}, u32[]{:S(2)}, u32[]{:S(2)}) async-start(bf16[4,10,96,128]{3,2,1,0:T(8,128)(2,1)} %get-tuple-element.18), calls=%async_computation.1 | async-start | bytes 1966080 | tf_op jit(solution)/shard_map/all_to_all | solution.py:272
  55.8 2.0 %copy-start.12 = (bf16[2,32,1280]{2,1,0:T(8,128)(2,1)S(1)}, bf16[2,32,1280]{2,1,0:T(8,128)(2,1)}, u32[]{:S(2)}) copy-start(bf16[2,32,1280]{2,1,0:T(8,128)(2,1)} %copy-done.11) | copy-start | bytes 491524
  55.8 20.6 %collective-permute-start.12 = (bf16[2,32,1280]{2,1,0:T(8,128)(2,1)S(1)}, bf16[2,32,1280]{2,1,0:T(8,128)(2,1)S(1)}, u32[]{:S(2)}, u32[]{:S(2)}) collective-permute-start(bf16[2,32,1280]{2,1,0:T(8,128)(2,1)S(1)} %copy-done.14), channel_id=1, source_target_pairs={{0,4},{1,5},{2,6},{3,7},{4,0},{5,1},{6,2},{7,3},{8,12},{9,13},{10,... | collective-permute-start | bytes 491528 | tf_op jit(solution)/shard_map/ppermute | solution.py:219
  57.8 18.6 %collective-permute-start.9 = (bf16[2,32,1280]{2,1,0:T(8,128)(2,1)S(1)}, bf16[2,32,1280]{2,1,0:T(8,128)(2,1)S(1)}, u32[]{:S(2)}, u32[]{:S(2)}) collective-permute-start(bf16[2,32,1280]{2,1,0:T(8,128)(2,1)S(1)} %copy-done.8), channel_id=1, source_target_pairs={{0,1},{1,0},{2,3},{3,2},{4,5},{5,4},{6,7},{7,6},{8,9},{9,8},{10,11... | collective-permute-start | bytes 491528 | tf_op jit(solution)/shard_map/ppermute | solution.py:219
  57.8 23.7 %collective-permute-start.11 = (bf16[2,32,1280]{2,1,0:T(8,128)(2,1)S(1)}, bf16[2,32,1280]{2,1,0:T(8,128)(2,1)S(1)}, u32[]{:S(2)}, u32[]{:S(2)}) collective-permute-start(bf16[2,32,1280]{2,1,0:T(8,128)(2,1)S(1)} %copy-done.12), channel_id=1, source_target_pairs={{0,4},{1,5},{2,6},{3,7},{4,0},{5,1},{6,2},{7,3},{8,12},{9,13},{10,... | collective-permute-start | bytes 491528 | tf_op jit(solution)/shard_map/ppermute | solution.py:219
  76.4 5.8 %collective-permute-start.13 = (bf16[2,32,1280]{2,1,0:T(8,128)(2,1)S(1)}, bf16[2,32,1280]{2,1,0:T(8,128)(2,1)S(1)}, u32[]{:S(2)}, u32[]{:S(2)}) collective-permute-start(bf16[2,32,1280]{2,1,0:T(8,128)(2,1)S(1)} %collective-permute-done.12.rest_5_), channel_id=1, source_target_pairs={{0,1},{1,0},{2,3},{3,2},{4,5},{5,4},{6,7},{7,6},{8,9},{9,8},{10,11... | collective-permute-start | bytes 491528 | tf_op jit(solution)/shard_map/ppermute | solution.py:219
  76.4 8.4 %collective-permute-start.10 = (bf16[2,32,1280]{2,1,0:T(8,128)(2,1)S(1)}, bf16[2,32,1280]{2,1,0:T(8,128)(2,1)S(1)}, u32[]{:S(2)}, u32[]{:S(2)}) collective-permute-start(bf16[2,32,1280]{2,1,0:T(8,128)(2,1)S(1)} %pad_maximum_fusion.2), channel_id=1, source_target_pairs={{0,2},{1,3},{2,0},{3,1},{4,6},{5,7},{6,4},{7,5},{8,10},{9,11},{10,... | collective-permute-start | bytes 491528 | tf_op jit(solution)/shard_map/ppermute | solution.py:219
  82.2 0.9 slice-start.1
  83.1 5.4 %copy-start.4 = (bf16[2,32,1280]{2,1,0:T(8,128)(2,1)S(1)}, bf16[2,32,1280]{2,1,0:T(8,128)(2,1)}, u32[]{:S(2)}) copy-start(bf16[2,32,1280]{2,1,0:T(8,128)(2,1)} %copy-done.3) | copy-start | bytes 491524
  83.1 5.4 %collective-permute-start.14 = (bf16[2,32,1280]{2,1,0:T(8,128)(2,1)S(1)}, bf16[2,32,1280]{2,1,0:T(8,128)(2,1)S(1)}, u32[]{:S(2)}, u32[]{:S(2)}) collective-permute-start(bf16[2,32,1280]{2,1,0:T(8,128)(2,1)S(1)} %pad_maximum_fusion.3), channel_id=1, source_target_pairs={{0,2},{1,3},{2,0},{3,1},{4,6},{5,7},{6,4},{7,5},{8,10},{9,11},{10,... | collective-permute-start | bytes 491528 | tf_op jit(solution)/shard_map/ppermute | solution.py:219
  (5 other events, 3.3 us)

commit v8 on v7

v8 whole, which is shorter than its diff:
```python
import functools

import jax
import jax.numpy as jnp
from jax import lax
from jax.experimental import pallas as pl
from jax.experimental.pallas import tpu as pltpu
from jax.sharding import PartitionSpec as P

TILE = 128
SLOTS = 3
PAIR = 2
ROWS = 16
ROOT = 0.7978845608028654
CUBIC = 0.044715
ANYWHERE = pl.BlockSpec(memory_space=pl.ANY)
RESIDENT = pl.BlockSpec(memory_space=pltpu.VMEM)
SCALAR = pl.BlockSpec(memory_space=pltpu.SMEM)


def room(mib):
    return pltpu.CompilerParams(vmem_limit_bytes=mib * 2**20)


def gelu_and_derivative(v):
    square = v * v
    th = jnp.tanh(ROOT * (v + CUBIC * (square * v)))
    half = 0.5 * (1.0 + th)
    inner = ROOT * (1.0 + (3.0 * CUBIC) * square)
    return v * half, half + 0.5 * v * (1.0 - th * th) * inner


def copy_all(pairs, sems):
    copies = [pltpu.make_async_copy(source, target, sems.at[i]) for i, (source, target) in enumerate(pairs)]
    for copy in copies:
        copy.start()
    for copy in copies:
        copy.wait()


def prepare_kernel(starts, whole, stacks, stay, leave, outgoing, sems):
    count, rows, width = stay.shape
    pairs = []
    for a, out in ((1, leave), (0, stay)):
        for b in range(count):
            span = pl.ds(pl.multiple_of(starts[a * count + b] * TILE, TILE), width)
            pairs.append((whole.at[:, span], out.at[b]))
    copy_all(pairs + [(stacks, outgoing.at[p]) for p in range(outgoing.shape[0])], sems)


def prepare_call(starts, whole, stacks, times):
    count = starts.shape[0] // PAIR
    rows, width = whole.shape[0], whole.shape[1] // (PAIR * count)
    hbm = pl.BlockSpec(memory_space=pltpu.HBM)
    return pl.pallas_call(
        prepare_kernel,
        out_shape=[jax.ShapeDtypeStruct((count, rows, width), whole.dtype)] * PAIR + [pltpu.HBM((times,) + stacks.shape, stacks.dtype)],
        in_specs=[SCALAR, ANYWHERE, ANYWHERE],
        out_specs=[ANYWHERE, ANYWHERE, hbm],
        scratch_shapes=[pltpu.SemaphoreType.DMA((PAIR * count + times,))],
        compiler_params=room(1),
        name="prepare",
    )(starts, *[pltpu.with_memory_space_constraint(array, pltpu.HBM) for array in (whole, stacks)])


def join_kernel(starts, *rest):
    blocks, whole, sems = rest[:-2], rest[-2], rest[-1]
    width = whole.shape[1] // len(blocks)
    copy_all([(block.at[0], whole.at[:, pl.ds(pl.multiple_of(starts[i] * TILE, TILE), width)]) for i, block in enumerate(blocks)], sems)


def join_call(starts, blocks):
    _, rows, width = blocks[0].shape
    return pl.pallas_call(
        join_kernel,
        out_shape=jax.ShapeDtypeStruct((rows, len(blocks) * width), blocks[0].dtype),
        in_specs=[SCALAR] + [ANYWHERE] * len(blocks),
        out_specs=ANYWHERE,
        scratch_shapes=[pltpu.SemaphoreType.DMA((len(blocks),))],
        compiler_params=room(1),
        name="join",
    )(starts, *blocks)


def pick(tiles, counts, tokens, s):
    picked = []
    for k in range(SLOTS):
        column = pl.multiple_of(tiles[s, k] * TILE, TILE)
        block = jnp.concatenate([piece[:, pl.ds(column, TILE)] for piece in tokens], axis=0)
        picked.append(jnp.where(k < counts[s], block, jnp.zeros_like(block)))
    return jnp.concatenate(picked, axis=1)


def stripe_kernel(pieces, tiles, counts, own, *rest):
    tokens, (weights, backs, hidden, grads, mine, term, sent, sems) = rest[:pieces], rest[pieces:]
    shards, stripes, size, _ = weights.shape
    blocks, rows, _ = backs.shape
    span = pl.ds(pl.multiple_of(own[0] * size, size), size)
    copies = []
    for s in range(stripes):
        cols = slice(s * TILE, (s + 1) * TILE)
        picked = pick(tiles, counts, tokens, s)
        stack = jnp.concatenate([weights[f, s] for f in range(shards)], axis=0)
        pre = jnp.dot(picked, stack, preferred_element_type=jnp.float32)
        act, slope = gelu_and_derivative(pre)
        hidden[:, :, cols] = act.astype(hidden.dtype).reshape(blocks, rows, TILE)
        back = backs[:, :, cols].reshape(blocks * rows, TILE)
        slope = (back.astype(jnp.float32) * slope).astype(jnp.bfloat16)
        term[s] = lax.dot_general(picked, slope, (((0,), (0,)), ((), ())), preferred_element_type=jnp.float32)
        for f in range(shards):
            sent[s, f] = term[s, f * size:(f + 1) * size].astype(sent.dtype)
        copies.append(pltpu.make_async_copy(sent.at[s], grads.at[:, s], sems.at[s]))
        copies[-1].start()
        mine[s] = term[s, span]
    for copy in copies:
        copy.wait()


def stripe_call(tiles, counts, own, tokens, weights, backs):
    shards, stripes, size, _ = weights.shape
    return pl.pallas_call(
        functools.partial(stripe_kernel, len(tokens)),
        out_shape=[
            jax.ShapeDtypeStruct(backs.shape, jnp.bfloat16),
            pltpu.HBM(weights.shape, jnp.bfloat16),
            jax.ShapeDtypeStruct(weights.shape[1:], jnp.float32),
        ],
        in_specs=[SCALAR] * 3 + [RESIDENT] * (len(tokens) + 2),
        out_specs=[RESIDENT, pl.BlockSpec(memory_space=pltpu.HBM), RESIDENT],
        scratch_shapes=[
            pltpu.VMEM((stripes, SLOTS * TILE, TILE), jnp.float32),
            pltpu.VMEM((stripes, shards, size, TILE), jnp.bfloat16),
            pltpu.SemaphoreType.DMA((stripes,)),
        ],
        compiler_params=room(16),
        name="stripes",
    )(tiles, counts, own, *tokens, weights, backs)


def sum_kernel(own, grads, mine, total, held, sems):
    shards, stripes = grads.shape[0], grads.shape[1]
    step = 5 if stripes % 5 == 0 else stripes
    copies = []
    for a in range(PAIR):
        for c in range(0, stripes, step):
            held[a, c:c + step] = sum(
                jnp.where(own[0] == f, mine[c:c + step], grads[f, c:c + step].astype(jnp.float32)) for f in range(a, shards, PAIR)
            )
            span = pl.ds(c, step)
            copies.append(pltpu.make_async_copy(held.at[a, span], total.at[a, span], sems.at[len(copies)]))
            copies[-1].start()
    for copy in copies:
        copy.wait()


def sum_call(own, grads, mine):
    shape = (PAIR,) + mine.shape
    return pl.pallas_call(
        sum_kernel,
        out_shape=jax.ShapeDtypeStruct(shape, jnp.float32),
        in_specs=[SCALAR, RESIDENT, RESIDENT],
        out_specs=ANYWHERE,
        scratch_shapes=[pltpu.VMEM(shape, jnp.float32), pltpu.SemaphoreType.DMA((PAIR * mine.shape[0],))],
        compiler_params=room(12),
        name="sum",
    )(own, grads, mine)


def take(arrays, refs):
    runs = []
    for a, b in refs:
        if runs and runs[-1][0] == a and runs[-1][2] == b:
            runs[-1][2] = b + 1
        else:
            runs.append([a, b, b + 1])
    pieces = [arrays[a] if (low, high) == (0, arrays[a].shape[0]) else arrays[a][low:high] for a, low, high in runs]
    return pieces[0] if len(pieces) == 1 else jnp.concatenate(pieces, axis=0)


def body(fsdp, tensor, tokens, tile_weights, cotangent, tile_list, tile_counts):
    z, t = lax.axis_index("fsdp"), lax.axis_index("tensor")
    half = z % PAIR
    size, stripes = tile_weights.shape[0], tile_weights.shape[1]
    share = stripes // PAIR
    whole_tiles = size % ROWS == 0
    bits = [1 << i for i in reversed(range((tensor - 1).bit_length()))]

    def swap(value, dz, dt):
        pairs = [(a * tensor + b, (a ^ dz) * tensor + (b ^ dt)) for a in range(fsdp) for b in range(tensor)]
        return lax.ppermute(value, ("fsdp", "tensor"), pairs)

    steps = [(a, b) for a in range(PAIR) for b in range(tensor)]
    starts = jnp.stack([(t ^ b) * stripes + (half ^ a) * share for a, b in steps]).astype(jnp.int32)

    by_stripe = jnp.transpose(tile_weights, (1, 0, 2)).reshape(PAIR, share, size, TILE)
    stay, leave, outgoing = prepare_call(starts, cotangent, by_stripe, fsdp // PAIR)
    weights = lax.all_to_all(outgoing.reshape(fsdp, share, size, TILE), "fsdp", split_axis=0, concat_axis=0, tiled=True)
    own = z.reshape(1).astype(jnp.int32)
    if not whole_tiles:
        weights = weights.transpose(1, 0, 2, 3).reshape(1, share, fsdp * size, TILE)

    near, origins = jnp.concatenate([tokens, swap(tokens, 1, 0)], axis=0), [(0, 0), (1, 0)]
    arrays = [stay, swap(leave, 1, 0)]
    groups = [[(a, b) for b in range(tensor)] for a in range(PAIR)]
    for bit in bits:
        far = swap(near, 0, bit)
        if bit > 1:
            near = jnp.concatenate([near, far], axis=0)
        count = bit
        arrays = arrays + [swap(take(arrays, [ref for group in groups for ref in group[count:]]), 0, bit)]
        new = [[(len(arrays) - 1, i * count + j) for j in range(count)] for i in range(len(groups))]
        groups = [group[:count] for group in groups] + new
        origins = origins + [(a, b ^ bit) for a, b in origins]
    backs = take(arrays, [group[0] for group in groups])

    tiles = lax.dynamic_slice_in_dim(tile_list, half * share, share, 0)
    counts = lax.dynamic_slice_in_dim(tile_counts, half * share, share, 0)
    hidden, grads, mine = stripe_call(tiles, counts, own if whole_tiles else own * 0, [near, far], weights, backs)

    if not whole_tiles:
        grads = grads.reshape(share, fsdp, size, TILE).transpose(1, 0, 2, 3)
        mine = lax.dynamic_index_in_dim(mine.reshape(share, fsdp, size, TILE), z, 1, keepdims=False)
    total = sum_call(own, lax.all_to_all(grads, "fsdp", split_axis=0, concat_axis=0, tiled=True), mine)

    blocks = {step: swap(hidden[i:i + 1], *step) if any(step) else hidden[i:i + 1] for i, step in enumerate(origins)}
    activations = join_call(starts, [blocks[step] for step in steps])
    return activations, total.reshape(stripes, size, TILE).transpose(1, 0, 2)


def solution(mesh):
    return jax.shard_map(
        functools.partial(body, mesh.shape["fsdp"], mesh.shape["tensor"]),
        mesh=mesh,
        in_specs=(
            P(("member", "fsdp", "tensor"), None),
            P(("member", "fsdp"), "tensor", None),
            P(("member", "fsdp", "tensor"), None),
            P("tensor", None),
            P("tensor"),
        ),
        out_specs=(P(("member", "fsdp", "tensor"), None), P(("member", "fsdp"), "tensor", None)),
        check_vma=False,
    )
```

time: 91.7 us -> 113 us (1.23)
  Pallas kernels: 8.91 us -> 37.6 us
  waiting for transfers between devices: 48.6 us -> 44.8 us
  local copies, waits for them, and re-layouts: 7.78 us -> 4.96 us
  other arithmetic: 1.4 us -> 0.1 us
    pallas_call x4 -> x3, Pallas kernels: 7.75 us -> 36.4 us  [the longest x1 31.5 us: prepare_call(): pl.pallas_call(prepare_kernel, out_shape=[jax.ShapeDtypeStruct((count, ro...]
    ppermute x15 -> x13, waiting for transfers between devices: 48.6 us -> 44.8 us  [swap(): return lax.ppermute(value, ('fsdp', 'tensor'), pairs)]
    all_to_all x1, starting transfers between devices: 6.45 us -> 3.87 us  [body(): lax.all_to_all(outgoing.reshape(fsdp, share, size, TILE), 'fsdp', split_a...]
    ppermute x15 -> x13, starting transfers between devices: 13.3 us -> 15.6 us  [swap(): return lax.ppermute(value, ('fsdp', 'tensor'), pairs)]
    another operation x3 -> x1, local copies, waits for them, and re-layouts: 2.3 us -> 0.08 us  [body(): jnp.stack([(t ^ b) * stripes + (half ^ a) * share for a, b in steps])]
    concatenate x4 -> x2, other arithmetic: 1.4 us -> 0.08 us  [take(): return pieces[0] if len(pieces) == 1 else jnp.concatenate(pieces, axis=0)]
    unnamed x36 -> x14, local copies, waits for them, and re-layouts: 4.39 us -> 3.6 us
  transfers between devices with their start and end apart: 17 -> 15, of which waited for: 7 -> 7; matrix products, arithmetic and copies ran while one was open for 2% -> 1% of each run, Pallas kernels for 4% -> 29%
where the time goes in v8:
time: 113 us; the launch traced here: 112 us
  waiting for transfers between devices  44.8 us (40%)
  Pallas kernels  37.6 us (33%)
  starting transfers between devices  24.1 us (21%)
  local copies, waits for them, and re-layouts  4.96 us (4%)
    ppermute x13, waiting for transfers between devices, swap(): return lax.ppermute(value, ('fsdp', 'tensor'), pairs)  44.8 us
    pallas_call x1, Pallas kernels, prepare_call(): pl.pallas_call(prepare_kernel, out_shape=[jax.ShapeDtypeStruct((count, ro...  31.5 us
    ppermute x13, starting transfers between devices, swap(): return lax.ppermute(value, ('fsdp', 'tensor'), pairs)  15.6 us
    all_to_all x1, starting transfers between devices, body(): lax.all_to_all(grads, 'fsdp', split_axis=0, concat_axis=0, tiled=True)  4.66 us
    all_to_all x1, starting transfers between devices, body(): lax.all_to_all(outgoing.reshape(fsdp, share, size, TILE), 'fsdp', split_a...  3.87 us
    unnamed x14, local copies, waits for them, and re-layouts  3.6 us
    pallas_call x1, Pallas kernels, stripe_call(): pl.pallas_call(functools.partial(stripe_kernel, len(tokens)), out_shape=[...  3.45 us
  transfers between devices with their start and end apart: 15, of which 7 were waited for; matrix products, arithmetic and copies ran while one was open for 1% of the time, Pallas kernels for 29%

profile of v8, /device:TPU:0, one launch (start us, length us, event | category | flops | bytes accessed | tf_op | source)
XLA Modules:
  0.0 112.4 jit_solution(14357312266526887697)
XLA Ops:
  0.6 3.1 %collective-permute-start = (bf16[32,2560]{1,0:T(8,128)(2,1)}, bf16[32,2560]{1,0:T(8,128)(2,1)S(1)}, u32[]{:S(2)}, u32[]{:S(2)}) collective-permute-start(bf16[32,2560]{1,0:T(8,128)(2,1)} %param.5), channel_id=1, source_target_pairs={{0,4},{1,5},{2,6},{3,7},{4,0},{5,1},{6,2},{7,3},{8,12},{9,13},{10,... | collective-permute-start | bytes 491528 | tf_op jit(solution)/shard_map/ppermute | solution.py:190
  3.7 0.1 stack.35.starts
  3.8 31.5 %prepare.1 = (bf16[4,32,1280]{2,1,0:T(8,128)(2,1)S(1)}, bf16[4,32,1280]{2,1,0:T(8,128)(2,1)S(1)}, bf16[2,2,10,96,128]{4,3,2,1,0:T(8,128)(2,1)}) custom-call(s32[8]{0:T(128)S(1)} %stack.35.starts, bf16[32,10240]{1,0:T(8,128)(2,1)} %whole.1, bf16[2,10,96,128]{3,2,1,0:T(8,128)(2,1)} %bitcast.18), custom_call_target="tpu_custom_call" | custom-call | tf_op jit(solution)/shard_map/prepare/pallas_call | solution.py:55
  35.4 3.9 %all-to-all-start = ((bf16[4,10,96,128]{3,2,1,0:T(8,128)(2,1)}), bf16[4,10,96,128]{3,2,1,0:T(8,128)(2,1)S(1)}, u32[]{:S(2)}, u32[]{:S(2)}) async-start(bf16[4,10,96,128]{3,2,1,0:T(8,128)(2,1)} %bitcast.16), calls=%async_computation | async-start | bytes 1966080 | tf_op jit(solution)/shard_map/all_to_all | solution.py:197
  39.2 2.0 %collective-permute-start.3 = (bf16[4,32,1280]{2,1,0:T(8,128)(2,1)S(1)}, bf16[4,32,1280]{2,1,0:T(8,128)(2,1)S(1)}, u32[]{:S(2)}, u32[]{:S(2)}) collective-permute-start(bf16[4,32,1280]{2,1,0:T(8,128)(2,1)S(1)} %get-tuple-element.10), channel_id=1, source_target_pairs={{0,4},{1,5},{2,6},{3,7},{4,0},{5,1},{6,2},{7,3},{8,12},{9,13},{10,... | collective-permute-start | bytes 983048 | tf_op jit(solution)/shard_map/ppermute | solution.py:190
  41.3 0.9 copy-done.3
  42.2 1.6 %collective-permute-start.1 = (bf16[64,2560]{1,0:T(8,128)(2,1)S(1)}, bf16[64,2560]{1,0:T(8,128)(2,1)S(1)}, u32[]{:S(2)}, u32[]{:S(2)}) collective-permute-start(bf16[64,2560]{1,0:T(8,128)(2,1)S(1)} %pad_maximum_fusion), channel_id=1, source_target_pairs={{0,2},{1,3},{2,0},{3,1},{4,6},{5,7},{6,4},{7,5},{8,10},{9,11},{10,... | collective-permute-start | bytes 983048 | tf_op jit(solution)/shard_map/ppermute | solution.py:190
  43.8 20.3 %collective-permute-done.3 = bf16[4,32,1280]{2,1,0:T(8,128)(2,1)S(1)} collective-permute-done((bf16[4,32,1280]{2,1,0:T(8,128)(2,1)S(1)}, bf16[4,32,1280]{2,1,0:T(8,128)(2,1)S(1)}, u32[]{:S(2)}, u32[]{:S(2)}) %collective-permute-start.3) | collective-permute-done | bytes 327712 | tf_op jit(solution)/shard_map/ppermute | solution.py:190
  64.2 1.6 %collective-permute-start.4 = (bf16[4,32,1280]{2,1,0:T(8,128)(2,1)S(1)}, bf16[4,32,1280]{2,1,0:T(8,128)(2,1)S(1)}, u32[]{:S(2)}, u32[]{:S(2)}) collective-permute-start(bf16[4,32,1280]{2,1,0:T(8,128)(2,1)S(1)} %pad_maximum_fusion.1), channel_id=1, source_target_pairs={{0,2},{1,3},{2,0},{3,1},{4,6},{5,7},{6,4},{7,5},{8,10},{9,11},{10,... | collective-permute-start | bytes 983048 | tf_op jit(solution)/shard_map/ppermute | solution.py:190
  65.9 5.4 %collective-permute-done.4 = bf16[4,32,1280]{2,1,0:T(8,128)(2,1)S(1)} collective-permute-done((bf16[4,32,1280]{2,1,0:T(8,128)(2,1)S(1)}, bf16[4,32,1280]{2,1,0:T(8,128)(2,1)S(1)}, u32[]{:S(2)}, u32[]{:S(2)}) %collective-permute-start.4) | collective-permute-done | bytes 327712 | tf_op jit(solution)/shard_map/ppermute | solution.py:190
  71.4 0.1 collective-permute-start.5
  71.5 0.6 copy-done.4
  72.1 0.1 dynamic_slice.7.counts
  72.3 0.1 copy.8.tiles
  72.4 0.8 collective-permute-done.5
  73.2 1.0 constant_dynamic-update-slice_fusion.3.rest_3_
  74.2 0.8 copy-done.1
  75.1 1.1 copy-done.2
  76.2 3.5 %stripes.1 = (bf16[8,32,1280]{2,1,0:T(8,128)(2,1)S(1)}, bf16[4,10,96,128]{3,2,1,0:T(8,128)(2,1)}, f32[10,96,128]{2,1,0:T(8,128)S(1)}) custom-call(s32[10,3]{1,0:T(8,128)S(1)} %copy.8.tiles, s32[10]{0:T(128)S(1)} %dynamic_slice.7.counts, s32[1]{0:T(128)} %bitcast.8.own, bf16[128,2560]{1,0:T(8,128)(2,1)S(1)} %constant_dynamic-update-slice_fusion.rest_0_, ...), custom_call_target="tpu_custom_call" | custom-call | tf_op jit(solution)/shard_map/stripes/pallas_call | solution.py:121
  79.6 4.7 %all-to-all-start.1 = ((bf16[4,10,96,128]{3,2,1,0:T(8,128)(2,1)}), bf16[4,10,96,128]{3,2,1,0:T(8,128)(2,1)S(1)}, u32[]{:S(2)}, u32[]{:S(2)}) async-start(bf16[4,10,96,128]{3,2,1,0:T(8,128)(2,1)} %get-tuple-element.12), calls=%async_computation.1 | async-start | bytes 1966080 | tf_op jit(solution)/shard_map/all_to_all | solution.py:223
  84.3 2.2 %collective-permute-start.12 = (bf16[1,32,1280]{2,1,0:T(8,128)(2,1)S(1)}, bf16[1,32,1280]{2,1,0:T(8,128)(2,1)S(1)}, u32[]{:S(2)}, u32[]{:S(2)}) collective-permute-start(bf16[1,32,1280]{2,1,0:T(8,128)(2,1)S(1)} %get-tuple-element.14), channel_id=1, source_target_pairs={{0,7},{1,6},{2,5},{3,4},{4,3},{5,2},{6,1},{7,0},{8,15},{9,14},{10,... | collective-permute-start | bytes 245768 | tf_op jit(solution)/shard_map/ppermute | solution.py:190
  86.5 0.9 collective-permute-start.11
  87.4 1.4 %collective-permute-start.10 = (bf16[1,32,1280]{2,1,0:T(8,128)(2,1)S(1)}, bf16[1,32,1280]{2,1,0:T(8,128)(2,1)S(1)}, u32[]{:S(2)}, u32[]{:S(2)}) collective-permute-start(bf16[1,32,1280]{2,1,0:T(8,128)(2,1)S(1)} %get-tuple-element.16), channel_id=1, source_target_pairs={{0,5},{1,4},{2,7},{3,6},{4,1},{5,0},{6,3},{7,2},{8,13},{9,12},{10,... | collective-permute-start | bytes 245768 | tf_op jit(solution)/shard_map/ppermute | solution.py:190
  88.8 0.3 collective-permute-start.9
  89.1 1.0 collective-permute-start.8
  90.1 13.1 %collective-permute-done.12.rest_7_ = bf16[1,32,1280]{2,1,0:T(8,128)(2,1)S(1)} collective-permute-done((bf16[1,32,1280]{2,1,0:T(8,128)(2,1)S(1)}, bf16[1,32,1280]{2,1,0:T(8,128)(2,1)S(1)}, u32[]{:S(2)}, u32[]{:S(2)}) %collective-permute-start.12) | collective-permute-done | bytes 81952 | tf_op jit(solution)/shard_map/ppermute | solution.py:190
  103.1 1.5 %collective-permute-start.7 = (bf16[1,32,1280]{2,1,0:T(8,128)(2,1)S(1)}, bf16[1,32,1280]{2,1,0:T(8,128)(2,1)S(1)}, u32[]{:S(2)}, u32[]{:S(2)}) collective-permute-start(bf16[1,32,1280]{2,1,0:T(8,128)(2,1)S(1)} %get-tuple-element.19), channel_id=1, source_target_pairs={{0,2},{1,3},{2,0},{3,1},{4,6},{5,7},{6,4},{7,5},{8,10},{9,11},{10,... | collective-permute-start | bytes 245768 | tf_op jit(solution)/shard_map/ppermute | solution.py:190
  104.6 0.3 collective-permute-done.11.rest_6_
  104.9 1.8 %collective-permute-done.10.rest_5_ = bf16[1,32,1280]{2,1,0:T(8,128)(2,1)S(1)} collective-permute-done((bf16[1,32,1280]{2,1,0:T(8,128)(2,1)S(1)}, bf16[1,32,1280]{2,1,0:T(8,128)(2,1)S(1)}, u32[]{:S(2)}, u32[]{:S(2)}) %collective-permute-start.10) | collective-permute-done | bytes 81952 | tf_op jit(solution)/shard_map/ppermute | solution.py:190
  106.7 3.1 %collective-permute-done.9.rest_4_ = bf16[1,32,1280]{2,1,0:T(8,128)(2,1)S(1)} collective-permute-done((bf16[1,32,1280]{2,1,0:T(8,128)(2,1)S(1)}, bf16[1,32,1280]{2,1,0:T(8,128)(2,1)S(1)}, u32[]{:S(2)}, u32[]{:S(2)}) %collective-permute-start.9) | collective-permute-done | bytes 81952 | tf_op jit(solution)/shard_map/ppermute | solution.py:190
  109.8 1.4 %join.1 = bf16[32,10240]{1,0:T(8,128)(2,1)} custom-call(s32[8]{0:T(128)S(1)} %stack.35.starts, bf16[1,32,1280]{2,1,0:T(8,128)(2,1)S(1)} %get-tuple-element.21.rest_0_, bf16[1,32,1280]{2,1,0:T(8,128)(2,1)S(1)} %collective-permute-done.6.rest_1_, bf16[1,32,1280]{2,1,0:T(8,128)(2,1)S(1)} %collective-permute-done.7.rest_2_, ...), custom_call_target="tpu_custom_call" | custom-call | tf_op jit(solution)/shard_map/join/pallas_call | solution.py:74
  111.3 1.2 %sum.1 = f32[2,10,96,128]{3,2,1,0:T(8,128)} custom-call(s32[1]{0:T(128)} %bitcast.8.own, bf16[4,10,96,128]{3,2,1,0:T(8,128)(2,1)S(1)} %all-to-all-done.1.grads, f32[10,96,128]{2,1,0:T(8,128)S(1)} %get-tuple-element.13.mine), custom_call_target="tpu_custom_call" | custom-call | tf_op jit(solution)/shard_map/sum/pallas_call | solution.py:158
  (30 shorter events, 0.4 us)
Async XLA Ops:
  0.6 71.6 %copy-start = (s32[20,3]{0,1:T(4,128)S(1)}, s32[20,3]{0,1:T(4,128)}, u32[]{:S(2)}) copy-start(s32[20,3]{0,1:T(4,128)} %param.8) | copy-start | bytes 724
  0.6 41.6 %collective-permute-start = (bf16[32,2560]{1,0:T(8,128)(2,1)}, bf16[32,2560]{1,0:T(8,128)(2,1)S(1)}, u32[]{:S(2)}, u32[]{:S(2)}) collective-permute-start(bf16[32,2560]{1,0:T(8,128)(2,1)} %param.5), channel_id=1, source_target_pairs={{0,4},{1,5},{2,6},{3,7},{4,0},{5,1},{6,2},{7,3},{8,12},{9,13},{10,... | collective-permute-start | bytes 491528 | tf_op jit(solution)/shard_map/ppermute | solution.py:190
  35.4 39.7 %all-to-all-start = ((bf16[4,10,96,128]{3,2,1,0:T(8,128)(2,1)}), bf16[4,10,96,128]{3,2,1,0:T(8,128)(2,1)S(1)}, u32[]{:S(2)}, u32[]{:S(2)}) async-start(bf16[4,10,96,128]{3,2,1,0:T(8,128)(2,1)} %bitcast.16), calls=%async_computation | async-start | bytes 1966080 | tf_op jit(solution)/shard_map/all_to_all | solution.py:197
  39.2 24.9 %collective-permute-start.3 = (bf16[4,32,1280]{2,1,0:T(8,128)(2,1)S(1)}, bf16[4,32,1280]{2,1,0:T(8,128)(2,1)S(1)}, u32[]{:S(2)}, u32[]{:S(2)}) collective-permute-start(bf16[4,32,1280]{2,1,0:T(8,128)(2,1)S(1)} %get-tuple-element.10), channel_id=1, source_target_pairs={{0,4},{1,5},{2,6},{3,7},{4,0},{5,1},{6,2},{7,3},{8,12},{9,13},{10,... | collective-permute-start | bytes 983048 | tf_op jit(solution)/shard_map/ppermute | solution.py:190
  41.3 0.9 copy-start.3
  42.2 23.5 %collective-permute-start.1 = (bf16[64,2560]{1,0:T(8,128)(2,1)S(1)}, bf16[64,2560]{1,0:T(8,128)(2,1)S(1)}, u32[]{:S(2)}, u32[]{:S(2)}) collective-permute-start(bf16[64,2560]{1,0:T(8,128)(2,1)S(1)} %pad_maximum_fusion), channel_id=1, source_target_pairs={{0,2},{1,3},{2,0},{3,1},{4,6},{5,7},{6,4},{7,5},{8,10},{9,11},{10,... | collective-permute-start | bytes 983048 | tf_op jit(solution)/shard_map/ppermute | solution.py:190
  64.2 7.1 %collective-permute-start.4 = (bf16[4,32,1280]{2,1,0:T(8,128)(2,1)S(1)}, bf16[4,32,1280]{2,1,0:T(8,128)(2,1)S(1)}, u32[]{:S(2)}, u32[]{:S(2)}) collective-permute-start(bf16[4,32,1280]{2,1,0:T(8,128)(2,1)S(1)} %pad_maximum_fusion.1), channel_id=1, source_target_pairs={{0,2},{1,3},{2,0},{3,1},{4,6},{5,7},{6,4},{7,5},{8,10},{9,11},{10,... | collective-permute-start | bytes 983048 | tf_op jit(solution)/shard_map/ppermute | solution.py:190
  65.8 8.4 %collective-permute-start.2 = (bf16[128,2560]{1,0:T(8,128)(2,1)S(1)}, bf16[128,2560]{1,0:T(8,128)(2,1)S(1)}, u32[]{:S(2)}, u32[]{:S(2)}) collective-permute-start(bf16[128,2560]{1,0:T(8,128)(2,1)S(1)} %constant_dynamic-update-slice_fusion.rest_0_), channel_id=1, source_target_pairs={{0,1},{1,0},{2,3},{3,2},{4,5},{5,4},{6,7},{7,6},{8,9},{9,8},{10,11... | collective-permute-start | bytes 1966088 | tf_op jit(solution)/shard_map/ppermute | solution.py:190
  71.4 1.8 %collective-permute-start.5 = (bf16[4,32,1280]{2,1,0:T(8,128)(2,1)S(1)}, bf16[4,32,1280]{2,1,0:T(8,128)(2,1)}, u32[]{:S(2)}, u32[]{:S(2)}) collective-permute-start(bf16[4,32,1280]{2,1,0:T(8,128)(2,1)S(1)} %pad_maximum_fusion.2), channel_id=1, source_target_pairs={{0,1},{1,0},{2,3},{3,2},{4,5},{5,4},{6,7},{7,6},{8,9},{9,8},{10,11... | collective-permute-start | bytes 983048 | tf_op jit(solution)/shard_map/ppermute | solution.py:190
  71.5 0.7 copy-start.4
  74.2 0.8 copy-start.1
  75.1 1.1 copy-start.2
  79.6 31.6 %all-to-all-start.1 = ((bf16[4,10,96,128]{3,2,1,0:T(8,128)(2,1)}), bf16[4,10,96,128]{3,2,1,0:T(8,128)(2,1)S(1)}, u32[]{:S(2)}, u32[]{:S(2)}) async-start(bf16[4,10,96,128]{3,2,1,0:T(8,128)(2,1)} %get-tuple-element.12), calls=%async_computation.1 | async-start | bytes 1966080 | tf_op jit(solution)/shard_map/all_to_all | solution.py:223
  84.3 18.8 %collective-permute-start.12 = (bf16[1,32,1280]{2,1,0:T(8,128)(2,1)S(1)}, bf16[1,32,1280]{2,1,0:T(8,128)(2,1)S(1)}, u32[]{:S(2)}, u32[]{:S(2)}) collective-permute-start(bf16[1,32,1280]{2,1,0:T(8,128)(2,1)S(1)} %get-tuple-element.14), channel_id=1, source_target_pairs={{0,7},{1,6},{2,5},{3,4},{4,3},{5,2},{6,1},{7,0},{8,15},{9,14},{10,... | collective-permute-start | bytes 245768 | tf_op jit(solution)/shard_map/ppermute | solution.py:190
  86.5 18.4 %collective-permute-start.11 = (bf16[1,32,1280]{2,1,0:T(8,128)(2,1)S(1)}, bf16[1,32,1280]{2,1,0:T(8,128)(2,1)S(1)}, u32[]{:S(2)}, u32[]{:S(2)}) collective-permute-start(bf16[1,32,1280]{2,1,0:T(8,128)(2,1)S(1)} %get-tuple-element.15), channel_id=1, source_target_pairs={{0,6},{1,7},{2,4},{3,5},{4,2},{5,3},{6,0},{7,1},{8,14},{9,15},{10,... | collective-permute-start | bytes 245768 | tf_op jit(solution)/shard_map/ppermute | solution.py:190
  87.4 19.2 %collective-permute-start.10 = (bf16[1,32,1280]{2,1,0:T(8,128)(2,1)S(1)}, bf16[1,32,1280]{2,1,0:T(8,128)(2,1)S(1)}, u32[]{:S(2)}, u32[]{:S(2)}) collective-permute-start(bf16[1,32,1280]{2,1,0:T(8,128)(2,1)S(1)} %get-tuple-element.16), channel_id=1, source_target_pairs={{0,5},{1,4},{2,7},{3,6},{4,1},{5,0},{6,3},{7,2},{8,13},{9,12},{10,... | collective-permute-start | bytes 245768 | tf_op jit(solution)/shard_map/ppermute | solution.py:190
  88.8 21.0 %collective-permute-start.9 = (bf16[1,32,1280]{2,1,0:T(8,128)(2,1)S(1)}, bf16[1,32,1280]{2,1,0:T(8,128)(2,1)S(1)}, u32[]{:S(2)}, u32[]{:S(2)}) collective-permute-start(bf16[1,32,1280]{2,1,0:T(8,128)(2,1)S(1)} %get-tuple-element.17), channel_id=1, source_target_pairs={{0,4},{1,5},{2,6},{3,7},{4,0},{5,1},{6,2},{7,3},{8,12},{9,13},{10,... | collective-permute-start | bytes 245768 | tf_op jit(solution)/shard_map/ppermute | solution.py:190
  89.1 20.7 %collective-permute-start.8 = (bf16[1,32,1280]{2,1,0:T(8,128)(2,1)S(1)}, bf16[1,32,1280]{2,1,0:T(8,128)(2,1)S(1)}, u32[]{:S(2)}, u32[]{:S(2)}) collective-permute-start(bf16[1,32,1280]{2,1,0:T(8,128)(2,1)S(1)} %get-tuple-element.18), channel_id=1, source_target_pairs={{0,3},{1,2},{2,1},{3,0},{4,7},{5,6},{6,5},{7,4},{8,11},{9,10},{10,... | collective-permute-start | bytes 245768 | tf_op jit(solution)/shard_map/ppermute | solution.py:190
  103.1 6.6 %collective-permute-start.7 = (bf16[1,32,1280]{2,1,0:T(8,128)(2,1)S(1)}, bf16[1,32,1280]{2,1,0:T(8,128)(2,1)S(1)}, u32[]{:S(2)}, u32[]{:S(2)}) collective-permute-start(bf16[1,32,1280]{2,1,0:T(8,128)(2,1)S(1)} %get-tuple-element.19), channel_id=1, source_target_pairs={{0,2},{1,3},{2,0},{3,1},{4,6},{5,7},{6,4},{7,5},{8,10},{9,11},{10,... | collective-permute-start | bytes 245768 | tf_op jit(solution)/shard_map/ppermute | solution.py:190
  104.9 4.9 %collective-permute-start.6 = (bf16[1,32,1280]{2,1,0:T(8,128)(2,1)S(1)}, bf16[1,32,1280]{2,1,0:T(8,128)(2,1)S(1)}, u32[]{:S(2)}, u32[]{:S(2)}) collective-permute-start(bf16[1,32,1280]{2,1,0:T(8,128)(2,1)S(1)} %get-tuple-element.20), channel_id=1, source_target_pairs={{0,1},{1,0},{2,3},{3,2},{4,5},{5,4},{6,7},{7,6},{8,9},{9,8},{10,11... | collective-permute-start | bytes 245768 | tf_op jit(solution)/shard_map/ppermute | solution.py:190

commit v9 on v7

--- a/solution.py
+++ b/solution.py
@@ -38,31 +38,20 @@
         copy.wait()
 
 
-def row_chunks(rows):
-    step = ROWS if rows % ROWS == 0 else rows
-    return [pl.ds(r, step) for r in range(0, rows, step)]
-
-
-def cut_kernel(starts, whole, *rest):
-    outs, sems = rest[:-1], rest[-1]
-    count, rows, width = outs[0].shape
-    pairs = []
-    for a in reversed(range(PAIR)):
-        for b in range(count):
-            span = pl.ds(pl.multiple_of(starts[a * count + b] * TILE, TILE), width)
-            pairs += [(whole.at[r, span], outs[a].at[b, r]) for r in row_chunks(rows)]
-    copy_all(pairs, sems)
+def cut_kernel(starts, whole, out, sems):
+    count, _, width = out.shape
+    copy_all([(whole.at[:, pl.ds(pl.multiple_of(starts[b] * TILE, TILE), width)], out.at[b]) for b in range(count)], sems)
 
 
 def cut_call(starts, whole):
-    count = starts.shape[0] // PAIR
+    count = starts.shape[0]
     rows, width = whole.shape[0], whole.shape[1] // (PAIR * count)
     return pl.pallas_call(
         cut_kernel,
-        out_shape=[jax.ShapeDtypeStruct((count, rows, width), whole.dtype)] * PAIR,
+        out_shape=jax.ShapeDtypeStruct((count, rows, width), whole.dtype),
         in_specs=[SCALAR, ANYWHERE],
-        out_specs=[ANYWHERE] * PAIR,
-        scratch_shapes=[pltpu.SemaphoreType.DMA((PAIR * count * len(row_chunks(rows)),))],
+        out_specs=ANYWHERE,
+        scratch_shapes=[pltpu.SemaphoreType.DMA((count,))],
         compiler_params=room(1),
         name="cut",
     )(starts, pltpu.with_memory_space_constraint(whole, pltpu.HBM))
@@ -70,12 +59,9 @@
 
 def join_kernel(refs, starts, *rest):
     arrays, whole, sems = rest[:-2], rest[-2], rest[-1]
-    rows, width = whole.shape[0], whole.shape[1] // len(refs)
-    pairs = []
-    for i, (a, b) in enumerate(refs):
-        span = pl.ds(pl.multiple_of(starts[i] * TILE, TILE), width)
-        pairs += [(arrays[a].at[b, r], whole.at[r, span]) for r in row_chunks(rows)]
-    copy_all(pairs, sems)
+    width = whole.shape[1] // len(refs)
+    spans = [pl.ds(pl.multiple_of(starts[i] * TILE, TILE), width) for i in range(len(refs))]
+    copy_all([(arrays[a].at[b], whole.at[:, span]) for (a, b), span in zip(refs, spans)], sems)
 
 
 def join_call(starts, arrays, refs):
@@ -85,7 +71,7 @@
         out_shape=jax.ShapeDtypeStruct((rows, len(refs) * width), arrays[0].dtype),
         in_specs=[SCALAR] + [ANYWHERE] * len(arrays),
         out_specs=ANYWHERE,
-        scratch_shapes=[pltpu.SemaphoreType.DMA((len(refs) * len(row_chunks(rows)),))],
+        scratch_shapes=[pltpu.SemaphoreType.DMA((len(refs),))],
         compiler_params=room(1),
         name="join",
     )(starts, *arrays)
@@ -101,34 +87,44 @@
 
 
 def forward_kernel(pieces, refs, tiles, counts, *rest):
-    tokens, weights, arrays, outs, slopes = rest[:pieces], rest[pieces], rest[pieces + 1:-5], rest[-5:-1], rest[-1]
-    shards, stripes = weights.shape[0], weights.shape[1]
+    tokens, weights, arrays = rest[:pieces], rest[pieces], rest[pieces + 1:-5]
+    outs, slopes, held, sems = rest[-5:-3], rest[-3], rest[-2], rest[-1]
+    shards, stripes, size, _ = weights.shape
     rows = arrays[0].shape[1]
-    part = outs[0].shape[0]
+    copies = [
+        pltpu.make_async_copy(weights.at[f, s], held.at[s, pl.ds(f * size, size)], sems.at[s, f])
+        for s in range(stripes) for f in range(shards)
+    ]
+    for copy in copies:
+        copy.start()
     for s in range(stripes):
         cols = slice(s * TILE, (s + 1) * TILE)
-        stack = jnp.concatenate([weights[f, s] for f in range(shards)], axis=0)
-        pre = jnp.dot(pick(tiles, counts, tokens, s), stack, preferred_element_type=jnp.float32)
+        picked = pick(tiles, counts, tokens, s)
+        for copy in copies[s * shards:(s + 1) * shards]:
+            copy.wait()
+        pre = jnp.dot(picked, held[s], preferred_element_type=jnp.float32)
         act, slope = gelu_and_derivative(pre)
         act = act.astype(jnp.bfloat16)
         for i in range(len(refs)):
-            outs[(i % PAIR) * 2 + i // PAIR // part][i // PAIR % part, :, cols] = act[i * rows:(i + 1) * rows]
+            outs[i % PAIR][i // PAIR, :, cols] = act[i * rows:(i + 1) * rows]
         back = jnp.concatenate([arrays[a][b, :, cols] for a, b in refs], axis=0)
         slopes[:, cols] = (back.astype(jnp.float32) * slope).astype(jnp.bfloat16)
 
 
 def forward_call(tiles, counts, tokens, weights, arrays, refs):
     _, rows, width = arrays[0].shape
+    shards, stripes, size, _ = weights.shape
     blocks = len(refs)
     return pl.pallas_call(
         functools.partial(forward_kernel, len(tokens), refs),
-        out_shape=[jax.ShapeDtypeStruct((blocks // PAIR // 2, rows, width), jnp.bfloat16)] * 4
+        out_shape=[jax.ShapeDtypeStruct((blocks // PAIR, rows, width), jnp.bfloat16)] * PAIR
         + [jax.ShapeDtypeStruct((blocks * rows, width), jnp.bfloat16)],
-        in_specs=[SCALAR] * 2 + [RESIDENT] * (len(tokens) + 1 + len(arrays)),
-        out_specs=[RESIDENT] * 5,
+        in_specs=[SCALAR] * 2 + [RESIDENT] * len(tokens) + [pl.BlockSpec(memory_space=pltpu.HBM)] + [RESIDENT] * len(arrays),
+        out_specs=[RESIDENT] * 3,
+        scratch_shapes=[pltpu.VMEM((stripes, shards * size, TILE), jnp.bfloat16), pltpu.SemaphoreType.DMA((stripes, shards))],
         compiler_params=room(12),
         name="forward",
-    )(tiles, counts, *tokens, weights, *arrays)
+    )(tiles, counts, *tokens, pltpu.with_memory_space_constraint(weights, pltpu.HBM), *arrays)
 
 
 def backward_kernel(pieces, tiles, counts, own, *rest):
@@ -218,17 +214,18 @@
         pairs = [(a * tensor + b, (a ^ dz) * tensor + (b ^ dt)) for a in range(fsdp) for b in range(tensor)]
         return lax.ppermute(value, ("fsdp", "tensor"), pairs)
 
-    def exchange(arrays, groups, steps):
+    def exchange(arrays, steps):
+        groups, origins = [[(a, b) for b in range(tensor)] for a in range(PAIR)], [(a, 0) for a in range(PAIR)]
         for bit in steps:
             count = len(groups[0]) // 2
             arrays = arrays + [swap(take(arrays, [ref for group in groups for ref in group[count:]]), 0, bit)]
             new = [[(len(arrays) - 1, i * count + j) for j in range(count)] for i in range(len(groups))]
             groups = [group[:count] for group in groups] + new
-        return arrays, [group[0] for group in groups]
-
-    def interleave(home, away):
-        shifted = [(a + len(home[0]), b) for a, b in away[1]]
-        return home[0] + away[0], [ref for two in zip(home[1], shifted) for ref in two]
+            origins = origins + [(a, b ^ bit) for a, b in origins]
+        return arrays, [group[0] for group in groups], origins
+
+    def first_tiles(steps):
+        return jnp.stack([(t ^ b) * stripes + (half ^ a) * share for a, b in steps]).astype(jnp.int32)
 
     by_stripe = jnp.transpose(tile_weights, (1, 0, 2))
     outgoing = jnp.tile(by_stripe.reshape(PAIR, share, size, TILE), (fsdp // PAIR, 1, 1, 1))
@@ -237,36 +234,26 @@
     if not whole_tiles:
         weights = weights.transpose(1, 0, 2, 3).reshape(1, share, fsdp * size, TILE)
 
-    pieces, order = [jnp.concatenate([tokens, swap(tokens, 1, 0)], axis=0)], [0]
+    leave = cut_call(first_tiles([(1, b) for b in range(tensor)]), cotangent)
+    stay = cut_call(first_tiles([(0, b) for b in range(tensor)]), cotangent)
+    near = jnp.concatenate([tokens, swap(tokens, 1, 0)], axis=0)
     for bit in bits:
-        pieces = pieces + [swap(piece, 0, bit) for piece in pieces]
-        order = order + [b ^ bit for b in order]
-
-    starts = jnp.stack([(t ^ b) * stripes + (half ^ a) * share for a in range(PAIR) for b in range(tensor)]).astype(jnp.int32)
-    stay, leave = cut_call(starts, cotangent)
-    all_blocks = [[(0, b) for b in range(tensor)]]
-    arrays, refs = interleave(exchange([stay], all_blocks, bits), exchange([swap(leave, 1, 0)], all_blocks, bits))
+        far = swap(near, 0, bit)
+        if bit > 1:
+            near = jnp.concatenate([near, far], axis=0)
+    arrays, refs, _ = exchange([stay, swap(leave, 1, 0)], bits)
 
     tiles = lax.dynamic_slice_in_dim(tile_list, half * share, share, 0)
     counts = lax.dynamic_slice_in_dim(tile_counts, half * share, share, 0)
-    home_near, home_far, away_near, away_far, slopes = forward_call(tiles, counts, pieces, weights, arrays, refs)
-
-    part = tensor // 2
-    two_arrays = [[(i // part, i % part) for i in range(tensor)]]
-    steps = list(reversed(bits))
-    arrays, refs = interleave(
-        exchange([home_near, home_far], two_arrays, steps), exchange([swap(away_near, 1, 0), swap(away_far, 1, 0)], two_arrays, steps)
-    )
-    origins = [0]
-    for bit in steps:
-        origins = origins + [b ^ bit for b in origins]
-    starts = jnp.stack([(t ^ b) * stripes + (half ^ a) * share for b in origins for a in range(PAIR)]).astype(jnp.int32)
-    activations = join_call(starts, arrays, refs)
+    home, away, slopes = forward_call(tiles, counts, [near, far], weights, arrays, refs)
+
+    arrays, refs, origins = exchange([home, swap(away, 1, 0)], list(reversed(bits)))
+    activations = join_call(first_tiles(origins), arrays, refs)
 
     if whole_tiles:
-        grads, mine = backward_call(tiles, counts, own, pieces, slopes, fsdp)
+        grads, mine = backward_call(tiles, counts, own, [near, far], slopes, fsdp)
     else:
-        grads, mine = backward_call(tiles, counts, own * 0, pieces, slopes, 1)
+        grads, mine = backward_call(tiles, counts, own * 0, [near, far], slopes, 1)
         grads = grads.reshape(share, fsdp, size, TILE).transpose(1, 0, 2, 3)
         mine = lax.dynamic_index_in_dim(mine.reshape(share, fsdp, size, TILE), z, 1, keepdims=False)
     total = sum_call(own, lax.all_to_all(grads, "fsdp", split_axis=0, concat_axis=0, tiled=True), mine)

time: 91.7 us -> 70.9 us (0.77)
  waiting for transfers between devices: 48.6 us -> 35.8 us
  starting transfers between devices: 23.7 us -> 16.2 us
  Pallas kernels: 8.91 us -> 12.7 us
  local copies, waits for them, and re-layouts: 7.78 us -> 4.47 us
  other arithmetic: 1.4 us -> 0.33 us
    ppermute x15 -> x9, waiting for transfers between devices: 48.6 us -> 27.7 us  [swap(): return lax.ppermute(value, ('fsdp', 'tensor'), pairs)]
    ppermute x15 -> x9, starting transfers between devices: 13.3 us -> 7.27 us  [swap(): return lax.ppermute(value, ('fsdp', 'tensor'), pairs)]
    all_to_all x1, waiting for transfers between devices: 0.01 us -> 4.23 us  [body(): lax.all_to_all(grads, 'fsdp', split_axis=0, concat_axis=0, tiled=True)]
    all_to_all x1, waiting for transfers between devices: 0.01 us -> 3.89 us  [body(): lax.all_to_all(outgoing, 'fsdp', split_axis=0, concat_axis=0, tiled=True)]
    pallas_call x1, Pallas kernels: 2.24 us -> 4.66 us  [forward_call(): pl.pallas_call(functools.partial(forward_kernel, len(tokens), refs), out_...]
    unnamed x36 -> x23, local copies, waits for them, and re-layouts: 4.39 us -> 2.14 us
    pallas_call x1 -> x2, Pallas kernels: 1.76 us -> 3.17 us  [cut_call(): pl.pallas_call(cut_kernel, out_shape=jax.ShapeDtypeStruct((count, rows, w...]
    concatenate x4, other arithmetic: 1.4 us -> 0.15 us  [take(): return pieces[0] if len(pieces) == 1 else jnp.concatenate(pieces, axis=0)]
  transfers between devices with their start and end apart: 17 -> 11, of which waited for: 7 -> 8; matrix products, arithmetic and copies ran while one was open for 2% -> 3% of each run, Pallas kernels for 4% -> 10%
where the time goes in v9:
time: 70.9 us; the launch traced here: 70.5 us
  waiting for transfers between devices  35.8 us (50%)
  starting transfers between devices  16.2 us (23%)
  Pallas kernels  12.7 us (18%)
  local copies, waits for them, and re-layouts  4.47 us (6%)
  between operations  0.93 us (1%)
    ppermute x9, waiting for transfers between devices, swap(): return lax.ppermute(value, ('fsdp', 'tensor'), pairs)  27.7 us
    ppermute x9, starting transfers between devices, swap(): return lax.ppermute(value, ('fsdp', 'tensor'), pairs)  7.27 us
    all_to_all x1, starting transfers between devices, body(): lax.all_to_all(outgoing, 'fsdp', split_axis=0, concat_axis=0, tiled=True)  5.4 us
    pallas_call x1, Pallas kernels, forward_call(): pl.pallas_call(functools.partial(forward_kernel, len(tokens), refs), out_...  4.66 us
    all_to_all x1, waiting for transfers between devices, body(): lax.all_to_all(grads, 'fsdp', split_axis=0, concat_axis=0, tiled=True)  4.23 us
    all_to_all x1, waiting for transfers between devices, body(): lax.all_to_all(outgoing, 'fsdp', split_axis=0, concat_axis=0, tiled=True)  3.89 us
    all_to_all x1, starting transfers between devices, body(): lax.all_to_all(grads, 'fsdp', split_axis=0, concat_axis=0, tiled=True)  3.52 us
    pallas_call x2, Pallas kernels, cut_call(): pl.pallas_call(cut_kernel, out_shape=jax.ShapeDtypeStruct((count, rows, w...  3.17 us
  transfers between devices with their start and end apart: 11, of which 8 were waited for; matrix products, arithmetic and copies ran while one was open for 3% of the time, Pallas kernels for 10%

profile of v9, /device:TPU:0, one launch (start us, length us, event | category | flops | bytes accessed | tf_op | source)
XLA Modules:
  0.0 70.5 jit_solution(2261516075005294544)
XLA Ops:
  0.6 3.1 %collective-permute-start = (bf16[32,2560]{1,0:T(8,128)(2,1)}, bf16[32,2560]{1,0:T(8,128)(2,1)S(1)}, u32[]{:S(2)}, u32[]{:S(2)}) collective-permute-start(bf16[32,2560]{1,0:T(8,128)(2,1)} %param.5), channel_id=1, source_target_pairs={{0,4},{1,5},{2,6},{3,7},{4,0},{5,1},{6,2},{7,3},{8,12},{9,13},{10,... | collective-permute-start | bytes 491528 | tf_op jit(solution)/shard_map/ppermute | solution.py:215
  3.7 0.1 pad_add_fusion.1.starts
  3.8 1.6 %cut.3 = bf16[4,32,1280]{2,1,0:T(8,128)(2,1)S(1)} custom-call(s32[4]{0:T(128)S(1)} %pad_add_fusion.1.starts, bf16[32,10240]{1,0:T(8,128)(2,1)} %whole.3), custom_call_target="tpu_custom_call" | custom-call | tf_op jit(solution)/shard_map/cut/pallas_call | solution.py:49
  5.4 0.1 collective-permute-start.3
  5.5 1.1 %tile.11 = bf16[2,2,10,96,128]{4,3,2,1,0:T(8,128)(2,1)} broadcast(bf16[2,10,96,128]{3,2,1,0:T(8,128)(2,1)S(1)} %bitcast.17), dimensions={1,2,3,4} | broadcast | bytes 1474560 | tf_op jit(solution)/shard_map/tile | solution.py:231
  6.6 5.4 %all-to-all-start = ((bf16[4,10,96,128]{3,2,1,0:T(8,128)(2,1)}), bf16[4,10,96,128]{3,2,1,0:T(8,128)(2,1)}, u32[]{:S(2)}, u32[]{:S(2)}) async-start(bf16[4,10,96,128]{3,2,1,0:T(8,128)(2,1)} %bitcast.10), calls=%async_computation | async-start | bytes 1966080 | tf_op jit(solution)/shard_map/all_to_all | solution.py:232
  12.1 0.1 pad_add_fusion.starts
  12.1 1.6 %cut.2.rest_3_ = bf16[4,32,1280]{2,1,0:T(8,128)(2,1)S(1)} custom-call(s32[4]{0:T(128)S(1)} %pad_add_fusion.starts, bf16[32,10240]{1,0:T(8,128)(2,1)} %whole.3), custom_call_target="tpu_custom_call" | custom-call | tf_op jit(solution)/shard_map/cut/pallas_call | solution.py:49
  13.7 0.7 %copy-done.1 = bf16[4,32,1280]{2,1,0:T(8,128)(2,1)} copy-done((bf16[4,32,1280]{2,1,0:T(8,128)(2,1)}, bf16[4,32,1280]{2,1,0:T(8,128)(2,1)S(1)}, u32[]{:S(2)}) %copy-start.1) | copy-done | bytes 327704
  14.5 1.6 %collective-permute-start.1 = (bf16[64,2560]{1,0:T(8,128)(2,1)S(1)}, bf16[64,2560]{1,0:T(8,128)(2,1)S(1)}, u32[]{:S(2)}, u32[]{:S(2)}) collective-permute-start(bf16[64,2560]{1,0:T(8,128)(2,1)S(1)} %pad_maximum_fusion), channel_id=1, source_target_pairs={{0,2},{1,3},{2,0},{3,1},{4,6},{5,7},{6,4},{7,5},{8,10},{9,11},{10,... | collective-permute-start | bytes 983048 | tf_op jit(solution)/shard_map/ppermute | solution.py:215
  16.1 0.9 %slice-done.1 = bf16[2,32,1280]{2,1,0:T(8,128)(2,1)S(1)} async-done(((bf16[4,32,1280]{2,1,0:T(8,128)(2,1)}), bf16[2,32,1280]{2,1,0:T(8,128)(2,1)S(1)}, s32[]{:S(2)}) %slice-start.1) | async-done | bytes 163864 | tf_op jit(solution)/shard_map/slice | solution.py:201
  17.1 0.7 collective-permute-start.4
  17.7 7.5 %collective-permute-done.1 = bf16[64,2560]{1,0:T(8,128)(2,1)S(1)} collective-permute-done((bf16[64,2560]{1,0:T(8,128)(2,1)S(1)}, bf16[64,2560]{1,0:T(8,128)(2,1)S(1)}, u32[]{:S(2)}, u32[]{:S(2)}) %collective-permute-start.1) | collective-permute-done | bytes 327712 | tf_op jit(solution)/shard_map/ppermute | solution.py:215
  25.3 4.9 %collective-permute-done.4.rest_5_ = bf16[4,32,1280]{2,1,0:T(8,128)(2,1)S(1)} collective-permute-done((bf16[4,32,1280]{2,1,0:T(8,128)(2,1)S(1)}, bf16[4,32,1280]{2,1,0:T(8,128)(2,1)S(1)}, u32[]{:S(2)}, u32[]{:S(2)}) %collective-permute-start.4) | collective-permute-done | bytes 327712 | tf_op jit(solution)/shard_map/ppermute | solution.py:215
  30.4 0.7 copy-done.9
  31.1 0.1 dynamic_slice.7.counts
  31.2 0.1 constant_dynamic-slice_fusion
  31.2 0.1 copy.8.tiles
  31.3 0.7 collective-permute-done.5.rest_6_
  32.0 3.9 %all-to-all-done.rest_2_ = bf16[4,10,96,128]{3,2,1,0:T(8,128)(2,1)} async-done(((bf16[4,10,96,128]{3,2,1,0:T(8,128)(2,1)}), bf16[4,10,96,128]{3,2,1,0:T(8,128)(2,1)}, u32[]{:S(2)}, u32[]{:S(2)}) %all-to-all-start) | async-done | bytes 983072 | tf_op jit(solution)/shard_map/all_to_all | solution.py:232
  35.9 4.7 %forward.1 = (bf16[4,32,1280]{2,1,0:T(8,128)(2,1)S(1)}, bf16[4,32,1280]{2,1,0:T(8,128)(2,1)S(1)}, bf16[256,1280]{1,0:T(8,128)(2,1)S(1)}) custom-call(s32[10,3]{1,0:T(8,128)S(1)} %copy.8.tiles, s32[10]{0:T(128)S(1)} %dynamic_slice.7.counts, bf16[128,2560]{1,0:T(8,128)(2,1)S(1)} %constant_dynamic-update-slice_fusion.rest_0_, ...), custom_call_target="tpu_custom_call" | custom-call | tf_op jit(solution)/shard_map/forward/pallas_call | solution.py:118
  40.6 2.3 %backward.1 = (bf16[4,10,96,128]{3,2,1,0:T(8,128)(2,1)}, f32[10,96,128]{2,1,0:T(8,128)S(1)}) custom-call(s32[10,3]{1,0:T(8,128)S(1)} %copy.8.tiles, s32[10]{0:T(128)S(1)} %dynamic_slice.7.counts, s32[1]{0:T(128)} %bitcast.11.own, bf16[128,2560]{1,0:T(8,128)(2,1)S(1)} %constant_dynamic-update-slice_fusion.rest_0_, ...), custom_call_target="tpu_custom_call" | custom-call | tf_op jit(solution)/shard_map/backward/pallas_call | solution.py:150
  42.9 3.5 %all-to-all-start.1 = ((bf16[4,10,96,128]{3,2,1,0:T(8,128)(2,1)}), bf16[4,10,96,128]{3,2,1,0:T(8,128)(2,1)S(1)}, u32[]{:S(2)}, u32[]{:S(2)}) async-start(bf16[4,10,96,128]{3,2,1,0:T(8,128)(2,1)} %get-tuple-element.10), calls=%async_computation.1 | async-start | bytes 1966080 | tf_op jit(solution)/shard_map/all_to_all | solution.py:259
  46.5 5.5 %collective-permute-done.6.rest_1_ = bf16[4,32,1280]{2,1,0:T(8,128)(2,1)S(1)} collective-permute-done((bf16[4,32,1280]{2,1,0:T(8,128)(2,1)S(1)}, bf16[4,32,1280]{2,1,0:T(8,128)(2,1)S(1)}, u32[]{:S(2)}, u32[]{:S(2)}) %collective-permute-start.6) | collective-permute-done | bytes 327712 | tf_op jit(solution)/shard_map/ppermute | solution.py:215
  52.1 0.6 copy-done.3
  52.7 1.0 %collective-permute-done.7.rest_2_ = bf16[4,32,1280]{2,1,0:T(8,128)(2,1)S(1)} collective-permute-done((bf16[4,32,1280]{2,1,0:T(8,128)(2,1)S(1)}, bf16[4,32,1280]{2,1,0:T(8,128)(2,1)S(1)}, u32[]{:S(2)}, u32[]{:S(2)}) %collective-permute-start.7) | collective-permute-done | bytes 327712 | tf_op jit(solution)/shard_map/ppermute | solution.py:215
  53.8 1.6 %collective-permute-start.8 = (bf16[4,32,1280]{2,1,0:T(8,128)(2,1)S(1)}, bf16[4,32,1280]{2,1,0:T(8,128)(2,1)S(1)}, u32[]{:S(2)}, u32[]{:S(2)}) collective-permute-start(bf16[4,32,1280]{2,1,0:T(8,128)(2,1)S(1)} %pad_maximum_fusion.4), channel_id=1, source_target_pairs={{0,2},{1,3},{2,0},{3,1},{4,6},{5,7},{6,4},{7,5},{8,10},{9,11},{10,... | collective-permute-start | bytes 983048 | tf_op jit(solution)/shard_map/ppermute | solution.py:215
  55.4 0.1 stack.49.starts
  55.4 8.2 %collective-permute-done.8.rest_3_ = bf16[4,32,1280]{2,1,0:T(8,128)(2,1)S(1)} collective-permute-done((bf16[4,32,1280]{2,1,0:T(8,128)(2,1)S(1)}, bf16[4,32,1280]{2,1,0:T(8,128)(2,1)S(1)}, u32[]{:S(2)}, u32[]{:S(2)}) %collective-permute-start.8) | collective-permute-done | bytes 327712 | tf_op jit(solution)/shard_map/ppermute | solution.py:215
  63.6 1.4 %join.1 = bf16[32,10240]{1,0:T(8,128)(2,1)} custom-call(s32[8]{0:T(128)S(1)} %stack.49.starts, bf16[4,32,1280]{2,1,0:T(8,128)(2,1)S(1)} %get-tuple-element.7.rest_0_, bf16[4,32,1280]{2,1,0:T(8,128)(2,1)S(1)} %copy-done.4, bf16[4,32,1280]{2,1,0:T(8,128)(2,1)S(1)} %collective-permute-done.7.rest_2_, bf16[4,32,1280]{2,1,0:T(8,128)(2,1)S(1)} %collective-permute-done.8.rest_3_), custom_call_target="tpu_custom_call" | custom-call | tf_op jit(solution)/shard_map/join/pallas_call | solution.py:69
  65.1 4.2 %all-to-all-done.1.grads = bf16[4,10,96,128]{3,2,1,0:T(8,128)(2,1)S(1)} async-done(((bf16[4,10,96,128]{3,2,1,0:T(8,128)(2,1)}), bf16[4,10,96,128]{3,2,1,0:T(8,128)(2,1)S(1)}, u32[]{:S(2)}, u32[]{:S(2)}) %all-to-all-start.1) | async-done | bytes 983072 | tf_op jit(solution)/shard_map/all_to_all | solution.py:259
  69.3 1.2 %sum.1 = f32[2,10,96,128]{3,2,1,0:T(8,128)} custom-call(s32[1]{0:T(128)} %bitcast.11.own, bf16[4,10,96,128]{3,2,1,0:T(8,128)(2,1)S(1)} %all-to-all-done.1.grads, f32[10,96,128]{2,1,0:T(8,128)S(1)} %get-tuple-element.11.mine), custom_call_target="tpu_custom_call" | custom-call | tf_op jit(solution)/shard_map/sum/pallas_call | solution.py:183
  (45 shorter events, 0.7 us)
Async XLA Ops:
  0.6 30.5 %copy-start = (s32[20,3]{0,1:T(4,128)S(1)}, s32[20,3]{0,1:T(4,128)}, u32[]{:S(2)}) copy-start(s32[20,3]{0,1:T(4,128)} %param.8) | copy-start | bytes 724
  0.6 13.8 %collective-permute-start = (bf16[32,2560]{1,0:T(8,128)(2,1)}, bf16[32,2560]{1,0:T(8,128)(2,1)S(1)}, u32[]{:S(2)}, u32[]{:S(2)}) collective-permute-start(bf16[32,2560]{1,0:T(8,128)(2,1)} %param.5), channel_id=1, source_target_pairs={{0,4},{1,5},{2,6},{3,7},{4,0},{5,1},{6,2},{7,3},{8,12},{9,13},{10,... | collective-permute-start | bytes 491528 | tf_op jit(solution)/shard_map/ppermute | solution.py:215
  3.8 1.7 %copy-start.8 = (bf16[96,20,128]{2,0,1:T(8,128)(2,1)S(1)}, bf16[96,20,128]{2,0,1:T(8,128)(2,1)}, u32[]{:S(2)}) copy-start(bf16[96,20,128]{2,0,1:T(8,128)(2,1)} %param.6) | copy-start | bytes 1474564
  5.4 10.7 %collective-permute-start.3 = (bf16[4,32,1280]{2,1,0:T(8,128)(2,1)S(1)}, bf16[4,32,1280]{2,1,0:T(8,128)(2,1)S(1)}, u32[]{:S(2)}, u32[]{:S(2)}) collective-permute-start(bf16[4,32,1280]{2,1,0:T(8,128)(2,1)S(1)} %cut.3), channel_id=1, source_target_pairs={{0,4},{1,5},{2,6},{3,7},{4,0},{5,1},{6,2},{7,3},{8,12},{9,13},{10,... | collective-permute-start | bytes 983048 | tf_op jit(solution)/shard_map/ppermute | solution.py:215
  6.6 5.4 %copy-start.7 = (bf16[32,2560]{1,0:T(8,128)(2,1)S(1)}, bf16[32,2560]{1,0:T(8,128)(2,1)}, u32[]{:S(2)}) copy-start(bf16[32,2560]{1,0:T(8,128)(2,1)} %param.5) | copy-start | bytes 491524
  6.6 29.3 %all-to-all-start = ((bf16[4,10,96,128]{3,2,1,0:T(8,128)(2,1)}), bf16[4,10,96,128]{3,2,1,0:T(8,128)(2,1)}, u32[]{:S(2)}, u32[]{:S(2)}) async-start(bf16[4,10,96,128]{3,2,1,0:T(8,128)(2,1)} %bitcast.10), calls=%async_computation | async-start | bytes 1966080 | tf_op jit(solution)/shard_map/all_to_all | solution.py:232
  13.7 0.7 %copy-start.1 = (bf16[4,32,1280]{2,1,0:T(8,128)(2,1)}, bf16[4,32,1280]{2,1,0:T(8,128)(2,1)S(1)}, u32[]{:S(2)}) copy-start(bf16[4,32,1280]{2,1,0:T(8,128)(2,1)S(1)} %cut.2.rest_3_) | copy-start | bytes 983044
  14.5 10.7 %collective-permute-start.1 = (bf16[64,2560]{1,0:T(8,128)(2,1)S(1)}, bf16[64,2560]{1,0:T(8,128)(2,1)S(1)}, u32[]{:S(2)}, u32[]{:S(2)}) collective-permute-start(bf16[64,2560]{1,0:T(8,128)(2,1)S(1)} %pad_maximum_fusion), channel_id=1, source_target_pairs={{0,2},{1,3},{2,0},{3,1},{4,6},{5,7},{6,4},{7,5},{8,10},{9,11},{10,... | collective-permute-start | bytes 983048 | tf_op jit(solution)/shard_map/ppermute | solution.py:215
  16.1 1.0 %slice-start.1 = ((bf16[4,32,1280]{2,1,0:T(8,128)(2,1)}), bf16[2,32,1280]{2,1,0:T(8,128)(2,1)S(1)}, s32[]{:S(2)}) async-start(bf16[4,32,1280]{2,1,0:T(8,128)(2,1)} %copy-done.1), calls=%async_computation.3 | async-start | bytes 327680 | tf_op jit(solution)/shard_map/slice | solution.py:201
  16.1 1.6 %copy-start.5 = (bf16[4,32,1280]{2,1,0:T(8,128)(2,1)}, bf16[4,32,1280]{2,1,0:T(8,128)(2,1)S(1)}, u32[]{:S(2)}) copy-start(bf16[4,32,1280]{2,1,0:T(8,128)(2,1)S(1)} %collective-permute-done.3.rest_4_) | copy-start | bytes 983044
  17.1 13.1 %collective-permute-start.4 = (bf16[4,32,1280]{2,1,0:T(8,128)(2,1)S(1)}, bf16[4,32,1280]{2,1,0:T(8,128)(2,1)S(1)}, u32[]{:S(2)}, u32[]{:S(2)}) collective-permute-start(bf16[4,32,1280]{2,1,0:T(8,128)(2,1)S(1)} %pad_maximum_fusion.1), channel_id=1, source_target_pairs={{0,2},{1,3},{2,0},{3,1},{4,6},{5,7},{6,4},{7,5},{8,10},{9,11},{10,... | collective-permute-start | bytes 983048 | tf_op jit(solution)/shard_map/ppermute | solution.py:215
  25.2 5.0 %slice-start = ((bf16[4,32,1280]{2,1,0:T(8,128)(2,1)}), bf16[1,32,1280]{2,1,0:T(8,128)(2,1)S(1)}, s32[]{:S(2)}) async-start(bf16[4,32,1280]{2,1,0:T(8,128)(2,1)} %copy-done.1), calls=%async_computation.2 | async-start | bytes 163840 | tf_op jit(solution)/shard_map/slice | solution.py:201
  25.2 5.0 %slice-start.3 = ((bf16[4,32,1280]{2,1,0:T(8,128)(2,1)}), bf16[1,32,1280]{2,1,0:T(8,128)(2,1)S(1)}, s32[]{:S(2)}) async-start(bf16[4,32,1280]{2,1,0:T(8,128)(2,1)} %copy-done.5), calls=%async_computation.5 | async-start | bytes 163840 | tf_op jit(solution)/shard_map/slice | solution.py:201
  25.3 6.7 %collective-permute-start.2 = (bf16[128,2560]{1,0:T(8,128)(2,1)S(1)}, bf16[128,2560]{1,0:T(8,128)(2,1)S(1)}, u32[]{:S(2)}, u32[]{:S(2)}) collective-permute-start(bf16[128,2560]{1,0:T(8,128)(2,1)S(1)} %constant_dynamic-update-slice_fusion.rest_0_), channel_id=1, source_target_pairs={{0,1},{1,0},{2,3},{3,2},{4,5},{5,4},{6,7},{7,6},{8,9},{9,8},{10,11... | collective-permute-start | bytes 1966088 | tf_op jit(solution)/shard_map/ppermute | solution.py:215
  30.2 5.7 %copy-start.2 = (bf16[4,32,1280]{2,1,0:T(8,128)(2,1)S(1)}, bf16[4,32,1280]{2,1,0:T(8,128)(2,1)}, u32[]{:S(2)}) copy-start(bf16[4,32,1280]{2,1,0:T(8,128)(2,1)} %copy-done.1) | copy-start | bytes 983044
  30.2 5.7 %copy-start.6 = (bf16[4,32,1280]{2,1,0:T(8,128)(2,1)S(1)}, bf16[4,32,1280]{2,1,0:T(8,128)(2,1)}, u32[]{:S(2)}) copy-start(bf16[4,32,1280]{2,1,0:T(8,128)(2,1)} %copy-done.5) | copy-start | bytes 983044
  30.3 1.7 %collective-permute-start.5 = (bf16[4,32,1280]{2,1,0:T(8,128)(2,1)S(1)}, bf16[4,32,1280]{2,1,0:T(8,128)(2,1)S(1)}, u32[]{:S(2)}, u32[]{:S(2)}) collective-permute-start(bf16[4,32,1280]{2,1,0:T(8,128)(2,1)S(1)} %pad_maximum_fusion.2), channel_id=1, source_target_pairs={{0,1},{1,0},{2,3},{3,2},{4,5},{5,4},{6,7},{7,6},{8,9},{9,8},{10,11... | collective-permute-start | bytes 983048 | tf_op jit(solution)/shard_map/ppermute | solution.py:215
  30.4 0.7 copy-start.9
  40.6 11.4 %collective-permute-start.6 = (bf16[4,32,1280]{2,1,0:T(8,128)(2,1)S(1)}, bf16[4,32,1280]{2,1,0:T(8,128)(2,1)S(1)}, u32[]{:S(2)}, u32[]{:S(2)}) collective-permute-start(bf16[4,32,1280]{2,1,0:T(8,128)(2,1)S(1)} %get-tuple-element.8), channel_id=1, source_target_pairs={{0,4},{1,5},{2,6},{3,7},{4,0},{5,1},{6,2},{7,3},{8,12},{9,13},{10,... | collective-permute-start | bytes 983048 | tf_op jit(solution)/shard_map/ppermute | solution.py:215
  42.9 26.4 %all-to-all-start.1 = ((bf16[4,10,96,128]{3,2,1,0:T(8,128)(2,1)}), bf16[4,10,96,128]{3,2,1,0:T(8,128)(2,1)S(1)}, u32[]{:S(2)}, u32[]{:S(2)}) async-start(bf16[4,10,96,128]{3,2,1,0:T(8,128)(2,1)} %get-tuple-element.10), calls=%async_computation.1 | async-start | bytes 1966080 | tf_op jit(solution)/shard_map/all_to_all | solution.py:259
  52.0 0.7 %copy-start.3 = (bf16[4,32,1280]{2,1,0:T(8,128)(2,1)}, bf16[4,32,1280]{2,1,0:T(8,128)(2,1)S(1)}, u32[]{:S(2)}) copy-start(bf16[4,32,1280]{2,1,0:T(8,128)(2,1)S(1)} %collective-permute-done.6.rest_1_) | copy-start | bytes 983044
  52.0 1.7 %collective-permute-start.7 = (bf16[4,32,1280]{2,1,0:T(8,128)(2,1)S(1)}, bf16[4,32,1280]{2,1,0:T(8,128)(2,1)S(1)}, u32[]{:S(2)}, u32[]{:S(2)}) collective-permute-start(bf16[4,32,1280]{2,1,0:T(8,128)(2,1)S(1)} %pad_maximum_fusion.3), channel_id=1, source_target_pairs={{0,1},{1,0},{2,3},{3,2},{4,5},{5,4},{6,7},{7,6},{8,9},{9,8},{10,11... | collective-permute-start | bytes 983048 | tf_op jit(solution)/shard_map/ppermute | solution.py:215
  52.7 1.0 %slice-start.2 = ((bf16[4,32,1280]{2,1,0:T(8,128)(2,1)}), bf16[1,32,1280]{2,1,0:T(8,128)(2,1)S(1)}, s32[]{:S(2)}) async-start(bf16[4,32,1280]{2,1,0:T(8,128)(2,1)} %copy-done.3), calls=%async_computation.4 | async-start | bytes 163840 | tf_op jit(solution)/shard_map/slice | solution.py:201
  53.7 9.9 %copy-start.4 = (bf16[4,32,1280]{2,1,0:T(8,128)(2,1)S(1)}, bf16[4,32,1280]{2,1,0:T(8,128)(2,1)}, u32[]{:S(2)}) copy-start(bf16[4,32,1280]{2,1,0:T(8,128)(2,1)} %copy-done.3) | copy-start | bytes 983044
  53.8 9.8 %collective-permute-start.8 = (bf16[4,32,1280]{2,1,0:T(8,128)(2,1)S(1)}, bf16[4,32,1280]{2,1,0:T(8,128)(2,1)S(1)}, u32[]{:S(2)}, u32[]{:S(2)}) collective-permute-start(bf16[4,32,1280]{2,1,0:T(8,128)(2,1)S(1)} %pad_maximum_fusion.4), channel_id=1, source_target_pairs={{0,2},{1,3},{2,0},{3,1},{4,6},{5,7},{6,4},{7,5},{8,10},{9,11},{10,... | collective-permute-start | bytes 983048 | tf_op jit(solution)/shard_map/ppermute | solution.py:215

commit v10 on v9

--- a/solution.py
+++ b/solution.py
@@ -11,6 +11,7 @@
 SLOTS = 3
 PAIR = 2
 ROWS = 16
+HEAD = 2
 ROOT = 0.7978845608028654
 CUBIC = 0.044715
 ANYWHERE = pl.BlockSpec(memory_space=pl.ANY)
@@ -86,22 +87,40 @@
     return jnp.concatenate(picked, axis=1)
 
 
-def forward_kernel(pieces, refs, tiles, counts, *rest):
-    tokens, weights, arrays = rest[:pieces], rest[pieces], rest[pieces + 1:-5]
-    outs, slopes, held, sems = rest[-5:-3], rest[-3], rest[-2], rest[-1]
+def turn_kernel(near, far, turned):
+    for i in range(turned.shape[0]):
+        cols = slice(i * TILE, (i + 1) * TILE)
+        turned[i] = jnp.concatenate([near[:, cols], far[:, cols]], axis=0).T
+
+
+def turn_call(near, far):
+    return pl.pallas_call(
+        turn_kernel,
+        out_shape=jax.ShapeDtypeStruct((near.shape[1] // TILE, TILE, near.shape[0] + far.shape[0]), near.dtype),
+        in_specs=[RESIDENT] * 2,
+        out_specs=RESIDENT,
+        compiler_params=room(12),
+        name="turn",
+    )(near, far)
+
+
+def forward_kernel(refs, tiles, counts, near, far, _, weights, *rest):
+    arrays, outs, slopes, held, sems = rest[:-5], rest[-5:-3], rest[-3], rest[-2], rest[-1]
     shards, stripes, size, _ = weights.shape
     rows = arrays[0].shape[1]
-    copies = [
-        pltpu.make_async_copy(weights.at[f, s], held.at[s, pl.ds(f * size, size)], sems.at[s, f])
-        for s in range(stripes) for f in range(shards)
-    ]
-    for copy in copies:
-        copy.start()
+    first = min(HEAD, stripes)
+    copies = {}
+    for c, (low, high) in enumerate(((0, first), (first, stripes))):
+        for f in range(shards if low < high else 0):
+            span = pl.ds(low, high - low)
+            copies[low, f] = pltpu.make_async_copy(weights.at[f, span], held.at[span, pl.ds(f * size, size)], sems.at[c, f])
+            copies[low, f].start()
     for s in range(stripes):
         cols = slice(s * TILE, (s + 1) * TILE)
-        picked = pick(tiles, counts, tokens, s)
-        for copy in copies[s * shards:(s + 1) * shards]:
-            copy.wait()
+        picked = pick(tiles, counts, (near, far), s)
+        for f in range(shards):
+            if (s, f) in copies:
+                copies[s, f].wait()
         pre = jnp.dot(picked, held[s], preferred_element_type=jnp.float32)
         act, slope = gelu_and_derivative(pre)
         act = act.astype(jnp.bfloat16)
@@ -111,31 +130,32 @@
         slopes[:, cols] = (back.astype(jnp.float32) * slope).astype(jnp.bfloat16)
 
 
-def forward_call(tiles, counts, tokens, weights, arrays, refs):
+def forward_call(tiles, counts, near, far, turned, weights, arrays, refs):
     _, rows, width = arrays[0].shape
     shards, stripes, size, _ = weights.shape
     blocks = len(refs)
     return pl.pallas_call(
-        functools.partial(forward_kernel, len(tokens), refs),
+        functools.partial(forward_kernel, refs),
         out_shape=[jax.ShapeDtypeStruct((blocks // PAIR, rows, width), jnp.bfloat16)] * PAIR
         + [jax.ShapeDtypeStruct((blocks * rows, width), jnp.bfloat16)],
-        in_specs=[SCALAR] * 2 + [RESIDENT] * len(tokens) + [pl.BlockSpec(memory_space=pltpu.HBM)] + [RESIDENT] * len(arrays),
+        in_specs=[SCALAR] * 2 + [RESIDENT] * 2 + [ANYWHERE, pl.BlockSpec(memory_space=pltpu.HBM)] + [RESIDENT] * len(arrays),
         out_specs=[RESIDENT] * 3,
-        scratch_shapes=[pltpu.VMEM((stripes, shards * size, TILE), jnp.bfloat16), pltpu.SemaphoreType.DMA((stripes, shards))],
+        scratch_shapes=[pltpu.VMEM((stripes, shards * size, TILE), jnp.bfloat16), pltpu.SemaphoreType.DMA((2, shards))],
         compiler_params=room(12),
         name="forward",
-    )(tiles, counts, *tokens, pltpu.with_memory_space_constraint(weights, pltpu.HBM), *arrays)
-
-
-def backward_kernel(pieces, tiles, counts, own, *rest):
-    tokens, slopes, grads, mine, term, sent, sems = rest[:pieces], *rest[pieces:]
+    )(tiles, counts, near, far, turned, pltpu.with_memory_space_constraint(weights, pltpu.HBM), *arrays)
+
+
+def backward_kernel(tiles, counts, own, turned, slopes, grads, mine, term, sent, sems):
     shards, stripes, size, _ = grads.shape
     span = pl.ds(pl.multiple_of(own[0] * size, size), size)
     copies = []
     for s in range(stripes):
-        picked = pick(tiles, counts, tokens, s)
-        slope = slopes[:, s * TILE:(s + 1) * TILE]
-        term[s] = lax.dot_general(picked, slope, (((0,), (0,)), ((), ())), preferred_element_type=jnp.float32)
+        picked = jnp.concatenate([turned[tiles[s, k]] for k in range(SLOTS)], axis=0)
+        sums = jnp.dot(picked, slopes[:, s * TILE:(s + 1) * TILE], preferred_element_type=jnp.float32)
+        for k in range(SLOTS):
+            block = sums[k * TILE:(k + 1) * TILE]
+            term[s, k * TILE:(k + 1) * TILE] = jnp.where(k < counts[s], block, jnp.zeros_like(block))
         for f in range(shards):
             sent[s, f] = term[s, f * size:(f + 1) * size].astype(sent.dtype)
         copies.append(pltpu.make_async_copy(sent.at[s], grads.at[:, s], sems.at[s]))
@@ -145,12 +165,12 @@
         copy.wait()
 
 
-def backward_call(tiles, counts, own, tokens, slopes, shards):
+def backward_call(tiles, counts, own, turned, slopes, shards):
     stripes, size = slopes.shape[1] // TILE, SLOTS * TILE // shards
     return pl.pallas_call(
-        functools.partial(backward_kernel, len(tokens)),
+        backward_kernel,
         out_shape=[pltpu.HBM((shards, stripes, size, TILE), jnp.bfloat16), jax.ShapeDtypeStruct((stripes, size, TILE), jnp.float32)],
-        in_specs=[SCALAR] * 3 + [RESIDENT] * (len(tokens) + 1),
+        in_specs=[SCALAR] * 3 + [RESIDENT] * 2,
         out_specs=[pl.BlockSpec(memory_space=pltpu.HBM), RESIDENT],
         scratch_shapes=[
             pltpu.VMEM((stripes, SLOTS * TILE, TILE), jnp.float32),
@@ -159,7 +179,7 @@
         ],
         compiler_params=room(12),
         name="backward",
-    )(tiles, counts, own, *tokens, slopes)
+    )(tiles, counts, own, turned, slopes)
 
 
 def sum_kernel(own, grads, mine, total, held, sems):
@@ -245,15 +265,16 @@
 
     tiles = lax.dynamic_slice_in_dim(tile_list, half * share, share, 0)
     counts = lax.dynamic_slice_in_dim(tile_counts, half * share, share, 0)
-    home, away, slopes = forward_call(tiles, counts, [near, far], weights, arrays, refs)
+    turned = turn_call(near, far)
+    home, away, slopes = forward_call(tiles, counts, near, far, turned, weights, arrays, refs)
 
     arrays, refs, origins = exchange([home, swap(away, 1, 0)], list(reversed(bits)))
     activations = join_call(first_tiles(origins), arrays, refs)
 
     if whole_tiles:
-        grads, mine = backward_call(tiles, counts, own, [near, far], slopes, fsdp)
+        grads, mine = backward_call(tiles, counts, own, turned, slopes, fsdp)
     else:
-        grads, mine = backward_call(tiles, counts, own * 0, [near, far], slopes, 1)
+        grads, mine = backward_call(tiles, counts, own * 0, turned, slopes, 1)
         grads = grads.reshape(share, fsdp, size, TILE).transpose(1, 0, 2, 3)
         mine = lax.dynamic_index_in_dim(mine.reshape(share, fsdp, size, TILE), z, 1, keepdims=False)
     total = sum_call(own, lax.all_to_all(grads, "fsdp", split_axis=0, concat_axis=0, tiled=True), mine)

time: 70.9 us -> 71.4 us (level)
  local copies, waits for them, and re-layouts: 4.47 us -> 2.57 us
  waiting for transfers between devices: 35.8 us -> 36.8 us
  starting transfers between devices: 16.2 us -> 17.1 us
  other arithmetic: 0.33 us -> 1.11 us
    ppermute x9, waiting for transfers between devices: 27.7 us -> 29.3 us  [swap(): return lax.ppermute(value, ('fsdp', 'tensor'), pairs)]
    unnamed x23 -> x19, local copies, waits for them, and re-layouts: 2.14 us -> 1.13 us
    slice x14 -> x10, local copies, waits for them, and re-layouts: 0.99 us -> 0.1 us  [take(): arrays[a][low:high]]
    ppermute x9, starting transfers between devices: 7.27 us -> 8.09 us  [swap(): return lax.ppermute(value, ('fsdp', 'tensor'), pairs)]
    concatenate x4, other arithmetic: 0.15 us -> 0.93 us  [take(): return pieces[0] if len(pieces) == 1 else jnp.concatenate(pieces, axis=0)]
    pallas_call x2 -> x3, Pallas kernels: 6.93 us -> 6.73 us  [the longest x1 4.11 us: forward_call(): pl.pallas_call(functools.partial(forward_kernel, refs), out_shape=[jax.Sh...]
  transfers between devices with their start and end apart: 11 -> 11, of which waited for: 8 -> 9; matrix products, arithmetic and copies ran while one was open for 3% -> 4% of each run, Pallas kernels for 10% -> 10%
where the time goes in v10:
time: 71.4 us; the launch traced here: 71 us
  waiting for transfers between devices  36.8 us (52%)
  starting transfers between devices  17.1 us (24%)
  Pallas kernels  12.5 us (18%)
  local copies, waits for them, and re-layouts  2.57 us (4%)
  other arithmetic  1.11 us (2%)
  between operations  0.91 us (1%)
    ppermute x9, waiting for transfers between devices, swap(): return lax.ppermute(value, ('fsdp', 'tensor'), pairs)  29.3 us
    ppermute x9, starting transfers between devices, swap(): return lax.ppermute(value, ('fsdp', 'tensor'), pairs)  8.09 us
    all_to_all x1, starting transfers between devices, body(): lax.all_to_all(outgoing, 'fsdp', split_axis=0, concat_axis=0, tiled=True)  5.41 us
    pallas_call x1, Pallas kernels, forward_call(): pl.pallas_call(functools.partial(forward_kernel, refs), out_shape=[jax.Sh...  4.11 us
    all_to_all x1, waiting for transfers between devices, body(): lax.all_to_all(grads, 'fsdp', split_axis=0, concat_axis=0, tiled=True)  3.94 us
    all_to_all x1, starting transfers between devices, body(): lax.all_to_all(grads, 'fsdp', split_axis=0, concat_axis=0, tiled=True)  3.66 us
    all_to_all x1, waiting for transfers between devices, body(): lax.all_to_all(outgoing, 'fsdp', split_axis=0, concat_axis=0, tiled=True)  3.57 us
    pallas_call x2, Pallas kernels, cut_call(): pl.pallas_call(cut_kernel, out_shape=jax.ShapeDtypeStruct((count, rows, w...  3.17 us
  transfers between devices with their start and end apart: 11, of which 9 were waited for; matrix products, arithmetic and copies ran while one was open for 4% of the time, Pallas kernels for 10%

profile of v10, /device:TPU:0, one launch (start us, length us, event | category | flops | bytes accessed | tf_op | source)
XLA Modules:
  0.0 71.0 jit_solution(14007429499642426679)
XLA Ops:
  0.7 3.1 %collective-permute-start = (bf16[32,2560]{1,0:T(8,128)(2,1)}, bf16[32,2560]{1,0:T(8,128)(2,1)S(1)}, u32[]{:S(2)}, u32[]{:S(2)}) collective-permute-start(bf16[32,2560]{1,0:T(8,128)(2,1)} %param.5), channel_id=1, source_target_pairs={{0,4},{1,5},{2,6},{3,7},{4,0},{5,1},{6,2},{7,3},{8,12},{9,13},{10,... | collective-permute-start | bytes 491528 | tf_op jit(solution)/shard_map/ppermute | solution.py:235
  3.7 0.1 pad_add_fusion.1.starts
  3.8 1.6 %cut.3 = bf16[4,32,1280]{2,1,0:T(8,128)(2,1)S(1)} custom-call(s32[4]{0:T(128)S(1)} %pad_add_fusion.1.starts, bf16[32,10240]{1,0:T(8,128)(2,1)} %whole.3), custom_call_target="tpu_custom_call" | custom-call | tf_op jit(solution)/shard_map/cut/pallas_call | solution.py:50
  5.4 0.1 collective-permute-start.3
  5.5 1.1 %tile.11 = bf16[2,2,10,96,128]{4,3,2,1,0:T(8,128)(2,1)} broadcast(bf16[2,10,96,128]{3,2,1,0:T(8,128)(2,1)S(1)} %bitcast.17), dimensions={1,2,3,4} | broadcast | bytes 1474560 | tf_op jit(solution)/shard_map/tile | solution.py:251
  6.6 5.4 %all-to-all-start = ((bf16[4,10,96,128]{3,2,1,0:T(8,128)(2,1)}), bf16[4,10,96,128]{3,2,1,0:T(8,128)(2,1)}, u32[]{:S(2)}, u32[]{:S(2)}) async-start(bf16[4,10,96,128]{3,2,1,0:T(8,128)(2,1)} %bitcast.10), calls=%async_computation | async-start | bytes 1966080 | tf_op jit(solution)/shard_map/all_to_all | solution.py:252
  12.1 0.1 pad_add_fusion.starts
  12.1 1.6 %cut.2.rest_0_ = bf16[4,32,1280]{2,1,0:T(8,128)(2,1)S(1)} custom-call(s32[4]{0:T(128)S(1)} %pad_add_fusion.starts, bf16[32,10240]{1,0:T(8,128)(2,1)} %whole.3), custom_call_target="tpu_custom_call" | custom-call | tf_op jit(solution)/shard_map/cut/pallas_call | solution.py:50
  13.8 1.6 %collective-permute-start.1 = (bf16[64,2560]{1,0:T(8,128)(2,1)S(1)}, bf16[64,2560]{1,0:T(8,128)(2,1)S(1)}, u32[]{:S(2)}, u32[]{:S(2)}) collective-permute-start(bf16[64,2560]{1,0:T(8,128)(2,1)S(1)} %pad_maximum_fusion), channel_id=1, source_target_pairs={{0,2},{1,3},{2,0},{3,1},{4,6},{5,7},{6,4},{7,5},{8,10},{9,11},{10,... | collective-permute-start | bytes 983048 | tf_op jit(solution)/shard_map/ppermute | solution.py:235
  15.4 0.7 %collective-permute-done.3.rest_1_ = bf16[4,32,1280]{2,1,0:T(8,128)(2,1)S(1)} collective-permute-done((bf16[4,32,1280]{2,1,0:T(8,128)(2,1)S(1)}, bf16[4,32,1280]{2,1,0:T(8,128)(2,1)S(1)}, u32[]{:S(2)}, u32[]{:S(2)}) %collective-permute-start.3) | collective-permute-done | bytes 327712 | tf_op jit(solution)/shard_map/ppermute | solution.py:235
  16.2 1.6 %collective-permute-start.4 = (bf16[4,32,1280]{2,1,0:T(8,128)(2,1)S(1)}, bf16[4,32,1280]{2,1,0:T(8,128)(2,1)S(1)}, u32[]{:S(2)}, u32[]{:S(2)}) collective-permute-start(bf16[4,32,1280]{2,1,0:T(8,128)(2,1)S(1)} %pad_maximum_fusion.1), channel_id=1, source_target_pairs={{0,2},{1,3},{2,0},{3,1},{4,6},{5,7},{6,4},{7,5},{8,10},{9,11},{10,... | collective-permute-start | bytes 983048 | tf_op jit(solution)/shard_map/ppermute | solution.py:235
  17.8 6.8 %collective-permute-done.1 = bf16[64,2560]{1,0:T(8,128)(2,1)S(1)} collective-permute-done((bf16[64,2560]{1,0:T(8,128)(2,1)S(1)}, bf16[64,2560]{1,0:T(8,128)(2,1)S(1)}, u32[]{:S(2)}, u32[]{:S(2)}) %collective-permute-start.1) | collective-permute-done | bytes 327712 | tf_op jit(solution)/shard_map/ppermute | solution.py:235
  24.6 4.9 %collective-permute-done.4.rest_2_ = bf16[4,32,1280]{2,1,0:T(8,128)(2,1)S(1)} collective-permute-done((bf16[4,32,1280]{2,1,0:T(8,128)(2,1)S(1)}, bf16[4,32,1280]{2,1,0:T(8,128)(2,1)S(1)}, u32[]{:S(2)}, u32[]{:S(2)}) %collective-permute-start.4) | collective-permute-done | bytes 327712 | tf_op jit(solution)/shard_map/ppermute | solution.py:235
  29.5 0.8 %pad_maximum_fusion.2 = bf16[4,32,1280]{2,1,0:T(8,128)(2,1)} fusion(bf16[1,32,1280]{2,1,0:T(8,128)(2,1)S(1)} %get-tuple-element.15, bf16[1,32,1280]{2,1,0:T(8,128)(2,1)S(1)} %get-tuple-element.14, bf16[1,32,1280]{2,1,0:T(8,128)(2,1)S(1)} %slice.51, bf16[1,32,1280]{2,1,0:T(8,128)(2,1)S(1)} %slice.50), kind=kLoop, calls=%fused_computation.2 | loop fusion | flops 491520 | bytes 655360 | tf_op jit(solution)/shard_map/concatenate | solution.py:222
  30.4 0.1 dynamic_slice.7.counts
  30.4 0.1 constant_dynamic-slice_fusion
  30.5 0.1 copy.8.tiles
  30.6 0.4 turn.1._.turned
  31.0 1.3 %collective-permute-done.5.rest_3_ = bf16[4,32,1280]{2,1,0:T(8,128)(2,1)} collective-permute-done((bf16[4,32,1280]{2,1,0:T(8,128)(2,1)}, bf16[4,32,1280]{2,1,0:T(8,128)(2,1)}, u32[]{:S(2)}, u32[]{:S(2)}) %collective-permute-start.5) | collective-permute-done | bytes 327712 | tf_op jit(solution)/shard_map/ppermute | solution.py:235
  32.3 3.6 %all-to-all-done.weights = bf16[4,10,96,128]{3,2,1,0:T(8,128)(2,1)} async-done(((bf16[4,10,96,128]{3,2,1,0:T(8,128)(2,1)}), bf16[4,10,96,128]{3,2,1,0:T(8,128)(2,1)}, u32[]{:S(2)}, u32[]{:S(2)}) %all-to-all-start) | async-done | bytes 983072 | tf_op jit(solution)/shard_map/all_to_all | solution.py:252
  35.9 1.0 %copy-done.4 = bf16[4,32,1280]{2,1,0:T(8,128)(2,1)S(1)} copy-done((bf16[4,32,1280]{2,1,0:T(8,128)(2,1)S(1)}, bf16[4,32,1280]{2,1,0:T(8,128)(2,1)}, u32[]{:S(2)}) %copy-start.4) | copy-done | bytes 327704
  36.9 4.1 %forward.1 = (bf16[4,32,1280]{2,1,0:T(8,128)(2,1)S(1)}, bf16[4,32,1280]{2,1,0:T(8,128)(2,1)}, bf16[256,1280]{1,0:T(8,128)(2,1)S(1)}) custom-call(s32[10,3]{1,0:T(8,128)S(1)} %copy.8.tiles, s32[10]{0:T(128)S(1)} %dynamic_slice.7.counts, bf16[128,2560]{1,0:T(8,128)(2,1)S(1)} %constant_dynamic-update-slice_fusion.near, ...), custom_call_target="tpu_custom_call" | custom-call | tf_op jit(solution)/shard_map/forward/pallas_call | solution.py:137
  41.1 2.2 %backward.1 = (bf16[4,10,96,128]{3,2,1,0:T(8,128)(2,1)}, f32[10,96,128]{2,1,0:T(8,128)S(1)}) custom-call(s32[10,3]{1,0:T(8,128)S(1)} %copy.8.tiles, s32[10]{0:T(128)S(1)} %dynamic_slice.7.counts, s32[1]{0:T(128)} %bitcast.11.own, bf16[20,128,256]{2,1,0:T(8,128)(2,1)S(1)} %turn.1._.turned, bf16[256,1280]{1,0:T(8,128)(2,1)S(1)} %get-tuple-element.9.slopes), custom_call_target="tpu_custom_call" | custom-call | tf_op jit(solution)/shard_map/backward/pallas_call | solution.py:170
  43.3 3.7 %all-to-all-start.1 = ((bf16[4,10,96,128]{3,2,1,0:T(8,128)(2,1)}), bf16[4,10,96,128]{3,2,1,0:T(8,128)(2,1)S(1)}, u32[]{:S(2)}, u32[]{:S(2)}) async-start(bf16[4,10,96,128]{3,2,1,0:T(8,128)(2,1)} %get-tuple-element.10), calls=%async_computation.1 | async-start | bytes 1966080 | tf_op jit(solution)/shard_map/all_to_all | solution.py:280
  47.0 5.8 %collective-permute-done.6.rest_1_ = bf16[4,32,1280]{2,1,0:T(8,128)(2,1)S(1)} collective-permute-done((bf16[4,32,1280]{2,1,0:T(8,128)(2,1)}, bf16[4,32,1280]{2,1,0:T(8,128)(2,1)S(1)}, u32[]{:S(2)}, u32[]{:S(2)}) %collective-permute-start.6) | collective-permute-done | bytes 327712 | tf_op jit(solution)/shard_map/ppermute | solution.py:235
  53.0 1.6 %collective-permute-done.7.rest_2_ = bf16[4,32,1280]{2,1,0:T(8,128)(2,1)S(1)} collective-permute-done((bf16[4,32,1280]{2,1,0:T(8,128)(2,1)S(1)}, bf16[4,32,1280]{2,1,0:T(8,128)(2,1)S(1)}, u32[]{:S(2)}, u32[]{:S(2)}) %collective-permute-start.7) | collective-permute-done | bytes 327712 | tf_op jit(solution)/shard_map/ppermute | solution.py:235
  54.6 1.6 %collective-permute-start.8 = (bf16[4,32,1280]{2,1,0:T(8,128)(2,1)S(1)}, bf16[4,32,1280]{2,1,0:T(8,128)(2,1)S(1)}, u32[]{:S(2)}, u32[]{:S(2)}) collective-permute-start(bf16[4,32,1280]{2,1,0:T(8,128)(2,1)S(1)} %pad_maximum_fusion.4), channel_id=1, source_target_pairs={{0,2},{1,3},{2,0},{3,1},{4,6},{5,7},{6,4},{7,5},{8,10},{9,11},{10,... | collective-permute-start | bytes 983048 | tf_op jit(solution)/shard_map/ppermute | solution.py:235
  56.2 0.1 stack.49.starts
  56.3 8.2 %collective-permute-done.8.rest_3_ = bf16[4,32,1280]{2,1,0:T(8,128)(2,1)S(1)} collective-permute-done((bf16[4,32,1280]{2,1,0:T(8,128)(2,1)S(1)}, bf16[4,32,1280]{2,1,0:T(8,128)(2,1)S(1)}, u32[]{:S(2)}, u32[]{:S(2)}) %collective-permute-start.8) | collective-permute-done | bytes 327712 | tf_op jit(solution)/shard_map/ppermute | solution.py:235
  64.5 1.4 %join.1 = bf16[32,10240]{1,0:T(8,128)(2,1)} custom-call(s32[8]{0:T(128)S(1)} %stack.49.starts, bf16[4,32,1280]{2,1,0:T(8,128)(2,1)S(1)} %copy-done.2, bf16[4,32,1280]{2,1,0:T(8,128)(2,1)S(1)} %collective-permute-done.6.rest_1_, bf16[4,32,1280]{2,1,0:T(8,128)(2,1)S(1)} %collective-permute-done.7.rest_2_, bf16[4,32,1280]{2,1,0:T(8,128)(2,1)S(1)} %collective-permute-done.8.rest_3_), custom_call_target="tpu_custom_call" | custom-call | tf_op jit(solution)/shard_map/join/pallas_call | solution.py:70
  65.9 3.9 %all-to-all-done.1.grads = bf16[4,10,96,128]{3,2,1,0:T(8,128)(2,1)S(1)} async-done(((bf16[4,10,96,128]{3,2,1,0:T(8,128)(2,1)}), bf16[4,10,96,128]{3,2,1,0:T(8,128)(2,1)S(1)}, u32[]{:S(2)}, u32[]{:S(2)}) %all-to-all-start.1) | async-done | bytes 983072 | tf_op jit(solution)/shard_map/all_to_all | solution.py:280
  69.8 1.2 %sum.1 = f32[2,10,96,128]{3,2,1,0:T(8,128)} custom-call(s32[1]{0:T(128)} %bitcast.11.own, bf16[4,10,96,128]{3,2,1,0:T(8,128)(2,1)S(1)} %all-to-all-done.1.grads, f32[10,96,128]{2,1,0:T(8,128)S(1)} %get-tuple-element.11.mine), custom_call_target="tpu_custom_call" | custom-call | tf_op jit(solution)/shard_map/sum/pallas_call | solution.py:203
  (38 shorter events, 0.5 us)
Async XLA Ops:
  0.6 29.8 %copy-start = (s32[20,3]{0,1:T(4,128)S(1)}, s32[20,3]{0,1:T(4,128)}, u32[]{:S(2)}) copy-start(s32[20,3]{0,1:T(4,128)} %param.8) | copy-start | bytes 724
  0.6 4.9 %copy-start.6 = (bf16[96,20,128]{2,0,1:T(8,128)(2,1)S(1)}, bf16[96,20,128]{2,0,1:T(8,128)(2,1)}, u32[]{:S(2)}) copy-start(bf16[96,20,128]{2,0,1:T(8,128)(2,1)} %param.6) | copy-start | bytes 1474564
  0.7 13.1 %collective-permute-start = (bf16[32,2560]{1,0:T(8,128)(2,1)}, bf16[32,2560]{1,0:T(8,128)(2,1)S(1)}, u32[]{:S(2)}, u32[]{:S(2)}) collective-permute-start(bf16[32,2560]{1,0:T(8,128)(2,1)} %param.5), channel_id=1, source_target_pairs={{0,4},{1,5},{2,6},{3,7},{4,0},{5,1},{6,2},{7,3},{8,12},{9,13},{10,... | collective-permute-start | bytes 491528 | tf_op jit(solution)/shard_map/ppermute | solution.py:235
  5.4 10.7 %collective-permute-start.3 = (bf16[4,32,1280]{2,1,0:T(8,128)(2,1)S(1)}, bf16[4,32,1280]{2,1,0:T(8,128)(2,1)S(1)}, u32[]{:S(2)}, u32[]{:S(2)}) collective-permute-start(bf16[4,32,1280]{2,1,0:T(8,128)(2,1)S(1)} %cut.3), channel_id=1, source_target_pairs={{0,4},{1,5},{2,6},{3,7},{4,0},{5,1},{6,2},{7,3},{8,12},{9,13},{10,... | collective-permute-start | bytes 983048 | tf_op jit(solution)/shard_map/ppermute | solution.py:235
  6.6 5.4 %copy-start.5 = (bf16[32,2560]{1,0:T(8,128)(2,1)S(1)}, bf16[32,2560]{1,0:T(8,128)(2,1)}, u32[]{:S(2)}) copy-start(bf16[32,2560]{1,0:T(8,128)(2,1)} %param.5) | copy-start | bytes 491524
  6.6 29.3 %all-to-all-start = ((bf16[4,10,96,128]{3,2,1,0:T(8,128)(2,1)}), bf16[4,10,96,128]{3,2,1,0:T(8,128)(2,1)}, u32[]{:S(2)}, u32[]{:S(2)}) async-start(bf16[4,10,96,128]{3,2,1,0:T(8,128)(2,1)} %bitcast.10), calls=%async_computation | async-start | bytes 1966080 | tf_op jit(solution)/shard_map/all_to_all | solution.py:252
  13.8 10.7 %collective-permute-start.1 = (bf16[64,2560]{1,0:T(8,128)(2,1)S(1)}, bf16[64,2560]{1,0:T(8,128)(2,1)S(1)}, u32[]{:S(2)}, u32[]{:S(2)}) collective-permute-start(bf16[64,2560]{1,0:T(8,128)(2,1)S(1)} %pad_maximum_fusion), channel_id=1, source_target_pairs={{0,2},{1,3},{2,0},{3,1},{4,6},{5,7},{6,4},{7,5},{8,10},{9,11},{10,... | collective-permute-start | bytes 983048 | tf_op jit(solution)/shard_map/ppermute | solution.py:235
  16.1 14.2 %copy-start.7 = (s32[20]{0:T(128)S(1)}, s32[20]{0:T(128)}, u32[]{:S(2)}) copy-start(s32[20]{0:T(128)} %param.9) | copy-start | bytes 244
  16.2 13.3 %collective-permute-start.4 = (bf16[4,32,1280]{2,1,0:T(8,128)(2,1)S(1)}, bf16[4,32,1280]{2,1,0:T(8,128)(2,1)S(1)}, u32[]{:S(2)}, u32[]{:S(2)}) collective-permute-start(bf16[4,32,1280]{2,1,0:T(8,128)(2,1)S(1)} %pad_maximum_fusion.1), channel_id=1, source_target_pairs={{0,2},{1,3},{2,0},{3,1},{4,6},{5,7},{6,4},{7,5},{8,10},{9,11},{10,... | collective-permute-start | bytes 983048 | tf_op jit(solution)/shard_map/ppermute | solution.py:235
  24.6 6.0 %collective-permute-start.2 = (bf16[128,2560]{1,0:T(8,128)(2,1)S(1)}, bf16[128,2560]{1,0:T(8,128)(2,1)S(1)}, u32[]{:S(2)}, u32[]{:S(2)}) collective-permute-start(bf16[128,2560]{1,0:T(8,128)(2,1)S(1)} %constant_dynamic-update-slice_fusion.near), channel_id=1, source_target_pairs={{0,1},{1,0},{2,3},{3,2},{4,5},{5,4},{6,7},{7,6},{8,9},{9,8},{10,11... | collective-permute-start | bytes 1966088 | tf_op jit(solution)/shard_map/ppermute | solution.py:235
  29.5 1.1 %copy-start.3 = (bf16[4,32,1280]{2,1,0:T(8,128)(2,1)}, bf16[4,32,1280]{2,1,0:T(8,128)(2,1)S(1)}, u32[]{:S(2)}) copy-start(bf16[4,32,1280]{2,1,0:T(8,128)(2,1)S(1)} %collective-permute-done.4.rest_2_) | copy-start | bytes 983044
  30.4 2.0 %collective-permute-start.5 = (bf16[4,32,1280]{2,1,0:T(8,128)(2,1)}, bf16[4,32,1280]{2,1,0:T(8,128)(2,1)}, u32[]{:S(2)}, u32[]{:S(2)}) collective-permute-start(bf16[4,32,1280]{2,1,0:T(8,128)(2,1)} %pad_maximum_fusion.2), channel_id=1, source_target_pairs={{0,1},{1,0},{2,3},{3,2},{4,5},{5,4},{6,7},{7,6},{8,9},{9,8},{10,11... | collective-permute-start | bytes 983048 | tf_op jit(solution)/shard_map/ppermute | solution.py:235
  35.9 1.0 %copy-start.4 = (bf16[4,32,1280]{2,1,0:T(8,128)(2,1)S(1)}, bf16[4,32,1280]{2,1,0:T(8,128)(2,1)}, u32[]{:S(2)}) copy-start(bf16[4,32,1280]{2,1,0:T(8,128)(2,1)} %copy-done.3) | copy-start | bytes 983044
  41.0 2.3 %copy-start.1 = (bf16[4,32,1280]{2,1,0:T(8,128)(2,1)}, bf16[4,32,1280]{2,1,0:T(8,128)(2,1)S(1)}, u32[]{:S(2)}) copy-start(bf16[4,32,1280]{2,1,0:T(8,128)(2,1)S(1)} %get-tuple-element.7.rest_0_) | copy-start | bytes 983044
  41.0 11.8 %collective-permute-start.6 = (bf16[4,32,1280]{2,1,0:T(8,128)(2,1)}, bf16[4,32,1280]{2,1,0:T(8,128)(2,1)S(1)}, u32[]{:S(2)}, u32[]{:S(2)}) collective-permute-start(bf16[4,32,1280]{2,1,0:T(8,128)(2,1)} %get-tuple-element.8), channel_id=1, source_target_pairs={{0,4},{1,5},{2,6},{3,7},{4,0},{5,1},{6,2},{7,3},{8,12},{9,13},{10,... | collective-permute-start | bytes 983048 | tf_op jit(solution)/shard_map/ppermute | solution.py:235
  43.3 3.7 %copy-start.2 = (bf16[4,32,1280]{2,1,0:T(8,128)(2,1)S(1)}, bf16[4,32,1280]{2,1,0:T(8,128)(2,1)}, u32[]{:S(2)}) copy-start(bf16[4,32,1280]{2,1,0:T(8,128)(2,1)} %copy-done.1) | copy-start | bytes 983044
  43.3 26.5 %all-to-all-start.1 = ((bf16[4,10,96,128]{3,2,1,0:T(8,128)(2,1)}), bf16[4,10,96,128]{3,2,1,0:T(8,128)(2,1)S(1)}, u32[]{:S(2)}, u32[]{:S(2)}) async-start(bf16[4,10,96,128]{3,2,1,0:T(8,128)(2,1)} %get-tuple-element.10), calls=%async_computation.1 | async-start | bytes 1966080 | tf_op jit(solution)/shard_map/all_to_all | solution.py:280
  52.9 1.7 %collective-permute-start.7 = (bf16[4,32,1280]{2,1,0:T(8,128)(2,1)S(1)}, bf16[4,32,1280]{2,1,0:T(8,128)(2,1)S(1)}, u32[]{:S(2)}, u32[]{:S(2)}) collective-permute-start(bf16[4,32,1280]{2,1,0:T(8,128)(2,1)S(1)} %pad_maximum_fusion.3), channel_id=1, source_target_pairs={{0,1},{1,0},{2,3},{3,2},{4,5},{5,4},{6,7},{7,6},{8,9},{9,8},{10,11... | collective-permute-start | bytes 983048 | tf_op jit(solution)/shard_map/ppermute | solution.py:235
  54.6 9.8 %collective-permute-start.8 = (bf16[4,32,1280]{2,1,0:T(8,128)(2,1)S(1)}, bf16[4,32,1280]{2,1,0:T(8,128)(2,1)S(1)}, u32[]{:S(2)}, u32[]{:S(2)}) collective-permute-start(bf16[4,32,1280]{2,1,0:T(8,128)(2,1)S(1)} %pad_maximum_fusion.4), channel_id=1, source_target_pairs={{0,2},{1,3},{2,0},{3,1},{4,6},{5,7},{6,4},{7,5},{8,10},{9,11},{10,... | collective-permute-start | bytes 983048 | tf_op jit(solution)/shard_map/ppermute | solution.py:235

commit v11 on v9

--- a/solution.py
+++ b/solution.py
@@ -43,8 +43,7 @@
     copy_all([(whole.at[:, pl.ds(pl.multiple_of(starts[b] * TILE, TILE), width)], out.at[b]) for b in range(count)], sems)
 
 
-def cut_call(starts, whole):
-    count = starts.shape[0]
+def cut_call(starts, whole, count):
     rows, width = whole.shape[0], whole.shape[1] // (PAIR * count)
     return pl.pallas_call(
         cut_kernel,
@@ -57,6 +56,23 @@
     )(starts, pltpu.with_memory_space_constraint(whole, pltpu.HBM))
 
 
+def collect_kernel(refs, *rest):
+    arrays, out = rest[:-1], rest[-1]
+    for i, (a, b) in enumerate(refs):
+        out[i] = arrays[a][b]
+
+
+def collect_call(arrays, refs):
+    return pl.pallas_call(
+        functools.partial(collect_kernel, refs),
+        out_shape=jax.ShapeDtypeStruct((len(refs),) + arrays[0].shape[1:], arrays[0].dtype),
+        in_specs=[RESIDENT] * len(arrays),
+        out_specs=RESIDENT,
+        compiler_params=room(6),
+        name="collect",
+    )(*arrays)
+
+
 def join_kernel(refs, starts, *rest):
     arrays, whole, sems = rest[:-2], rest[-2], rest[-1]
     width = whole.shape[1] // len(refs)
@@ -77,89 +93,88 @@
     )(starts, *arrays)
 
 
-def pick(tiles, counts, tokens, s):
+class Table:
+    def __init__(self, ref, blocks, stripes):
+        self.ref, self.lists, self.counts = ref, blocks, blocks + SLOTS * stripes
+        self.first, self.own = ref[self.counts + stripes], ref[self.counts + stripes + 1]
+
+    def tile(self, s, k):
+        return self.ref[self.lists + (self.first + s) * SLOTS + k]
+
+    def count(self, s):
+        return self.ref[self.counts + self.first + s]
+
+
+def pick(table, near, far, s):
     picked = []
     for k in range(SLOTS):
-        column = pl.multiple_of(tiles[s, k] * TILE, TILE)
-        block = jnp.concatenate([piece[:, pl.ds(column, TILE)] for piece in tokens], axis=0)
-        picked.append(jnp.where(k < counts[s], block, jnp.zeros_like(block)))
+        cols = pl.ds(pl.multiple_of(table.tile(s, k) * TILE, TILE), TILE)
+        block = jnp.concatenate([near[:, cols], far[:, cols]], axis=0)
+        picked.append(jnp.where(k < table.count(s), block, jnp.zeros_like(block)))
     return jnp.concatenate(picked, axis=1)
 
 
-def forward_kernel(pieces, refs, tiles, counts, *rest):
-    tokens, weights, arrays = rest[:pieces], rest[pieces], rest[pieces + 1:-5]
-    outs, slopes, held, sems = rest[-5:-3], rest[-3], rest[-2], rest[-1]
-    shards, stripes, size, _ = weights.shape
-    rows = arrays[0].shape[1]
-    copies = [
-        pltpu.make_async_copy(weights.at[f, s], held.at[s, pl.ds(f * size, size)], sems.at[s, f])
-        for s in range(stripes) for f in range(shards)
-    ]
-    for copy in copies:
-        copy.start()
+def forward_kernel(sizes, scalars, near, far, weights, backs, home, away, slopes):
+    table = Table(scalars, *sizes)
+    shards, stripes = weights.shape[0], weights.shape[1]
+    blocks, rows, _ = backs.shape
     for s in range(stripes):
         cols = slice(s * TILE, (s + 1) * TILE)
-        picked = pick(tiles, counts, tokens, s)
-        for copy in copies[s * shards:(s + 1) * shards]:
-            copy.wait()
-        pre = jnp.dot(picked, held[s], preferred_element_type=jnp.float32)
+        stack = jnp.concatenate([weights[f, s] for f in range(shards)], axis=0)
+        pre = jnp.dot(pick(table, near, far, s), stack, preferred_element_type=jnp.float32)
         act, slope = gelu_and_derivative(pre)
         act = act.astype(jnp.bfloat16)
-        for i in range(len(refs)):
-            outs[i % PAIR][i // PAIR, :, cols] = act[i * rows:(i + 1) * rows]
-        back = jnp.concatenate([arrays[a][b, :, cols] for a, b in refs], axis=0)
+        for i in range(blocks):
+            (home, away)[i % PAIR][i // PAIR, :, cols] = act[i * rows:(i + 1) * rows]
+        back = backs[:, :, cols].reshape(blocks * rows, TILE)
         slopes[:, cols] = (back.astype(jnp.float32) * slope).astype(jnp.bfloat16)
 
 
-def forward_call(tiles, counts, tokens, weights, arrays, refs):
-    _, rows, width = arrays[0].shape
-    shards, stripes, size, _ = weights.shape
-    blocks = len(refs)
-    return pl.pallas_call(
-        functools.partial(forward_kernel, len(tokens), refs),
+def forward_call(sizes, scalars, near, far, weights, backs):
+    blocks, rows, width = backs.shape
+    return pl.pallas_call(
+        functools.partial(forward_kernel, sizes),
         out_shape=[jax.ShapeDtypeStruct((blocks // PAIR, rows, width), jnp.bfloat16)] * PAIR
         + [jax.ShapeDtypeStruct((blocks * rows, width), jnp.bfloat16)],
-        in_specs=[SCALAR] * 2 + [RESIDENT] * len(tokens) + [pl.BlockSpec(memory_space=pltpu.HBM)] + [RESIDENT] * len(arrays),
+        in_specs=[SCALAR] + [RESIDENT] * 4,
         out_specs=[RESIDENT] * 3,
-        scratch_shapes=[pltpu.VMEM((stripes, shards * size, TILE), jnp.bfloat16), pltpu.SemaphoreType.DMA((stripes, shards))],
-        compiler_params=room(12),
+        compiler_params=room(10),
         name="forward",
-    )(tiles, counts, *tokens, pltpu.with_memory_space_constraint(weights, pltpu.HBM), *arrays)
-
-
-def backward_kernel(pieces, tiles, counts, own, *rest):
-    tokens, slopes, grads, mine, term, sent, sems = rest[:pieces], *rest[pieces:]
+    )(scalars, near, far, weights, backs)
+
+
+def backward_kernel(sizes, scalars, near, far, slopes, grads, mine, sent, sems):
+    table = Table(scalars, *sizes)
     shards, stripes, size, _ = grads.shape
-    span = pl.ds(pl.multiple_of(own[0] * size, size), size)
     copies = []
     for s in range(stripes):
-        picked = pick(tiles, counts, tokens, s)
+        picked = pick(table, near, far, s)
         slope = slopes[:, s * TILE:(s + 1) * TILE]
-        term[s] = lax.dot_general(picked, slope, (((0,), (0,)), ((), ())), preferred_element_type=jnp.float32)
+        term = lax.dot_general(picked, slope, (((0,), (0,)), ((), ())), preferred_element_type=jnp.float32)
+        pieces = [term[f * size:(f + 1) * size] for f in range(shards)]
         for f in range(shards):
-            sent[s, f] = term[s, f * size:(f + 1) * size].astype(sent.dtype)
+            sent[s, f] = pieces[f].astype(sent.dtype)
         copies.append(pltpu.make_async_copy(sent.at[s], grads.at[:, s], sems.at[s]))
         copies[-1].start()
-        mine[s] = term[s, span]
+        chosen = pieces[0]
+        for f in range(1, shards):
+            chosen = jnp.where(table.own == f, pieces[f], chosen)
+        mine[s] = chosen
     for copy in copies:
         copy.wait()
 
 
-def backward_call(tiles, counts, own, tokens, slopes, shards):
+def backward_call(sizes, scalars, near, far, slopes, shards):
     stripes, size = slopes.shape[1] // TILE, SLOTS * TILE // shards
     return pl.pallas_call(
-        functools.partial(backward_kernel, len(tokens)),
+        functools.partial(backward_kernel, sizes),
         out_shape=[pltpu.HBM((shards, stripes, size, TILE), jnp.bfloat16), jax.ShapeDtypeStruct((stripes, size, TILE), jnp.float32)],
-        in_specs=[SCALAR] * 3 + [RESIDENT] * (len(tokens) + 1),
+        in_specs=[SCALAR] + [RESIDENT] * 3,
         out_specs=[pl.BlockSpec(memory_space=pltpu.HBM), RESIDENT],
-        scratch_shapes=[
-            pltpu.VMEM((stripes, SLOTS * TILE, TILE), jnp.float32),
-            pltpu.VMEM((stripes, shards, size, TILE), jnp.bfloat16),
-            pltpu.SemaphoreType.DMA((stripes,)),
-        ],
-        compiler_params=room(12),
+        scratch_shapes=[pltpu.VMEM((stripes, shards, size, TILE), jnp.bfloat16), pltpu.SemaphoreType.DMA((stripes,))],
+        compiler_params=room(10),
         name="backward",
-    )(tiles, counts, own, *tokens, slopes)
+    )(scalars, near, far, slopes)
 
 
 def sum_kernel(own, grads, mine, total, held, sems):
@@ -234,26 +249,25 @@
     if not whole_tiles:
         weights = weights.transpose(1, 0, 2, 3).reshape(1, share, fsdp * size, TILE)
 
-    leave = cut_call(first_tiles([(1, b) for b in range(tensor)]), cotangent)
-    stay = cut_call(first_tiles([(0, b) for b in range(tensor)]), cotangent)
+    leave = cut_call(first_tiles([(1, b) for b in range(tensor)]), cotangent, tensor)
+    sizes = (tensor, stripes)
+    ends = jnp.stack([half * share, z]).astype(jnp.int32)
+    scalars = jnp.concatenate([first_tiles([(0, b) for b in range(tensor)]), tile_list.reshape(-1), tile_counts, ends])
+    stay = cut_call(scalars, cotangent, tensor)
     near = jnp.concatenate([tokens, swap(tokens, 1, 0)], axis=0)
     for bit in bits:
         far = swap(near, 0, bit)
         if bit > 1:
             near = jnp.concatenate([near, far], axis=0)
     arrays, refs, _ = exchange([stay, swap(leave, 1, 0)], bits)
-
-    tiles = lax.dynamic_slice_in_dim(tile_list, half * share, share, 0)
-    counts = lax.dynamic_slice_in_dim(tile_counts, half * share, share, 0)
-    home, away, slopes = forward_call(tiles, counts, [near, far], weights, arrays, refs)
+    backs = collect_call(arrays, refs)
+    home, away, slopes = forward_call(sizes, scalars, near, far, weights, backs)
 
     arrays, refs, origins = exchange([home, swap(away, 1, 0)], list(reversed(bits)))
     activations = join_call(first_tiles(origins), arrays, refs)
 
-    if whole_tiles:
-        grads, mine = backward_call(tiles, counts, own, [near, far], slopes, fsdp)
-    else:
-        grads, mine = backward_call(tiles, counts, own * 0, [near, far], slopes, 1)
+    grads, mine = backward_call(sizes, scalars, near, far, slopes, fsdp if whole_tiles else 1)
+    if not whole_tiles:
         grads = grads.reshape(share, fsdp, size, TILE).transpose(1, 0, 2, 3)
         mine = lax.dynamic_index_in_dim(mine.reshape(share, fsdp, size, TILE), z, 1, keepdims=False)
     total = sum_call(own, lax.all_to_all(grads, "fsdp", split_axis=0, concat_axis=0, tiled=True), mine)

time: 70.9 us -> 70.4 us (level)
  Pallas kernels: 12.7 us -> 10.4 us
  local copies, waits for them, and re-layouts: 4.47 us -> 5.95 us
    all_to_all x1, waiting for transfers between devices: 4.23 us -> 9.44 us  [body(): lax.all_to_all(grads, 'fsdp', split_axis=0, concat_axis=0, tiled=True)]
    ppermute x9, waiting for transfers between devices: 27.7 us -> 24.7 us  [swap(): return lax.ppermute(value, ('fsdp', 'tensor'), pairs)]
    pallas_call x2 -> x3, Pallas kernels: 6.93 us -> 4.65 us  [the longest x1 2.56 us: forward_call(): pl.pallas_call(functools.partial(forward_kernel, sizes), out_shape=[jax.S...]
    all_to_all x1, waiting for transfers between devices: 3.89 us -> 2.19 us  [body(): lax.all_to_all(outgoing, 'fsdp', split_axis=0, concat_axis=0, tiled=True)]
    unnamed x23 -> x27, local copies, waits for them, and re-layouts: 2.14 us -> 3.54 us
where the time goes in v11:
time: 70.4 us; the launch traced here: 70 us
  waiting for transfers between devices  36.4 us (52%)
  starting transfers between devices  16.1 us (23%)
  Pallas kernels  10.4 us (15%)
  local copies, waits for them, and re-layouts  5.95 us (8%)
  between operations  0.95 us (1%)
    ppermute x9, waiting for transfers between devices, swap(): return lax.ppermute(value, ('fsdp', 'tensor'), pairs)  24.7 us
    all_to_all x1, waiting for transfers between devices, body(): lax.all_to_all(grads, 'fsdp', split_axis=0, concat_axis=0, tiled=True)  9.44 us
    ppermute x9, starting transfers between devices, swap(): return lax.ppermute(value, ('fsdp', 'tensor'), pairs)  7.14 us
    all_to_all x1, starting transfers between devices, body(): lax.all_to_all(outgoing, 'fsdp', split_axis=0, concat_axis=0, tiled=True)  5.41 us
    unnamed x27, local copies, waits for them, and re-layouts  3.54 us
    all_to_all x1, starting transfers between devices, body(): lax.all_to_all(grads, 'fsdp', split_axis=0, concat_axis=0, tiled=True)  3.51 us
    pallas_call x2, Pallas kernels, cut_call(): pl.pallas_call(cut_kernel, out_shape=jax.ShapeDtypeStruct((count, rows, w...  3.18 us
    pallas_call x1, Pallas kernels, forward_call(): pl.pallas_call(functools.partial(forward_kernel, sizes), out_shape=[jax.S...  2.56 us
  transfers between devices with their start and end apart: 11, of which 8 were waited for; matrix products, arithmetic and copies ran while one was open for 3% of the time, Pallas kernels for 10%

profile of v11, /device:TPU:0, one launch (start us, length us, event | category | flops | bytes accessed | tf_op | source)
XLA Modules:
  0.0 70.0 jit_solution(16209725144732426465)
XLA Ops:
  0.6 3.1 %collective-permute-start = (bf16[32,2560]{1,0:T(8,128)(2,1)}, bf16[32,2560]{1,0:T(8,128)(2,1)S(1)}, u32[]{:S(2)}, u32[]{:S(2)}) collective-permute-start(bf16[32,2560]{1,0:T(8,128)(2,1)} %param.5), channel_id=1, source_target_pairs={{0,4},{1,5},{2,6},{3,7},{4,0},{5,1},{6,2},{7,3},{8,12},{9,13},{10,... | collective-permute-start | bytes 491528 | tf_op jit(solution)/shard_map/ppermute | solution.py:230
  3.7 0.1 pad_add_fusion.starts
  3.8 1.6 %cut.3 = bf16[4,32,1280]{2,1,0:T(8,128)(2,1)S(1)} custom-call(s32[4]{0:T(128)S(1)} %pad_add_fusion.starts, bf16[32,10240]{1,0:T(8,128)(2,1)} %whole.3), custom_call_target="tpu_custom_call" | custom-call | tf_op jit(solution)/shard_map/cut/pallas_call | solution.py:48
  5.4 0.1 collective-permute-start.3
  5.5 1.1 %tile.11 = bf16[2,2,10,96,128]{4,3,2,1,0:T(8,128)(2,1)} broadcast(bf16[2,10,96,128]{3,2,1,0:T(8,128)(2,1)S(1)} %bitcast.18), dimensions={1,2,3,4} | broadcast | bytes 1474560 | tf_op jit(solution)/shard_map/tile | solution.py:246
  6.6 5.4 %all-to-all-start = ((bf16[4,10,96,128]{3,2,1,0:T(8,128)(2,1)}), bf16[4,10,96,128]{3,2,1,0:T(8,128)(2,1)S(1)}, u32[]{:S(2)}, u32[]{:S(2)}) async-start(bf16[4,10,96,128]{3,2,1,0:T(8,128)(2,1)} %bitcast.12), calls=%async_computation | async-start | bytes 1966080 | tf_op jit(solution)/shard_map/all_to_all | solution.py:247
  12.1 0.7 copy-done.10
  12.7 0.1 copy.8
  12.8 0.1 reshape.15
  12.9 0.6 copy-done.11
  13.7 1.6 %cut.2.rest_0_ = bf16[4,32,1280]{2,1,0:T(8,128)(2,1)S(1)} custom-call(s32[86]{0:T(128)S(1)} %concatenate.22.starts.scalars, bf16[32,10240]{1,0:T(8,128)(2,1)} %whole.3), custom_call_target="tpu_custom_call" | custom-call | tf_op jit(solution)/shard_map/cut/pallas_call | solution.py:48
  15.3 0.7 %copy-done = bf16[4,32,1280]{2,1,0:T(8,128)(2,1)} copy-done((bf16[4,32,1280]{2,1,0:T(8,128)(2,1)}, bf16[4,32,1280]{2,1,0:T(8,128)(2,1)S(1)}, u32[]{:S(2)}) %copy-start) | copy-done | bytes 327704
  16.0 1.6 %collective-permute-start.1 = (bf16[64,2560]{1,0:T(8,128)(2,1)S(1)}, bf16[64,2560]{1,0:T(8,128)(2,1)S(1)}, u32[]{:S(2)}, u32[]{:S(2)}) collective-permute-start(bf16[64,2560]{1,0:T(8,128)(2,1)S(1)} %pad_maximum_fusion), channel_id=1, source_target_pairs={{0,2},{1,3},{2,0},{3,1},{4,6},{5,7},{6,4},{7,5},{8,10},{9,11},{10,... | collective-permute-start | bytes 983048 | tf_op jit(solution)/shard_map/ppermute | solution.py:230
  17.7 1.0 %slice-done.1 = bf16[2,32,1280]{2,1,0:T(8,128)(2,1)S(1)} async-done(((bf16[4,32,1280]{2,1,0:T(8,128)(2,1)}), bf16[2,32,1280]{2,1,0:T(8,128)(2,1)S(1)}, s32[]{:S(2)}) %slice-start.1) | async-done | bytes 163864 | tf_op jit(solution)/shard_map/slice | solution.py:216
  18.7 0.6 collective-permute-start.4
  19.2 7.5 %collective-permute-done.1 = bf16[64,2560]{1,0:T(8,128)(2,1)S(1)} collective-permute-done((bf16[64,2560]{1,0:T(8,128)(2,1)S(1)}, bf16[64,2560]{1,0:T(8,128)(2,1)S(1)}, u32[]{:S(2)}, u32[]{:S(2)}) %collective-permute-start.1) | collective-permute-done | bytes 327712 | tf_op jit(solution)/shard_map/ppermute | solution.py:230
  26.9 4.9 %collective-permute-done.4.rest_2_ = bf16[4,32,1280]{2,1,0:T(8,128)(2,1)S(1)} collective-permute-done((bf16[4,32,1280]{2,1,0:T(8,128)(2,1)S(1)}, bf16[4,32,1280]{2,1,0:T(8,128)(2,1)S(1)}, u32[]{:S(2)}, u32[]{:S(2)}) %collective-permute-start.4) | collective-permute-done | bytes 327712 | tf_op jit(solution)/shard_map/ppermute | solution.py:230
  31.9 1.6 %collective-permute-done.5.rest_3_ = bf16[4,32,1280]{2,1,0:T(8,128)(2,1)S(1)} collective-permute-done((bf16[4,32,1280]{2,1,0:T(8,128)(2,1)S(1)}, bf16[4,32,1280]{2,1,0:T(8,128)(2,1)S(1)}, u32[]{:S(2)}, u32[]{:S(2)}) %collective-permute-start.5) | collective-permute-done | bytes 327712 | tf_op jit(solution)/shard_map/ppermute | solution.py:230
  33.6 2.2 %all-to-all-done.weights = bf16[4,10,96,128]{3,2,1,0:T(8,128)(2,1)S(1)} async-done(((bf16[4,10,96,128]{3,2,1,0:T(8,128)(2,1)}), bf16[4,10,96,128]{3,2,1,0:T(8,128)(2,1)S(1)}, u32[]{:S(2)}, u32[]{:S(2)}) %all-to-all-start) | async-done | bytes 983072 | tf_op jit(solution)/shard_map/all_to_all | solution.py:247
  35.8 2.6 %forward.1 = (bf16[4,32,1280]{2,1,0:T(8,128)(2,1)S(1)}, bf16[4,32,1280]{2,1,0:T(8,128)(2,1)}, bf16[256,1280]{1,0:T(8,128)(2,1)S(1)}) custom-call(s32[86]{0:T(128)S(1)} %concatenate.22.starts.scalars, bf16[128,2560]{1,0:T(8,128)(2,1)S(1)} %constant_dynamic-update-slice_fusion.near, bf16[128,2560]{1,0:T(8,128)(2,1)S(1)} %collective-permute-done.2.far, ...), custom_call_target="tpu_custom_call" | custom-call | tf_op jit(solution)/shard_map/forward/pallas_call | solution.py:135
  38.3 2.0 %backward.1 = (bf16[4,10,96,128]{3,2,1,0:T(8,128)(2,1)}, f32[10,96,128]{2,1,0:T(8,128)S(1)}) custom-call(s32[86]{0:T(128)S(1)} %concatenate.22.starts.scalars, bf16[128,2560]{1,0:T(8,128)(2,1)S(1)} %constant_dynamic-update-slice_fusion.near, bf16[128,2560]{1,0:T(8,128)(2,1)S(1)} %collective-permute-done.2.far, bf16[256,1280]{1,0:T(8,128)(2,1)S(1)} %get-tuple-element.9.slopes), custom_call_target="tpu_custom_call" | custom-call | tf_op jit(solution)/shard_map/backward/pallas_call | solution.py:169
  40.4 0.8 %copy-done.6 = f32[10,96,128]{2,1,0:T(8,128)} copy-done((f32[10,96,128]{2,1,0:T(8,128)}, f32[10,96,128]{2,1,0:T(8,128)S(1)}, u32[]{:S(2)}) %copy-start.6) | copy-done | bytes 491544
  41.2 3.5 %all-to-all-start.1 = ((bf16[4,10,96,128]{3,2,1,0:T(8,128)(2,1)}), bf16[4,10,96,128]{3,2,1,0:T(8,128)(2,1)S(1)}, u32[]{:S(2)}, u32[]{:S(2)}) async-start(bf16[4,10,96,128]{3,2,1,0:T(8,128)(2,1)} %get-tuple-element.10), calls=%async_computation.1 | async-start | bytes 1966080 | tf_op jit(solution)/shard_map/all_to_all | solution.py:273
  44.7 1.6 %collective-permute-done.6.rest_1_ = bf16[4,32,1280]{2,1,0:T(8,128)(2,1)S(1)} collective-permute-done((bf16[4,32,1280]{2,1,0:T(8,128)(2,1)}, bf16[4,32,1280]{2,1,0:T(8,128)(2,1)S(1)}, u32[]{:S(2)}, u32[]{:S(2)}) %collective-permute-start.6) | collective-permute-done | bytes 327712 | tf_op jit(solution)/shard_map/ppermute | solution.py:230
  46.4 0.6 copy-done.2
  47.0 1.0 %collective-permute-done.7.rest_2_ = bf16[4,32,1280]{2,1,0:T(8,128)(2,1)S(1)} collective-permute-done((bf16[4,32,1280]{2,1,0:T(8,128)(2,1)S(1)}, bf16[4,32,1280]{2,1,0:T(8,128)(2,1)S(1)}, u32[]{:S(2)}, u32[]{:S(2)}) %collective-permute-start.7) | collective-permute-done | bytes 327712 | tf_op jit(solution)/shard_map/ppermute | solution.py:230
  48.1 1.6 %collective-permute-start.8 = (bf16[4,32,1280]{2,1,0:T(8,128)(2,1)S(1)}, bf16[4,32,1280]{2,1,0:T(8,128)(2,1)S(1)}, u32[]{:S(2)}, u32[]{:S(2)}) collective-permute-start(bf16[4,32,1280]{2,1,0:T(8,128)(2,1)S(1)} %pad_maximum_fusion.4), channel_id=1, source_target_pairs={{0,2},{1,3},{2,0},{3,1},{4,6},{5,7},{6,4},{7,5},{8,10},{9,11},{10,... | collective-permute-start | bytes 983048 | tf_op jit(solution)/shard_map/ppermute | solution.py:230
  49.7 0.1 stack.52.starts
  49.8 8.2 %collective-permute-done.8.rest_3_ = bf16[4,32,1280]{2,1,0:T(8,128)(2,1)S(1)} collective-permute-done((bf16[4,32,1280]{2,1,0:T(8,128)(2,1)S(1)}, bf16[4,32,1280]{2,1,0:T(8,128)(2,1)S(1)}, u32[]{:S(2)}, u32[]{:S(2)}) %collective-permute-start.8) | collective-permute-done | bytes 327712 | tf_op jit(solution)/shard_map/ppermute | solution.py:230
  58.0 1.4 %join.1 = bf16[32,10240]{1,0:T(8,128)(2,1)} custom-call(s32[8]{0:T(128)S(1)} %stack.52.starts, bf16[4,32,1280]{2,1,0:T(8,128)(2,1)S(1)} %get-tuple-element.7.rest_0_, bf16[4,32,1280]{2,1,0:T(8,128)(2,1)S(1)} %copy-done.3, bf16[4,32,1280]{2,1,0:T(8,128)(2,1)S(1)} %collective-permute-done.7.rest_2_, bf16[4,32,1280]{2,1,0:T(8,128)(2,1)S(1)} %collective-permute-done.8.rest_3_), custom_call_target="tpu_custom_call" | custom-call | tf_op jit(solution)/shard_map/join/pallas_call | solution.py:85
  59.4 9.4 %all-to-all-done.1.grads = bf16[4,10,96,128]{3,2,1,0:T(8,128)(2,1)S(1)} async-done(((bf16[4,10,96,128]{3,2,1,0:T(8,128)(2,1)}), bf16[4,10,96,128]{3,2,1,0:T(8,128)(2,1)S(1)}, u32[]{:S(2)}, u32[]{:S(2)}) %all-to-all-start.1) | async-done | bytes 983072 | tf_op jit(solution)/shard_map/all_to_all | solution.py:273
  68.8 1.2 %sum.1 = f32[2,10,96,128]{3,2,1,0:T(8,128)} custom-call(s32[1]{0:T(128)} %bitcast.9.own, bf16[4,10,96,128]{3,2,1,0:T(8,128)(2,1)S(1)} %all-to-all-done.1.grads, f32[10,96,128]{2,1,0:T(8,128)S(1)} %copy-done.7), custom_call_target="tpu_custom_call" | custom-call | tf_op jit(solution)/shard_map/sum/pallas_call | solution.py:198
  (49 shorter events, 0.7 us)
Async XLA Ops:
  0.6 15.4 %collective-permute-start = (bf16[32,2560]{1,0:T(8,128)(2,1)}, bf16[32,2560]{1,0:T(8,128)(2,1)S(1)}, u32[]{:S(2)}, u32[]{:S(2)}) collective-permute-start(bf16[32,2560]{1,0:T(8,128)(2,1)} %param.5), channel_id=1, source_target_pairs={{0,4},{1,5},{2,6},{3,7},{4,0},{5,1},{6,2},{7,3},{8,12},{9,13},{10,... | collective-permute-start | bytes 491528 | tf_op jit(solution)/shard_map/ppermute | solution.py:230
  3.8 1.7 %copy-start.9 = (bf16[96,20,128]{2,0,1:T(8,128)(2,1)S(1)}, bf16[96,20,128]{2,0,1:T(8,128)(2,1)}, u32[]{:S(2)}) copy-start(bf16[96,20,128]{2,0,1:T(8,128)(2,1)} %param.6) | copy-start | bytes 1474564
  5.4 12.2 %collective-permute-start.3 = (bf16[4,32,1280]{2,1,0:T(8,128)(2,1)S(1)}, bf16[4,32,1280]{2,1,0:T(8,128)(2,1)S(1)}, u32[]{:S(2)}, u32[]{:S(2)}) collective-permute-start(bf16[4,32,1280]{2,1,0:T(8,128)(2,1)S(1)} %cut.3), channel_id=1, source_target_pairs={{0,4},{1,5},{2,6},{3,7},{4,0},{5,1},{6,2},{7,3},{8,12},{9,13},{10,... | collective-permute-start | bytes 983048 | tf_op jit(solution)/shard_map/ppermute | solution.py:230
  6.6 5.4 %copy-start.8 = (bf16[32,2560]{1,0:T(8,128)(2,1)S(1)}, bf16[32,2560]{1,0:T(8,128)(2,1)}, u32[]{:S(2)}) copy-start(bf16[32,2560]{1,0:T(8,128)(2,1)} %param.5) | copy-start | bytes 491524
  6.6 29.2 %all-to-all-start = ((bf16[4,10,96,128]{3,2,1,0:T(8,128)(2,1)}), bf16[4,10,96,128]{3,2,1,0:T(8,128)(2,1)S(1)}, u32[]{:S(2)}, u32[]{:S(2)}) async-start(bf16[4,10,96,128]{3,2,1,0:T(8,128)(2,1)} %bitcast.12), calls=%async_computation | async-start | bytes 1966080 | tf_op jit(solution)/shard_map/all_to_all | solution.py:247
  12.0 0.7 copy-start.10
  12.9 0.7 copy-start.11
  15.3 0.7 %copy-start = (bf16[4,32,1280]{2,1,0:T(8,128)(2,1)}, bf16[4,32,1280]{2,1,0:T(8,128)(2,1)S(1)}, u32[]{:S(2)}) copy-start(bf16[4,32,1280]{2,1,0:T(8,128)(2,1)S(1)} %cut.2.rest_0_) | copy-start | bytes 983044
  16.0 10.7 %collective-permute-start.1 = (bf16[64,2560]{1,0:T(8,128)(2,1)S(1)}, bf16[64,2560]{1,0:T(8,128)(2,1)S(1)}, u32[]{:S(2)}, u32[]{:S(2)}) collective-permute-start(bf16[64,2560]{1,0:T(8,128)(2,1)S(1)} %pad_maximum_fusion), channel_id=1, source_target_pairs={{0,2},{1,3},{2,0},{3,1},{4,6},{5,7},{6,4},{7,5},{8,10},{9,11},{10,... | collective-permute-start | bytes 983048 | tf_op jit(solution)/shard_map/ppermute | solution.py:230
  17.6 1.0 %slice-start.1 = ((bf16[4,32,1280]{2,1,0:T(8,128)(2,1)}), bf16[2,32,1280]{2,1,0:T(8,128)(2,1)S(1)}, s32[]{:S(2)}) async-start(bf16[4,32,1280]{2,1,0:T(8,128)(2,1)} %copy-done), calls=%async_computation.3 | async-start | bytes 327680 | tf_op jit(solution)/shard_map/slice | solution.py:216
  17.6 1.6 %copy-start.4 = (bf16[4,32,1280]{2,1,0:T(8,128)(2,1)}, bf16[4,32,1280]{2,1,0:T(8,128)(2,1)S(1)}, u32[]{:S(2)}) copy-start(bf16[4,32,1280]{2,1,0:T(8,128)(2,1)S(1)} %collective-permute-done.3.rest_1_) | copy-start | bytes 983044
  18.7 13.1 %collective-permute-start.4 = (bf16[4,32,1280]{2,1,0:T(8,128)(2,1)S(1)}, bf16[4,32,1280]{2,1,0:T(8,128)(2,1)S(1)}, u32[]{:S(2)}, u32[]{:S(2)}) collective-permute-start(bf16[4,32,1280]{2,1,0:T(8,128)(2,1)S(1)} %pad_maximum_fusion.1), channel_id=1, source_target_pairs={{0,2},{1,3},{2,0},{3,1},{4,6},{5,7},{6,4},{7,5},{8,10},{9,11},{10,... | collective-permute-start | bytes 983048 | tf_op jit(solution)/shard_map/ppermute | solution.py:230
  26.8 5.0 %slice-start = ((bf16[4,32,1280]{2,1,0:T(8,128)(2,1)}), bf16[1,32,1280]{2,1,0:T(8,128)(2,1)S(1)}, s32[]{:S(2)}) async-start(bf16[4,32,1280]{2,1,0:T(8,128)(2,1)} %copy-done), calls=%async_computation.2 | async-start | bytes 163840 | tf_op jit(solution)/shard_map/slice | solution.py:216
  26.8 5.0 %slice-start.3 = ((bf16[4,32,1280]{2,1,0:T(8,128)(2,1)}), bf16[1,32,1280]{2,1,0:T(8,128)(2,1)S(1)}, s32[]{:S(2)}) async-start(bf16[4,32,1280]{2,1,0:T(8,128)(2,1)} %copy-done.4), calls=%async_computation.5 | async-start | bytes 163840 | tf_op jit(solution)/shard_map/slice | solution.py:216
  26.8 6.8 %collective-permute-start.2 = (bf16[128,2560]{1,0:T(8,128)(2,1)S(1)}, bf16[128,2560]{1,0:T(8,128)(2,1)S(1)}, u32[]{:S(2)}, u32[]{:S(2)}) collective-permute-start(bf16[128,2560]{1,0:T(8,128)(2,1)S(1)} %constant_dynamic-update-slice_fusion.near), channel_id=1, source_target_pairs={{0,1},{1,0},{2,3},{3,2},{4,5},{5,4},{6,7},{7,6},{8,9},{9,8},{10,11... | collective-permute-start | bytes 1966088 | tf_op jit(solution)/shard_map/ppermute | solution.py:230
  31.8 1.8 %copy-start.1 = (bf16[4,32,1280]{2,1,0:T(8,128)(2,1)S(1)}, bf16[4,32,1280]{2,1,0:T(8,128)(2,1)}, u32[]{:S(2)}) copy-start(bf16[4,32,1280]{2,1,0:T(8,128)(2,1)} %copy-done) | copy-start | bytes 983044
  31.8 1.8 %copy-start.5 = (bf16[4,32,1280]{2,1,0:T(8,128)(2,1)S(1)}, bf16[4,32,1280]{2,1,0:T(8,128)(2,1)}, u32[]{:S(2)}) copy-start(bf16[4,32,1280]{2,1,0:T(8,128)(2,1)} %copy-done.4) | copy-start | bytes 983044
  31.8 1.7 %collective-permute-start.5 = (bf16[4,32,1280]{2,1,0:T(8,128)(2,1)S(1)}, bf16[4,32,1280]{2,1,0:T(8,128)(2,1)S(1)}, u32[]{:S(2)}, u32[]{:S(2)}) collective-permute-start(bf16[4,32,1280]{2,1,0:T(8,128)(2,1)S(1)} %pad_maximum_fusion.2), channel_id=1, source_target_pairs={{0,1},{1,0},{2,3},{3,2},{4,5},{5,4},{6,7},{7,6},{8,9},{9,8},{10,11... | collective-permute-start | bytes 983048 | tf_op jit(solution)/shard_map/ppermute | solution.py:230
  38.3 8.0 %collective-permute-start.6 = (bf16[4,32,1280]{2,1,0:T(8,128)(2,1)}, bf16[4,32,1280]{2,1,0:T(8,128)(2,1)S(1)}, u32[]{:S(2)}, u32[]{:S(2)}) collective-permute-start(bf16[4,32,1280]{2,1,0:T(8,128)(2,1)} %get-tuple-element.8), channel_id=1, source_target_pairs={{0,4},{1,5},{2,6},{3,7},{4,0},{5,1},{6,2},{7,3},{8,12},{9,13},{10,... | collective-permute-start | bytes 983048 | tf_op jit(solution)/shard_map/ppermute | solution.py:230
  40.4 0.8 %copy-start.6 = (f32[10,96,128]{2,1,0:T(8,128)}, f32[10,96,128]{2,1,0:T(8,128)S(1)}, u32[]{:S(2)}) copy-start(f32[10,96,128]{2,1,0:T(8,128)S(1)} %get-tuple-element.11.mine) | copy-start | bytes 1474564
  41.2 27.7 %all-to-all-start.1 = ((bf16[4,10,96,128]{3,2,1,0:T(8,128)(2,1)}), bf16[4,10,96,128]{3,2,1,0:T(8,128)(2,1)S(1)}, u32[]{:S(2)}, u32[]{:S(2)}) async-start(bf16[4,10,96,128]{3,2,1,0:T(8,128)(2,1)} %get-tuple-element.10), calls=%async_computation.1 | async-start | bytes 1966080 | tf_op jit(solution)/shard_map/all_to_all | solution.py:273
  46.3 0.7 %copy-start.2 = (bf16[4,32,1280]{2,1,0:T(8,128)(2,1)}, bf16[4,32,1280]{2,1,0:T(8,128)(2,1)S(1)}, u32[]{:S(2)}) copy-start(bf16[4,32,1280]{2,1,0:T(8,128)(2,1)S(1)} %collective-permute-done.6.rest_1_) | copy-start | bytes 983044
  46.4 1.7 %collective-permute-start.7 = (bf16[4,32,1280]{2,1,0:T(8,128)(2,1)S(1)}, bf16[4,32,1280]{2,1,0:T(8,128)(2,1)S(1)}, u32[]{:S(2)}, u32[]{:S(2)}) collective-permute-start(bf16[4,32,1280]{2,1,0:T(8,128)(2,1)S(1)} %pad_maximum_fusion.3), channel_id=1, source_target_pairs={{0,1},{1,0},{2,3},{3,2},{4,5},{5,4},{6,7},{7,6},{8,9},{9,8},{10,11... | collective-permute-start | bytes 983048 | tf_op jit(solution)/shard_map/ppermute | solution.py:230
  47.0 1.0 %slice-start.2 = ((bf16[4,32,1280]{2,1,0:T(8,128)(2,1)}), bf16[1,32,1280]{2,1,0:T(8,128)(2,1)S(1)}, s32[]{:S(2)}) async-start(bf16[4,32,1280]{2,1,0:T(8,128)(2,1)} %copy-done.2), calls=%async_computation.4 | async-start | bytes 163840 | tf_op jit(solution)/shard_map/slice | solution.py:216
  48.1 9.9 %copy-start.3 = (bf16[4,32,1280]{2,1,0:T(8,128)(2,1)S(1)}, bf16[4,32,1280]{2,1,0:T(8,128)(2,1)}, u32[]{:S(2)}) copy-start(bf16[4,32,1280]{2,1,0:T(8,128)(2,1)} %copy-done.2) | copy-start | bytes 983044
  48.1 9.8 %collective-permute-start.8 = (bf16[4,32,1280]{2,1,0:T(8,128)(2,1)S(1)}, bf16[4,32,1280]{2,1,0:T(8,128)(2,1)S(1)}, u32[]{:S(2)}, u32[]{:S(2)}) collective-permute-start(bf16[4,32,1280]{2,1,0:T(8,128)(2,1)S(1)} %pad_maximum_fusion.4), channel_id=1, source_target_pairs={{0,2},{1,3},{2,0},{3,1},{4,6},{5,7},{6,4},{7,5},{8,10},{9,11},{10,... | collective-permute-start | bytes 983048 | tf_op jit(solution)/shard_map/ppermute | solution.py:230
  49.8 19.1 %copy-start.7 = (f32[10,96,128]{2,1,0:T(8,128)S(1)}, f32[10,96,128]{2,1,0:T(8,128)}, u32[]{:S(2)}) copy-start(f32[10,96,128]{2,1,0:T(8,128)} %copy-done.6) | copy-start | bytes 1474564

commit v12 on v11

--- a/solution.py
+++ b/solution.py
@@ -11,6 +11,8 @@
 SLOTS = 3
 PAIR = 2
 ROWS = 16
+DIRECT = 8
+STACK_FLOPS = 2 * 10**9
 ROOT = 0.7978845608028654
 CUBIC = 0.044715
 ANYWHERE = pl.BlockSpec(memory_space=pl.ANY)
@@ -116,12 +118,10 @@
 
 def forward_kernel(sizes, scalars, near, far, weights, backs, home, away, slopes):
     table = Table(scalars, *sizes)
-    shards, stripes = weights.shape[0], weights.shape[1]
     blocks, rows, _ = backs.shape
-    for s in range(stripes):
+    for s in range(weights.shape[0]):
         cols = slice(s * TILE, (s + 1) * TILE)
-        stack = jnp.concatenate([weights[f, s] for f in range(shards)], axis=0)
-        pre = jnp.dot(pick(table, near, far, s), stack, preferred_element_type=jnp.float32)
+        pre = jnp.dot(pick(table, near, far, s), weights[s], preferred_element_type=jnp.float32)
         act, slope = gelu_and_derivative(pre)
         act = act.astype(jnp.bfloat16)
         for i in range(blocks):
@@ -143,67 +143,80 @@
     )(scalars, near, far, weights, backs)
 
 
-def backward_kernel(sizes, scalars, near, far, slopes, grads, mine, sent, sems):
+def stack_kernel(scalars, *rest):
+    pieces, out = rest[:-1], rest[-1]
+    size = pieces[0].shape[1]
+    for p, piece in enumerate(pieces):
+        span = pl.ds(pl.multiple_of(scalars[p] * size, size), size)
+        for s in range(piece.shape[0]):
+            out[s, span] = piece[s]
+
+
+def stack_call(places, pieces):
+    stripes, size, _ = pieces[0].shape
+    return pl.pallas_call(
+        stack_kernel,
+        out_shape=jax.ShapeDtypeStruct((stripes, size * len(pieces), TILE), pieces[0].dtype),
+        in_specs=[SCALAR] + [RESIDENT] * len(pieces),
+        out_specs=RESIDENT,
+        compiler_params=room(6),
+        cost_estimate=pl.CostEstimate(flops=STACK_FLOPS, bytes_accessed=0, transcendentals=0),
+        name="stack",
+    )(places, *pieces)
+
+
+def backward_kernel(sizes, scalars, near, far, slopes, *rest):
+    outs, term = rest[:-1], rest[-1]
     table = Table(scalars, *sizes)
-    shards, stripes, size, _ = grads.shape
-    copies = []
+    stripes, size, _ = outs[0].shape
+    spans = [pl.ds(pl.multiple_of((table.own ^ p) * size, size), size) for p in range(len(outs))]
     for s in range(stripes):
         picked = pick(table, near, far, s)
         slope = slopes[:, s * TILE:(s + 1) * TILE]
-        term = lax.dot_general(picked, slope, (((0,), (0,)), ((), ())), preferred_element_type=jnp.float32)
-        pieces = [term[f * size:(f + 1) * size] for f in range(shards)]
-        for f in range(shards):
-            sent[s, f] = pieces[f].astype(sent.dtype)
-        copies.append(pltpu.make_async_copy(sent.at[s], grads.at[:, s], sems.at[s]))
-        copies[-1].start()
-        chosen = pieces[0]
-        for f in range(1, shards):
-            chosen = jnp.where(table.own == f, pieces[f], chosen)
-        mine[s] = chosen
-    for copy in copies:
-        copy.wait()
-
-
-def backward_call(sizes, scalars, near, far, slopes, shards):
-    stripes, size = slopes.shape[1] // TILE, SLOTS * TILE // shards
+        term[s] = lax.dot_general(picked, slope, (((0,), (0,)), ((), ())), preferred_element_type=jnp.float32)
+        for out, span in zip(outs, spans):
+            out[s] = term[s, span].astype(out.dtype)
+
+
+def backward_call(sizes, scalars, near, far, slopes, parts):
+    stripes, size = slopes.shape[1] // TILE, SLOTS * TILE // parts
     return pl.pallas_call(
         functools.partial(backward_kernel, sizes),
-        out_shape=[pltpu.HBM((shards, stripes, size, TILE), jnp.bfloat16), jax.ShapeDtypeStruct((stripes, size, TILE), jnp.float32)],
+        out_shape=[jax.ShapeDtypeStruct((stripes, size, TILE), jnp.bfloat16 if p else jnp.float32) for p in range(parts)],
         in_specs=[SCALAR] + [RESIDENT] * 3,
-        out_specs=[pl.BlockSpec(memory_space=pltpu.HBM), RESIDENT],
-        scratch_shapes=[pltpu.VMEM((stripes, shards, size, TILE), jnp.bfloat16), pltpu.SemaphoreType.DMA((stripes,))],
+        out_specs=[RESIDENT] * parts,
+        scratch_shapes=[pltpu.VMEM((stripes, SLOTS * TILE, TILE), jnp.float32)],
         compiler_params=room(10),
         name="backward",
     )(scalars, near, far, slopes)
 
 
-def sum_kernel(own, grads, mine, total, held, sems):
-    shards, stripes = grads.shape[0], grads.shape[1]
+def sum_kernel(half, *rest):
+    pieces, total, held, sems = rest[:-3], rest[-3], rest[-2], rest[-1]
+    stripes = pieces[0].shape[0]
     step = 5 if stripes % 5 == 0 else stripes
     copies = []
     for a in range(PAIR):
         for c in range(0, stripes, step):
-            held[a, c:c + step] = sum(
-                jnp.where(own[0] == f, mine[c:c + step], grads[f, c:c + step].astype(jnp.float32)) for f in range(a, shards, PAIR)
-            )
+            held[a, c:c + step] = sum(piece[c:c + step].astype(jnp.float32) for piece in pieces[a::PAIR])
             span = pl.ds(c, step)
-            copies.append(pltpu.make_async_copy(held.at[a, span], total.at[a, span], sems.at[len(copies)]))
+            copies.append(pltpu.make_async_copy(held.at[a, span], total.at[half[0] ^ a, span], sems.at[len(copies)]))
             copies[-1].start()
     for copy in copies:
         copy.wait()
 
 
-def sum_call(own, grads, mine):
-    shape = (PAIR,) + mine.shape
+def sum_call(half, pieces):
+    shape = (PAIR,) + pieces[0].shape
     return pl.pallas_call(
         sum_kernel,
         out_shape=jax.ShapeDtypeStruct(shape, jnp.float32),
-        in_specs=[SCALAR, RESIDENT, RESIDENT],
+        in_specs=[SCALAR] + [RESIDENT] * len(pieces),
         out_specs=ANYWHERE,
-        scratch_shapes=[pltpu.VMEM(shape, jnp.float32), pltpu.SemaphoreType.DMA((PAIR * mine.shape[0],))],
-        compiler_params=room(12),
+        scratch_shapes=[pltpu.VMEM(shape, jnp.float32), pltpu.SemaphoreType.DMA((PAIR * shape[1],))],
+        compiler_params=room(10),
         name="sum",
-    )(own, grads, mine)
+    )(half, *pieces)
 
 
 def take(arrays, refs):
@@ -239,19 +252,36 @@
             origins = origins + [(a, b ^ bit) for a, b in origins]
         return arrays, [group[0] for group in groups], origins
 
+    def spread(arrays, order):
+        refs, origins = [(a, order.index(0)) for a in range(PAIR)], [(a, 0) for a in range(PAIR)]
+        for b in order:
+            if b:
+                i = order.index(b)
+                refs = refs + [(len(arrays), a) for a in range(PAIR)]
+                arrays = arrays + [swap(take(arrays, [(a, i) for a in range(PAIR)]), 0, b)]
+                origins = origins + [(a, b) for a in range(PAIR)]
+        return arrays, refs, origins
+
     def first_tiles(steps):
         return jnp.stack([(t ^ b) * stripes + (half ^ a) * share for a, b in steps]).astype(jnp.int32)
 
+    direct = whole_tiles and fsdp <= DIRECT
+    leave = cut_call(first_tiles([(1, b) for b in range(tensor)]), cotangent, tensor)
+    arrived = swap(leave, 1, 0)
     by_stripe = jnp.transpose(tile_weights, (1, 0, 2))
-    outgoing = jnp.tile(by_stripe.reshape(PAIR, share, size, TILE), (fsdp // PAIR, 1, 1, 1))
-    weights = lax.all_to_all(outgoing, "fsdp", split_axis=0, concat_axis=0, tiled=True)
-    own = z.reshape(1).astype(jnp.int32)
-    if not whole_tiles:
-        weights = weights.transpose(1, 0, 2, 3).reshape(1, share, fsdp * size, TILE)
-
-    leave = cut_call(first_tiles([(1, b) for b in range(tensor)]), cotangent, tensor)
+    if direct:
+        same = lax.dynamic_slice_in_dim(by_stripe, half * share, share, 0)
+        other = lax.dynamic_slice_in_dim(by_stripe, (1 - half) * share, share, 0)
+        late, arrived = lax.optimization_barrier((other, arrived))
+        pieces = [same] + [swap((late if p == 1 else other) if p % PAIR else same, p, 0) for p in range(1, fsdp)]
+        weights = stack_call(jnp.stack([z ^ p for p in range(fsdp)]).astype(jnp.int32), pieces)
+    else:
+        outgoing = jnp.tile(by_stripe.reshape(PAIR, share, size, TILE), (fsdp // PAIR, 1, 1, 1))
+        stacks = lax.all_to_all(outgoing, "fsdp", split_axis=0, concat_axis=0, tiled=True)
+        weights = stacks.transpose(1, 0, 2, 3).reshape(share, fsdp * size, TILE)
+
     sizes = (tensor, stripes)
-    ends = jnp.stack([half * share, z]).astype(jnp.int32)
+    ends = jnp.stack([half * share, z if direct else z * 0]).astype(jnp.int32)
     scalars = jnp.concatenate([first_tiles([(0, b) for b in range(tensor)]), tile_list.reshape(-1), tile_counts, ends])
     stay = cut_call(scalars, cotangent, tensor)
     near = jnp.concatenate([tokens, swap(tokens, 1, 0)], axis=0)
@@ -259,18 +289,24 @@
         far = swap(near, 0, bit)
         if bit > 1:
             near = jnp.concatenate([near, far], axis=0)
-    arrays, refs, _ = exchange([stay, swap(leave, 1, 0)], bits)
+    arrays, refs, origins = exchange([stay, arrived], bits)
     backs = collect_call(arrays, refs)
     home, away, slopes = forward_call(sizes, scalars, near, far, weights, backs)
 
-    arrays, refs, origins = exchange([home, swap(away, 1, 0)], list(reversed(bits)))
-    activations = join_call(first_tiles(origins), arrays, refs)
-
-    grads, mine = backward_call(sizes, scalars, near, far, slopes, fsdp if whole_tiles else 1)
-    if not whole_tiles:
-        grads = grads.reshape(share, fsdp, size, TILE).transpose(1, 0, 2, 3)
-        mine = lax.dynamic_index_in_dim(mine.reshape(share, fsdp, size, TILE), z, 1, keepdims=False)
-    total = sum_call(own, lax.all_to_all(grads, "fsdp", split_axis=0, concat_axis=0, tiled=True), mine)
+    back_home = swap(away, 1, 0)
+
+    grads = list(backward_call(sizes, scalars, near, far, slopes, fsdp if direct else 1))
+    if direct:
+        grads[1], back_home = lax.optimization_barrier((grads[1], back_home))
+        total = sum_call(half.reshape(1).astype(jnp.int32), [grads[0]] + [swap(grads[p], p, 0) for p in range(1, fsdp)])
+    else:
+        split = grads[0].reshape(share, fsdp, size, TILE).transpose(1, 0, 2, 3)
+        arrived = lax.all_to_all(split.astype(jnp.bfloat16), "fsdp", split_axis=0, concat_axis=0, tiled=True)
+        here = (jnp.arange(fsdp) == z)[:, None, None, None]
+        total = jnp.where(here, split, arrived.astype(jnp.float32))
+        total = jnp.sum(total.reshape(fsdp // PAIR, PAIR, share, size, TILE), axis=0)
+    arrays, refs, steps = spread([home, back_home], [b for a, b in origins if a == 0])
+    activations = join_call(first_tiles(steps), arrays, refs)
     return activations, total.reshape(stripes, size, TILE).transpose(1, 0, 2)
 
 

time: 70.4 us -> 76.2 us (1.082)
  waiting for transfers between devices: 36.4 us -> 45 us
  local copies, waits for them, and re-layouts: 5.95 us -> 3.36 us
  other arithmetic: 0.25 us -> 1.69 us
    ppermute x9 -> x16, waiting for transfers between devices: 24.7 us -> 45 us  [swap(): return lax.ppermute(value, ('fsdp', 'tensor'), pairs)]
    all_to_all x2 -> x0, waiting for transfers between devices: 11.6 us -> none  [the longest x1 9.44 us: body(): lax.all_to_all(grads, 'fsdp', split_axis=0, concat_axis=0, tiled=True)]
    all_to_all x2 -> x0, starting transfers between devices: 8.92 us -> none  [the longest x1 5.41 us: body(): lax.all_to_all(outgoing, 'fsdp', split_axis=0, concat_axis=0, tiled=True)]
    ppermute x9 -> x16, starting transfers between devices: 7.14 us -> 15.4 us  [swap(): return lax.ppermute(value, ('fsdp', 'tensor'), pairs)]
    unnamed x27 -> x15, local copies, waits for them, and re-layouts: 3.54 us -> 2.17 us
    concatenate x4 -> x5, other arithmetic: 0.15 us -> 1.52 us  [take(): return pieces[0] if len(pieces) == 1 else jnp.concatenate(pieces, axis=0)]
    another operation x1 -> x0, local copies, waits for them, and re-layouts: 1.1 us -> none  [body(): jnp.tile(by_stripe.reshape(PAIR, share, size, TILE), (fsdp // PAIR, 1, 1,...]
    pallas_call x1 -> x2, Pallas kernels: 2.05 us -> 1.98 us  [the longest x1 1.37 us: backward_call(): pl.pallas_call(functools.partial(backward_kernel, sizes), out_shape=[jax....]
  transfers between devices with their start and end apart: 11 -> 16, of which waited for: 8 -> 6; matrix products, arithmetic and copies ran while one was open for 3% -> 3% of each run, Pallas kernels for 10% -> 7%
where the time goes in v12:
time: 76.2 us; the launch traced here: 76 us
  waiting for transfers between devices  45 us (59%)
  starting transfers between devices  15.4 us (20%)
  Pallas kernels  9.64 us (13%)
  local copies, waits for them, and re-layouts  3.36 us (4%)
  other arithmetic  1.69 us (2%)
  between operations  0.9 us (1%)
    ppermute x16, waiting for transfers between devices, swap(): return lax.ppermute(value, ('fsdp', 'tensor'), pairs)  45 us
    ppermute x16, starting transfers between devices, swap(): return lax.ppermute(value, ('fsdp', 'tensor'), pairs)  15.4 us
    pallas_call x2, Pallas kernels, cut_call(): pl.pallas_call(cut_kernel, out_shape=jax.ShapeDtypeStruct((count, rows, w...  3.18 us
    unnamed x15, local copies, waits for them, and re-layouts  2.17 us
    pallas_call x1, Pallas kernels, forward_call(): pl.pallas_call(functools.partial(forward_kernel, sizes), out_shape=[jax.S...  1.85 us
  transfers between devices with their start and end apart: 16, of which 6 were waited for; matrix products, arithmetic and copies ran while one was open for 3% of the time, Pallas kernels for 7%

profile of v12, /device:TPU:0, one launch (start us, length us, event | category | flops | bytes accessed | tf_op | source)
XLA Modules:
  0.0 76.0 jit_solution(6304076522352965519)
XLA Ops:
  0.6 3.1 %collective-permute-start = (bf16[32,2560]{1,0:T(8,128)(2,1)}, bf16[32,2560]{1,0:T(8,128)(2,1)S(1)}, u32[]{:S(2)}, u32[]{:S(2)}) collective-permute-start(bf16[32,2560]{1,0:T(8,128)(2,1)} %param.5), channel_id=1, source_target_pairs={{0,4},{1,5},{2,6},{3,7},{4,0},{5,1},{6,2},{7,3},{8,12},{9,13},{10,... | collective-permute-start | bytes 491528 | tf_op jit(solution)/shard_map/ppermute | solution.py:243
  3.7 0.1 pad_add_fusion.1.starts
  3.8 1.6 %cut.2 = bf16[4,32,1280]{2,1,0:T(8,128)(2,1)S(1)} custom-call(s32[4]{0:T(128)S(1)} %pad_add_fusion.1.starts, bf16[32,10240]{1,0:T(8,128)(2,1)} %whole.3), custom_call_target="tpu_custom_call" | custom-call | tf_op jit(solution)/shard_map/cut/pallas_call | solution.py:50
  5.4 0.1 collective-permute-start.3
  5.6 4.1 %collective-permute-start.6 = (bf16[10,96,128]{2,1,0:T(8,128)(2,1)S(1)}, bf16[10,96,128]{2,1,0:T(8,128)(2,1)S(1)}, u32[]{:S(2)}, u32[]{:S(2)}) collective-permute-start(bf16[10,96,128]{2,1,0:T(8,128)(2,1)S(1)} %get-tuple-element.13), channel_id=1, source_target_pairs={{0,12},{1,13},{2,14},{3,15},{4,8},{5,9},{6,10},{7,11},{8,4},{9,5},... | collective-permute-start | bytes 737288 | tf_op jit(solution)/shard_map/ppermute | solution.py:243
  9.7 0.7 copy-done.4
  10.3 0.1 copy.8
  10.4 0.1 reshape.13
  10.5 0.6 copy-done.5
  11.3 1.6 %cut.3.rest_0_ = bf16[4,32,1280]{2,1,0:T(8,128)(2,1)S(1)} custom-call(s32[86]{0:T(128)S(1)} %concatenate.25.starts.scalars, bf16[32,10240]{1,0:T(8,128)(2,1)} %whole.3), custom_call_target="tpu_custom_call" | custom-call | tf_op jit(solution)/shard_map/cut/pallas_call | solution.py:50
  12.9 0.7 copy-done
  13.6 1.6 %collective-permute-start.1 = (bf16[64,2560]{1,0:T(8,128)(2,1)S(1)}, bf16[64,2560]{1,0:T(8,128)(2,1)S(1)}, u32[]{:S(2)}, u32[]{:S(2)}) collective-permute-start(bf16[64,2560]{1,0:T(8,128)(2,1)S(1)} %pad_maximum_fusion), channel_id=1, source_target_pairs={{0,2},{1,3},{2,0},{3,1},{4,6},{5,7},{6,4},{7,5},{8,10},{9,11},{10,... | collective-permute-start | bytes 983048 | tf_op jit(solution)/shard_map/ppermute | solution.py:243
  15.2 9.2 %collective-permute-done.3.rest_1_ = bf16[4,32,1280]{2,1,0:T(8,128)(2,1)S(1)} collective-permute-done((bf16[4,32,1280]{2,1,0:T(8,128)(2,1)S(1)}, bf16[4,32,1280]{2,1,0:T(8,128)(2,1)S(1)}, u32[]{:S(2)}, u32[]{:S(2)}) %collective-permute-start.3) | collective-permute-done | bytes 327712 | tf_op jit(solution)/shard_map/ppermute | solution.py:243
  24.5 0.8 %slice-done.1 = bf16[2,32,1280]{2,1,0:T(8,128)(2,1)S(1)} async-done(((bf16[4,32,1280]{2,1,0:T(8,128)(2,1)}), bf16[2,32,1280]{2,1,0:T(8,128)(2,1)S(1)}, s32[]{:S(2)}) %slice-start.1) | async-done | bytes 163864 | tf_op jit(solution)/shard_map/slice | solution.py:229
  25.3 0.9 %collective-permute-start.7 = (bf16[4,32,1280]{2,1,0:T(8,128)(2,1)S(1)}, bf16[4,32,1280]{2,1,0:T(8,128)(2,1)S(1)}, u32[]{:S(2)}, u32[]{:S(2)}) collective-permute-start(bf16[4,32,1280]{2,1,0:T(8,128)(2,1)S(1)} %pad_maximum_fusion.1), channel_id=1, source_target_pairs={{0,2},{1,3},{2,0},{3,1},{4,6},{5,7},{6,4},{7,5},{8,10},{9,11},{10,... | collective-permute-start | bytes 983048 | tf_op jit(solution)/shard_map/ppermute | solution.py:243
  26.4 6.6 %collective-permute-done.7.rest_2_ = bf16[4,32,1280]{2,1,0:T(8,128)(2,1)S(1)} collective-permute-done((bf16[4,32,1280]{2,1,0:T(8,128)(2,1)S(1)}, bf16[4,32,1280]{2,1,0:T(8,128)(2,1)S(1)}, u32[]{:S(2)}, u32[]{:S(2)}) %collective-permute-start.7) | collective-permute-done | bytes 327712 | tf_op jit(solution)/shard_map/ppermute | solution.py:243
  33.0 0.8 %pad_maximum_fusion.2 = bf16[4,32,1280]{2,1,0:T(8,128)(2,1)} fusion(bf16[1,32,1280]{2,1,0:T(8,128)(2,1)S(1)} %get-tuple-element.33, bf16[1,32,1280]{2,1,0:T(8,128)(2,1)S(1)} %get-tuple-element.32, bf16[1,32,1280]{2,1,0:T(8,128)(2,1)S(1)} %slice.39, bf16[1,32,1280]{2,1,0:T(8,128)(2,1)S(1)} %slice-done), kind=kLoop, calls=%fused_computation.2 | loop fusion | flops 491520 | bytes 655360 | tf_op jit(solution)/shard_map/concatenate | solution.py:230
  33.9 0.6 stack.74.weights
  34.5 1.1 %collective-permute-done.8.rest_3_ = bf16[4,32,1280]{2,1,0:T(8,128)(2,1)S(1)} collective-permute-done((bf16[4,32,1280]{2,1,0:T(8,128)(2,1)}, bf16[4,32,1280]{2,1,0:T(8,128)(2,1)S(1)}, u32[]{:S(2)}, u32[]{:S(2)}) %collective-permute-start.8) | collective-permute-done | bytes 327712 | tf_op jit(solution)/shard_map/ppermute | solution.py:243
  35.7 1.9 %forward.1 = (bf16[4,32,1280]{2,1,0:T(8,128)(2,1)S(1)}, bf16[4,32,1280]{2,1,0:T(8,128)(2,1)S(1)}, bf16[256,1280]{1,0:T(8,128)(2,1)S(1)}) custom-call(s32[86]{0:T(128)S(1)} %concatenate.25.starts.scalars, bf16[128,2560]{1,0:T(8,128)(2,1)S(1)} %constant_dynamic-update-slice_fusion.near, bf16[128,2560]{1,0:T(8,128)(2,1)S(1)} %collective-permute-done.2.far, ...), custom_call_target="tpu_custom_call" | custom-call | tf_op jit(solution)/shard_map/forward/pallas_call | solution.py:135
  37.5 1.4 %backward.1 = (f32[10,96,128]{2,1,0:T(8,128)S(1)}, bf16[10,96,128]{2,1,0:T(8,128)(2,1)S(1)}, bf16[10,96,128]{2,1,0:T(8,128)(2,1)S(1)}, bf16[10,96,128]{2,1,0:T(8,128)(2,1)S(1)}) custom-call(s32[86]{0:T(128)S(1)} %concatenate.25.starts.scalars, bf16[128,2560]{1,0:T(8,128)(2,1)S(1)} %constant_dynamic-update-slice_fusion.near, ...), custom_call_target="tpu_custom_call" | custom-call | tf_op jit(solution)/shard_map/backward/pallas_call | solution.py:183
  38.9 2.5 %collective-permute-start.14 = (bf16[10,96,128]{2,1,0:T(8,128)(2,1)S(1)}, bf16[10,96,128]{2,1,0:T(8,128)(2,1)S(1)}, u32[]{:S(2)}, u32[]{:S(2)}) collective-permute-start(bf16[10,96,128]{2,1,0:T(8,128)(2,1)S(1)} %get-tuple-element.22), channel_id=1, source_target_pairs={{0,8},{1,9},{2,10},{3,11},{4,12},{5,13},{6,14},{7,15},{8,0},{9,1},... | collective-permute-start | bytes 737288 | tf_op jit(solution)/shard_map/ppermute | solution.py:243
  41.4 0.9 %collective-permute-start.15 = (bf16[10,96,128]{2,1,0:T(8,128)(2,1)S(1)}, bf16[10,96,128]{2,1,0:T(8,128)(2,1)S(1)}, u32[]{:S(2)}, u32[]{:S(2)}) collective-permute-start(bf16[10,96,128]{2,1,0:T(8,128)(2,1)S(1)} %get-tuple-element.23), channel_id=1, source_target_pairs={{0,12},{1,13},{2,14},{3,15},{4,8},{5,9},{6,10},{7,11},{8,4},{9,5},... | collective-permute-start | bytes 737288 | tf_op jit(solution)/shard_map/ppermute | solution.py:243
  42.3 0.2 collective-permute-start.9
  42.5 19.0 %collective-permute-done.9.rest_1_ = bf16[4,32,1280]{2,1,0:T(8,128)(2,1)S(1)} collective-permute-done((bf16[4,32,1280]{2,1,0:T(8,128)(2,1)S(1)}, bf16[4,32,1280]{2,1,0:T(8,128)(2,1)S(1)}, u32[]{:S(2)}, u32[]{:S(2)}) %collective-permute-start.9) | collective-permute-done | bytes 327712 | tf_op jit(solution)/shard_map/ppermute | solution.py:243
  61.6 1.8 %collective-permute-start.10 = (bf16[2,32,1280]{2,1,0:T(8,128)(2,1)S(1)}, bf16[2,32,1280]{2,1,0:T(8,128)(2,1)S(1)}, u32[]{:S(2)}, u32[]{:S(2)}) collective-permute-start(bf16[2,32,1280]{2,1,0:T(8,128)(2,1)S(1)} %pad_maximum_fusion.3), channel_id=1, source_target_pairs={{0,2},{1,3},{2,0},{3,1},{4,6},{5,7},{6,4},{7,5},{8,10},{9,11},{10,... | collective-permute-start | bytes 491528 | tf_op jit(solution)/shard_map/ppermute | solution.py:243
  63.6 0.7 pad_maximum_fusion.5
  64.2 2.7 %collective-permute-done.10.rest_2_ = bf16[2,32,1280]{2,1,0:T(8,128)(2,1)S(1)} collective-permute-done((bf16[2,32,1280]{2,1,0:T(8,128)(2,1)S(1)}, bf16[2,32,1280]{2,1,0:T(8,128)(2,1)S(1)}, u32[]{:S(2)}, u32[]{:S(2)}) %collective-permute-start.10) | collective-permute-done | bytes 163872 | tf_op jit(solution)/shard_map/ppermute | solution.py:243
  67.0 0.1 stack.66.starts
  67.0 6.3 %collective-permute-done.12.rest_4_ = bf16[2,32,1280]{2,1,0:T(8,128)(2,1)S(1)} collective-permute-done((bf16[2,32,1280]{2,1,0:T(8,128)(2,1)}, bf16[2,32,1280]{2,1,0:T(8,128)(2,1)S(1)}, u32[]{:S(2)}, u32[]{:S(2)}) %collective-permute-start.12) | collective-permute-done | bytes 163872 | tf_op jit(solution)/shard_map/ppermute | solution.py:243
  73.4 1.4 %join.1 = bf16[32,10240]{1,0:T(8,128)(2,1)} custom-call(s32[8]{0:T(128)S(1)} %stack.66.starts, bf16[4,32,1280]{2,1,0:T(8,128)(2,1)S(1)} %get-tuple-element.15.rest_0_, bf16[4,32,1280]{2,1,0:T(8,128)(2,1)S(1)} %collective-permute-done.9.rest_1_, bf16[2,32,1280]{2,1,0:T(8,128)(2,1)S(1)} %collective-permute-done.10.rest_2_, ...), custom_call_target="tpu_custom_call" | custom-call | tf_op jit(solution)/shard_map/join/pallas_call | solution.py:87
  74.8 1.1 %sum.1 = f32[2,10,96,128]{3,2,1,0:T(8,128)} custom-call(s32[1]{0:T(128)} %bitcast.15.half, f32[10,96,128]{2,1,0:T(8,128)S(1)} %get-tuple-element.20.rest_0_, bf16[10,96,128]{2,1,0:T(8,128)(2,1)S(1)} %collective-permute-done.13.rest_1_, bf16[10,96,128]{2,1,0:T(8,128)(2,1)S(1)} %collective-permute-done.14.rest_2_, ...), custom_call_target="tpu_custom_call" | custom-call | tf_op jit(solution)/shard_map/sum/pallas_call | solution.py:211
  (45 shorter events, 0.8 us)
Async XLA Ops:
  0.6 13.0 %collective-permute-start = (bf16[32,2560]{1,0:T(8,128)(2,1)}, bf16[32,2560]{1,0:T(8,128)(2,1)S(1)}, u32[]{:S(2)}, u32[]{:S(2)}) collective-permute-start(bf16[32,2560]{1,0:T(8,128)(2,1)} %param.5), channel_id=1, source_target_pairs={{0,4},{1,5},{2,6},{3,7},{4,0},{5,1},{6,2},{7,3},{8,12},{9,13},{10,... | collective-permute-start | bytes 491528 | tf_op jit(solution)/shard_map/ppermute | solution.py:243
  3.8 1.7 %copy-start.3 = (bf16[96,20,128]{2,0,1:T(8,128)(2,1)S(1)}, bf16[96,20,128]{2,0,1:T(8,128)(2,1)}, u32[]{:S(2)}) copy-start(bf16[96,20,128]{2,0,1:T(8,128)(2,1)} %param.6) | copy-start | bytes 1474564
  5.4 19.0 %collective-permute-start.3 = (bf16[4,32,1280]{2,1,0:T(8,128)(2,1)S(1)}, bf16[4,32,1280]{2,1,0:T(8,128)(2,1)S(1)}, u32[]{:S(2)}, u32[]{:S(2)}) collective-permute-start(bf16[4,32,1280]{2,1,0:T(8,128)(2,1)S(1)} %cut.2), channel_id=1, source_target_pairs={{0,4},{1,5},{2,6},{3,7},{4,0},{5,1},{6,2},{7,3},{8,12},{9,13},{10,... | collective-permute-start | bytes 983048 | tf_op jit(solution)/shard_map/ppermute | solution.py:243
  5.5 4.1 %copy-start.2 = (bf16[32,2560]{1,0:T(8,128)(2,1)S(1)}, bf16[32,2560]{1,0:T(8,128)(2,1)}, u32[]{:S(2)}) copy-start(bf16[32,2560]{1,0:T(8,128)(2,1)} %param.5) | copy-start | bytes 491524
  5.6 28.3 %collective-permute-start.6 = (bf16[10,96,128]{2,1,0:T(8,128)(2,1)S(1)}, bf16[10,96,128]{2,1,0:T(8,128)(2,1)S(1)}, u32[]{:S(2)}, u32[]{:S(2)}) collective-permute-start(bf16[10,96,128]{2,1,0:T(8,128)(2,1)S(1)} %get-tuple-element.13), channel_id=1, source_target_pairs={{0,12},{1,13},{2,14},{3,15},{4,8},{5,9},{6,10},{7,11},{8,4},{9,5},... | collective-permute-start | bytes 737288 | tf_op jit(solution)/shard_map/ppermute | solution.py:243
  9.6 24.2 %collective-permute-start.5 = (bf16[10,96,128]{2,1,0:T(8,128)(2,1)S(1)}, bf16[10,96,128]{2,1,0:T(8,128)(2,1)S(1)}, u32[]{:S(2)}, u32[]{:S(2)}) collective-permute-start(bf16[10,96,128]{2,1,0:T(8,128)(2,1)S(1)} %get-tuple-element.25.rest_0_), channel_id=1, source_target_pairs={{0,8},{1,9},{2,10},{3,11},{4,12},{5,13},{6,14},{7,15},{8,0},{9,1},... | collective-permute-start | bytes 737288 | tf_op jit(solution)/shard_map/ppermute | solution.py:243
  9.6 0.7 copy-start.4
  10.5 0.7 copy-start.5
  12.9 0.7 copy-start
  13.6 12.6 %collective-permute-start.1 = (bf16[64,2560]{1,0:T(8,128)(2,1)S(1)}, bf16[64,2560]{1,0:T(8,128)(2,1)S(1)}, u32[]{:S(2)}, u32[]{:S(2)}) collective-permute-start(bf16[64,2560]{1,0:T(8,128)(2,1)S(1)} %pad_maximum_fusion), channel_id=1, source_target_pairs={{0,2},{1,3},{2,0},{3,1},{4,6},{5,7},{6,4},{7,5},{8,10},{9,11},{10,... | collective-permute-start | bytes 983048 | tf_op jit(solution)/shard_map/ppermute | solution.py:243
  24.4 0.9 %slice-start.1 = ((bf16[4,32,1280]{2,1,0:T(8,128)(2,1)}), bf16[2,32,1280]{2,1,0:T(8,128)(2,1)S(1)}, s32[]{:S(2)}) async-start(bf16[4,32,1280]{2,1,0:T(8,128)(2,1)} %copy-done), calls=%async_computation.1 | async-start | bytes 327680 | tf_op jit(solution)/shard_map/slice | solution.py:229
  24.4 9.5 %collective-permute-start.4 = (bf16[10,96,128]{2,1,0:T(8,128)(2,1)S(1)}, bf16[10,96,128]{2,1,0:T(8,128)(2,1)S(1)}, u32[]{:S(2)}, u32[]{:S(2)}) collective-permute-start(bf16[10,96,128]{2,1,0:T(8,128)(2,1)S(1)} %get-tuple-element.13), channel_id=1, source_target_pairs={{0,4},{1,5},{2,6},{3,7},{4,0},{5,1},{6,2},{7,3},{8,12},{9,13},{10,... | collective-permute-start | bytes 737288 | tf_op jit(solution)/shard_map/ppermute | solution.py:243
  25.3 7.6 %collective-permute-start.7 = (bf16[4,32,1280]{2,1,0:T(8,128)(2,1)S(1)}, bf16[4,32,1280]{2,1,0:T(8,128)(2,1)S(1)}, u32[]{:S(2)}, u32[]{:S(2)}) collective-permute-start(bf16[4,32,1280]{2,1,0:T(8,128)(2,1)S(1)} %pad_maximum_fusion.1), channel_id=1, source_target_pairs={{0,2},{1,3},{2,0},{3,1},{4,6},{5,7},{6,4},{7,5},{8,10},{9,11},{10,... | collective-permute-start | bytes 983048 | tf_op jit(solution)/shard_map/ppermute | solution.py:243
  26.3 6.7 %slice-start = ((bf16[4,32,1280]{2,1,0:T(8,128)(2,1)}), bf16[1,32,1280]{2,1,0:T(8,128)(2,1)S(1)}, s32[]{:S(2)}) async-start(bf16[4,32,1280]{2,1,0:T(8,128)(2,1)} %copy-done), calls=%async_computation | async-start | bytes 163840 | tf_op jit(solution)/shard_map/slice | solution.py:229
  26.3 9.4 %collective-permute-start.2 = (bf16[128,2560]{1,0:T(8,128)(2,1)S(1)}, bf16[128,2560]{1,0:T(8,128)(2,1)S(1)}, u32[]{:S(2)}, u32[]{:S(2)}) collective-permute-start(bf16[128,2560]{1,0:T(8,128)(2,1)S(1)} %constant_dynamic-update-slice_fusion.near), channel_id=1, source_target_pairs={{0,1},{1,0},{2,3},{3,2},{4,5},{5,4},{6,7},{7,6},{8,9},{9,8},{10,11... | collective-permute-start | bytes 1966088 | tf_op jit(solution)/shard_map/ppermute | solution.py:243
  33.8 1.8 %collective-permute-start.8 = (bf16[4,32,1280]{2,1,0:T(8,128)(2,1)}, bf16[4,32,1280]{2,1,0:T(8,128)(2,1)S(1)}, u32[]{:S(2)}, u32[]{:S(2)}) collective-permute-start(bf16[4,32,1280]{2,1,0:T(8,128)(2,1)} %pad_maximum_fusion.2), channel_id=1, source_target_pairs={{0,1},{1,0},{2,3},{3,2},{4,5},{5,4},{6,7},{7,6},{8,9},{9,8},{10,11... | collective-permute-start | bytes 983048 | tf_op jit(solution)/shard_map/ppermute | solution.py:243
  33.9 1.8 %copy-start.1 = (bf16[4,32,1280]{2,1,0:T(8,128)(2,1)S(1)}, bf16[4,32,1280]{2,1,0:T(8,128)(2,1)}, u32[]{:S(2)}) copy-start(bf16[4,32,1280]{2,1,0:T(8,128)(2,1)} %copy-done) | copy-start | bytes 983044
  38.9 35.9 %collective-permute-start.14 = (bf16[10,96,128]{2,1,0:T(8,128)(2,1)S(1)}, bf16[10,96,128]{2,1,0:T(8,128)(2,1)S(1)}, u32[]{:S(2)}, u32[]{:S(2)}) collective-permute-start(bf16[10,96,128]{2,1,0:T(8,128)(2,1)S(1)} %get-tuple-element.22), channel_id=1, source_target_pairs={{0,8},{1,9},{2,10},{3,11},{4,12},{5,13},{6,14},{7,15},{8,0},{9,1},... | collective-permute-start | bytes 737288 | tf_op jit(solution)/shard_map/ppermute | solution.py:243
  41.4 33.4 %collective-permute-start.15 = (bf16[10,96,128]{2,1,0:T(8,128)(2,1)S(1)}, bf16[10,96,128]{2,1,0:T(8,128)(2,1)S(1)}, u32[]{:S(2)}, u32[]{:S(2)}) collective-permute-start(bf16[10,96,128]{2,1,0:T(8,128)(2,1)S(1)} %get-tuple-element.23), channel_id=1, source_target_pairs={{0,12},{1,13},{2,14},{3,15},{4,8},{5,9},{6,10},{7,11},{8,4},{9,5},... | collective-permute-start | bytes 737288 | tf_op jit(solution)/shard_map/ppermute | solution.py:243
  42.3 19.3 %collective-permute-start.9 = (bf16[4,32,1280]{2,1,0:T(8,128)(2,1)S(1)}, bf16[4,32,1280]{2,1,0:T(8,128)(2,1)S(1)}, u32[]{:S(2)}, u32[]{:S(2)}) collective-permute-start(bf16[4,32,1280]{2,1,0:T(8,128)(2,1)S(1)} %get-tuple-element.18), channel_id=1, source_target_pairs={{0,4},{1,5},{2,6},{3,7},{4,0},{5,1},{6,2},{7,3},{8,12},{9,13},{10,... | collective-permute-start | bytes 983048 | tf_op jit(solution)/shard_map/ppermute | solution.py:243
  61.6 5.4 %collective-permute-start.10 = (bf16[2,32,1280]{2,1,0:T(8,128)(2,1)S(1)}, bf16[2,32,1280]{2,1,0:T(8,128)(2,1)S(1)}, u32[]{:S(2)}, u32[]{:S(2)}) collective-permute-start(bf16[2,32,1280]{2,1,0:T(8,128)(2,1)S(1)} %pad_maximum_fusion.3), channel_id=1, source_target_pairs={{0,2},{1,3},{2,0},{3,1},{4,6},{5,7},{6,4},{7,5},{8,10},{9,11},{10,... | collective-permute-start | bytes 491528 | tf_op jit(solution)/shard_map/ppermute | solution.py:243
  63.4 3.6 %collective-permute-start.11 = (bf16[2,32,1280]{2,1,0:T(8,128)(2,1)S(1)}, bf16[2,32,1280]{2,1,0:T(8,128)(2,1)S(1)}, u32[]{:S(2)}, u32[]{:S(2)}) collective-permute-start(bf16[2,32,1280]{2,1,0:T(8,128)(2,1)S(1)} %pad_maximum_fusion.4), channel_id=1, source_target_pairs={{0,1},{1,0},{2,3},{3,2},{4,5},{5,4},{6,7},{7,6},{8,9},{9,8},{10,11... | collective-permute-start | bytes 491528 | tf_op jit(solution)/shard_map/ppermute | solution.py:243
  63.5 11.3 %collective-permute-start.13 = (bf16[10,96,128]{2,1,0:T(8,128)(2,1)S(1)}, bf16[10,96,128]{2,1,0:T(8,128)(2,1)S(1)}, u32[]{:S(2)}, u32[]{:S(2)}) collective-permute-start(bf16[10,96,128]{2,1,0:T(8,128)(2,1)S(1)} %get-tuple-element.21), channel_id=1, source_target_pairs={{0,4},{1,5},{2,6},{3,7},{4,0},{5,1},{6,2},{7,3},{8,12},{9,13},{10,... | collective-permute-start | bytes 737288 | tf_op jit(solution)/shard_map/ppermute | solution.py:243
  66.9 6.4 %collective-permute-start.12 = (bf16[2,32,1280]{2,1,0:T(8,128)(2,1)}, bf16[2,32,1280]{2,1,0:T(8,128)(2,1)S(1)}, u32[]{:S(2)}, u32[]{:S(2)}) collective-permute-start(bf16[2,32,1280]{2,1,0:T(8,128)(2,1)} %pad_maximum_fusion.5), channel_id=1, source_target_pairs={{0,3},{1,2},{2,1},{3,0},{4,7},{5,6},{6,5},{7,4},{8,11},{9,10},{10,... | collective-permute-start | bytes 491528 | tf_op jit(solution)/shard_map/ppermute | solution.py:243

commit v13 on v12

--- a/solution.py
+++ b/solution.py
@@ -273,7 +273,7 @@
         same = lax.dynamic_slice_in_dim(by_stripe, half * share, share, 0)
         other = lax.dynamic_slice_in_dim(by_stripe, (1 - half) * share, share, 0)
         late, arrived = lax.optimization_barrier((other, arrived))
-        pieces = [same] + [swap((late if p == 1 else other) if p % PAIR else same, p, 0) for p in range(1, fsdp)]
+        pieces = [same] + [swap(late if p % PAIR else same, p, 0) for p in range(1, fsdp)]
         weights = stack_call(jnp.stack([z ^ p for p in range(fsdp)]).astype(jnp.int32), pieces)
     else:
         outgoing = jnp.tile(by_stripe.reshape(PAIR, share, size, TILE), (fsdp // PAIR, 1, 1, 1))
@@ -297,7 +297,7 @@
 
     grads = list(backward_call(sizes, scalars, near, far, slopes, fsdp if direct else 1))
     if direct:
-        grads[1], back_home = lax.optimization_barrier((grads[1], back_home))
+        grads[1::PAIR], back_home = lax.optimization_barrier((grads[1::PAIR], back_home))
         total = sum_call(half.reshape(1).astype(jnp.int32), [grads[0]] + [swap(grads[p], p, 0) for p in range(1, fsdp)])
     else:
         split = grads[0].reshape(share, fsdp, size, TILE).transpose(1, 0, 2, 3)

time: 76.2 us -> 72.5 us (0.951)
  waiting for transfers between devices: 45 us -> 35 us
  starting transfers between devices: 15.4 us -> 22.5 us
  local copies, waits for them, and re-layouts: 3.36 us -> 2.55 us
    ppermute x16, waiting for transfers between devices: 45 us -> 35 us  [swap(): return lax.ppermute(value, ('fsdp', 'tensor'), pairs)]
    ppermute x16, starting transfers between devices: 15.4 us -> 22.5 us  [swap(): return lax.ppermute(value, ('fsdp', 'tensor'), pairs)]
    slice x9, local copies, waits for them, and re-layouts: 0.88 us -> 0.07 us  [take(): arrays[a][low:high]]
where the time goes in v13:
time: 72.5 us; the launch traced here: 72.3 us
  waiting for transfers between devices  35 us (48%)
  starting transfers between devices  22.5 us (31%)
  Pallas kernels  9.63 us (13%)
  local copies, waits for them, and re-layouts  2.55 us (4%)
  other arithmetic  1.69 us (2%)
  between operations  0.89 us (1%)
    ppermute x16, waiting for transfers between devices, swap(): return lax.ppermute(value, ('fsdp', 'tensor'), pairs)  35 us
    ppermute x16, starting transfers between devices, swap(): return lax.ppermute(value, ('fsdp', 'tensor'), pairs)  22.5 us
    pallas_call x2, Pallas kernels, cut_call(): pl.pallas_call(cut_kernel, out_shape=jax.ShapeDtypeStruct((count, rows, w...  3.18 us
    unnamed x15, local copies, waits for them, and re-layouts  2.17 us
    pallas_call x1, Pallas kernels, forward_call(): pl.pallas_call(functools.partial(forward_kernel, sizes), out_shape=[jax.S...  1.85 us
    concatenate x5, other arithmetic, take(): return pieces[0] if len(pieces) == 1 else jnp.concatenate(pieces, axis=0)  1.52 us
  transfers between devices with their start and end apart: 16, of which 6 were waited for; matrix products, arithmetic and copies ran while one was open for 3% of the time, Pallas kernels for 7%

profile of v13, /device:TPU:0, one launch (start us, length us, event | category | flops | bytes accessed | tf_op | source)
XLA Modules:
  0.0 72.3 jit_solution(12980673779363188439)
XLA Ops:
  0.6 3.1 %collective-permute-start = (bf16[32,2560]{1,0:T(8,128)(2,1)}, bf16[32,2560]{1,0:T(8,128)(2,1)S(1)}, u32[]{:S(2)}, u32[]{:S(2)}) collective-permute-start(bf16[32,2560]{1,0:T(8,128)(2,1)} %param.5), channel_id=1, source_target_pairs={{0,4},{1,5},{2,6},{3,7},{4,0},{5,1},{6,2},{7,3},{8,12},{9,13},{10,... | collective-permute-start | bytes 491528 | tf_op jit(solution)/shard_map/ppermute | solution.py:243
  3.8 1.6 %cut.2 = bf16[4,32,1280]{2,1,0:T(8,128)(2,1)S(1)} custom-call(s32[4]{0:T(128)S(1)} %pad_add_fusion.1.starts, bf16[32,10240]{1,0:T(8,128)(2,1)} %whole.3), custom_call_target="tpu_custom_call" | custom-call | tf_op jit(solution)/shard_map/cut/pallas_call | solution.py:50
  5.4 0.1 collective-permute-start.3
  5.6 3.0 %collective-permute-start.5 = (bf16[10,96,128]{2,1,0:T(8,128)(2,1)S(1)}, bf16[10,96,128]{2,1,0:T(8,128)(2,1)S(1)}, u32[]{:S(2)}, u32[]{:S(2)}) collective-permute-start(bf16[10,96,128]{2,1,0:T(8,128)(2,1)S(1)} %get-tuple-element.27.rest_0_), channel_id=1, source_target_pairs={{0,8},{1,9},{2,10},{3,11},{4,12},{5,13},{6,14},{7,15},{8,0},{9,1},... | collective-permute-start | bytes 737288 | tf_op jit(solution)/shard_map/ppermute | solution.py:243
  8.7 0.7 copy-done.4
  9.3 0.1 copy.8
  9.4 0.1 reshape.13
  9.5 0.6 copy-done.5
  10.2 1.6 %cut.3.rest_0_ = bf16[4,32,1280]{2,1,0:T(8,128)(2,1)S(1)} custom-call(s32[86]{0:T(128)S(1)} %concatenate.25.starts.scalars, bf16[32,10240]{1,0:T(8,128)(2,1)} %whole.3), custom_call_target="tpu_custom_call" | custom-call | tf_op jit(solution)/shard_map/cut/pallas_call | solution.py:50
  11.9 0.7 copy-done
  12.6 3.2 %collective-permute-start.1 = (bf16[64,2560]{1,0:T(8,128)(2,1)S(1)}, bf16[64,2560]{1,0:T(8,128)(2,1)S(1)}, u32[]{:S(2)}, u32[]{:S(2)}) collective-permute-start(bf16[64,2560]{1,0:T(8,128)(2,1)S(1)} %pad_maximum_fusion), channel_id=1, source_target_pairs={{0,2},{1,3},{2,0},{3,1},{4,6},{5,7},{6,4},{7,5},{8,10},{9,11},{10,... | collective-permute-start | bytes 983048 | tf_op jit(solution)/shard_map/ppermute | solution.py:243
  15.8 4.6 %collective-permute-done.3.rest_1_ = bf16[4,32,1280]{2,1,0:T(8,128)(2,1)S(1)} collective-permute-done((bf16[4,32,1280]{2,1,0:T(8,128)(2,1)S(1)}, bf16[4,32,1280]{2,1,0:T(8,128)(2,1)S(1)}, u32[]{:S(2)}, u32[]{:S(2)}) %collective-permute-start.3) | collective-permute-done | bytes 327712 | tf_op jit(solution)/shard_map/ppermute | solution.py:243
  20.5 3.8 %collective-permute-start.6 = (bf16[10,96,128]{2,1,0:T(8,128)(2,1)S(1)}, bf16[10,96,128]{2,1,0:T(8,128)(2,1)S(1)}, u32[]{:S(2)}, u32[]{:S(2)}) collective-permute-start(bf16[10,96,128]{2,1,0:T(8,128)(2,1)S(1)} %get-tuple-element.14), channel_id=1, source_target_pairs={{0,12},{1,13},{2,14},{3,15},{4,8},{5,9},{6,10},{7,11},{8,4},{9,5},... | collective-permute-start | bytes 737288 | tf_op jit(solution)/shard_map/ppermute | solution.py:243
  24.3 1.6 %collective-permute-start.7 = (bf16[4,32,1280]{2,1,0:T(8,128)(2,1)S(1)}, bf16[4,32,1280]{2,1,0:T(8,128)(2,1)S(1)}, u32[]{:S(2)}, u32[]{:S(2)}) collective-permute-start(bf16[4,32,1280]{2,1,0:T(8,128)(2,1)S(1)} %pad_maximum_fusion.1), channel_id=1, source_target_pairs={{0,2},{1,3},{2,0},{3,1},{4,6},{5,7},{6,4},{7,5},{8,10},{9,11},{10,... | collective-permute-start | bytes 983048 | tf_op jit(solution)/shard_map/ppermute | solution.py:243
  26.0 6.7 %collective-permute-done.7.rest_2_ = bf16[4,32,1280]{2,1,0:T(8,128)(2,1)S(1)} collective-permute-done((bf16[4,32,1280]{2,1,0:T(8,128)(2,1)S(1)}, bf16[4,32,1280]{2,1,0:T(8,128)(2,1)S(1)}, u32[]{:S(2)}, u32[]{:S(2)}) %collective-permute-start.7) | collective-permute-done | bytes 327712 | tf_op jit(solution)/shard_map/ppermute | solution.py:243
  32.7 0.8 %pad_maximum_fusion.2 = bf16[4,32,1280]{2,1,0:T(8,128)(2,1)} fusion(bf16[1,32,1280]{2,1,0:T(8,128)(2,1)S(1)} %get-tuple-element.35, bf16[1,32,1280]{2,1,0:T(8,128)(2,1)S(1)} %get-tuple-element.34, bf16[1,32,1280]{2,1,0:T(8,128)(2,1)S(1)} %slice.39, bf16[1,32,1280]{2,1,0:T(8,128)(2,1)S(1)} %slice-done), kind=kLoop, calls=%fused_computation.2 | loop fusion | flops 491520 | bytes 655360 | tf_op jit(solution)/shard_map/concatenate | solution.py:230
  33.6 1.3 %collective-permute-done.4.rest_1_ = bf16[10,96,128]{2,1,0:T(8,128)(2,1)S(1)} collective-permute-done((bf16[10,96,128]{2,1,0:T(8,128)(2,1)S(1)}, bf16[10,96,128]{2,1,0:T(8,128)(2,1)S(1)}, u32[]{:S(2)}, u32[]{:S(2)}) %collective-permute-start.4) | collective-permute-done | bytes 245792 | tf_op jit(solution)/shard_map/ppermute | solution.py:243
  34.9 0.6 stack.74.weights
  35.6 1.8 %forward.1 = (bf16[4,32,1280]{2,1,0:T(8,128)(2,1)S(1)}, bf16[4,32,1280]{2,1,0:T(8,128)(2,1)S(1)}, bf16[256,1280]{1,0:T(8,128)(2,1)S(1)}) custom-call(s32[86]{0:T(128)S(1)} %concatenate.25.starts.scalars, bf16[128,2560]{1,0:T(8,128)(2,1)S(1)} %constant_dynamic-update-slice_fusion.near, bf16[128,2560]{1,0:T(8,128)(2,1)S(1)} %collective-permute-done.2.far, ...), custom_call_target="tpu_custom_call" | custom-call | tf_op jit(solution)/shard_map/forward/pallas_call | solution.py:135
  37.5 1.4 %backward.1 = (f32[10,96,128]{2,1,0:T(8,128)S(1)}, bf16[10,96,128]{2,1,0:T(8,128)(2,1)S(1)}, bf16[10,96,128]{2,1,0:T(8,128)(2,1)S(1)}, bf16[10,96,128]{2,1,0:T(8,128)(2,1)S(1)}) custom-call(s32[86]{0:T(128)S(1)} %concatenate.25.starts.scalars, bf16[128,2560]{1,0:T(8,128)(2,1)S(1)} %constant_dynamic-update-slice_fusion.near, ...), custom_call_target="tpu_custom_call" | custom-call | tf_op jit(solution)/shard_map/backward/pallas_call | solution.py:183
  38.8 0.6 collective-permute-start.14
  39.5 1.7 %collective-permute-start.9 = (bf16[4,32,1280]{2,1,0:T(8,128)(2,1)S(1)}, bf16[4,32,1280]{2,1,0:T(8,128)(2,1)S(1)}, u32[]{:S(2)}, u32[]{:S(2)}) collective-permute-start(bf16[4,32,1280]{2,1,0:T(8,128)(2,1)S(1)} %get-tuple-element.20), channel_id=1, source_target_pairs={{0,4},{1,5},{2,6},{3,7},{4,0},{5,1},{6,2},{7,3},{8,12},{9,13},{10,... | collective-permute-start | bytes 983048 | tf_op jit(solution)/shard_map/ppermute | solution.py:243
  41.1 13.1 %collective-permute-done.9.rest_1_ = bf16[4,32,1280]{2,1,0:T(8,128)(2,1)S(1)} collective-permute-done((bf16[4,32,1280]{2,1,0:T(8,128)(2,1)S(1)}, bf16[4,32,1280]{2,1,0:T(8,128)(2,1)S(1)}, u32[]{:S(2)}, u32[]{:S(2)}) %collective-permute-start.9) | collective-permute-done | bytes 327712 | tf_op jit(solution)/shard_map/ppermute | solution.py:243
  54.2 1.8 %collective-permute-start.10 = (bf16[2,32,1280]{2,1,0:T(8,128)(2,1)S(1)}, bf16[2,32,1280]{2,1,0:T(8,128)(2,1)S(1)}, u32[]{:S(2)}, u32[]{:S(2)}) collective-permute-start(bf16[2,32,1280]{2,1,0:T(8,128)(2,1)S(1)} %pad_maximum_fusion.3), channel_id=1, source_target_pairs={{0,2},{1,3},{2,0},{3,1},{4,6},{5,7},{6,4},{7,5},{8,10},{9,11},{10,... | collective-permute-start | bytes 491528 | tf_op jit(solution)/shard_map/ppermute | solution.py:243
  56.1 0.4 collective-permute-start.13
  56.5 3.1 %collective-permute-start.15 = (bf16[10,96,128]{2,1,0:T(8,128)(2,1)S(1)}, bf16[10,96,128]{2,1,0:T(8,128)(2,1)S(1)}, u32[]{:S(2)}, u32[]{:S(2)}) collective-permute-start(bf16[10,96,128]{2,1,0:T(8,128)(2,1)S(1)} %get-tuple-element.25), channel_id=1, source_target_pairs={{0,12},{1,13},{2,14},{3,15},{4,8},{5,9},{6,10},{7,11},{8,4},{9,5},... | collective-permute-start | bytes 737288 | tf_op jit(solution)/shard_map/ppermute | solution.py:243
  59.6 0.7 pad_maximum_fusion.5
  60.3 0.1 stack.66.starts
  60.4 6.5 %collective-permute-done.12.rest_4_ = bf16[2,32,1280]{2,1,0:T(8,128)(2,1)S(1)} collective-permute-done((bf16[2,32,1280]{2,1,0:T(8,128)(2,1)}, bf16[2,32,1280]{2,1,0:T(8,128)(2,1)S(1)}, u32[]{:S(2)}, u32[]{:S(2)}) %collective-permute-start.12) | collective-permute-done | bytes 163872 | tf_op jit(solution)/shard_map/ppermute | solution.py:243
  67.0 1.4 %join.1 = bf16[32,10240]{1,0:T(8,128)(2,1)} custom-call(s32[8]{0:T(128)S(1)} %stack.66.starts, bf16[4,32,1280]{2,1,0:T(8,128)(2,1)S(1)} %get-tuple-element.16.rest_0_, bf16[4,32,1280]{2,1,0:T(8,128)(2,1)S(1)} %collective-permute-done.9.rest_1_, bf16[2,32,1280]{2,1,0:T(8,128)(2,1)S(1)} %collective-permute-done.10.rest_2_, ...), custom_call_target="tpu_custom_call" | custom-call | tf_op jit(solution)/shard_map/join/pallas_call | solution.py:87
  68.4 2.7 %collective-permute-done.15.rest_3_ = bf16[10,96,128]{2,1,0:T(8,128)(2,1)S(1)} collective-permute-done((bf16[10,96,128]{2,1,0:T(8,128)(2,1)S(1)}, bf16[10,96,128]{2,1,0:T(8,128)(2,1)S(1)}, u32[]{:S(2)}, u32[]{:S(2)}) %collective-permute-start.15) | collective-permute-done | bytes 245792 | tf_op jit(solution)/shard_map/ppermute | solution.py:243
  71.2 1.1 %sum.1 = f32[2,10,96,128]{3,2,1,0:T(8,128)} custom-call(s32[1]{0:T(128)} %bitcast.15.half, f32[10,96,128]{2,1,0:T(8,128)S(1)} %get-tuple-element.22.rest_0_, bf16[10,96,128]{2,1,0:T(8,128)(2,1)S(1)} %collective-permute-done.13.rest_1_, bf16[10,96,128]{2,1,0:T(8,128)(2,1)S(1)} %collective-permute-done.14.rest_2_, ...), custom_call_target="tpu_custom_call" | custom-call | tf_op jit(solution)/shard_map/sum/pallas_call | solution.py:211
  (45 shorter events, 0.7 us)
Async XLA Ops:
  0.6 11.9 %collective-permute-start = (bf16[32,2560]{1,0:T(8,128)(2,1)}, bf16[32,2560]{1,0:T(8,128)(2,1)S(1)}, u32[]{:S(2)}, u32[]{:S(2)}) collective-permute-start(bf16[32,2560]{1,0:T(8,128)(2,1)} %param.5), channel_id=1, source_target_pairs={{0,4},{1,5},{2,6},{3,7},{4,0},{5,1},{6,2},{7,3},{8,12},{9,13},{10,... | collective-permute-start | bytes 491528 | tf_op jit(solution)/shard_map/ppermute | solution.py:243
  3.8 1.7 %copy-start.3 = (bf16[96,20,128]{2,0,1:T(8,128)(2,1)S(1)}, bf16[96,20,128]{2,0,1:T(8,128)(2,1)}, u32[]{:S(2)}) copy-start(bf16[96,20,128]{2,0,1:T(8,128)(2,1)} %param.6) | copy-start | bytes 1474564
  5.4 15.0 %collective-permute-start.3 = (bf16[4,32,1280]{2,1,0:T(8,128)(2,1)S(1)}, bf16[4,32,1280]{2,1,0:T(8,128)(2,1)S(1)}, u32[]{:S(2)}, u32[]{:S(2)}) collective-permute-start(bf16[4,32,1280]{2,1,0:T(8,128)(2,1)S(1)} %cut.2), channel_id=1, source_target_pairs={{0,4},{1,5},{2,6},{3,7},{4,0},{5,1},{6,2},{7,3},{8,12},{9,13},{10,... | collective-permute-start | bytes 983048 | tf_op jit(solution)/shard_map/ppermute | solution.py:243
  5.5 3.1 %copy-start.2 = (bf16[32,2560]{1,0:T(8,128)(2,1)S(1)}, bf16[32,2560]{1,0:T(8,128)(2,1)}, u32[]{:S(2)}) copy-start(bf16[32,2560]{1,0:T(8,128)(2,1)} %param.5) | copy-start | bytes 491524
  5.6 28.0 %collective-permute-start.5 = (bf16[10,96,128]{2,1,0:T(8,128)(2,1)S(1)}, bf16[10,96,128]{2,1,0:T(8,128)(2,1)S(1)}, u32[]{:S(2)}, u32[]{:S(2)}) collective-permute-start(bf16[10,96,128]{2,1,0:T(8,128)(2,1)S(1)} %get-tuple-element.27.rest_0_), channel_id=1, source_target_pairs={{0,8},{1,9},{2,10},{3,11},{4,12},{5,13},{6,14},{7,15},{8,0},{9,1},... | collective-permute-start | bytes 737288 | tf_op jit(solution)/shard_map/ppermute | solution.py:243
  8.6 0.7 copy-start.4
  9.5 0.7 copy-start.5
  11.8 0.7 %copy-start = (bf16[4,32,1280]{2,1,0:T(8,128)(2,1)}, bf16[4,32,1280]{2,1,0:T(8,128)(2,1)S(1)}, u32[]{:S(2)}) copy-start(bf16[4,32,1280]{2,1,0:T(8,128)(2,1)S(1)} %cut.3.rest_0_) | copy-start | bytes 983044
  12.6 13.3 %collective-permute-start.1 = (bf16[64,2560]{1,0:T(8,128)(2,1)S(1)}, bf16[64,2560]{1,0:T(8,128)(2,1)S(1)}, u32[]{:S(2)}, u32[]{:S(2)}) collective-permute-start(bf16[64,2560]{1,0:T(8,128)(2,1)S(1)} %pad_maximum_fusion), channel_id=1, source_target_pairs={{0,2},{1,3},{2,0},{3,1},{4,6},{5,7},{6,4},{7,5},{8,10},{9,11},{10,... | collective-permute-start | bytes 983048 | tf_op jit(solution)/shard_map/ppermute | solution.py:243
  20.4 3.9 %slice-start.1 = ((bf16[4,32,1280]{2,1,0:T(8,128)(2,1)}), bf16[2,32,1280]{2,1,0:T(8,128)(2,1)S(1)}, s32[]{:S(2)}) async-start(bf16[4,32,1280]{2,1,0:T(8,128)(2,1)} %copy-done), calls=%async_computation.1 | async-start | bytes 327680 | tf_op jit(solution)/shard_map/slice | solution.py:229
  20.5 13.1 %collective-permute-start.6 = (bf16[10,96,128]{2,1,0:T(8,128)(2,1)S(1)}, bf16[10,96,128]{2,1,0:T(8,128)(2,1)S(1)}, u32[]{:S(2)}, u32[]{:S(2)}) collective-permute-start(bf16[10,96,128]{2,1,0:T(8,128)(2,1)S(1)} %get-tuple-element.14), channel_id=1, source_target_pairs={{0,12},{1,13},{2,14},{3,15},{4,8},{5,9},{6,10},{7,11},{8,4},{9,5},... | collective-permute-start | bytes 737288 | tf_op jit(solution)/shard_map/ppermute | solution.py:243
  24.3 10.6 %collective-permute-start.4 = (bf16[10,96,128]{2,1,0:T(8,128)(2,1)S(1)}, bf16[10,96,128]{2,1,0:T(8,128)(2,1)S(1)}, u32[]{:S(2)}, u32[]{:S(2)}) collective-permute-start(bf16[10,96,128]{2,1,0:T(8,128)(2,1)S(1)} %get-tuple-element.14), channel_id=1, source_target_pairs={{0,4},{1,5},{2,6},{3,7},{4,0},{5,1},{6,2},{7,3},{8,12},{9,13},{10,... | collective-permute-start | bytes 737288 | tf_op jit(solution)/shard_map/ppermute | solution.py:243
  24.3 8.4 %collective-permute-start.7 = (bf16[4,32,1280]{2,1,0:T(8,128)(2,1)S(1)}, bf16[4,32,1280]{2,1,0:T(8,128)(2,1)S(1)}, u32[]{:S(2)}, u32[]{:S(2)}) collective-permute-start(bf16[4,32,1280]{2,1,0:T(8,128)(2,1)S(1)} %pad_maximum_fusion.1), channel_id=1, source_target_pairs={{0,2},{1,3},{2,0},{3,1},{4,6},{5,7},{6,4},{7,5},{8,10},{9,11},{10,... | collective-permute-start | bytes 983048 | tf_op jit(solution)/shard_map/ppermute | solution.py:243
  25.9 6.8 %slice-start = ((bf16[4,32,1280]{2,1,0:T(8,128)(2,1)}), bf16[1,32,1280]{2,1,0:T(8,128)(2,1)S(1)}, s32[]{:S(2)}) async-start(bf16[4,32,1280]{2,1,0:T(8,128)(2,1)} %copy-done), calls=%async_computation | async-start | bytes 163840 | tf_op jit(solution)/shard_map/slice | solution.py:229
  25.9 9.7 %collective-permute-start.2 = (bf16[128,2560]{1,0:T(8,128)(2,1)S(1)}, bf16[128,2560]{1,0:T(8,128)(2,1)S(1)}, u32[]{:S(2)}, u32[]{:S(2)}) collective-permute-start(bf16[128,2560]{1,0:T(8,128)(2,1)S(1)} %constant_dynamic-update-slice_fusion.near), channel_id=1, source_target_pairs={{0,1},{1,0},{2,3},{3,2},{4,5},{5,4},{6,7},{7,6},{8,9},{9,8},{10,11... | collective-permute-start | bytes 1966088 | tf_op jit(solution)/shard_map/ppermute | solution.py:243
  33.5 2.0 %collective-permute-start.8 = (bf16[4,32,1280]{2,1,0:T(8,128)(2,1)}, bf16[4,32,1280]{2,1,0:T(8,128)(2,1)S(1)}, u32[]{:S(2)}, u32[]{:S(2)}) collective-permute-start(bf16[4,32,1280]{2,1,0:T(8,128)(2,1)} %pad_maximum_fusion.2), channel_id=1, source_target_pairs={{0,1},{1,0},{2,3},{3,2},{4,5},{5,4},{6,7},{7,6},{8,9},{9,8},{10,11... | collective-permute-start | bytes 983048 | tf_op jit(solution)/shard_map/ppermute | solution.py:243
  33.6 2.0 %copy-start.1 = (bf16[4,32,1280]{2,1,0:T(8,128)(2,1)S(1)}, bf16[4,32,1280]{2,1,0:T(8,128)(2,1)}, u32[]{:S(2)}) copy-start(bf16[4,32,1280]{2,1,0:T(8,128)(2,1)} %copy-done) | copy-start | bytes 983044
  38.8 29.6 %collective-permute-start.14 = (bf16[10,96,128]{2,1,0:T(8,128)(2,1)S(1)}, bf16[10,96,128]{2,1,0:T(8,128)(2,1)S(1)}, u32[]{:S(2)}, u32[]{:S(2)}) collective-permute-start(bf16[10,96,128]{2,1,0:T(8,128)(2,1)S(1)} %get-tuple-element.24), channel_id=1, source_target_pairs={{0,8},{1,9},{2,10},{3,11},{4,12},{5,13},{6,14},{7,15},{8,0},{9,1},... | collective-permute-start | bytes 737288 | tf_op jit(solution)/shard_map/ppermute | solution.py:243
  39.5 14.7 %collective-permute-start.9 = (bf16[4,32,1280]{2,1,0:T(8,128)(2,1)S(1)}, bf16[4,32,1280]{2,1,0:T(8,128)(2,1)S(1)}, u32[]{:S(2)}, u32[]{:S(2)}) collective-permute-start(bf16[4,32,1280]{2,1,0:T(8,128)(2,1)S(1)} %get-tuple-element.20), channel_id=1, source_target_pairs={{0,4},{1,5},{2,6},{3,7},{4,0},{5,1},{6,2},{7,3},{8,12},{9,13},{10,... | collective-permute-start | bytes 983048 | tf_op jit(solution)/shard_map/ppermute | solution.py:243
  54.2 6.1 %collective-permute-start.10 = (bf16[2,32,1280]{2,1,0:T(8,128)(2,1)S(1)}, bf16[2,32,1280]{2,1,0:T(8,128)(2,1)S(1)}, u32[]{:S(2)}, u32[]{:S(2)}) collective-permute-start(bf16[2,32,1280]{2,1,0:T(8,128)(2,1)S(1)} %pad_maximum_fusion.3), channel_id=1, source_target_pairs={{0,2},{1,3},{2,0},{3,1},{4,6},{5,7},{6,4},{7,5},{8,10},{9,11},{10,... | collective-permute-start | bytes 491528 | tf_op jit(solution)/shard_map/ppermute | solution.py:243
  56.1 4.4 %collective-permute-start.11 = (bf16[2,32,1280]{2,1,0:T(8,128)(2,1)S(1)}, bf16[2,32,1280]{2,1,0:T(8,128)(2,1)S(1)}, u32[]{:S(2)}, u32[]{:S(2)}) collective-permute-start(bf16[2,32,1280]{2,1,0:T(8,128)(2,1)S(1)} %pad_maximum_fusion.4), channel_id=1, source_target_pairs={{0,1},{1,0},{2,3},{3,2},{4,5},{5,4},{6,7},{7,6},{8,9},{9,8},{10,11... | collective-permute-start | bytes 491528 | tf_op jit(solution)/shard_map/ppermute | solution.py:243
  56.1 12.3 %collective-permute-start.13 = (bf16[10,96,128]{2,1,0:T(8,128)(2,1)S(1)}, bf16[10,96,128]{2,1,0:T(8,128)(2,1)S(1)}, u32[]{:S(2)}, u32[]{:S(2)}) collective-permute-start(bf16[10,96,128]{2,1,0:T(8,128)(2,1)S(1)} %get-tuple-element.23), channel_id=1, source_target_pairs={{0,4},{1,5},{2,6},{3,7},{4,0},{5,1},{6,2},{7,3},{8,12},{9,13},{10,... | collective-permute-start | bytes 737288 | tf_op jit(solution)/shard_map/ppermute | solution.py:243
  56.5 14.6 %collective-permute-start.15 = (bf16[10,96,128]{2,1,0:T(8,128)(2,1)S(1)}, bf16[10,96,128]{2,1,0:T(8,128)(2,1)S(1)}, u32[]{:S(2)}, u32[]{:S(2)}) collective-permute-start(bf16[10,96,128]{2,1,0:T(8,128)(2,1)S(1)} %get-tuple-element.25), channel_id=1, source_target_pairs={{0,12},{1,13},{2,14},{3,15},{4,8},{5,9},{6,10},{7,11},{8,4},{9,5},... | collective-permute-start | bytes 737288 | tf_op jit(solution)/shard_map/ppermute | solution.py:243
  60.3 6.6 %collective-permute-start.12 = (bf16[2,32,1280]{2,1,0:T(8,128)(2,1)}, bf16[2,32,1280]{2,1,0:T(8,128)(2,1)S(1)}, u32[]{:S(2)}, u32[]{:S(2)}) collective-permute-start(bf16[2,32,1280]{2,1,0:T(8,128)(2,1)} %pad_maximum_fusion.5), channel_id=1, source_target_pairs={{0,3},{1,2},{2,1},{3,0},{4,7},{5,6},{6,5},{7,4},{8,11},{9,10},{10,... | collective-permute-start | bytes 491528 | tf_op jit(solution)/shard_map/ppermute | solution.py:243

commit v14 on v13

--- a/solution.py
+++ b/solution.py
@@ -141,6 +141,23 @@
         compiler_params=room(10),
         name="forward",
     )(scalars, near, far, weights, backs)
+
+
+def pack_kernel(home, away, *outs):
+    for i, out in enumerate(outs):
+        out[0] = home[i]
+        out[1] = away[i]
+
+
+def pack_call(home, away):
+    return pl.pallas_call(
+        pack_kernel,
+        out_shape=[jax.ShapeDtypeStruct((PAIR,) + home.shape[1:], home.dtype)] * home.shape[0],
+        in_specs=[RESIDENT] * PAIR,
+        out_specs=[RESIDENT] * home.shape[0],
+        compiler_params=room(6),
+        name="pack",
+    )(home, away)
 
 
 def stack_kernel(scalars, *rest):
@@ -243,24 +260,14 @@
         return lax.ppermute(value, ("fsdp", "tensor"), pairs)
 
     def exchange(arrays, steps):
-        groups, origins = [[(a, b) for b in range(tensor)] for a in range(PAIR)], [(a, 0) for a in range(PAIR)]
+        groups, origins = [[(a, b) for b in range(tensor)] for a in range(PAIR)], [0]
         for bit in steps:
             count = len(groups[0]) // 2
             arrays = arrays + [swap(take(arrays, [ref for group in groups for ref in group[count:]]), 0, bit)]
             new = [[(len(arrays) - 1, i * count + j) for j in range(count)] for i in range(len(groups))]
             groups = [group[:count] for group in groups] + new
-            origins = origins + [(a, b ^ bit) for a, b in origins]
+            origins = origins + [b ^ bit for b in origins]
         return arrays, [group[0] for group in groups], origins
-
-    def spread(arrays, order):
-        refs, origins = [(a, order.index(0)) for a in range(PAIR)], [(a, 0) for a in range(PAIR)]
-        for b in order:
-            if b:
-                i = order.index(b)
-                refs = refs + [(len(arrays), a) for a in range(PAIR)]
-                arrays = arrays + [swap(take(arrays, [(a, i) for a in range(PAIR)]), 0, b)]
-                origins = origins + [(a, b) for a in range(PAIR)]
-        return arrays, refs, origins
 
     def first_tiles(steps):
         return jnp.stack([(t ^ b) * stripes + (half ^ a) * share for a, b in steps]).astype(jnp.int32)
@@ -268,12 +275,14 @@
     direct = whole_tiles and fsdp <= DIRECT
     leave = cut_call(first_tiles([(1, b) for b in range(tensor)]), cotangent, tensor)
     arrived = swap(leave, 1, 0)
+    near = swap(tokens, 1, 0)
     by_stripe = jnp.transpose(tile_weights, (1, 0, 2))
     if direct:
         same = lax.dynamic_slice_in_dim(by_stripe, half * share, share, 0)
         other = lax.dynamic_slice_in_dim(by_stripe, (1 - half) * share, share, 0)
+        middle, near = lax.optimization_barrier((other, near))
         late, arrived = lax.optimization_barrier((other, arrived))
-        pieces = [same] + [swap(late if p % PAIR else same, p, 0) for p in range(1, fsdp)]
+        pieces = [same] + [swap((late if p == 1 else middle) if p % PAIR else same, p, 0) for p in range(1, fsdp)]
         weights = stack_call(jnp.stack([z ^ p for p in range(fsdp)]).astype(jnp.int32), pieces)
     else:
         outgoing = jnp.tile(by_stripe.reshape(PAIR, share, size, TILE), (fsdp // PAIR, 1, 1, 1))
@@ -284,7 +293,7 @@
     ends = jnp.stack([half * share, z if direct else z * 0]).astype(jnp.int32)
     scalars = jnp.concatenate([first_tiles([(0, b) for b in range(tensor)]), tile_list.reshape(-1), tile_counts, ends])
     stay = cut_call(scalars, cotangent, tensor)
-    near = jnp.concatenate([tokens, swap(tokens, 1, 0)], axis=0)
+    near = jnp.concatenate([tokens, near], axis=0)
     for bit in bits:
         far = swap(near, 0, bit)
         if bit > 1:
@@ -298,15 +307,19 @@
     grads = list(backward_call(sizes, scalars, near, far, slopes, fsdp if direct else 1))
     if direct:
         grads[1::PAIR], back_home = lax.optimization_barrier((grads[1::PAIR], back_home))
-        total = sum_call(half.reshape(1).astype(jnp.int32), [grads[0]] + [swap(grads[p], p, 0) for p in range(1, fsdp)])
+        across = {p: swap(grads[p], p, 0) for p in range(PAIR, fsdp, PAIR)}
+        across, back_home = lax.optimization_barrier((across, back_home))
+        total = sum_call(half.reshape(1).astype(jnp.int32), [grads[0]] + [across[p] if p in across else swap(grads[p], p, 0) for p in range(1, fsdp)])
     else:
         split = grads[0].reshape(share, fsdp, size, TILE).transpose(1, 0, 2, 3)
         arrived = lax.all_to_all(split.astype(jnp.bfloat16), "fsdp", split_axis=0, concat_axis=0, tiled=True)
         here = (jnp.arange(fsdp) == z)[:, None, None, None]
         total = jnp.where(here, split, arrived.astype(jnp.float32))
         total = jnp.sum(total.reshape(fsdp // PAIR, PAIR, share, size, TILE), axis=0)
-    arrays, refs, steps = spread([home, back_home], [b for a, b in origins if a == 0])
-    activations = join_call(first_tiles(steps), arrays, refs)
+    packed = list(pack_call(home, back_home))
+    arrays = packed[:1] + [swap(packed[i], 0, b) for i, b in enumerate(origins) if i]
+    refs = [(i, a) for i in range(tensor) for a in range(PAIR)]
+    activations = join_call(first_tiles([(a, b) for b in origins for a in range(PAIR)]), arrays, refs)
     return activations, total.reshape(stripes, size, TILE).transpose(1, 0, 2)
 
 

time: 72.5 us -> 65.2 us (0.90)
  waiting for transfers between devices: 35 us -> 29.7 us
  starting transfers between devices: 22.5 us -> 20.4 us
  local copies, waits for them, and re-layouts: 2.55 us -> 3.33 us
    ppermute x16, waiting for transfers between devices: 35 us -> 29.7 us  [swap(): return lax.ppermute(value, ('fsdp', 'tensor'), pairs)]
    ppermute x16, starting transfers between devices: 22.5 us -> 20.4 us  [swap(): return lax.ppermute(value, ('fsdp', 'tensor'), pairs)]
    slice x9 -> x7, local copies, waits for them, and re-layouts: 0.07 us -> 0.85 us  [take(): arrays[a][low:high]]
    concatenate x5 -> x2, other arithmetic: 1.52 us -> 0.8 us  [take(): return pieces[0] if len(pieces) == 1 else jnp.concatenate(pieces, axis=0)]
  transfers between devices with their start and end apart: 16 -> 16, of which waited for: 6 -> 8; matrix products, arithmetic and copies ran while one was open for 3% -> 2% of each run, Pallas kernels for 7% -> 10%
where the time goes in v14:
time: 65.2 us; the launch traced here: 65 us
  waiting for transfers between devices  29.7 us (46%)
  starting transfers between devices  20.4 us (31%)
  Pallas kernels  9.68 us (15%)
  local copies, waits for them, and re-layouts  3.33 us (5%)
  other arithmetic  0.97 us (1%)
  between operations  0.84 us (1%)
    ppermute x16, waiting for transfers between devices, swap(): return lax.ppermute(value, ('fsdp', 'tensor'), pairs)  29.7 us
    ppermute x16, starting transfers between devices, swap(): return lax.ppermute(value, ('fsdp', 'tensor'), pairs)  20.4 us
    pallas_call x2, Pallas kernels, cut_call(): pl.pallas_call(cut_kernel, out_shape=jax.ShapeDtypeStruct((count, rows, w...  3.18 us
    unnamed x15, local copies, waits for them, and re-layouts  2.17 us
    pallas_call x1, Pallas kernels, forward_call(): pl.pallas_call(functools.partial(forward_kernel, sizes), out_shape=[jax.S...  1.86 us
    pallas_call x1, Pallas kernels, join_call(): pl.pallas_call(functools.partial(join_kernel, refs), out_shape=jax.ShapeD...  1.44 us
    pallas_call x1, Pallas kernels, backward_call(): pl.pallas_call(functools.partial(backward_kernel, sizes), out_shape=[jax....  1.37 us
  transfers between devices with their start and end apart: 16, of which 8 were waited for; matrix products, arithmetic and copies ran while one was open for 2% of the time, Pallas kernels for 10%

profile of v14, /device:TPU:0, one launch (start us, length us, event | category | flops | bytes accessed | tf_op | source)
XLA Modules:
  0.0 65.0 jit_solution(1998437433919568988)
XLA Ops:
  0.6 3.1 %collective-permute-start = (bf16[32,2560]{1,0:T(8,128)(2,1)}, bf16[32,2560]{1,0:T(8,128)(2,1)S(1)}, u32[]{:S(2)}, u32[]{:S(2)}) collective-permute-start(bf16[32,2560]{1,0:T(8,128)(2,1)} %param.5), channel_id=1, source_target_pairs={{0,4},{1,5},{2,6},{3,7},{4,0},{5,1},{6,2},{7,3},{8,12},{9,13},{10,... | collective-permute-start | bytes 491528 | tf_op jit(solution)/shard_map/ppermute | solution.py:260
  3.8 1.6 %cut.2 = bf16[4,32,1280]{2,1,0:T(8,128)(2,1)S(1)} custom-call(s32[4]{0:T(128)S(1)} %pad_add_fusion.1.starts, bf16[32,10240]{1,0:T(8,128)(2,1)} %whole.3), custom_call_target="tpu_custom_call" | custom-call | tf_op jit(solution)/shard_map/cut/pallas_call | solution.py:50
  5.4 0.1 collective-permute-start.3
  5.6 3.0 %collective-permute-start.5 = (bf16[10,96,128]{2,1,0:T(8,128)(2,1)S(1)}, bf16[10,96,128]{2,1,0:T(8,128)(2,1)S(1)}, u32[]{:S(2)}, u32[]{:S(2)}) collective-permute-start(bf16[10,96,128]{2,1,0:T(8,128)(2,1)S(1)} %get-tuple-element.42.rest_0_), channel_id=1, source_target_pairs={{0,8},{1,9},{2,10},{3,11},{4,12},{5,13},{6,14},{7,15},{8,0},{9,1},... | collective-permute-start | bytes 737288 | tf_op jit(solution)/shard_map/ppermute | solution.py:260
  8.7 0.7 %copy-done.4 = s32[20,3]{0,1:T(4,128)S(1)} copy-done((s32[20,3]{0,1:T(4,128)S(1)}, s32[20,3]{0,1:T(4,128)}, u32[]{:S(2)}) %copy-start.4) | copy-done | bytes 264
  9.3 0.1 copy.8
  9.4 0.1 reshape.13
  9.5 0.6 copy-done.5
  10.2 1.6 %cut.3.rest_0_ = bf16[4,32,1280]{2,1,0:T(8,128)(2,1)S(1)} custom-call(s32[86]{0:T(128)S(1)} %concatenate.16.starts.scalars, bf16[32,10240]{1,0:T(8,128)(2,1)} %whole.3), custom_call_target="tpu_custom_call" | custom-call | tf_op jit(solution)/shard_map/cut/pallas_call | solution.py:50
  11.9 0.7 %copy-done = bf16[4,32,1280]{2,1,0:T(8,128)(2,1)} copy-done((bf16[4,32,1280]{2,1,0:T(8,128)(2,1)}, bf16[4,32,1280]{2,1,0:T(8,128)(2,1)S(1)}, u32[]{:S(2)}) %copy-start) | copy-done | bytes 327704
  12.6 5.0 %collective-permute-start.6 = (bf16[10,96,128]{2,1,0:T(8,128)(2,1)S(1)}, bf16[10,96,128]{2,1,0:T(8,128)(2,1)S(1)}, u32[]{:S(2)}, u32[]{:S(2)}) collective-permute-start(bf16[10,96,128]{2,1,0:T(8,128)(2,1)S(1)} %get-tuple-element.24), channel_id=1, source_target_pairs={{0,12},{1,13},{2,14},{3,15},{4,8},{5,9},{6,10},{7,11},{8,4},{9,5},... | collective-permute-start | bytes 737288 | tf_op jit(solution)/shard_map/ppermute | solution.py:260
  17.6 1.6 %collective-permute-start.1 = (bf16[64,2560]{1,0:T(8,128)(2,1)S(1)}, bf16[64,2560]{1,0:T(8,128)(2,1)S(1)}, u32[]{:S(2)}, u32[]{:S(2)}) collective-permute-start(bf16[64,2560]{1,0:T(8,128)(2,1)S(1)} %pad_maximum_fusion), channel_id=1, source_target_pairs={{0,2},{1,3},{2,0},{3,1},{4,6},{5,7},{6,4},{7,5},{8,10},{9,11},{10,... | collective-permute-start | bytes 983048 | tf_op jit(solution)/shard_map/ppermute | solution.py:260
  19.2 1.2 %collective-permute-done.3.rest_1_ = bf16[4,32,1280]{2,1,0:T(8,128)(2,1)S(1)} collective-permute-done((bf16[4,32,1280]{2,1,0:T(8,128)(2,1)S(1)}, bf16[4,32,1280]{2,1,0:T(8,128)(2,1)S(1)}, u32[]{:S(2)}, u32[]{:S(2)}) %collective-permute-start.3) | collective-permute-done | bytes 327712 | tf_op jit(solution)/shard_map/ppermute | solution.py:260
  20.5 0.8 %slice-done.1 = bf16[2,32,1280]{2,1,0:T(8,128)(2,1)S(1)} async-done(((bf16[4,32,1280]{2,1,0:T(8,128)(2,1)}), bf16[2,32,1280]{2,1,0:T(8,128)(2,1)S(1)}, s32[]{:S(2)}) %slice-start.1) | async-done | bytes 163864 | tf_op jit(solution)/shard_map/slice | solution.py:246
  21.4 1.7 %collective-permute-start.7 = (bf16[4,32,1280]{2,1,0:T(8,128)(2,1)S(1)}, bf16[4,32,1280]{2,1,0:T(8,128)(2,1)S(1)}, u32[]{:S(2)}, u32[]{:S(2)}) collective-permute-start(bf16[4,32,1280]{2,1,0:T(8,128)(2,1)S(1)} %pad_maximum_fusion.1), channel_id=1, source_target_pairs={{0,2},{1,3},{2,0},{3,1},{4,6},{5,7},{6,4},{7,5},{8,10},{9,11},{10,... | collective-permute-start | bytes 983048 | tf_op jit(solution)/shard_map/ppermute | solution.py:260
  23.1 2.9 %collective-permute-done.1 = bf16[64,2560]{1,0:T(8,128)(2,1)S(1)} collective-permute-done((bf16[64,2560]{1,0:T(8,128)(2,1)S(1)}, bf16[64,2560]{1,0:T(8,128)(2,1)S(1)}, u32[]{:S(2)}, u32[]{:S(2)}) %collective-permute-start.1) | collective-permute-done | bytes 327712 | tf_op jit(solution)/shard_map/ppermute | solution.py:260
  26.2 5.6 %collective-permute-done.7.rest_2_ = bf16[4,32,1280]{2,1,0:T(8,128)(2,1)S(1)} collective-permute-done((bf16[4,32,1280]{2,1,0:T(8,128)(2,1)S(1)}, bf16[4,32,1280]{2,1,0:T(8,128)(2,1)S(1)}, u32[]{:S(2)}, u32[]{:S(2)}) %collective-permute-start.7) | collective-permute-done | bytes 327712 | tf_op jit(solution)/shard_map/ppermute | solution.py:260
  31.8 0.8 %pad_maximum_fusion.2 = bf16[4,32,1280]{2,1,0:T(8,128)(2,1)} fusion(bf16[1,32,1280]{2,1,0:T(8,128)(2,1)S(1)} %get-tuple-element.45, bf16[1,32,1280]{2,1,0:T(8,128)(2,1)S(1)} %get-tuple-element.44, bf16[1,32,1280]{2,1,0:T(8,128)(2,1)S(1)} %slice.21, bf16[1,32,1280]{2,1,0:T(8,128)(2,1)S(1)} %slice-done), kind=kLoop, calls=%fused_computation.2 | loop fusion | flops 491520 | bytes 655360 | tf_op jit(solution)/shard_map/concatenate | solution.py:247
  32.7 0.6 stack.74.weights
  33.3 1.1 %collective-permute-done.8.rest_3_ = bf16[4,32,1280]{2,1,0:T(8,128)(2,1)S(1)} collective-permute-done((bf16[4,32,1280]{2,1,0:T(8,128)(2,1)}, bf16[4,32,1280]{2,1,0:T(8,128)(2,1)S(1)}, u32[]{:S(2)}, u32[]{:S(2)}) %collective-permute-start.8) | collective-permute-done | bytes 327712 | tf_op jit(solution)/shard_map/ppermute | solution.py:260
  34.5 1.9 %forward.1 = (bf16[4,32,1280]{2,1,0:T(8,128)(2,1)S(1)}, bf16[4,32,1280]{2,1,0:T(8,128)(2,1)S(1)}, bf16[256,1280]{1,0:T(8,128)(2,1)S(1)}) custom-call(s32[86]{0:T(128)S(1)} %concatenate.16.starts.scalars, bf16[128,2560]{1,0:T(8,128)(2,1)S(1)} %constant_dynamic-update-slice_fusion.near, bf16[128,2560]{1,0:T(8,128)(2,1)S(1)} %collective-permute-done.2.far, ...), custom_call_target="tpu_custom_call" | custom-call | tf_op jit(solution)/shard_map/forward/pallas_call | solution.py:135
  36.4 1.4 %backward.1 = (f32[10,96,128]{2,1,0:T(8,128)S(1)}, bf16[10,96,128]{2,1,0:T(8,128)(2,1)S(1)}, bf16[10,96,128]{2,1,0:T(8,128)(2,1)S(1)}, bf16[10,96,128]{2,1,0:T(8,128)(2,1)S(1)}) custom-call(s32[86]{0:T(128)S(1)} %concatenate.16.starts.scalars, bf16[128,2560]{1,0:T(8,128)(2,1)S(1)} %constant_dynamic-update-slice_fusion.near, ...), custom_call_target="tpu_custom_call" | custom-call | tf_op jit(solution)/shard_map/backward/pallas_call | solution.py:200
  37.8 2.5 %collective-permute-start.9 = (bf16[10,96,128]{2,1,0:T(8,128)(2,1)S(1)}, bf16[10,96,128]{2,1,0:T(8,128)(2,1)S(1)}, u32[]{:S(2)}, u32[]{:S(2)}) collective-permute-start(bf16[10,96,128]{2,1,0:T(8,128)(2,1)S(1)} %get-tuple-element.28), channel_id=1, source_target_pairs={{0,8},{1,9},{2,10},{3,11},{4,12},{5,13},{6,14},{7,15},{8,0},{9,1},... | collective-permute-start | bytes 737288 | tf_op jit(solution)/shard_map/ppermute | solution.py:260
  40.4 11.1 %collective-permute-done.10.away = bf16[4,32,1280]{2,1,0:T(8,128)(2,1)S(1)} collective-permute-done((bf16[4,32,1280]{2,1,0:T(8,128)(2,1)S(1)}, bf16[4,32,1280]{2,1,0:T(8,128)(2,1)S(1)}, u32[]{:S(2)}, u32[]{:S(2)}) %collective-permute-start.10) | collective-permute-done | bytes 327712 | tf_op jit(solution)/shard_map/ppermute | solution.py:260
  51.4 0.9 %collective-permute-start.15 = (bf16[10,96,128]{2,1,0:T(8,128)(2,1)S(1)}, bf16[10,96,128]{2,1,0:T(8,128)(2,1)S(1)}, u32[]{:S(2)}, u32[]{:S(2)}) collective-permute-start(bf16[10,96,128]{2,1,0:T(8,128)(2,1)S(1)} %get-tuple-element.41), channel_id=1, source_target_pairs={{0,12},{1,13},{2,14},{3,15},{4,8},{5,9},{6,10},{7,11},{8,4},{9,5},... | collective-permute-start | bytes 737288 | tf_op jit(solution)/shard_map/ppermute | solution.py:260
  52.4 1.5 %collective-permute-start.11 = (bf16[2,32,1280]{2,1,0:T(8,128)(2,1)S(1)}, bf16[2,32,1280]{2,1,0:T(8,128)(2,1)S(1)}, u32[]{:S(2)}, u32[]{:S(2)}) collective-permute-start(bf16[2,32,1280]{2,1,0:T(8,128)(2,1)S(1)} %get-tuple-element.35), channel_id=1, source_target_pairs={{0,2},{1,3},{2,0},{3,1},{4,6},{5,7},{6,4},{7,5},{8,10},{9,11},{10,... | collective-permute-start | bytes 491528 | tf_op jit(solution)/shard_map/ppermute | solution.py:260
  54.0 0.7 %collective-permute-start.13 = (bf16[2,32,1280]{2,1,0:T(8,128)(2,1)S(1)}, bf16[2,32,1280]{2,1,0:T(8,128)(2,1)S(1)}, u32[]{:S(2)}, u32[]{:S(2)}) collective-permute-start(bf16[2,32,1280]{2,1,0:T(8,128)(2,1)S(1)} %get-tuple-element.37), channel_id=1, source_target_pairs={{0,3},{1,2},{2,1},{3,0},{4,7},{5,6},{6,5},{7,4},{8,11},{9,10},{10,... | collective-permute-start | bytes 491528 | tf_op jit(solution)/shard_map/ppermute | solution.py:260
  54.7 3.9 %collective-permute-done.11.rest_1_ = bf16[2,32,1280]{2,1,0:T(8,128)(2,1)S(1)} collective-permute-done((bf16[2,32,1280]{2,1,0:T(8,128)(2,1)S(1)}, bf16[2,32,1280]{2,1,0:T(8,128)(2,1)S(1)}, u32[]{:S(2)}, u32[]{:S(2)}) %collective-permute-start.11) | collective-permute-done | bytes 163872 | tf_op jit(solution)/shard_map/ppermute | solution.py:260
  58.6 1.8 %collective-permute-done.13.rest_3_ = bf16[2,32,1280]{2,1,0:T(8,128)(2,1)S(1)} collective-permute-done((bf16[2,32,1280]{2,1,0:T(8,128)(2,1)S(1)}, bf16[2,32,1280]{2,1,0:T(8,128)(2,1)S(1)}, u32[]{:S(2)}, u32[]{:S(2)}) %collective-permute-start.13) | collective-permute-done | bytes 163872 | tf_op jit(solution)/shard_map/ppermute | solution.py:260
  60.4 1.4 %join.1 = bf16[32,10240]{1,0:T(8,128)(2,1)} custom-call(s32[8]{0:T(128)S(1)} %stack.66.starts, bf16[2,32,1280]{2,1,0:T(8,128)(2,1)S(1)} %get-tuple-element.34.rest_0_, bf16[2,32,1280]{2,1,0:T(8,128)(2,1)S(1)} %collective-permute-done.11.rest_1_, bf16[2,32,1280]{2,1,0:T(8,128)(2,1)S(1)} %collective-permute-done.12.rest_2_, ...), custom_call_target="tpu_custom_call" | custom-call | tf_op jit(solution)/shard_map/join/pallas_call | solution.py:87
  61.9 2.0 %collective-permute-done.14.rest_1_ = bf16[10,96,128]{2,1,0:T(8,128)(2,1)S(1)} collective-permute-done((bf16[10,96,128]{2,1,0:T(8,128)(2,1)S(1)}, bf16[10,96,128]{2,1,0:T(8,128)(2,1)S(1)}, u32[]{:S(2)}, u32[]{:S(2)}) %collective-permute-start.14) | collective-permute-done | bytes 245792 | tf_op jit(solution)/shard_map/ppermute | solution.py:260
  63.9 1.1 %sum.1 = f32[2,10,96,128]{3,2,1,0:T(8,128)} custom-call(s32[1]{0:T(128)} %bitcast.15.half, f32[10,96,128]{2,1,0:T(8,128)S(1)} %get-tuple-element.38.rest_0_, bf16[10,96,128]{2,1,0:T(8,128)(2,1)S(1)} %collective-permute-done.14.rest_1_, bf16[10,96,128]{2,1,0:T(8,128)(2,1)S(1)} %collective-permute-done.9.rest_2_, ...), custom_call_target="tpu_custom_call" | custom-call | tf_op jit(solution)/shard_map/sum/pallas_call | solution.py:228
  (41 shorter events, 0.9 us)
Async XLA Ops:
  0.6 11.9 %collective-permute-start = (bf16[32,2560]{1,0:T(8,128)(2,1)}, bf16[32,2560]{1,0:T(8,128)(2,1)S(1)}, u32[]{:S(2)}, u32[]{:S(2)}) collective-permute-start(bf16[32,2560]{1,0:T(8,128)(2,1)} %param.5), channel_id=1, source_target_pairs={{0,4},{1,5},{2,6},{3,7},{4,0},{5,1},{6,2},{7,3},{8,12},{9,13},{10,... | collective-permute-start | bytes 491528 | tf_op jit(solution)/shard_map/ppermute | solution.py:260
  3.8 1.7 %copy-start.3 = (bf16[96,20,128]{2,0,1:T(8,128)(2,1)S(1)}, bf16[96,20,128]{2,0,1:T(8,128)(2,1)}, u32[]{:S(2)}) copy-start(bf16[96,20,128]{2,0,1:T(8,128)(2,1)} %param.6) | copy-start | bytes 1474564
  5.4 15.0 %collective-permute-start.3 = (bf16[4,32,1280]{2,1,0:T(8,128)(2,1)S(1)}, bf16[4,32,1280]{2,1,0:T(8,128)(2,1)S(1)}, u32[]{:S(2)}, u32[]{:S(2)}) collective-permute-start(bf16[4,32,1280]{2,1,0:T(8,128)(2,1)S(1)} %cut.2), channel_id=1, source_target_pairs={{0,4},{1,5},{2,6},{3,7},{4,0},{5,1},{6,2},{7,3},{8,12},{9,13},{10,... | collective-permute-start | bytes 983048 | tf_op jit(solution)/shard_map/ppermute | solution.py:260
  5.5 3.1 %copy-start.2 = (bf16[32,2560]{1,0:T(8,128)(2,1)S(1)}, bf16[32,2560]{1,0:T(8,128)(2,1)}, u32[]{:S(2)}) copy-start(bf16[32,2560]{1,0:T(8,128)(2,1)} %param.5) | copy-start | bytes 491524
  5.6 27.1 %collective-permute-start.5 = (bf16[10,96,128]{2,1,0:T(8,128)(2,1)S(1)}, bf16[10,96,128]{2,1,0:T(8,128)(2,1)S(1)}, u32[]{:S(2)}, u32[]{:S(2)}) collective-permute-start(bf16[10,96,128]{2,1,0:T(8,128)(2,1)S(1)} %get-tuple-element.42.rest_0_), channel_id=1, source_target_pairs={{0,8},{1,9},{2,10},{3,11},{4,12},{5,13},{6,14},{7,15},{8,0},{9,1},... | collective-permute-start | bytes 737288 | tf_op jit(solution)/shard_map/ppermute | solution.py:260
  8.6 0.7 %copy-start.4 = (s32[20,3]{0,1:T(4,128)S(1)}, s32[20,3]{0,1:T(4,128)}, u32[]{:S(2)}) copy-start(s32[20,3]{0,1:T(4,128)} %param.8) | copy-start | bytes 724
  9.5 0.7 %copy-start.5 = (s32[20]{0:T(128)S(1)}, s32[20]{0:T(128)}, u32[]{:S(2)}) copy-start(s32[20]{0:T(128)} %param.9) | copy-start | bytes 244
  11.8 0.7 %copy-start = (bf16[4,32,1280]{2,1,0:T(8,128)(2,1)}, bf16[4,32,1280]{2,1,0:T(8,128)(2,1)S(1)}, u32[]{:S(2)}) copy-start(bf16[4,32,1280]{2,1,0:T(8,128)(2,1)S(1)} %cut.3.rest_0_) | copy-start | bytes 983044
  12.6 20.1 %collective-permute-start.6 = (bf16[10,96,128]{2,1,0:T(8,128)(2,1)S(1)}, bf16[10,96,128]{2,1,0:T(8,128)(2,1)S(1)}, u32[]{:S(2)}, u32[]{:S(2)}) collective-permute-start(bf16[10,96,128]{2,1,0:T(8,128)(2,1)S(1)} %get-tuple-element.24), channel_id=1, source_target_pairs={{0,12},{1,13},{2,14},{3,15},{4,8},{5,9},{6,10},{7,11},{8,4},{9,5},... | collective-permute-start | bytes 737288 | tf_op jit(solution)/shard_map/ppermute | solution.py:260
  17.6 8.4 %collective-permute-start.1 = (bf16[64,2560]{1,0:T(8,128)(2,1)S(1)}, bf16[64,2560]{1,0:T(8,128)(2,1)S(1)}, u32[]{:S(2)}, u32[]{:S(2)}) collective-permute-start(bf16[64,2560]{1,0:T(8,128)(2,1)S(1)} %pad_maximum_fusion), channel_id=1, source_target_pairs={{0,2},{1,3},{2,0},{3,1},{4,6},{5,7},{6,4},{7,5},{8,10},{9,11},{10,... | collective-permute-start | bytes 983048 | tf_op jit(solution)/shard_map/ppermute | solution.py:260
  20.4 0.9 %slice-start.1 = ((bf16[4,32,1280]{2,1,0:T(8,128)(2,1)}), bf16[2,32,1280]{2,1,0:T(8,128)(2,1)S(1)}, s32[]{:S(2)}) async-start(bf16[4,32,1280]{2,1,0:T(8,128)(2,1)} %copy-done), calls=%async_computation.1 | async-start | bytes 327680 | tf_op jit(solution)/shard_map/slice | solution.py:246
  20.5 12.3 %collective-permute-start.4 = (bf16[10,96,128]{2,1,0:T(8,128)(2,1)S(1)}, bf16[10,96,128]{2,1,0:T(8,128)(2,1)S(1)}, u32[]{:S(2)}, u32[]{:S(2)}) collective-permute-start(bf16[10,96,128]{2,1,0:T(8,128)(2,1)S(1)} %get-tuple-element.24), channel_id=1, source_target_pairs={{0,4},{1,5},{2,6},{3,7},{4,0},{5,1},{6,2},{7,3},{8,12},{9,13},{10,... | collective-permute-start | bytes 737288 | tf_op jit(solution)/shard_map/ppermute | solution.py:260
  21.4 10.4 %collective-permute-start.7 = (bf16[4,32,1280]{2,1,0:T(8,128)(2,1)S(1)}, bf16[4,32,1280]{2,1,0:T(8,128)(2,1)S(1)}, u32[]{:S(2)}, u32[]{:S(2)}) collective-permute-start(bf16[4,32,1280]{2,1,0:T(8,128)(2,1)S(1)} %pad_maximum_fusion.1), channel_id=1, source_target_pairs={{0,2},{1,3},{2,0},{3,1},{4,6},{5,7},{6,4},{7,5},{8,10},{9,11},{10,... | collective-permute-start | bytes 983048 | tf_op jit(solution)/shard_map/ppermute | solution.py:260
  26.1 5.7 %slice-start = ((bf16[4,32,1280]{2,1,0:T(8,128)(2,1)}), bf16[1,32,1280]{2,1,0:T(8,128)(2,1)S(1)}, s32[]{:S(2)}) async-start(bf16[4,32,1280]{2,1,0:T(8,128)(2,1)} %copy-done), calls=%async_computation | async-start | bytes 163840 | tf_op jit(solution)/shard_map/slice | solution.py:246
  26.1 8.4 %collective-permute-start.2 = (bf16[128,2560]{1,0:T(8,128)(2,1)S(1)}, bf16[128,2560]{1,0:T(8,128)(2,1)S(1)}, u32[]{:S(2)}, u32[]{:S(2)}) collective-permute-start(bf16[128,2560]{1,0:T(8,128)(2,1)S(1)} %constant_dynamic-update-slice_fusion.near), channel_id=1, source_target_pairs={{0,1},{1,0},{2,3},{3,2},{4,5},{5,4},{6,7},{7,6},{8,9},{9,8},{10,11... | collective-permute-start | bytes 1966088 | tf_op jit(solution)/shard_map/ppermute | solution.py:260
  32.6 1.8 %collective-permute-start.8 = (bf16[4,32,1280]{2,1,0:T(8,128)(2,1)}, bf16[4,32,1280]{2,1,0:T(8,128)(2,1)S(1)}, u32[]{:S(2)}, u32[]{:S(2)}) collective-permute-start(bf16[4,32,1280]{2,1,0:T(8,128)(2,1)} %pad_maximum_fusion.2), channel_id=1, source_target_pairs={{0,1},{1,0},{2,3},{3,2},{4,5},{5,4},{6,7},{7,6},{8,9},{9,8},{10,11... | collective-permute-start | bytes 983048 | tf_op jit(solution)/shard_map/ppermute | solution.py:260
  32.7 1.8 %copy-start.1 = (bf16[4,32,1280]{2,1,0:T(8,128)(2,1)S(1)}, bf16[4,32,1280]{2,1,0:T(8,128)(2,1)}, u32[]{:S(2)}) copy-start(bf16[4,32,1280]{2,1,0:T(8,128)(2,1)} %copy-done) | copy-start | bytes 983044
  36.4 15.1 %collective-permute-start.10 = (bf16[4,32,1280]{2,1,0:T(8,128)(2,1)S(1)}, bf16[4,32,1280]{2,1,0:T(8,128)(2,1)S(1)}, u32[]{:S(2)}, u32[]{:S(2)}) collective-permute-start(bf16[4,32,1280]{2,1,0:T(8,128)(2,1)S(1)} %get-tuple-element.31), channel_id=1, source_target_pairs={{0,4},{1,5},{2,6},{3,7},{4,0},{5,1},{6,2},{7,3},{8,12},{9,13},{10,... | collective-permute-start | bytes 983048 | tf_op jit(solution)/shard_map/ppermute | solution.py:260
  37.8 14.5 %collective-permute-start.9 = (bf16[10,96,128]{2,1,0:T(8,128)(2,1)S(1)}, bf16[10,96,128]{2,1,0:T(8,128)(2,1)S(1)}, u32[]{:S(2)}, u32[]{:S(2)}) collective-permute-start(bf16[10,96,128]{2,1,0:T(8,128)(2,1)S(1)} %get-tuple-element.28), channel_id=1, source_target_pairs={{0,8},{1,9},{2,10},{3,11},{4,12},{5,13},{6,14},{7,15},{8,0},{9,1},... | collective-permute-start | bytes 737288 | tf_op jit(solution)/shard_map/ppermute | solution.py:260
  51.4 12.4 %collective-permute-start.14 = (bf16[10,96,128]{2,1,0:T(8,128)(2,1)S(1)}, bf16[10,96,128]{2,1,0:T(8,128)(2,1)S(1)}, u32[]{:S(2)}, u32[]{:S(2)}) collective-permute-start(bf16[10,96,128]{2,1,0:T(8,128)(2,1)S(1)} %get-tuple-element.39), channel_id=1, source_target_pairs={{0,4},{1,5},{2,6},{3,7},{4,0},{5,1},{6,2},{7,3},{8,12},{9,13},{10,... | collective-permute-start | bytes 737288 | tf_op jit(solution)/shard_map/ppermute | solution.py:260
  51.4 12.4 %collective-permute-start.15 = (bf16[10,96,128]{2,1,0:T(8,128)(2,1)S(1)}, bf16[10,96,128]{2,1,0:T(8,128)(2,1)S(1)}, u32[]{:S(2)}, u32[]{:S(2)}) collective-permute-start(bf16[10,96,128]{2,1,0:T(8,128)(2,1)S(1)} %get-tuple-element.41), channel_id=1, source_target_pairs={{0,12},{1,13},{2,14},{3,15},{4,8},{5,9},{6,10},{7,11},{8,4},{9,5},... | collective-permute-start | bytes 737288 | tf_op jit(solution)/shard_map/ppermute | solution.py:260
  52.4 6.2 %collective-permute-start.11 = (bf16[2,32,1280]{2,1,0:T(8,128)(2,1)S(1)}, bf16[2,32,1280]{2,1,0:T(8,128)(2,1)S(1)}, u32[]{:S(2)}, u32[]{:S(2)}) collective-permute-start(bf16[2,32,1280]{2,1,0:T(8,128)(2,1)S(1)} %get-tuple-element.35), channel_id=1, source_target_pairs={{0,2},{1,3},{2,0},{3,1},{4,6},{5,7},{6,4},{7,5},{8,10},{9,11},{10,... | collective-permute-start | bytes 491528 | tf_op jit(solution)/shard_map/ppermute | solution.py:260
  54.0 4.7 %collective-permute-start.12 = (bf16[2,32,1280]{2,1,0:T(8,128)(2,1)S(1)}, bf16[2,32,1280]{2,1,0:T(8,128)(2,1)S(1)}, u32[]{:S(2)}, u32[]{:S(2)}) collective-permute-start(bf16[2,32,1280]{2,1,0:T(8,128)(2,1)S(1)} %get-tuple-element.36), channel_id=1, source_target_pairs={{0,1},{1,0},{2,3},{3,2},{4,5},{5,4},{6,7},{7,6},{8,9},{9,8},{10,11... | collective-permute-start | bytes 491528 | tf_op jit(solution)/shard_map/ppermute | solution.py:260
  54.0 6.5 %collective-permute-start.13 = (bf16[2,32,1280]{2,1,0:T(8,128)(2,1)S(1)}, bf16[2,32,1280]{2,1,0:T(8,128)(2,1)S(1)}, u32[]{:S(2)}, u32[]{:S(2)}) collective-permute-start(bf16[2,32,1280]{2,1,0:T(8,128)(2,1)S(1)} %get-tuple-element.37), channel_id=1, source_target_pairs={{0,3},{1,2},{2,1},{3,0},{4,7},{5,6},{6,5},{7,4},{8,11},{9,10},{10,... | collective-permute-start | bytes 491528 | tf_op jit(solution)/shard_map/ppermute | solution.py:260

commit v15 on v14

--- a/solution.py
+++ b/solution.py
@@ -143,21 +143,20 @@
     )(scalars, near, far, weights, backs)
 
 
-def pack_kernel(home, away, *outs):
+def split_kernel(array, *outs):
     for i, out in enumerate(outs):
-        out[0] = home[i]
-        out[1] = away[i]
-
-
-def pack_call(home, away):
-    return pl.pallas_call(
-        pack_kernel,
-        out_shape=[jax.ShapeDtypeStruct((PAIR,) + home.shape[1:], home.dtype)] * home.shape[0],
-        in_specs=[RESIDENT] * PAIR,
-        out_specs=[RESIDENT] * home.shape[0],
+        out[0] = array[i]
+
+
+def split_call(array):
+    return pl.pallas_call(
+        split_kernel,
+        out_shape=[jax.ShapeDtypeStruct((1,) + array.shape[1:], array.dtype)] * array.shape[0],
+        in_specs=[RESIDENT],
+        out_specs=[RESIDENT] * array.shape[0],
         compiler_params=room(6),
-        name="pack",
-    )(home, away)
+        name="split",
+    )(array)
 
 
 def stack_kernel(scalars, *rest):
@@ -305,8 +304,17 @@
     back_home = swap(away, 1, 0)
 
     grads = list(backward_call(sizes, scalars, near, far, slopes, fsdp if direct else 1))
+    home_arrays, blocks = [home], [(0, b, (0, i)) for i, b in enumerate(origins)]
+    for bit in bits:
+        sent = [block for block in blocks if block[1] & bit]
+        home_arrays = home_arrays + [swap(take(home_arrays, [ref for _, _, ref in sent]), 0, bit)]
+        if direct and bit == bits[0]:
+            grads[3::PAIR], home_arrays[-1] = lax.optimization_barrier((grads[3::PAIR], home_arrays[-1]))
+        received = [(source ^ bit, target ^ bit, (len(home_arrays) - 1, i)) for i, (source, target, _) in enumerate(sent)]
+        blocks = [block for block in blocks if not block[1] & bit] + received
+
     if direct:
-        grads[1::PAIR], back_home = lax.optimization_barrier((grads[1::PAIR], back_home))
+        grads[1], back_home = lax.optimization_barrier((grads[1], back_home))
         across = {p: swap(grads[p], p, 0) for p in range(PAIR, fsdp, PAIR)}
         across, back_home = lax.optimization_barrier((across, back_home))
         total = sum_call(half.reshape(1).astype(jnp.int32), [grads[0]] + [across[p] if p in across else swap(grads[p], p, 0) for p in range(1, fsdp)])
@@ -316,10 +324,10 @@
         here = (jnp.arange(fsdp) == z)[:, None, None, None]
         total = jnp.where(here, split, arrived.astype(jnp.float32))
         total = jnp.sum(total.reshape(fsdp // PAIR, PAIR, share, size, TILE), axis=0)
-    packed = list(pack_call(home, back_home))
-    arrays = packed[:1] + [swap(packed[i], 0, b) for i, b in enumerate(origins) if i]
-    refs = [(i, a) for i in range(tensor) for a in range(PAIR)]
-    activations = join_call(first_tiles([(a, b) for b in origins for a in range(PAIR)]), arrays, refs)
+    pieces = split_call(back_home)
+    arrays = home_arrays + [pieces[i] if b == 0 else swap(pieces[i], 0, b) for i, b in enumerate(origins)]
+    refs = [ref for _, _, ref in blocks] + [(len(home_arrays) + i, 0) for i in range(tensor)]
+    activations = join_call(first_tiles([(0, b) for b, _, _ in blocks] + [(1, b) for b in origins]), arrays, refs)
     return activations, total.reshape(stripes, size, TILE).transpose(1, 0, 2)
 
 

time: 65.2 us -> 67.9 us (1.041)
  starting transfers between devices: 20.4 us -> 23.1 us
    ppermute x16 -> x18, starting transfers between devices: 20.4 us -> 23.1 us  [swap(): return lax.ppermute(value, ('fsdp', 'tensor'), pairs)]
    ppermute x16 -> x18, waiting for transfers between devices: 29.7 us -> 29.4 us  [swap(): return lax.ppermute(value, ('fsdp', 'tensor'), pairs)]
  transfers between devices with their start and end apart: 16 -> 18, of which waited for: 8 -> 8; matrix products, arithmetic and copies ran while one was open for 2% -> 2% of each run, Pallas kernels for 10% -> 10%
where the time goes in v15:
time: 67.9 us; the launch traced here: 67.4 us
  waiting for transfers between devices  29.4 us (43%)
  starting transfers between devices  23.1 us (34%)
  Pallas kernels  9.66 us (14%)
  local copies, waits for them, and re-layouts  3.35 us (5%)
  other arithmetic  1.01 us (1%)
  between operations  0.88 us (1%)
    ppermute x18, waiting for transfers between devices, swap(): return lax.ppermute(value, ('fsdp', 'tensor'), pairs)  29.4 us
    ppermute x18, starting transfers between devices, swap(): return lax.ppermute(value, ('fsdp', 'tensor'), pairs)  23.1 us
    pallas_call x2, Pallas kernels, cut_call(): pl.pallas_call(cut_kernel, out_shape=jax.ShapeDtypeStruct((count, rows, w...  3.18 us
    unnamed x15, local copies, waits for them, and re-layouts  2.17 us
    pallas_call x1, Pallas kernels, forward_call(): pl.pallas_call(functools.partial(forward_kernel, sizes), out_shape=[jax.S...  1.86 us
    pallas_call x1, Pallas kernels, join_call(): pl.pallas_call(functools.partial(join_kernel, refs), out_shape=jax.ShapeD...  1.44 us
    pallas_call x1, Pallas kernels, backward_call(): pl.pallas_call(functools.partial(backward_kernel, sizes), out_shape=[jax....  1.37 us
  transfers between devices with their start and end apart: 18, of which 8 were waited for; matrix products, arithmetic and copies ran while one was open for 2% of the time, Pallas kernels for 10%

profile of v15, /device:TPU:0, one launch (start us, length us, event | category | flops | bytes accessed | tf_op | source)
XLA Modules:
  0.0 67.4 jit_solution(3819318211670696469)
XLA Ops:
  0.6 3.1 %collective-permute-start = (bf16[32,2560]{1,0:T(8,128)(2,1)}, bf16[32,2560]{1,0:T(8,128)(2,1)S(1)}, u32[]{:S(2)}, u32[]{:S(2)}) collective-permute-start(bf16[32,2560]{1,0:T(8,128)(2,1)} %param.5), channel_id=1, source_target_pairs={{0,4},{1,5},{2,6},{3,7},{4,0},{5,1},{6,2},{7,3},{8,12},{9,13},{10,... | collective-permute-start | bytes 491528 | tf_op jit(solution)/shard_map/ppermute | solution.py:259
  3.8 1.6 %cut.2 = bf16[4,32,1280]{2,1,0:T(8,128)(2,1)S(1)} custom-call(s32[4]{0:T(128)S(1)} %pad_add_fusion.1.starts, bf16[32,10240]{1,0:T(8,128)(2,1)} %whole.3), custom_call_target="tpu_custom_call" | custom-call | tf_op jit(solution)/shard_map/cut/pallas_call | solution.py:50
  5.4 0.1 collective-permute-start.3
  5.6 3.0 %collective-permute-start.5 = (bf16[10,96,128]{2,1,0:T(8,128)(2,1)S(1)}, bf16[10,96,128]{2,1,0:T(8,128)(2,1)S(1)}, u32[]{:S(2)}, u32[]{:S(2)}) collective-permute-start(bf16[10,96,128]{2,1,0:T(8,128)(2,1)S(1)} %get-tuple-element.44.rest_0_), channel_id=1, source_target_pairs={{0,8},{1,9},{2,10},{3,11},{4,12},{5,13},{6,14},{7,15},{8,0},{9,1},... | collective-permute-start | bytes 737288 | tf_op jit(solution)/shard_map/ppermute | solution.py:259
  8.7 0.7 copy-done.4
  9.3 0.1 copy.8
  9.5 0.6 copy-done.5
  10.2 1.6 %cut.3.rest_0_ = bf16[4,32,1280]{2,1,0:T(8,128)(2,1)S(1)} custom-call(s32[86]{0:T(128)S(1)} %concatenate.22.starts.scalars, bf16[32,10240]{1,0:T(8,128)(2,1)} %whole.3), custom_call_target="tpu_custom_call" | custom-call | tf_op jit(solution)/shard_map/cut/pallas_call | solution.py:50
  11.9 0.7 %copy-done = bf16[4,32,1280]{2,1,0:T(8,128)(2,1)} copy-done((bf16[4,32,1280]{2,1,0:T(8,128)(2,1)}, bf16[4,32,1280]{2,1,0:T(8,128)(2,1)S(1)}, u32[]{:S(2)}) %copy-start) | copy-done | bytes 327704
  12.6 5.0 %collective-permute-start.6 = (bf16[10,96,128]{2,1,0:T(8,128)(2,1)S(1)}, bf16[10,96,128]{2,1,0:T(8,128)(2,1)S(1)}, u32[]{:S(2)}, u32[]{:S(2)}) collective-permute-start(bf16[10,96,128]{2,1,0:T(8,128)(2,1)S(1)} %get-tuple-element.25), channel_id=1, source_target_pairs={{0,12},{1,13},{2,14},{3,15},{4,8},{5,9},{6,10},{7,11},{8,4},{9,5},... | collective-permute-start | bytes 737288 | tf_op jit(solution)/shard_map/ppermute | solution.py:259
  17.6 1.6 %collective-permute-start.1 = (bf16[64,2560]{1,0:T(8,128)(2,1)S(1)}, bf16[64,2560]{1,0:T(8,128)(2,1)S(1)}, u32[]{:S(2)}, u32[]{:S(2)}) collective-permute-start(bf16[64,2560]{1,0:T(8,128)(2,1)S(1)} %pad_maximum_fusion), channel_id=1, source_target_pairs={{0,2},{1,3},{2,0},{3,1},{4,6},{5,7},{6,4},{7,5},{8,10},{9,11},{10,... | collective-permute-start | bytes 983048 | tf_op jit(solution)/shard_map/ppermute | solution.py:259
  19.2 1.2 %collective-permute-done.3.rest_1_ = bf16[4,32,1280]{2,1,0:T(8,128)(2,1)S(1)} collective-permute-done((bf16[4,32,1280]{2,1,0:T(8,128)(2,1)S(1)}, bf16[4,32,1280]{2,1,0:T(8,128)(2,1)S(1)}, u32[]{:S(2)}, u32[]{:S(2)}) %collective-permute-start.3) | collective-permute-done | bytes 327712 | tf_op jit(solution)/shard_map/ppermute | solution.py:259
  20.5 0.8 %slice-done.1 = bf16[2,32,1280]{2,1,0:T(8,128)(2,1)S(1)} async-done(((bf16[4,32,1280]{2,1,0:T(8,128)(2,1)}), bf16[2,32,1280]{2,1,0:T(8,128)(2,1)S(1)}, s32[]{:S(2)}) %slice-start.1) | async-done | bytes 163864 | tf_op jit(solution)/shard_map/slice | solution.py:245
  21.4 1.7 %collective-permute-start.7 = (bf16[4,32,1280]{2,1,0:T(8,128)(2,1)S(1)}, bf16[4,32,1280]{2,1,0:T(8,128)(2,1)S(1)}, u32[]{:S(2)}, u32[]{:S(2)}) collective-permute-start(bf16[4,32,1280]{2,1,0:T(8,128)(2,1)S(1)} %pad_maximum_fusion.1), channel_id=1, source_target_pairs={{0,2},{1,3},{2,0},{3,1},{4,6},{5,7},{6,4},{7,5},{8,10},{9,11},{10,... | collective-permute-start | bytes 983048 | tf_op jit(solution)/shard_map/ppermute | solution.py:259
  23.1 2.9 %collective-permute-done.1 = bf16[64,2560]{1,0:T(8,128)(2,1)S(1)} collective-permute-done((bf16[64,2560]{1,0:T(8,128)(2,1)S(1)}, bf16[64,2560]{1,0:T(8,128)(2,1)S(1)}, u32[]{:S(2)}, u32[]{:S(2)}) %collective-permute-start.1) | collective-permute-done | bytes 327712 | tf_op jit(solution)/shard_map/ppermute | solution.py:259
  26.2 5.6 %collective-permute-done.7.rest_2_ = bf16[4,32,1280]{2,1,0:T(8,128)(2,1)S(1)} collective-permute-done((bf16[4,32,1280]{2,1,0:T(8,128)(2,1)S(1)}, bf16[4,32,1280]{2,1,0:T(8,128)(2,1)S(1)}, u32[]{:S(2)}, u32[]{:S(2)}) %collective-permute-start.7) | collective-permute-done | bytes 327712 | tf_op jit(solution)/shard_map/ppermute | solution.py:259
  31.8 0.8 %pad_maximum_fusion.2 = bf16[4,32,1280]{2,1,0:T(8,128)(2,1)} fusion(bf16[1,32,1280]{2,1,0:T(8,128)(2,1)S(1)} %get-tuple-element.50, bf16[1,32,1280]{2,1,0:T(8,128)(2,1)S(1)} %get-tuple-element.49, bf16[1,32,1280]{2,1,0:T(8,128)(2,1)S(1)} %slice.33, bf16[1,32,1280]{2,1,0:T(8,128)(2,1)S(1)} %slice-done), kind=kLoop, calls=%fused_computation.2 | loop fusion | flops 491520 | bytes 655360 | tf_op jit(solution)/shard_map/concatenate | solution.py:246
  32.7 0.6 stack.74.weights
  33.3 1.1 %collective-permute-done.8.rest_3_ = bf16[4,32,1280]{2,1,0:T(8,128)(2,1)S(1)} collective-permute-done((bf16[4,32,1280]{2,1,0:T(8,128)(2,1)}, bf16[4,32,1280]{2,1,0:T(8,128)(2,1)S(1)}, u32[]{:S(2)}, u32[]{:S(2)}) %collective-permute-start.8) | collective-permute-done | bytes 327712 | tf_op jit(solution)/shard_map/ppermute | solution.py:259
  34.5 1.9 %forward.1 = (bf16[4,32,1280]{2,1,0:T(8,128)(2,1)S(1)}, bf16[4,32,1280]{2,1,0:T(8,128)(2,1)S(1)}, bf16[256,1280]{1,0:T(8,128)(2,1)S(1)}) custom-call(s32[86]{0:T(128)S(1)} %concatenate.22.starts.scalars, bf16[128,2560]{1,0:T(8,128)(2,1)S(1)} %constant_dynamic-update-slice_fusion.near, bf16[128,2560]{1,0:T(8,128)(2,1)S(1)} %collective-permute-done.2.far, ...), custom_call_target="tpu_custom_call" | custom-call | tf_op jit(solution)/shard_map/forward/pallas_call | solution.py:135
  36.4 1.5 %collective-permute-start.9 = (bf16[2,32,1280]{2,1,0:T(8,128)(2,1)S(1)}, bf16[2,32,1280]{2,1,0:T(8,128)(2,1)S(1)}, u32[]{:S(2)}, u32[]{:S(2)}) collective-permute-start(bf16[2,32,1280]{2,1,0:T(8,128)(2,1)S(1)} %pad_maximum_fusion.3), channel_id=1, source_target_pairs={{0,2},{1,3},{2,0},{3,1},{4,6},{5,7},{6,4},{7,5},{8,10},{9,11},{10,... | collective-permute-start | bytes 491528 | tf_op jit(solution)/shard_map/ppermute | solution.py:259
  38.0 1.4 %backward.1 = (f32[10,96,128]{2,1,0:T(8,128)S(1)}, bf16[10,96,128]{2,1,0:T(8,128)(2,1)S(1)}, bf16[10,96,128]{2,1,0:T(8,128)(2,1)S(1)}, bf16[10,96,128]{2,1,0:T(8,128)(2,1)S(1)}) custom-call(s32[86]{0:T(128)S(1)} %concatenate.22.starts.scalars, bf16[128,2560]{1,0:T(8,128)(2,1)S(1)} %constant_dynamic-update-slice_fusion.near, ...), custom_call_target="tpu_custom_call" | custom-call | tf_op jit(solution)/shard_map/backward/pallas_call | solution.py:199
  39.3 2.6 %collective-permute-start.11 = (bf16[10,96,128]{2,1,0:T(8,128)(2,1)S(1)}, bf16[10,96,128]{2,1,0:T(8,128)(2,1)S(1)}, u32[]{:S(2)}, u32[]{:S(2)}) collective-permute-start(bf16[10,96,128]{2,1,0:T(8,128)(2,1)S(1)} %get-tuple-element.31), channel_id=1, source_target_pairs={{0,8},{1,9},{2,10},{3,11},{4,12},{5,13},{6,14},{7,15},{8,0},{9,1},... | collective-permute-start | bytes 737288 | tf_op jit(solution)/shard_map/ppermute | solution.py:259
  41.9 0.8 %collective-permute-done.9.rest_1_ = bf16[2,32,1280]{2,1,0:T(8,128)(2,1)S(1)} collective-permute-done((bf16[2,32,1280]{2,1,0:T(8,128)(2,1)S(1)}, bf16[2,32,1280]{2,1,0:T(8,128)(2,1)S(1)}, u32[]{:S(2)}, u32[]{:S(2)}) %collective-permute-start.9) | collective-permute-done | bytes 163872 | tf_op jit(solution)/shard_map/ppermute | solution.py:259
  42.8 2.0 %collective-permute-start.17 = (bf16[10,96,128]{2,1,0:T(8,128)(2,1)S(1)}, bf16[10,96,128]{2,1,0:T(8,128)(2,1)S(1)}, u32[]{:S(2)}, u32[]{:S(2)}) collective-permute-start(bf16[10,96,128]{2,1,0:T(8,128)(2,1)S(1)} %get-tuple-element.43), channel_id=1, source_target_pairs={{0,12},{1,13},{2,14},{3,15},{4,8},{5,9},{6,10},{7,11},{8,4},{9,5},... | collective-permute-start | bytes 737288 | tf_op jit(solution)/shard_map/ppermute | solution.py:259
  44.8 7.5 %collective-permute-done.12.array = bf16[4,32,1280]{2,1,0:T(8,128)(2,1)S(1)} collective-permute-done((bf16[4,32,1280]{2,1,0:T(8,128)(2,1)S(1)}, bf16[4,32,1280]{2,1,0:T(8,128)(2,1)S(1)}, u32[]{:S(2)}, u32[]{:S(2)}) %collective-permute-start.12) | collective-permute-done | bytes 327712 | tf_op jit(solution)/shard_map/ppermute | solution.py:259
  52.3 7.1 %collective-permute-done.11.rest_2_ = bf16[10,96,128]{2,1,0:T(8,128)(2,1)S(1)} collective-permute-done((bf16[10,96,128]{2,1,0:T(8,128)(2,1)S(1)}, bf16[10,96,128]{2,1,0:T(8,128)(2,1)S(1)}, u32[]{:S(2)}, u32[]{:S(2)}) %collective-permute-start.11) | collective-permute-done | bytes 245792 | tf_op jit(solution)/shard_map/ppermute | solution.py:259
  59.4 0.6 collective-permute-start.13
  60.1 1.6 %collective-permute-start.15 = (bf16[1,32,1280]{2,1,0:T(8,128)(2,1)S(1)}, bf16[1,32,1280]{2,1,0:T(8,128)(2,1)S(1)}, u32[]{:S(2)}, u32[]{:S(2)}) collective-permute-start(bf16[1,32,1280]{2,1,0:T(8,128)(2,1)S(1)} %get-tuple-element.39), channel_id=1, source_target_pairs={{0,3},{1,2},{2,1},{3,0},{4,7},{5,6},{6,5},{7,4},{8,11},{9,10},{10,... | collective-permute-start | bytes 245768 | tf_op jit(solution)/shard_map/ppermute | solution.py:259
  61.7 3.1 %collective-permute-done.13.rest_4_ = bf16[1,32,1280]{2,1,0:T(8,128)(2,1)S(1)} collective-permute-done((bf16[1,32,1280]{2,1,0:T(8,128)(2,1)S(1)}, bf16[1,32,1280]{2,1,0:T(8,128)(2,1)S(1)}, u32[]{:S(2)}, u32[]{:S(2)}) %collective-permute-start.13) | collective-permute-done | bytes 81952 | tf_op jit(solution)/shard_map/ppermute | solution.py:259
  64.8 1.4 %join.1 = bf16[32,10240]{1,0:T(8,128)(2,1)} custom-call(s32[8]{0:T(128)S(1)} %stack.66.starts, bf16[4,32,1280]{2,1,0:T(8,128)(2,1)S(1)} %get-tuple-element.27.rest_0_, bf16[2,32,1280]{2,1,0:T(8,128)(2,1)S(1)} %collective-permute-done.9.rest_1_, bf16[2,32,1280]{2,1,0:T(8,128)(2,1)S(1)} %collective-permute-done.10.rest_2_, ...), custom_call_target="tpu_custom_call" | custom-call | tf_op jit(solution)/shard_map/join/pallas_call | solution.py:87
  66.3 1.1 %sum.1 = f32[2,10,96,128]{3,2,1,0:T(8,128)} custom-call(s32[1]{0:T(128)} %bitcast.15.half, f32[10,96,128]{2,1,0:T(8,128)S(1)} %get-tuple-element.40.rest_0_, bf16[10,96,128]{2,1,0:T(8,128)(2,1)S(1)} %collective-permute-done.16.rest_1_, bf16[10,96,128]{2,1,0:T(8,128)(2,1)S(1)} %collective-permute-done.11.rest_2_, ...), custom_call_target="tpu_custom_call" | custom-call | tf_op jit(solution)/shard_map/sum/pallas_call | solution.py:227
  (49 shorter events, 1.0 us)
Async XLA Ops:
  0.6 11.9 %collective-permute-start = (bf16[32,2560]{1,0:T(8,128)(2,1)}, bf16[32,2560]{1,0:T(8,128)(2,1)S(1)}, u32[]{:S(2)}, u32[]{:S(2)}) collective-permute-start(bf16[32,2560]{1,0:T(8,128)(2,1)} %param.5), channel_id=1, source_target_pairs={{0,4},{1,5},{2,6},{3,7},{4,0},{5,1},{6,2},{7,3},{8,12},{9,13},{10,... | collective-permute-start | bytes 491528 | tf_op jit(solution)/shard_map/ppermute | solution.py:259
  3.8 1.7 %copy-start.3 = (bf16[96,20,128]{2,0,1:T(8,128)(2,1)S(1)}, bf16[96,20,128]{2,0,1:T(8,128)(2,1)}, u32[]{:S(2)}) copy-start(bf16[96,20,128]{2,0,1:T(8,128)(2,1)} %param.6) | copy-start | bytes 1474564
  5.4 15.0 %collective-permute-start.3 = (bf16[4,32,1280]{2,1,0:T(8,128)(2,1)S(1)}, bf16[4,32,1280]{2,1,0:T(8,128)(2,1)S(1)}, u32[]{:S(2)}, u32[]{:S(2)}) collective-permute-start(bf16[4,32,1280]{2,1,0:T(8,128)(2,1)S(1)} %cut.2), channel_id=1, source_target_pairs={{0,4},{1,5},{2,6},{3,7},{4,0},{5,1},{6,2},{7,3},{8,12},{9,13},{10,... | collective-permute-start | bytes 983048 | tf_op jit(solution)/shard_map/ppermute | solution.py:259
  5.5 3.1 %copy-start.2 = (bf16[32,2560]{1,0:T(8,128)(2,1)S(1)}, bf16[32,2560]{1,0:T(8,128)(2,1)}, u32[]{:S(2)}) copy-start(bf16[32,2560]{1,0:T(8,128)(2,1)} %param.5) | copy-start | bytes 491524
  5.6 27.1 %collective-permute-start.5 = (bf16[10,96,128]{2,1,0:T(8,128)(2,1)S(1)}, bf16[10,96,128]{2,1,0:T(8,128)(2,1)S(1)}, u32[]{:S(2)}, u32[]{:S(2)}) collective-permute-start(bf16[10,96,128]{2,1,0:T(8,128)(2,1)S(1)} %get-tuple-element.44.rest_0_), channel_id=1, source_target_pairs={{0,8},{1,9},{2,10},{3,11},{4,12},{5,13},{6,14},{7,15},{8,0},{9,1},... | collective-permute-start | bytes 737288 | tf_op jit(solution)/shard_map/ppermute | solution.py:259
  8.6 0.7 %copy-start.4 = (s32[20,3]{0,1:T(4,128)S(1)}, s32[20,3]{0,1:T(4,128)}, u32[]{:S(2)}) copy-start(s32[20,3]{0,1:T(4,128)} %param.8) | copy-start | bytes 724
  9.5 0.7 copy-start.5
  11.8 0.7 %copy-start = (bf16[4,32,1280]{2,1,0:T(8,128)(2,1)}, bf16[4,32,1280]{2,1,0:T(8,128)(2,1)S(1)}, u32[]{:S(2)}) copy-start(bf16[4,32,1280]{2,1,0:T(8,128)(2,1)S(1)} %cut.3.rest_0_) | copy-start | bytes 983044
  12.6 20.1 %collective-permute-start.6 = (bf16[10,96,128]{2,1,0:T(8,128)(2,1)S(1)}, bf16[10,96,128]{2,1,0:T(8,128)(2,1)S(1)}, u32[]{:S(2)}, u32[]{:S(2)}) collective-permute-start(bf16[10,96,128]{2,1,0:T(8,128)(2,1)S(1)} %get-tuple-element.25), channel_id=1, source_target_pairs={{0,12},{1,13},{2,14},{3,15},{4,8},{5,9},{6,10},{7,11},{8,4},{9,5},... | collective-permute-start | bytes 737288 | tf_op jit(solution)/shard_map/ppermute | solution.py:259
  17.6 8.4 %collective-permute-start.1 = (bf16[64,2560]{1,0:T(8,128)(2,1)S(1)}, bf16[64,2560]{1,0:T(8,128)(2,1)S(1)}, u32[]{:S(2)}, u32[]{:S(2)}) collective-permute-start(bf16[64,2560]{1,0:T(8,128)(2,1)S(1)} %pad_maximum_fusion), channel_id=1, source_target_pairs={{0,2},{1,3},{2,0},{3,1},{4,6},{5,7},{6,4},{7,5},{8,10},{9,11},{10,... | collective-permute-start | bytes 983048 | tf_op jit(solution)/shard_map/ppermute | solution.py:259
  20.4 0.9 %slice-start.1 = ((bf16[4,32,1280]{2,1,0:T(8,128)(2,1)}), bf16[2,32,1280]{2,1,0:T(8,128)(2,1)S(1)}, s32[]{:S(2)}) async-start(bf16[4,32,1280]{2,1,0:T(8,128)(2,1)} %copy-done), calls=%async_computation.1 | async-start | bytes 327680 | tf_op jit(solution)/shard_map/slice | solution.py:245
  20.5 12.3 %collective-permute-start.4 = (bf16[10,96,128]{2,1,0:T(8,128)(2,1)S(1)}, bf16[10,96,128]{2,1,0:T(8,128)(2,1)S(1)}, u32[]{:S(2)}, u32[]{:S(2)}) collective-permute-start(bf16[10,96,128]{2,1,0:T(8,128)(2,1)S(1)} %get-tuple-element.25), channel_id=1, source_target_pairs={{0,4},{1,5},{2,6},{3,7},{4,0},{5,1},{6,2},{7,3},{8,12},{9,13},{10,... | collective-permute-start | bytes 737288 | tf_op jit(solution)/shard_map/ppermute | solution.py:259
  21.4 10.4 %collective-permute-start.7 = (bf16[4,32,1280]{2,1,0:T(8,128)(2,1)S(1)}, bf16[4,32,1280]{2,1,0:T(8,128)(2,1)S(1)}, u32[]{:S(2)}, u32[]{:S(2)}) collective-permute-start(bf16[4,32,1280]{2,1,0:T(8,128)(2,1)S(1)} %pad_maximum_fusion.1), channel_id=1, source_target_pairs={{0,2},{1,3},{2,0},{3,1},{4,6},{5,7},{6,4},{7,5},{8,10},{9,11},{10,... | collective-permute-start | bytes 983048 | tf_op jit(solution)/shard_map/ppermute | solution.py:259
  26.1 5.7 %slice-start = ((bf16[4,32,1280]{2,1,0:T(8,128)(2,1)}), bf16[1,32,1280]{2,1,0:T(8,128)(2,1)S(1)}, s32[]{:S(2)}) async-start(bf16[4,32,1280]{2,1,0:T(8,128)(2,1)} %copy-done), calls=%async_computation | async-start | bytes 163840 | tf_op jit(solution)/shard_map/slice | solution.py:245
  26.1 8.4 %collective-permute-start.2 = (bf16[128,2560]{1,0:T(8,128)(2,1)S(1)}, bf16[128,2560]{1,0:T(8,128)(2,1)S(1)}, u32[]{:S(2)}, u32[]{:S(2)}) collective-permute-start(bf16[128,2560]{1,0:T(8,128)(2,1)S(1)} %constant_dynamic-update-slice_fusion.near), channel_id=1, source_target_pairs={{0,1},{1,0},{2,3},{3,2},{4,5},{5,4},{6,7},{7,6},{8,9},{9,8},{10,11... | collective-permute-start | bytes 1966088 | tf_op jit(solution)/shard_map/ppermute | solution.py:259
  32.6 1.8 %collective-permute-start.8 = (bf16[4,32,1280]{2,1,0:T(8,128)(2,1)}, bf16[4,32,1280]{2,1,0:T(8,128)(2,1)S(1)}, u32[]{:S(2)}, u32[]{:S(2)}) collective-permute-start(bf16[4,32,1280]{2,1,0:T(8,128)(2,1)} %pad_maximum_fusion.2), channel_id=1, source_target_pairs={{0,1},{1,0},{2,3},{3,2},{4,5},{5,4},{6,7},{7,6},{8,9},{9,8},{10,11... | collective-permute-start | bytes 983048 | tf_op jit(solution)/shard_map/ppermute | solution.py:259
  32.7 1.8 %copy-start.1 = (bf16[4,32,1280]{2,1,0:T(8,128)(2,1)S(1)}, bf16[4,32,1280]{2,1,0:T(8,128)(2,1)}, u32[]{:S(2)}) copy-start(bf16[4,32,1280]{2,1,0:T(8,128)(2,1)} %copy-done) | copy-start | bytes 983044
  36.4 6.3 %collective-permute-start.9 = (bf16[2,32,1280]{2,1,0:T(8,128)(2,1)S(1)}, bf16[2,32,1280]{2,1,0:T(8,128)(2,1)S(1)}, u32[]{:S(2)}, u32[]{:S(2)}) collective-permute-start(bf16[2,32,1280]{2,1,0:T(8,128)(2,1)S(1)} %pad_maximum_fusion.3), channel_id=1, source_target_pairs={{0,2},{1,3},{2,0},{3,1},{4,6},{5,7},{6,4},{7,5},{8,10},{9,11},{10,... | collective-permute-start | bytes 491528 | tf_op jit(solution)/shard_map/ppermute | solution.py:259
  38.0 14.3 %collective-permute-start.12 = (bf16[4,32,1280]{2,1,0:T(8,128)(2,1)S(1)}, bf16[4,32,1280]{2,1,0:T(8,128)(2,1)S(1)}, u32[]{:S(2)}, u32[]{:S(2)}) collective-permute-start(bf16[4,32,1280]{2,1,0:T(8,128)(2,1)S(1)} %get-tuple-element.33), channel_id=1, source_target_pairs={{0,4},{1,5},{2,6},{3,7},{4,0},{5,1},{6,2},{7,3},{8,12},{9,13},{10,... | collective-permute-start | bytes 983048 | tf_op jit(solution)/shard_map/ppermute | solution.py:259
  39.3 20.1 %collective-permute-start.11 = (bf16[10,96,128]{2,1,0:T(8,128)(2,1)S(1)}, bf16[10,96,128]{2,1,0:T(8,128)(2,1)S(1)}, u32[]{:S(2)}, u32[]{:S(2)}) collective-permute-start(bf16[10,96,128]{2,1,0:T(8,128)(2,1)S(1)} %get-tuple-element.31), channel_id=1, source_target_pairs={{0,8},{1,9},{2,10},{3,11},{4,12},{5,13},{6,14},{7,15},{8,0},{9,1},... | collective-permute-start | bytes 737288 | tf_op jit(solution)/shard_map/ppermute | solution.py:259
  42.7 17.3 %collective-permute-start.10 = (bf16[2,32,1280]{2,1,0:T(8,128)(2,1)S(1)}, bf16[2,32,1280]{2,1,0:T(8,128)(2,1)S(1)}, u32[]{:S(2)}, u32[]{:S(2)}) collective-permute-start(bf16[2,32,1280]{2,1,0:T(8,128)(2,1)S(1)} %pad_maximum_fusion.4), channel_id=1, source_target_pairs={{0,1},{1,0},{2,3},{3,2},{4,5},{5,4},{6,7},{7,6},{8,9},{9,8},{10,11... | collective-permute-start | bytes 491528 | tf_op jit(solution)/shard_map/ppermute | solution.py:259
  42.8 23.5 %collective-permute-start.17 = (bf16[10,96,128]{2,1,0:T(8,128)(2,1)S(1)}, bf16[10,96,128]{2,1,0:T(8,128)(2,1)S(1)}, u32[]{:S(2)}, u32[]{:S(2)}) collective-permute-start(bf16[10,96,128]{2,1,0:T(8,128)(2,1)S(1)} %get-tuple-element.43), channel_id=1, source_target_pairs={{0,12},{1,13},{2,14},{3,15},{4,8},{5,9},{6,10},{7,11},{8,4},{9,5},... | collective-permute-start | bytes 737288 | tf_op jit(solution)/shard_map/ppermute | solution.py:259
  52.3 14.0 %collective-permute-start.16 = (bf16[10,96,128]{2,1,0:T(8,128)(2,1)S(1)}, bf16[10,96,128]{2,1,0:T(8,128)(2,1)S(1)}, u32[]{:S(2)}, u32[]{:S(2)}) collective-permute-start(bf16[10,96,128]{2,1,0:T(8,128)(2,1)S(1)} %get-tuple-element.41), channel_id=1, source_target_pairs={{0,4},{1,5},{2,6},{3,7},{4,0},{5,1},{6,2},{7,3},{8,12},{9,13},{10,... | collective-permute-start | bytes 737288 | tf_op jit(solution)/shard_map/ppermute | solution.py:259
  59.4 5.4 %collective-permute-start.13 = (bf16[1,32,1280]{2,1,0:T(8,128)(2,1)S(1)}, bf16[1,32,1280]{2,1,0:T(8,128)(2,1)S(1)}, u32[]{:S(2)}, u32[]{:S(2)}) collective-permute-start(bf16[1,32,1280]{2,1,0:T(8,128)(2,1)S(1)} %get-tuple-element.37), channel_id=1, source_target_pairs={{0,2},{1,3},{2,0},{3,1},{4,6},{5,7},{6,4},{7,5},{8,10},{9,11},{10,... | collective-permute-start | bytes 245768 | tf_op jit(solution)/shard_map/ppermute | solution.py:259
  60.1 4.8 %collective-permute-start.14 = (bf16[1,32,1280]{2,1,0:T(8,128)(2,1)S(1)}, bf16[1,32,1280]{2,1,0:T(8,128)(2,1)S(1)}, u32[]{:S(2)}, u32[]{:S(2)}) collective-permute-start(bf16[1,32,1280]{2,1,0:T(8,128)(2,1)S(1)} %get-tuple-element.38), channel_id=1, source_target_pairs={{0,1},{1,0},{2,3},{3,2},{4,5},{5,4},{6,7},{7,6},{8,9},{9,8},{10,11... | collective-permute-start | bytes 245768 | tf_op jit(solution)/shard_map/ppermute | solution.py:259
  60.1 4.8 %collective-permute-start.15 = (bf16[1,32,1280]{2,1,0:T(8,128)(2,1)S(1)}, bf16[1,32,1280]{2,1,0:T(8,128)(2,1)S(1)}, u32[]{:S(2)}, u32[]{:S(2)}) collective-permute-start(bf16[1,32,1280]{2,1,0:T(8,128)(2,1)S(1)} %get-tuple-element.39), channel_id=1, source_target_pairs={{0,3},{1,2},{2,1},{3,0},{4,7},{5,6},{6,5},{7,4},{8,11},{9,10},{10,... | collective-permute-start | bytes 245768 | tf_op jit(solution)/shard_map/ppermute | solution.py:259

commit v16 on v15

--- a/solution.py
+++ b/solution.py
@@ -13,6 +13,7 @@
 ROWS = 16
 DIRECT = 8
 STACK_FLOPS = 2 * 10**9
+SPLIT_FLOPS = 2 * 10**9
 ROOT = 0.7978845608028654
 CUBIC = 0.044715
 ANYWHERE = pl.BlockSpec(memory_space=pl.ANY)
@@ -155,6 +156,7 @@
         in_specs=[RESIDENT],
         out_specs=[RESIDENT] * array.shape[0],
         compiler_params=room(6),
+        cost_estimate=pl.CostEstimate(flops=SPLIT_FLOPS, bytes_accessed=0, transcendentals=0),
         name="split",
     )(array)
 
@@ -316,7 +318,6 @@
     if direct:
         grads[1], back_home = lax.optimization_barrier((grads[1], back_home))
         across = {p: swap(grads[p], p, 0) for p in range(PAIR, fsdp, PAIR)}
-        across, back_home = lax.optimization_barrier((across, back_home))
         total = sum_call(half.reshape(1).astype(jnp.int32), [grads[0]] + [across[p] if p in across else swap(grads[p], p, 0) for p in range(1, fsdp)])
     else:
         split = grads[0].reshape(share, fsdp, size, TILE).transpose(1, 0, 2, 3)
@@ -325,9 +326,10 @@
         total = jnp.where(here, split, arrived.astype(jnp.float32))
         total = jnp.sum(total.reshape(fsdp // PAIR, PAIR, share, size, TILE), axis=0)
     pieces = split_call(back_home)
-    arrays = home_arrays + [pieces[i] if b == 0 else swap(pieces[i], 0, b) for i, b in enumerate(origins)]
+    order = sorted(range(tensor), key=lambda i: -origins[i])
+    arrays = home_arrays + [swap(pieces[i], 0, origins[i]) if origins[i] else pieces[i] for i in order]
     refs = [ref for _, _, ref in blocks] + [(len(home_arrays) + i, 0) for i in range(tensor)]
-    activations = join_call(first_tiles([(0, b) for b, _, _ in blocks] + [(1, b) for b in origins]), arrays, refs)
+    activations = join_call(first_tiles([(0, b) for b, _, _ in blocks] + [(1, origins[i]) for i in order]), arrays, refs)
     return activations, total.reshape(stripes, size, TILE).transpose(1, 0, 2)
 
 

time: 67.9 us -> 65.5 us (0.965)
  starting transfers between devices: 23.1 us -> 21.6 us
    ppermute x18, starting transfers between devices: 23.1 us -> 21.6 us  [swap(): return lax.ppermute(value, ('fsdp', 'tensor'), pairs)]
  transfers between devices with their start and end apart: 18 -> 18, of which waited for: 8 -> 12; matrix products, arithmetic and copies ran while one was open for 2% -> 2% of each run, Pallas kernels for 10% -> 10%
where the time goes in v16:
time: 65.5 us; the launch traced here: 65.2 us
  waiting for transfers between devices  28.8 us (44%)
  starting transfers between devices  21.6 us (33%)
  Pallas kernels  9.65 us (15%)
  local copies, waits for them, and re-layouts  3.35 us (5%)
  other arithmetic  1.01 us (2%)
  between operations  0.88 us (1%)
    ppermute x18, waiting for transfers between devices, swap(): return lax.ppermute(value, ('fsdp', 'tensor'), pairs)  28.8 us
    ppermute x18, starting transfers between devices, swap(): return lax.ppermute(value, ('fsdp', 'tensor'), pairs)  21.6 us
    pallas_call x2, Pallas kernels, cut_call(): pl.pallas_call(cut_kernel, out_shape=jax.ShapeDtypeStruct((count, rows, w...  3.18 us
    unnamed x15, local copies, waits for them, and re-layouts  2.17 us
    pallas_call x1, Pallas kernels, forward_call(): pl.pallas_call(functools.partial(forward_kernel, sizes), out_shape=[jax.S...  1.86 us
    pallas_call x1, Pallas kernels, join_call(): pl.pallas_call(functools.partial(join_kernel, refs), out_shape=jax.ShapeD...  1.44 us
    pallas_call x1, Pallas kernels, backward_call(): pl.pallas_call(functools.partial(backward_kernel, sizes), out_shape=[jax....  1.37 us
  transfers between devices with their start and end apart: 18, of which 12 were waited for; matrix products, arithmetic and copies ran while one was open for 2% of the time, Pallas kernels for 10%

profile of v16, /device:TPU:0, one launch (start us, length us, event | category | flops | bytes accessed | tf_op | source)
XLA Modules:
  0.0 65.2 jit_solution(10207394612816497261)
XLA Ops:
  0.6 3.1 %collective-permute-start = (bf16[32,2560]{1,0:T(8,128)(2,1)}, bf16[32,2560]{1,0:T(8,128)(2,1)S(1)}, u32[]{:S(2)}, u32[]{:S(2)}) collective-permute-start(bf16[32,2560]{1,0:T(8,128)(2,1)} %param.5), channel_id=1, source_target_pairs={{0,4},{1,5},{2,6},{3,7},{4,0},{5,1},{6,2},{7,3},{8,12},{9,13},{10,... | collective-permute-start | bytes 491528 | tf_op jit(solution)/shard_map/ppermute | solution.py:261
  3.8 1.6 %cut.2 = bf16[4,32,1280]{2,1,0:T(8,128)(2,1)S(1)} custom-call(s32[4]{0:T(128)S(1)} %pad_add_fusion.1.starts, bf16[32,10240]{1,0:T(8,128)(2,1)} %whole.3), custom_call_target="tpu_custom_call" | custom-call | tf_op jit(solution)/shard_map/cut/pallas_call | solution.py:51
  5.6 3.0 %collective-permute-start.5 = (bf16[10,96,128]{2,1,0:T(8,128)(2,1)S(1)}, bf16[10,96,128]{2,1,0:T(8,128)(2,1)S(1)}, u32[]{:S(2)}, u32[]{:S(2)}) collective-permute-start(bf16[10,96,128]{2,1,0:T(8,128)(2,1)S(1)} %get-tuple-element.40.rest_0_), channel_id=1, source_target_pairs={{0,8},{1,9},{2,10},{3,11},{4,12},{5,13},{6,14},{7,15},{8,0},{9,1},... | collective-permute-start | bytes 737288 | tf_op jit(solution)/shard_map/ppermute | solution.py:261
  8.7 0.7 %copy-done.4 = s32[20,3]{0,1:T(4,128)S(1)} copy-done((s32[20,3]{0,1:T(4,128)S(1)}, s32[20,3]{0,1:T(4,128)}, u32[]{:S(2)}) %copy-start.4) | copy-done | bytes 264
  9.5 0.6 copy-done.5
  10.2 1.6 %cut.3.rest_0_ = bf16[4,32,1280]{2,1,0:T(8,128)(2,1)S(1)} custom-call(s32[86]{0:T(128)S(1)} %concatenate.22.starts.scalars, bf16[32,10240]{1,0:T(8,128)(2,1)} %whole.3), custom_call_target="tpu_custom_call" | custom-call | tf_op jit(solution)/shard_map/cut/pallas_call | solution.py:51
  11.9 0.7 %copy-done = bf16[4,32,1280]{2,1,0:T(8,128)(2,1)} copy-done((bf16[4,32,1280]{2,1,0:T(8,128)(2,1)}, bf16[4,32,1280]{2,1,0:T(8,128)(2,1)S(1)}, u32[]{:S(2)}) %copy-start) | copy-done | bytes 327704
  12.6 5.0 %collective-permute-start.6 = (bf16[10,96,128]{2,1,0:T(8,128)(2,1)S(1)}, bf16[10,96,128]{2,1,0:T(8,128)(2,1)S(1)}, u32[]{:S(2)}, u32[]{:S(2)}) collective-permute-start(bf16[10,96,128]{2,1,0:T(8,128)(2,1)S(1)} %get-tuple-element.23), channel_id=1, source_target_pairs={{0,12},{1,13},{2,14},{3,15},{4,8},{5,9},{6,10},{7,11},{8,4},{9,5},... | collective-permute-start | bytes 737288 | tf_op jit(solution)/shard_map/ppermute | solution.py:261
  17.6 1.6 %collective-permute-start.1 = (bf16[64,2560]{1,0:T(8,128)(2,1)S(1)}, bf16[64,2560]{1,0:T(8,128)(2,1)S(1)}, u32[]{:S(2)}, u32[]{:S(2)}) collective-permute-start(bf16[64,2560]{1,0:T(8,128)(2,1)S(1)} %pad_maximum_fusion), channel_id=1, source_target_pairs={{0,2},{1,3},{2,0},{3,1},{4,6},{5,7},{6,4},{7,5},{8,10},{9,11},{10,... | collective-permute-start | bytes 983048 | tf_op jit(solution)/shard_map/ppermute | solution.py:261
  19.2 1.2 %collective-permute-done.3.rest_1_ = bf16[4,32,1280]{2,1,0:T(8,128)(2,1)S(1)} collective-permute-done((bf16[4,32,1280]{2,1,0:T(8,128)(2,1)S(1)}, bf16[4,32,1280]{2,1,0:T(8,128)(2,1)S(1)}, u32[]{:S(2)}, u32[]{:S(2)}) %collective-permute-start.3) | collective-permute-done | bytes 327712 | tf_op jit(solution)/shard_map/ppermute | solution.py:261
  20.5 0.8 %slice-done.1 = bf16[2,32,1280]{2,1,0:T(8,128)(2,1)S(1)} async-done(((bf16[4,32,1280]{2,1,0:T(8,128)(2,1)}), bf16[2,32,1280]{2,1,0:T(8,128)(2,1)S(1)}, s32[]{:S(2)}) %slice-start.1) | async-done | bytes 163864 | tf_op jit(solution)/shard_map/slice | solution.py:247
  21.4 1.7 %collective-permute-start.7 = (bf16[4,32,1280]{2,1,0:T(8,128)(2,1)S(1)}, bf16[4,32,1280]{2,1,0:T(8,128)(2,1)S(1)}, u32[]{:S(2)}, u32[]{:S(2)}) collective-permute-start(bf16[4,32,1280]{2,1,0:T(8,128)(2,1)S(1)} %pad_maximum_fusion.1), channel_id=1, source_target_pairs={{0,2},{1,3},{2,0},{3,1},{4,6},{5,7},{6,4},{7,5},{8,10},{9,11},{10,... | collective-permute-start | bytes 983048 | tf_op jit(solution)/shard_map/ppermute | solution.py:261
  23.1 2.9 %collective-permute-done.1 = bf16[64,2560]{1,0:T(8,128)(2,1)S(1)} collective-permute-done((bf16[64,2560]{1,0:T(8,128)(2,1)S(1)}, bf16[64,2560]{1,0:T(8,128)(2,1)S(1)}, u32[]{:S(2)}, u32[]{:S(2)}) %collective-permute-start.1) | collective-permute-done | bytes 327712 | tf_op jit(solution)/shard_map/ppermute | solution.py:261
  26.2 5.6 %collective-permute-done.7.rest_2_ = bf16[4,32,1280]{2,1,0:T(8,128)(2,1)S(1)} collective-permute-done((bf16[4,32,1280]{2,1,0:T(8,128)(2,1)S(1)}, bf16[4,32,1280]{2,1,0:T(8,128)(2,1)S(1)}, u32[]{:S(2)}, u32[]{:S(2)}) %collective-permute-start.7) | collective-permute-done | bytes 327712 | tf_op jit(solution)/shard_map/ppermute | solution.py:261
  31.8 0.8 %pad_maximum_fusion.2 = bf16[4,32,1280]{2,1,0:T(8,128)(2,1)} fusion(bf16[1,32,1280]{2,1,0:T(8,128)(2,1)S(1)} %get-tuple-element.46, bf16[1,32,1280]{2,1,0:T(8,128)(2,1)S(1)} %get-tuple-element.45, bf16[1,32,1280]{2,1,0:T(8,128)(2,1)S(1)} %slice.33, bf16[1,32,1280]{2,1,0:T(8,128)(2,1)S(1)} %slice-done), kind=kLoop, calls=%fused_computation.2 | loop fusion | flops 491520 | bytes 655360 | tf_op jit(solution)/shard_map/concatenate | solution.py:248
  32.7 0.6 stack.74.weights
  33.3 1.1 %collective-permute-done.8.rest_3_ = bf16[4,32,1280]{2,1,0:T(8,128)(2,1)S(1)} collective-permute-done((bf16[4,32,1280]{2,1,0:T(8,128)(2,1)}, bf16[4,32,1280]{2,1,0:T(8,128)(2,1)S(1)}, u32[]{:S(2)}, u32[]{:S(2)}) %collective-permute-start.8) | collective-permute-done | bytes 327712 | tf_op jit(solution)/shard_map/ppermute | solution.py:261
  34.5 1.9 %forward.1 = (bf16[4,32,1280]{2,1,0:T(8,128)(2,1)S(1)}, bf16[4,32,1280]{2,1,0:T(8,128)(2,1)S(1)}, bf16[256,1280]{1,0:T(8,128)(2,1)S(1)}) custom-call(s32[86]{0:T(128)S(1)} %concatenate.22.starts.scalars, bf16[128,2560]{1,0:T(8,128)(2,1)S(1)} %constant_dynamic-update-slice_fusion.near, bf16[128,2560]{1,0:T(8,128)(2,1)S(1)} %collective-permute-done.2.far, ...), custom_call_target="tpu_custom_call" | custom-call | tf_op jit(solution)/shard_map/forward/pallas_call | solution.py:136
  36.4 1.6 %collective-permute-start.9 = (bf16[2,32,1280]{2,1,0:T(8,128)(2,1)S(1)}, bf16[2,32,1280]{2,1,0:T(8,128)(2,1)S(1)}, u32[]{:S(2)}, u32[]{:S(2)}) collective-permute-start(bf16[2,32,1280]{2,1,0:T(8,128)(2,1)S(1)} %pad_maximum_fusion.3), channel_id=1, source_target_pairs={{0,2},{1,3},{2,0},{3,1},{4,6},{5,7},{6,4},{7,5},{8,10},{9,11},{10,... | collective-permute-start | bytes 491528 | tf_op jit(solution)/shard_map/ppermute | solution.py:261
  38.0 1.4 %backward.1 = (f32[10,96,128]{2,1,0:T(8,128)S(1)}, bf16[10,96,128]{2,1,0:T(8,128)(2,1)S(1)}, bf16[10,96,128]{2,1,0:T(8,128)(2,1)S(1)}, bf16[10,96,128]{2,1,0:T(8,128)(2,1)S(1)}) custom-call(s32[86]{0:T(128)S(1)} %concatenate.22.starts.scalars, bf16[128,2560]{1,0:T(8,128)(2,1)S(1)} %constant_dynamic-update-slice_fusion.near, ...), custom_call_target="tpu_custom_call" | custom-call | tf_op jit(solution)/shard_map/backward/pallas_call | solution.py:201
  39.3 2.6 %collective-permute-start.16 = (bf16[10,96,128]{2,1,0:T(8,128)(2,1)S(1)}, bf16[10,96,128]{2,1,0:T(8,128)(2,1)S(1)}, u32[]{:S(2)}, u32[]{:S(2)}) collective-permute-start(bf16[10,96,128]{2,1,0:T(8,128)(2,1)S(1)} %get-tuple-element.38), channel_id=1, source_target_pairs={{0,8},{1,9},{2,10},{3,11},{4,12},{5,13},{6,14},{7,15},{8,0},{9,1},... | collective-permute-start | bytes 737288 | tf_op jit(solution)/shard_map/ppermute | solution.py:261
  41.9 0.8 %collective-permute-done.9.rest_1_ = bf16[2,32,1280]{2,1,0:T(8,128)(2,1)S(1)} collective-permute-done((bf16[2,32,1280]{2,1,0:T(8,128)(2,1)S(1)}, bf16[2,32,1280]{2,1,0:T(8,128)(2,1)S(1)}, u32[]{:S(2)}, u32[]{:S(2)}) %collective-permute-start.9) | collective-permute-done | bytes 163872 | tf_op jit(solution)/shard_map/ppermute | solution.py:261
  42.8 2.0 %collective-permute-start.17 = (bf16[10,96,128]{2,1,0:T(8,128)(2,1)S(1)}, bf16[10,96,128]{2,1,0:T(8,128)(2,1)S(1)}, u32[]{:S(2)}, u32[]{:S(2)}) collective-permute-start(bf16[10,96,128]{2,1,0:T(8,128)(2,1)S(1)} %get-tuple-element.39), channel_id=1, source_target_pairs={{0,12},{1,13},{2,14},{3,15},{4,8},{5,9},{6,10},{7,11},{8,4},{9,5},... | collective-permute-start | bytes 737288 | tf_op jit(solution)/shard_map/ppermute | solution.py:261
  44.8 7.5 %collective-permute-done.11.array = bf16[4,32,1280]{2,1,0:T(8,128)(2,1)S(1)} collective-permute-done((bf16[4,32,1280]{2,1,0:T(8,128)(2,1)S(1)}, bf16[4,32,1280]{2,1,0:T(8,128)(2,1)S(1)}, u32[]{:S(2)}, u32[]{:S(2)}) %collective-permute-start.11) | collective-permute-done | bytes 327712 | tf_op jit(solution)/shard_map/ppermute | solution.py:261
  52.4 0.6 collective-permute-start.13
  53.0 3.5 %collective-permute-done.12.rest_3_ = bf16[1,32,1280]{2,1,0:T(8,128)(2,1)S(1)} collective-permute-done((bf16[1,32,1280]{2,1,0:T(8,128)(2,1)S(1)}, bf16[1,32,1280]{2,1,0:T(8,128)(2,1)S(1)}, u32[]{:S(2)}, u32[]{:S(2)}) %collective-permute-start.12) | collective-permute-done | bytes 81952 | tf_op jit(solution)/shard_map/ppermute | solution.py:261
  56.7 1.1 %collective-permute-done.13.rest_4_ = bf16[1,32,1280]{2,1,0:T(8,128)(2,1)S(1)} collective-permute-done((bf16[1,32,1280]{2,1,0:T(8,128)(2,1)S(1)}, bf16[1,32,1280]{2,1,0:T(8,128)(2,1)S(1)}, u32[]{:S(2)}, u32[]{:S(2)}) %collective-permute-start.13) | collective-permute-done | bytes 81952 | tf_op jit(solution)/shard_map/ppermute | solution.py:261
  57.9 1.4 %join.1 = bf16[32,10240]{1,0:T(8,128)(2,1)} custom-call(s32[8]{0:T(128)S(1)} %stack.66.starts, bf16[4,32,1280]{2,1,0:T(8,128)(2,1)S(1)} %get-tuple-element.25.rest_0_, bf16[2,32,1280]{2,1,0:T(8,128)(2,1)S(1)} %collective-permute-done.9.rest_1_, bf16[2,32,1280]{2,1,0:T(8,128)(2,1)S(1)} %collective-permute-done.10.rest_2_, ...), custom_call_target="tpu_custom_call" | custom-call | tf_op jit(solution)/shard_map/join/pallas_call | solution.py:88
  59.3 0.1 collective-permute-done.16.rest_2_
  59.4 0.6 collective-permute-done.17.rest_3_
  60.0 4.1 %collective-permute-done.15.rest_1_ = bf16[10,96,128]{2,1,0:T(8,128)(2,1)S(1)} collective-permute-done((bf16[10,96,128]{2,1,0:T(8,128)(2,1)S(1)}, bf16[10,96,128]{2,1,0:T(8,128)(2,1)S(1)}, u32[]{:S(2)}, u32[]{:S(2)}) %collective-permute-start.15) | collective-permute-done | bytes 245792 | tf_op jit(solution)/shard_map/ppermute | solution.py:261
  64.1 1.1 %sum.1 = f32[2,10,96,128]{3,2,1,0:T(8,128)} custom-call(s32[1]{0:T(128)} %bitcast.15.half, f32[10,96,128]{2,1,0:T(8,128)S(1)} %get-tuple-element.36.rest_0_, bf16[10,96,128]{2,1,0:T(8,128)(2,1)S(1)} %collective-permute-done.15.rest_1_, bf16[10,96,128]{2,1,0:T(8,128)(2,1)S(1)} %collective-permute-done.16.rest_2_, ...), custom_call_target="tpu_custom_call" | custom-call | tf_op jit(solution)/shard_map/sum/pallas_call | solution.py:229
  (49 shorter events, 1.4 us)
Async XLA Ops:
  0.6 11.9 %collective-permute-start = (bf16[32,2560]{1,0:T(8,128)(2,1)}, bf16[32,2560]{1,0:T(8,128)(2,1)S(1)}, u32[]{:S(2)}, u32[]{:S(2)}) collective-permute-start(bf16[32,2560]{1,0:T(8,128)(2,1)} %param.5), channel_id=1, source_target_pairs={{0,4},{1,5},{2,6},{3,7},{4,0},{5,1},{6,2},{7,3},{8,12},{9,13},{10,... | collective-permute-start | bytes 491528 | tf_op jit(solution)/shard_map/ppermute | solution.py:261
  3.8 1.7 %copy-start.3 = (bf16[96,20,128]{2,0,1:T(8,128)(2,1)S(1)}, bf16[96,20,128]{2,0,1:T(8,128)(2,1)}, u32[]{:S(2)}) copy-start(bf16[96,20,128]{2,0,1:T(8,128)(2,1)} %param.6) | copy-start | bytes 1474564
  5.4 15.0 %collective-permute-start.3 = (bf16[4,32,1280]{2,1,0:T(8,128)(2,1)S(1)}, bf16[4,32,1280]{2,1,0:T(8,128)(2,1)S(1)}, u32[]{:S(2)}, u32[]{:S(2)}) collective-permute-start(bf16[4,32,1280]{2,1,0:T(8,128)(2,1)S(1)} %cut.2), channel_id=1, source_target_pairs={{0,4},{1,5},{2,6},{3,7},{4,0},{5,1},{6,2},{7,3},{8,12},{9,13},{10,... | collective-permute-start | bytes 983048 | tf_op jit(solution)/shard_map/ppermute | solution.py:261
  5.5 3.1 %copy-start.2 = (bf16[32,2560]{1,0:T(8,128)(2,1)S(1)}, bf16[32,2560]{1,0:T(8,128)(2,1)}, u32[]{:S(2)}) copy-start(bf16[32,2560]{1,0:T(8,128)(2,1)} %param.5) | copy-start | bytes 491524
  5.6 27.1 %collective-permute-start.5 = (bf16[10,96,128]{2,1,0:T(8,128)(2,1)S(1)}, bf16[10,96,128]{2,1,0:T(8,128)(2,1)S(1)}, u32[]{:S(2)}, u32[]{:S(2)}) collective-permute-start(bf16[10,96,128]{2,1,0:T(8,128)(2,1)S(1)} %get-tuple-element.40.rest_0_), channel_id=1, source_target_pairs={{0,8},{1,9},{2,10},{3,11},{4,12},{5,13},{6,14},{7,15},{8,0},{9,1},... | collective-permute-start | bytes 737288 | tf_op jit(solution)/shard_map/ppermute | solution.py:261
  8.6 0.7 %copy-start.4 = (s32[20,3]{0,1:T(4,128)S(1)}, s32[20,3]{0,1:T(4,128)}, u32[]{:S(2)}) copy-start(s32[20,3]{0,1:T(4,128)} %param.8) | copy-start | bytes 724
  9.5 0.7 %copy-start.5 = (s32[20]{0:T(128)S(1)}, s32[20]{0:T(128)}, u32[]{:S(2)}) copy-start(s32[20]{0:T(128)} %param.9) | copy-start | bytes 244
  11.8 0.7 %copy-start = (bf16[4,32,1280]{2,1,0:T(8,128)(2,1)}, bf16[4,32,1280]{2,1,0:T(8,128)(2,1)S(1)}, u32[]{:S(2)}) copy-start(bf16[4,32,1280]{2,1,0:T(8,128)(2,1)S(1)} %cut.3.rest_0_) | copy-start | bytes 983044
  12.6 20.1 %collective-permute-start.6 = (bf16[10,96,128]{2,1,0:T(8,128)(2,1)S(1)}, bf16[10,96,128]{2,1,0:T(8,128)(2,1)S(1)}, u32[]{:S(2)}, u32[]{:S(2)}) collective-permute-start(bf16[10,96,128]{2,1,0:T(8,128)(2,1)S(1)} %get-tuple-element.23), channel_id=1, source_target_pairs={{0,12},{1,13},{2,14},{3,15},{4,8},{5,9},{6,10},{7,11},{8,4},{9,5},... | collective-permute-start | bytes 737288 | tf_op jit(solution)/shard_map/ppermute | solution.py:261
  17.6 8.4 %collective-permute-start.1 = (bf16[64,2560]{1,0:T(8,128)(2,1)S(1)}, bf16[64,2560]{1,0:T(8,128)(2,1)S(1)}, u32[]{:S(2)}, u32[]{:S(2)}) collective-permute-start(bf16[64,2560]{1,0:T(8,128)(2,1)S(1)} %pad_maximum_fusion), channel_id=1, source_target_pairs={{0,2},{1,3},{2,0},{3,1},{4,6},{5,7},{6,4},{7,5},{8,10},{9,11},{10,... | collective-permute-start | bytes 983048 | tf_op jit(solution)/shard_map/ppermute | solution.py:261
  20.4 0.9 %slice-start.1 = ((bf16[4,32,1280]{2,1,0:T(8,128)(2,1)}), bf16[2,32,1280]{2,1,0:T(8,128)(2,1)S(1)}, s32[]{:S(2)}) async-start(bf16[4,32,1280]{2,1,0:T(8,128)(2,1)} %copy-done), calls=%async_computation.1 | async-start | bytes 327680 | tf_op jit(solution)/shard_map/slice | solution.py:247
  20.5 12.3 %collective-permute-start.4 = (bf16[10,96,128]{2,1,0:T(8,128)(2,1)S(1)}, bf16[10,96,128]{2,1,0:T(8,128)(2,1)S(1)}, u32[]{:S(2)}, u32[]{:S(2)}) collective-permute-start(bf16[10,96,128]{2,1,0:T(8,128)(2,1)S(1)} %get-tuple-element.23), channel_id=1, source_target_pairs={{0,4},{1,5},{2,6},{3,7},{4,0},{5,1},{6,2},{7,3},{8,12},{9,13},{10,... | collective-permute-start | bytes 737288 | tf_op jit(solution)/shard_map/ppermute | solution.py:261
  21.4 10.4 %collective-permute-start.7 = (bf16[4,32,1280]{2,1,0:T(8,128)(2,1)S(1)}, bf16[4,32,1280]{2,1,0:T(8,128)(2,1)S(1)}, u32[]{:S(2)}, u32[]{:S(2)}) collective-permute-start(bf16[4,32,1280]{2,1,0:T(8,128)(2,1)S(1)} %pad_maximum_fusion.1), channel_id=1, source_target_pairs={{0,2},{1,3},{2,0},{3,1},{4,6},{5,7},{6,4},{7,5},{8,10},{9,11},{10,... | collective-permute-start | bytes 983048 | tf_op jit(solution)/shard_map/ppermute | solution.py:261
  26.1 5.7 %slice-start = ((bf16[4,32,1280]{2,1,0:T(8,128)(2,1)}), bf16[1,32,1280]{2,1,0:T(8,128)(2,1)S(1)}, s32[]{:S(2)}) async-start(bf16[4,32,1280]{2,1,0:T(8,128)(2,1)} %copy-done), calls=%async_computation | async-start | bytes 163840 | tf_op jit(solution)/shard_map/slice | solution.py:247
  26.1 8.4 %collective-permute-start.2 = (bf16[128,2560]{1,0:T(8,128)(2,1)S(1)}, bf16[128,2560]{1,0:T(8,128)(2,1)S(1)}, u32[]{:S(2)}, u32[]{:S(2)}) collective-permute-start(bf16[128,2560]{1,0:T(8,128)(2,1)S(1)} %constant_dynamic-update-slice_fusion.near), channel_id=1, source_target_pairs={{0,1},{1,0},{2,3},{3,2},{4,5},{5,4},{6,7},{7,6},{8,9},{9,8},{10,11... | collective-permute-start | bytes 1966088 | tf_op jit(solution)/shard_map/ppermute | solution.py:261
  32.6 1.8 %collective-permute-start.8 = (bf16[4,32,1280]{2,1,0:T(8,128)(2,1)}, bf16[4,32,1280]{2,1,0:T(8,128)(2,1)S(1)}, u32[]{:S(2)}, u32[]{:S(2)}) collective-permute-start(bf16[4,32,1280]{2,1,0:T(8,128)(2,1)} %pad_maximum_fusion.2), channel_id=1, source_target_pairs={{0,1},{1,0},{2,3},{3,2},{4,5},{5,4},{6,7},{7,6},{8,9},{9,8},{10,11... | collective-permute-start | bytes 983048 | tf_op jit(solution)/shard_map/ppermute | solution.py:261
  32.7 1.8 %copy-start.1 = (bf16[4,32,1280]{2,1,0:T(8,128)(2,1)S(1)}, bf16[4,32,1280]{2,1,0:T(8,128)(2,1)}, u32[]{:S(2)}) copy-start(bf16[4,32,1280]{2,1,0:T(8,128)(2,1)} %copy-done) | copy-start | bytes 983044
  36.4 6.3 %collective-permute-start.9 = (bf16[2,32,1280]{2,1,0:T(8,128)(2,1)S(1)}, bf16[2,32,1280]{2,1,0:T(8,128)(2,1)S(1)}, u32[]{:S(2)}, u32[]{:S(2)}) collective-permute-start(bf16[2,32,1280]{2,1,0:T(8,128)(2,1)S(1)} %pad_maximum_fusion.3), channel_id=1, source_target_pairs={{0,2},{1,3},{2,0},{3,1},{4,6},{5,7},{6,4},{7,5},{8,10},{9,11},{10,... | collective-permute-start | bytes 491528 | tf_op jit(solution)/shard_map/ppermute | solution.py:261
  38.0 14.3 %collective-permute-start.11 = (bf16[4,32,1280]{2,1,0:T(8,128)(2,1)S(1)}, bf16[4,32,1280]{2,1,0:T(8,128)(2,1)S(1)}, u32[]{:S(2)}, u32[]{:S(2)}) collective-permute-start(bf16[4,32,1280]{2,1,0:T(8,128)(2,1)S(1)} %get-tuple-element.30), channel_id=1, source_target_pairs={{0,4},{1,5},{2,6},{3,7},{4,0},{5,1},{6,2},{7,3},{8,12},{9,13},{10,... | collective-permute-start | bytes 983048 | tf_op jit(solution)/shard_map/ppermute | solution.py:261
  39.3 20.1 %collective-permute-start.16 = (bf16[10,96,128]{2,1,0:T(8,128)(2,1)S(1)}, bf16[10,96,128]{2,1,0:T(8,128)(2,1)S(1)}, u32[]{:S(2)}, u32[]{:S(2)}) collective-permute-start(bf16[10,96,128]{2,1,0:T(8,128)(2,1)S(1)} %get-tuple-element.38), channel_id=1, source_target_pairs={{0,8},{1,9},{2,10},{3,11},{4,12},{5,13},{6,14},{7,15},{8,0},{9,1},... | collective-permute-start | bytes 737288 | tf_op jit(solution)/shard_map/ppermute | solution.py:261
  42.7 9.7 %collective-permute-start.10 = (bf16[2,32,1280]{2,1,0:T(8,128)(2,1)S(1)}, bf16[2,32,1280]{2,1,0:T(8,128)(2,1)S(1)}, u32[]{:S(2)}, u32[]{:S(2)}) collective-permute-start(bf16[2,32,1280]{2,1,0:T(8,128)(2,1)S(1)} %pad_maximum_fusion.4), channel_id=1, source_target_pairs={{0,1},{1,0},{2,3},{3,2},{4,5},{5,4},{6,7},{7,6},{8,9},{9,8},{10,11... | collective-permute-start | bytes 491528 | tf_op jit(solution)/shard_map/ppermute | solution.py:261
  42.8 17.2 %collective-permute-start.17 = (bf16[10,96,128]{2,1,0:T(8,128)(2,1)S(1)}, bf16[10,96,128]{2,1,0:T(8,128)(2,1)S(1)}, u32[]{:S(2)}, u32[]{:S(2)}) collective-permute-start(bf16[10,96,128]{2,1,0:T(8,128)(2,1)S(1)} %get-tuple-element.39), channel_id=1, source_target_pairs={{0,12},{1,13},{2,14},{3,15},{4,8},{5,9},{6,10},{7,11},{8,4},{9,5},... | collective-permute-start | bytes 737288 | tf_op jit(solution)/shard_map/ppermute | solution.py:261
  52.3 11.8 %collective-permute-start.15 = (bf16[10,96,128]{2,1,0:T(8,128)(2,1)S(1)}, bf16[10,96,128]{2,1,0:T(8,128)(2,1)S(1)}, u32[]{:S(2)}, u32[]{:S(2)}) collective-permute-start(bf16[10,96,128]{2,1,0:T(8,128)(2,1)S(1)} %get-tuple-element.37), channel_id=1, source_target_pairs={{0,4},{1,5},{2,6},{3,7},{4,0},{5,1},{6,2},{7,3},{8,12},{9,13},{10,... | collective-permute-start | bytes 737288 | tf_op jit(solution)/shard_map/ppermute | solution.py:261
  52.3 4.2 %collective-permute-start.12 = (bf16[1,32,1280]{2,1,0:T(8,128)(2,1)S(1)}, bf16[1,32,1280]{2,1,0:T(8,128)(2,1)S(1)}, u32[]{:S(2)}, u32[]{:S(2)}) collective-permute-start(bf16[1,32,1280]{2,1,0:T(8,128)(2,1)S(1)} %get-tuple-element.32), channel_id=1, source_target_pairs={{0,3},{1,2},{2,1},{3,0},{4,7},{5,6},{6,5},{7,4},{8,11},{9,10},{10,... | collective-permute-start | bytes 245768 | tf_op jit(solution)/shard_map/ppermute | solution.py:261
  52.4 5.3 %collective-permute-start.13 = (bf16[1,32,1280]{2,1,0:T(8,128)(2,1)S(1)}, bf16[1,32,1280]{2,1,0:T(8,128)(2,1)S(1)}, u32[]{:S(2)}, u32[]{:S(2)}) collective-permute-start(bf16[1,32,1280]{2,1,0:T(8,128)(2,1)S(1)} %get-tuple-element.33), channel_id=1, source_target_pairs={{0,2},{1,3},{2,0},{3,1},{4,6},{5,7},{6,4},{7,5},{8,10},{9,11},{10,... | collective-permute-start | bytes 245768 | tf_op jit(solution)/shard_map/ppermute | solution.py:261
  56.6 1.3 %collective-permute-start.14 = (bf16[1,32,1280]{2,1,0:T(8,128)(2,1)S(1)}, bf16[1,32,1280]{2,1,0:T(8,128)(2,1)S(1)}, u32[]{:S(2)}, u32[]{:S(2)}) collective-permute-start(bf16[1,32,1280]{2,1,0:T(8,128)(2,1)S(1)} %get-tuple-element.34), channel_id=1, source_target_pairs={{0,1},{1,0},{2,3},{3,2},{4,5},{5,4},{6,7},{7,6},{8,9},{9,8},{10,11... | collective-permute-start | bytes 245768 | tf_op jit(solution)/shard_map/ppermute | solution.py:261

commit v17 on v16

--- a/solution.py
+++ b/solution.py
@@ -11,6 +11,7 @@
 SLOTS = 3
 PAIR = 2
 ROWS = 16
+HOPS = 2
 DIRECT = 8
 STACK_FLOPS = 2 * 10**9
 SPLIT_FLOPS = 2 * 10**9
@@ -41,18 +42,20 @@
         copy.wait()
 
 
-def cut_kernel(starts, whole, out, sems):
-    count, _, width = out.shape
-    copy_all([(whole.at[:, pl.ds(pl.multiple_of(starts[b] * TILE, TILE), width)], out.at[b]) for b in range(count)], sems)
-
-
-def cut_call(starts, whole, count):
+def cut_kernel(starts, whole, *rest):
+    outs, sems = rest[:-1], rest[-1]
+    blocks = [out.at[b] for out in outs for b in range(out.shape[0])]
+    width = outs[0].shape[2]
+    copy_all([(whole.at[:, pl.ds(pl.multiple_of(starts[i] * TILE, TILE), width)], block) for i, block in enumerate(blocks)], sems)
+
+
+def cut_call(starts, whole, count, parts):
     rows, width = whole.shape[0], whole.shape[1] // (PAIR * count)
     return pl.pallas_call(
         cut_kernel,
-        out_shape=jax.ShapeDtypeStruct((count, rows, width), whole.dtype),
+        out_shape=[jax.ShapeDtypeStruct((count // parts, rows, width), whole.dtype)] * parts,
         in_specs=[SCALAR, ANYWHERE],
-        out_specs=ANYWHERE,
+        out_specs=[ANYWHERE] * parts,
         scratch_shapes=[pltpu.SemaphoreType.DMA((count,))],
         compiler_params=room(1),
         name="cut",
@@ -117,16 +120,19 @@
     return jnp.concatenate(picked, axis=1)
 
 
-def forward_kernel(sizes, scalars, near, far, weights, backs, home, away, slopes):
+def forward_kernel(sizes, scalars, near, far, weights, backs, home, *rest):
+    away, slopes = rest[:-1], rest[-1]
     table = Table(scalars, *sizes)
     blocks, rows, _ = backs.shape
+    part = away[0].shape[0]
+    outs = [home.at[i // PAIR] if i % PAIR == 0 else away[i // PAIR // part].at[i // PAIR % part] for i in range(blocks)]
     for s in range(weights.shape[0]):
         cols = slice(s * TILE, (s + 1) * TILE)
         pre = jnp.dot(pick(table, near, far, s), weights[s], preferred_element_type=jnp.float32)
         act, slope = gelu_and_derivative(pre)
         act = act.astype(jnp.bfloat16)
         for i in range(blocks):
-            (home, away)[i % PAIR][i // PAIR, :, cols] = act[i * rows:(i + 1) * rows]
+            outs[i][:, cols] = act[i * rows:(i + 1) * rows]
         back = backs[:, :, cols].reshape(blocks * rows, TILE)
         slopes[:, cols] = (back.astype(jnp.float32) * slope).astype(jnp.bfloat16)
 
@@ -135,30 +141,32 @@
     blocks, rows, width = backs.shape
     return pl.pallas_call(
         functools.partial(forward_kernel, sizes),
-        out_shape=[jax.ShapeDtypeStruct((blocks // PAIR, rows, width), jnp.bfloat16)] * PAIR
+        out_shape=[jax.ShapeDtypeStruct((blocks // PAIR // parts, rows, width), jnp.bfloat16) for parts in (1,) + (HOPS,) * HOPS]
         + [jax.ShapeDtypeStruct((blocks * rows, width), jnp.bfloat16)],
         in_specs=[SCALAR] + [RESIDENT] * 4,
-        out_specs=[RESIDENT] * 3,
+        out_specs=[RESIDENT] * (HOPS + 2),
         compiler_params=room(10),
         name="forward",
     )(scalars, near, far, weights, backs)
 
 
-def split_kernel(array, *outs):
-    for i, out in enumerate(outs):
-        out[0] = array[i]
-
-
-def split_call(array):
-    return pl.pallas_call(
-        split_kernel,
-        out_shape=[jax.ShapeDtypeStruct((1,) + array.shape[1:], array.dtype)] * array.shape[0],
-        in_specs=[RESIDENT],
-        out_specs=[RESIDENT] * array.shape[0],
+def split_kernel(parts, *rest):
+    blocks = [array[i] for array in rest[:parts] for i in range(array.shape[0])]
+    for block, out in zip(blocks, rest[parts:]):
+        out[0] = block
+
+
+def split_call(*arrays):
+    count = sum(array.shape[0] for array in arrays)
+    return pl.pallas_call(
+        functools.partial(split_kernel, len(arrays)),
+        out_shape=[jax.ShapeDtypeStruct((1,) + arrays[0].shape[1:], arrays[0].dtype)] * count,
+        in_specs=[RESIDENT] * len(arrays),
+        out_specs=[RESIDENT] * count,
         compiler_params=room(6),
         cost_estimate=pl.CostEstimate(flops=SPLIT_FLOPS, bytes_accessed=0, transcendentals=0),
         name="split",
-    )(array)
+    )(*arrays)
 
 
 def stack_kernel(scalars, *rest):
@@ -260,8 +268,8 @@
         pairs = [(a * tensor + b, (a ^ dz) * tensor + (b ^ dt)) for a in range(fsdp) for b in range(tensor)]
         return lax.ppermute(value, ("fsdp", "tensor"), pairs)
 
-    def exchange(arrays, steps):
-        groups, origins = [[(a, b) for b in range(tensor)] for a in range(PAIR)], [0]
+    def exchange(arrays, groups, steps):
+        origins = [0]
         for bit in steps:
             count = len(groups[0]) // 2
             arrays = arrays + [swap(take(arrays, [ref for group in groups for ref in group[count:]]), 0, bit)]
@@ -274,16 +282,15 @@
         return jnp.stack([(t ^ b) * stripes + (half ^ a) * share for a, b in steps]).astype(jnp.int32)
 
     direct = whole_tiles and fsdp <= DIRECT
-    leave = cut_call(first_tiles([(1, b) for b in range(tensor)]), cotangent, tensor)
-    arrived = swap(leave, 1, 0)
+    leave = cut_call(first_tiles([(1, b) for b in range(tensor)]), cotangent, tensor, HOPS)
+    arrived = [swap(part, 1, 0) for part in leave]
     near = swap(tokens, 1, 0)
     by_stripe = jnp.transpose(tile_weights, (1, 0, 2))
     if direct:
         same = lax.dynamic_slice_in_dim(by_stripe, half * share, share, 0)
         other = lax.dynamic_slice_in_dim(by_stripe, (1 - half) * share, share, 0)
-        middle, near = lax.optimization_barrier((other, near))
         late, arrived = lax.optimization_barrier((other, arrived))
-        pieces = [same] + [swap((late if p == 1 else middle) if p % PAIR else same, p, 0) for p in range(1, fsdp)]
+        pieces = [same] + [swap((late if p == 1 else other) if p % PAIR else same, p, 0) for p in range(1, fsdp)]
         weights = stack_call(jnp.stack([z ^ p for p in range(fsdp)]).astype(jnp.int32), pieces)
     else:
         outgoing = jnp.tile(by_stripe.reshape(PAIR, share, size, TILE), (fsdp // PAIR, 1, 1, 1))
@@ -291,27 +298,26 @@
         weights = stacks.transpose(1, 0, 2, 3).reshape(share, fsdp * size, TILE)
 
     sizes = (tensor, stripes)
+    part = tensor // HOPS
     ends = jnp.stack([half * share, z if direct else z * 0]).astype(jnp.int32)
     scalars = jnp.concatenate([first_tiles([(0, b) for b in range(tensor)]), tile_list.reshape(-1), tile_counts, ends])
-    stay = cut_call(scalars, cotangent, tensor)
+    stay, = cut_call(scalars, cotangent, tensor, 1)
     near = jnp.concatenate([tokens, near], axis=0)
     for bit in bits:
         far = swap(near, 0, bit)
         if bit > 1:
             near = jnp.concatenate([near, far], axis=0)
-    arrays, refs, origins = exchange([stay, arrived], bits)
+    arrays, refs, origins = exchange([stay, *arrived], [[(0, b) for b in range(tensor)], [(1 + i // part, i % part) for i in range(tensor)]], bits)
     backs = collect_call(arrays, refs)
-    home, away, slopes = forward_call(sizes, scalars, near, far, weights, backs)
-
-    back_home = swap(away, 1, 0)
+    home, *away, slopes = forward_call(sizes, scalars, near, far, weights, backs)
+
+    back_home = [swap(array, 1, 0) for array in away]
 
     grads = list(backward_call(sizes, scalars, near, far, slopes, fsdp if direct else 1))
     home_arrays, blocks = [home], [(0, b, (0, i)) for i, b in enumerate(origins)]
     for bit in bits:
         sent = [block for block in blocks if block[1] & bit]
         home_arrays = home_arrays + [swap(take(home_arrays, [ref for _, _, ref in sent]), 0, bit)]
-        if direct and bit == bits[0]:
-            grads[3::PAIR], home_arrays[-1] = lax.optimization_barrier((grads[3::PAIR], home_arrays[-1]))
         received = [(source ^ bit, target ^ bit, (len(home_arrays) - 1, i)) for i, (source, target, _) in enumerate(sent)]
         blocks = [block for block in blocks if not block[1] & bit] + received
 
@@ -325,7 +331,7 @@
         here = (jnp.arange(fsdp) == z)[:, None, None, None]
         total = jnp.where(here, split, arrived.astype(jnp.float32))
         total = jnp.sum(total.reshape(fsdp // PAIR, PAIR, share, size, TILE), axis=0)
-    pieces = split_call(back_home)
+    pieces = split_call(*back_home)
     order = sorted(range(tensor), key=lambda i: -origins[i])
     arrays = home_arrays + [swap(pieces[i], 0, origins[i]) if origins[i] else pieces[i] for i in order]
     refs = [ref for _, _, ref in blocks] + [(len(home_arrays) + i, 0) for i in range(tensor)]

time: 65.5 us -> 65.2 us (level)
  waiting for transfers between devices: 28.8 us -> 26.7 us
  starting transfers between devices: 21.6 us -> 23.6 us
  other arithmetic: 1.01 us -> 0.29 us
    ppermute x18 -> x20, waiting for transfers between devices: 28.8 us -> 26.7 us  [swap(): return lax.ppermute(value, ('fsdp', 'tensor'), pairs)]
    ppermute x18 -> x20, starting transfers between devices: 21.6 us -> 23.6 us  [swap(): return lax.ppermute(value, ('fsdp', 'tensor'), pairs)]
    slice x9, local copies, waits for them, and re-layouts: 0.87 us -> 0.05 us  [take(): arrays[a][low:high]]
    concatenate x4, other arithmetic: 0.84 us -> 0.11 us  [take(): return pieces[0] if len(pieces) == 1 else jnp.concatenate(pieces, axis=0)]
    dynamic_slice x1, local copies, waits for them, and re-layouts: 0.04 us -> 0.73 us  [body(): other = lax.dynamic_slice_in_dim(by_stripe, (1 - half) * share, share, 0)]
    unnamed x15 -> x19, local copies, waits for them, and re-layouts: 2.17 us -> 2.82 us
  transfers between devices with their start and end apart: 18 -> 20, of which waited for: 12 -> 9; matrix products, arithmetic and copies ran while one was open for 2% -> 2% of each run, Pallas kernels for 10% -> 10%
where the time goes in v17:
time: 65.2 us; the launch traced here: 65 us
  waiting for transfers between devices  26.7 us (41%)
  starting transfers between devices  23.6 us (36%)
  Pallas kernels  9.65 us (15%)
  local copies, waits for them, and re-layouts  3.87 us (6%)
  between operations  0.92 us (1%)
    ppermute x20, waiting for transfers between devices, swap(): return lax.ppermute(value, ('fsdp', 'tensor'), pairs)  26.7 us
    ppermute x20, starting transfers between devices, swap(): return lax.ppermute(value, ('fsdp', 'tensor'), pairs)  23.6 us
    pallas_call x2, Pallas kernels, cut_call(): pl.pallas_call(cut_kernel, out_shape=[jax.ShapeDtypeStruct((count // part...  3.18 us
    unnamed x19, local copies, waits for them, and re-layouts  2.82 us
    pallas_call x1, Pallas kernels, forward_call(): pl.pallas_call(functools.partial(forward_kernel, sizes), out_shape=[jax.S...  1.85 us
    pallas_call x1, Pallas kernels, join_call(): pl.pallas_call(functools.partial(join_kernel, refs), out_shape=jax.ShapeD...  1.44 us
    pallas_call x1, Pallas kernels, backward_call(): pl.pallas_call(functools.partial(backward_kernel, sizes), out_shape=[jax....  1.37 us
  transfers between devices with their start and end apart: 20, of which 9 were waited for; matrix products, arithmetic and copies ran while one was open for 2% of the time, Pallas kernels for 10%

profile of v17, /device:TPU:0, one launch (start us, length us, event | category | flops | bytes accessed | tf_op | source)
XLA Modules:
  0.0 65.0 jit_solution(8726616989432026763)
XLA Ops:
  0.6 3.1 %collective-permute-start = (bf16[32,2560]{1,0:T(8,128)(2,1)}, bf16[32,2560]{1,0:T(8,128)(2,1)S(1)}, u32[]{:S(2)}, u32[]{:S(2)}) collective-permute-start(bf16[32,2560]{1,0:T(8,128)(2,1)} %param.5), channel_id=1, source_target_pairs={{0,4},{1,5},{2,6},{3,7},{4,0},{5,1},{6,2},{7,3},{8,12},{9,13},{10,... | collective-permute-start | bytes 491528 | tf_op jit(solution)/shard_map/ppermute | solution.py:269
  3.8 1.6 %cut.2 = (bf16[2,32,1280]{2,1,0:T(8,128)(2,1)S(1)}, bf16[2,32,1280]{2,1,0:T(8,128)(2,1)S(1)}) custom-call(s32[4]{0:T(128)S(1)} %pad_add_fusion.1.starts, bf16[32,10240]{1,0:T(8,128)(2,1)} %whole.3), custom_call_target="tpu_custom_call" | custom-call | tf_op jit(solution)/shard_map/cut/pallas_call | solution.py:54
  5.5 2.0 %collective-permute-start.4 = (bf16[2,32,1280]{2,1,0:T(8,128)(2,1)S(1)}, bf16[2,32,1280]{2,1,0:T(8,128)(2,1)S(1)}, u32[]{:S(2)}, u32[]{:S(2)}) collective-permute-start(bf16[2,32,1280]{2,1,0:T(8,128)(2,1)S(1)} %get-tuple-element.23), channel_id=1, source_target_pairs={{0,4},{1,5},{2,6},{3,7},{4,0},{5,1},{6,2},{7,3},{8,12},{9,13},{10,... | collective-permute-start | bytes 491528 | tf_op jit(solution)/shard_map/ppermute | solution.py:269
  7.5 0.7 %dynamic-slice_bitcast_fusion = (bf16[10,96,128]{2,1,0:T(8,128)(2,1)}, bf16[10,96,128]{2,1,0:T(8,128)(2,1)S(1)}) fusion(bf16[96,20,128]{2,0,1:T(8,128)(2,1)S(1)} %copy-done.5, s32[]{:T(128)S(6)} %select_n.15, s32[]{:T(128)S(6)} %select_n.14), kind=kLoop, calls=%fused_computation.3 | loop fusion | bytes 983048 | tf_op jit(solution)/shard_map/dynamic_slice | solution.py:291
  8.2 2.5 %collective-permute-start.7 = (bf16[10,96,128]{2,1,0:T(8,128)(2,1)}, bf16[10,96,128]{2,1,0:T(8,128)(2,1)S(1)}, u32[]{:S(2)}, u32[]{:S(2)}) collective-permute-start(bf16[10,96,128]{2,1,0:T(8,128)(2,1)} %get-tuple-element.24), channel_id=1, source_target_pairs={{0,12},{1,13},{2,14},{3,15},{4,8},{5,9},{6,10},{7,11},{8,4},{9,5},... | collective-permute-start | bytes 737288 | tf_op jit(solution)/shard_map/ppermute | solution.py:269
  10.9 0.7 %copy-done.6 = s32[20,3]{0,1:T(4,128)S(1)} copy-done((s32[20,3]{0,1:T(4,128)S(1)}, s32[20,3]{0,1:T(4,128)}, u32[]{:S(2)}) %copy-start.6) | copy-done | bytes 264
  11.7 0.6 copy-done.7
  12.5 1.6 %cut.3.rest_0_ = bf16[4,32,1280]{2,1,0:T(8,128)(2,1)S(1)} custom-call(s32[86]{0:T(128)S(1)} %concatenate.22.starts.scalars, bf16[32,10240]{1,0:T(8,128)(2,1)} %whole.3), custom_call_target="tpu_custom_call" | custom-call | tf_op jit(solution)/shard_map/cut/pallas_call | solution.py:54
  14.1 0.7 %copy-done = bf16[4,32,1280]{2,1,0:T(8,128)(2,1)} copy-done((bf16[4,32,1280]{2,1,0:T(8,128)(2,1)}, bf16[4,32,1280]{2,1,0:T(8,128)(2,1)S(1)}, u32[]{:S(2)}) %copy-start) | copy-done | bytes 327704
  14.8 1.6 %collective-permute-start.1 = (bf16[64,2560]{1,0:T(8,128)(2,1)S(1)}, bf16[64,2560]{1,0:T(8,128)(2,1)S(1)}, u32[]{:S(2)}, u32[]{:S(2)}) collective-permute-start(bf16[64,2560]{1,0:T(8,128)(2,1)S(1)} %pad_maximum_fusion), channel_id=1, source_target_pairs={{0,2},{1,3},{2,0},{3,1},{4,6},{5,7},{6,4},{7,5},{8,10},{9,11},{10,... | collective-permute-start | bytes 983048 | tf_op jit(solution)/shard_map/ppermute | solution.py:269
  17.0 1.8 %collective-permute-start.5 = (bf16[10,96,128]{2,1,0:T(8,128)(2,1)}, bf16[10,96,128]{2,1,0:T(8,128)(2,1)S(1)}, u32[]{:S(2)}, u32[]{:S(2)}) collective-permute-start(bf16[10,96,128]{2,1,0:T(8,128)(2,1)} %get-tuple-element.24), channel_id=1, source_target_pairs={{0,4},{1,5},{2,6},{3,7},{4,0},{5,1},{6,2},{7,3},{8,12},{9,13},{10,... | collective-permute-start | bytes 737288 | tf_op jit(solution)/shard_map/ppermute | solution.py:269
  18.9 0.8 %collective-permute-start.8 = (bf16[4,32,1280]{2,1,0:T(8,128)(2,1)S(1)}, bf16[4,32,1280]{2,1,0:T(8,128)(2,1)S(1)}, u32[]{:S(2)}, u32[]{:S(2)}) collective-permute-start(bf16[4,32,1280]{2,1,0:T(8,128)(2,1)S(1)} %pad_maximum_fusion.1), channel_id=1, source_target_pairs={{0,2},{1,3},{2,0},{3,1},{4,6},{5,7},{6,4},{7,5},{8,10},{9,11},{10,... | collective-permute-start | bytes 983048 | tf_op jit(solution)/shard_map/ppermute | solution.py:269
  19.7 5.9 %collective-permute-done.1 = bf16[64,2560]{1,0:T(8,128)(2,1)S(1)} collective-permute-done((bf16[64,2560]{1,0:T(8,128)(2,1)S(1)}, bf16[64,2560]{1,0:T(8,128)(2,1)S(1)}, u32[]{:S(2)}, u32[]{:S(2)}) %collective-permute-start.1) | collective-permute-done | bytes 327712 | tf_op jit(solution)/shard_map/ppermute | solution.py:269
  25.7 4.6 %collective-permute-done.8.rest_3_ = bf16[4,32,1280]{2,1,0:T(8,128)(2,1)S(1)} collective-permute-done((bf16[4,32,1280]{2,1,0:T(8,128)(2,1)S(1)}, bf16[4,32,1280]{2,1,0:T(8,128)(2,1)S(1)}, u32[]{:S(2)}, u32[]{:S(2)}) %collective-permute-start.8) | collective-permute-done | bytes 327712 | tf_op jit(solution)/shard_map/ppermute | solution.py:269
  30.5 1.5 %collective-permute-done.6.rest_2_ = bf16[10,96,128]{2,1,0:T(8,128)(2,1)S(1)} collective-permute-done((bf16[10,96,128]{2,1,0:T(8,128)(2,1)S(1)}, bf16[10,96,128]{2,1,0:T(8,128)(2,1)S(1)}, u32[]{:S(2)}, u32[]{:S(2)}) %collective-permute-start.6) | collective-permute-done | bytes 245792 | tf_op jit(solution)/shard_map/ppermute | solution.py:269
  32.7 1.9 %forward.1 = (bf16[4,32,1280]{2,1,0:T(8,128)(2,1)S(1)}, bf16[2,32,1280]{2,1,0:T(8,128)(2,1)S(1)}, bf16[2,32,1280]{2,1,0:T(8,128)(2,1)S(1)}, bf16[256,1280]{1,0:T(8,128)(2,1)S(1)}) custom-call(s32[86]{0:T(128)S(1)} %concatenate.22.starts.scalars, bf16[128,2560]{1,0:T(8,128)(2,1)S(1)} %constant_dynamic-update-slice_fusion.near, ...), custom_call_target="tpu_custom_call" | custom-call | tf_op jit(solution)/shard_map/forward/pallas_call | solution.py:142
  34.5 1.0 %collective-permute-start.12 = (bf16[2,32,1280]{2,1,0:T(8,128)(2,1)S(1)}, bf16[2,32,1280]{2,1,0:T(8,128)(2,1)S(1)}, u32[]{:S(2)}, u32[]{:S(2)}) collective-permute-start(bf16[2,32,1280]{2,1,0:T(8,128)(2,1)S(1)} %get-tuple-element.30), channel_id=1, source_target_pairs={{0,4},{1,5},{2,6},{3,7},{4,0},{5,1},{6,2},{7,3},{8,12},{9,13},{10,... | collective-permute-start | bytes 491528 | tf_op jit(solution)/shard_map/ppermute | solution.py:269
  35.5 1.1 %collective-permute-start.13 = (bf16[2,32,1280]{2,1,0:T(8,128)(2,1)S(1)}, bf16[2,32,1280]{2,1,0:T(8,128)(2,1)S(1)}, u32[]{:S(2)}, u32[]{:S(2)}) collective-permute-start(bf16[2,32,1280]{2,1,0:T(8,128)(2,1)S(1)} %get-tuple-element.31), channel_id=1, source_target_pairs={{0,4},{1,5},{2,6},{3,7},{4,0},{5,1},{6,2},{7,3},{8,12},{9,13},{10,... | collective-permute-start | bytes 491528 | tf_op jit(solution)/shard_map/ppermute | solution.py:269
  36.7 1.5 %collective-permute-start.10 = (bf16[2,32,1280]{2,1,0:T(8,128)(2,1)S(1)}, bf16[2,32,1280]{2,1,0:T(8,128)(2,1)S(1)}, u32[]{:S(2)}, u32[]{:S(2)}) collective-permute-start(bf16[2,32,1280]{2,1,0:T(8,128)(2,1)S(1)} %pad_maximum_fusion.3), channel_id=1, source_target_pairs={{0,2},{1,3},{2,0},{3,1},{4,6},{5,7},{6,4},{7,5},{8,10},{9,11},{10,... | collective-permute-start | bytes 491528 | tf_op jit(solution)/shard_map/ppermute | solution.py:269
  38.2 1.4 %backward.1 = (f32[10,96,128]{2,1,0:T(8,128)S(1)}, bf16[10,96,128]{2,1,0:T(8,128)(2,1)S(1)}, bf16[10,96,128]{2,1,0:T(8,128)(2,1)S(1)}, bf16[10,96,128]{2,1,0:T(8,128)(2,1)S(1)}) custom-call(s32[86]{0:T(128)S(1)} %concatenate.22.starts.scalars, bf16[128,2560]{1,0:T(8,128)(2,1)S(1)} %constant_dynamic-update-slice_fusion.near, ...), custom_call_target="tpu_custom_call" | custom-call | tf_op jit(solution)/shard_map/backward/pallas_call | solution.py:209
  39.6 3.3 %collective-permute-start.18 = (bf16[10,96,128]{2,1,0:T(8,128)(2,1)S(1)}, bf16[10,96,128]{2,1,0:T(8,128)(2,1)S(1)}, u32[]{:S(2)}, u32[]{:S(2)}) collective-permute-start(bf16[10,96,128]{2,1,0:T(8,128)(2,1)S(1)} %get-tuple-element.40), channel_id=1, source_target_pairs={{0,8},{1,9},{2,10},{3,11},{4,12},{5,13},{6,14},{7,15},{8,0},{9,1},... | collective-permute-start | bytes 737288 | tf_op jit(solution)/shard_map/ppermute | solution.py:269
  42.8 1.4 %collective-permute-start.19 = (bf16[10,96,128]{2,1,0:T(8,128)(2,1)S(1)}, bf16[10,96,128]{2,1,0:T(8,128)(2,1)S(1)}, u32[]{:S(2)}, u32[]{:S(2)}) collective-permute-start(bf16[10,96,128]{2,1,0:T(8,128)(2,1)S(1)} %get-tuple-element.41), channel_id=1, source_target_pairs={{0,12},{1,13},{2,14},{3,15},{4,8},{5,9},{6,10},{7,11},{8,4},{9,5},... | collective-permute-start | bytes 737288 | tf_op jit(solution)/shard_map/ppermute | solution.py:269
  44.2 3.3 %collective-permute-done.13.rest_1_ = bf16[2,32,1280]{2,1,0:T(8,128)(2,1)S(1)} collective-permute-done((bf16[2,32,1280]{2,1,0:T(8,128)(2,1)S(1)}, bf16[2,32,1280]{2,1,0:T(8,128)(2,1)S(1)}, u32[]{:S(2)}, u32[]{:S(2)}) %collective-permute-start.13) | collective-permute-done | bytes 163872 | tf_op jit(solution)/shard_map/ppermute | solution.py:269
  47.7 2.2 %collective-permute-start.15 = (bf16[1,32,1280]{2,1,0:T(8,128)(2,1)S(1)}, bf16[1,32,1280]{2,1,0:T(8,128)(2,1)S(1)}, u32[]{:S(2)}, u32[]{:S(2)}) collective-permute-start(bf16[1,32,1280]{2,1,0:T(8,128)(2,1)S(1)} %get-tuple-element.35), channel_id=1, source_target_pairs={{0,2},{1,3},{2,0},{3,1},{4,6},{5,7},{6,4},{7,5},{8,10},{9,11},{10,... | collective-permute-start | bytes 245768 | tf_op jit(solution)/shard_map/ppermute | solution.py:269
  49.9 1.9 %collective-permute-done.14.rest_3_ = bf16[1,32,1280]{2,1,0:T(8,128)(2,1)S(1)} collective-permute-done((bf16[1,32,1280]{2,1,0:T(8,128)(2,1)S(1)}, bf16[1,32,1280]{2,1,0:T(8,128)(2,1)S(1)}, u32[]{:S(2)}, u32[]{:S(2)}) %collective-permute-start.14) | collective-permute-done | bytes 81952 | tf_op jit(solution)/shard_map/ppermute | solution.py:269
  51.8 0.8 %collective-permute-start.11 = (bf16[2,32,1280]{2,1,0:T(8,128)(2,1)S(1)}, bf16[2,32,1280]{2,1,0:T(8,128)(2,1)S(1)}, u32[]{:S(2)}, u32[]{:S(2)}) collective-permute-start(bf16[2,32,1280]{2,1,0:T(8,128)(2,1)S(1)} %pad_maximum_fusion.4), channel_id=1, source_target_pairs={{0,1},{1,0},{2,3},{3,2},{4,5},{5,4},{6,7},{7,6},{8,9},{9,8},{10,11... | collective-permute-start | bytes 491528 | tf_op jit(solution)/shard_map/ppermute | solution.py:269
  52.5 1.5 %collective-permute-done.15.rest_4_ = bf16[1,32,1280]{2,1,0:T(8,128)(2,1)S(1)} collective-permute-done((bf16[1,32,1280]{2,1,0:T(8,128)(2,1)S(1)}, bf16[1,32,1280]{2,1,0:T(8,128)(2,1)S(1)}, u32[]{:S(2)}, u32[]{:S(2)}) %collective-permute-start.15) | collective-permute-done | bytes 81952 | tf_op jit(solution)/shard_map/ppermute | solution.py:269
  54.4 1.0 %collective-permute-done.16.rest_5_ = bf16[1,32,1280]{2,1,0:T(8,128)(2,1)S(1)} collective-permute-done((bf16[1,32,1280]{2,1,0:T(8,128)(2,1)S(1)}, bf16[1,32,1280]{2,1,0:T(8,128)(2,1)S(1)}, u32[]{:S(2)}, u32[]{:S(2)}) %collective-permute-start.16) | collective-permute-done | bytes 81952 | tf_op jit(solution)/shard_map/ppermute | solution.py:269
  55.3 1.4 %join.1 = bf16[32,10240]{1,0:T(8,128)(2,1)} custom-call(s32[8]{0:T(128)S(1)} %stack.66.starts, bf16[4,32,1280]{2,1,0:T(8,128)(2,1)S(1)} %get-tuple-element.27.rest_0_, bf16[2,32,1280]{2,1,0:T(8,128)(2,1)S(1)} %collective-permute-done.10.rest_1_, bf16[2,32,1280]{2,1,0:T(8,128)(2,1)S(1)} %collective-permute-done.11.rest_2_, ...), custom_call_target="tpu_custom_call" | custom-call | tf_op jit(solution)/shard_map/join/pallas_call | solution.py:91
  56.8 3.5 %collective-permute-done.18.rest_2_ = bf16[10,96,128]{2,1,0:T(8,128)(2,1)S(1)} collective-permute-done((bf16[10,96,128]{2,1,0:T(8,128)(2,1)S(1)}, bf16[10,96,128]{2,1,0:T(8,128)(2,1)S(1)}, u32[]{:S(2)}, u32[]{:S(2)}) %collective-permute-start.18) | collective-permute-done | bytes 245792 | tf_op jit(solution)/shard_map/ppermute | solution.py:269
  60.3 3.6 %collective-permute-done.17.rest_1_ = bf16[10,96,128]{2,1,0:T(8,128)(2,1)S(1)} collective-permute-done((bf16[10,96,128]{2,1,0:T(8,128)(2,1)S(1)}, bf16[10,96,128]{2,1,0:T(8,128)(2,1)S(1)}, u32[]{:S(2)}, u32[]{:S(2)}) %collective-permute-start.17) | collective-permute-done | bytes 245792 | tf_op jit(solution)/shard_map/ppermute | solution.py:269
  63.9 1.1 %sum.1 = f32[2,10,96,128]{3,2,1,0:T(8,128)} custom-call(s32[1]{0:T(128)} %bitcast.15.half, f32[10,96,128]{2,1,0:T(8,128)S(1)} %get-tuple-element.38.rest_0_, bf16[10,96,128]{2,1,0:T(8,128)(2,1)S(1)} %collective-permute-done.17.rest_1_, bf16[10,96,128]{2,1,0:T(8,128)(2,1)S(1)} %collective-permute-done.18.rest_2_, ...), custom_call_target="tpu_custom_call" | custom-call | tf_op jit(solution)/shard_map/sum/pallas_call | solution.py:237
  (57 shorter events, 2.8 us)
Async XLA Ops:
  0.6 6.9 %copy-start.5 = (bf16[96,20,128]{2,0,1:T(8,128)(2,1)S(1)}, bf16[96,20,128]{2,0,1:T(8,128)(2,1)}, u32[]{:S(2)}) copy-start(bf16[96,20,128]{2,0,1:T(8,128)(2,1)} %param.6) | copy-start | bytes 1474564
  0.6 14.1 %collective-permute-start = (bf16[32,2560]{1,0:T(8,128)(2,1)}, bf16[32,2560]{1,0:T(8,128)(2,1)S(1)}, u32[]{:S(2)}, u32[]{:S(2)}) collective-permute-start(bf16[32,2560]{1,0:T(8,128)(2,1)} %param.5), channel_id=1, source_target_pairs={{0,4},{1,5},{2,6},{3,7},{4,0},{5,1},{6,2},{7,3},{8,12},{9,13},{10,... | collective-permute-start | bytes 491528 | tf_op jit(solution)/shard_map/ppermute | solution.py:269
  5.4 11.0 %collective-permute-start.3 = (bf16[2,32,1280]{2,1,0:T(8,128)(2,1)S(1)}, bf16[2,32,1280]{2,1,0:T(8,128)(2,1)S(1)}, u32[]{:S(2)}, u32[]{:S(2)}) collective-permute-start(bf16[2,32,1280]{2,1,0:T(8,128)(2,1)S(1)} %get-tuple-element.22), channel_id=1, source_target_pairs={{0,4},{1,5},{2,6},{3,7},{4,0},{5,1},{6,2},{7,3},{8,12},{9,13},{10,... | collective-permute-start | bytes 491528 | tf_op jit(solution)/shard_map/ppermute | solution.py:269
  5.5 10.9 %collective-permute-start.4 = (bf16[2,32,1280]{2,1,0:T(8,128)(2,1)S(1)}, bf16[2,32,1280]{2,1,0:T(8,128)(2,1)S(1)}, u32[]{:S(2)}, u32[]{:S(2)}) collective-permute-start(bf16[2,32,1280]{2,1,0:T(8,128)(2,1)S(1)} %get-tuple-element.23), channel_id=1, source_target_pairs={{0,4},{1,5},{2,6},{3,7},{4,0},{5,1},{6,2},{7,3},{8,12},{9,13},{10,... | collective-permute-start | bytes 491528 | tf_op jit(solution)/shard_map/ppermute | solution.py:269
  7.5 3.3 %copy-start.4 = (bf16[32,2560]{1,0:T(8,128)(2,1)S(1)}, bf16[32,2560]{1,0:T(8,128)(2,1)}, u32[]{:S(2)}) copy-start(bf16[32,2560]{1,0:T(8,128)(2,1)} %param.5) | copy-start | bytes 491524
  8.2 22.3 %collective-permute-start.7 = (bf16[10,96,128]{2,1,0:T(8,128)(2,1)}, bf16[10,96,128]{2,1,0:T(8,128)(2,1)S(1)}, u32[]{:S(2)}, u32[]{:S(2)}) collective-permute-start(bf16[10,96,128]{2,1,0:T(8,128)(2,1)} %get-tuple-element.24), channel_id=1, source_target_pairs={{0,12},{1,13},{2,14},{3,15},{4,8},{5,9},{6,10},{7,11},{8,4},{9,5},... | collective-permute-start | bytes 737288 | tf_op jit(solution)/shard_map/ppermute | solution.py:269
  10.7 21.3 %collective-permute-start.6 = (bf16[10,96,128]{2,1,0:T(8,128)(2,1)S(1)}, bf16[10,96,128]{2,1,0:T(8,128)(2,1)S(1)}, u32[]{:S(2)}, u32[]{:S(2)}) collective-permute-start(bf16[10,96,128]{2,1,0:T(8,128)(2,1)S(1)} %get-tuple-element.43.rest_0_), channel_id=1, source_target_pairs={{0,8},{1,9},{2,10},{3,11},{4,12},{5,13},{6,14},{7,15},{8,0},{9,1},... | collective-permute-start | bytes 737288 | tf_op jit(solution)/shard_map/ppermute | solution.py:269
  10.8 0.7 %copy-start.6 = (s32[20,3]{0,1:T(4,128)S(1)}, s32[20,3]{0,1:T(4,128)}, u32[]{:S(2)}) copy-start(s32[20,3]{0,1:T(4,128)} %param.8) | copy-start | bytes 724
  11.7 0.7 %copy-start.7 = (s32[20]{0:T(128)S(1)}, s32[20]{0:T(128)}, u32[]{:S(2)}) copy-start(s32[20]{0:T(128)} %param.9) | copy-start | bytes 244
  14.1 0.7 %copy-start = (bf16[4,32,1280]{2,1,0:T(8,128)(2,1)}, bf16[4,32,1280]{2,1,0:T(8,128)(2,1)S(1)}, u32[]{:S(2)}) copy-start(bf16[4,32,1280]{2,1,0:T(8,128)(2,1)S(1)} %cut.3.rest_0_) | copy-start | bytes 983044
  14.8 4.0 %slice-start.1 = ((bf16[4,32,1280]{2,1,0:T(8,128)(2,1)}), bf16[2,32,1280]{2,1,0:T(8,128)(2,1)S(1)}, s32[]{:S(2)}) async-start(bf16[4,32,1280]{2,1,0:T(8,128)(2,1)} %copy-done), calls=%async_computation.1 | async-start | bytes 327680 | tf_op jit(solution)/shard_map/slice | solution.py:255
  14.8 10.7 %collective-permute-start.1 = (bf16[64,2560]{1,0:T(8,128)(2,1)S(1)}, bf16[64,2560]{1,0:T(8,128)(2,1)S(1)}, u32[]{:S(2)}, u32[]{:S(2)}) collective-permute-start(bf16[64,2560]{1,0:T(8,128)(2,1)S(1)} %pad_maximum_fusion), channel_id=1, source_target_pairs={{0,2},{1,3},{2,0},{3,1},{4,6},{5,7},{6,4},{7,5},{8,10},{9,11},{10,... | collective-permute-start | bytes 983048 | tf_op jit(solution)/shard_map/ppermute | solution.py:269
  16.4 0.7 %copy-start.2 = (bf16[2,32,1280]{2,1,0:T(8,128)(2,1)}, bf16[2,32,1280]{2,1,0:T(8,128)(2,1)S(1)}, u32[]{:S(2)}) copy-start(bf16[2,32,1280]{2,1,0:T(8,128)(2,1)S(1)} %collective-permute-done.3.rest_1_) | copy-start | bytes 491524
  17.0 14.9 %collective-permute-start.5 = (bf16[10,96,128]{2,1,0:T(8,128)(2,1)}, bf16[10,96,128]{2,1,0:T(8,128)(2,1)S(1)}, u32[]{:S(2)}, u32[]{:S(2)}) collective-permute-start(bf16[10,96,128]{2,1,0:T(8,128)(2,1)} %get-tuple-element.24), channel_id=1, source_target_pairs={{0,4},{1,5},{2,6},{3,7},{4,0},{5,1},{6,2},{7,3},{8,12},{9,13},{10,... | collective-permute-start | bytes 737288 | tf_op jit(solution)/shard_map/ppermute | solution.py:269
  18.9 11.4 %collective-permute-start.8 = (bf16[4,32,1280]{2,1,0:T(8,128)(2,1)S(1)}, bf16[4,32,1280]{2,1,0:T(8,128)(2,1)S(1)}, u32[]{:S(2)}, u32[]{:S(2)}) collective-permute-start(bf16[4,32,1280]{2,1,0:T(8,128)(2,1)S(1)} %pad_maximum_fusion.1), channel_id=1, source_target_pairs={{0,2},{1,3},{2,0},{3,1},{4,6},{5,7},{6,4},{7,5},{8,10},{9,11},{10,... | collective-permute-start | bytes 983048 | tf_op jit(solution)/shard_map/ppermute | solution.py:269
  25.6 4.7 %slice-start = ((bf16[4,32,1280]{2,1,0:T(8,128)(2,1)}), bf16[1,32,1280]{2,1,0:T(8,128)(2,1)S(1)}, s32[]{:S(2)}) async-start(bf16[4,32,1280]{2,1,0:T(8,128)(2,1)} %copy-done), calls=%async_computation | async-start | bytes 163840 | tf_op jit(solution)/shard_map/slice | solution.py:255
  25.6 4.7 %slice-start.2 = ((bf16[2,32,1280]{2,1,0:T(8,128)(2,1)}), bf16[1,32,1280]{2,1,0:T(8,128)(2,1)S(1)}, s32[]{:S(2)}) async-start(bf16[2,32,1280]{2,1,0:T(8,128)(2,1)} %copy-done.2), calls=%async_computation.2 | async-start | bytes 163840 | tf_op jit(solution)/shard_map/slice | solution.py:255
  25.6 7.1 %collective-permute-start.2 = (bf16[128,2560]{1,0:T(8,128)(2,1)S(1)}, bf16[128,2560]{1,0:T(8,128)(2,1)S(1)}, u32[]{:S(2)}, u32[]{:S(2)}) collective-permute-start(bf16[128,2560]{1,0:T(8,128)(2,1)S(1)} %constant_dynamic-update-slice_fusion.near), channel_id=1, source_target_pairs={{0,1},{1,0},{2,3},{3,2},{4,5},{5,4},{6,7},{7,6},{8,9},{9,8},{10,11... | collective-permute-start | bytes 1966088 | tf_op jit(solution)/shard_map/ppermute | solution.py:269
  30.3 2.3 %collective-permute-start.9 = (bf16[4,32,1280]{2,1,0:T(8,128)(2,1)S(1)}, bf16[4,32,1280]{2,1,0:T(8,128)(2,1)S(1)}, u32[]{:S(2)}, u32[]{:S(2)}) collective-permute-start(bf16[4,32,1280]{2,1,0:T(8,128)(2,1)S(1)} %pad_maximum_fusion.2), channel_id=1, source_target_pairs={{0,1},{1,0},{2,3},{3,2},{4,5},{5,4},{6,7},{7,6},{8,9},{9,8},{10,11... | collective-permute-start | bytes 983048 | tf_op jit(solution)/shard_map/ppermute | solution.py:269
  30.5 2.1 %copy-start.1 = (bf16[4,32,1280]{2,1,0:T(8,128)(2,1)S(1)}, bf16[4,32,1280]{2,1,0:T(8,128)(2,1)}, u32[]{:S(2)}) copy-start(bf16[4,32,1280]{2,1,0:T(8,128)(2,1)} %copy-done) | copy-start | bytes 983044
  30.5 2.1 %copy-start.3 = (bf16[2,32,1280]{2,1,0:T(8,128)(2,1)S(1)}, bf16[2,32,1280]{2,1,0:T(8,128)(2,1)}, u32[]{:S(2)}) copy-start(bf16[2,32,1280]{2,1,0:T(8,128)(2,1)} %copy-done.2) | copy-start | bytes 491524
  34.5 9.7 %collective-permute-start.12 = (bf16[2,32,1280]{2,1,0:T(8,128)(2,1)S(1)}, bf16[2,32,1280]{2,1,0:T(8,128)(2,1)S(1)}, u32[]{:S(2)}, u32[]{:S(2)}) collective-permute-start(bf16[2,32,1280]{2,1,0:T(8,128)(2,1)S(1)} %get-tuple-element.30), channel_id=1, source_target_pairs={{0,4},{1,5},{2,6},{3,7},{4,0},{5,1},{6,2},{7,3},{8,12},{9,13},{10,... | collective-permute-start | bytes 491528 | tf_op jit(solution)/shard_map/ppermute | solution.py:269
  35.5 12.0 %collective-permute-start.13 = (bf16[2,32,1280]{2,1,0:T(8,128)(2,1)S(1)}, bf16[2,32,1280]{2,1,0:T(8,128)(2,1)S(1)}, u32[]{:S(2)}, u32[]{:S(2)}) collective-permute-start(bf16[2,32,1280]{2,1,0:T(8,128)(2,1)S(1)} %get-tuple-element.31), channel_id=1, source_target_pairs={{0,4},{1,5},{2,6},{3,7},{4,0},{5,1},{6,2},{7,3},{8,12},{9,13},{10,... | collective-permute-start | bytes 491528 | tf_op jit(solution)/shard_map/ppermute | solution.py:269
  36.7 13.2 %collective-permute-start.10 = (bf16[2,32,1280]{2,1,0:T(8,128)(2,1)S(1)}, bf16[2,32,1280]{2,1,0:T(8,128)(2,1)S(1)}, u32[]{:S(2)}, u32[]{:S(2)}) collective-permute-start(bf16[2,32,1280]{2,1,0:T(8,128)(2,1)S(1)} %pad_maximum_fusion.3), channel_id=1, source_target_pairs={{0,2},{1,3},{2,0},{3,1},{4,6},{5,7},{6,4},{7,5},{8,10},{9,11},{10,... | collective-permute-start | bytes 491528 | tf_op jit(solution)/shard_map/ppermute | solution.py:269
  39.6 20.7 %collective-permute-start.18 = (bf16[10,96,128]{2,1,0:T(8,128)(2,1)S(1)}, bf16[10,96,128]{2,1,0:T(8,128)(2,1)S(1)}, u32[]{:S(2)}, u32[]{:S(2)}) collective-permute-start(bf16[10,96,128]{2,1,0:T(8,128)(2,1)S(1)} %get-tuple-element.40), channel_id=1, source_target_pairs={{0,8},{1,9},{2,10},{3,11},{4,12},{5,13},{6,14},{7,15},{8,0},{9,1},... | collective-permute-start | bytes 737288 | tf_op jit(solution)/shard_map/ppermute | solution.py:269
  42.8 17.4 %collective-permute-start.19 = (bf16[10,96,128]{2,1,0:T(8,128)(2,1)S(1)}, bf16[10,96,128]{2,1,0:T(8,128)(2,1)S(1)}, u32[]{:S(2)}, u32[]{:S(2)}) collective-permute-start(bf16[10,96,128]{2,1,0:T(8,128)(2,1)S(1)} %get-tuple-element.41), channel_id=1, source_target_pairs={{0,12},{1,13},{2,14},{3,15},{4,8},{5,9},{6,10},{7,11},{8,4},{9,5},... | collective-permute-start | bytes 737288 | tf_op jit(solution)/shard_map/ppermute | solution.py:269
  47.6 4.2 %collective-permute-start.14 = (bf16[1,32,1280]{2,1,0:T(8,128)(2,1)S(1)}, bf16[1,32,1280]{2,1,0:T(8,128)(2,1)S(1)}, u32[]{:S(2)}, u32[]{:S(2)}) collective-permute-start(bf16[1,32,1280]{2,1,0:T(8,128)(2,1)S(1)} %get-tuple-element.34), channel_id=1, source_target_pairs={{0,3},{1,2},{2,1},{3,0},{4,7},{5,6},{6,5},{7,4},{8,11},{9,10},{10,... | collective-permute-start | bytes 245768 | tf_op jit(solution)/shard_map/ppermute | solution.py:269
  47.7 6.4 %collective-permute-start.15 = (bf16[1,32,1280]{2,1,0:T(8,128)(2,1)S(1)}, bf16[1,32,1280]{2,1,0:T(8,128)(2,1)S(1)}, u32[]{:S(2)}, u32[]{:S(2)}) collective-permute-start(bf16[1,32,1280]{2,1,0:T(8,128)(2,1)S(1)} %get-tuple-element.35), channel_id=1, source_target_pairs={{0,2},{1,3},{2,0},{3,1},{4,6},{5,7},{6,4},{7,5},{8,10},{9,11},{10,... | collective-permute-start | bytes 245768 | tf_op jit(solution)/shard_map/ppermute | solution.py:269
  49.9 14.0 %collective-permute-start.17 = (bf16[10,96,128]{2,1,0:T(8,128)(2,1)S(1)}, bf16[10,96,128]{2,1,0:T(8,128)(2,1)S(1)}, u32[]{:S(2)}, u32[]{:S(2)}) collective-permute-start(bf16[10,96,128]{2,1,0:T(8,128)(2,1)S(1)} %get-tuple-element.39), channel_id=1, source_target_pairs={{0,4},{1,5},{2,6},{3,7},{4,0},{5,1},{6,2},{7,3},{8,12},{9,13},{10,... | collective-permute-start | bytes 737288 | tf_op jit(solution)/shard_map/ppermute | solution.py:269
  51.8 3.6 %collective-permute-start.11 = (bf16[2,32,1280]{2,1,0:T(8,128)(2,1)S(1)}, bf16[2,32,1280]{2,1,0:T(8,128)(2,1)S(1)}, u32[]{:S(2)}, u32[]{:S(2)}) collective-permute-start(bf16[2,32,1280]{2,1,0:T(8,128)(2,1)S(1)} %pad_maximum_fusion.4), channel_id=1, source_target_pairs={{0,1},{1,0},{2,3},{3,2},{4,5},{5,4},{6,7},{7,6},{8,9},{9,8},{10,11... | collective-permute-start | bytes 491528 | tf_op jit(solution)/shard_map/ppermute | solution.py:269
  54.0 1.3 %collective-permute-start.16 = (bf16[1,32,1280]{2,1,0:T(8,128)(2,1)S(1)}, bf16[1,32,1280]{2,1,0:T(8,128)(2,1)S(1)}, u32[]{:S(2)}, u32[]{:S(2)}) collective-permute-start(bf16[1,32,1280]{2,1,0:T(8,128)(2,1)S(1)} %get-tuple-element.36), channel_id=1, source_target_pairs={{0,1},{1,0},{2,3},{3,2},{4,5},{5,4},{6,7},{7,6},{8,9},{9,8},{10,11... | collective-permute-start | bytes 245768 | tf_op jit(solution)/shard_map/ppermute | solution.py:269

commit v18 on v17

--- a/solution.py
+++ b/solution.py
@@ -12,6 +12,7 @@
 PAIR = 2
 ROWS = 16
 HOPS = 2
+AWAY = 1
 DIRECT = 8
 STACK_FLOPS = 2 * 10**9
 SPLIT_FLOPS = 2 * 10**9
@@ -141,10 +142,10 @@
     blocks, rows, width = backs.shape
     return pl.pallas_call(
         functools.partial(forward_kernel, sizes),
-        out_shape=[jax.ShapeDtypeStruct((blocks // PAIR // parts, rows, width), jnp.bfloat16) for parts in (1,) + (HOPS,) * HOPS]
+        out_shape=[jax.ShapeDtypeStruct((blocks // PAIR // parts, rows, width), jnp.bfloat16) for parts in (1,) + (AWAY,) * AWAY]
         + [jax.ShapeDtypeStruct((blocks * rows, width), jnp.bfloat16)],
         in_specs=[SCALAR] + [RESIDENT] * 4,
-        out_specs=[RESIDENT] * (HOPS + 2),
+        out_specs=[RESIDENT] * (AWAY + 2),
         compiler_params=room(10),
         name="forward",
     )(scalars, near, far, weights, backs)
@@ -315,7 +316,7 @@
 
     grads = list(backward_call(sizes, scalars, near, far, slopes, fsdp if direct else 1))
     home_arrays, blocks = [home], [(0, b, (0, i)) for i, b in enumerate(origins)]
-    for bit in bits:
+    for bit in reversed(bits):
         sent = [block for block in blocks if block[1] & bit]
         home_arrays = home_arrays + [swap(take(home_arrays, [ref for _, _, ref in sent]), 0, bit)]
         received = [(source ^ bit, target ^ bit, (len(home_arrays) - 1, i)) for i, (source, target, _) in enumerate(sent)]

time: 65.2 us -> 64.2 us (0.985)
  starting transfers between devices: 23.6 us -> 20.6 us
  waiting for transfers between devices: 26.7 us -> 28.7 us
    ppermute x20 -> x19, starting transfers between devices: 23.6 us -> 20.6 us  [swap(): return lax.ppermute(value, ('fsdp', 'tensor'), pairs)]
    ppermute x20 -> x19, waiting for transfers between devices: 26.7 us -> 28.7 us  [swap(): return lax.ppermute(value, ('fsdp', 'tensor'), pairs)]
  transfers between devices with their start and end apart: 20 -> 19, of which waited for: 9 -> 8; matrix products, arithmetic and copies ran while one was open for 2% -> 2% of each run, Pallas kernels for 10% -> 10%
where the time goes in v18:
time: 64.2 us; the launch traced here: 64 us
  waiting for transfers between devices  28.7 us (45%)
  starting transfers between devices  20.6 us (32%)
  Pallas kernels  9.65 us (15%)
  local copies, waits for them, and re-layouts  3.88 us (6%)
  between operations  0.92 us (1%)
    ppermute x19, waiting for transfers between devices, swap(): return lax.ppermute(value, ('fsdp', 'tensor'), pairs)  28.7 us
    ppermute x19, starting transfers between devices, swap(): return lax.ppermute(value, ('fsdp', 'tensor'), pairs)  20.6 us
    pallas_call x2, Pallas kernels, cut_call(): pl.pallas_call(cut_kernel, out_shape=[jax.ShapeDtypeStruct((count // part...  3.18 us
    unnamed x19, local copies, waits for them, and re-layouts  2.83 us
    pallas_call x1, Pallas kernels, forward_call(): pl.pallas_call(functools.partial(forward_kernel, sizes), out_shape=[jax.S...  1.84 us
    pallas_call x1, Pallas kernels, join_call(): pl.pallas_call(functools.partial(join_kernel, refs), out_shape=jax.ShapeD...  1.44 us
    pallas_call x1, Pallas kernels, backward_call(): pl.pallas_call(functools.partial(backward_kernel, sizes), out_shape=[jax....  1.37 us
  transfers between devices with their start and end apart: 19, of which 8 were waited for; matrix products, arithmetic and copies ran while one was open for 2% of the time, Pallas kernels for 10%

profile of v18, /device:TPU:0, one launch (start us, length us, event | category | flops | bytes accessed | tf_op | source)
XLA Modules:
  0.0 64.0 jit_solution(8298976477123406144)
XLA Ops:
  0.6 3.1 %collective-permute-start = (bf16[32,2560]{1,0:T(8,128)(2,1)}, bf16[32,2560]{1,0:T(8,128)(2,1)S(1)}, u32[]{:S(2)}, u32[]{:S(2)}) collective-permute-start(bf16[32,2560]{1,0:T(8,128)(2,1)} %param.5), channel_id=1, source_target_pairs={{0,4},{1,5},{2,6},{3,7},{4,0},{5,1},{6,2},{7,3},{8,12},{9,13},{10,... | collective-permute-start | bytes 491528 | tf_op jit(solution)/shard_map/ppermute | solution.py:270
  3.8 1.6 %cut.2 = (bf16[2,32,1280]{2,1,0:T(8,128)(2,1)S(1)}, bf16[2,32,1280]{2,1,0:T(8,128)(2,1)S(1)}) custom-call(s32[4]{0:T(128)S(1)} %pad_add_fusion.1.starts, bf16[32,10240]{1,0:T(8,128)(2,1)} %whole.3), custom_call_target="tpu_custom_call" | custom-call | tf_op jit(solution)/shard_map/cut/pallas_call | solution.py:55
  5.5 2.0 %collective-permute-start.4 = (bf16[2,32,1280]{2,1,0:T(8,128)(2,1)S(1)}, bf16[2,32,1280]{2,1,0:T(8,128)(2,1)S(1)}, u32[]{:S(2)}, u32[]{:S(2)}) collective-permute-start(bf16[2,32,1280]{2,1,0:T(8,128)(2,1)S(1)} %get-tuple-element.21), channel_id=1, source_target_pairs={{0,4},{1,5},{2,6},{3,7},{4,0},{5,1},{6,2},{7,3},{8,12},{9,13},{10,... | collective-permute-start | bytes 491528 | tf_op jit(solution)/shard_map/ppermute | solution.py:270
  7.5 0.7 %dynamic-slice_bitcast_fusion = (bf16[10,96,128]{2,1,0:T(8,128)(2,1)}, bf16[10,96,128]{2,1,0:T(8,128)(2,1)S(1)}) fusion(bf16[96,20,128]{2,0,1:T(8,128)(2,1)S(1)} %copy-done.5, s32[]{:T(128)S(6)} %select_n.15, s32[]{:T(128)S(6)} %select_n.14), kind=kLoop, calls=%fused_computation.3 | loop fusion | bytes 983048 | tf_op jit(solution)/shard_map/dynamic_slice | solution.py:292
  8.2 2.5 %collective-permute-start.7 = (bf16[10,96,128]{2,1,0:T(8,128)(2,1)}, bf16[10,96,128]{2,1,0:T(8,128)(2,1)S(1)}, u32[]{:S(2)}, u32[]{:S(2)}) collective-permute-start(bf16[10,96,128]{2,1,0:T(8,128)(2,1)} %get-tuple-element.22), channel_id=1, source_target_pairs={{0,12},{1,13},{2,14},{3,15},{4,8},{5,9},{6,10},{7,11},{8,4},{9,5},... | collective-permute-start | bytes 737288 | tf_op jit(solution)/shard_map/ppermute | solution.py:270
  10.9 0.7 %copy-done.6 = s32[20,3]{0,1:T(4,128)S(1)} copy-done((s32[20,3]{0,1:T(4,128)S(1)}, s32[20,3]{0,1:T(4,128)}, u32[]{:S(2)}) %copy-start.6) | copy-done | bytes 264
  11.7 0.6 %copy-done.7 = s32[20]{0:T(128)S(1)} copy-done((s32[20]{0:T(128)S(1)}, s32[20]{0:T(128)}, u32[]{:S(2)}) %copy-start.7) | copy-done | bytes 104
  12.5 1.6 %cut.3.rest_0_ = bf16[4,32,1280]{2,1,0:T(8,128)(2,1)S(1)} custom-call(s32[86]{0:T(128)S(1)} %concatenate.19.starts.scalars, bf16[32,10240]{1,0:T(8,128)(2,1)} %whole.3), custom_call_target="tpu_custom_call" | custom-call | tf_op jit(solution)/shard_map/cut/pallas_call | solution.py:55
  14.1 0.7 %copy-done = bf16[4,32,1280]{2,1,0:T(8,128)(2,1)} copy-done((bf16[4,32,1280]{2,1,0:T(8,128)(2,1)}, bf16[4,32,1280]{2,1,0:T(8,128)(2,1)S(1)}, u32[]{:S(2)}) %copy-start) | copy-done | bytes 327704
  14.8 1.6 %collective-permute-start.1 = (bf16[64,2560]{1,0:T(8,128)(2,1)S(1)}, bf16[64,2560]{1,0:T(8,128)(2,1)S(1)}, u32[]{:S(2)}, u32[]{:S(2)}) collective-permute-start(bf16[64,2560]{1,0:T(8,128)(2,1)S(1)} %pad_maximum_fusion), channel_id=1, source_target_pairs={{0,2},{1,3},{2,0},{3,1},{4,6},{5,7},{6,4},{7,5},{8,10},{9,11},{10,... | collective-permute-start | bytes 983048 | tf_op jit(solution)/shard_map/ppermute | solution.py:270
  16.4 0.7 %copy-done.2 = bf16[2,32,1280]{2,1,0:T(8,128)(2,1)} copy-done((bf16[2,32,1280]{2,1,0:T(8,128)(2,1)}, bf16[2,32,1280]{2,1,0:T(8,128)(2,1)S(1)}, u32[]{:S(2)}) %copy-start.2) | copy-done | bytes 163864
  17.1 1.8 %collective-permute-start.5 = (bf16[10,96,128]{2,1,0:T(8,128)(2,1)}, bf16[10,96,128]{2,1,0:T(8,128)(2,1)S(1)}, u32[]{:S(2)}, u32[]{:S(2)}) collective-permute-start(bf16[10,96,128]{2,1,0:T(8,128)(2,1)} %get-tuple-element.22), channel_id=1, source_target_pairs={{0,4},{1,5},{2,6},{3,7},{4,0},{5,1},{6,2},{7,3},{8,12},{9,13},{10,... | collective-permute-start | bytes 737288 | tf_op jit(solution)/shard_map/ppermute | solution.py:270
  18.9 0.8 %collective-permute-start.8 = (bf16[4,32,1280]{2,1,0:T(8,128)(2,1)S(1)}, bf16[4,32,1280]{2,1,0:T(8,128)(2,1)S(1)}, u32[]{:S(2)}, u32[]{:S(2)}) collective-permute-start(bf16[4,32,1280]{2,1,0:T(8,128)(2,1)S(1)} %pad_maximum_fusion.1), channel_id=1, source_target_pairs={{0,2},{1,3},{2,0},{3,1},{4,6},{5,7},{6,4},{7,5},{8,10},{9,11},{10,... | collective-permute-start | bytes 983048 | tf_op jit(solution)/shard_map/ppermute | solution.py:270
  19.7 5.9 %collective-permute-done.1 = bf16[64,2560]{1,0:T(8,128)(2,1)S(1)} collective-permute-done((bf16[64,2560]{1,0:T(8,128)(2,1)S(1)}, bf16[64,2560]{1,0:T(8,128)(2,1)S(1)}, u32[]{:S(2)}, u32[]{:S(2)}) %collective-permute-start.1) | collective-permute-done | bytes 327712 | tf_op jit(solution)/shard_map/ppermute | solution.py:270
  25.7 4.6 %collective-permute-done.8.rest_3_ = bf16[4,32,1280]{2,1,0:T(8,128)(2,1)S(1)} collective-permute-done((bf16[4,32,1280]{2,1,0:T(8,128)(2,1)S(1)}, bf16[4,32,1280]{2,1,0:T(8,128)(2,1)S(1)}, u32[]{:S(2)}, u32[]{:S(2)}) %collective-permute-start.8) | collective-permute-done | bytes 327712 | tf_op jit(solution)/shard_map/ppermute | solution.py:270
  30.5 1.5 %collective-permute-done.6.rest_2_ = bf16[10,96,128]{2,1,0:T(8,128)(2,1)S(1)} collective-permute-done((bf16[10,96,128]{2,1,0:T(8,128)(2,1)S(1)}, bf16[10,96,128]{2,1,0:T(8,128)(2,1)S(1)}, u32[]{:S(2)}, u32[]{:S(2)}) %collective-permute-start.6) | collective-permute-done | bytes 245792 | tf_op jit(solution)/shard_map/ppermute | solution.py:270
  32.0 0.6 stack.74.weights
  32.7 1.8 %forward.1 = (bf16[4,32,1280]{2,1,0:T(8,128)(2,1)S(1)}, bf16[4,32,1280]{2,1,0:T(8,128)(2,1)S(1)}, bf16[256,1280]{1,0:T(8,128)(2,1)S(1)}) custom-call(s32[86]{0:T(128)S(1)} %concatenate.19.starts.scalars, bf16[128,2560]{1,0:T(8,128)(2,1)S(1)} %constant_dynamic-update-slice_fusion.near, bf16[128,2560]{1,0:T(8,128)(2,1)S(1)} %collective-permute-done.2.far, ...), custom_call_target="tpu_custom_call" | custom-call | tf_op jit(solution)/shard_map/forward/pallas_call | solution.py:143
  34.6 1.1 %collective-permute-start.12 = (bf16[4,32,1280]{2,1,0:T(8,128)(2,1)S(1)}, bf16[4,32,1280]{2,1,0:T(8,128)(2,1)S(1)}, u32[]{:S(2)}, u32[]{:S(2)}) collective-permute-start(bf16[4,32,1280]{2,1,0:T(8,128)(2,1)S(1)} %get-tuple-element.28), channel_id=1, source_target_pairs={{0,4},{1,5},{2,6},{3,7},{4,0},{5,1},{6,2},{7,3},{8,12},{9,13},{10,... | collective-permute-start | bytes 983048 | tf_op jit(solution)/shard_map/ppermute | solution.py:270
  35.7 1.4 %backward.1 = (f32[10,96,128]{2,1,0:T(8,128)S(1)}, bf16[10,96,128]{2,1,0:T(8,128)(2,1)S(1)}, bf16[10,96,128]{2,1,0:T(8,128)(2,1)S(1)}, bf16[10,96,128]{2,1,0:T(8,128)(2,1)S(1)}) custom-call(s32[86]{0:T(128)S(1)} %concatenate.19.starts.scalars, bf16[128,2560]{1,0:T(8,128)(2,1)S(1)} %constant_dynamic-update-slice_fusion.near, ...), custom_call_target="tpu_custom_call" | custom-call | tf_op jit(solution)/shard_map/backward/pallas_call | solution.py:210
  37.1 4.1 %collective-permute-start.17 = (bf16[10,96,128]{2,1,0:T(8,128)(2,1)S(1)}, bf16[10,96,128]{2,1,0:T(8,128)(2,1)S(1)}, u32[]{:S(2)}, u32[]{:S(2)}) collective-permute-start(bf16[10,96,128]{2,1,0:T(8,128)(2,1)S(1)} %get-tuple-element.36), channel_id=1, source_target_pairs={{0,8},{1,9},{2,10},{3,11},{4,12},{5,13},{6,14},{7,15},{8,0},{9,1},... | collective-permute-start | bytes 737288 | tf_op jit(solution)/shard_map/ppermute | solution.py:270
  41.2 1.5 %collective-permute-start.11 = (bf16[2,32,1280]{2,1,0:T(8,128)(2,1)S(1)}, bf16[2,32,1280]{2,1,0:T(8,128)(2,1)S(1)}, u32[]{:S(2)}, u32[]{:S(2)}) collective-permute-start(bf16[2,32,1280]{2,1,0:T(8,128)(2,1)S(1)} %pad_maximum_fusion.3), channel_id=1, source_target_pairs={{0,2},{1,3},{2,0},{3,1},{4,6},{5,7},{6,4},{7,5},{8,10},{9,11},{10,... | collective-permute-start | bytes 491528 | tf_op jit(solution)/shard_map/ppermute | solution.py:270
  42.8 7.0 %collective-permute-done.12.rest_0_ = bf16[4,32,1280]{2,1,0:T(8,128)(2,1)S(1)} collective-permute-done((bf16[4,32,1280]{2,1,0:T(8,128)(2,1)S(1)}, bf16[4,32,1280]{2,1,0:T(8,128)(2,1)S(1)}, u32[]{:S(2)}, u32[]{:S(2)}) %collective-permute-start.12) | collective-permute-done | bytes 327712 | tf_op jit(solution)/shard_map/ppermute | solution.py:270
  49.9 0.8 %collective-permute-start.13 = (bf16[1,32,1280]{2,1,0:T(8,128)(2,1)S(1)}, bf16[1,32,1280]{2,1,0:T(8,128)(2,1)S(1)}, u32[]{:S(2)}, u32[]{:S(2)}) collective-permute-start(bf16[1,32,1280]{2,1,0:T(8,128)(2,1)S(1)} %get-tuple-element.30), channel_id=1, source_target_pairs={{0,3},{1,2},{2,1},{3,0},{4,7},{5,6},{6,5},{7,4},{8,11},{9,10},{10,... | collective-permute-start | bytes 245768 | tf_op jit(solution)/shard_map/ppermute | solution.py:270
  50.7 0.8 %collective-permute-start.14 = (bf16[1,32,1280]{2,1,0:T(8,128)(2,1)S(1)}, bf16[1,32,1280]{2,1,0:T(8,128)(2,1)S(1)}, u32[]{:S(2)}, u32[]{:S(2)}) collective-permute-start(bf16[1,32,1280]{2,1,0:T(8,128)(2,1)S(1)} %get-tuple-element.31), channel_id=1, source_target_pairs={{0,2},{1,3},{2,0},{3,1},{4,6},{5,7},{6,4},{7,5},{8,10},{9,11},{10,... | collective-permute-start | bytes 245768 | tf_op jit(solution)/shard_map/ppermute | solution.py:270
  51.5 3.2 %collective-permute-done.13.rest_3_ = bf16[1,32,1280]{2,1,0:T(8,128)(2,1)S(1)} collective-permute-done((bf16[1,32,1280]{2,1,0:T(8,128)(2,1)S(1)}, bf16[1,32,1280]{2,1,0:T(8,128)(2,1)S(1)}, u32[]{:S(2)}, u32[]{:S(2)}) %collective-permute-start.13) | collective-permute-done | bytes 81952 | tf_op jit(solution)/shard_map/ppermute | solution.py:270
  54.7 0.1 collective-permute-start.15
  54.9 1.5 %collective-permute-done.14.rest_4_ = bf16[1,32,1280]{2,1,0:T(8,128)(2,1)S(1)} collective-permute-done((bf16[1,32,1280]{2,1,0:T(8,128)(2,1)S(1)}, bf16[1,32,1280]{2,1,0:T(8,128)(2,1)S(1)}, u32[]{:S(2)}, u32[]{:S(2)}) %collective-permute-start.14) | collective-permute-done | bytes 81952 | tf_op jit(solution)/shard_map/ppermute | solution.py:270
  56.4 1.4 %join.1 = bf16[32,10240]{1,0:T(8,128)(2,1)} custom-call(s32[8]{0:T(128)S(1)} %stack.66.starts, bf16[4,32,1280]{2,1,0:T(8,128)(2,1)S(1)} %get-tuple-element.25.rest_0_, bf16[2,32,1280]{2,1,0:T(8,128)(2,1)S(1)} %collective-permute-done.10.rest_1_, bf16[2,32,1280]{2,1,0:T(8,128)(2,1)S(1)} %collective-permute-done.11.rest_2_, ...), custom_call_target="tpu_custom_call" | custom-call | tf_op jit(solution)/shard_map/join/pallas_call | solution.py:92
  57.9 0.7 %collective-permute-done.17.rest_2_ = bf16[10,96,128]{2,1,0:T(8,128)(2,1)S(1)} collective-permute-done((bf16[10,96,128]{2,1,0:T(8,128)(2,1)S(1)}, bf16[10,96,128]{2,1,0:T(8,128)(2,1)S(1)}, u32[]{:S(2)}, u32[]{:S(2)}) %collective-permute-start.17) | collective-permute-done | bytes 245792 | tf_op jit(solution)/shard_map/ppermute | solution.py:270
  58.6 4.3 %collective-permute-done.16.rest_1_ = bf16[10,96,128]{2,1,0:T(8,128)(2,1)S(1)} collective-permute-done((bf16[10,96,128]{2,1,0:T(8,128)(2,1)S(1)}, bf16[10,96,128]{2,1,0:T(8,128)(2,1)S(1)}, u32[]{:S(2)}, u32[]{:S(2)}) %collective-permute-start.16) | collective-permute-done | bytes 245792 | tf_op jit(solution)/shard_map/ppermute | solution.py:270
  62.8 1.1 %sum.1 = f32[2,10,96,128]{3,2,1,0:T(8,128)} custom-call(s32[1]{0:T(128)} %bitcast.15.half, f32[10,96,128]{2,1,0:T(8,128)S(1)} %get-tuple-element.34.rest_0_, bf16[10,96,128]{2,1,0:T(8,128)(2,1)S(1)} %collective-permute-done.16.rest_1_, bf16[10,96,128]{2,1,0:T(8,128)(2,1)S(1)} %collective-permute-done.17.rest_2_, ...), custom_call_target="tpu_custom_call" | custom-call | tf_op jit(solution)/shard_map/sum/pallas_call | solution.py:238
  (55 shorter events, 1.3 us)
Async XLA Ops:
  0.6 6.9 %copy-start.5 = (bf16[96,20,128]{2,0,1:T(8,128)(2,1)S(1)}, bf16[96,20,128]{2,0,1:T(8,128)(2,1)}, u32[]{:S(2)}) copy-start(bf16[96,20,128]{2,0,1:T(8,128)(2,1)} %param.6) | copy-start | bytes 1474564
  0.6 14.1 %collective-permute-start = (bf16[32,2560]{1,0:T(8,128)(2,1)}, bf16[32,2560]{1,0:T(8,128)(2,1)S(1)}, u32[]{:S(2)}, u32[]{:S(2)}) collective-permute-start(bf16[32,2560]{1,0:T(8,128)(2,1)} %param.5), channel_id=1, source_target_pairs={{0,4},{1,5},{2,6},{3,7},{4,0},{5,1},{6,2},{7,3},{8,12},{9,13},{10,... | collective-permute-start | bytes 491528 | tf_op jit(solution)/shard_map/ppermute | solution.py:270
  5.4 11.0 %collective-permute-start.3 = (bf16[2,32,1280]{2,1,0:T(8,128)(2,1)S(1)}, bf16[2,32,1280]{2,1,0:T(8,128)(2,1)S(1)}, u32[]{:S(2)}, u32[]{:S(2)}) collective-permute-start(bf16[2,32,1280]{2,1,0:T(8,128)(2,1)S(1)} %get-tuple-element.20), channel_id=1, source_target_pairs={{0,4},{1,5},{2,6},{3,7},{4,0},{5,1},{6,2},{7,3},{8,12},{9,13},{10,... | collective-permute-start | bytes 491528 | tf_op jit(solution)/shard_map/ppermute | solution.py:270
  5.5 10.9 %collective-permute-start.4 = (bf16[2,32,1280]{2,1,0:T(8,128)(2,1)S(1)}, bf16[2,32,1280]{2,1,0:T(8,128)(2,1)S(1)}, u32[]{:S(2)}, u32[]{:S(2)}) collective-permute-start(bf16[2,32,1280]{2,1,0:T(8,128)(2,1)S(1)} %get-tuple-element.21), channel_id=1, source_target_pairs={{0,4},{1,5},{2,6},{3,7},{4,0},{5,1},{6,2},{7,3},{8,12},{9,13},{10,... | collective-permute-start | bytes 491528 | tf_op jit(solution)/shard_map/ppermute | solution.py:270
  7.5 3.3 %copy-start.4 = (bf16[32,2560]{1,0:T(8,128)(2,1)S(1)}, bf16[32,2560]{1,0:T(8,128)(2,1)}, u32[]{:S(2)}) copy-start(bf16[32,2560]{1,0:T(8,128)(2,1)} %param.5) | copy-start | bytes 491524
  8.2 22.3 %collective-permute-start.7 = (bf16[10,96,128]{2,1,0:T(8,128)(2,1)}, bf16[10,96,128]{2,1,0:T(8,128)(2,1)S(1)}, u32[]{:S(2)}, u32[]{:S(2)}) collective-permute-start(bf16[10,96,128]{2,1,0:T(8,128)(2,1)} %get-tuple-element.22), channel_id=1, source_target_pairs={{0,12},{1,13},{2,14},{3,15},{4,8},{5,9},{6,10},{7,11},{8,4},{9,5},... | collective-permute-start | bytes 737288 | tf_op jit(solution)/shard_map/ppermute | solution.py:270
  10.7 21.3 %collective-permute-start.6 = (bf16[10,96,128]{2,1,0:T(8,128)(2,1)S(1)}, bf16[10,96,128]{2,1,0:T(8,128)(2,1)S(1)}, u32[]{:S(2)}, u32[]{:S(2)}) collective-permute-start(bf16[10,96,128]{2,1,0:T(8,128)(2,1)S(1)} %get-tuple-element.39.rest_0_), channel_id=1, source_target_pairs={{0,8},{1,9},{2,10},{3,11},{4,12},{5,13},{6,14},{7,15},{8,0},{9,1},... | collective-permute-start | bytes 737288 | tf_op jit(solution)/shard_map/ppermute | solution.py:270
  10.8 0.7 %copy-start.6 = (s32[20,3]{0,1:T(4,128)S(1)}, s32[20,3]{0,1:T(4,128)}, u32[]{:S(2)}) copy-start(s32[20,3]{0,1:T(4,128)} %param.8) | copy-start | bytes 724
  11.7 0.7 %copy-start.7 = (s32[20]{0:T(128)S(1)}, s32[20]{0:T(128)}, u32[]{:S(2)}) copy-start(s32[20]{0:T(128)} %param.9) | copy-start | bytes 244
  14.1 0.7 %copy-start = (bf16[4,32,1280]{2,1,0:T(8,128)(2,1)}, bf16[4,32,1280]{2,1,0:T(8,128)(2,1)S(1)}, u32[]{:S(2)}) copy-start(bf16[4,32,1280]{2,1,0:T(8,128)(2,1)S(1)} %cut.3.rest_0_) | copy-start | bytes 983044
  14.8 4.0 %slice-start.1 = ((bf16[4,32,1280]{2,1,0:T(8,128)(2,1)}), bf16[2,32,1280]{2,1,0:T(8,128)(2,1)S(1)}, s32[]{:S(2)}) async-start(bf16[4,32,1280]{2,1,0:T(8,128)(2,1)} %copy-done), calls=%async_computation.1 | async-start | bytes 327680 | tf_op jit(solution)/shard_map/slice | solution.py:256
  14.8 10.7 %collective-permute-start.1 = (bf16[64,2560]{1,0:T(8,128)(2,1)S(1)}, bf16[64,2560]{1,0:T(8,128)(2,1)S(1)}, u32[]{:S(2)}, u32[]{:S(2)}) collective-permute-start(bf16[64,2560]{1,0:T(8,128)(2,1)S(1)} %pad_maximum_fusion), channel_id=1, source_target_pairs={{0,2},{1,3},{2,0},{3,1},{4,6},{5,7},{6,4},{7,5},{8,10},{9,11},{10,... | collective-permute-start | bytes 983048 | tf_op jit(solution)/shard_map/ppermute | solution.py:270
  16.4 0.7 %copy-start.2 = (bf16[2,32,1280]{2,1,0:T(8,128)(2,1)}, bf16[2,32,1280]{2,1,0:T(8,128)(2,1)S(1)}, u32[]{:S(2)}) copy-start(bf16[2,32,1280]{2,1,0:T(8,128)(2,1)S(1)} %collective-permute-done.3.rest_1_) | copy-start | bytes 491524
  17.1 14.9 %collective-permute-start.5 = (bf16[10,96,128]{2,1,0:T(8,128)(2,1)}, bf16[10,96,128]{2,1,0:T(8,128)(2,1)S(1)}, u32[]{:S(2)}, u32[]{:S(2)}) collective-permute-start(bf16[10,96,128]{2,1,0:T(8,128)(2,1)} %get-tuple-element.22), channel_id=1, source_target_pairs={{0,4},{1,5},{2,6},{3,7},{4,0},{5,1},{6,2},{7,3},{8,12},{9,13},{10,... | collective-permute-start | bytes 737288 | tf_op jit(solution)/shard_map/ppermute | solution.py:270
  18.9 11.4 %collective-permute-start.8 = (bf16[4,32,1280]{2,1,0:T(8,128)(2,1)S(1)}, bf16[4,32,1280]{2,1,0:T(8,128)(2,1)S(1)}, u32[]{:S(2)}, u32[]{:S(2)}) collective-permute-start(bf16[4,32,1280]{2,1,0:T(8,128)(2,1)S(1)} %pad_maximum_fusion.1), channel_id=1, source_target_pairs={{0,2},{1,3},{2,0},{3,1},{4,6},{5,7},{6,4},{7,5},{8,10},{9,11},{10,... | collective-permute-start | bytes 983048 | tf_op jit(solution)/shard_map/ppermute | solution.py:270
  25.6 4.7 %slice-start = ((bf16[4,32,1280]{2,1,0:T(8,128)(2,1)}), bf16[1,32,1280]{2,1,0:T(8,128)(2,1)S(1)}, s32[]{:S(2)}) async-start(bf16[4,32,1280]{2,1,0:T(8,128)(2,1)} %copy-done), calls=%async_computation | async-start | bytes 163840 | tf_op jit(solution)/shard_map/slice | solution.py:256
  25.6 4.7 %slice-start.2 = ((bf16[2,32,1280]{2,1,0:T(8,128)(2,1)}), bf16[1,32,1280]{2,1,0:T(8,128)(2,1)S(1)}, s32[]{:S(2)}) async-start(bf16[2,32,1280]{2,1,0:T(8,128)(2,1)} %copy-done.2), calls=%async_computation.2 | async-start | bytes 163840 | tf_op jit(solution)/shard_map/slice | solution.py:256
  25.6 7.1 %collective-permute-start.2 = (bf16[128,2560]{1,0:T(8,128)(2,1)S(1)}, bf16[128,2560]{1,0:T(8,128)(2,1)S(1)}, u32[]{:S(2)}, u32[]{:S(2)}) collective-permute-start(bf16[128,2560]{1,0:T(8,128)(2,1)S(1)} %constant_dynamic-update-slice_fusion.near), channel_id=1, source_target_pairs={{0,1},{1,0},{2,3},{3,2},{4,5},{5,4},{6,7},{7,6},{8,9},{9,8},{10,11... | collective-permute-start | bytes 1966088 | tf_op jit(solution)/shard_map/ppermute | solution.py:270
  30.3 2.3 %collective-permute-start.9 = (bf16[4,32,1280]{2,1,0:T(8,128)(2,1)S(1)}, bf16[4,32,1280]{2,1,0:T(8,128)(2,1)S(1)}, u32[]{:S(2)}, u32[]{:S(2)}) collective-permute-start(bf16[4,32,1280]{2,1,0:T(8,128)(2,1)S(1)} %pad_maximum_fusion.2), channel_id=1, source_target_pairs={{0,1},{1,0},{2,3},{3,2},{4,5},{5,4},{6,7},{7,6},{8,9},{9,8},{10,11... | collective-permute-start | bytes 983048 | tf_op jit(solution)/shard_map/ppermute | solution.py:270
  30.5 2.1 %copy-start.1 = (bf16[4,32,1280]{2,1,0:T(8,128)(2,1)S(1)}, bf16[4,32,1280]{2,1,0:T(8,128)(2,1)}, u32[]{:S(2)}) copy-start(bf16[4,32,1280]{2,1,0:T(8,128)(2,1)} %copy-done) | copy-start | bytes 983044
  30.5 2.1 %copy-start.3 = (bf16[2,32,1280]{2,1,0:T(8,128)(2,1)S(1)}, bf16[2,32,1280]{2,1,0:T(8,128)(2,1)}, u32[]{:S(2)}) copy-start(bf16[2,32,1280]{2,1,0:T(8,128)(2,1)} %copy-done.2) | copy-start | bytes 491524
  34.6 6.7 %collective-permute-start.10 = (bf16[2,32,1280]{2,1,0:T(8,128)(2,1)S(1)}, bf16[2,32,1280]{2,1,0:T(8,128)(2,1)S(1)}, u32[]{:S(2)}, u32[]{:S(2)}) collective-permute-start(bf16[2,32,1280]{2,1,0:T(8,128)(2,1)S(1)} %slice.29), channel_id=1, source_target_pairs={{0,1},{1,0},{2,3},{3,2},{4,5},{5,4},{6,7},{7,6},{8,9},{9,8},{10,11... | collective-permute-start | bytes 491528 | tf_op jit(solution)/shard_map/ppermute | solution.py:270
  34.6 15.2 %collective-permute-start.12 = (bf16[4,32,1280]{2,1,0:T(8,128)(2,1)S(1)}, bf16[4,32,1280]{2,1,0:T(8,128)(2,1)S(1)}, u32[]{:S(2)}, u32[]{:S(2)}) collective-permute-start(bf16[4,32,1280]{2,1,0:T(8,128)(2,1)S(1)} %get-tuple-element.28), channel_id=1, source_target_pairs={{0,4},{1,5},{2,6},{3,7},{4,0},{5,1},{6,2},{7,3},{8,12},{9,13},{10,... | collective-permute-start | bytes 983048 | tf_op jit(solution)/shard_map/ppermute | solution.py:270
  37.1 21.5 %collective-permute-start.17 = (bf16[10,96,128]{2,1,0:T(8,128)(2,1)S(1)}, bf16[10,96,128]{2,1,0:T(8,128)(2,1)S(1)}, u32[]{:S(2)}, u32[]{:S(2)}) collective-permute-start(bf16[10,96,128]{2,1,0:T(8,128)(2,1)S(1)} %get-tuple-element.36), channel_id=1, source_target_pairs={{0,8},{1,9},{2,10},{3,11},{4,12},{5,13},{6,14},{7,15},{8,0},{9,1},... | collective-permute-start | bytes 737288 | tf_op jit(solution)/shard_map/ppermute | solution.py:270
  41.2 17.4 %collective-permute-start.18 = (bf16[10,96,128]{2,1,0:T(8,128)(2,1)S(1)}, bf16[10,96,128]{2,1,0:T(8,128)(2,1)S(1)}, u32[]{:S(2)}, u32[]{:S(2)}) collective-permute-start(bf16[10,96,128]{2,1,0:T(8,128)(2,1)S(1)} %get-tuple-element.37), channel_id=1, source_target_pairs={{0,12},{1,13},{2,14},{3,15},{4,8},{5,9},{6,10},{7,11},{8,4},{9,5},... | collective-permute-start | bytes 737288 | tf_op jit(solution)/shard_map/ppermute | solution.py:270
  41.2 9.4 %collective-permute-start.11 = (bf16[2,32,1280]{2,1,0:T(8,128)(2,1)S(1)}, bf16[2,32,1280]{2,1,0:T(8,128)(2,1)S(1)}, u32[]{:S(2)}, u32[]{:S(2)}) collective-permute-start(bf16[2,32,1280]{2,1,0:T(8,128)(2,1)S(1)} %pad_maximum_fusion.3), channel_id=1, source_target_pairs={{0,2},{1,3},{2,0},{3,1},{4,6},{5,7},{6,4},{7,5},{8,10},{9,11},{10,... | collective-permute-start | bytes 491528 | tf_op jit(solution)/shard_map/ppermute | solution.py:270
  49.8 13.0 %collective-permute-start.16 = (bf16[10,96,128]{2,1,0:T(8,128)(2,1)S(1)}, bf16[10,96,128]{2,1,0:T(8,128)(2,1)S(1)}, u32[]{:S(2)}, u32[]{:S(2)}) collective-permute-start(bf16[10,96,128]{2,1,0:T(8,128)(2,1)S(1)} %get-tuple-element.35), channel_id=1, source_target_pairs={{0,4},{1,5},{2,6},{3,7},{4,0},{5,1},{6,2},{7,3},{8,12},{9,13},{10,... | collective-permute-start | bytes 737288 | tf_op jit(solution)/shard_map/ppermute | solution.py:270
  49.9 4.8 %collective-permute-start.13 = (bf16[1,32,1280]{2,1,0:T(8,128)(2,1)S(1)}, bf16[1,32,1280]{2,1,0:T(8,128)(2,1)S(1)}, u32[]{:S(2)}, u32[]{:S(2)}) collective-permute-start(bf16[1,32,1280]{2,1,0:T(8,128)(2,1)S(1)} %get-tuple-element.30), channel_id=1, source_target_pairs={{0,3},{1,2},{2,1},{3,0},{4,7},{5,6},{6,5},{7,4},{8,11},{9,10},{10,... | collective-permute-start | bytes 245768 | tf_op jit(solution)/shard_map/ppermute | solution.py:270
  50.7 5.8 %collective-permute-start.14 = (bf16[1,32,1280]{2,1,0:T(8,128)(2,1)S(1)}, bf16[1,32,1280]{2,1,0:T(8,128)(2,1)S(1)}, u32[]{:S(2)}, u32[]{:S(2)}) collective-permute-start(bf16[1,32,1280]{2,1,0:T(8,128)(2,1)S(1)} %get-tuple-element.31), channel_id=1, source_target_pairs={{0,2},{1,3},{2,0},{3,1},{4,6},{5,7},{6,4},{7,5},{8,10},{9,11},{10,... | collective-permute-start | bytes 245768 | tf_op jit(solution)/shard_map/ppermute | solution.py:270
  54.7 1.8 %collective-permute-start.15 = (bf16[1,32,1280]{2,1,0:T(8,128)(2,1)S(1)}, bf16[1,32,1280]{2,1,0:T(8,128)(2,1)S(1)}, u32[]{:S(2)}, u32[]{:S(2)}) collective-permute-start(bf16[1,32,1280]{2,1,0:T(8,128)(2,1)S(1)} %get-tuple-element.32), channel_id=1, source_target_pairs={{0,1},{1,0},{2,3},{3,2},{4,5},{5,4},{6,7},{7,6},{8,9},{9,8},{10,11... | collective-permute-start | bytes 245768 | tf_op jit(solution)/shard_map/ppermute | solution.py:270

commit v19 on v18

--- a/solution.py
+++ b/solution.py
@@ -319,13 +319,14 @@
     for bit in reversed(bits):
         sent = [block for block in blocks if block[1] & bit]
         home_arrays = home_arrays + [swap(take(home_arrays, [ref for _, _, ref in sent]), 0, bit)]
+        if direct and len(home_arrays) == 2:
+            grads[1], home_arrays[1] = lax.optimization_barrier((grads[1], home_arrays[1]))
         received = [(source ^ bit, target ^ bit, (len(home_arrays) - 1, i)) for i, (source, target, _) in enumerate(sent)]
         blocks = [block for block in blocks if not block[1] & bit] + received
 
     if direct:
-        grads[1], back_home = lax.optimization_barrier((grads[1], back_home))
         across = {p: swap(grads[p], p, 0) for p in range(PAIR, fsdp, PAIR)}
-        total = sum_call(half.reshape(1).astype(jnp.int32), [grads[0]] + [across[p] if p in across else swap(grads[p], p, 0) for p in range(1, fsdp)])
+        sent = [across[p] if p in across else swap(grads[p], p, 0) for p in range(1, fsdp)]
     else:
         split = grads[0].reshape(share, fsdp, size, TILE).transpose(1, 0, 2, 3)
         arrived = lax.all_to_all(split.astype(jnp.bfloat16), "fsdp", split_axis=0, concat_axis=0, tiled=True)
@@ -337,6 +338,10 @@
     arrays = home_arrays + [swap(pieces[i], 0, origins[i]) if origins[i] else pieces[i] for i in order]
     refs = [ref for _, _, ref in blocks] + [(len(home_arrays) + i, 0) for i in range(tensor)]
     activations = join_call(first_tiles([(0, b) for b, _, _ in blocks] + [(1, origins[i]) for i in order]), arrays, refs)
+    if direct:
+        which = half.reshape(1).astype(jnp.int32)
+        activations, which = lax.optimization_barrier((activations, which))
+        total = sum_call(which, [grads[0]] + sent)
     return activations, total.reshape(stripes, size, TILE).transpose(1, 0, 2)
 
 

time: 64.2 us -> 62.3 us (0.970)
  waiting for transfers between devices: 28.7 us -> 25.8 us
    ppermute x19, waiting for transfers between devices: 28.7 us -> 25.8 us  [swap(): return lax.ppermute(value, ('fsdp', 'tensor'), pairs)]
  transfers between devices with their start and end apart: 19 -> 19, of which waited for: 8 -> 8; matrix products, arithmetic and copies ran while one was open for 2% -> 2% of each run, Pallas kernels for 10% -> 11%
where the time goes in v19:
time: 62.3 us; the launch traced here: 61.7 us
  waiting for transfers between devices  25.8 us (41%)
  starting transfers between devices  21.1 us (34%)
  Pallas kernels  9.66 us (16%)
  local copies, waits for them, and re-layouts  3.88 us (6%)
  between operations  0.92 us (1%)
    ppermute x19, waiting for transfers between devices, swap(): return lax.ppermute(value, ('fsdp', 'tensor'), pairs)  25.8 us
    ppermute x19, starting transfers between devices, swap(): return lax.ppermute(value, ('fsdp', 'tensor'), pairs)  21.1 us
    pallas_call x2, Pallas kernels, cut_call(): pl.pallas_call(cut_kernel, out_shape=[jax.ShapeDtypeStruct((count // part...  3.18 us
    unnamed x19, local copies, waits for them, and re-layouts  2.83 us
    pallas_call x1, Pallas kernels, forward_call(): pl.pallas_call(functools.partial(forward_kernel, sizes), out_shape=[jax.S...  1.86 us
    pallas_call x1, Pallas kernels, join_call(): pl.pallas_call(functools.partial(join_kernel, refs), out_shape=jax.ShapeD...  1.44 us
    pallas_call x1, Pallas kernels, backward_call(): pl.pallas_call(functools.partial(backward_kernel, sizes), out_shape=[jax....  1.36 us
  transfers between devices with their start and end apart: 19, of which 8 were waited for; matrix products, arithmetic and copies ran while one was open for 2% of the time, Pallas kernels for 11%

profile of v19, /device:TPU:0, one launch (start us, length us, event | category | flops | bytes accessed | tf_op | source)
XLA Modules:
  0.0 61.7 jit_solution(3073163360343132517)
XLA Ops:
  0.6 3.1 %collective-permute-start = (bf16[32,2560]{1,0:T(8,128)(2,1)}, bf16[32,2560]{1,0:T(8,128)(2,1)S(1)}, u32[]{:S(2)}, u32[]{:S(2)}) collective-permute-start(bf16[32,2560]{1,0:T(8,128)(2,1)} %param.5), channel_id=1, source_target_pairs={{0,4},{1,5},{2,6},{3,7},{4,0},{5,1},{6,2},{7,3},{8,12},{9,13},{10,... | collective-permute-start | bytes 491528 | tf_op jit(solution)/shard_map/ppermute | solution.py:270
  3.8 1.6 %cut.2 = (bf16[2,32,1280]{2,1,0:T(8,128)(2,1)S(1)}, bf16[2,32,1280]{2,1,0:T(8,128)(2,1)S(1)}) custom-call(s32[4]{0:T(128)S(1)} %pad_add_fusion.1.starts, bf16[32,10240]{1,0:T(8,128)(2,1)} %whole.3), custom_call_target="tpu_custom_call" | custom-call | tf_op jit(solution)/shard_map/cut/pallas_call | solution.py:55
  5.5 2.0 %collective-permute-start.4 = (bf16[2,32,1280]{2,1,0:T(8,128)(2,1)S(1)}, bf16[2,32,1280]{2,1,0:T(8,128)(2,1)S(1)}, u32[]{:S(2)}, u32[]{:S(2)}) collective-permute-start(bf16[2,32,1280]{2,1,0:T(8,128)(2,1)S(1)} %get-tuple-element.23), channel_id=1, source_target_pairs={{0,4},{1,5},{2,6},{3,7},{4,0},{5,1},{6,2},{7,3},{8,12},{9,13},{10,... | collective-permute-start | bytes 491528 | tf_op jit(solution)/shard_map/ppermute | solution.py:270
  7.5 0.7 %dynamic-slice_bitcast_fusion = (bf16[10,96,128]{2,1,0:T(8,128)(2,1)}, bf16[10,96,128]{2,1,0:T(8,128)(2,1)S(1)}) fusion(bf16[96,20,128]{2,0,1:T(8,128)(2,1)S(1)} %copy-done.5, s32[]{:T(128)S(6)} %select_n.15, s32[]{:T(128)S(6)} %select_n.14), kind=kLoop, calls=%fused_computation.3 | loop fusion | bytes 983048 | tf_op jit(solution)/shard_map/dynamic_slice | solution.py:292
  8.2 2.5 %collective-permute-start.7 = (bf16[10,96,128]{2,1,0:T(8,128)(2,1)}, bf16[10,96,128]{2,1,0:T(8,128)(2,1)S(1)}, u32[]{:S(2)}, u32[]{:S(2)}) collective-permute-start(bf16[10,96,128]{2,1,0:T(8,128)(2,1)} %get-tuple-element.24), channel_id=1, source_target_pairs={{0,12},{1,13},{2,14},{3,15},{4,8},{5,9},{6,10},{7,11},{8,4},{9,5},... | collective-permute-start | bytes 737288 | tf_op jit(solution)/shard_map/ppermute | solution.py:270
  10.9 0.7 %copy-done.6 = s32[20,3]{0,1:T(4,128)S(1)} copy-done((s32[20,3]{0,1:T(4,128)S(1)}, s32[20,3]{0,1:T(4,128)}, u32[]{:S(2)}) %copy-start.6) | copy-done | bytes 264
  11.7 0.6 %copy-done.7 = s32[20]{0:T(128)S(1)} copy-done((s32[20]{0:T(128)S(1)}, s32[20]{0:T(128)}, u32[]{:S(2)}) %copy-start.7) | copy-done | bytes 104
  12.5 1.6 %cut.3.rest_0_ = bf16[4,32,1280]{2,1,0:T(8,128)(2,1)S(1)} custom-call(s32[86]{0:T(128)S(1)} %concatenate.19.starts.scalars, bf16[32,10240]{1,0:T(8,128)(2,1)} %whole.3), custom_call_target="tpu_custom_call" | custom-call | tf_op jit(solution)/shard_map/cut/pallas_call | solution.py:55
  14.1 0.7 %copy-done = bf16[4,32,1280]{2,1,0:T(8,128)(2,1)} copy-done((bf16[4,32,1280]{2,1,0:T(8,128)(2,1)}, bf16[4,32,1280]{2,1,0:T(8,128)(2,1)S(1)}, u32[]{:S(2)}) %copy-start) | copy-done | bytes 327704
  14.8 1.6 %collective-permute-start.1 = (bf16[64,2560]{1,0:T(8,128)(2,1)S(1)}, bf16[64,2560]{1,0:T(8,128)(2,1)S(1)}, u32[]{:S(2)}, u32[]{:S(2)}) collective-permute-start(bf16[64,2560]{1,0:T(8,128)(2,1)S(1)} %pad_maximum_fusion), channel_id=1, source_target_pairs={{0,2},{1,3},{2,0},{3,1},{4,6},{5,7},{6,4},{7,5},{8,10},{9,11},{10,... | collective-permute-start | bytes 983048 | tf_op jit(solution)/shard_map/ppermute | solution.py:270
  16.4 0.7 %copy-done.2 = bf16[2,32,1280]{2,1,0:T(8,128)(2,1)} copy-done((bf16[2,32,1280]{2,1,0:T(8,128)(2,1)}, bf16[2,32,1280]{2,1,0:T(8,128)(2,1)S(1)}, u32[]{:S(2)}) %copy-start.2) | copy-done | bytes 163864
  17.1 1.8 %collective-permute-start.5 = (bf16[10,96,128]{2,1,0:T(8,128)(2,1)}, bf16[10,96,128]{2,1,0:T(8,128)(2,1)S(1)}, u32[]{:S(2)}, u32[]{:S(2)}) collective-permute-start(bf16[10,96,128]{2,1,0:T(8,128)(2,1)} %get-tuple-element.24), channel_id=1, source_target_pairs={{0,4},{1,5},{2,6},{3,7},{4,0},{5,1},{6,2},{7,3},{8,12},{9,13},{10,... | collective-permute-start | bytes 737288 | tf_op jit(solution)/shard_map/ppermute | solution.py:270
  18.9 0.8 %collective-permute-start.8 = (bf16[4,32,1280]{2,1,0:T(8,128)(2,1)S(1)}, bf16[4,32,1280]{2,1,0:T(8,128)(2,1)S(1)}, u32[]{:S(2)}, u32[]{:S(2)}) collective-permute-start(bf16[4,32,1280]{2,1,0:T(8,128)(2,1)S(1)} %pad_maximum_fusion.1), channel_id=1, source_target_pairs={{0,2},{1,3},{2,0},{3,1},{4,6},{5,7},{6,4},{7,5},{8,10},{9,11},{10,... | collective-permute-start | bytes 983048 | tf_op jit(solution)/shard_map/ppermute | solution.py:270
  19.7 5.9 %collective-permute-done.1 = bf16[64,2560]{1,0:T(8,128)(2,1)S(1)} collective-permute-done((bf16[64,2560]{1,0:T(8,128)(2,1)S(1)}, bf16[64,2560]{1,0:T(8,128)(2,1)S(1)}, u32[]{:S(2)}, u32[]{:S(2)}) %collective-permute-start.1) | collective-permute-done | bytes 327712 | tf_op jit(solution)/shard_map/ppermute | solution.py:270
  25.7 4.6 %collective-permute-done.8.rest_3_ = bf16[4,32,1280]{2,1,0:T(8,128)(2,1)S(1)} collective-permute-done((bf16[4,32,1280]{2,1,0:T(8,128)(2,1)S(1)}, bf16[4,32,1280]{2,1,0:T(8,128)(2,1)S(1)}, u32[]{:S(2)}, u32[]{:S(2)}) %collective-permute-start.8) | collective-permute-done | bytes 327712 | tf_op jit(solution)/shard_map/ppermute | solution.py:270
  30.5 1.5 %collective-permute-done.6.rest_2_ = bf16[10,96,128]{2,1,0:T(8,128)(2,1)S(1)} collective-permute-done((bf16[10,96,128]{2,1,0:T(8,128)(2,1)S(1)}, bf16[10,96,128]{2,1,0:T(8,128)(2,1)S(1)}, u32[]{:S(2)}, u32[]{:S(2)}) %collective-permute-start.6) | collective-permute-done | bytes 245792 | tf_op jit(solution)/shard_map/ppermute | solution.py:270
  32.0 0.6 stack.74.weights
  32.7 1.9 %forward.1 = (bf16[4,32,1280]{2,1,0:T(8,128)(2,1)S(1)}, bf16[4,32,1280]{2,1,0:T(8,128)(2,1)S(1)}, bf16[256,1280]{1,0:T(8,128)(2,1)S(1)}) custom-call(s32[86]{0:T(128)S(1)} %concatenate.19.starts.scalars, bf16[128,2560]{1,0:T(8,128)(2,1)S(1)} %constant_dynamic-update-slice_fusion.near, bf16[128,2560]{1,0:T(8,128)(2,1)S(1)} %collective-permute-done.2.far, ...), custom_call_target="tpu_custom_call" | custom-call | tf_op jit(solution)/shard_map/forward/pallas_call | solution.py:143
  34.7 1.0 %collective-permute-start.12 = (bf16[4,32,1280]{2,1,0:T(8,128)(2,1)S(1)}, bf16[4,32,1280]{2,1,0:T(8,128)(2,1)S(1)}, u32[]{:S(2)}, u32[]{:S(2)}) collective-permute-start(bf16[4,32,1280]{2,1,0:T(8,128)(2,1)S(1)} %get-tuple-element.31), channel_id=1, source_target_pairs={{0,4},{1,5},{2,6},{3,7},{4,0},{5,1},{6,2},{7,3},{8,12},{9,13},{10,... | collective-permute-start | bytes 983048 | tf_op jit(solution)/shard_map/ppermute | solution.py:270
  35.7 1.4 %backward.1 = (f32[10,96,128]{2,1,0:T(8,128)S(1)}, bf16[10,96,128]{2,1,0:T(8,128)(2,1)S(1)}, bf16[10,96,128]{2,1,0:T(8,128)(2,1)S(1)}, bf16[10,96,128]{2,1,0:T(8,128)(2,1)S(1)}) custom-call(s32[86]{0:T(128)S(1)} %concatenate.19.starts.scalars, bf16[128,2560]{1,0:T(8,128)(2,1)S(1)} %constant_dynamic-update-slice_fusion.near, ...), custom_call_target="tpu_custom_call" | custom-call | tf_op jit(solution)/shard_map/backward/pallas_call | solution.py:210
  37.1 4.1 %collective-permute-start.17 = (bf16[10,96,128]{2,1,0:T(8,128)(2,1)S(1)}, bf16[10,96,128]{2,1,0:T(8,128)(2,1)S(1)}, u32[]{:S(2)}, u32[]{:S(2)}) collective-permute-start(bf16[10,96,128]{2,1,0:T(8,128)(2,1)S(1)} %get-tuple-element.40), channel_id=1, source_target_pairs={{0,8},{1,9},{2,10},{3,11},{4,12},{5,13},{6,14},{7,15},{8,0},{9,1},... | collective-permute-start | bytes 737288 | tf_op jit(solution)/shard_map/ppermute | solution.py:270
  41.2 1.6 %collective-permute-start.11 = (bf16[2,32,1280]{2,1,0:T(8,128)(2,1)S(1)}, bf16[2,32,1280]{2,1,0:T(8,128)(2,1)S(1)}, u32[]{:S(2)}, u32[]{:S(2)}) collective-permute-start(bf16[2,32,1280]{2,1,0:T(8,128)(2,1)S(1)} %pad_maximum_fusion.3), channel_id=1, source_target_pairs={{0,2},{1,3},{2,0},{3,1},{4,6},{5,7},{6,4},{7,5},{8,10},{9,11},{10,... | collective-permute-start | bytes 491528 | tf_op jit(solution)/shard_map/ppermute | solution.py:270
  42.8 0.6 %collective-permute-start.16 = (bf16[10,96,128]{2,1,0:T(8,128)(2,1)S(1)}, bf16[10,96,128]{2,1,0:T(8,128)(2,1)S(1)}, u32[]{:S(2)}, u32[]{:S(2)}) collective-permute-start(bf16[10,96,128]{2,1,0:T(8,128)(2,1)S(1)} %get-tuple-element.39), channel_id=1, source_target_pairs={{0,4},{1,5},{2,6},{3,7},{4,0},{5,1},{6,2},{7,3},{8,12},{9,13},{10,... | collective-permute-start | bytes 737288 | tf_op jit(solution)/shard_map/ppermute | solution.py:270
  43.4 6.9 %collective-permute-done.12.rest_0_ = bf16[4,32,1280]{2,1,0:T(8,128)(2,1)S(1)} collective-permute-done((bf16[4,32,1280]{2,1,0:T(8,128)(2,1)S(1)}, bf16[4,32,1280]{2,1,0:T(8,128)(2,1)S(1)}, u32[]{:S(2)}, u32[]{:S(2)}) %collective-permute-start.12) | collective-permute-done | bytes 327712 | tf_op jit(solution)/shard_map/ppermute | solution.py:270
  50.3 0.3 collective-permute-start.13
  50.6 1.3 %collective-permute-start.14 = (bf16[1,32,1280]{2,1,0:T(8,128)(2,1)S(1)}, bf16[1,32,1280]{2,1,0:T(8,128)(2,1)S(1)}, u32[]{:S(2)}, u32[]{:S(2)}) collective-permute-start(bf16[1,32,1280]{2,1,0:T(8,128)(2,1)S(1)} %get-tuple-element.33), channel_id=1, source_target_pairs={{0,2},{1,3},{2,0},{3,1},{4,6},{5,7},{6,4},{7,5},{8,10},{9,11},{10,... | collective-permute-start | bytes 245768 | tf_op jit(solution)/shard_map/ppermute | solution.py:270
  51.9 3.2 %collective-permute-done.13.rest_3_ = bf16[1,32,1280]{2,1,0:T(8,128)(2,1)S(1)} collective-permute-done((bf16[1,32,1280]{2,1,0:T(8,128)(2,1)S(1)}, bf16[1,32,1280]{2,1,0:T(8,128)(2,1)S(1)}, u32[]{:S(2)}, u32[]{:S(2)}) %collective-permute-start.13) | collective-permute-done | bytes 81952 | tf_op jit(solution)/shard_map/ppermute | solution.py:270
  55.3 1.6 %collective-permute-done.14.rest_4_ = bf16[1,32,1280]{2,1,0:T(8,128)(2,1)S(1)} collective-permute-done((bf16[1,32,1280]{2,1,0:T(8,128)(2,1)S(1)}, bf16[1,32,1280]{2,1,0:T(8,128)(2,1)S(1)}, u32[]{:S(2)}, u32[]{:S(2)}) %collective-permute-start.14) | collective-permute-done | bytes 81952 | tf_op jit(solution)/shard_map/ppermute | solution.py:270
  56.9 1.4 %join.1 = bf16[32,10240]{1,0:T(8,128)(2,1)} custom-call(s32[8]{0:T(128)S(1)} %stack.66.starts, bf16[4,32,1280]{2,1,0:T(8,128)(2,1)S(1)} %get-tuple-element.27.rest_0_, bf16[2,32,1280]{2,1,0:T(8,128)(2,1)S(1)} %collective-permute-done.10.rest_1_, bf16[2,32,1280]{2,1,0:T(8,128)(2,1)S(1)} %collective-permute-done.11.rest_2_, ...), custom_call_target="tpu_custom_call" | custom-call | tf_op jit(solution)/shard_map/join/pallas_call | solution.py:92
  58.3 0.2 collective-permute-done.17.rest_2_
  58.6 2.0 %collective-permute-done.16.rest_1_ = bf16[10,96,128]{2,1,0:T(8,128)(2,1)S(1)} collective-permute-done((bf16[10,96,128]{2,1,0:T(8,128)(2,1)S(1)}, bf16[10,96,128]{2,1,0:T(8,128)(2,1)S(1)}, u32[]{:S(2)}, u32[]{:S(2)}) %collective-permute-start.16) | collective-permute-done | bytes 245792 | tf_op jit(solution)/shard_map/ppermute | solution.py:270
  60.6 1.1 %sum.1 = f32[2,10,96,128]{3,2,1,0:T(8,128)} custom-call(s32[1]{0:T(128)} %bitcast.15.half, f32[10,96,128]{2,1,0:T(8,128)S(1)} %get-tuple-element.38.rest_0_, bf16[10,96,128]{2,1,0:T(8,128)(2,1)S(1)} %collective-permute-done.16.rest_1_, bf16[10,96,128]{2,1,0:T(8,128)(2,1)S(1)} %collective-permute-done.17.rest_2_, ...), custom_call_target="tpu_custom_call" | custom-call | tf_op jit(solution)/shard_map/sum/pallas_call | solution.py:238
  (55 shorter events, 1.4 us)
Async XLA Ops:
  0.6 6.9 %copy-start.5 = (bf16[96,20,128]{2,0,1:T(8,128)(2,1)S(1)}, bf16[96,20,128]{2,0,1:T(8,128)(2,1)}, u32[]{:S(2)}) copy-start(bf16[96,20,128]{2,0,1:T(8,128)(2,1)} %param.6) | copy-start | bytes 1474564
  0.6 14.1 %collective-permute-start = (bf16[32,2560]{1,0:T(8,128)(2,1)}, bf16[32,2560]{1,0:T(8,128)(2,1)S(1)}, u32[]{:S(2)}, u32[]{:S(2)}) collective-permute-start(bf16[32,2560]{1,0:T(8,128)(2,1)} %param.5), channel_id=1, source_target_pairs={{0,4},{1,5},{2,6},{3,7},{4,0},{5,1},{6,2},{7,3},{8,12},{9,13},{10,... | collective-permute-start | bytes 491528 | tf_op jit(solution)/shard_map/ppermute | solution.py:270
  5.4 11.0 %collective-permute-start.3 = (bf16[2,32,1280]{2,1,0:T(8,128)(2,1)S(1)}, bf16[2,32,1280]{2,1,0:T(8,128)(2,1)S(1)}, u32[]{:S(2)}, u32[]{:S(2)}) collective-permute-start(bf16[2,32,1280]{2,1,0:T(8,128)(2,1)S(1)} %get-tuple-element.22), channel_id=1, source_target_pairs={{0,4},{1,5},{2,6},{3,7},{4,0},{5,1},{6,2},{7,3},{8,12},{9,13},{10,... | collective-permute-start | bytes 491528 | tf_op jit(solution)/shard_map/ppermute | solution.py:270
  5.5 10.9 %collective-permute-start.4 = (bf16[2,32,1280]{2,1,0:T(8,128)(2,1)S(1)}, bf16[2,32,1280]{2,1,0:T(8,128)(2,1)S(1)}, u32[]{:S(2)}, u32[]{:S(2)}) collective-permute-start(bf16[2,32,1280]{2,1,0:T(8,128)(2,1)S(1)} %get-tuple-element.23), channel_id=1, source_target_pairs={{0,4},{1,5},{2,6},{3,7},{4,0},{5,1},{6,2},{7,3},{8,12},{9,13},{10,... | collective-permute-start | bytes 491528 | tf_op jit(solution)/shard_map/ppermute | solution.py:270
  7.5 3.3 %copy-start.4 = (bf16[32,2560]{1,0:T(8,128)(2,1)S(1)}, bf16[32,2560]{1,0:T(8,128)(2,1)}, u32[]{:S(2)}) copy-start(bf16[32,2560]{1,0:T(8,128)(2,1)} %param.5) | copy-start | bytes 491524
  8.2 22.3 %collective-permute-start.7 = (bf16[10,96,128]{2,1,0:T(8,128)(2,1)}, bf16[10,96,128]{2,1,0:T(8,128)(2,1)S(1)}, u32[]{:S(2)}, u32[]{:S(2)}) collective-permute-start(bf16[10,96,128]{2,1,0:T(8,128)(2,1)} %get-tuple-element.24), channel_id=1, source_target_pairs={{0,12},{1,13},{2,14},{3,15},{4,8},{5,9},{6,10},{7,11},{8,4},{9,5},... | collective-permute-start | bytes 737288 | tf_op jit(solution)/shard_map/ppermute | solution.py:270
  10.7 21.3 %collective-permute-start.6 = (bf16[10,96,128]{2,1,0:T(8,128)(2,1)S(1)}, bf16[10,96,128]{2,1,0:T(8,128)(2,1)S(1)}, u32[]{:S(2)}, u32[]{:S(2)}) collective-permute-start(bf16[10,96,128]{2,1,0:T(8,128)(2,1)S(1)} %get-tuple-element.43.rest_0_), channel_id=1, source_target_pairs={{0,8},{1,9},{2,10},{3,11},{4,12},{5,13},{6,14},{7,15},{8,0},{9,1},... | collective-permute-start | bytes 737288 | tf_op jit(solution)/shard_map/ppermute | solution.py:270
  10.8 0.7 %copy-start.6 = (s32[20,3]{0,1:T(4,128)S(1)}, s32[20,3]{0,1:T(4,128)}, u32[]{:S(2)}) copy-start(s32[20,3]{0,1:T(4,128)} %param.8) | copy-start | bytes 724
  11.7 0.7 %copy-start.7 = (s32[20]{0:T(128)S(1)}, s32[20]{0:T(128)}, u32[]{:S(2)}) copy-start(s32[20]{0:T(128)} %param.9) | copy-start | bytes 244
  14.1 0.7 %copy-start = (bf16[4,32,1280]{2,1,0:T(8,128)(2,1)}, bf16[4,32,1280]{2,1,0:T(8,128)(2,1)S(1)}, u32[]{:S(2)}) copy-start(bf16[4,32,1280]{2,1,0:T(8,128)(2,1)S(1)} %cut.3.rest_0_) | copy-start | bytes 983044
  14.8 4.0 %slice-start.1 = ((bf16[4,32,1280]{2,1,0:T(8,128)(2,1)}), bf16[2,32,1280]{2,1,0:T(8,128)(2,1)S(1)}, s32[]{:S(2)}) async-start(bf16[4,32,1280]{2,1,0:T(8,128)(2,1)} %copy-done), calls=%async_computation.1 | async-start | bytes 327680 | tf_op jit(solution)/shard_map/slice | solution.py:256
  14.8 10.7 %collective-permute-start.1 = (bf16[64,2560]{1,0:T(8,128)(2,1)S(1)}, bf16[64,2560]{1,0:T(8,128)(2,1)S(1)}, u32[]{:S(2)}, u32[]{:S(2)}) collective-permute-start(bf16[64,2560]{1,0:T(8,128)(2,1)S(1)} %pad_maximum_fusion), channel_id=1, source_target_pairs={{0,2},{1,3},{2,0},{3,1},{4,6},{5,7},{6,4},{7,5},{8,10},{9,11},{10,... | collective-permute-start | bytes 983048 | tf_op jit(solution)/shard_map/ppermute | solution.py:270
  16.4 0.7 %copy-start.2 = (bf16[2,32,1280]{2,1,0:T(8,128)(2,1)}, bf16[2,32,1280]{2,1,0:T(8,128)(2,1)S(1)}, u32[]{:S(2)}) copy-start(bf16[2,32,1280]{2,1,0:T(8,128)(2,1)S(1)} %collective-permute-done.3.rest_1_) | copy-start | bytes 491524
  17.1 14.9 %collective-permute-start.5 = (bf16[10,96,128]{2,1,0:T(8,128)(2,1)}, bf16[10,96,128]{2,1,0:T(8,128)(2,1)S(1)}, u32[]{:S(2)}, u32[]{:S(2)}) collective-permute-start(bf16[10,96,128]{2,1,0:T(8,128)(2,1)} %get-tuple-element.24), channel_id=1, source_target_pairs={{0,4},{1,5},{2,6},{3,7},{4,0},{5,1},{6,2},{7,3},{8,12},{9,13},{10,... | collective-permute-start | bytes 737288 | tf_op jit(solution)/shard_map/ppermute | solution.py:270
  18.9 11.4 %collective-permute-start.8 = (bf16[4,32,1280]{2,1,0:T(8,128)(2,1)S(1)}, bf16[4,32,1280]{2,1,0:T(8,128)(2,1)S(1)}, u32[]{:S(2)}, u32[]{:S(2)}) collective-permute-start(bf16[4,32,1280]{2,1,0:T(8,128)(2,1)S(1)} %pad_maximum_fusion.1), channel_id=1, source_target_pairs={{0,2},{1,3},{2,0},{3,1},{4,6},{5,7},{6,4},{7,5},{8,10},{9,11},{10,... | collective-permute-start | bytes 983048 | tf_op jit(solution)/shard_map/ppermute | solution.py:270
  25.6 4.7 %slice-start = ((bf16[4,32,1280]{2,1,0:T(8,128)(2,1)}), bf16[1,32,1280]{2,1,0:T(8,128)(2,1)S(1)}, s32[]{:S(2)}) async-start(bf16[4,32,1280]{2,1,0:T(8,128)(2,1)} %copy-done), calls=%async_computation | async-start | bytes 163840 | tf_op jit(solution)/shard_map/slice | solution.py:256
  25.6 4.7 %slice-start.2 = ((bf16[2,32,1280]{2,1,0:T(8,128)(2,1)}), bf16[1,32,1280]{2,1,0:T(8,128)(2,1)S(1)}, s32[]{:S(2)}) async-start(bf16[2,32,1280]{2,1,0:T(8,128)(2,1)} %copy-done.2), calls=%async_computation.2 | async-start | bytes 163840 | tf_op jit(solution)/shard_map/slice | solution.py:256
  25.6 7.1 %collective-permute-start.2 = (bf16[128,2560]{1,0:T(8,128)(2,1)S(1)}, bf16[128,2560]{1,0:T(8,128)(2,1)S(1)}, u32[]{:S(2)}, u32[]{:S(2)}) collective-permute-start(bf16[128,2560]{1,0:T(8,128)(2,1)S(1)} %constant_dynamic-update-slice_fusion.near), channel_id=1, source_target_pairs={{0,1},{1,0},{2,3},{3,2},{4,5},{5,4},{6,7},{7,6},{8,9},{9,8},{10,11... | collective-permute-start | bytes 1966088 | tf_op jit(solution)/shard_map/ppermute | solution.py:270
  30.3 2.3 %collective-permute-start.9 = (bf16[4,32,1280]{2,1,0:T(8,128)(2,1)S(1)}, bf16[4,32,1280]{2,1,0:T(8,128)(2,1)S(1)}, u32[]{:S(2)}, u32[]{:S(2)}) collective-permute-start(bf16[4,32,1280]{2,1,0:T(8,128)(2,1)S(1)} %pad_maximum_fusion.2), channel_id=1, source_target_pairs={{0,1},{1,0},{2,3},{3,2},{4,5},{5,4},{6,7},{7,6},{8,9},{9,8},{10,11... | collective-permute-start | bytes 983048 | tf_op jit(solution)/shard_map/ppermute | solution.py:270
  30.5 2.1 %copy-start.1 = (bf16[4,32,1280]{2,1,0:T(8,128)(2,1)S(1)}, bf16[4,32,1280]{2,1,0:T(8,128)(2,1)}, u32[]{:S(2)}) copy-start(bf16[4,32,1280]{2,1,0:T(8,128)(2,1)} %copy-done) | copy-start | bytes 983044
  30.5 2.1 %copy-start.3 = (bf16[2,32,1280]{2,1,0:T(8,128)(2,1)S(1)}, bf16[2,32,1280]{2,1,0:T(8,128)(2,1)}, u32[]{:S(2)}) copy-start(bf16[2,32,1280]{2,1,0:T(8,128)(2,1)} %copy-done.2) | copy-start | bytes 491524
  34.6 6.6 %collective-permute-start.10 = (bf16[2,32,1280]{2,1,0:T(8,128)(2,1)S(1)}, bf16[2,32,1280]{2,1,0:T(8,128)(2,1)S(1)}, u32[]{:S(2)}, u32[]{:S(2)}) collective-permute-start(bf16[2,32,1280]{2,1,0:T(8,128)(2,1)S(1)} %slice.29), channel_id=1, source_target_pairs={{0,1},{1,0},{2,3},{3,2},{4,5},{5,4},{6,7},{7,6},{8,9},{9,8},{10,11... | collective-permute-start | bytes 491528 | tf_op jit(solution)/shard_map/ppermute | solution.py:270
  34.7 15.7 %collective-permute-start.12 = (bf16[4,32,1280]{2,1,0:T(8,128)(2,1)S(1)}, bf16[4,32,1280]{2,1,0:T(8,128)(2,1)S(1)}, u32[]{:S(2)}, u32[]{:S(2)}) collective-permute-start(bf16[4,32,1280]{2,1,0:T(8,128)(2,1)S(1)} %get-tuple-element.31), channel_id=1, source_target_pairs={{0,4},{1,5},{2,6},{3,7},{4,0},{5,1},{6,2},{7,3},{8,12},{9,13},{10,... | collective-permute-start | bytes 983048 | tf_op jit(solution)/shard_map/ppermute | solution.py:270
  37.1 21.5 %collective-permute-start.17 = (bf16[10,96,128]{2,1,0:T(8,128)(2,1)S(1)}, bf16[10,96,128]{2,1,0:T(8,128)(2,1)S(1)}, u32[]{:S(2)}, u32[]{:S(2)}) collective-permute-start(bf16[10,96,128]{2,1,0:T(8,128)(2,1)S(1)} %get-tuple-element.40), channel_id=1, source_target_pairs={{0,8},{1,9},{2,10},{3,11},{4,12},{5,13},{6,14},{7,15},{8,0},{9,1},... | collective-permute-start | bytes 737288 | tf_op jit(solution)/shard_map/ppermute | solution.py:270
  41.2 17.4 %collective-permute-start.18 = (bf16[10,96,128]{2,1,0:T(8,128)(2,1)S(1)}, bf16[10,96,128]{2,1,0:T(8,128)(2,1)S(1)}, u32[]{:S(2)}, u32[]{:S(2)}) collective-permute-start(bf16[10,96,128]{2,1,0:T(8,128)(2,1)S(1)} %get-tuple-element.41), channel_id=1, source_target_pairs={{0,12},{1,13},{2,14},{3,15},{4,8},{5,9},{6,10},{7,11},{8,4},{9,5},... | collective-permute-start | bytes 737288 | tf_op jit(solution)/shard_map/ppermute | solution.py:270
  41.2 9.4 %collective-permute-start.11 = (bf16[2,32,1280]{2,1,0:T(8,128)(2,1)S(1)}, bf16[2,32,1280]{2,1,0:T(8,128)(2,1)S(1)}, u32[]{:S(2)}, u32[]{:S(2)}) collective-permute-start(bf16[2,32,1280]{2,1,0:T(8,128)(2,1)S(1)} %pad_maximum_fusion.3), channel_id=1, source_target_pairs={{0,2},{1,3},{2,0},{3,1},{4,6},{5,7},{6,4},{7,5},{8,10},{9,11},{10,... | collective-permute-start | bytes 491528 | tf_op jit(solution)/shard_map/ppermute | solution.py:270
  42.8 17.8 %collective-permute-start.16 = (bf16[10,96,128]{2,1,0:T(8,128)(2,1)S(1)}, bf16[10,96,128]{2,1,0:T(8,128)(2,1)S(1)}, u32[]{:S(2)}, u32[]{:S(2)}) collective-permute-start(bf16[10,96,128]{2,1,0:T(8,128)(2,1)S(1)} %get-tuple-element.39), channel_id=1, source_target_pairs={{0,4},{1,5},{2,6},{3,7},{4,0},{5,1},{6,2},{7,3},{8,12},{9,13},{10,... | collective-permute-start | bytes 737288 | tf_op jit(solution)/shard_map/ppermute | solution.py:270
  50.3 4.8 %collective-permute-start.13 = (bf16[1,32,1280]{2,1,0:T(8,128)(2,1)S(1)}, bf16[1,32,1280]{2,1,0:T(8,128)(2,1)S(1)}, u32[]{:S(2)}, u32[]{:S(2)}) collective-permute-start(bf16[1,32,1280]{2,1,0:T(8,128)(2,1)S(1)} %get-tuple-element.32), channel_id=1, source_target_pairs={{0,3},{1,2},{2,1},{3,0},{4,7},{5,6},{6,5},{7,4},{8,11},{9,10},{10,... | collective-permute-start | bytes 245768 | tf_op jit(solution)/shard_map/ppermute | solution.py:270
  50.6 6.2 %collective-permute-start.14 = (bf16[1,32,1280]{2,1,0:T(8,128)(2,1)S(1)}, bf16[1,32,1280]{2,1,0:T(8,128)(2,1)S(1)}, u32[]{:S(2)}, u32[]{:S(2)}) collective-permute-start(bf16[1,32,1280]{2,1,0:T(8,128)(2,1)S(1)} %get-tuple-element.33), channel_id=1, source_target_pairs={{0,2},{1,3},{2,0},{3,1},{4,6},{5,7},{6,4},{7,5},{8,10},{9,11},{10,... | collective-permute-start | bytes 245768 | tf_op jit(solution)/shard_map/ppermute | solution.py:270
  55.1 1.7 %collective-permute-start.15 = (bf16[1,32,1280]{2,1,0:T(8,128)(2,1)S(1)}, bf16[1,32,1280]{2,1,0:T(8,128)(2,1)S(1)}, u32[]{:S(2)}, u32[]{:S(2)}) collective-permute-start(bf16[1,32,1280]{2,1,0:T(8,128)(2,1)S(1)} %get-tuple-element.34), channel_id=1, source_target_pairs={{0,1},{1,0},{2,3},{3,2},{4,5},{5,4},{6,7},{7,6},{8,9},{9,8},{10,11... | collective-permute-start | bytes 245768 | tf_op jit(solution)/shard_map/ppermute | solution.py:270

commit v20 on v19

--- a/solution.py
+++ b/solution.py
@@ -220,30 +220,35 @@
 
 def sum_kernel(half, *rest):
     pieces, total, held, sems = rest[:-3], rest[-3], rest[-2], rest[-1]
-    stripes = pieces[0].shape[0]
+    stripes = held.shape[0]
     step = 5 if stripes % 5 == 0 else stripes
     copies = []
-    for a in range(PAIR):
-        for c in range(0, stripes, step):
-            held[a, c:c + step] = sum(piece[c:c + step].astype(jnp.float32) for piece in pieces[a::PAIR])
-            span = pl.ds(c, step)
-            copies.append(pltpu.make_async_copy(held.at[a, span], total.at[half[0] ^ a, span], sems.at[len(copies)]))
-            copies[-1].start()
+    for c in range(0, stripes, step):
+        span = pl.ds(c, step)
+        held[span] = sum(piece[span].astype(jnp.float32) for piece in pieces)
+        copies.append(pltpu.make_async_copy(held.at[span], total.at[half[0], span], sems.at[len(copies)]))
+        copies[-1].start()
     for copy in copies:
         copy.wait()
 
 
-def sum_call(half, pieces):
-    shape = (PAIR,) + pieces[0].shape
-    return pl.pallas_call(
-        sum_kernel,
-        out_shape=jax.ShapeDtypeStruct(shape, jnp.float32),
-        in_specs=[SCALAR] + [RESIDENT] * len(pieces),
+def sum_into_kernel(half, before, *rest):
+    sum_kernel(half, *rest)
+
+
+def sum_call(half, pieces, before=None):
+    shape = pieces[0].shape
+    first = [] if before is None else [before]
+    return pl.pallas_call(
+        sum_kernel if before is None else sum_into_kernel,
+        out_shape=jax.ShapeDtypeStruct((PAIR,) + shape, jnp.float32),
+        in_specs=[SCALAR] + [ANYWHERE] * len(first) + [RESIDENT] * len(pieces),
         out_specs=ANYWHERE,
-        scratch_shapes=[pltpu.VMEM(shape, jnp.float32), pltpu.SemaphoreType.DMA((PAIR * shape[1],))],
+        scratch_shapes=[pltpu.VMEM(shape, jnp.float32), pltpu.SemaphoreType.DMA((shape[0],))],
+        input_output_aliases={1: 0} if first else {},
         compiler_params=room(10),
         name="sum",
-    )(half, *pieces)
+    )(half, *first, *pieces)
 
 
 def take(arrays, refs):
@@ -298,11 +303,11 @@
         stacks = lax.all_to_all(outgoing, "fsdp", split_axis=0, concat_axis=0, tiled=True)
         weights = stacks.transpose(1, 0, 2, 3).reshape(share, fsdp * size, TILE)
 
-    sizes = (tensor, stripes)
+    sizes = (0, stripes)
     part = tensor // HOPS
     ends = jnp.stack([half * share, z if direct else z * 0]).astype(jnp.int32)
-    scalars = jnp.concatenate([first_tiles([(0, b) for b in range(tensor)]), tile_list.reshape(-1), tile_counts, ends])
-    stay, = cut_call(scalars, cotangent, tensor, 1)
+    scalars = jnp.concatenate([tile_list.reshape(-1), tile_counts, ends])
+    stay, = cut_call(first_tiles([(0, b) for b in range(tensor)]), cotangent, tensor, 1)
     near = jnp.concatenate([tokens, near], axis=0)
     for bit in bits:
         far = swap(near, 0, bit)
@@ -341,7 +346,8 @@
     if direct:
         which = half.reshape(1).astype(jnp.int32)
         activations, which = lax.optimization_barrier((activations, which))
-        total = sum_call(which, [grads[0]] + sent)
+        pieces = [grads[0]] + sent
+        total = sum_call(1 - which, pieces[1::PAIR], sum_call(which, pieces[::PAIR]))
     return activations, total.reshape(stripes, size, TILE).transpose(1, 0, 2)
 
 

time: 62.3 us -> 62.8 us (level)
  the two profiles are of different devices: /device:TPU:0 before, /device:TPU:18 now
where the time goes in v20:
time: 62.8 us; the launch traced here: 62.6 us
  waiting for transfers between devices  30.4 us (48%)
  starting transfers between devices  17.1 us (27%)
  Pallas kernels  10.3 us (16%)
  local copies, waits for them, and re-layouts  3.43 us (5%)
  between operations  0.95 us (2%)
    ppermute x19, waiting for transfers between devices, swap(): return lax.ppermute(value, ('fsdp', 'tensor'), pairs)  30.4 us
    ppermute x19, starting transfers between devices, swap(): return lax.ppermute(value, ('fsdp', 'tensor'), pairs)  17.1 us
    pallas_call x2, Pallas kernels, cut_call(): pl.pallas_call(cut_kernel, out_shape=[jax.ShapeDtypeStruct((count // part...  3.17 us
    unnamed x19, local copies, waits for them, and re-layouts  2.46 us
    pallas_call x1, Pallas kernels, forward_call(): pl.pallas_call(functools.partial(forward_kernel, sizes), out_shape=[jax.S...  1.83 us
    pallas_call x2, Pallas kernels, sum_call(): pl.pallas_call(sum_kernel if before is None else sum_into_kernel, out_sha...  1.78 us
    pallas_call x1, Pallas kernels, join_call(): pl.pallas_call(functools.partial(join_kernel, refs), out_shape=jax.ShapeD...  1.44 us
    pallas_call x1, Pallas kernels, backward_call(): pl.pallas_call(functools.partial(backward_kernel, sizes), out_shape=[jax....  1.37 us
  transfers between devices with their start and end apart: 19, of which 7 were waited for; matrix products, arithmetic and copies ran while one was open for 2% of the time, Pallas kernels for 12%

profile of v20, /device:TPU:18, one launch (start us, length us, event | category | flops | bytes accessed | tf_op | source)
XLA Modules:
  0.0 62.6 jit_solution(5177700724775467803)
XLA Ops:
  0.6 1.6 %collective-permute-start = (bf16[32,2560]{1,0:T(8,128)(2,1)}, bf16[32,2560]{1,0:T(8,128)(2,1)S(1)}, u32[]{:S(2)}, u32[]{:S(2)}) collective-permute-start(bf16[32,2560]{1,0:T(8,128)(2,1)} %param.5), channel_id=1, source_target_pairs={{0,4},{1,5},{2,6},{3,7},{4,0},{5,1},{6,2},{7,3},{8,12},{9,13},{10,... | collective-permute-start | bytes 491528 | tf_op jit(solution)/shard_map/ppermute | solution.py:275
  2.4 1.6 %cut.2 = (bf16[2,32,1280]{2,1,0:T(8,128)(2,1)S(1)}, bf16[2,32,1280]{2,1,0:T(8,128)(2,1)S(1)}) custom-call(s32[4]{0:T(128)S(1)} %pad_add_fusion.2.starts, bf16[32,10240]{1,0:T(8,128)(2,1)} %whole.3), custom_call_target="tpu_custom_call" | custom-call | tf_op jit(solution)/shard_map/cut/pallas_call | solution.py:55
  4.0 0.5 collective-permute-start.3
  4.5 1.6 %collective-permute-start.4 = (bf16[2,32,1280]{2,1,0:T(8,128)(2,1)S(1)}, bf16[2,32,1280]{2,1,0:T(8,128)(2,1)S(1)}, u32[]{:S(2)}, u32[]{:S(2)}) collective-permute-start(bf16[2,32,1280]{2,1,0:T(8,128)(2,1)S(1)} %get-tuple-element.23), channel_id=1, source_target_pairs={{0,4},{1,5},{2,6},{3,7},{4,0},{5,1},{6,2},{7,3},{8,12},{9,13},{10,... | collective-permute-start | bytes 491528 | tf_op jit(solution)/shard_map/ppermute | solution.py:275
  6.0 0.7 %dynamic-slice_bitcast_fusion = (bf16[10,96,128]{2,1,0:T(8,128)(2,1)}, bf16[10,96,128]{2,1,0:T(8,128)(2,1)S(1)}) fusion(bf16[96,20,128]{2,0,1:T(8,128)(2,1)S(1)} %copy-done.5, s32[]{:T(128)S(6)} %select_n.15, s32[]{:T(128)S(6)} %select_n.14), kind=kLoop, calls=%fused_computation.3 | loop fusion | bytes 983048 | tf_op jit(solution)/shard_map/dynamic_slice | solution.py:297
  6.8 2.8 %collective-permute-start.6 = (bf16[10,96,128]{2,1,0:T(8,128)(2,1)S(1)}, bf16[10,96,128]{2,1,0:T(8,128)(2,1)S(1)}, u32[]{:S(2)}, u32[]{:S(2)}) collective-permute-start(bf16[10,96,128]{2,1,0:T(8,128)(2,1)S(1)} %get-tuple-element.43.rest_0_), channel_id=1, source_target_pairs={{0,8},{1,9},{2,10},{3,11},{4,12},{5,13},{6,14},{7,15},{8,0},{9,1},... | collective-permute-start | bytes 737288 | tf_op jit(solution)/shard_map/ppermute | solution.py:275
  9.7 1.6 %cut.3.rest_0_ = bf16[4,32,1280]{2,1,0:T(8,128)(2,1)S(1)} custom-call(s32[4]{0:T(128)S(1)} %pad_add_fusion.3.starts, bf16[32,10240]{1,0:T(8,128)(2,1)} %whole.3), custom_call_target="tpu_custom_call" | custom-call | tf_op jit(solution)/shard_map/cut/pallas_call | solution.py:55
  11.3 0.7 %copy-done = bf16[4,32,1280]{2,1,0:T(8,128)(2,1)} copy-done((bf16[4,32,1280]{2,1,0:T(8,128)(2,1)}, bf16[4,32,1280]{2,1,0:T(8,128)(2,1)S(1)}, u32[]{:S(2)}) %copy-start) | copy-done | bytes 327704
  12.1 0.6 collective-permute-start.1
  12.7 7.6 %collective-permute-done.4.rest_2_ = bf16[2,32,1280]{2,1,0:T(8,128)(2,1)S(1)} collective-permute-done((bf16[2,32,1280]{2,1,0:T(8,128)(2,1)S(1)}, bf16[2,32,1280]{2,1,0:T(8,128)(2,1)S(1)}, u32[]{:S(2)}, u32[]{:S(2)}) %collective-permute-start.4) | collective-permute-done | bytes 163872 | tf_op jit(solution)/shard_map/ppermute | solution.py:275
  20.3 2.5 %collective-permute-start.5 = (bf16[10,96,128]{2,1,0:T(8,128)(2,1)}, bf16[10,96,128]{2,1,0:T(8,128)(2,1)S(1)}, u32[]{:S(2)}, u32[]{:S(2)}) collective-permute-start(bf16[10,96,128]{2,1,0:T(8,128)(2,1)} %get-tuple-element.24), channel_id=1, source_target_pairs={{0,4},{1,5},{2,6},{3,7},{4,0},{5,1},{6,2},{7,3},{8,12},{9,13},{10,... | collective-permute-start | bytes 737288 | tf_op jit(solution)/shard_map/ppermute | solution.py:275
  22.8 0.6 collective-permute-start.8
  23.6 6.4 %collective-permute-done.8.rest_3_ = bf16[4,32,1280]{2,1,0:T(8,128)(2,1)S(1)} collective-permute-done((bf16[4,32,1280]{2,1,0:T(8,128)(2,1)S(1)}, bf16[4,32,1280]{2,1,0:T(8,128)(2,1)S(1)}, u32[]{:S(2)}, u32[]{:S(2)}) %collective-permute-start.8) | collective-permute-done | bytes 327712 | tf_op jit(solution)/shard_map/ppermute | solution.py:275
  30.2 0.6 copy-done.6
  31.0 0.6 %copy-done.7 = s32[20]{0:T(128)S(1)} copy-done((s32[20]{0:T(128)S(1)}, s32[20]{0:T(128)}, u32[]{:S(2)}) %copy-start.7) | copy-done | bytes 104
  31.8 0.6 stack.78.weights
  32.4 0.3 copy-done.1
  32.8 1.8 %forward.1 = (bf16[4,32,1280]{2,1,0:T(8,128)(2,1)S(1)}, bf16[4,32,1280]{2,1,0:T(8,128)(2,1)S(1)}, bf16[256,1280]{1,0:T(8,128)(2,1)S(1)}) custom-call(s32[82]{0:T(128)S(1)} %pad_add_fusion.scalars, bf16[128,2560]{1,0:T(8,128)(2,1)S(1)} %constant_dynamic-update-slice_fusion.near, bf16[128,2560]{1,0:T(8,128)(2,1)S(1)} %collective-permute-done.2.far, ...), custom_call_target="tpu_custom_call" | custom-call | tf_op jit(solution)/shard_map/forward/pallas_call | solution.py:143
  34.7 0.6 collective-permute-start.10
  35.2 0.5 collective-permute-start.12
  35.7 1.4 %backward.1 = (f32[10,96,128]{2,1,0:T(8,128)S(1)}, bf16[10,96,128]{2,1,0:T(8,128)(2,1)S(1)}, bf16[10,96,128]{2,1,0:T(8,128)(2,1)S(1)}, bf16[10,96,128]{2,1,0:T(8,128)(2,1)S(1)}) custom-call(s32[82]{0:T(128)S(1)} %pad_add_fusion.scalars, bf16[128,2560]{1,0:T(8,128)(2,1)S(1)} %constant_dynamic-update-slice_fusion.near, ...), custom_call_target="tpu_custom_call" | custom-call | tf_op jit(solution)/shard_map/backward/pallas_call | solution.py:210
  37.2 3.0 %collective-permute-start.18 = (bf16[10,96,128]{2,1,0:T(8,128)(2,1)S(1)}, bf16[10,96,128]{2,1,0:T(8,128)(2,1)S(1)}, u32[]{:S(2)}, u32[]{:S(2)}) collective-permute-start(bf16[10,96,128]{2,1,0:T(8,128)(2,1)S(1)} %get-tuple-element.41), channel_id=1, source_target_pairs={{0,12},{1,13},{2,14},{3,15},{4,8},{5,9},{6,10},{7,11},{8,4},{9,5},... | collective-permute-start | bytes 737288 | tf_op jit(solution)/shard_map/ppermute | solution.py:275
  40.2 0.6 collective-permute-start.11
  40.8 1.4 %collective-permute-start.17 = (bf16[10,96,128]{2,1,0:T(8,128)(2,1)S(1)}, bf16[10,96,128]{2,1,0:T(8,128)(2,1)S(1)}, u32[]{:S(2)}, u32[]{:S(2)}) collective-permute-start(bf16[10,96,128]{2,1,0:T(8,128)(2,1)S(1)} %get-tuple-element.40), channel_id=1, source_target_pairs={{0,4},{1,5},{2,6},{3,7},{4,0},{5,1},{6,2},{7,3},{8,12},{9,13},{10,... | collective-permute-start | bytes 737288 | tf_op jit(solution)/shard_map/ppermute | solution.py:275
  42.2 3.6 %collective-permute-done.12.rest_0_ = bf16[4,32,1280]{2,1,0:T(8,128)(2,1)S(1)} collective-permute-done((bf16[4,32,1280]{2,1,0:T(8,128)(2,1)S(1)}, bf16[4,32,1280]{2,1,0:T(8,128)(2,1)S(1)}, u32[]{:S(2)}, u32[]{:S(2)}) %collective-permute-start.12) | collective-permute-done | bytes 327712 | tf_op jit(solution)/shard_map/ppermute | solution.py:275
  45.9 0.6 collective-permute-start.14
  46.5 3.6 %collective-permute-done.13.rest_3_ = bf16[1,32,1280]{2,1,0:T(8,128)(2,1)S(1)} collective-permute-done((bf16[1,32,1280]{2,1,0:T(8,128)(2,1)S(1)}, bf16[1,32,1280]{2,1,0:T(8,128)(2,1)S(1)}, u32[]{:S(2)}, u32[]{:S(2)}) %collective-permute-start.13) | collective-permute-done | bytes 81952 | tf_op jit(solution)/shard_map/ppermute | solution.py:275
  50.2 1.0 %collective-permute-done.14.rest_4_ = bf16[1,32,1280]{2,1,0:T(8,128)(2,1)S(1)} collective-permute-done((bf16[1,32,1280]{2,1,0:T(8,128)(2,1)S(1)}, bf16[1,32,1280]{2,1,0:T(8,128)(2,1)S(1)}, u32[]{:S(2)}, u32[]{:S(2)}) %collective-permute-start.14) | collective-permute-done | bytes 81952 | tf_op jit(solution)/shard_map/ppermute | solution.py:275
  51.4 1.4 %join.1 = bf16[32,10240]{1,0:T(8,128)(2,1)} custom-call(s32[8]{0:T(128)S(1)} %stack.69.starts, bf16[4,32,1280]{2,1,0:T(8,128)(2,1)S(1)} %get-tuple-element.27.rest_0_, bf16[2,32,1280]{2,1,0:T(8,128)(2,1)S(1)} %collective-permute-done.10.rest_1_, bf16[2,32,1280]{2,1,0:T(8,128)(2,1)S(1)} %collective-permute-done.11.rest_2_, ...), custom_call_target="tpu_custom_call" | custom-call | tf_op jit(solution)/shard_map/join/pallas_call | solution.py:92
  52.9 0.9 %sum.2.before = f32[2,10,96,128]{3,2,1,0:T(8,128)} custom-call(s32[1]{0:T(128)} %bitcast.15.half, f32[10,96,128]{2,1,0:T(8,128)S(1)} %get-tuple-element.38.rest_0_, bf16[10,96,128]{2,1,0:T(8,128)(2,1)S(1)} %collective-permute-done.16.rest_1_), custom_call_target="tpu_custom_call" | custom-call | tf_op jit(solution)/shard_map/sum/pallas_call | solution.py:242
  53.8 7.9 %collective-permute-done.18.rest_1_ = bf16[10,96,128]{2,1,0:T(8,128)(2,1)S(1)} collective-permute-done((bf16[10,96,128]{2,1,0:T(8,128)(2,1)S(1)}, bf16[10,96,128]{2,1,0:T(8,128)(2,1)S(1)}, u32[]{:S(2)}, u32[]{:S(2)}) %collective-permute-start.18) | collective-permute-done | bytes 245792 | tf_op jit(solution)/shard_map/ppermute | solution.py:275
  61.7 0.9 %sum.3 = f32[2,10,96,128]{3,2,1,0:T(8,128)} custom-call(s32[1]{0:T(128)S(6)} %sub.7.half, f32[2,10,96,128]{3,2,1,0:T(8,128)} %sum.2.before, bf16[10,96,128]{2,1,0:T(8,128)(2,1)S(1)} %collective-permute-done.17.rest_0_, bf16[10,96,128]{2,1,0:T(8,128)(2,1)S(1)} %collective-permute-done.18.rest_1_), custom_call_target="tpu_custom_call", output_to_operand_aliasing={{}: (1, {})} | custom-call | tf_op jit(solution)/shard_map/sum/pallas_call | solution.py:242
  (57 shorter events, 1.4 us)
Async XLA Ops:
  0.6 5.4 %copy-start.5 = (bf16[96,20,128]{2,0,1:T(8,128)(2,1)S(1)}, bf16[96,20,128]{2,0,1:T(8,128)(2,1)}, u32[]{:S(2)}) copy-start(bf16[96,20,128]{2,0,1:T(8,128)(2,1)} %param.6) | copy-start | bytes 1474564
  0.6 11.4 %collective-permute-start = (bf16[32,2560]{1,0:T(8,128)(2,1)}, bf16[32,2560]{1,0:T(8,128)(2,1)S(1)}, u32[]{:S(2)}, u32[]{:S(2)}) collective-permute-start(bf16[32,2560]{1,0:T(8,128)(2,1)} %param.5), channel_id=1, source_target_pairs={{0,4},{1,5},{2,6},{3,7},{4,0},{5,1},{6,2},{7,3},{8,12},{9,13},{10,... | collective-permute-start | bytes 491528 | tf_op jit(solution)/shard_map/ppermute | solution.py:275
  4.0 8.7 %collective-permute-start.3 = (bf16[2,32,1280]{2,1,0:T(8,128)(2,1)S(1)}, bf16[2,32,1280]{2,1,0:T(8,128)(2,1)S(1)}, u32[]{:S(2)}, u32[]{:S(2)}) collective-permute-start(bf16[2,32,1280]{2,1,0:T(8,128)(2,1)S(1)} %get-tuple-element.22), channel_id=1, source_target_pairs={{0,4},{1,5},{2,6},{3,7},{4,0},{5,1},{6,2},{7,3},{8,12},{9,13},{10,... | collective-permute-start | bytes 491528 | tf_op jit(solution)/shard_map/ppermute | solution.py:275
  4.5 15.8 %collective-permute-start.4 = (bf16[2,32,1280]{2,1,0:T(8,128)(2,1)S(1)}, bf16[2,32,1280]{2,1,0:T(8,128)(2,1)S(1)}, u32[]{:S(2)}, u32[]{:S(2)}) collective-permute-start(bf16[2,32,1280]{2,1,0:T(8,128)(2,1)S(1)} %get-tuple-element.23), channel_id=1, source_target_pairs={{0,4},{1,5},{2,6},{3,7},{4,0},{5,1},{6,2},{7,3},{8,12},{9,13},{10,... | collective-permute-start | bytes 491528 | tf_op jit(solution)/shard_map/ppermute | solution.py:275
  6.0 3.5 %copy-start.4 = (bf16[32,2560]{1,0:T(8,128)(2,1)S(1)}, bf16[32,2560]{1,0:T(8,128)(2,1)}, u32[]{:S(2)}) copy-start(bf16[32,2560]{1,0:T(8,128)(2,1)} %param.5) | copy-start | bytes 491524
  6.8 25.0 %collective-permute-start.7 = (bf16[10,96,128]{2,1,0:T(8,128)(2,1)}, bf16[10,96,128]{2,1,0:T(8,128)(2,1)S(1)}, u32[]{:S(2)}, u32[]{:S(2)}) collective-permute-start(bf16[10,96,128]{2,1,0:T(8,128)(2,1)} %get-tuple-element.24), channel_id=1, source_target_pairs={{0,12},{1,13},{2,14},{3,15},{4,8},{5,9},{6,10},{7,11},{8,4},{9,5},... | collective-permute-start | bytes 737288 | tf_op jit(solution)/shard_map/ppermute | solution.py:275
  6.8 25.0 %collective-permute-start.6 = (bf16[10,96,128]{2,1,0:T(8,128)(2,1)S(1)}, bf16[10,96,128]{2,1,0:T(8,128)(2,1)S(1)}, u32[]{:S(2)}, u32[]{:S(2)}) collective-permute-start(bf16[10,96,128]{2,1,0:T(8,128)(2,1)S(1)} %get-tuple-element.43.rest_0_), channel_id=1, source_target_pairs={{0,8},{1,9},{2,10},{3,11},{4,12},{5,13},{6,14},{7,15},{8,0},{9,1},... | collective-permute-start | bytes 737288 | tf_op jit(solution)/shard_map/ppermute | solution.py:275
  11.3 0.7 %copy-start = (bf16[4,32,1280]{2,1,0:T(8,128)(2,1)}, bf16[4,32,1280]{2,1,0:T(8,128)(2,1)S(1)}, u32[]{:S(2)}) copy-start(bf16[4,32,1280]{2,1,0:T(8,128)(2,1)S(1)} %cut.3.rest_0_) | copy-start | bytes 983044
  12.1 10.7 %slice-start.1 = ((bf16[4,32,1280]{2,1,0:T(8,128)(2,1)}), bf16[2,32,1280]{2,1,0:T(8,128)(2,1)S(1)}, s32[]{:S(2)}) async-start(bf16[4,32,1280]{2,1,0:T(8,128)(2,1)} %copy-done), calls=%async_computation.1 | async-start | bytes 327680 | tf_op jit(solution)/shard_map/slice | solution.py:261
  12.1 11.4 %collective-permute-start.1 = (bf16[64,2560]{1,0:T(8,128)(2,1)S(1)}, bf16[64,2560]{1,0:T(8,128)(2,1)S(1)}, u32[]{:S(2)}, u32[]{:S(2)}) collective-permute-start(bf16[64,2560]{1,0:T(8,128)(2,1)S(1)} %pad_maximum_fusion), channel_id=1, source_target_pairs={{0,2},{1,3},{2,0},{3,1},{4,6},{5,7},{6,4},{7,5},{8,10},{9,11},{10,... | collective-permute-start | bytes 983048 | tf_op jit(solution)/shard_map/ppermute | solution.py:275
  12.7 7.6 %copy-start.2 = (bf16[2,32,1280]{2,1,0:T(8,128)(2,1)}, bf16[2,32,1280]{2,1,0:T(8,128)(2,1)S(1)}, u32[]{:S(2)}) copy-start(bf16[2,32,1280]{2,1,0:T(8,128)(2,1)S(1)} %collective-permute-done.3.rest_1_) | copy-start | bytes 491524
  20.3 11.5 %collective-permute-start.5 = (bf16[10,96,128]{2,1,0:T(8,128)(2,1)}, bf16[10,96,128]{2,1,0:T(8,128)(2,1)S(1)}, u32[]{:S(2)}, u32[]{:S(2)}) collective-permute-start(bf16[10,96,128]{2,1,0:T(8,128)(2,1)} %get-tuple-element.24), channel_id=1, source_target_pairs={{0,4},{1,5},{2,6},{3,7},{4,0},{5,1},{6,2},{7,3},{8,12},{9,13},{10,... | collective-permute-start | bytes 737288 | tf_op jit(solution)/shard_map/ppermute | solution.py:275
  22.8 7.1 %collective-permute-start.8 = (bf16[4,32,1280]{2,1,0:T(8,128)(2,1)S(1)}, bf16[4,32,1280]{2,1,0:T(8,128)(2,1)S(1)}, u32[]{:S(2)}, u32[]{:S(2)}) collective-permute-start(bf16[4,32,1280]{2,1,0:T(8,128)(2,1)S(1)} %pad_maximum_fusion.1), channel_id=1, source_target_pairs={{0,2},{1,3},{2,0},{3,1},{4,6},{5,7},{6,4},{7,5},{8,10},{9,11},{10,... | collective-permute-start | bytes 983048 | tf_op jit(solution)/shard_map/ppermute | solution.py:275
  23.5 6.5 %slice-start = ((bf16[4,32,1280]{2,1,0:T(8,128)(2,1)}), bf16[1,32,1280]{2,1,0:T(8,128)(2,1)S(1)}, s32[]{:S(2)}) async-start(bf16[4,32,1280]{2,1,0:T(8,128)(2,1)} %copy-done), calls=%async_computation | async-start | bytes 163840 | tf_op jit(solution)/shard_map/slice | solution.py:261
  23.5 6.5 %slice-start.2 = ((bf16[2,32,1280]{2,1,0:T(8,128)(2,1)}), bf16[1,32,1280]{2,1,0:T(8,128)(2,1)S(1)}, s32[]{:S(2)}) async-start(bf16[2,32,1280]{2,1,0:T(8,128)(2,1)} %copy-done.2), calls=%async_computation.2 | async-start | bytes 163840 | tf_op jit(solution)/shard_map/slice | solution.py:261
  23.5 9.3 %collective-permute-start.2 = (bf16[128,2560]{1,0:T(8,128)(2,1)S(1)}, bf16[128,2560]{1,0:T(8,128)(2,1)S(1)}, u32[]{:S(2)}, u32[]{:S(2)}) collective-permute-start(bf16[128,2560]{1,0:T(8,128)(2,1)S(1)} %constant_dynamic-update-slice_fusion.near), channel_id=1, source_target_pairs={{0,1},{1,0},{2,3},{3,2},{4,5},{5,4},{6,7},{7,6},{8,9},{9,8},{10,11... | collective-permute-start | bytes 1966088 | tf_op jit(solution)/shard_map/ppermute | solution.py:275
  30.1 2.3 %collective-permute-start.9 = (bf16[4,32,1280]{2,1,0:T(8,128)(2,1)S(1)}, bf16[4,32,1280]{2,1,0:T(8,128)(2,1)S(1)}, u32[]{:S(2)}, u32[]{:S(2)}) collective-permute-start(bf16[4,32,1280]{2,1,0:T(8,128)(2,1)S(1)} %pad_maximum_fusion.2), channel_id=1, source_target_pairs={{0,1},{1,0},{2,3},{3,2},{4,5},{5,4},{6,7},{7,6},{8,9},{9,8},{10,11... | collective-permute-start | bytes 983048 | tf_op jit(solution)/shard_map/ppermute | solution.py:275
  30.1 0.7 %copy-start.6 = (s32[20,3]{0,1:T(4,128)S(1)}, s32[20,3]{0,1:T(4,128)}, u32[]{:S(2)}) copy-start(s32[20,3]{0,1:T(4,128)} %param.8) | copy-start | bytes 724
  31.0 0.7 %copy-start.7 = (s32[20]{0:T(128)S(1)}, s32[20]{0:T(128)}, u32[]{:S(2)}) copy-start(s32[20]{0:T(128)} %param.9) | copy-start | bytes 244
  31.8 1.0 %copy-start.1 = (bf16[4,32,1280]{2,1,0:T(8,128)(2,1)S(1)}, bf16[4,32,1280]{2,1,0:T(8,128)(2,1)}, u32[]{:S(2)}) copy-start(bf16[4,32,1280]{2,1,0:T(8,128)(2,1)} %copy-done) | copy-start | bytes 983044
  31.8 1.0 %copy-start.3 = (bf16[2,32,1280]{2,1,0:T(8,128)(2,1)S(1)}, bf16[2,32,1280]{2,1,0:T(8,128)(2,1)}, u32[]{:S(2)}) copy-start(bf16[2,32,1280]{2,1,0:T(8,128)(2,1)} %copy-done.2) | copy-start | bytes 491524
  34.7 5.5 %collective-permute-start.10 = (bf16[2,32,1280]{2,1,0:T(8,128)(2,1)S(1)}, bf16[2,32,1280]{2,1,0:T(8,128)(2,1)S(1)}, u32[]{:S(2)}, u32[]{:S(2)}) collective-permute-start(bf16[2,32,1280]{2,1,0:T(8,128)(2,1)S(1)} %slice.29), channel_id=1, source_target_pairs={{0,1},{1,0},{2,3},{3,2},{4,5},{5,4},{6,7},{7,6},{8,9},{9,8},{10,11... | collective-permute-start | bytes 491528 | tf_op jit(solution)/shard_map/ppermute | solution.py:275
  35.2 10.6 %collective-permute-start.12 = (bf16[4,32,1280]{2,1,0:T(8,128)(2,1)S(1)}, bf16[4,32,1280]{2,1,0:T(8,128)(2,1)S(1)}, u32[]{:S(2)}, u32[]{:S(2)}) collective-permute-start(bf16[4,32,1280]{2,1,0:T(8,128)(2,1)S(1)} %get-tuple-element.31), channel_id=1, source_target_pairs={{0,4},{1,5},{2,6},{3,7},{4,0},{5,1},{6,2},{7,3},{8,12},{9,13},{10,... | collective-permute-start | bytes 983048 | tf_op jit(solution)/shard_map/ppermute | solution.py:275
  37.1 15.8 %collective-permute-start.16 = (bf16[10,96,128]{2,1,0:T(8,128)(2,1)S(1)}, bf16[10,96,128]{2,1,0:T(8,128)(2,1)S(1)}, u32[]{:S(2)}, u32[]{:S(2)}) collective-permute-start(bf16[10,96,128]{2,1,0:T(8,128)(2,1)S(1)} %get-tuple-element.39), channel_id=1, source_target_pairs={{0,8},{1,9},{2,10},{3,11},{4,12},{5,13},{6,14},{7,15},{8,0},{9,1},... | collective-permute-start | bytes 737288 | tf_op jit(solution)/shard_map/ppermute | solution.py:275
  37.2 24.5 %collective-permute-start.18 = (bf16[10,96,128]{2,1,0:T(8,128)(2,1)S(1)}, bf16[10,96,128]{2,1,0:T(8,128)(2,1)S(1)}, u32[]{:S(2)}, u32[]{:S(2)}) collective-permute-start(bf16[10,96,128]{2,1,0:T(8,128)(2,1)S(1)} %get-tuple-element.41), channel_id=1, source_target_pairs={{0,12},{1,13},{2,14},{3,15},{4,8},{5,9},{6,10},{7,11},{8,4},{9,5},... | collective-permute-start | bytes 737288 | tf_op jit(solution)/shard_map/ppermute | solution.py:275
  40.2 5.7 %collective-permute-start.11 = (bf16[2,32,1280]{2,1,0:T(8,128)(2,1)S(1)}, bf16[2,32,1280]{2,1,0:T(8,128)(2,1)S(1)}, u32[]{:S(2)}, u32[]{:S(2)}) collective-permute-start(bf16[2,32,1280]{2,1,0:T(8,128)(2,1)S(1)} %pad_maximum_fusion.3), channel_id=1, source_target_pairs={{0,2},{1,3},{2,0},{3,1},{4,6},{5,7},{6,4},{7,5},{8,10},{9,11},{10,... | collective-permute-start | bytes 491528 | tf_op jit(solution)/shard_map/ppermute | solution.py:275
  40.8 20.9 %collective-permute-start.17 = (bf16[10,96,128]{2,1,0:T(8,128)(2,1)S(1)}, bf16[10,96,128]{2,1,0:T(8,128)(2,1)S(1)}, u32[]{:S(2)}, u32[]{:S(2)}) collective-permute-start(bf16[10,96,128]{2,1,0:T(8,128)(2,1)S(1)} %get-tuple-element.40), channel_id=1, source_target_pairs={{0,4},{1,5},{2,6},{3,7},{4,0},{5,1},{6,2},{7,3},{8,12},{9,13},{10,... | collective-permute-start | bytes 737288 | tf_op jit(solution)/shard_map/ppermute | solution.py:275
  45.8 4.3 %collective-permute-start.13 = (bf16[1,32,1280]{2,1,0:T(8,128)(2,1)S(1)}, bf16[1,32,1280]{2,1,0:T(8,128)(2,1)S(1)}, u32[]{:S(2)}, u32[]{:S(2)}) collective-permute-start(bf16[1,32,1280]{2,1,0:T(8,128)(2,1)S(1)} %get-tuple-element.32), channel_id=1, source_target_pairs={{0,3},{1,2},{2,1},{3,0},{4,7},{5,6},{6,5},{7,4},{8,11},{9,10},{10,... | collective-permute-start | bytes 245768 | tf_op jit(solution)/shard_map/ppermute | solution.py:275
  45.9 5.3 %collective-permute-start.14 = (bf16[1,32,1280]{2,1,0:T(8,128)(2,1)S(1)}, bf16[1,32,1280]{2,1,0:T(8,128)(2,1)S(1)}, u32[]{:S(2)}, u32[]{:S(2)}) collective-permute-start(bf16[1,32,1280]{2,1,0:T(8,128)(2,1)S(1)} %get-tuple-element.33), channel_id=1, source_target_pairs={{0,2},{1,3},{2,0},{3,1},{4,6},{5,7},{6,4},{7,5},{8,10},{9,11},{10,... | collective-permute-start | bytes 245768 | tf_op jit(solution)/shard_map/ppermute | solution.py:275
  50.1 1.3 %collective-permute-start.15 = (bf16[1,32,1280]{2,1,0:T(8,128)(2,1)S(1)}, bf16[1,32,1280]{2,1,0:T(8,128)(2,1)S(1)}, u32[]{:S(2)}, u32[]{:S(2)}) collective-permute-start(bf16[1,32,1280]{2,1,0:T(8,128)(2,1)S(1)} %get-tuple-element.34), channel_id=1, source_target_pairs={{0,1},{1,0},{2,3},{3,2},{4,5},{5,4},{6,7},{7,6},{8,9},{9,8},{10,11... | collective-permute-start | bytes 245768 | tf_op jit(solution)/shard_map/ppermute | solution.py:275

commit v21 on v20

--- a/solution.py
+++ b/solution.py
@@ -12,7 +12,7 @@
 PAIR = 2
 ROWS = 16
 HOPS = 2
-AWAY = 1
+AWAY = 2
 DIRECT = 8
 STACK_FLOPS = 2 * 10**9
 SPLIT_FLOPS = 2 * 10**9
@@ -317,7 +317,10 @@
     backs = collect_call(arrays, refs)
     home, *away, slopes = forward_call(sizes, scalars, near, far, weights, backs)
 
-    back_home = [swap(array, 1, 0) for array in away]
+    back_home = [swap(away[0], 1, 0)]
+    for array in away[1:]:
+        array, back_home[-1] = lax.optimization_barrier((array, back_home[-1]))
+        back_home.append(swap(array, 1, 0))
 
     grads = list(backward_call(sizes, scalars, near, far, slopes, fsdp if direct else 1))
     home_arrays, blocks = [home], [(0, b, (0, i)) for i, b in enumerate(origins)]

time: 62.8 us -> 68.6 us (1.092)
  the two profiles are of different devices: /device:TPU:18 before, /device:TPU:25 now
where the time goes in v21:
time: 68.6 us; the launch traced here: 68.4 us
  starting transfers between devices  34.1 us (50%)
  waiting for transfers between devices  19.2 us (28%)
  Pallas kernels  10.3 us (15%)
  local copies, waits for them, and re-layouts  3.44 us (5%)
  between operations  0.92 us (1%)
    ppermute x20, starting transfers between devices, swap(): return lax.ppermute(value, ('fsdp', 'tensor'), pairs)  34.1 us
    ppermute x20, waiting for transfers between devices, swap(): return lax.ppermute(value, ('fsdp', 'tensor'), pairs)  19.2 us
    pallas_call x2, Pallas kernels, cut_call(): pl.pallas_call(cut_kernel, out_shape=[jax.ShapeDtypeStruct((count // part...  3.17 us
    unnamed x19, local copies, waits for them, and re-layouts  2.46 us
    pallas_call x1, Pallas kernels, forward_call(): pl.pallas_call(functools.partial(forward_kernel, sizes), out_shape=[jax.S...  1.84 us
    pallas_call x2, Pallas kernels, sum_call(): pl.pallas_call(sum_kernel if before is None else sum_into_kernel, out_sha...  1.78 us
    pallas_call x1, Pallas kernels, join_call(): pl.pallas_call(functools.partial(join_kernel, refs), out_shape=jax.ShapeD...  1.44 us
  transfers between devices with their start and end apart: 20, of which 6 were waited for; matrix products, arithmetic and copies ran while one was open for 2% of the time, Pallas kernels for 11%

profile of v21, /device:TPU:25, one launch (start us, length us, event | category | flops | bytes accessed | tf_op | source)
XLA Modules:
  0.0 68.4 jit_solution(8295748219897129682)
XLA Ops:
  1.0 1.6 %cut.2 = (bf16[2,32,1280]{2,1,0:T(8,128)(2,1)S(1)}, bf16[2,32,1280]{2,1,0:T(8,128)(2,1)S(1)}) custom-call(s32[4]{0:T(128)S(1)} %pad_add_fusion.2.starts, bf16[32,10240]{1,0:T(8,128)(2,1)} %whole.3), custom_call_target="tpu_custom_call" | custom-call | tf_op jit(solution)/shard_map/cut/pallas_call | solution.py:55
  2.5 1.4 %collective-permute-start.3 = (bf16[2,32,1280]{2,1,0:T(8,128)(2,1)S(1)}, bf16[2,32,1280]{2,1,0:T(8,128)(2,1)S(1)}, u32[]{:S(2)}, u32[]{:S(2)}) collective-permute-start(bf16[2,32,1280]{2,1,0:T(8,128)(2,1)S(1)} %get-tuple-element.25), channel_id=1, source_target_pairs={{0,4},{1,5},{2,6},{3,7},{4,0},{5,1},{6,2},{7,3},{8,12},{9,13},{10,... | collective-permute-start | bytes 491528 | tf_op jit(solution)/shard_map/ppermute | solution.py:275
  4.1 0.7 %dynamic-slice_bitcast_fusion = (bf16[10,96,128]{2,1,0:T(8,128)(2,1)}, bf16[10,96,128]{2,1,0:T(8,128)(2,1)S(1)}) fusion(bf16[96,20,128]{2,0,1:T(8,128)(2,1)S(1)} %copy-done.5, s32[]{:T(128)S(6)} %select_n.15, s32[]{:T(128)S(6)} %select_n.14), kind=kLoop, calls=%fused_computation.3 | loop fusion | bytes 983048 | tf_op jit(solution)/shard_map/dynamic_slice | solution.py:297
  4.8 1.1 %collective-permute-start.7 = (bf16[10,96,128]{2,1,0:T(8,128)(2,1)}, bf16[10,96,128]{2,1,0:T(8,128)(2,1)S(1)}, u32[]{:S(2)}, u32[]{:S(2)}) collective-permute-start(bf16[10,96,128]{2,1,0:T(8,128)(2,1)} %get-tuple-element.27), channel_id=1, source_target_pairs={{0,12},{1,13},{2,14},{3,15},{4,8},{5,9},{6,10},{7,11},{8,4},{9,5},... | collective-permute-start | bytes 737288 | tf_op jit(solution)/shard_map/ppermute | solution.py:275
  5.9 1.4 %collective-permute-start.6 = (bf16[10,96,128]{2,1,0:T(8,128)(2,1)S(1)}, bf16[10,96,128]{2,1,0:T(8,128)(2,1)S(1)}, u32[]{:S(2)}, u32[]{:S(2)}) collective-permute-start(bf16[10,96,128]{2,1,0:T(8,128)(2,1)S(1)} %get-tuple-element.49.rest_0_), channel_id=1, source_target_pairs={{0,8},{1,9},{2,10},{3,11},{4,12},{5,13},{6,14},{7,15},{8,0},{9,1},... | collective-permute-start | bytes 737288 | tf_op jit(solution)/shard_map/ppermute | solution.py:275
  7.4 1.6 %cut.3.rest_0_ = bf16[4,32,1280]{2,1,0:T(8,128)(2,1)S(1)} custom-call(s32[4]{0:T(128)S(1)} %pad_add_fusion.3.starts, bf16[32,10240]{1,0:T(8,128)(2,1)} %whole.3), custom_call_target="tpu_custom_call" | custom-call | tf_op jit(solution)/shard_map/cut/pallas_call | solution.py:55
  9.0 0.7 %copy-done = bf16[4,32,1280]{2,1,0:T(8,128)(2,1)} copy-done((bf16[4,32,1280]{2,1,0:T(8,128)(2,1)}, bf16[4,32,1280]{2,1,0:T(8,128)(2,1)S(1)}, u32[]{:S(2)}) %copy-start) | copy-done | bytes 327704
  9.8 1.3 %collective-permute-start.1 = (bf16[64,2560]{1,0:T(8,128)(2,1)S(1)}, bf16[64,2560]{1,0:T(8,128)(2,1)S(1)}, u32[]{:S(2)}, u32[]{:S(2)}) collective-permute-start(bf16[64,2560]{1,0:T(8,128)(2,1)S(1)} %pad_maximum_fusion), channel_id=1, source_target_pairs={{0,2},{1,3},{2,0},{3,1},{4,6},{5,7},{6,4},{7,5},{8,10},{9,11},{10,... | collective-permute-start | bytes 983048 | tf_op jit(solution)/shard_map/ppermute | solution.py:275
  11.0 4.2 %collective-permute-done.4.rest_2_ = bf16[2,32,1280]{2,1,0:T(8,128)(2,1)S(1)} collective-permute-done((bf16[2,32,1280]{2,1,0:T(8,128)(2,1)S(1)}, bf16[2,32,1280]{2,1,0:T(8,128)(2,1)S(1)}, u32[]{:S(2)}, u32[]{:S(2)}) %collective-permute-start.4) | collective-permute-done | bytes 163872 | tf_op jit(solution)/shard_map/ppermute | solution.py:275
  15.3 1.3 %collective-permute-start.8 = (bf16[4,32,1280]{2,1,0:T(8,128)(2,1)S(1)}, bf16[4,32,1280]{2,1,0:T(8,128)(2,1)S(1)}, u32[]{:S(2)}, u32[]{:S(2)}) collective-permute-start(bf16[4,32,1280]{2,1,0:T(8,128)(2,1)S(1)} %pad_maximum_fusion.1), channel_id=1, source_target_pairs={{0,2},{1,3},{2,0},{3,1},{4,6},{5,7},{6,4},{7,5},{8,10},{9,11},{10,... | collective-permute-start | bytes 983048 | tf_op jit(solution)/shard_map/ppermute | solution.py:275
  17.0 6.6 %collective-permute-start.2 = (bf16[128,2560]{1,0:T(8,128)(2,1)S(1)}, bf16[128,2560]{1,0:T(8,128)(2,1)S(1)}, u32[]{:S(2)}, u32[]{:S(2)}) collective-permute-start(bf16[128,2560]{1,0:T(8,128)(2,1)S(1)} %constant_dynamic-update-slice_fusion.near), channel_id=1, source_target_pairs={{0,1},{1,0},{2,3},{3,2},{4,5},{5,4},{6,7},{7,6},{8,9},{9,8},{10,11... | collective-permute-start | bytes 1966088 | tf_op jit(solution)/shard_map/ppermute | solution.py:275
  23.7 5.5 %collective-permute-start.9 = (bf16[4,32,1280]{2,1,0:T(8,128)(2,1)S(1)}, bf16[4,32,1280]{2,1,0:T(8,128)(2,1)S(1)}, u32[]{:S(2)}, u32[]{:S(2)}) collective-permute-start(bf16[4,32,1280]{2,1,0:T(8,128)(2,1)S(1)} %pad_maximum_fusion.2), channel_id=1, source_target_pairs={{0,1},{1,0},{2,3},{3,2},{4,5},{5,4},{6,7},{7,6},{8,9},{9,8},{10,11... | collective-permute-start | bytes 983048 | tf_op jit(solution)/shard_map/ppermute | solution.py:275
  29.3 0.6 copy-done.6
  30.1 0.6 copy-done.7
  30.9 0.6 stack.78.weights
  31.9 1.8 %forward.1 = (bf16[4,32,1280]{2,1,0:T(8,128)(2,1)S(1)}, bf16[2,32,1280]{2,1,0:T(8,128)(2,1)S(1)}, bf16[2,32,1280]{2,1,0:T(8,128)(2,1)S(1)}, bf16[256,1280]{1,0:T(8,128)(2,1)S(1)}) custom-call(s32[82]{0:T(128)S(1)} %pad_add_fusion.scalars, bf16[128,2560]{1,0:T(8,128)(2,1)S(1)} %constant_dynamic-update-slice_fusion.near, ...), custom_call_target="tpu_custom_call" | custom-call | tf_op jit(solution)/shard_map/forward/pallas_call | solution.py:143
  33.8 0.9 %collective-permute-start.10 = (bf16[2,32,1280]{2,1,0:T(8,128)(2,1)S(1)}, bf16[2,32,1280]{2,1,0:T(8,128)(2,1)S(1)}, u32[]{:S(2)}, u32[]{:S(2)}) collective-permute-start(bf16[2,32,1280]{2,1,0:T(8,128)(2,1)S(1)} %slice.29), channel_id=1, source_target_pairs={{0,1},{1,0},{2,3},{3,2},{4,5},{5,4},{6,7},{7,6},{8,9},{9,8},{10,11... | collective-permute-start | bytes 491528 | tf_op jit(solution)/shard_map/ppermute | solution.py:275
  34.7 0.9 %collective-permute-start.12 = (bf16[2,32,1280]{2,1,0:T(8,128)(2,1)S(1)}, bf16[2,32,1280]{2,1,0:T(8,128)(2,1)S(1)}, u32[]{:S(2)}, u32[]{:S(2)}) collective-permute-start(bf16[2,32,1280]{2,1,0:T(8,128)(2,1)S(1)} %get-tuple-element.35), channel_id=1, source_target_pairs={{0,4},{1,5},{2,6},{3,7},{4,0},{5,1},{6,2},{7,3},{8,12},{9,13},{10,... | collective-permute-start | bytes 491528 | tf_op jit(solution)/shard_map/ppermute | solution.py:275
  35.7 1.4 %backward.1 = (f32[10,96,128]{2,1,0:T(8,128)S(1)}, bf16[10,96,128]{2,1,0:T(8,128)(2,1)S(1)}, bf16[10,96,128]{2,1,0:T(8,128)(2,1)S(1)}, bf16[10,96,128]{2,1,0:T(8,128)(2,1)S(1)}) custom-call(s32[82]{0:T(128)S(1)} %pad_add_fusion.scalars, bf16[128,2560]{1,0:T(8,128)(2,1)S(1)} %constant_dynamic-update-slice_fusion.near, ...), custom_call_target="tpu_custom_call" | custom-call | tf_op jit(solution)/shard_map/backward/pallas_call | solution.py:210
  37.1 2.6 %collective-permute-start.19 = (bf16[10,96,128]{2,1,0:T(8,128)(2,1)S(1)}, bf16[10,96,128]{2,1,0:T(8,128)(2,1)S(1)}, u32[]{:S(2)}, u32[]{:S(2)}) collective-permute-start(bf16[10,96,128]{2,1,0:T(8,128)(2,1)S(1)} %get-tuple-element.47), channel_id=1, source_target_pairs={{0,12},{1,13},{2,14},{3,15},{4,8},{5,9},{6,10},{7,11},{8,4},{9,5},... | collective-permute-start | bytes 737288 | tf_op jit(solution)/shard_map/ppermute | solution.py:275
  39.7 0.8 %collective-permute-done.12.rest_0_ = bf16[2,32,1280]{2,1,0:T(8,128)(2,1)S(1)} collective-permute-done((bf16[2,32,1280]{2,1,0:T(8,128)(2,1)S(1)}, bf16[2,32,1280]{2,1,0:T(8,128)(2,1)S(1)}, u32[]{:S(2)}, u32[]{:S(2)}) %collective-permute-start.12) | collective-permute-done | bytes 163872 | tf_op jit(solution)/shard_map/ppermute | solution.py:275
  40.5 0.5 collective-permute-start.13
  41.0 1.3 %collective-permute-start.11 = (bf16[2,32,1280]{2,1,0:T(8,128)(2,1)S(1)}, bf16[2,32,1280]{2,1,0:T(8,128)(2,1)S(1)}, u32[]{:S(2)}, u32[]{:S(2)}) collective-permute-start(bf16[2,32,1280]{2,1,0:T(8,128)(2,1)S(1)} %pad_maximum_fusion.3), channel_id=1, source_target_pairs={{0,2},{1,3},{2,0},{3,1},{4,6},{5,7},{6,4},{7,5},{8,10},{9,11},{10,... | collective-permute-start | bytes 491528 | tf_op jit(solution)/shard_map/ppermute | solution.py:275
  42.3 1.0 %collective-permute-start.18 = (bf16[10,96,128]{2,1,0:T(8,128)(2,1)S(1)}, bf16[10,96,128]{2,1,0:T(8,128)(2,1)S(1)}, u32[]{:S(2)}, u32[]{:S(2)}) collective-permute-start(bf16[10,96,128]{2,1,0:T(8,128)(2,1)S(1)} %get-tuple-element.46), channel_id=1, source_target_pairs={{0,4},{1,5},{2,6},{3,7},{4,0},{5,1},{6,2},{7,3},{8,12},{9,13},{10,... | collective-permute-start | bytes 737288 | tf_op jit(solution)/shard_map/ppermute | solution.py:275
  43.3 9.7 %collective-permute-done.13.rest_1_ = bf16[2,32,1280]{2,1,0:T(8,128)(2,1)S(1)} collective-permute-done((bf16[2,32,1280]{2,1,0:T(8,128)(2,1)S(1)}, bf16[2,32,1280]{2,1,0:T(8,128)(2,1)S(1)}, u32[]{:S(2)}, u32[]{:S(2)}) %collective-permute-start.13) | collective-permute-done | bytes 163872 | tf_op jit(solution)/shard_map/ppermute | solution.py:275
  53.0 7.2 %collective-permute-start.14 = (bf16[1,32,1280]{2,1,0:T(8,128)(2,1)S(1)}, bf16[1,32,1280]{2,1,0:T(8,128)(2,1)S(1)}, u32[]{:S(2)}, u32[]{:S(2)}) collective-permute-start(bf16[1,32,1280]{2,1,0:T(8,128)(2,1)S(1)} %get-tuple-element.38), channel_id=1, source_target_pairs={{0,3},{1,2},{2,1},{3,0},{4,7},{5,6},{6,5},{7,4},{8,11},{9,10},{10,... | collective-permute-start | bytes 245768 | tf_op jit(solution)/shard_map/ppermute | solution.py:275
  60.4 2.9 %collective-permute-done.14.rest_3_ = bf16[1,32,1280]{2,1,0:T(8,128)(2,1)S(1)} collective-permute-done((bf16[1,32,1280]{2,1,0:T(8,128)(2,1)S(1)}, bf16[1,32,1280]{2,1,0:T(8,128)(2,1)S(1)}, u32[]{:S(2)}, u32[]{:S(2)}) %collective-permute-start.14) | collective-permute-done | bytes 81952 | tf_op jit(solution)/shard_map/ppermute | solution.py:275
  63.4 0.4 collective-permute-start.16
  63.9 1.3 %collective-permute-done.15.rest_4_ = bf16[1,32,1280]{2,1,0:T(8,128)(2,1)S(1)} collective-permute-done((bf16[1,32,1280]{2,1,0:T(8,128)(2,1)S(1)}, bf16[1,32,1280]{2,1,0:T(8,128)(2,1)S(1)}, u32[]{:S(2)}, u32[]{:S(2)}) %collective-permute-start.15) | collective-permute-done | bytes 81952 | tf_op jit(solution)/shard_map/ppermute | solution.py:275
  65.1 1.4 %join.1 = bf16[32,10240]{1,0:T(8,128)(2,1)} custom-call(s32[8]{0:T(128)S(1)} %stack.69.starts, bf16[4,32,1280]{2,1,0:T(8,128)(2,1)S(1)} %get-tuple-element.30.rest_0_, bf16[2,32,1280]{2,1,0:T(8,128)(2,1)S(1)} %collective-permute-done.10.rest_1_, bf16[2,32,1280]{2,1,0:T(8,128)(2,1)S(1)} %collective-permute-done.11.rest_2_, ...), custom_call_target="tpu_custom_call" | custom-call | tf_op jit(solution)/shard_map/join/pallas_call | solution.py:92
  66.6 0.9 %sum.2.before = f32[2,10,96,128]{3,2,1,0:T(8,128)} custom-call(s32[1]{0:T(128)} %bitcast.15.half, f32[10,96,128]{2,1,0:T(8,128)S(1)} %get-tuple-element.44.rest_0_, bf16[10,96,128]{2,1,0:T(8,128)(2,1)S(1)} %collective-permute-done.17.rest_1_), custom_call_target="tpu_custom_call" | custom-call | tf_op jit(solution)/shard_map/sum/pallas_call | solution.py:242
  67.5 0.9 %sum.3 = f32[2,10,96,128]{3,2,1,0:T(8,128)} custom-call(s32[1]{0:T(128)S(6)} %sub.7.half, f32[2,10,96,128]{3,2,1,0:T(8,128)} %sum.2.before, bf16[10,96,128]{2,1,0:T(8,128)(2,1)S(1)} %collective-permute-done.18.rest_0_, bf16[10,96,128]{2,1,0:T(8,128)(2,1)S(1)} %collective-permute-done.19.rest_1_), custom_call_target="tpu_custom_call", output_to_operand_aliasing={{}: (1, {})} | custom-call | tf_op jit(solution)/shard_map/sum/pallas_call | solution.py:242
  (59 shorter events, 2.4 us)
Async XLA Ops:
  0.6 3.5 %copy-start.5 = (bf16[96,20,128]{2,0,1:T(8,128)(2,1)S(1)}, bf16[96,20,128]{2,0,1:T(8,128)(2,1)}, u32[]{:S(2)}) copy-start(bf16[96,20,128]{2,0,1:T(8,128)(2,1)} %param.6) | copy-start | bytes 1474564
  0.6 9.1 %collective-permute-start = (bf16[32,2560]{1,0:T(8,128)(2,1)}, bf16[32,2560]{1,0:T(8,128)(2,1)S(1)}, u32[]{:S(2)}, u32[]{:S(2)}) collective-permute-start(bf16[32,2560]{1,0:T(8,128)(2,1)} %param.5), channel_id=1, source_target_pairs={{0,4},{1,5},{2,6},{3,7},{4,0},{5,1},{6,2},{7,3},{8,12},{9,13},{10,... | collective-permute-start | bytes 491528 | tf_op jit(solution)/shard_map/ppermute | solution.py:275
  2.5 8.5 %collective-permute-start.3 = (bf16[2,32,1280]{2,1,0:T(8,128)(2,1)S(1)}, bf16[2,32,1280]{2,1,0:T(8,128)(2,1)S(1)}, u32[]{:S(2)}, u32[]{:S(2)}) collective-permute-start(bf16[2,32,1280]{2,1,0:T(8,128)(2,1)S(1)} %get-tuple-element.25), channel_id=1, source_target_pairs={{0,4},{1,5},{2,6},{3,7},{4,0},{5,1},{6,2},{7,3},{8,12},{9,13},{10,... | collective-permute-start | bytes 491528 | tf_op jit(solution)/shard_map/ppermute | solution.py:275
  3.9 11.3 %collective-permute-start.4 = (bf16[2,32,1280]{2,1,0:T(8,128)(2,1)S(1)}, bf16[2,32,1280]{2,1,0:T(8,128)(2,1)S(1)}, u32[]{:S(2)}, u32[]{:S(2)}) collective-permute-start(bf16[2,32,1280]{2,1,0:T(8,128)(2,1)S(1)} %get-tuple-element.26), channel_id=1, source_target_pairs={{0,4},{1,5},{2,6},{3,7},{4,0},{5,1},{6,2},{7,3},{8,12},{9,13},{10,... | collective-permute-start | bytes 491528 | tf_op jit(solution)/shard_map/ppermute | solution.py:275
  4.1 3.2 %copy-start.4 = (bf16[32,2560]{1,0:T(8,128)(2,1)S(1)}, bf16[32,2560]{1,0:T(8,128)(2,1)}, u32[]{:S(2)}) copy-start(bf16[32,2560]{1,0:T(8,128)(2,1)} %param.5) | copy-start | bytes 491524
  4.8 26.0 %collective-permute-start.7 = (bf16[10,96,128]{2,1,0:T(8,128)(2,1)}, bf16[10,96,128]{2,1,0:T(8,128)(2,1)S(1)}, u32[]{:S(2)}, u32[]{:S(2)}) collective-permute-start(bf16[10,96,128]{2,1,0:T(8,128)(2,1)} %get-tuple-element.27), channel_id=1, source_target_pairs={{0,12},{1,13},{2,14},{3,15},{4,8},{5,9},{6,10},{7,11},{8,4},{9,5},... | collective-permute-start | bytes 737288 | tf_op jit(solution)/shard_map/ppermute | solution.py:275
  5.9 25.0 %collective-permute-start.6 = (bf16[10,96,128]{2,1,0:T(8,128)(2,1)S(1)}, bf16[10,96,128]{2,1,0:T(8,128)(2,1)S(1)}, u32[]{:S(2)}, u32[]{:S(2)}) collective-permute-start(bf16[10,96,128]{2,1,0:T(8,128)(2,1)S(1)} %get-tuple-element.49.rest_0_), channel_id=1, source_target_pairs={{0,8},{1,9},{2,10},{3,11},{4,12},{5,13},{6,14},{7,15},{8,0},{9,1},... | collective-permute-start | bytes 737288 | tf_op jit(solution)/shard_map/ppermute | solution.py:275
  9.0 0.7 %copy-start = (bf16[4,32,1280]{2,1,0:T(8,128)(2,1)}, bf16[4,32,1280]{2,1,0:T(8,128)(2,1)S(1)}, u32[]{:S(2)}) copy-start(bf16[4,32,1280]{2,1,0:T(8,128)(2,1)S(1)} %cut.3.rest_0_) | copy-start | bytes 983044
  9.8 5.5 %slice-start.1 = ((bf16[4,32,1280]{2,1,0:T(8,128)(2,1)}), bf16[2,32,1280]{2,1,0:T(8,128)(2,1)S(1)}, s32[]{:S(2)}) async-start(bf16[4,32,1280]{2,1,0:T(8,128)(2,1)} %copy-done), calls=%async_computation.1 | async-start | bytes 327680 | tf_op jit(solution)/shard_map/slice | solution.py:261
  9.8 7.2 %collective-permute-start.1 = (bf16[64,2560]{1,0:T(8,128)(2,1)S(1)}, bf16[64,2560]{1,0:T(8,128)(2,1)S(1)}, u32[]{:S(2)}, u32[]{:S(2)}) collective-permute-start(bf16[64,2560]{1,0:T(8,128)(2,1)S(1)} %pad_maximum_fusion), channel_id=1, source_target_pairs={{0,2},{1,3},{2,0},{3,1},{4,6},{5,7},{6,4},{7,5},{8,10},{9,11},{10,... | collective-permute-start | bytes 983048 | tf_op jit(solution)/shard_map/ppermute | solution.py:275
  11.0 4.2 %copy-start.2 = (bf16[2,32,1280]{2,1,0:T(8,128)(2,1)}, bf16[2,32,1280]{2,1,0:T(8,128)(2,1)S(1)}, u32[]{:S(2)}) copy-start(bf16[2,32,1280]{2,1,0:T(8,128)(2,1)S(1)} %collective-permute-done.3.rest_1_) | copy-start | bytes 491524
  15.2 15.6 %collective-permute-start.5 = (bf16[10,96,128]{2,1,0:T(8,128)(2,1)}, bf16[10,96,128]{2,1,0:T(8,128)(2,1)S(1)}, u32[]{:S(2)}, u32[]{:S(2)}) collective-permute-start(bf16[10,96,128]{2,1,0:T(8,128)(2,1)} %get-tuple-element.27), channel_id=1, source_target_pairs={{0,4},{1,5},{2,6},{3,7},{4,0},{5,1},{6,2},{7,3},{8,12},{9,13},{10,... | collective-permute-start | bytes 737288 | tf_op jit(solution)/shard_map/ppermute | solution.py:275
  15.3 8.4 %collective-permute-start.8 = (bf16[4,32,1280]{2,1,0:T(8,128)(2,1)S(1)}, bf16[4,32,1280]{2,1,0:T(8,128)(2,1)S(1)}, u32[]{:S(2)}, u32[]{:S(2)}) collective-permute-start(bf16[4,32,1280]{2,1,0:T(8,128)(2,1)S(1)} %pad_maximum_fusion.1), channel_id=1, source_target_pairs={{0,2},{1,3},{2,0},{3,1},{4,6},{5,7},{6,4},{7,5},{8,10},{9,11},{10,... | collective-permute-start | bytes 983048 | tf_op jit(solution)/shard_map/ppermute | solution.py:275
  17.0 6.7 %slice-start = ((bf16[4,32,1280]{2,1,0:T(8,128)(2,1)}), bf16[1,32,1280]{2,1,0:T(8,128)(2,1)S(1)}, s32[]{:S(2)}) async-start(bf16[4,32,1280]{2,1,0:T(8,128)(2,1)} %copy-done), calls=%async_computation | async-start | bytes 163840 | tf_op jit(solution)/shard_map/slice | solution.py:261
  17.0 6.7 %slice-start.2 = ((bf16[2,32,1280]{2,1,0:T(8,128)(2,1)}), bf16[1,32,1280]{2,1,0:T(8,128)(2,1)S(1)}, s32[]{:S(2)}) async-start(bf16[2,32,1280]{2,1,0:T(8,128)(2,1)} %copy-done.2), calls=%async_computation.2 | async-start | bytes 163840 | tf_op jit(solution)/shard_map/slice | solution.py:261
  17.0 14.9 %collective-permute-start.2 = (bf16[128,2560]{1,0:T(8,128)(2,1)S(1)}, bf16[128,2560]{1,0:T(8,128)(2,1)S(1)}, u32[]{:S(2)}, u32[]{:S(2)}) collective-permute-start(bf16[128,2560]{1,0:T(8,128)(2,1)S(1)} %constant_dynamic-update-slice_fusion.near), channel_id=1, source_target_pairs={{0,1},{1,0},{2,3},{3,2},{4,5},{5,4},{6,7},{7,6},{8,9},{9,8},{10,11... | collective-permute-start | bytes 1966088 | tf_op jit(solution)/shard_map/ppermute | solution.py:275
  23.7 7.8 %collective-permute-start.9 = (bf16[4,32,1280]{2,1,0:T(8,128)(2,1)S(1)}, bf16[4,32,1280]{2,1,0:T(8,128)(2,1)S(1)}, u32[]{:S(2)}, u32[]{:S(2)}) collective-permute-start(bf16[4,32,1280]{2,1,0:T(8,128)(2,1)S(1)} %pad_maximum_fusion.2), channel_id=1, source_target_pairs={{0,1},{1,0},{2,3},{3,2},{4,5},{5,4},{6,7},{7,6},{8,9},{9,8},{10,11... | collective-permute-start | bytes 983048 | tf_op jit(solution)/shard_map/ppermute | solution.py:275
  29.2 0.7 copy-start.6
  30.1 0.7 copy-start.7
  30.8 1.0 %copy-start.1 = (bf16[4,32,1280]{2,1,0:T(8,128)(2,1)S(1)}, bf16[4,32,1280]{2,1,0:T(8,128)(2,1)}, u32[]{:S(2)}) copy-start(bf16[4,32,1280]{2,1,0:T(8,128)(2,1)} %copy-done) | copy-start | bytes 983044
  30.9 1.0 %copy-start.3 = (bf16[2,32,1280]{2,1,0:T(8,128)(2,1)S(1)}, bf16[2,32,1280]{2,1,0:T(8,128)(2,1)}, u32[]{:S(2)}) copy-start(bf16[2,32,1280]{2,1,0:T(8,128)(2,1)} %copy-done.2) | copy-start | bytes 491524
  33.8 5.9 %collective-permute-start.10 = (bf16[2,32,1280]{2,1,0:T(8,128)(2,1)S(1)}, bf16[2,32,1280]{2,1,0:T(8,128)(2,1)S(1)}, u32[]{:S(2)}, u32[]{:S(2)}) collective-permute-start(bf16[2,32,1280]{2,1,0:T(8,128)(2,1)S(1)} %slice.29), channel_id=1, source_target_pairs={{0,1},{1,0},{2,3},{3,2},{4,5},{5,4},{6,7},{7,6},{8,9},{9,8},{10,11... | collective-permute-start | bytes 491528 | tf_op jit(solution)/shard_map/ppermute | solution.py:275
  34.7 5.8 %collective-permute-start.12 = (bf16[2,32,1280]{2,1,0:T(8,128)(2,1)S(1)}, bf16[2,32,1280]{2,1,0:T(8,128)(2,1)S(1)}, u32[]{:S(2)}, u32[]{:S(2)}) collective-permute-start(bf16[2,32,1280]{2,1,0:T(8,128)(2,1)S(1)} %get-tuple-element.35), channel_id=1, source_target_pairs={{0,4},{1,5},{2,6},{3,7},{4,0},{5,1},{6,2},{7,3},{8,12},{9,13},{10,... | collective-permute-start | bytes 491528 | tf_op jit(solution)/shard_map/ppermute | solution.py:275
  37.0 29.5 %collective-permute-start.17 = (bf16[10,96,128]{2,1,0:T(8,128)(2,1)S(1)}, bf16[10,96,128]{2,1,0:T(8,128)(2,1)S(1)}, u32[]{:S(2)}, u32[]{:S(2)}) collective-permute-start(bf16[10,96,128]{2,1,0:T(8,128)(2,1)S(1)} %get-tuple-element.45), channel_id=1, source_target_pairs={{0,8},{1,9},{2,10},{3,11},{4,12},{5,13},{6,14},{7,15},{8,0},{9,1},... | collective-permute-start | bytes 737288 | tf_op jit(solution)/shard_map/ppermute | solution.py:275
  37.1 30.4 %collective-permute-start.19 = (bf16[10,96,128]{2,1,0:T(8,128)(2,1)S(1)}, bf16[10,96,128]{2,1,0:T(8,128)(2,1)S(1)}, u32[]{:S(2)}, u32[]{:S(2)}) collective-permute-start(bf16[10,96,128]{2,1,0:T(8,128)(2,1)S(1)} %get-tuple-element.47), channel_id=1, source_target_pairs={{0,12},{1,13},{2,14},{3,15},{4,8},{5,9},{6,10},{7,11},{8,4},{9,5},... | collective-permute-start | bytes 737288 | tf_op jit(solution)/shard_map/ppermute | solution.py:275
  40.5 12.4 %collective-permute-start.13 = (bf16[2,32,1280]{2,1,0:T(8,128)(2,1)S(1)}, bf16[2,32,1280]{2,1,0:T(8,128)(2,1)S(1)}, u32[]{:S(2)}, u32[]{:S(2)}) collective-permute-start(bf16[2,32,1280]{2,1,0:T(8,128)(2,1)S(1)} %get-tuple-element.37), channel_id=1, source_target_pairs={{0,4},{1,5},{2,6},{3,7},{4,0},{5,1},{6,2},{7,3},{8,12},{9,13},{10,... | collective-permute-start | bytes 491528 | tf_op jit(solution)/shard_map/ppermute | solution.py:275
  41.0 19.2 %collective-permute-start.11 = (bf16[2,32,1280]{2,1,0:T(8,128)(2,1)S(1)}, bf16[2,32,1280]{2,1,0:T(8,128)(2,1)S(1)}, u32[]{:S(2)}, u32[]{:S(2)}) collective-permute-start(bf16[2,32,1280]{2,1,0:T(8,128)(2,1)S(1)} %pad_maximum_fusion.3), channel_id=1, source_target_pairs={{0,2},{1,3},{2,0},{3,1},{4,6},{5,7},{6,4},{7,5},{8,10},{9,11},{10,... | collective-permute-start | bytes 491528 | tf_op jit(solution)/shard_map/ppermute | solution.py:275
  42.3 25.2 %collective-permute-start.18 = (bf16[10,96,128]{2,1,0:T(8,128)(2,1)S(1)}, bf16[10,96,128]{2,1,0:T(8,128)(2,1)S(1)}, u32[]{:S(2)}, u32[]{:S(2)}) collective-permute-start(bf16[10,96,128]{2,1,0:T(8,128)(2,1)S(1)} %get-tuple-element.46), channel_id=1, source_target_pairs={{0,4},{1,5},{2,6},{3,7},{4,0},{5,1},{6,2},{7,3},{8,12},{9,13},{10,... | collective-permute-start | bytes 737288 | tf_op jit(solution)/shard_map/ppermute | solution.py:275
  53.0 10.4 %collective-permute-start.14 = (bf16[1,32,1280]{2,1,0:T(8,128)(2,1)S(1)}, bf16[1,32,1280]{2,1,0:T(8,128)(2,1)S(1)}, u32[]{:S(2)}, u32[]{:S(2)}) collective-permute-start(bf16[1,32,1280]{2,1,0:T(8,128)(2,1)S(1)} %get-tuple-element.38), channel_id=1, source_target_pairs={{0,3},{1,2},{2,1},{3,0},{4,7},{5,6},{6,5},{7,4},{8,11},{9,10},{10,... | collective-permute-start | bytes 245768 | tf_op jit(solution)/shard_map/ppermute | solution.py:275
  60.2 4.9 %collective-permute-start.15 = (bf16[1,32,1280]{2,1,0:T(8,128)(2,1)S(1)}, bf16[1,32,1280]{2,1,0:T(8,128)(2,1)S(1)}, u32[]{:S(2)}, u32[]{:S(2)}) collective-permute-start(bf16[1,32,1280]{2,1,0:T(8,128)(2,1)S(1)} %get-tuple-element.39), channel_id=1, source_target_pairs={{0,2},{1,3},{2,0},{3,1},{4,6},{5,7},{6,4},{7,5},{8,10},{9,11},{10,... | collective-permute-start | bytes 245768 | tf_op jit(solution)/shard_map/ppermute | solution.py:275
  63.4 1.8 %collective-permute-start.16 = (bf16[1,32,1280]{2,1,0:T(8,128)(2,1)S(1)}, bf16[1,32,1280]{2,1,0:T(8,128)(2,1)S(1)}, u32[]{:S(2)}, u32[]{:S(2)}) collective-permute-start(bf16[1,32,1280]{2,1,0:T(8,128)(2,1)S(1)} %get-tuple-element.40), channel_id=1, source_target_pairs={{0,1},{1,0},{2,3},{3,2},{4,5},{5,4},{6,7},{7,6},{8,9},{9,8},{10,11... | collective-permute-start | bytes 245768 | tf_op jit(solution)/shard_map/ppermute | solution.py:275

commit v22 on v20

--- a/solution.py
+++ b/solution.py
@@ -288,7 +288,10 @@
         return jnp.stack([(t ^ b) * stripes + (half ^ a) * share for a, b in steps]).astype(jnp.int32)
 
     direct = whole_tiles and fsdp <= DIRECT
-    leave = cut_call(first_tiles([(1, b) for b in range(tensor)]), cotangent, tensor, HOPS)
+    leave = []
+    for first in range(0, tensor, tensor // HOPS):
+        columns = [((t ^ b) * stripes + (1 - half) * share) * TILE for b in range(first, first + tensor // HOPS)]
+        leave.append(jnp.stack([lax.dynamic_slice_in_dim(cotangent, column, share * TILE, 1) for column in columns]))
     arrived = [swap(part, 1, 0) for part in leave]
     near = swap(tokens, 1, 0)
     by_stripe = jnp.transpose(tile_weights, (1, 0, 2))

time: 62.8 us -> 62.4 us (level)
  the two profiles are of different devices: /device:TPU:18 before, /device:TPU:16 now
where the time goes in v22:
time: 62.4 us; the launch traced here: 62.1 us
  waiting for transfers between devices  26.8 us (43%)
  starting transfers between devices  20.9 us (33%)
  Pallas kernels  8.68 us (14%)
  local copies, waits for them, and re-layouts  4.46 us (7%)
  between operations  0.95 us (2%)
    ppermute x19, waiting for transfers between devices, swap(): return lax.ppermute(value, ('fsdp', 'tensor'), pairs)  26.8 us
    ppermute x19, starting transfers between devices, swap(): return lax.ppermute(value, ('fsdp', 'tensor'), pairs)  20.9 us
    unnamed x19, local copies, waits for them, and re-layouts  2.46 us
    pallas_call x1, Pallas kernels, forward_call(): pl.pallas_call(functools.partial(forward_kernel, sizes), out_shape=[jax.S...  1.83 us
    pallas_call x2, Pallas kernels, sum_call(): pl.pallas_call(sum_kernel if before is None else sum_into_kernel, out_sha...  1.78 us
    pallas_call x1, Pallas kernels, cut_call(): pl.pallas_call(cut_kernel, out_shape=[jax.ShapeDtypeStruct((count // part...  1.59 us
    pallas_call x1, Pallas kernels, join_call(): pl.pallas_call(functools.partial(join_kernel, refs), out_shape=jax.ShapeD...  1.44 us
    pallas_call x1, Pallas kernels, backward_call(): pl.pallas_call(functools.partial(backward_kernel, sizes), out_shape=[jax....  1.37 us
  transfers between devices with their start and end apart: 19, of which 6 were waited for; matrix products, arithmetic and copies ran while one was open for 4% of the time, Pallas kernels for 10%

profile of v22, /device:TPU:16, one launch (start us, length us, event | category | flops | bytes accessed | tf_op | source)
XLA Modules:
  0.0 62.1 jit_solution(12146696209845615549)
XLA Ops:
  0.6 1.6 %collective-permute-start = (bf16[32,2560]{1,0:T(8,128)(2,1)}, bf16[32,2560]{1,0:T(8,128)(2,1)S(1)}, u32[]{:S(2)}, u32[]{:S(2)}) collective-permute-start(bf16[32,2560]{1,0:T(8,128)(2,1)} %param.5), channel_id=1, source_target_pairs={{0,4},{1,5},{2,6},{3,7},{4,0},{5,1},{6,2},{7,3},{8,12},{9,13},{10,... | collective-permute-start | bytes 491528 | tf_op jit(solution)/shard_map/ppermute | solution.py:275
  2.3 1.0 %dynamic-slice_bitcast_fusion.3 = (bf16[1,32,1280]{2,1,0:T(8,128)(2,1)S(1)}, bf16[1,32,1280]{2,1,0:T(8,128)(2,1)S(1)}, bf16[1,32,1280]{2,1,0:T(8,128)(2,1)S(1)}, bf16[1,32,1280]{2,1,0:T(8,128)(2,1)S(1)}) fusion(bf16[32,10240]{1,0:T(8,128)(2,1)} %whole.1, s32[]{:T(128)S(6)} %select_n.30, s32[]{:T(128)S(6)} %select_n.29, s32[]{:T(128)S(6)} %select_n.28, ...), kind=kLoop, calls=%fused_computation.9 | loop fusion | bytes 655376 | tf_op jit(solution)/shard_map/stack | solution.py:294
  3.3 0.5 collective-permute-start.3
  3.9 1.6 %collective-permute-start.4 = (bf16[2,32,1280]{2,1,0:T(8,128)(2,1)S(1)}, bf16[2,32,1280]{2,1,0:T(8,128)(2,1)S(1)}, u32[]{:S(2)}, u32[]{:S(2)}) collective-permute-start(bf16[2,32,1280]{2,1,0:T(8,128)(2,1)S(1)} %pad_maximum_fusion.4), channel_id=1, source_target_pairs={{0,4},{1,5},{2,6},{3,7},{4,0},{5,1},{6,2},{7,3},{8,12},{9,13},{10,... | collective-permute-start | bytes 491528 | tf_op jit(solution)/shard_map/ppermute | solution.py:275
  5.5 0.7 %dynamic-slice_bitcast_fusion = (bf16[10,96,128]{2,1,0:T(8,128)(2,1)}, bf16[10,96,128]{2,1,0:T(8,128)(2,1)S(1)}) fusion(bf16[96,20,128]{2,0,1:T(8,128)(2,1)S(1)} %copy-done.5, s32[]{:T(128)S(6)} %select_n.27, s32[]{:T(128)S(6)} %select_n.26), kind=kLoop, calls=%fused_computation.3 | loop fusion | bytes 983048 | tf_op jit(solution)/shard_map/dynamic_slice | solution.py:300
  6.3 2.8 %collective-permute-start.6 = (bf16[10,96,128]{2,1,0:T(8,128)(2,1)S(1)}, bf16[10,96,128]{2,1,0:T(8,128)(2,1)S(1)}, u32[]{:S(2)}, u32[]{:S(2)}) collective-permute-start(bf16[10,96,128]{2,1,0:T(8,128)(2,1)S(1)} %get-tuple-element.43.rest_0_), channel_id=1, source_target_pairs={{0,8},{1,9},{2,10},{3,11},{4,12},{5,13},{6,14},{7,15},{8,0},{9,1},... | collective-permute-start | bytes 737288 | tf_op jit(solution)/shard_map/ppermute | solution.py:275
  9.2 1.6 %cut.1.rest_0_ = bf16[4,32,1280]{2,1,0:T(8,128)(2,1)S(1)} custom-call(s32[4]{0:T(128)S(1)} %pad_add_fusion.2.starts, bf16[32,10240]{1,0:T(8,128)(2,1)} %whole.1), custom_call_target="tpu_custom_call" | custom-call | tf_op jit(solution)/shard_map/cut/pallas_call | solution.py:55
  10.8 0.7 %copy-done = bf16[4,32,1280]{2,1,0:T(8,128)(2,1)} copy-done((bf16[4,32,1280]{2,1,0:T(8,128)(2,1)}, bf16[4,32,1280]{2,1,0:T(8,128)(2,1)S(1)}, u32[]{:S(2)}) %copy-start) | copy-done | bytes 327704
  11.5 1.6 %collective-permute-start.1 = (bf16[64,2560]{1,0:T(8,128)(2,1)S(1)}, bf16[64,2560]{1,0:T(8,128)(2,1)S(1)}, u32[]{:S(2)}, u32[]{:S(2)}) collective-permute-start(bf16[64,2560]{1,0:T(8,128)(2,1)S(1)} %pad_maximum_fusion), channel_id=1, source_target_pairs={{0,2},{1,3},{2,0},{3,1},{4,6},{5,7},{6,4},{7,5},{8,10},{9,11},{10,... | collective-permute-start | bytes 983048 | tf_op jit(solution)/shard_map/ppermute | solution.py:275
  13.1 6.4 %collective-permute-done.4.rest_2_ = bf16[2,32,1280]{2,1,0:T(8,128)(2,1)S(1)} collective-permute-done((bf16[2,32,1280]{2,1,0:T(8,128)(2,1)S(1)}, bf16[2,32,1280]{2,1,0:T(8,128)(2,1)S(1)}, u32[]{:S(2)}, u32[]{:S(2)}) %collective-permute-start.4) | collective-permute-done | bytes 163872 | tf_op jit(solution)/shard_map/ppermute | solution.py:275
  19.6 2.4 %collective-permute-start.5 = (bf16[10,96,128]{2,1,0:T(8,128)(2,1)}, bf16[10,96,128]{2,1,0:T(8,128)(2,1)S(1)}, u32[]{:S(2)}, u32[]{:S(2)}) collective-permute-start(bf16[10,96,128]{2,1,0:T(8,128)(2,1)} %get-tuple-element.20), channel_id=1, source_target_pairs={{0,4},{1,5},{2,6},{3,7},{4,0},{5,1},{6,2},{7,3},{8,12},{9,13},{10,... | collective-permute-start | bytes 737288 | tf_op jit(solution)/shard_map/ppermute | solution.py:275
  22.0 1.6 %collective-permute-start.8 = (bf16[4,32,1280]{2,1,0:T(8,128)(2,1)S(1)}, bf16[4,32,1280]{2,1,0:T(8,128)(2,1)S(1)}, u32[]{:S(2)}, u32[]{:S(2)}) collective-permute-start(bf16[4,32,1280]{2,1,0:T(8,128)(2,1)S(1)} %pad_maximum_fusion.1), channel_id=1, source_target_pairs={{0,2},{1,3},{2,0},{3,1},{4,6},{5,7},{6,4},{7,5},{8,10},{9,11},{10,... | collective-permute-start | bytes 983048 | tf_op jit(solution)/shard_map/ppermute | solution.py:275
  23.8 5.8 %collective-permute-done.8.rest_3_ = bf16[4,32,1280]{2,1,0:T(8,128)(2,1)S(1)} collective-permute-done((bf16[4,32,1280]{2,1,0:T(8,128)(2,1)S(1)}, bf16[4,32,1280]{2,1,0:T(8,128)(2,1)S(1)}, u32[]{:S(2)}, u32[]{:S(2)}) %collective-permute-start.8) | collective-permute-done | bytes 327712 | tf_op jit(solution)/shard_map/ppermute | solution.py:275
  29.8 0.6 copy-done.6
  30.6 0.6 %copy-done.7 = s32[20]{0:T(128)S(1)} copy-done((s32[20]{0:T(128)S(1)}, s32[20]{0:T(128)}, u32[]{:S(2)}) %copy-start.7) | copy-done | bytes 104
  31.3 0.6 stack.94.weights
  32.0 0.3 copy-done.1
  32.4 1.8 %forward.1 = (bf16[4,32,1280]{2,1,0:T(8,128)(2,1)S(1)}, bf16[4,32,1280]{2,1,0:T(8,128)(2,1)S(1)}, bf16[256,1280]{1,0:T(8,128)(2,1)S(1)}) custom-call(s32[82]{0:T(128)S(1)} %pad_add_fusion.scalars, bf16[128,2560]{1,0:T(8,128)(2,1)S(1)} %constant_dynamic-update-slice_fusion.near, bf16[128,2560]{1,0:T(8,128)(2,1)S(1)} %collective-permute-done.2.far, ...), custom_call_target="tpu_custom_call" | custom-call | tf_op jit(solution)/shard_map/forward/pallas_call | solution.py:143
  34.2 0.6 collective-permute-start.10
  34.8 0.3 collective-permute-start.12
  35.1 1.4 %backward.1 = (f32[10,96,128]{2,1,0:T(8,128)S(1)}, bf16[10,96,128]{2,1,0:T(8,128)(2,1)S(1)}, bf16[10,96,128]{2,1,0:T(8,128)(2,1)S(1)}, bf16[10,96,128]{2,1,0:T(8,128)(2,1)S(1)}) custom-call(s32[82]{0:T(128)S(1)} %pad_add_fusion.scalars, bf16[128,2560]{1,0:T(8,128)(2,1)S(1)} %constant_dynamic-update-slice_fusion.near, ...), custom_call_target="tpu_custom_call" | custom-call | tf_op jit(solution)/shard_map/backward/pallas_call | solution.py:210
  36.5 3.2 %collective-permute-start.18 = (bf16[10,96,128]{2,1,0:T(8,128)(2,1)S(1)}, bf16[10,96,128]{2,1,0:T(8,128)(2,1)S(1)}, u32[]{:S(2)}, u32[]{:S(2)}) collective-permute-start(bf16[10,96,128]{2,1,0:T(8,128)(2,1)S(1)} %get-tuple-element.37), channel_id=1, source_target_pairs={{0,12},{1,13},{2,14},{3,15},{4,8},{5,9},{6,10},{7,11},{8,4},{9,5},... | collective-permute-start | bytes 737288 | tf_op jit(solution)/shard_map/ppermute | solution.py:275
  39.8 1.6 %collective-permute-start.11 = (bf16[2,32,1280]{2,1,0:T(8,128)(2,1)S(1)}, bf16[2,32,1280]{2,1,0:T(8,128)(2,1)S(1)}, u32[]{:S(2)}, u32[]{:S(2)}) collective-permute-start(bf16[2,32,1280]{2,1,0:T(8,128)(2,1)S(1)} %pad_maximum_fusion.5), channel_id=1, source_target_pairs={{0,2},{1,3},{2,0},{3,1},{4,6},{5,7},{6,4},{7,5},{8,10},{9,11},{10,... | collective-permute-start | bytes 491528 | tf_op jit(solution)/shard_map/ppermute | solution.py:275
  41.3 1.2 %collective-permute-start.17 = (bf16[10,96,128]{2,1,0:T(8,128)(2,1)S(1)}, bf16[10,96,128]{2,1,0:T(8,128)(2,1)S(1)}, u32[]{:S(2)}, u32[]{:S(2)}) collective-permute-start(bf16[10,96,128]{2,1,0:T(8,128)(2,1)S(1)} %get-tuple-element.36), channel_id=1, source_target_pairs={{0,4},{1,5},{2,6},{3,7},{4,0},{5,1},{6,2},{7,3},{8,12},{9,13},{10,... | collective-permute-start | bytes 737288 | tf_op jit(solution)/shard_map/ppermute | solution.py:275
  42.5 3.0 %collective-permute-done.12.rest_0_ = bf16[4,32,1280]{2,1,0:T(8,128)(2,1)S(1)} collective-permute-done((bf16[4,32,1280]{2,1,0:T(8,128)(2,1)S(1)}, bf16[4,32,1280]{2,1,0:T(8,128)(2,1)S(1)}, u32[]{:S(2)}, u32[]{:S(2)}) %collective-permute-start.12) | collective-permute-done | bytes 327712 | tf_op jit(solution)/shard_map/ppermute | solution.py:275
  45.6 1.5 %collective-permute-start.14 = (bf16[1,32,1280]{2,1,0:T(8,128)(2,1)S(1)}, bf16[1,32,1280]{2,1,0:T(8,128)(2,1)S(1)}, u32[]{:S(2)}, u32[]{:S(2)}) collective-permute-start(bf16[1,32,1280]{2,1,0:T(8,128)(2,1)S(1)} %get-tuple-element.29), channel_id=1, source_target_pairs={{0,2},{1,3},{2,0},{3,1},{4,6},{5,7},{6,4},{7,5},{8,10},{9,11},{10,... | collective-permute-start | bytes 245768 | tf_op jit(solution)/shard_map/ppermute | solution.py:275
  47.1 3.1 %collective-permute-done.13.rest_3_ = bf16[1,32,1280]{2,1,0:T(8,128)(2,1)S(1)} collective-permute-done((bf16[1,32,1280]{2,1,0:T(8,128)(2,1)S(1)}, bf16[1,32,1280]{2,1,0:T(8,128)(2,1)S(1)}, u32[]{:S(2)}, u32[]{:S(2)}) %collective-permute-start.13) | collective-permute-done | bytes 81952 | tf_op jit(solution)/shard_map/ppermute | solution.py:275
  50.5 1.6 %collective-permute-done.14.rest_4_ = bf16[1,32,1280]{2,1,0:T(8,128)(2,1)S(1)} collective-permute-done((bf16[1,32,1280]{2,1,0:T(8,128)(2,1)S(1)}, bf16[1,32,1280]{2,1,0:T(8,128)(2,1)S(1)}, u32[]{:S(2)}, u32[]{:S(2)}) %collective-permute-start.14) | collective-permute-done | bytes 81952 | tf_op jit(solution)/shard_map/ppermute | solution.py:275
  52.1 1.4 %join.1 = bf16[32,10240]{1,0:T(8,128)(2,1)} custom-call(s32[8]{0:T(128)S(1)} %stack.80.starts, bf16[4,32,1280]{2,1,0:T(8,128)(2,1)S(1)} %get-tuple-element.23.rest_0_, bf16[2,32,1280]{2,1,0:T(8,128)(2,1)S(1)} %collective-permute-done.10.rest_1_, bf16[2,32,1280]{2,1,0:T(8,128)(2,1)S(1)} %collective-permute-done.11.rest_2_, ...), custom_call_target="tpu_custom_call" | custom-call | tf_op jit(solution)/shard_map/join/pallas_call | solution.py:92
  53.5 0.9 %sum.2.before = f32[2,10,96,128]{3,2,1,0:T(8,128)} custom-call(s32[1]{0:T(128)} %bitcast.19.half, f32[10,96,128]{2,1,0:T(8,128)S(1)} %get-tuple-element.34.rest_0_, bf16[10,96,128]{2,1,0:T(8,128)(2,1)S(1)} %collective-permute-done.16.rest_1_), custom_call_target="tpu_custom_call" | custom-call | tf_op jit(solution)/shard_map/sum/pallas_call | solution.py:242
  54.4 6.8 %collective-permute-done.18.rest_1_ = bf16[10,96,128]{2,1,0:T(8,128)(2,1)S(1)} collective-permute-done((bf16[10,96,128]{2,1,0:T(8,128)(2,1)S(1)}, bf16[10,96,128]{2,1,0:T(8,128)(2,1)S(1)}, u32[]{:S(2)}, u32[]{:S(2)}) %collective-permute-start.18) | collective-permute-done | bytes 245792 | tf_op jit(solution)/shard_map/ppermute | solution.py:275
  61.3 0.9 %sum.3 = f32[2,10,96,128]{3,2,1,0:T(8,128)} custom-call(s32[1]{0:T(128)S(6)} %sub.5.half, f32[2,10,96,128]{3,2,1,0:T(8,128)} %sum.2.before, bf16[10,96,128]{2,1,0:T(8,128)(2,1)S(1)} %collective-permute-done.17.rest_0_, bf16[10,96,128]{2,1,0:T(8,128)(2,1)S(1)} %collective-permute-done.18.rest_1_), custom_call_target="tpu_custom_call", output_to_operand_aliasing={{}: (1, {})} | custom-call | tf_op jit(solution)/shard_map/sum/pallas_call | solution.py:242
  (58 shorter events, 1.3 us)
Async XLA Ops:
  0.6 10.9 %collective-permute-start = (bf16[32,2560]{1,0:T(8,128)(2,1)}, bf16[32,2560]{1,0:T(8,128)(2,1)S(1)}, u32[]{:S(2)}, u32[]{:S(2)}) collective-permute-start(bf16[32,2560]{1,0:T(8,128)(2,1)} %param.5), channel_id=1, source_target_pairs={{0,4},{1,5},{2,6},{3,7},{4,0},{5,1},{6,2},{7,3},{8,12},{9,13},{10,... | collective-permute-start | bytes 491528 | tf_op jit(solution)/shard_map/ppermute | solution.py:275
  3.3 2.2 %copy-start.5 = (bf16[96,20,128]{2,0,1:T(8,128)(2,1)S(1)}, bf16[96,20,128]{2,0,1:T(8,128)(2,1)}, u32[]{:S(2)}) copy-start(bf16[96,20,128]{2,0,1:T(8,128)(2,1)} %param.6) | copy-start | bytes 1474564
  3.3 9.8 %collective-permute-start.3 = (bf16[2,32,1280]{2,1,0:T(8,128)(2,1)S(1)}, bf16[2,32,1280]{2,1,0:T(8,128)(2,1)S(1)}, u32[]{:S(2)}, u32[]{:S(2)}) collective-permute-start(bf16[2,32,1280]{2,1,0:T(8,128)(2,1)S(1)} %pad_maximum_fusion.3), channel_id=1, source_target_pairs={{0,4},{1,5},{2,6},{3,7},{4,0},{5,1},{6,2},{7,3},{8,12},{9,13},{10,... | collective-permute-start | bytes 491528 | tf_op jit(solution)/shard_map/ppermute | solution.py:275
  3.9 15.7 %collective-permute-start.4 = (bf16[2,32,1280]{2,1,0:T(8,128)(2,1)S(1)}, bf16[2,32,1280]{2,1,0:T(8,128)(2,1)S(1)}, u32[]{:S(2)}, u32[]{:S(2)}) collective-permute-start(bf16[2,32,1280]{2,1,0:T(8,128)(2,1)S(1)} %pad_maximum_fusion.4), channel_id=1, source_target_pairs={{0,4},{1,5},{2,6},{3,7},{4,0},{5,1},{6,2},{7,3},{8,12},{9,13},{10,... | collective-permute-start | bytes 491528 | tf_op jit(solution)/shard_map/ppermute | solution.py:275
  5.5 3.5 %copy-start.4 = (bf16[32,2560]{1,0:T(8,128)(2,1)S(1)}, bf16[32,2560]{1,0:T(8,128)(2,1)}, u32[]{:S(2)}) copy-start(bf16[32,2560]{1,0:T(8,128)(2,1)} %param.5) | copy-start | bytes 491524
  6.2 25.1 %collective-permute-start.7 = (bf16[10,96,128]{2,1,0:T(8,128)(2,1)}, bf16[10,96,128]{2,1,0:T(8,128)(2,1)S(1)}, u32[]{:S(2)}, u32[]{:S(2)}) collective-permute-start(bf16[10,96,128]{2,1,0:T(8,128)(2,1)} %get-tuple-element.20), channel_id=1, source_target_pairs={{0,12},{1,13},{2,14},{3,15},{4,8},{5,9},{6,10},{7,11},{8,4},{9,5},... | collective-permute-start | bytes 737288 | tf_op jit(solution)/shard_map/ppermute | solution.py:275
  6.3 25.1 %collective-permute-start.6 = (bf16[10,96,128]{2,1,0:T(8,128)(2,1)S(1)}, bf16[10,96,128]{2,1,0:T(8,128)(2,1)S(1)}, u32[]{:S(2)}, u32[]{:S(2)}) collective-permute-start(bf16[10,96,128]{2,1,0:T(8,128)(2,1)S(1)} %get-tuple-element.43.rest_0_), channel_id=1, source_target_pairs={{0,8},{1,9},{2,10},{3,11},{4,12},{5,13},{6,14},{7,15},{8,0},{9,1},... | collective-permute-start | bytes 737288 | tf_op jit(solution)/shard_map/ppermute | solution.py:275
  10.8 0.7 %copy-start = (bf16[4,32,1280]{2,1,0:T(8,128)(2,1)}, bf16[4,32,1280]{2,1,0:T(8,128)(2,1)S(1)}, u32[]{:S(2)}) copy-start(bf16[4,32,1280]{2,1,0:T(8,128)(2,1)S(1)} %cut.1.rest_0_) | copy-start | bytes 983044
  11.5 10.5 %slice-start.1 = ((bf16[4,32,1280]{2,1,0:T(8,128)(2,1)}), bf16[2,32,1280]{2,1,0:T(8,128)(2,1)S(1)}, s32[]{:S(2)}) async-start(bf16[4,32,1280]{2,1,0:T(8,128)(2,1)} %copy-done), calls=%async_computation.1 | async-start | bytes 327680 | tf_op jit(solution)/shard_map/slice | solution.py:261
  11.5 12.1 %collective-permute-start.1 = (bf16[64,2560]{1,0:T(8,128)(2,1)S(1)}, bf16[64,2560]{1,0:T(8,128)(2,1)S(1)}, u32[]{:S(2)}, u32[]{:S(2)}) collective-permute-start(bf16[64,2560]{1,0:T(8,128)(2,1)S(1)} %pad_maximum_fusion), channel_id=1, source_target_pairs={{0,2},{1,3},{2,0},{3,1},{4,6},{5,7},{6,4},{7,5},{8,10},{9,11},{10,... | collective-permute-start | bytes 983048 | tf_op jit(solution)/shard_map/ppermute | solution.py:275
  13.1 6.5 %copy-start.2 = (bf16[2,32,1280]{2,1,0:T(8,128)(2,1)}, bf16[2,32,1280]{2,1,0:T(8,128)(2,1)S(1)}, u32[]{:S(2)}) copy-start(bf16[2,32,1280]{2,1,0:T(8,128)(2,1)S(1)} %collective-permute-done.3.rest_1_) | copy-start | bytes 491524
  19.6 11.8 %collective-permute-start.5 = (bf16[10,96,128]{2,1,0:T(8,128)(2,1)}, bf16[10,96,128]{2,1,0:T(8,128)(2,1)S(1)}, u32[]{:S(2)}, u32[]{:S(2)}) collective-permute-start(bf16[10,96,128]{2,1,0:T(8,128)(2,1)} %get-tuple-element.20), channel_id=1, source_target_pairs={{0,4},{1,5},{2,6},{3,7},{4,0},{5,1},{6,2},{7,3},{8,12},{9,13},{10,... | collective-permute-start | bytes 737288 | tf_op jit(solution)/shard_map/ppermute | solution.py:275
  22.0 7.5 %collective-permute-start.8 = (bf16[4,32,1280]{2,1,0:T(8,128)(2,1)S(1)}, bf16[4,32,1280]{2,1,0:T(8,128)(2,1)S(1)}, u32[]{:S(2)}, u32[]{:S(2)}) collective-permute-start(bf16[4,32,1280]{2,1,0:T(8,128)(2,1)S(1)} %pad_maximum_fusion.1), channel_id=1, source_target_pairs={{0,2},{1,3},{2,0},{3,1},{4,6},{5,7},{6,4},{7,5},{8,10},{9,11},{10,... | collective-permute-start | bytes 983048 | tf_op jit(solution)/shard_map/ppermute | solution.py:275
  23.7 5.9 %slice-start = ((bf16[4,32,1280]{2,1,0:T(8,128)(2,1)}), bf16[1,32,1280]{2,1,0:T(8,128)(2,1)S(1)}, s32[]{:S(2)}) async-start(bf16[4,32,1280]{2,1,0:T(8,128)(2,1)} %copy-done), calls=%async_computation | async-start | bytes 163840 | tf_op jit(solution)/shard_map/slice | solution.py:261
  23.7 5.9 %slice-start.2 = ((bf16[2,32,1280]{2,1,0:T(8,128)(2,1)}), bf16[1,32,1280]{2,1,0:T(8,128)(2,1)S(1)}, s32[]{:S(2)}) async-start(bf16[2,32,1280]{2,1,0:T(8,128)(2,1)} %copy-done.2), calls=%async_computation.2 | async-start | bytes 163840 | tf_op jit(solution)/shard_map/slice | solution.py:261
  23.7 8.7 %collective-permute-start.2 = (bf16[128,2560]{1,0:T(8,128)(2,1)S(1)}, bf16[128,2560]{1,0:T(8,128)(2,1)S(1)}, u32[]{:S(2)}, u32[]{:S(2)}) collective-permute-start(bf16[128,2560]{1,0:T(8,128)(2,1)S(1)} %constant_dynamic-update-slice_fusion.near), channel_id=1, source_target_pairs={{0,1},{1,0},{2,3},{3,2},{4,5},{5,4},{6,7},{7,6},{8,9},{9,8},{10,11... | collective-permute-start | bytes 1966088 | tf_op jit(solution)/shard_map/ppermute | solution.py:275
  29.6 2.3 %collective-permute-start.9 = (bf16[4,32,1280]{2,1,0:T(8,128)(2,1)S(1)}, bf16[4,32,1280]{2,1,0:T(8,128)(2,1)S(1)}, u32[]{:S(2)}, u32[]{:S(2)}) collective-permute-start(bf16[4,32,1280]{2,1,0:T(8,128)(2,1)S(1)} %pad_maximum_fusion.2), channel_id=1, source_target_pairs={{0,1},{1,0},{2,3},{3,2},{4,5},{5,4},{6,7},{7,6},{8,9},{9,8},{10,11... | collective-permute-start | bytes 983048 | tf_op jit(solution)/shard_map/ppermute | solution.py:275
  29.7 0.7 %copy-start.6 = (s32[20,3]{0,1:T(4,128)S(1)}, s32[20,3]{0,1:T(4,128)}, u32[]{:S(2)}) copy-start(s32[20,3]{0,1:T(4,128)} %param.8) | copy-start | bytes 724
  30.6 0.7 %copy-start.7 = (s32[20]{0:T(128)S(1)}, s32[20]{0:T(128)}, u32[]{:S(2)}) copy-start(s32[20]{0:T(128)} %param.9) | copy-start | bytes 244
  31.3 1.0 %copy-start.1 = (bf16[4,32,1280]{2,1,0:T(8,128)(2,1)S(1)}, bf16[4,32,1280]{2,1,0:T(8,128)(2,1)}, u32[]{:S(2)}) copy-start(bf16[4,32,1280]{2,1,0:T(8,128)(2,1)} %copy-done) | copy-start | bytes 983044
  31.3 1.0 %copy-start.3 = (bf16[2,32,1280]{2,1,0:T(8,128)(2,1)S(1)}, bf16[2,32,1280]{2,1,0:T(8,128)(2,1)}, u32[]{:S(2)}) copy-start(bf16[2,32,1280]{2,1,0:T(8,128)(2,1)} %copy-done.2) | copy-start | bytes 491524
  34.2 5.5 %collective-permute-start.10 = (bf16[2,32,1280]{2,1,0:T(8,128)(2,1)S(1)}, bf16[2,32,1280]{2,1,0:T(8,128)(2,1)S(1)}, u32[]{:S(2)}, u32[]{:S(2)}) collective-permute-start(bf16[2,32,1280]{2,1,0:T(8,128)(2,1)S(1)} %slice.29), channel_id=1, source_target_pairs={{0,1},{1,0},{2,3},{3,2},{4,5},{5,4},{6,7},{7,6},{8,9},{9,8},{10,11... | collective-permute-start | bytes 491528 | tf_op jit(solution)/shard_map/ppermute | solution.py:275
  34.8 10.7 %collective-permute-start.12 = (bf16[4,32,1280]{2,1,0:T(8,128)(2,1)S(1)}, bf16[4,32,1280]{2,1,0:T(8,128)(2,1)S(1)}, u32[]{:S(2)}, u32[]{:S(2)}) collective-permute-start(bf16[4,32,1280]{2,1,0:T(8,128)(2,1)S(1)} %get-tuple-element.27), channel_id=1, source_target_pairs={{0,4},{1,5},{2,6},{3,7},{4,0},{5,1},{6,2},{7,3},{8,12},{9,13},{10,... | collective-permute-start | bytes 983048 | tf_op jit(solution)/shard_map/ppermute | solution.py:275
  36.5 17.1 %collective-permute-start.16 = (bf16[10,96,128]{2,1,0:T(8,128)(2,1)S(1)}, bf16[10,96,128]{2,1,0:T(8,128)(2,1)S(1)}, u32[]{:S(2)}, u32[]{:S(2)}) collective-permute-start(bf16[10,96,128]{2,1,0:T(8,128)(2,1)S(1)} %get-tuple-element.35), channel_id=1, source_target_pairs={{0,8},{1,9},{2,10},{3,11},{4,12},{5,13},{6,14},{7,15},{8,0},{9,1},... | collective-permute-start | bytes 737288 | tf_op jit(solution)/shard_map/ppermute | solution.py:275
  36.5 24.7 %collective-permute-start.18 = (bf16[10,96,128]{2,1,0:T(8,128)(2,1)S(1)}, bf16[10,96,128]{2,1,0:T(8,128)(2,1)S(1)}, u32[]{:S(2)}, u32[]{:S(2)}) collective-permute-start(bf16[10,96,128]{2,1,0:T(8,128)(2,1)S(1)} %get-tuple-element.37), channel_id=1, source_target_pairs={{0,12},{1,13},{2,14},{3,15},{4,8},{5,9},{6,10},{7,11},{8,4},{9,5},... | collective-permute-start | bytes 737288 | tf_op jit(solution)/shard_map/ppermute | solution.py:275
  39.8 5.8 %collective-permute-start.11 = (bf16[2,32,1280]{2,1,0:T(8,128)(2,1)S(1)}, bf16[2,32,1280]{2,1,0:T(8,128)(2,1)S(1)}, u32[]{:S(2)}, u32[]{:S(2)}) collective-permute-start(bf16[2,32,1280]{2,1,0:T(8,128)(2,1)S(1)} %pad_maximum_fusion.5), channel_id=1, source_target_pairs={{0,2},{1,3},{2,0},{3,1},{4,6},{5,7},{6,4},{7,5},{8,10},{9,11},{10,... | collective-permute-start | bytes 491528 | tf_op jit(solution)/shard_map/ppermute | solution.py:275
  41.3 19.9 %collective-permute-start.17 = (bf16[10,96,128]{2,1,0:T(8,128)(2,1)S(1)}, bf16[10,96,128]{2,1,0:T(8,128)(2,1)S(1)}, u32[]{:S(2)}, u32[]{:S(2)}) collective-permute-start(bf16[10,96,128]{2,1,0:T(8,128)(2,1)S(1)} %get-tuple-element.36), channel_id=1, source_target_pairs={{0,4},{1,5},{2,6},{3,7},{4,0},{5,1},{6,2},{7,3},{8,12},{9,13},{10,... | collective-permute-start | bytes 737288 | tf_op jit(solution)/shard_map/ppermute | solution.py:275
  45.5 4.8 %collective-permute-start.13 = (bf16[1,32,1280]{2,1,0:T(8,128)(2,1)S(1)}, bf16[1,32,1280]{2,1,0:T(8,128)(2,1)S(1)}, u32[]{:S(2)}, u32[]{:S(2)}) collective-permute-start(bf16[1,32,1280]{2,1,0:T(8,128)(2,1)S(1)} %get-tuple-element.28), channel_id=1, source_target_pairs={{0,3},{1,2},{2,1},{3,0},{4,7},{5,6},{6,5},{7,4},{8,11},{9,10},{10,... | collective-permute-start | bytes 245768 | tf_op jit(solution)/shard_map/ppermute | solution.py:275
  45.6 6.5 %collective-permute-start.14 = (bf16[1,32,1280]{2,1,0:T(8,128)(2,1)S(1)}, bf16[1,32,1280]{2,1,0:T(8,128)(2,1)S(1)}, u32[]{:S(2)}, u32[]{:S(2)}) collective-permute-start(bf16[1,32,1280]{2,1,0:T(8,128)(2,1)S(1)} %get-tuple-element.29), channel_id=1, source_target_pairs={{0,2},{1,3},{2,0},{3,1},{4,6},{5,7},{6,4},{7,5},{8,10},{9,11},{10,... | collective-permute-start | bytes 245768 | tf_op jit(solution)/shard_map/ppermute | solution.py:275
  50.3 1.8 %collective-permute-start.15 = (bf16[1,32,1280]{2,1,0:T(8,128)(2,1)S(1)}, bf16[1,32,1280]{2,1,0:T(8,128)(2,1)S(1)}, u32[]{:S(2)}, u32[]{:S(2)}) collective-permute-start(bf16[1,32,1280]{2,1,0:T(8,128)(2,1)S(1)} %get-tuple-element.30), channel_id=1, source_target_pairs={{0,1},{1,0},{2,3},{3,2},{4,5},{5,4},{6,7},{7,6},{8,9},{9,8},{10,11... | collective-permute-start | bytes 245768 | tf_op jit(solution)/shard_map/ppermute | solution.py:275

commit v23 on v22

--- a/solution.py
+++ b/solution.py
@@ -298,7 +298,7 @@
     if direct:
         same = lax.dynamic_slice_in_dim(by_stripe, half * share, share, 0)
         other = lax.dynamic_slice_in_dim(by_stripe, (1 - half) * share, share, 0)
-        late, arrived = lax.optimization_barrier((other, arrived))
+        late, arrived[0] = lax.optimization_barrier((other, arrived[0]))
         pieces = [same] + [swap((late if p == 1 else other) if p % PAIR else same, p, 0) for p in range(1, fsdp)]
         weights = stack_call(jnp.stack([z ^ p for p in range(fsdp)]).astype(jnp.int32), pieces)
     else:

time: 62.4 us -> 63.1 us (1.011)
  the two profiles are of different devices: /device:TPU:16 before, /device:TPU:12 now
where the time goes in v23:
time: 63.1 us; the launch traced here: 62.9 us
  waiting for transfers between devices  26.4 us (42%)
  starting transfers between devices  21.8 us (35%)
  Pallas kernels  8.67 us (14%)
  local copies, waits for them, and re-layouts  4.77 us (8%)
  between operations  0.92 us (1%)
    ppermute x19, waiting for transfers between devices, swap(): return lax.ppermute(value, ('fsdp', 'tensor'), pairs)  26.4 us
    ppermute x19, starting transfers between devices, swap(): return lax.ppermute(value, ('fsdp', 'tensor'), pairs)  21.8 us
    unnamed x19, local copies, waits for them, and re-layouts  2.77 us
    pallas_call x1, Pallas kernels, forward_call(): pl.pallas_call(functools.partial(forward_kernel, sizes), out_shape=[jax.S...  1.83 us
    pallas_call x2, Pallas kernels, sum_call(): pl.pallas_call(sum_kernel if before is None else sum_into_kernel, out_sha...  1.77 us
    pallas_call x1, Pallas kernels, cut_call(): pl.pallas_call(cut_kernel, out_shape=[jax.ShapeDtypeStruct((count // part...  1.59 us
    pallas_call x1, Pallas kernels, join_call(): pl.pallas_call(functools.partial(join_kernel, refs), out_shape=jax.ShapeD...  1.44 us
    pallas_call x1, Pallas kernels, backward_call(): pl.pallas_call(functools.partial(backward_kernel, sizes), out_shape=[jax....  1.37 us
  transfers between devices with their start and end apart: 19, of which 9 were waited for; matrix products, arithmetic and copies ran while one was open for 4% of the time, Pallas kernels for 9%

profile of v23, /device:TPU:12, one launch (start us, length us, event | category | flops | bytes accessed | tf_op | source)
XLA Modules:
  0.0 62.9 jit_solution(8219735071892613647)
XLA Ops:
  1.1 1.0 %dynamic-slice_bitcast_fusion.3 = (bf16[1,32,1280]{2,1,0:T(8,128)(2,1)S(1)}, bf16[1,32,1280]{2,1,0:T(8,128)(2,1)S(1)}, bf16[1,32,1280]{2,1,0:T(8,128)(2,1)S(1)}, bf16[1,32,1280]{2,1,0:T(8,128)(2,1)S(1)}) fusion(bf16[32,10240]{1,0:T(8,128)(2,1)} %whole.1, s32[]{:T(128)S(6)} %select_n.30, s32[]{:T(128)S(6)} %select_n.29, s32[]{:T(128)S(6)} %select_n.28, ...), kind=kLoop, calls=%fused_computation.9 | loop fusion | bytes 655376 | tf_op jit(solution)/shard_map/stack | solution.py:294
  2.2 1.6 %collective-permute-start.3 = (bf16[2,32,1280]{2,1,0:T(8,128)(2,1)S(1)}, bf16[2,32,1280]{2,1,0:T(8,128)(2,1)S(1)}, u32[]{:S(2)}, u32[]{:S(2)}) collective-permute-start(bf16[2,32,1280]{2,1,0:T(8,128)(2,1)S(1)} %pad_maximum_fusion.3), channel_id=1, source_target_pairs={{0,4},{1,5},{2,6},{3,7},{4,0},{5,1},{6,2},{7,3},{8,12},{9,13},{10,... | collective-permute-start | bytes 491528 | tf_op jit(solution)/shard_map/ppermute | solution.py:275
  4.4 0.7 %dynamic-slice_bitcast_fusion = (bf16[10,96,128]{2,1,0:T(8,128)(2,1)}, bf16[10,96,128]{2,1,0:T(8,128)(2,1)S(1)}) fusion(bf16[96,20,128]{2,0,1:T(8,128)(2,1)S(1)} %copy-done.5, s32[]{:T(128)S(6)} %select_n.27, s32[]{:T(128)S(6)} %select_n.26), kind=kLoop, calls=%fused_computation.3 | loop fusion | bytes 983048 | tf_op jit(solution)/shard_map/dynamic_slice | solution.py:300
  5.1 2.7 %collective-permute-start.6 = (bf16[10,96,128]{2,1,0:T(8,128)(2,1)}, bf16[10,96,128]{2,1,0:T(8,128)(2,1)S(1)}, u32[]{:S(2)}, u32[]{:S(2)}) collective-permute-start(bf16[10,96,128]{2,1,0:T(8,128)(2,1)} %get-tuple-element.19), channel_id=1, source_target_pairs={{0,12},{1,13},{2,14},{3,15},{4,8},{5,9},{6,10},{7,11},{8,4},{9,5},... | collective-permute-start | bytes 737288 | tf_op jit(solution)/shard_map/ppermute | solution.py:275
  7.8 1.2 %collective-permute-start.5 = (bf16[10,96,128]{2,1,0:T(8,128)(2,1)S(1)}, bf16[10,96,128]{2,1,0:T(8,128)(2,1)S(1)}, u32[]{:S(2)}, u32[]{:S(2)}) collective-permute-start(bf16[10,96,128]{2,1,0:T(8,128)(2,1)S(1)} %get-tuple-element.41.rest_0_), channel_id=1, source_target_pairs={{0,8},{1,9},{2,10},{3,11},{4,12},{5,13},{6,14},{7,15},{8,0},{9,1},... | collective-permute-start | bytes 737288 | tf_op jit(solution)/shard_map/ppermute | solution.py:275
  9.2 1.6 %cut.1.rest_0_ = bf16[4,32,1280]{2,1,0:T(8,128)(2,1)S(1)} custom-call(s32[4]{0:T(128)S(1)} %pad_add_fusion.2.starts, bf16[32,10240]{1,0:T(8,128)(2,1)} %whole.1), custom_call_target="tpu_custom_call" | custom-call | tf_op jit(solution)/shard_map/cut/pallas_call | solution.py:55
  10.8 0.7 %copy-done = bf16[4,32,1280]{2,1,0:T(8,128)(2,1)} copy-done((bf16[4,32,1280]{2,1,0:T(8,128)(2,1)}, bf16[4,32,1280]{2,1,0:T(8,128)(2,1)S(1)}, u32[]{:S(2)}) %copy-start) | copy-done | bytes 327704
  11.5 1.6 %collective-permute-start.1 = (bf16[64,2560]{1,0:T(8,128)(2,1)S(1)}, bf16[64,2560]{1,0:T(8,128)(2,1)S(1)}, u32[]{:S(2)}, u32[]{:S(2)}) collective-permute-start(bf16[64,2560]{1,0:T(8,128)(2,1)S(1)} %pad_maximum_fusion), channel_id=1, source_target_pairs={{0,2},{1,3},{2,0},{3,1},{4,6},{5,7},{6,4},{7,5},{8,10},{9,11},{10,... | collective-permute-start | bytes 983048 | tf_op jit(solution)/shard_map/ppermute | solution.py:275
  13.1 1.9 %collective-permute-done.7.rest_2_ = bf16[2,32,1280]{2,1,0:T(8,128)(2,1)S(1)} collective-permute-done((bf16[2,32,1280]{2,1,0:T(8,128)(2,1)S(1)}, bf16[2,32,1280]{2,1,0:T(8,128)(2,1)S(1)}, u32[]{:S(2)}, u32[]{:S(2)}) %collective-permute-start.7) | collective-permute-done | bytes 163872 | tf_op jit(solution)/shard_map/ppermute | solution.py:275
  15.1 1.6 %collective-permute-start.8 = (bf16[4,32,1280]{2,1,0:T(8,128)(2,1)S(1)}, bf16[4,32,1280]{2,1,0:T(8,128)(2,1)S(1)}, u32[]{:S(2)}, u32[]{:S(2)}) collective-permute-start(bf16[4,32,1280]{2,1,0:T(8,128)(2,1)S(1)} %pad_maximum_fusion.1), channel_id=1, source_target_pairs={{0,2},{1,3},{2,0},{3,1},{4,6},{5,7},{6,4},{7,5},{8,10},{9,11},{10,... | collective-permute-start | bytes 983048 | tf_op jit(solution)/shard_map/ppermute | solution.py:275
  16.6 0.7 %copy-done.2 = bf16[2,32,1280]{2,1,0:T(8,128)(2,1)} copy-done((bf16[2,32,1280]{2,1,0:T(8,128)(2,1)}, bf16[2,32,1280]{2,1,0:T(8,128)(2,1)S(1)}, u32[]{:S(2)}) %copy-start.2) | copy-done | bytes 163864
  17.3 1.3 %collective-permute-start.4 = (bf16[10,96,128]{2,1,0:T(8,128)(2,1)}, bf16[10,96,128]{2,1,0:T(8,128)(2,1)S(1)}, u32[]{:S(2)}, u32[]{:S(2)}) collective-permute-start(bf16[10,96,128]{2,1,0:T(8,128)(2,1)} %get-tuple-element.19), channel_id=1, source_target_pairs={{0,4},{1,5},{2,6},{3,7},{4,0},{5,1},{6,2},{7,3},{8,12},{9,13},{10,... | collective-permute-start | bytes 737288 | tf_op jit(solution)/shard_map/ppermute | solution.py:275
  18.6 3.6 %collective-permute-done.1 = bf16[64,2560]{1,0:T(8,128)(2,1)S(1)} collective-permute-done((bf16[64,2560]{1,0:T(8,128)(2,1)S(1)}, bf16[64,2560]{1,0:T(8,128)(2,1)S(1)}, u32[]{:S(2)}, u32[]{:S(2)}) %collective-permute-start.1) | collective-permute-done | bytes 327712 | tf_op jit(solution)/shard_map/ppermute | solution.py:275
  22.4 4.3 %collective-permute-done.8.rest_3_ = bf16[4,32,1280]{2,1,0:T(8,128)(2,1)S(1)} collective-permute-done((bf16[4,32,1280]{2,1,0:T(8,128)(2,1)S(1)}, bf16[4,32,1280]{2,1,0:T(8,128)(2,1)S(1)}, u32[]{:S(2)}, u32[]{:S(2)}) %collective-permute-start.8) | collective-permute-done | bytes 327712 | tf_op jit(solution)/shard_map/ppermute | solution.py:275
  27.7 0.6 %copy-done.7 = s32[20]{0:T(128)S(1)} copy-done((s32[20]{0:T(128)S(1)}, s32[20]{0:T(128)}, u32[]{:S(2)}) %copy-start.7) | copy-done | bytes 104
  28.5 1.2 %collective-permute-done.4.rest_1_ = bf16[10,96,128]{2,1,0:T(8,128)(2,1)S(1)} collective-permute-done((bf16[10,96,128]{2,1,0:T(8,128)(2,1)}, bf16[10,96,128]{2,1,0:T(8,128)(2,1)S(1)}, u32[]{:S(2)}, u32[]{:S(2)}) %collective-permute-start.4) | collective-permute-done | bytes 245792 | tf_op jit(solution)/shard_map/ppermute | solution.py:275
  30.4 1.8 %forward.1 = (bf16[4,32,1280]{2,1,0:T(8,128)(2,1)S(1)}, bf16[4,32,1280]{2,1,0:T(8,128)(2,1)S(1)}, bf16[256,1280]{1,0:T(8,128)(2,1)S(1)}) custom-call(s32[82]{0:T(128)S(1)} %pad_add_fusion.scalars, bf16[128,2560]{1,0:T(8,128)(2,1)S(1)} %constant_dynamic-update-slice_fusion.near, bf16[128,2560]{1,0:T(8,128)(2,1)S(1)} %collective-permute-done.2.far, ...), custom_call_target="tpu_custom_call" | custom-call | tf_op jit(solution)/shard_map/forward/pallas_call | solution.py:143
  32.4 0.8 %collective-permute-start.12 = (bf16[4,32,1280]{2,1,0:T(8,128)(2,1)S(1)}, bf16[4,32,1280]{2,1,0:T(8,128)(2,1)S(1)}, u32[]{:S(2)}, u32[]{:S(2)}) collective-permute-start(bf16[4,32,1280]{2,1,0:T(8,128)(2,1)S(1)} %get-tuple-element.25), channel_id=1, source_target_pairs={{0,4},{1,5},{2,6},{3,7},{4,0},{5,1},{6,2},{7,3},{8,12},{9,13},{10,... | collective-permute-start | bytes 983048 | tf_op jit(solution)/shard_map/ppermute | solution.py:275
  33.1 1.4 %backward.1 = (f32[10,96,128]{2,1,0:T(8,128)S(1)}, bf16[10,96,128]{2,1,0:T(8,128)(2,1)S(1)}, bf16[10,96,128]{2,1,0:T(8,128)(2,1)S(1)}, bf16[10,96,128]{2,1,0:T(8,128)(2,1)S(1)}) custom-call(s32[82]{0:T(128)S(1)} %pad_add_fusion.scalars, bf16[128,2560]{1,0:T(8,128)(2,1)S(1)} %constant_dynamic-update-slice_fusion.near, ...), custom_call_target="tpu_custom_call" | custom-call | tf_op jit(solution)/shard_map/backward/pallas_call | solution.py:210
  34.5 4.8 %collective-permute-start.16 = (bf16[10,96,128]{2,1,0:T(8,128)(2,1)S(1)}, bf16[10,96,128]{2,1,0:T(8,128)(2,1)S(1)}, u32[]{:S(2)}, u32[]{:S(2)}) collective-permute-start(bf16[10,96,128]{2,1,0:T(8,128)(2,1)S(1)} %get-tuple-element.33), channel_id=1, source_target_pairs={{0,8},{1,9},{2,10},{3,11},{4,12},{5,13},{6,14},{7,15},{8,0},{9,1},... | collective-permute-start | bytes 737288 | tf_op jit(solution)/shard_map/ppermute | solution.py:275
  39.3 0.6 collective-permute-start.18
  39.9 0.6 %collective-permute-start.11 = (bf16[2,32,1280]{2,1,0:T(8,128)(2,1)S(1)}, bf16[2,32,1280]{2,1,0:T(8,128)(2,1)S(1)}, u32[]{:S(2)}, u32[]{:S(2)}) collective-permute-start(bf16[2,32,1280]{2,1,0:T(8,128)(2,1)S(1)} %pad_maximum_fusion.5), channel_id=1, source_target_pairs={{0,2},{1,3},{2,0},{3,1},{4,6},{5,7},{6,4},{7,5},{8,10},{9,11},{10,... | collective-permute-start | bytes 491528 | tf_op jit(solution)/shard_map/ppermute | solution.py:275
  40.6 1.4 %collective-permute-start.17 = (bf16[10,96,128]{2,1,0:T(8,128)(2,1)S(1)}, bf16[10,96,128]{2,1,0:T(8,128)(2,1)S(1)}, u32[]{:S(2)}, u32[]{:S(2)}) collective-permute-start(bf16[10,96,128]{2,1,0:T(8,128)(2,1)S(1)} %get-tuple-element.34), channel_id=1, source_target_pairs={{0,4},{1,5},{2,6},{3,7},{4,0},{5,1},{6,2},{7,3},{8,12},{9,13},{10,... | collective-permute-start | bytes 737288 | tf_op jit(solution)/shard_map/ppermute | solution.py:275
  42.0 4.1 %collective-permute-done.12.rest_0_ = bf16[4,32,1280]{2,1,0:T(8,128)(2,1)S(1)} collective-permute-done((bf16[4,32,1280]{2,1,0:T(8,128)(2,1)S(1)}, bf16[4,32,1280]{2,1,0:T(8,128)(2,1)S(1)}, u32[]{:S(2)}, u32[]{:S(2)}) %collective-permute-start.12) | collective-permute-done | bytes 327712 | tf_op jit(solution)/shard_map/ppermute | solution.py:275
  46.5 1.4 %collective-permute-start.14 = (bf16[1,32,1280]{2,1,0:T(8,128)(2,1)S(1)}, bf16[1,32,1280]{2,1,0:T(8,128)(2,1)S(1)}, u32[]{:S(2)}, u32[]{:S(2)}) collective-permute-start(bf16[1,32,1280]{2,1,0:T(8,128)(2,1)S(1)} %get-tuple-element.27), channel_id=1, source_target_pairs={{0,2},{1,3},{2,0},{3,1},{4,6},{5,7},{6,4},{7,5},{8,10},{9,11},{10,... | collective-permute-start | bytes 245768 | tf_op jit(solution)/shard_map/ppermute | solution.py:275
  47.9 2.8 %collective-permute-done.13.rest_3_ = bf16[1,32,1280]{2,1,0:T(8,128)(2,1)S(1)} collective-permute-done((bf16[1,32,1280]{2,1,0:T(8,128)(2,1)S(1)}, bf16[1,32,1280]{2,1,0:T(8,128)(2,1)S(1)}, u32[]{:S(2)}, u32[]{:S(2)}) %collective-permute-start.13) | collective-permute-done | bytes 81952 | tf_op jit(solution)/shard_map/ppermute | solution.py:275
  51.3 1.4 %collective-permute-done.14.rest_4_ = bf16[1,32,1280]{2,1,0:T(8,128)(2,1)S(1)} collective-permute-done((bf16[1,32,1280]{2,1,0:T(8,128)(2,1)S(1)}, bf16[1,32,1280]{2,1,0:T(8,128)(2,1)S(1)}, u32[]{:S(2)}, u32[]{:S(2)}) %collective-permute-start.14) | collective-permute-done | bytes 81952 | tf_op jit(solution)/shard_map/ppermute | solution.py:275
  52.7 1.4 %join.1 = bf16[32,10240]{1,0:T(8,128)(2,1)} custom-call(s32[8]{0:T(128)S(1)} %stack.80.starts, bf16[4,32,1280]{2,1,0:T(8,128)(2,1)S(1)} %get-tuple-element.21.rest_0_, bf16[2,32,1280]{2,1,0:T(8,128)(2,1)S(1)} %collective-permute-done.10.rest_1_, bf16[2,32,1280]{2,1,0:T(8,128)(2,1)S(1)} %collective-permute-done.11.rest_2_, ...), custom_call_target="tpu_custom_call" | custom-call | tf_op jit(solution)/shard_map/join/pallas_call | solution.py:92
  54.1 2.1 %collective-permute-done.16.rest_1_ = bf16[10,96,128]{2,1,0:T(8,128)(2,1)S(1)} collective-permute-done((bf16[10,96,128]{2,1,0:T(8,128)(2,1)S(1)}, bf16[10,96,128]{2,1,0:T(8,128)(2,1)S(1)}, u32[]{:S(2)}, u32[]{:S(2)}) %collective-permute-start.16) | collective-permute-done | bytes 245792 | tf_op jit(solution)/shard_map/ppermute | solution.py:275
  56.2 0.9 %sum.2.before = f32[2,10,96,128]{3,2,1,0:T(8,128)} custom-call(s32[1]{0:T(128)} %bitcast.19.half, f32[10,96,128]{2,1,0:T(8,128)S(1)} %get-tuple-element.32.rest_0_, bf16[10,96,128]{2,1,0:T(8,128)(2,1)S(1)} %collective-permute-done.16.rest_1_), custom_call_target="tpu_custom_call" | custom-call | tf_op jit(solution)/shard_map/sum/pallas_call | solution.py:242
  57.1 4.9 %collective-permute-done.18.rest_1_ = bf16[10,96,128]{2,1,0:T(8,128)(2,1)S(1)} collective-permute-done((bf16[10,96,128]{2,1,0:T(8,128)(2,1)S(1)}, bf16[10,96,128]{2,1,0:T(8,128)(2,1)S(1)}, u32[]{:S(2)}, u32[]{:S(2)}) %collective-permute-start.18) | collective-permute-done | bytes 245792 | tf_op jit(solution)/shard_map/ppermute | solution.py:275
  62.0 0.9 %sum.3 = f32[2,10,96,128]{3,2,1,0:T(8,128)} custom-call(s32[1]{0:T(128)S(6)} %sub.5.half, f32[2,10,96,128]{3,2,1,0:T(8,128)} %sum.2.before, bf16[10,96,128]{2,1,0:T(8,128)(2,1)S(1)} %collective-permute-done.17.rest_0_, bf16[10,96,128]{2,1,0:T(8,128)(2,1)S(1)} %collective-permute-done.18.rest_1_), custom_call_target="tpu_custom_call", output_to_operand_aliasing={{}: (1, {})} | custom-call | tf_op jit(solution)/shard_map/sum/pallas_call | solution.py:242
  (58 shorter events, 4.2 us)
Async XLA Ops:
  0.6 10.9 %collective-permute-start = (bf16[32,2560]{1,0:T(8,128)(2,1)}, bf16[32,2560]{1,0:T(8,128)(2,1)S(1)}, u32[]{:S(2)}, u32[]{:S(2)}) collective-permute-start(bf16[32,2560]{1,0:T(8,128)(2,1)} %param.5), channel_id=1, source_target_pairs={{0,4},{1,5},{2,6},{3,7},{4,0},{5,1},{6,2},{7,3},{8,12},{9,13},{10,... | collective-permute-start | bytes 491528 | tf_op jit(solution)/shard_map/ppermute | solution.py:275
  2.2 2.2 %copy-start.5 = (bf16[96,20,128]{2,0,1:T(8,128)(2,1)S(1)}, bf16[96,20,128]{2,0,1:T(8,128)(2,1)}, u32[]{:S(2)}) copy-start(bf16[96,20,128]{2,0,1:T(8,128)(2,1)} %param.6) | copy-start | bytes 1474564
  2.2 14.4 %collective-permute-start.3 = (bf16[2,32,1280]{2,1,0:T(8,128)(2,1)S(1)}, bf16[2,32,1280]{2,1,0:T(8,128)(2,1)S(1)}, u32[]{:S(2)}, u32[]{:S(2)}) collective-permute-start(bf16[2,32,1280]{2,1,0:T(8,128)(2,1)S(1)} %pad_maximum_fusion.3), channel_id=1, source_target_pairs={{0,4},{1,5},{2,6},{3,7},{4,0},{5,1},{6,2},{7,3},{8,12},{9,13},{10,... | collective-permute-start | bytes 491528 | tf_op jit(solution)/shard_map/ppermute | solution.py:275
  3.9 11.1 %collective-permute-start.7 = (bf16[2,32,1280]{2,1,0:T(8,128)(2,1)S(1)}, bf16[2,32,1280]{2,1,0:T(8,128)(2,1)S(1)}, u32[]{:S(2)}, u32[]{:S(2)}) collective-permute-start(bf16[2,32,1280]{2,1,0:T(8,128)(2,1)S(1)} %pad_maximum_fusion.4), channel_id=1, source_target_pairs={{0,4},{1,5},{2,6},{3,7},{4,0},{5,1},{6,2},{7,3},{8,12},{9,13},{10,... | collective-permute-start | bytes 491528 | tf_op jit(solution)/shard_map/ppermute | solution.py:275
  4.4 4.7 %copy-start.4 = (bf16[32,2560]{1,0:T(8,128)(2,1)S(1)}, bf16[32,2560]{1,0:T(8,128)(2,1)}, u32[]{:S(2)}) copy-start(bf16[32,2560]{1,0:T(8,128)(2,1)} %param.5) | copy-start | bytes 491524
  5.1 23.3 %collective-permute-start.6 = (bf16[10,96,128]{2,1,0:T(8,128)(2,1)}, bf16[10,96,128]{2,1,0:T(8,128)(2,1)S(1)}, u32[]{:S(2)}, u32[]{:S(2)}) collective-permute-start(bf16[10,96,128]{2,1,0:T(8,128)(2,1)} %get-tuple-element.19), channel_id=1, source_target_pairs={{0,12},{1,13},{2,14},{3,15},{4,8},{5,9},{6,10},{7,11},{8,4},{9,5},... | collective-permute-start | bytes 737288 | tf_op jit(solution)/shard_map/ppermute | solution.py:275
  7.8 20.6 %collective-permute-start.5 = (bf16[10,96,128]{2,1,0:T(8,128)(2,1)S(1)}, bf16[10,96,128]{2,1,0:T(8,128)(2,1)S(1)}, u32[]{:S(2)}, u32[]{:S(2)}) collective-permute-start(bf16[10,96,128]{2,1,0:T(8,128)(2,1)S(1)} %get-tuple-element.41.rest_0_), channel_id=1, source_target_pairs={{0,8},{1,9},{2,10},{3,11},{4,12},{5,13},{6,14},{7,15},{8,0},{9,1},... | collective-permute-start | bytes 737288 | tf_op jit(solution)/shard_map/ppermute | solution.py:275
  10.8 0.7 %copy-start = (bf16[4,32,1280]{2,1,0:T(8,128)(2,1)}, bf16[4,32,1280]{2,1,0:T(8,128)(2,1)S(1)}, u32[]{:S(2)}) copy-start(bf16[4,32,1280]{2,1,0:T(8,128)(2,1)S(1)} %cut.1.rest_0_) | copy-start | bytes 983044
  11.5 3.5 %slice-start.1 = ((bf16[4,32,1280]{2,1,0:T(8,128)(2,1)}), bf16[2,32,1280]{2,1,0:T(8,128)(2,1)S(1)}, s32[]{:S(2)}) async-start(bf16[4,32,1280]{2,1,0:T(8,128)(2,1)} %copy-done), calls=%async_computation.1 | async-start | bytes 327680 | tf_op jit(solution)/shard_map/slice | solution.py:261
  11.5 10.7 %collective-permute-start.1 = (bf16[64,2560]{1,0:T(8,128)(2,1)S(1)}, bf16[64,2560]{1,0:T(8,128)(2,1)S(1)}, u32[]{:S(2)}, u32[]{:S(2)}) collective-permute-start(bf16[64,2560]{1,0:T(8,128)(2,1)S(1)} %pad_maximum_fusion), channel_id=1, source_target_pairs={{0,2},{1,3},{2,0},{3,1},{4,6},{5,7},{6,4},{7,5},{8,10},{9,11},{10,... | collective-permute-start | bytes 983048 | tf_op jit(solution)/shard_map/ppermute | solution.py:275
  15.1 11.6 %collective-permute-start.8 = (bf16[4,32,1280]{2,1,0:T(8,128)(2,1)S(1)}, bf16[4,32,1280]{2,1,0:T(8,128)(2,1)S(1)}, u32[]{:S(2)}, u32[]{:S(2)}) collective-permute-start(bf16[4,32,1280]{2,1,0:T(8,128)(2,1)S(1)} %pad_maximum_fusion.1), channel_id=1, source_target_pairs={{0,2},{1,3},{2,0},{3,1},{4,6},{5,7},{6,4},{7,5},{8,10},{9,11},{10,... | collective-permute-start | bytes 983048 | tf_op jit(solution)/shard_map/ppermute | solution.py:275
  16.6 0.7 %copy-start.2 = (bf16[2,32,1280]{2,1,0:T(8,128)(2,1)}, bf16[2,32,1280]{2,1,0:T(8,128)(2,1)S(1)}, u32[]{:S(2)}) copy-start(bf16[2,32,1280]{2,1,0:T(8,128)(2,1)S(1)} %collective-permute-done.3.rest_1_) | copy-start | bytes 491524
  17.3 12.4 %collective-permute-start.4 = (bf16[10,96,128]{2,1,0:T(8,128)(2,1)}, bf16[10,96,128]{2,1,0:T(8,128)(2,1)S(1)}, u32[]{:S(2)}, u32[]{:S(2)}) collective-permute-start(bf16[10,96,128]{2,1,0:T(8,128)(2,1)} %get-tuple-element.19), channel_id=1, source_target_pairs={{0,4},{1,5},{2,6},{3,7},{4,0},{5,1},{6,2},{7,3},{8,12},{9,13},{10,... | collective-permute-start | bytes 737288 | tf_op jit(solution)/shard_map/ppermute | solution.py:275
  22.3 4.4 %slice-start = ((bf16[4,32,1280]{2,1,0:T(8,128)(2,1)}), bf16[1,32,1280]{2,1,0:T(8,128)(2,1)S(1)}, s32[]{:S(2)}) async-start(bf16[4,32,1280]{2,1,0:T(8,128)(2,1)} %copy-done), calls=%async_computation | async-start | bytes 163840 | tf_op jit(solution)/shard_map/slice | solution.py:261
  22.3 4.4 %slice-start.2 = ((bf16[2,32,1280]{2,1,0:T(8,128)(2,1)}), bf16[1,32,1280]{2,1,0:T(8,128)(2,1)S(1)}, s32[]{:S(2)}) async-start(bf16[2,32,1280]{2,1,0:T(8,128)(2,1)} %copy-done.2), calls=%async_computation.2 | async-start | bytes 163840 | tf_op jit(solution)/shard_map/slice | solution.py:261
  22.3 8.1 %collective-permute-start.2 = (bf16[128,2560]{1,0:T(8,128)(2,1)S(1)}, bf16[128,2560]{1,0:T(8,128)(2,1)S(1)}, u32[]{:S(2)}, u32[]{:S(2)}) collective-permute-start(bf16[128,2560]{1,0:T(8,128)(2,1)S(1)} %constant_dynamic-update-slice_fusion.near), channel_id=1, source_target_pairs={{0,1},{1,0},{2,3},{3,2},{4,5},{5,4},{6,7},{7,6},{8,9},{9,8},{10,11... | collective-permute-start | bytes 1966088 | tf_op jit(solution)/shard_map/ppermute | solution.py:275
  26.8 3.6 %collective-permute-start.9 = (bf16[4,32,1280]{2,1,0:T(8,128)(2,1)S(1)}, bf16[4,32,1280]{2,1,0:T(8,128)(2,1)S(1)}, u32[]{:S(2)}, u32[]{:S(2)}) collective-permute-start(bf16[4,32,1280]{2,1,0:T(8,128)(2,1)S(1)} %pad_maximum_fusion.2), channel_id=1, source_target_pairs={{0,1},{1,0},{2,3},{3,2},{4,5},{5,4},{6,7},{7,6},{8,9},{9,8},{10,11... | collective-permute-start | bytes 983048 | tf_op jit(solution)/shard_map/ppermute | solution.py:275
  26.8 0.7 %copy-start.6 = (s32[20,3]{0,1:T(4,128)S(1)}, s32[20,3]{0,1:T(4,128)}, u32[]{:S(2)}) copy-start(s32[20,3]{0,1:T(4,128)} %param.8) | copy-start | bytes 724
  27.7 0.7 %copy-start.7 = (s32[20]{0:T(128)S(1)}, s32[20]{0:T(128)}, u32[]{:S(2)}) copy-start(s32[20]{0:T(128)} %param.9) | copy-start | bytes 244
  28.4 1.9 %copy-start.1 = (bf16[4,32,1280]{2,1,0:T(8,128)(2,1)S(1)}, bf16[4,32,1280]{2,1,0:T(8,128)(2,1)}, u32[]{:S(2)}) copy-start(bf16[4,32,1280]{2,1,0:T(8,128)(2,1)} %copy-done) | copy-start | bytes 983044
  28.4 1.9 %copy-start.3 = (bf16[2,32,1280]{2,1,0:T(8,128)(2,1)S(1)}, bf16[2,32,1280]{2,1,0:T(8,128)(2,1)}, u32[]{:S(2)}) copy-start(bf16[2,32,1280]{2,1,0:T(8,128)(2,1)} %copy-done.2) | copy-start | bytes 491524
  32.3 7.6 %collective-permute-start.10 = (bf16[2,32,1280]{2,1,0:T(8,128)(2,1)S(1)}, bf16[2,32,1280]{2,1,0:T(8,128)(2,1)S(1)}, u32[]{:S(2)}, u32[]{:S(2)}) collective-permute-start(bf16[2,32,1280]{2,1,0:T(8,128)(2,1)S(1)} %slice.29), channel_id=1, source_target_pairs={{0,1},{1,0},{2,3},{3,2},{4,5},{5,4},{6,7},{7,6},{8,9},{9,8},{10,11... | collective-permute-start | bytes 491528 | tf_op jit(solution)/shard_map/ppermute | solution.py:275
  32.4 13.7 %collective-permute-start.12 = (bf16[4,32,1280]{2,1,0:T(8,128)(2,1)S(1)}, bf16[4,32,1280]{2,1,0:T(8,128)(2,1)S(1)}, u32[]{:S(2)}, u32[]{:S(2)}) collective-permute-start(bf16[4,32,1280]{2,1,0:T(8,128)(2,1)S(1)} %get-tuple-element.25), channel_id=1, source_target_pairs={{0,4},{1,5},{2,6},{3,7},{4,0},{5,1},{6,2},{7,3},{8,12},{9,13},{10,... | collective-permute-start | bytes 983048 | tf_op jit(solution)/shard_map/ppermute | solution.py:275
  34.5 21.7 %collective-permute-start.16 = (bf16[10,96,128]{2,1,0:T(8,128)(2,1)S(1)}, bf16[10,96,128]{2,1,0:T(8,128)(2,1)S(1)}, u32[]{:S(2)}, u32[]{:S(2)}) collective-permute-start(bf16[10,96,128]{2,1,0:T(8,128)(2,1)S(1)} %get-tuple-element.33), channel_id=1, source_target_pairs={{0,8},{1,9},{2,10},{3,11},{4,12},{5,13},{6,14},{7,15},{8,0},{9,1},... | collective-permute-start | bytes 737288 | tf_op jit(solution)/shard_map/ppermute | solution.py:275
  39.3 22.7 %collective-permute-start.18 = (bf16[10,96,128]{2,1,0:T(8,128)(2,1)S(1)}, bf16[10,96,128]{2,1,0:T(8,128)(2,1)S(1)}, u32[]{:S(2)}, u32[]{:S(2)}) collective-permute-start(bf16[10,96,128]{2,1,0:T(8,128)(2,1)S(1)} %get-tuple-element.35), channel_id=1, source_target_pairs={{0,12},{1,13},{2,14},{3,15},{4,8},{5,9},{6,10},{7,11},{8,4},{9,5},... | collective-permute-start | bytes 737288 | tf_op jit(solution)/shard_map/ppermute | solution.py:275
  39.9 6.6 %collective-permute-start.11 = (bf16[2,32,1280]{2,1,0:T(8,128)(2,1)S(1)}, bf16[2,32,1280]{2,1,0:T(8,128)(2,1)S(1)}, u32[]{:S(2)}, u32[]{:S(2)}) collective-permute-start(bf16[2,32,1280]{2,1,0:T(8,128)(2,1)S(1)} %pad_maximum_fusion.5), channel_id=1, source_target_pairs={{0,2},{1,3},{2,0},{3,1},{4,6},{5,7},{6,4},{7,5},{8,10},{9,11},{10,... | collective-permute-start | bytes 491528 | tf_op jit(solution)/shard_map/ppermute | solution.py:275
  40.6 21.4 %collective-permute-start.17 = (bf16[10,96,128]{2,1,0:T(8,128)(2,1)S(1)}, bf16[10,96,128]{2,1,0:T(8,128)(2,1)S(1)}, u32[]{:S(2)}, u32[]{:S(2)}) collective-permute-start(bf16[10,96,128]{2,1,0:T(8,128)(2,1)S(1)} %get-tuple-element.34), channel_id=1, source_target_pairs={{0,4},{1,5},{2,6},{3,7},{4,0},{5,1},{6,2},{7,3},{8,12},{9,13},{10,... | collective-permute-start | bytes 737288 | tf_op jit(solution)/shard_map/ppermute | solution.py:275
  46.1 4.6 %collective-permute-start.13 = (bf16[1,32,1280]{2,1,0:T(8,128)(2,1)S(1)}, bf16[1,32,1280]{2,1,0:T(8,128)(2,1)S(1)}, u32[]{:S(2)}, u32[]{:S(2)}) collective-permute-start(bf16[1,32,1280]{2,1,0:T(8,128)(2,1)S(1)} %get-tuple-element.26), channel_id=1, source_target_pairs={{0,3},{1,2},{2,1},{3,0},{4,7},{5,6},{6,5},{7,4},{8,11},{9,10},{10,... | collective-permute-start | bytes 245768 | tf_op jit(solution)/shard_map/ppermute | solution.py:275
  46.5 6.2 %collective-permute-start.14 = (bf16[1,32,1280]{2,1,0:T(8,128)(2,1)S(1)}, bf16[1,32,1280]{2,1,0:T(8,128)(2,1)S(1)}, u32[]{:S(2)}, u32[]{:S(2)}) collective-permute-start(bf16[1,32,1280]{2,1,0:T(8,128)(2,1)S(1)} %get-tuple-element.27), channel_id=1, source_target_pairs={{0,2},{1,3},{2,0},{3,1},{4,6},{5,7},{6,4},{7,5},{8,10},{9,11},{10,... | collective-permute-start | bytes 245768 | tf_op jit(solution)/shard_map/ppermute | solution.py:275
  50.7 2.0 %collective-permute-start.15 = (bf16[1,32,1280]{2,1,0:T(8,128)(2,1)S(1)}, bf16[1,32,1280]{2,1,0:T(8,128)(2,1)S(1)}, u32[]{:S(2)}, u32[]{:S(2)}) collective-permute-start(bf16[1,32,1280]{2,1,0:T(8,128)(2,1)S(1)} %get-tuple-element.28), channel_id=1, source_target_pairs={{0,1},{1,0},{2,3},{3,2},{4,5},{5,4},{6,7},{7,6},{8,9},{9,8},{10,11... | collective-permute-start | bytes 245768 | tf_op jit(solution)/shard_map/ppermute | solution.py:275

commit v24 on v22

--- a/solution.py
+++ b/solution.py
@@ -313,6 +313,8 @@
     stay, = cut_call(first_tiles([(0, b) for b in range(tensor)]), cotangent, tensor, 1)
     near = jnp.concatenate([tokens, near], axis=0)
     for bit in bits:
+        if bit == bits[-1]:
+            near, scalars = lax.optimization_barrier((near, scalars))
         far = swap(near, 0, bit)
         if bit > 1:
             near = jnp.concatenate([near, far], axis=0)

time: 62.4 us -> 63 us (level)
  the two profiles are of different devices: /device:TPU:16 before, /device:TPU:0 now
where the time goes in v24:
time: 63 us; the launch traced here: 61.8 us
  waiting for transfers between devices  26.9 us (43%)
  starting transfers between devices  22.8 us (36%)
  Pallas kernels  8.68 us (14%)
  local copies, waits for them, and re-layouts  1.42 us (2%)
  other arithmetic  1.15 us (2%)
  between operations  0.88 us (1%)
    ppermute x19, waiting for transfers between devices, swap(): return lax.ppermute(value, ('fsdp', 'tensor'), pairs)  26.9 us
    ppermute x19, starting transfers between devices, swap(): return lax.ppermute(value, ('fsdp', 'tensor'), pairs)  22.8 us
    pallas_call x1, Pallas kernels, forward_call(): pl.pallas_call(functools.partial(forward_kernel, sizes), out_shape=[jax.S...  1.84 us
    pallas_call x2, Pallas kernels, sum_call(): pl.pallas_call(sum_kernel if before is None else sum_into_kernel, out_sha...  1.77 us
    pallas_call x1, Pallas kernels, cut_call(): pl.pallas_call(cut_kernel, out_shape=[jax.ShapeDtypeStruct((count // part...  1.59 us
    pallas_call x1, Pallas kernels, join_call(): pl.pallas_call(functools.partial(join_kernel, refs), out_shape=jax.ShapeD...  1.44 us
    pallas_call x1, Pallas kernels, backward_call(): pl.pallas_call(functools.partial(backward_kernel, sizes), out_shape=[jax....  1.37 us
  transfers between devices with their start and end apart: 19, of which 9 were waited for; matrix products, arithmetic and copies ran while one was open for 4% of the time, Pallas kernels for 10%

profile of v24, /device:TPU:0, one launch (start us, length us, event | category | flops | bytes accessed | tf_op | source)
XLA Modules:
  0.0 61.8 jit_solution(6033245039046361292)
XLA Ops:
  0.6 3.1 %collective-permute-start = (bf16[32,2560]{1,0:T(8,128)(2,1)}, bf16[32,2560]{1,0:T(8,128)(2,1)S(1)}, u32[]{:S(2)}, u32[]{:S(2)}) collective-permute-start(bf16[32,2560]{1,0:T(8,128)(2,1)} %param.5), channel_id=1, source_target_pairs={{0,4},{1,5},{2,6},{3,7},{4,0},{5,1},{6,2},{7,3},{8,12},{9,13},{10,... | collective-permute-start | bytes 491528 | tf_op jit(solution)/shard_map/ppermute | solution.py:275
  3.7 1.0 %dynamic-slice_bitcast_fusion.3 = (bf16[1,32,1280]{2,1,0:T(8,128)(2,1)S(1)}, bf16[1,32,1280]{2,1,0:T(8,128)(2,1)S(1)}, bf16[1,32,1280]{2,1,0:T(8,128)(2,1)S(1)}, bf16[1,32,1280]{2,1,0:T(8,128)(2,1)S(1)}) fusion(bf16[32,10240]{1,0:T(8,128)(2,1)} %whole.1, s32[]{:T(128)S(6)} %select_n.30, s32[]{:T(128)S(6)} %select_n.29, s32[]{:T(128)S(6)} %select_n.28, ...), kind=kLoop, calls=%fused_computation.10 | loop fusion | bytes 655376 | tf_op jit(solution)/shard_map/stack | solution.py:294
  4.9 2.0 %collective-permute-start.4 = (bf16[2,32,1280]{2,1,0:T(8,128)(2,1)S(1)}, bf16[2,32,1280]{2,1,0:T(8,128)(2,1)S(1)}, u32[]{:S(2)}, u32[]{:S(2)}) collective-permute-start(bf16[2,32,1280]{2,1,0:T(8,128)(2,1)S(1)} %pad_maximum_fusion.5), channel_id=1, source_target_pairs={{0,4},{1,5},{2,6},{3,7},{4,0},{5,1},{6,2},{7,3},{8,12},{9,13},{10,... | collective-permute-start | bytes 491528 | tf_op jit(solution)/shard_map/ppermute | solution.py:275
  7.0 2.5 %collective-permute-start.7 = (bf16[10,96,128]{2,1,0:T(8,128)(2,1)S(1)}, bf16[10,96,128]{2,1,0:T(8,128)(2,1)S(1)}, u32[]{:S(2)}, u32[]{:S(2)}) collective-permute-start(bf16[10,96,128]{2,1,0:T(8,128)(2,1)S(1)} %get-tuple-element.24), channel_id=1, source_target_pairs={{0,12},{1,13},{2,14},{3,15},{4,8},{5,9},{6,10},{7,11},{8,4},{9,5},... | collective-permute-start | bytes 737288 | tf_op jit(solution)/shard_map/ppermute | solution.py:275
  9.6 0.2 collective-permute-start.6
  9.8 1.6 %cut.1.rest_0_ = bf16[4,32,1280]{2,1,0:T(8,128)(2,1)S(1)} custom-call(s32[4]{0:T(128)S(1)} %pad_add_fusion.2.starts, bf16[32,10240]{1,0:T(8,128)(2,1)} %whole.1), custom_call_target="tpu_custom_call" | custom-call | tf_op jit(solution)/shard_map/cut/pallas_call | solution.py:55
  11.7 1.6 %collective-permute-start.1 = (bf16[64,2560]{1,0:T(8,128)(2,1)S(1)}, bf16[64,2560]{1,0:T(8,128)(2,1)S(1)}, u32[]{:S(2)}, u32[]{:S(2)}) collective-permute-start(bf16[64,2560]{1,0:T(8,128)(2,1)S(1)} %pad_maximum_fusion.1), channel_id=1, source_target_pairs={{0,2},{1,3},{2,0},{3,1},{4,6},{5,7},{6,4},{7,5},{8,10},{9,11},{10,... | collective-permute-start | bytes 983048 | tf_op jit(solution)/shard_map/ppermute | solution.py:275
  13.4 9.4 %collective-permute-done.4.rest_2_ = bf16[2,32,1280]{2,1,0:T(8,128)(2,1)S(1)} collective-permute-done((bf16[2,32,1280]{2,1,0:T(8,128)(2,1)S(1)}, bf16[2,32,1280]{2,1,0:T(8,128)(2,1)S(1)}, u32[]{:S(2)}, u32[]{:S(2)}) %collective-permute-start.4) | collective-permute-done | bytes 163872 | tf_op jit(solution)/shard_map/ppermute | solution.py:275
  22.9 2.2 %collective-permute-start.8 = (bf16[4,32,1280]{2,1,0:T(8,128)(2,1)S(1)}, bf16[4,32,1280]{2,1,0:T(8,128)(2,1)S(1)}, u32[]{:S(2)}, u32[]{:S(2)}) collective-permute-start(bf16[4,32,1280]{2,1,0:T(8,128)(2,1)S(1)} %pad_maximum_fusion.2), channel_id=1, source_target_pairs={{0,2},{1,3},{2,0},{3,1},{4,6},{5,7},{6,4},{7,5},{8,10},{9,11},{10,... | collective-permute-start | bytes 983048 | tf_op jit(solution)/shard_map/ppermute | solution.py:275
  25.2 4.9 %collective-permute-done.8.rest_3_ = bf16[4,32,1280]{2,1,0:T(8,128)(2,1)S(1)} collective-permute-done((bf16[4,32,1280]{2,1,0:T(8,128)(2,1)S(1)}, bf16[4,32,1280]{2,1,0:T(8,128)(2,1)S(1)}, u32[]{:S(2)}, u32[]{:S(2)}) %collective-permute-start.8) | collective-permute-done | bytes 327712 | tf_op jit(solution)/shard_map/ppermute | solution.py:275
  30.1 0.8 %pad_maximum_fusion.3 = bf16[4,32,1280]{2,1,0:T(8,128)(2,1)} fusion(bf16[1,32,1280]{2,1,0:T(8,128)(2,1)S(1)} %get-tuple-element.49, bf16[1,32,1280]{2,1,0:T(8,128)(2,1)S(1)} %get-tuple-element.48, bf16[1,32,1280]{2,1,0:T(8,128)(2,1)S(1)} %slice.26, bf16[1,32,1280]{2,1,0:T(8,128)(2,1)S(1)} %slice-done), kind=kLoop, calls=%fused_computation.3 | loop fusion | flops 491520 | bytes 655360 | tf_op jit(solution)/shard_map/concatenate | solution.py:262
  31.0 0.6 collective-permute-done.5.rest_1_
  31.6 0.6 stack.94.weights
  32.2 0.5 collective-permute-done.9.rest_4_
  32.8 1.8 %forward.1 = (bf16[4,32,1280]{2,1,0:T(8,128)(2,1)S(1)}, bf16[4,32,1280]{2,1,0:T(8,128)(2,1)S(1)}, bf16[256,1280]{1,0:T(8,128)(2,1)S(1)}) custom-call(s32[82]{0:T(128)S(1)} %pad_add_fusion.scalars, bf16[128,2560]{1,0:T(8,128)(2,1)S(1)} %pad_maximum_fusion.near, bf16[128,2560]{1,0:T(8,128)(2,1)S(1)} %collective-permute-done.2.far, ...), custom_call_target="tpu_custom_call" | custom-call | tf_op jit(solution)/shard_map/forward/pallas_call | solution.py:143
  34.7 0.2 collective-permute-start.10
  34.9 2.0 %collective-permute-start.12 = (bf16[4,32,1280]{2,1,0:T(8,128)(2,1)S(1)}, bf16[4,32,1280]{2,1,0:T(8,128)(2,1)S(1)}, u32[]{:S(2)}, u32[]{:S(2)}) collective-permute-start(bf16[4,32,1280]{2,1,0:T(8,128)(2,1)S(1)} %get-tuple-element.31), channel_id=1, source_target_pairs={{0,4},{1,5},{2,6},{3,7},{4,0},{5,1},{6,2},{7,3},{8,12},{9,13},{10,... | collective-permute-start | bytes 983048 | tf_op jit(solution)/shard_map/ppermute | solution.py:275
  36.9 1.4 %backward.1 = (f32[10,96,128]{2,1,0:T(8,128)S(1)}, bf16[10,96,128]{2,1,0:T(8,128)(2,1)S(1)}, bf16[10,96,128]{2,1,0:T(8,128)(2,1)S(1)}, bf16[10,96,128]{2,1,0:T(8,128)(2,1)S(1)}) custom-call(s32[82]{0:T(128)S(1)} %pad_add_fusion.scalars, bf16[128,2560]{1,0:T(8,128)(2,1)S(1)} %pad_maximum_fusion.near, bf16[128,2560]{1,0:T(8,128)(2,1)S(1)} %collective-permute-done.2.far, ...), custom_call_target="tpu_custom_call" | custom-call | tf_op jit(solution)/shard_map/backward/pallas_call | solution.py:210
  38.3 2.6 %collective-permute-start.16 = (bf16[10,96,128]{2,1,0:T(8,128)(2,1)S(1)}, bf16[10,96,128]{2,1,0:T(8,128)(2,1)S(1)}, u32[]{:S(2)}, u32[]{:S(2)}) collective-permute-start(bf16[10,96,128]{2,1,0:T(8,128)(2,1)S(1)} %get-tuple-element.39), channel_id=1, source_target_pairs={{0,8},{1,9},{2,10},{3,11},{4,12},{5,13},{6,14},{7,15},{8,0},{9,1},... | collective-permute-start | bytes 737288 | tf_op jit(solution)/shard_map/ppermute | solution.py:275
  40.9 1.3 %collective-permute-start.18 = (bf16[10,96,128]{2,1,0:T(8,128)(2,1)S(1)}, bf16[10,96,128]{2,1,0:T(8,128)(2,1)S(1)}, u32[]{:S(2)}, u32[]{:S(2)}) collective-permute-start(bf16[10,96,128]{2,1,0:T(8,128)(2,1)S(1)} %get-tuple-element.41), channel_id=1, source_target_pairs={{0,12},{1,13},{2,14},{3,15},{4,8},{5,9},{6,10},{7,11},{8,4},{9,5},... | collective-permute-start | bytes 737288 | tf_op jit(solution)/shard_map/ppermute | solution.py:275
  42.2 1.5 %collective-permute-start.11 = (bf16[2,32,1280]{2,1,0:T(8,128)(2,1)S(1)}, bf16[2,32,1280]{2,1,0:T(8,128)(2,1)S(1)}, u32[]{:S(2)}, u32[]{:S(2)}) collective-permute-start(bf16[2,32,1280]{2,1,0:T(8,128)(2,1)S(1)} %pad_maximum_fusion.6), channel_id=1, source_target_pairs={{0,2},{1,3},{2,0},{3,1},{4,6},{5,7},{6,4},{7,5},{8,10},{9,11},{10,... | collective-permute-start | bytes 491528 | tf_op jit(solution)/shard_map/ppermute | solution.py:275
  43.8 0.5 collective-permute-start.17
  44.2 6.5 %collective-permute-done.12.rest_0_ = bf16[4,32,1280]{2,1,0:T(8,128)(2,1)S(1)} collective-permute-done((bf16[4,32,1280]{2,1,0:T(8,128)(2,1)S(1)}, bf16[4,32,1280]{2,1,0:T(8,128)(2,1)S(1)}, u32[]{:S(2)}, u32[]{:S(2)}) %collective-permute-start.12) | collective-permute-done | bytes 327712 | tf_op jit(solution)/shard_map/ppermute | solution.py:275
  50.8 1.1 %collective-permute-start.13 = (bf16[1,32,1280]{2,1,0:T(8,128)(2,1)S(1)}, bf16[1,32,1280]{2,1,0:T(8,128)(2,1)S(1)}, u32[]{:S(2)}, u32[]{:S(2)}) collective-permute-start(bf16[1,32,1280]{2,1,0:T(8,128)(2,1)S(1)} %get-tuple-element.32), channel_id=1, source_target_pairs={{0,3},{1,2},{2,1},{3,0},{4,7},{5,6},{6,5},{7,4},{8,11},{9,10},{10,... | collective-permute-start | bytes 245768 | tf_op jit(solution)/shard_map/ppermute | solution.py:275
  51.9 1.1 %collective-permute-start.14 = (bf16[1,32,1280]{2,1,0:T(8,128)(2,1)S(1)}, bf16[1,32,1280]{2,1,0:T(8,128)(2,1)S(1)}, u32[]{:S(2)}, u32[]{:S(2)}) collective-permute-start(bf16[1,32,1280]{2,1,0:T(8,128)(2,1)S(1)} %get-tuple-element.33), channel_id=1, source_target_pairs={{0,2},{1,3},{2,0},{3,1},{4,6},{5,7},{6,4},{7,5},{8,10},{9,11},{10,... | collective-permute-start | bytes 245768 | tf_op jit(solution)/shard_map/ppermute | solution.py:275
  52.9 2.1 %collective-permute-done.13.rest_3_ = bf16[1,32,1280]{2,1,0:T(8,128)(2,1)S(1)} collective-permute-done((bf16[1,32,1280]{2,1,0:T(8,128)(2,1)S(1)}, bf16[1,32,1280]{2,1,0:T(8,128)(2,1)S(1)}, u32[]{:S(2)}, u32[]{:S(2)}) %collective-permute-start.13) | collective-permute-done | bytes 81952 | tf_op jit(solution)/shard_map/ppermute | solution.py:275
  55.1 0.6 %collective-permute-start.15 = (bf16[1,32,1280]{2,1,0:T(8,128)(2,1)S(1)}, bf16[1,32,1280]{2,1,0:T(8,128)(2,1)S(1)}, u32[]{:S(2)}, u32[]{:S(2)}) collective-permute-start(bf16[1,32,1280]{2,1,0:T(8,128)(2,1)S(1)} %get-tuple-element.34), channel_id=1, source_target_pairs={{0,1},{1,0},{2,3},{3,2},{4,5},{5,4},{6,7},{7,6},{8,9},{9,8},{10,11... | collective-permute-start | bytes 245768 | tf_op jit(solution)/shard_map/ppermute | solution.py:275
  55.8 1.5 %collective-permute-done.14.rest_4_ = bf16[1,32,1280]{2,1,0:T(8,128)(2,1)S(1)} collective-permute-done((bf16[1,32,1280]{2,1,0:T(8,128)(2,1)S(1)}, bf16[1,32,1280]{2,1,0:T(8,128)(2,1)S(1)}, u32[]{:S(2)}, u32[]{:S(2)}) %collective-permute-start.14) | collective-permute-done | bytes 81952 | tf_op jit(solution)/shard_map/ppermute | solution.py:275
  57.3 1.4 %join.1 = bf16[32,10240]{1,0:T(8,128)(2,1)} custom-call(s32[8]{0:T(128)S(1)} %stack.80.starts, bf16[4,32,1280]{2,1,0:T(8,128)(2,1)S(1)} %get-tuple-element.27.rest_0_, bf16[2,32,1280]{2,1,0:T(8,128)(2,1)S(1)} %collective-permute-done.10.rest_1_, bf16[2,32,1280]{2,1,0:T(8,128)(2,1)S(1)} %collective-permute-done.11.rest_2_, ...), custom_call_target="tpu_custom_call" | custom-call | tf_op jit(solution)/shard_map/join/pallas_call | solution.py:92
  58.8 0.9 %sum.2.before = f32[2,10,96,128]{3,2,1,0:T(8,128)} custom-call(s32[1]{0:T(128)} %bitcast.19.half, f32[10,96,128]{2,1,0:T(8,128)S(1)} %get-tuple-element.38.rest_0_, bf16[10,96,128]{2,1,0:T(8,128)(2,1)S(1)} %collective-permute-done.16.rest_1_), custom_call_target="tpu_custom_call" | custom-call | tf_op jit(solution)/shard_map/sum/pallas_call | solution.py:242
  59.8 1.2 %collective-permute-done.17.rest_0_ = bf16[10,96,128]{2,1,0:T(8,128)(2,1)S(1)} collective-permute-done((bf16[10,96,128]{2,1,0:T(8,128)(2,1)S(1)}, bf16[10,96,128]{2,1,0:T(8,128)(2,1)S(1)}, u32[]{:S(2)}, u32[]{:S(2)}) %collective-permute-start.17) | collective-permute-done | bytes 245792 | tf_op jit(solution)/shard_map/ppermute | solution.py:275
  60.9 0.9 %sum.3 = f32[2,10,96,128]{3,2,1,0:T(8,128)} custom-call(s32[1]{0:T(128)S(6)} %sub.5.half, f32[2,10,96,128]{3,2,1,0:T(8,128)} %sum.2.before, bf16[10,96,128]{2,1,0:T(8,128)(2,1)S(1)} %collective-permute-done.17.rest_0_, bf16[10,96,128]{2,1,0:T(8,128)(2,1)S(1)} %collective-permute-done.18.rest_1_), custom_call_target="tpu_custom_call", output_to_operand_aliasing={{}: (1, {})} | custom-call | tf_op jit(solution)/shard_map/sum/pallas_call | solution.py:242
  (50 shorter events, 1.2 us)
Async XLA Ops:
  0.6 6.3 %copy-start.3 = (bf16[96,20,128]{2,0,1:T(8,128)(2,1)S(1)}, bf16[96,20,128]{2,0,1:T(8,128)(2,1)}, u32[]{:S(2)}) copy-start(bf16[96,20,128]{2,0,1:T(8,128)(2,1)} %param.6) | copy-start | bytes 1474564
  0.6 11.0 %collective-permute-start = (bf16[32,2560]{1,0:T(8,128)(2,1)}, bf16[32,2560]{1,0:T(8,128)(2,1)S(1)}, u32[]{:S(2)}, u32[]{:S(2)}) collective-permute-start(bf16[32,2560]{1,0:T(8,128)(2,1)} %param.5), channel_id=1, source_target_pairs={{0,4},{1,5},{2,6},{3,7},{4,0},{5,1},{6,2},{7,3},{8,12},{9,13},{10,... | collective-permute-start | bytes 491528 | tf_op jit(solution)/shard_map/ppermute | solution.py:275
  4.8 8.6 %collective-permute-start.3 = (bf16[2,32,1280]{2,1,0:T(8,128)(2,1)S(1)}, bf16[2,32,1280]{2,1,0:T(8,128)(2,1)S(1)}, u32[]{:S(2)}, u32[]{:S(2)}) collective-permute-start(bf16[2,32,1280]{2,1,0:T(8,128)(2,1)S(1)} %pad_maximum_fusion.4), channel_id=1, source_target_pairs={{0,4},{1,5},{2,6},{3,7},{4,0},{5,1},{6,2},{7,3},{8,12},{9,13},{10,... | collective-permute-start | bytes 491528 | tf_op jit(solution)/shard_map/ppermute | solution.py:275
  4.9 17.8 %collective-permute-start.4 = (bf16[2,32,1280]{2,1,0:T(8,128)(2,1)S(1)}, bf16[2,32,1280]{2,1,0:T(8,128)(2,1)S(1)}, u32[]{:S(2)}, u32[]{:S(2)}) collective-permute-start(bf16[2,32,1280]{2,1,0:T(8,128)(2,1)S(1)} %pad_maximum_fusion.5), channel_id=1, source_target_pairs={{0,4},{1,5},{2,6},{3,7},{4,0},{5,1},{6,2},{7,3},{8,12},{9,13},{10,... | collective-permute-start | bytes 491528 | tf_op jit(solution)/shard_map/ppermute | solution.py:275
  7.0 4.5 %copy-start.4 = (s32[20,3]{0,1:T(4,128)S(1)}, s32[20,3]{0,1:T(4,128)}, u32[]{:S(2)}) copy-start(s32[20,3]{0,1:T(4,128)} %param.8) | copy-start | bytes 724
  7.0 4.7 %copy-start.2 = (bf16[32,2560]{1,0:T(8,128)(2,1)S(1)}, bf16[32,2560]{1,0:T(8,128)(2,1)}, u32[]{:S(2)}) copy-start(bf16[32,2560]{1,0:T(8,128)(2,1)} %param.5) | copy-start | bytes 491524
  7.0 24.0 %collective-permute-start.7 = (bf16[10,96,128]{2,1,0:T(8,128)(2,1)S(1)}, bf16[10,96,128]{2,1,0:T(8,128)(2,1)S(1)}, u32[]{:S(2)}, u32[]{:S(2)}) collective-permute-start(bf16[10,96,128]{2,1,0:T(8,128)(2,1)S(1)} %get-tuple-element.24), channel_id=1, source_target_pairs={{0,12},{1,13},{2,14},{3,15},{4,8},{5,9},{6,10},{7,11},{8,4},{9,5},... | collective-permute-start | bytes 737288 | tf_op jit(solution)/shard_map/ppermute | solution.py:275
  9.6 21.4 %collective-permute-start.6 = (bf16[10,96,128]{2,1,0:T(8,128)(2,1)S(1)}, bf16[10,96,128]{2,1,0:T(8,128)(2,1)S(1)}, u32[]{:S(2)}, u32[]{:S(2)}) collective-permute-start(bf16[10,96,128]{2,1,0:T(8,128)(2,1)S(1)} %get-tuple-element.47.rest_0_), channel_id=1, source_target_pairs={{0,8},{1,9},{2,10},{3,11},{4,12},{5,13},{6,14},{7,15},{8,0},{9,1},... | collective-permute-start | bytes 737288 | tf_op jit(solution)/shard_map/ppermute | solution.py:275
  9.8 3.4 %copy-start.5 = (s32[20]{0:T(128)S(1)}, s32[20]{0:T(128)}, u32[]{:S(2)}) copy-start(s32[20]{0:T(128)} %param.9) | copy-start | bytes 244
  11.4 11.4 %copy-start = (bf16[4,32,1280]{2,1,0:T(8,128)(2,1)}, bf16[4,32,1280]{2,1,0:T(8,128)(2,1)S(1)}, u32[]{:S(2)}) copy-start(bf16[4,32,1280]{2,1,0:T(8,128)(2,1)S(1)} %cut.1.rest_0_) | copy-start | bytes 983044
  11.7 13.4 %collective-permute-start.1 = (bf16[64,2560]{1,0:T(8,128)(2,1)S(1)}, bf16[64,2560]{1,0:T(8,128)(2,1)S(1)}, u32[]{:S(2)}, u32[]{:S(2)}) collective-permute-start(bf16[64,2560]{1,0:T(8,128)(2,1)S(1)} %pad_maximum_fusion.1), channel_id=1, source_target_pairs={{0,2},{1,3},{2,0},{3,1},{4,6},{5,7},{6,4},{7,5},{8,10},{9,11},{10,... | collective-permute-start | bytes 983048 | tf_op jit(solution)/shard_map/ppermute | solution.py:275
  22.8 8.8 %collective-permute-start.5 = (bf16[10,96,128]{2,1,0:T(8,128)(2,1)S(1)}, bf16[10,96,128]{2,1,0:T(8,128)(2,1)S(1)}, u32[]{:S(2)}, u32[]{:S(2)}) collective-permute-start(bf16[10,96,128]{2,1,0:T(8,128)(2,1)S(1)} %get-tuple-element.24), channel_id=1, source_target_pairs={{0,4},{1,5},{2,6},{3,7},{4,0},{5,1},{6,2},{7,3},{8,12},{9,13},{10,... | collective-permute-start | bytes 737288 | tf_op jit(solution)/shard_map/ppermute | solution.py:275
  22.9 7.3 %collective-permute-start.8 = (bf16[4,32,1280]{2,1,0:T(8,128)(2,1)S(1)}, bf16[4,32,1280]{2,1,0:T(8,128)(2,1)S(1)}, u32[]{:S(2)}, u32[]{:S(2)}) collective-permute-start(bf16[4,32,1280]{2,1,0:T(8,128)(2,1)S(1)} %pad_maximum_fusion.2), channel_id=1, source_target_pairs={{0,2},{1,3},{2,0},{3,1},{4,6},{5,7},{6,4},{7,5},{8,10},{9,11},{10,... | collective-permute-start | bytes 983048 | tf_op jit(solution)/shard_map/ppermute | solution.py:275
  25.1 5.1 %slice-start = ((bf16[4,32,1280]{2,1,0:T(8,128)(2,1)}), bf16[1,32,1280]{2,1,0:T(8,128)(2,1)S(1)}, s32[]{:S(2)}) async-start(bf16[4,32,1280]{2,1,0:T(8,128)(2,1)} %copy-done), calls=%async_computation | async-start | bytes 163840 | tf_op jit(solution)/shard_map/slice | solution.py:261
  25.1 7.7 %collective-permute-start.2 = (bf16[128,2560]{1,0:T(8,128)(2,1)S(1)}, bf16[128,2560]{1,0:T(8,128)(2,1)S(1)}, u32[]{:S(2)}, u32[]{:S(2)}) collective-permute-start(bf16[128,2560]{1,0:T(8,128)(2,1)S(1)} %pad_maximum_fusion.near), channel_id=1, source_target_pairs={{0,1},{1,0},{2,3},{3,2},{4,5},{5,4},{6,7},{7,6},{8,9},{9,8},{10,11... | collective-permute-start | bytes 1966088 | tf_op jit(solution)/shard_map/ppermute | solution.py:275
  30.9 1.8 %collective-permute-start.9 = (bf16[4,32,1280]{2,1,0:T(8,128)(2,1)}, bf16[4,32,1280]{2,1,0:T(8,128)(2,1)S(1)}, u32[]{:S(2)}, u32[]{:S(2)}) collective-permute-start(bf16[4,32,1280]{2,1,0:T(8,128)(2,1)} %pad_maximum_fusion.3), channel_id=1, source_target_pairs={{0,1},{1,0},{2,3},{3,2},{4,5},{5,4},{6,7},{7,6},{8,9},{9,8},{10,11... | collective-permute-start | bytes 983048 | tf_op jit(solution)/shard_map/ppermute | solution.py:275
  31.0 1.8 %copy-start.1 = (bf16[4,32,1280]{2,1,0:T(8,128)(2,1)S(1)}, bf16[4,32,1280]{2,1,0:T(8,128)(2,1)}, u32[]{:S(2)}) copy-start(bf16[4,32,1280]{2,1,0:T(8,128)(2,1)} %copy-done) | copy-start | bytes 983044
  34.7 7.5 %collective-permute-start.10 = (bf16[2,32,1280]{2,1,0:T(8,128)(2,1)S(1)}, bf16[2,32,1280]{2,1,0:T(8,128)(2,1)S(1)}, u32[]{:S(2)}, u32[]{:S(2)}) collective-permute-start(bf16[2,32,1280]{2,1,0:T(8,128)(2,1)S(1)} %slice.29), channel_id=1, source_target_pairs={{0,1},{1,0},{2,3},{3,2},{4,5},{5,4},{6,7},{7,6},{8,9},{9,8},{10,11... | collective-permute-start | bytes 491528 | tf_op jit(solution)/shard_map/ppermute | solution.py:275
  34.9 15.9 %collective-permute-start.12 = (bf16[4,32,1280]{2,1,0:T(8,128)(2,1)S(1)}, bf16[4,32,1280]{2,1,0:T(8,128)(2,1)S(1)}, u32[]{:S(2)}, u32[]{:S(2)}) collective-permute-start(bf16[4,32,1280]{2,1,0:T(8,128)(2,1)S(1)} %get-tuple-element.31), channel_id=1, source_target_pairs={{0,4},{1,5},{2,6},{3,7},{4,0},{5,1},{6,2},{7,3},{8,12},{9,13},{10,... | collective-permute-start | bytes 983048 | tf_op jit(solution)/shard_map/ppermute | solution.py:275
  38.3 20.5 %collective-permute-start.16 = (bf16[10,96,128]{2,1,0:T(8,128)(2,1)S(1)}, bf16[10,96,128]{2,1,0:T(8,128)(2,1)S(1)}, u32[]{:S(2)}, u32[]{:S(2)}) collective-permute-start(bf16[10,96,128]{2,1,0:T(8,128)(2,1)S(1)} %get-tuple-element.39), channel_id=1, source_target_pairs={{0,8},{1,9},{2,10},{3,11},{4,12},{5,13},{6,14},{7,15},{8,0},{9,1},... | collective-permute-start | bytes 737288 | tf_op jit(solution)/shard_map/ppermute | solution.py:275
  40.9 18.8 %collective-permute-start.18 = (bf16[10,96,128]{2,1,0:T(8,128)(2,1)S(1)}, bf16[10,96,128]{2,1,0:T(8,128)(2,1)S(1)}, u32[]{:S(2)}, u32[]{:S(2)}) collective-permute-start(bf16[10,96,128]{2,1,0:T(8,128)(2,1)S(1)} %get-tuple-element.41), channel_id=1, source_target_pairs={{0,12},{1,13},{2,14},{3,15},{4,8},{5,9},{6,10},{7,11},{8,4},{9,5},... | collective-permute-start | bytes 737288 | tf_op jit(solution)/shard_map/ppermute | solution.py:275
  42.2 9.7 %collective-permute-start.11 = (bf16[2,32,1280]{2,1,0:T(8,128)(2,1)S(1)}, bf16[2,32,1280]{2,1,0:T(8,128)(2,1)S(1)}, u32[]{:S(2)}, u32[]{:S(2)}) collective-permute-start(bf16[2,32,1280]{2,1,0:T(8,128)(2,1)S(1)} %pad_maximum_fusion.6), channel_id=1, source_target_pairs={{0,2},{1,3},{2,0},{3,1},{4,6},{5,7},{6,4},{7,5},{8,10},{9,11},{10,... | collective-permute-start | bytes 491528 | tf_op jit(solution)/shard_map/ppermute | solution.py:275
  43.8 17.2 %collective-permute-start.17 = (bf16[10,96,128]{2,1,0:T(8,128)(2,1)S(1)}, bf16[10,96,128]{2,1,0:T(8,128)(2,1)S(1)}, u32[]{:S(2)}, u32[]{:S(2)}) collective-permute-start(bf16[10,96,128]{2,1,0:T(8,128)(2,1)S(1)} %get-tuple-element.40), channel_id=1, source_target_pairs={{0,4},{1,5},{2,6},{3,7},{4,0},{5,1},{6,2},{7,3},{8,12},{9,13},{10,... | collective-permute-start | bytes 737288 | tf_op jit(solution)/shard_map/ppermute | solution.py:275
  50.8 4.3 %collective-permute-start.13 = (bf16[1,32,1280]{2,1,0:T(8,128)(2,1)S(1)}, bf16[1,32,1280]{2,1,0:T(8,128)(2,1)S(1)}, u32[]{:S(2)}, u32[]{:S(2)}) collective-permute-start(bf16[1,32,1280]{2,1,0:T(8,128)(2,1)S(1)} %get-tuple-element.32), channel_id=1, source_target_pairs={{0,3},{1,2},{2,1},{3,0},{4,7},{5,6},{6,5},{7,4},{8,11},{9,10},{10,... | collective-permute-start | bytes 245768 | tf_op jit(solution)/shard_map/ppermute | solution.py:275
  51.9 5.4 %collective-permute-start.14 = (bf16[1,32,1280]{2,1,0:T(8,128)(2,1)S(1)}, bf16[1,32,1280]{2,1,0:T(8,128)(2,1)S(1)}, u32[]{:S(2)}, u32[]{:S(2)}) collective-permute-start(bf16[1,32,1280]{2,1,0:T(8,128)(2,1)S(1)} %get-tuple-element.33), channel_id=1, source_target_pairs={{0,2},{1,3},{2,0},{3,1},{4,6},{5,7},{6,4},{7,5},{8,10},{9,11},{10,... | collective-permute-start | bytes 245768 | tf_op jit(solution)/shard_map/ppermute | solution.py:275
  55.1 2.3 %collective-permute-start.15 = (bf16[1,32,1280]{2,1,0:T(8,128)(2,1)S(1)}, bf16[1,32,1280]{2,1,0:T(8,128)(2,1)S(1)}, u32[]{:S(2)}, u32[]{:S(2)}) collective-permute-start(bf16[1,32,1280]{2,1,0:T(8,128)(2,1)S(1)} %get-tuple-element.34), channel_id=1, source_target_pairs={{0,1},{1,0},{2,3},{3,2},{4,5},{5,4},{6,7},{7,6},{8,9},{9,8},{10,11... | collective-permute-start | bytes 245768 | tf_op jit(solution)/shard_map/ppermute | solution.py:275

commit v25 on v19

--- a/solution.py
+++ b/solution.py
@@ -283,7 +283,10 @@
         return jnp.stack([(t ^ b) * stripes + (half ^ a) * share for a, b in steps]).astype(jnp.int32)
 
     direct = whole_tiles and fsdp <= DIRECT
-    leave = cut_call(first_tiles([(1, b) for b in range(tensor)]), cotangent, tensor, HOPS)
+    leave = []
+    for first in range(0, tensor, tensor // HOPS):
+        columns = [((t ^ b) * stripes + (1 - half) * share) * TILE for b in range(first, first + tensor // HOPS)]
+        leave.append(jnp.stack([lax.dynamic_slice_in_dim(cotangent, column, share * TILE, 1) for column in columns]))
     arrived = [swap(part, 1, 0) for part in leave]
     near = swap(tokens, 1, 0)
     by_stripe = jnp.transpose(tile_weights, (1, 0, 2))

time: 62.3 us -> 61.6 us (0.989)
  Pallas kernels: 9.66 us -> 8.05 us
    pallas_call x2 -> x1, Pallas kernels: 3.18 us -> 1.6 us  [cut_call(): pl.pallas_call(cut_kernel, out_shape=[jax.ShapeDtypeStruct((count // part...]
    another operation x0 -> x1, local copies, waits for them, and re-layouts: none -> 1.03 us  [body(): jnp.stack([lax.dynamic_slice_in_dim(cotangent, column, share * TILE, 1) f...]
    unnamed x19, local copies, waits for them, and re-layouts: 2.83 us -> 2.18 us
  transfers between devices with their start and end apart: 19 -> 19, of which waited for: 8 -> 9; matrix products, arithmetic and copies ran while one was open for 2% -> 4% of each run, Pallas kernels for 11% -> 8%
where the time goes in v25:
time: 61.6 us; the launch traced here: 61.1 us
  waiting for transfers between devices  26.1 us (42%)
  starting transfers between devices  21.5 us (35%)
  Pallas kernels  8.05 us (13%)
  local copies, waits for them, and re-layouts  4.26 us (7%)
  between operations  0.93 us (2%)
    ppermute x19, waiting for transfers between devices, swap(): return lax.ppermute(value, ('fsdp', 'tensor'), pairs)  26.1 us
    ppermute x19, starting transfers between devices, swap(): return lax.ppermute(value, ('fsdp', 'tensor'), pairs)  21.5 us
    unnamed x19, local copies, waits for them, and re-layouts  2.18 us
    pallas_call x1, Pallas kernels, forward_call(): pl.pallas_call(functools.partial(forward_kernel, sizes), out_shape=[jax.S...  1.83 us
    pallas_call x1, Pallas kernels, cut_call(): pl.pallas_call(cut_kernel, out_shape=[jax.ShapeDtypeStruct((count // part...  1.6 us
    pallas_call x1, Pallas kernels, join_call(): pl.pallas_call(functools.partial(join_kernel, refs), out_shape=jax.ShapeD...  1.44 us
    pallas_call x1, Pallas kernels, backward_call(): pl.pallas_call(functools.partial(backward_kernel, sizes), out_shape=[jax....  1.37 us
  transfers between devices with their start and end apart: 19, of which 9 were waited for; matrix products, arithmetic and copies ran while one was open for 4% of the time, Pallas kernels for 8%

profile of v25, /device:TPU:0, one launch (start us, length us, event | category | flops | bytes accessed | tf_op | source)
XLA Modules:
  0.0 61.1 jit_solution(15026961807754340520)
XLA Ops:
  0.6 3.1 %collective-permute-start = (bf16[32,2560]{1,0:T(8,128)(2,1)}, bf16[32,2560]{1,0:T(8,128)(2,1)S(1)}, u32[]{:S(2)}, u32[]{:S(2)}) collective-permute-start(bf16[32,2560]{1,0:T(8,128)(2,1)} %param.5), channel_id=1, source_target_pairs={{0,4},{1,5},{2,6},{3,7},{4,0},{5,1},{6,2},{7,3},{8,12},{9,13},{10,... | collective-permute-start | bytes 491528 | tf_op jit(solution)/shard_map/ppermute | solution.py:270
  3.7 1.0 %dynamic-slice_bitcast_fusion.3 = (bf16[1,32,1280]{2,1,0:T(8,128)(2,1)S(1)}, bf16[1,32,1280]{2,1,0:T(8,128)(2,1)S(1)}, bf16[1,32,1280]{2,1,0:T(8,128)(2,1)S(1)}, bf16[1,32,1280]{2,1,0:T(8,128)(2,1)S(1)}) fusion(bf16[32,10240]{1,0:T(8,128)(2,1)} %whole.1, s32[]{:T(128)S(6)} %select_n.30, s32[]{:T(128)S(6)} %select_n.29, s32[]{:T(128)S(6)} %select_n.28, ...), kind=kLoop, calls=%fused_computation.9 | loop fusion | bytes 655376 | tf_op jit(solution)/shard_map/stack | solution.py:289
  4.9 2.0 %collective-permute-start.4 = (bf16[2,32,1280]{2,1,0:T(8,128)(2,1)S(1)}, bf16[2,32,1280]{2,1,0:T(8,128)(2,1)S(1)}, u32[]{:S(2)}, u32[]{:S(2)}) collective-permute-start(bf16[2,32,1280]{2,1,0:T(8,128)(2,1)S(1)} %pad_maximum_fusion.4), channel_id=1, source_target_pairs={{0,4},{1,5},{2,6},{3,7},{4,0},{5,1},{6,2},{7,3},{8,12},{9,13},{10,... | collective-permute-start | bytes 491528 | tf_op jit(solution)/shard_map/ppermute | solution.py:270
  7.0 0.7 %dynamic-slice_bitcast_fusion = (bf16[10,96,128]{2,1,0:T(8,128)(2,1)}, bf16[10,96,128]{2,1,0:T(8,128)(2,1)S(1)}) fusion(bf16[96,20,128]{2,0,1:T(8,128)(2,1)S(1)} %copy-done.5, s32[]{:T(128)S(6)} %select_n.27, s32[]{:T(128)S(6)} %select_n.26), kind=kLoop, calls=%fused_computation.3 | loop fusion | bytes 983048 | tf_op jit(solution)/shard_map/dynamic_slice | solution.py:295
  7.7 2.5 %collective-permute-start.7 = (bf16[10,96,128]{2,1,0:T(8,128)(2,1)}, bf16[10,96,128]{2,1,0:T(8,128)(2,1)S(1)}, u32[]{:S(2)}, u32[]{:S(2)}) collective-permute-start(bf16[10,96,128]{2,1,0:T(8,128)(2,1)} %get-tuple-element.20), channel_id=1, source_target_pairs={{0,12},{1,13},{2,14},{3,15},{4,8},{5,9},{6,10},{7,11},{8,4},{9,5},... | collective-permute-start | bytes 737288 | tf_op jit(solution)/shard_map/ppermute | solution.py:270
  10.3 0.7 %copy-done.6 = s32[20,3]{0,1:T(4,128)S(1)} copy-done((s32[20,3]{0,1:T(4,128)S(1)}, s32[20,3]{0,1:T(4,128)}, u32[]{:S(2)}) %copy-start.6) | copy-done | bytes 264
  11.2 0.6 %copy-done.7 = s32[20]{0:T(128)S(1)} copy-done((s32[20]{0:T(128)S(1)}, s32[20]{0:T(128)}, u32[]{:S(2)}) %copy-start.7) | copy-done | bytes 104
  11.9 1.6 %cut.1.rest_0_ = bf16[4,32,1280]{2,1,0:T(8,128)(2,1)S(1)} custom-call(s32[86]{0:T(128)S(1)} %concatenate.19.starts.scalars, bf16[32,10240]{1,0:T(8,128)(2,1)} %whole.1), custom_call_target="tpu_custom_call" | custom-call | tf_op jit(solution)/shard_map/cut/pallas_call | solution.py:55
  13.5 0.7 %copy-done = bf16[4,32,1280]{2,1,0:T(8,128)(2,1)} copy-done((bf16[4,32,1280]{2,1,0:T(8,128)(2,1)}, bf16[4,32,1280]{2,1,0:T(8,128)(2,1)S(1)}, u32[]{:S(2)}) %copy-start) | copy-done | bytes 327704
  14.3 1.6 %collective-permute-start.1 = (bf16[64,2560]{1,0:T(8,128)(2,1)S(1)}, bf16[64,2560]{1,0:T(8,128)(2,1)S(1)}, u32[]{:S(2)}, u32[]{:S(2)}) collective-permute-start(bf16[64,2560]{1,0:T(8,128)(2,1)S(1)} %pad_maximum_fusion), channel_id=1, source_target_pairs={{0,2},{1,3},{2,0},{3,1},{4,6},{5,7},{6,4},{7,5},{8,10},{9,11},{10,... | collective-permute-start | bytes 983048 | tf_op jit(solution)/shard_map/ppermute | solution.py:270
  15.9 0.8 %collective-permute-done.4.rest_2_ = bf16[2,32,1280]{2,1,0:T(8,128)(2,1)S(1)} collective-permute-done((bf16[2,32,1280]{2,1,0:T(8,128)(2,1)S(1)}, bf16[2,32,1280]{2,1,0:T(8,128)(2,1)S(1)}, u32[]{:S(2)}, u32[]{:S(2)}) %collective-permute-start.4) | collective-permute-done | bytes 163872 | tf_op jit(solution)/shard_map/ppermute | solution.py:270
  16.7 1.6 %collective-permute-start.5 = (bf16[10,96,128]{2,1,0:T(8,128)(2,1)}, bf16[10,96,128]{2,1,0:T(8,128)(2,1)S(1)}, u32[]{:S(2)}, u32[]{:S(2)}) collective-permute-start(bf16[10,96,128]{2,1,0:T(8,128)(2,1)} %get-tuple-element.20), channel_id=1, source_target_pairs={{0,4},{1,5},{2,6},{3,7},{4,0},{5,1},{6,2},{7,3},{8,12},{9,13},{10,... | collective-permute-start | bytes 737288 | tf_op jit(solution)/shard_map/ppermute | solution.py:270
  18.4 1.3 %collective-permute-start.8 = (bf16[4,32,1280]{2,1,0:T(8,128)(2,1)S(1)}, bf16[4,32,1280]{2,1,0:T(8,128)(2,1)S(1)}, u32[]{:S(2)}, u32[]{:S(2)}) collective-permute-start(bf16[4,32,1280]{2,1,0:T(8,128)(2,1)S(1)} %pad_maximum_fusion.1), channel_id=1, source_target_pairs={{0,2},{1,3},{2,0},{3,1},{4,6},{5,7},{6,4},{7,5},{8,10},{9,11},{10,... | collective-permute-start | bytes 983048 | tf_op jit(solution)/shard_map/ppermute | solution.py:270
  19.6 5.4 %collective-permute-done.1 = bf16[64,2560]{1,0:T(8,128)(2,1)S(1)} collective-permute-done((bf16[64,2560]{1,0:T(8,128)(2,1)S(1)}, bf16[64,2560]{1,0:T(8,128)(2,1)S(1)}, u32[]{:S(2)}, u32[]{:S(2)}) %collective-permute-start.1) | collective-permute-done | bytes 327712 | tf_op jit(solution)/shard_map/ppermute | solution.py:270
  25.1 4.6 %collective-permute-done.8.rest_3_ = bf16[4,32,1280]{2,1,0:T(8,128)(2,1)S(1)} collective-permute-done((bf16[4,32,1280]{2,1,0:T(8,128)(2,1)S(1)}, bf16[4,32,1280]{2,1,0:T(8,128)(2,1)S(1)}, u32[]{:S(2)}, u32[]{:S(2)}) %collective-permute-start.8) | collective-permute-done | bytes 327712 | tf_op jit(solution)/shard_map/ppermute | solution.py:270
  30.0 1.4 %collective-permute-done.6.rest_2_ = bf16[10,96,128]{2,1,0:T(8,128)(2,1)S(1)} collective-permute-done((bf16[10,96,128]{2,1,0:T(8,128)(2,1)S(1)}, bf16[10,96,128]{2,1,0:T(8,128)(2,1)S(1)}, u32[]{:S(2)}, u32[]{:S(2)}) %collective-permute-start.6) | collective-permute-done | bytes 245792 | tf_op jit(solution)/shard_map/ppermute | solution.py:270
  31.4 0.6 stack.90.weights
  32.1 1.8 %forward.1 = (bf16[4,32,1280]{2,1,0:T(8,128)(2,1)S(1)}, bf16[4,32,1280]{2,1,0:T(8,128)(2,1)S(1)}, bf16[256,1280]{1,0:T(8,128)(2,1)S(1)}) custom-call(s32[86]{0:T(128)S(1)} %concatenate.19.starts.scalars, bf16[128,2560]{1,0:T(8,128)(2,1)S(1)} %constant_dynamic-update-slice_fusion.near, bf16[128,2560]{1,0:T(8,128)(2,1)S(1)} %collective-permute-done.2.far, ...), custom_call_target="tpu_custom_call" | custom-call | tf_op jit(solution)/shard_map/forward/pallas_call | solution.py:143
  34.1 1.4 %collective-permute-start.12 = (bf16[4,32,1280]{2,1,0:T(8,128)(2,1)S(1)}, bf16[4,32,1280]{2,1,0:T(8,128)(2,1)S(1)}, u32[]{:S(2)}, u32[]{:S(2)}) collective-permute-start(bf16[4,32,1280]{2,1,0:T(8,128)(2,1)S(1)} %get-tuple-element.27), channel_id=1, source_target_pairs={{0,4},{1,5},{2,6},{3,7},{4,0},{5,1},{6,2},{7,3},{8,12},{9,13},{10,... | collective-permute-start | bytes 983048 | tf_op jit(solution)/shard_map/ppermute | solution.py:270
  35.5 1.4 %backward.1 = (f32[10,96,128]{2,1,0:T(8,128)S(1)}, bf16[10,96,128]{2,1,0:T(8,128)(2,1)S(1)}, bf16[10,96,128]{2,1,0:T(8,128)(2,1)S(1)}, bf16[10,96,128]{2,1,0:T(8,128)(2,1)S(1)}) custom-call(s32[86]{0:T(128)S(1)} %concatenate.19.starts.scalars, bf16[128,2560]{1,0:T(8,128)(2,1)S(1)} %constant_dynamic-update-slice_fusion.near, ...), custom_call_target="tpu_custom_call" | custom-call | tf_op jit(solution)/shard_map/backward/pallas_call | solution.py:210
  36.8 3.5 %collective-permute-start.17 = (bf16[10,96,128]{2,1,0:T(8,128)(2,1)S(1)}, bf16[10,96,128]{2,1,0:T(8,128)(2,1)S(1)}, u32[]{:S(2)}, u32[]{:S(2)}) collective-permute-start(bf16[10,96,128]{2,1,0:T(8,128)(2,1)S(1)} %get-tuple-element.36), channel_id=1, source_target_pairs={{0,8},{1,9},{2,10},{3,11},{4,12},{5,13},{6,14},{7,15},{8,0},{9,1},... | collective-permute-start | bytes 737288 | tf_op jit(solution)/shard_map/ppermute | solution.py:270
  40.5 1.6 %collective-permute-start.11 = (bf16[2,32,1280]{2,1,0:T(8,128)(2,1)S(1)}, bf16[2,32,1280]{2,1,0:T(8,128)(2,1)S(1)}, u32[]{:S(2)}, u32[]{:S(2)}) collective-permute-start(bf16[2,32,1280]{2,1,0:T(8,128)(2,1)S(1)} %pad_maximum_fusion.5), channel_id=1, source_target_pairs={{0,2},{1,3},{2,0},{3,1},{4,6},{5,7},{6,4},{7,5},{8,10},{9,11},{10,... | collective-permute-start | bytes 491528 | tf_op jit(solution)/shard_map/ppermute | solution.py:270
  42.1 0.5 collective-permute-start.16
  42.6 7.3 %collective-permute-done.12.rest_0_ = bf16[4,32,1280]{2,1,0:T(8,128)(2,1)S(1)} collective-permute-done((bf16[4,32,1280]{2,1,0:T(8,128)(2,1)S(1)}, bf16[4,32,1280]{2,1,0:T(8,128)(2,1)S(1)}, u32[]{:S(2)}, u32[]{:S(2)}) %collective-permute-start.12) | collective-permute-done | bytes 327712 | tf_op jit(solution)/shard_map/ppermute | solution.py:270
  49.9 0.4 collective-permute-start.13
  50.3 1.3 %collective-permute-start.14 = (bf16[1,32,1280]{2,1,0:T(8,128)(2,1)S(1)}, bf16[1,32,1280]{2,1,0:T(8,128)(2,1)S(1)}, u32[]{:S(2)}, u32[]{:S(2)}) collective-permute-start(bf16[1,32,1280]{2,1,0:T(8,128)(2,1)S(1)} %get-tuple-element.29), channel_id=1, source_target_pairs={{0,2},{1,3},{2,0},{3,1},{4,6},{5,7},{6,4},{7,5},{8,10},{9,11},{10,... | collective-permute-start | bytes 245768 | tf_op jit(solution)/shard_map/ppermute | solution.py:270
  51.5 3.1 %collective-permute-done.13.rest_3_ = bf16[1,32,1280]{2,1,0:T(8,128)(2,1)S(1)} collective-permute-done((bf16[1,32,1280]{2,1,0:T(8,128)(2,1)S(1)}, bf16[1,32,1280]{2,1,0:T(8,128)(2,1)S(1)}, u32[]{:S(2)}, u32[]{:S(2)}) %collective-permute-start.13) | collective-permute-done | bytes 81952 | tf_op jit(solution)/shard_map/ppermute | solution.py:270
  54.6 0.3 collective-permute-start.15
  54.9 1.5 %collective-permute-done.14.rest_4_ = bf16[1,32,1280]{2,1,0:T(8,128)(2,1)S(1)} collective-permute-done((bf16[1,32,1280]{2,1,0:T(8,128)(2,1)S(1)}, bf16[1,32,1280]{2,1,0:T(8,128)(2,1)S(1)}, u32[]{:S(2)}, u32[]{:S(2)}) %collective-permute-start.14) | collective-permute-done | bytes 81952 | tf_op jit(solution)/shard_map/ppermute | solution.py:270
  56.4 1.4 %join.1 = bf16[32,10240]{1,0:T(8,128)(2,1)} custom-call(s32[8]{0:T(128)S(1)} %stack.77.starts, bf16[4,32,1280]{2,1,0:T(8,128)(2,1)S(1)} %get-tuple-element.23.rest_0_, bf16[2,32,1280]{2,1,0:T(8,128)(2,1)S(1)} %collective-permute-done.10.rest_1_, bf16[2,32,1280]{2,1,0:T(8,128)(2,1)S(1)} %collective-permute-done.11.rest_2_, ...), custom_call_target="tpu_custom_call" | custom-call | tf_op jit(solution)/shard_map/join/pallas_call | solution.py:92
  58.1 1.9 %collective-permute-done.16.rest_1_ = bf16[10,96,128]{2,1,0:T(8,128)(2,1)S(1)} collective-permute-done((bf16[10,96,128]{2,1,0:T(8,128)(2,1)S(1)}, bf16[10,96,128]{2,1,0:T(8,128)(2,1)S(1)}, u32[]{:S(2)}, u32[]{:S(2)}) %collective-permute-start.16) | collective-permute-done | bytes 245792 | tf_op jit(solution)/shard_map/ppermute | solution.py:270
  60.0 1.1 %sum.1 = f32[2,10,96,128]{3,2,1,0:T(8,128)} custom-call(s32[1]{0:T(128)} %bitcast.19.half, f32[10,96,128]{2,1,0:T(8,128)S(1)} %get-tuple-element.34.rest_0_, bf16[10,96,128]{2,1,0:T(8,128)(2,1)S(1)} %collective-permute-done.16.rest_1_, bf16[10,96,128]{2,1,0:T(8,128)(2,1)S(1)} %collective-permute-done.17.rest_2_, ...), custom_call_target="tpu_custom_call" | custom-call | tf_op jit(solution)/shard_map/sum/pallas_call | solution.py:238
  (56 shorter events, 1.6 us)
Async XLA Ops:
  0.6 13.6 %collective-permute-start = (bf16[32,2560]{1,0:T(8,128)(2,1)}, bf16[32,2560]{1,0:T(8,128)(2,1)S(1)}, u32[]{:S(2)}, u32[]{:S(2)}) collective-permute-start(bf16[32,2560]{1,0:T(8,128)(2,1)} %param.5), channel_id=1, source_target_pairs={{0,4},{1,5},{2,6},{3,7},{4,0},{5,1},{6,2},{7,3},{8,12},{9,13},{10,... | collective-permute-start | bytes 491528 | tf_op jit(solution)/shard_map/ppermute | solution.py:270
  4.8 2.2 %copy-start.5 = (bf16[96,20,128]{2,0,1:T(8,128)(2,1)S(1)}, bf16[96,20,128]{2,0,1:T(8,128)(2,1)}, u32[]{:S(2)}) copy-start(bf16[96,20,128]{2,0,1:T(8,128)(2,1)} %param.6) | copy-start | bytes 1474564
  4.8 11.1 %collective-permute-start.3 = (bf16[2,32,1280]{2,1,0:T(8,128)(2,1)S(1)}, bf16[2,32,1280]{2,1,0:T(8,128)(2,1)S(1)}, u32[]{:S(2)}, u32[]{:S(2)}) collective-permute-start(bf16[2,32,1280]{2,1,0:T(8,128)(2,1)S(1)} %pad_maximum_fusion.3), channel_id=1, source_target_pairs={{0,4},{1,5},{2,6},{3,7},{4,0},{5,1},{6,2},{7,3},{8,12},{9,13},{10,... | collective-permute-start | bytes 491528 | tf_op jit(solution)/shard_map/ppermute | solution.py:270
  4.9 11.7 %collective-permute-start.4 = (bf16[2,32,1280]{2,1,0:T(8,128)(2,1)S(1)}, bf16[2,32,1280]{2,1,0:T(8,128)(2,1)S(1)}, u32[]{:S(2)}, u32[]{:S(2)}) collective-permute-start(bf16[2,32,1280]{2,1,0:T(8,128)(2,1)S(1)} %pad_maximum_fusion.4), channel_id=1, source_target_pairs={{0,4},{1,5},{2,6},{3,7},{4,0},{5,1},{6,2},{7,3},{8,12},{9,13},{10,... | collective-permute-start | bytes 491528 | tf_op jit(solution)/shard_map/ppermute | solution.py:270
  7.0 3.3 %copy-start.4 = (bf16[32,2560]{1,0:T(8,128)(2,1)S(1)}, bf16[32,2560]{1,0:T(8,128)(2,1)}, u32[]{:S(2)}) copy-start(bf16[32,2560]{1,0:T(8,128)(2,1)} %param.5) | copy-start | bytes 491524
  7.7 22.3 %collective-permute-start.7 = (bf16[10,96,128]{2,1,0:T(8,128)(2,1)}, bf16[10,96,128]{2,1,0:T(8,128)(2,1)S(1)}, u32[]{:S(2)}, u32[]{:S(2)}) collective-permute-start(bf16[10,96,128]{2,1,0:T(8,128)(2,1)} %get-tuple-element.20), channel_id=1, source_target_pairs={{0,12},{1,13},{2,14},{3,15},{4,8},{5,9},{6,10},{7,11},{8,4},{9,5},... | collective-permute-start | bytes 737288 | tf_op jit(solution)/shard_map/ppermute | solution.py:270
  10.2 21.2 %collective-permute-start.6 = (bf16[10,96,128]{2,1,0:T(8,128)(2,1)S(1)}, bf16[10,96,128]{2,1,0:T(8,128)(2,1)S(1)}, u32[]{:S(2)}, u32[]{:S(2)}) collective-permute-start(bf16[10,96,128]{2,1,0:T(8,128)(2,1)S(1)} %get-tuple-element.43.rest_0_), channel_id=1, source_target_pairs={{0,8},{1,9},{2,10},{3,11},{4,12},{5,13},{6,14},{7,15},{8,0},{9,1},... | collective-permute-start | bytes 737288 | tf_op jit(solution)/shard_map/ppermute | solution.py:270
  10.3 0.7 %copy-start.6 = (s32[20,3]{0,1:T(4,128)S(1)}, s32[20,3]{0,1:T(4,128)}, u32[]{:S(2)}) copy-start(s32[20,3]{0,1:T(4,128)} %param.8) | copy-start | bytes 724
  11.2 0.7 %copy-start.7 = (s32[20]{0:T(128)S(1)}, s32[20]{0:T(128)}, u32[]{:S(2)}) copy-start(s32[20]{0:T(128)} %param.9) | copy-start | bytes 244
  13.5 0.7 %copy-start = (bf16[4,32,1280]{2,1,0:T(8,128)(2,1)}, bf16[4,32,1280]{2,1,0:T(8,128)(2,1)S(1)}, u32[]{:S(2)}) copy-start(bf16[4,32,1280]{2,1,0:T(8,128)(2,1)S(1)} %cut.1.rest_0_) | copy-start | bytes 983044
  14.3 4.0 %slice-start.1 = ((bf16[4,32,1280]{2,1,0:T(8,128)(2,1)}), bf16[2,32,1280]{2,1,0:T(8,128)(2,1)S(1)}, s32[]{:S(2)}) async-start(bf16[4,32,1280]{2,1,0:T(8,128)(2,1)} %copy-done), calls=%async_computation.1 | async-start | bytes 327680 | tf_op jit(solution)/shard_map/slice | solution.py:256
  14.3 10.7 %collective-permute-start.1 = (bf16[64,2560]{1,0:T(8,128)(2,1)S(1)}, bf16[64,2560]{1,0:T(8,128)(2,1)S(1)}, u32[]{:S(2)}, u32[]{:S(2)}) collective-permute-start(bf16[64,2560]{1,0:T(8,128)(2,1)S(1)} %pad_maximum_fusion), channel_id=1, source_target_pairs={{0,2},{1,3},{2,0},{3,1},{4,6},{5,7},{6,4},{7,5},{8,10},{9,11},{10,... | collective-permute-start | bytes 983048 | tf_op jit(solution)/shard_map/ppermute | solution.py:270
  15.9 0.8 %copy-start.2 = (bf16[2,32,1280]{2,1,0:T(8,128)(2,1)}, bf16[2,32,1280]{2,1,0:T(8,128)(2,1)S(1)}, u32[]{:S(2)}) copy-start(bf16[2,32,1280]{2,1,0:T(8,128)(2,1)S(1)} %collective-permute-done.3.rest_1_) | copy-start | bytes 491524
  16.7 14.7 %collective-permute-start.5 = (bf16[10,96,128]{2,1,0:T(8,128)(2,1)}, bf16[10,96,128]{2,1,0:T(8,128)(2,1)S(1)}, u32[]{:S(2)}, u32[]{:S(2)}) collective-permute-start(bf16[10,96,128]{2,1,0:T(8,128)(2,1)} %get-tuple-element.20), channel_id=1, source_target_pairs={{0,4},{1,5},{2,6},{3,7},{4,0},{5,1},{6,2},{7,3},{8,12},{9,13},{10,... | collective-permute-start | bytes 737288 | tf_op jit(solution)/shard_map/ppermute | solution.py:270
  18.4 11.4 %collective-permute-start.8 = (bf16[4,32,1280]{2,1,0:T(8,128)(2,1)S(1)}, bf16[4,32,1280]{2,1,0:T(8,128)(2,1)S(1)}, u32[]{:S(2)}, u32[]{:S(2)}) collective-permute-start(bf16[4,32,1280]{2,1,0:T(8,128)(2,1)S(1)} %pad_maximum_fusion.1), channel_id=1, source_target_pairs={{0,2},{1,3},{2,0},{3,1},{4,6},{5,7},{6,4},{7,5},{8,10},{9,11},{10,... | collective-permute-start | bytes 983048 | tf_op jit(solution)/shard_map/ppermute | solution.py:270
  25.0 4.7 %slice-start = ((bf16[4,32,1280]{2,1,0:T(8,128)(2,1)}), bf16[1,32,1280]{2,1,0:T(8,128)(2,1)S(1)}, s32[]{:S(2)}) async-start(bf16[4,32,1280]{2,1,0:T(8,128)(2,1)} %copy-done), calls=%async_computation | async-start | bytes 163840 | tf_op jit(solution)/shard_map/slice | solution.py:256
  25.1 4.7 %slice-start.2 = ((bf16[2,32,1280]{2,1,0:T(8,128)(2,1)}), bf16[1,32,1280]{2,1,0:T(8,128)(2,1)S(1)}, s32[]{:S(2)}) async-start(bf16[2,32,1280]{2,1,0:T(8,128)(2,1)} %copy-done.2), calls=%async_computation.2 | async-start | bytes 163840 | tf_op jit(solution)/shard_map/slice | solution.py:256
  25.1 7.0 %collective-permute-start.2 = (bf16[128,2560]{1,0:T(8,128)(2,1)S(1)}, bf16[128,2560]{1,0:T(8,128)(2,1)S(1)}, u32[]{:S(2)}, u32[]{:S(2)}) collective-permute-start(bf16[128,2560]{1,0:T(8,128)(2,1)S(1)} %constant_dynamic-update-slice_fusion.near), channel_id=1, source_target_pairs={{0,1},{1,0},{2,3},{3,2},{4,5},{5,4},{6,7},{7,6},{8,9},{9,8},{10,11... | collective-permute-start | bytes 1966088 | tf_op jit(solution)/shard_map/ppermute | solution.py:270
  29.8 2.2 %collective-permute-start.9 = (bf16[4,32,1280]{2,1,0:T(8,128)(2,1)S(1)}, bf16[4,32,1280]{2,1,0:T(8,128)(2,1)S(1)}, u32[]{:S(2)}, u32[]{:S(2)}) collective-permute-start(bf16[4,32,1280]{2,1,0:T(8,128)(2,1)S(1)} %pad_maximum_fusion.2), channel_id=1, source_target_pairs={{0,1},{1,0},{2,3},{3,2},{4,5},{5,4},{6,7},{7,6},{8,9},{9,8},{10,11... | collective-permute-start | bytes 983048 | tf_op jit(solution)/shard_map/ppermute | solution.py:270
  30.0 2.1 %copy-start.1 = (bf16[4,32,1280]{2,1,0:T(8,128)(2,1)S(1)}, bf16[4,32,1280]{2,1,0:T(8,128)(2,1)}, u32[]{:S(2)}) copy-start(bf16[4,32,1280]{2,1,0:T(8,128)(2,1)} %copy-done) | copy-start | bytes 983044
  30.0 2.1 %copy-start.3 = (bf16[2,32,1280]{2,1,0:T(8,128)(2,1)S(1)}, bf16[2,32,1280]{2,1,0:T(8,128)(2,1)}, u32[]{:S(2)}) copy-start(bf16[2,32,1280]{2,1,0:T(8,128)(2,1)} %copy-done.2) | copy-start | bytes 491524
  34.0 6.5 %collective-permute-start.10 = (bf16[2,32,1280]{2,1,0:T(8,128)(2,1)S(1)}, bf16[2,32,1280]{2,1,0:T(8,128)(2,1)S(1)}, u32[]{:S(2)}, u32[]{:S(2)}) collective-permute-start(bf16[2,32,1280]{2,1,0:T(8,128)(2,1)S(1)} %slice.29), channel_id=1, source_target_pairs={{0,1},{1,0},{2,3},{3,2},{4,5},{5,4},{6,7},{7,6},{8,9},{9,8},{10,11... | collective-permute-start | bytes 491528 | tf_op jit(solution)/shard_map/ppermute | solution.py:270
  34.1 15.8 %collective-permute-start.12 = (bf16[4,32,1280]{2,1,0:T(8,128)(2,1)S(1)}, bf16[4,32,1280]{2,1,0:T(8,128)(2,1)S(1)}, u32[]{:S(2)}, u32[]{:S(2)}) collective-permute-start(bf16[4,32,1280]{2,1,0:T(8,128)(2,1)S(1)} %get-tuple-element.27), channel_id=1, source_target_pairs={{0,4},{1,5},{2,6},{3,7},{4,0},{5,1},{6,2},{7,3},{8,12},{9,13},{10,... | collective-permute-start | bytes 983048 | tf_op jit(solution)/shard_map/ppermute | solution.py:270
  36.8 21.0 %collective-permute-start.17 = (bf16[10,96,128]{2,1,0:T(8,128)(2,1)S(1)}, bf16[10,96,128]{2,1,0:T(8,128)(2,1)S(1)}, u32[]{:S(2)}, u32[]{:S(2)}) collective-permute-start(bf16[10,96,128]{2,1,0:T(8,128)(2,1)S(1)} %get-tuple-element.36), channel_id=1, source_target_pairs={{0,8},{1,9},{2,10},{3,11},{4,12},{5,13},{6,14},{7,15},{8,0},{9,1},... | collective-permute-start | bytes 737288 | tf_op jit(solution)/shard_map/ppermute | solution.py:270
  40.3 17.7 %collective-permute-start.18 = (bf16[10,96,128]{2,1,0:T(8,128)(2,1)S(1)}, bf16[10,96,128]{2,1,0:T(8,128)(2,1)S(1)}, u32[]{:S(2)}, u32[]{:S(2)}) collective-permute-start(bf16[10,96,128]{2,1,0:T(8,128)(2,1)S(1)} %get-tuple-element.37), channel_id=1, source_target_pairs={{0,12},{1,13},{2,14},{3,15},{4,8},{5,9},{6,10},{7,11},{8,4},{9,5},... | collective-permute-start | bytes 737288 | tf_op jit(solution)/shard_map/ppermute | solution.py:270
  40.5 9.7 %collective-permute-start.11 = (bf16[2,32,1280]{2,1,0:T(8,128)(2,1)S(1)}, bf16[2,32,1280]{2,1,0:T(8,128)(2,1)S(1)}, u32[]{:S(2)}, u32[]{:S(2)}) collective-permute-start(bf16[2,32,1280]{2,1,0:T(8,128)(2,1)S(1)} %pad_maximum_fusion.5), channel_id=1, source_target_pairs={{0,2},{1,3},{2,0},{3,1},{4,6},{5,7},{6,4},{7,5},{8,10},{9,11},{10,... | collective-permute-start | bytes 491528 | tf_op jit(solution)/shard_map/ppermute | solution.py:270
  42.1 17.9 %collective-permute-start.16 = (bf16[10,96,128]{2,1,0:T(8,128)(2,1)S(1)}, bf16[10,96,128]{2,1,0:T(8,128)(2,1)S(1)}, u32[]{:S(2)}, u32[]{:S(2)}) collective-permute-start(bf16[10,96,128]{2,1,0:T(8,128)(2,1)S(1)} %get-tuple-element.35), channel_id=1, source_target_pairs={{0,4},{1,5},{2,6},{3,7},{4,0},{5,1},{6,2},{7,3},{8,12},{9,13},{10,... | collective-permute-start | bytes 737288 | tf_op jit(solution)/shard_map/ppermute | solution.py:270
  49.9 4.7 %collective-permute-start.13 = (bf16[1,32,1280]{2,1,0:T(8,128)(2,1)S(1)}, bf16[1,32,1280]{2,1,0:T(8,128)(2,1)S(1)}, u32[]{:S(2)}, u32[]{:S(2)}) collective-permute-start(bf16[1,32,1280]{2,1,0:T(8,128)(2,1)S(1)} %get-tuple-element.28), channel_id=1, source_target_pairs={{0,3},{1,2},{2,1},{3,0},{4,7},{5,6},{6,5},{7,4},{8,11},{9,10},{10,... | collective-permute-start | bytes 245768 | tf_op jit(solution)/shard_map/ppermute | solution.py:270
  50.3 6.2 %collective-permute-start.14 = (bf16[1,32,1280]{2,1,0:T(8,128)(2,1)S(1)}, bf16[1,32,1280]{2,1,0:T(8,128)(2,1)S(1)}, u32[]{:S(2)}, u32[]{:S(2)}) collective-permute-start(bf16[1,32,1280]{2,1,0:T(8,128)(2,1)S(1)} %get-tuple-element.29), channel_id=1, source_target_pairs={{0,2},{1,3},{2,0},{3,1},{4,6},{5,7},{6,4},{7,5},{8,10},{9,11},{10,... | collective-permute-start | bytes 245768 | tf_op jit(solution)/shard_map/ppermute | solution.py:270
  54.6 1.8 %collective-permute-start.15 = (bf16[1,32,1280]{2,1,0:T(8,128)(2,1)S(1)}, bf16[1,32,1280]{2,1,0:T(8,128)(2,1)S(1)}, u32[]{:S(2)}, u32[]{:S(2)}) collective-permute-start(bf16[1,32,1280]{2,1,0:T(8,128)(2,1)S(1)} %get-tuple-element.30), channel_id=1, source_target_pairs={{0,1},{1,0},{2,3},{3,2},{4,5},{5,4},{6,7},{7,6},{8,9},{9,8},{10,11... | collective-permute-start | bytes 245768 | tf_op jit(solution)/shard_map/ppermute | solution.py:270

commit v26 on v22

--- a/solution.py
+++ b/solution.py
@@ -306,11 +306,11 @@
         stacks = lax.all_to_all(outgoing, "fsdp", split_axis=0, concat_axis=0, tiled=True)
         weights = stacks.transpose(1, 0, 2, 3).reshape(share, fsdp * size, TILE)
 
-    sizes = (0, stripes)
+    sizes = (tensor, stripes)
     part = tensor // HOPS
     ends = jnp.stack([half * share, z if direct else z * 0]).astype(jnp.int32)
-    scalars = jnp.concatenate([tile_list.reshape(-1), tile_counts, ends])
-    stay, = cut_call(first_tiles([(0, b) for b in range(tensor)]), cotangent, tensor, 1)
+    scalars = jnp.concatenate([first_tiles([(0, b) for b in range(tensor)]), tile_list.reshape(-1), tile_counts, ends])
+    stay, = cut_call(scalars, cotangent, tensor, 1)
     near = jnp.concatenate([tokens, near], axis=0)
     for bit in bits:
         far = swap(near, 0, bit)

time: 62.4 us -> 61.3 us (0.982)
  the two profiles are of different devices: /device:TPU:16 before, /device:TPU:0 now
where the time goes in v26:
time: 61.3 us; the launch traced here: 60.9 us
  waiting for transfers between devices  25.3 us (41%)
  starting transfers between devices  21.4 us (35%)
  Pallas kernels  8.7 us (14%)
  local copies, waits for them, and re-layouts  4.26 us (7%)
  between operations  0.94 us (2%)
    ppermute x19, waiting for transfers between devices, swap(): return lax.ppermute(value, ('fsdp', 'tensor'), pairs)  25.3 us
    ppermute x19, starting transfers between devices, swap(): return lax.ppermute(value, ('fsdp', 'tensor'), pairs)  21.4 us
    unnamed x19, local copies, waits for them, and re-layouts  2.18 us
    pallas_call x1, Pallas kernels, forward_call(): pl.pallas_call(functools.partial(forward_kernel, sizes), out_shape=[jax.S...  1.85 us
    pallas_call x2, Pallas kernels, sum_call(): pl.pallas_call(sum_kernel if before is None else sum_into_kernel, out_sha...  1.77 us
    pallas_call x1, Pallas kernels, cut_call(): pl.pallas_call(cut_kernel, out_shape=[jax.ShapeDtypeStruct((count // part...  1.6 us
    pallas_call x1, Pallas kernels, join_call(): pl.pallas_call(functools.partial(join_kernel, refs), out_shape=jax.ShapeD...  1.44 us
    pallas_call x1, Pallas kernels, backward_call(): pl.pallas_call(functools.partial(backward_kernel, sizes), out_shape=[jax....  1.37 us
  transfers between devices with their start and end apart: 19, of which 8 were waited for; matrix products, arithmetic and copies ran while one was open for 4% of the time, Pallas kernels for 10%

profile of v26, /device:TPU:0, one launch (start us, length us, event | category | flops | bytes accessed | tf_op | source)
XLA Modules:
  0.0 60.9 jit_solution(16544493149081528140)
XLA Ops:
  0.6 3.1 %collective-permute-start = (bf16[32,2560]{1,0:T(8,128)(2,1)}, bf16[32,2560]{1,0:T(8,128)(2,1)S(1)}, u32[]{:S(2)}, u32[]{:S(2)}) collective-permute-start(bf16[32,2560]{1,0:T(8,128)(2,1)} %param.5), channel_id=1, source_target_pairs={{0,4},{1,5},{2,6},{3,7},{4,0},{5,1},{6,2},{7,3},{8,12},{9,13},{10,... | collective-permute-start | bytes 491528 | tf_op jit(solution)/shard_map/ppermute | solution.py:275
  3.7 1.0 %dynamic-slice_bitcast_fusion.3 = (bf16[1,32,1280]{2,1,0:T(8,128)(2,1)S(1)}, bf16[1,32,1280]{2,1,0:T(8,128)(2,1)S(1)}, bf16[1,32,1280]{2,1,0:T(8,128)(2,1)S(1)}, bf16[1,32,1280]{2,1,0:T(8,128)(2,1)S(1)}) fusion(bf16[32,10240]{1,0:T(8,128)(2,1)} %whole.1, s32[]{:T(128)S(6)} %select_n.30, s32[]{:T(128)S(6)} %select_n.29, s32[]{:T(128)S(6)} %select_n.28, ...), kind=kLoop, calls=%fused_computation.9 | loop fusion | bytes 655376 | tf_op jit(solution)/shard_map/stack | solution.py:294
  4.9 2.0 %collective-permute-start.4 = (bf16[2,32,1280]{2,1,0:T(8,128)(2,1)S(1)}, bf16[2,32,1280]{2,1,0:T(8,128)(2,1)S(1)}, u32[]{:S(2)}, u32[]{:S(2)}) collective-permute-start(bf16[2,32,1280]{2,1,0:T(8,128)(2,1)S(1)} %pad_maximum_fusion.4), channel_id=1, source_target_pairs={{0,4},{1,5},{2,6},{3,7},{4,0},{5,1},{6,2},{7,3},{8,12},{9,13},{10,... | collective-permute-start | bytes 491528 | tf_op jit(solution)/shard_map/ppermute | solution.py:275
  7.0 0.7 %dynamic-slice_bitcast_fusion = (bf16[10,96,128]{2,1,0:T(8,128)(2,1)}, bf16[10,96,128]{2,1,0:T(8,128)(2,1)S(1)}) fusion(bf16[96,20,128]{2,0,1:T(8,128)(2,1)S(1)} %copy-done.5, s32[]{:T(128)S(6)} %select_n.27, s32[]{:T(128)S(6)} %select_n.26), kind=kLoop, calls=%fused_computation.3 | loop fusion | bytes 983048 | tf_op jit(solution)/shard_map/dynamic_slice | solution.py:300
  7.7 2.5 %collective-permute-start.7 = (bf16[10,96,128]{2,1,0:T(8,128)(2,1)}, bf16[10,96,128]{2,1,0:T(8,128)(2,1)S(1)}, u32[]{:S(2)}, u32[]{:S(2)}) collective-permute-start(bf16[10,96,128]{2,1,0:T(8,128)(2,1)} %get-tuple-element.20), channel_id=1, source_target_pairs={{0,12},{1,13},{2,14},{3,15},{4,8},{5,9},{6,10},{7,11},{8,4},{9,5},... | collective-permute-start | bytes 737288 | tf_op jit(solution)/shard_map/ppermute | solution.py:275
  10.3 0.7 %copy-done.6 = s32[20,3]{0,1:T(4,128)S(1)} copy-done((s32[20,3]{0,1:T(4,128)S(1)}, s32[20,3]{0,1:T(4,128)}, u32[]{:S(2)}) %copy-start.6) | copy-done | bytes 264
  11.2 0.6 %copy-done.7 = s32[20]{0:T(128)S(1)} copy-done((s32[20]{0:T(128)S(1)}, s32[20]{0:T(128)}, u32[]{:S(2)}) %copy-start.7) | copy-done | bytes 104
  11.9 1.6 %cut.1.rest_0_ = bf16[4,32,1280]{2,1,0:T(8,128)(2,1)S(1)} custom-call(s32[86]{0:T(128)S(1)} %concatenate.19.starts.scalars, bf16[32,10240]{1,0:T(8,128)(2,1)} %whole.1), custom_call_target="tpu_custom_call" | custom-call | tf_op jit(solution)/shard_map/cut/pallas_call | solution.py:55
  13.5 0.7 %copy-done = bf16[4,32,1280]{2,1,0:T(8,128)(2,1)} copy-done((bf16[4,32,1280]{2,1,0:T(8,128)(2,1)}, bf16[4,32,1280]{2,1,0:T(8,128)(2,1)S(1)}, u32[]{:S(2)}) %copy-start) | copy-done | bytes 327704
  14.3 1.6 %collective-permute-start.1 = (bf16[64,2560]{1,0:T(8,128)(2,1)S(1)}, bf16[64,2560]{1,0:T(8,128)(2,1)S(1)}, u32[]{:S(2)}, u32[]{:S(2)}) collective-permute-start(bf16[64,2560]{1,0:T(8,128)(2,1)S(1)} %pad_maximum_fusion), channel_id=1, source_target_pairs={{0,2},{1,3},{2,0},{3,1},{4,6},{5,7},{6,4},{7,5},{8,10},{9,11},{10,... | collective-permute-start | bytes 983048 | tf_op jit(solution)/shard_map/ppermute | solution.py:275
  15.9 0.8 %collective-permute-done.4.rest_2_ = bf16[2,32,1280]{2,1,0:T(8,128)(2,1)S(1)} collective-permute-done((bf16[2,32,1280]{2,1,0:T(8,128)(2,1)S(1)}, bf16[2,32,1280]{2,1,0:T(8,128)(2,1)S(1)}, u32[]{:S(2)}, u32[]{:S(2)}) %collective-permute-start.4) | collective-permute-done | bytes 163872 | tf_op jit(solution)/shard_map/ppermute | solution.py:275
  16.7 1.6 %collective-permute-start.5 = (bf16[10,96,128]{2,1,0:T(8,128)(2,1)}, bf16[10,96,128]{2,1,0:T(8,128)(2,1)S(1)}, u32[]{:S(2)}, u32[]{:S(2)}) collective-permute-start(bf16[10,96,128]{2,1,0:T(8,128)(2,1)} %get-tuple-element.20), channel_id=1, source_target_pairs={{0,4},{1,5},{2,6},{3,7},{4,0},{5,1},{6,2},{7,3},{8,12},{9,13},{10,... | collective-permute-start | bytes 737288 | tf_op jit(solution)/shard_map/ppermute | solution.py:275
  18.4 1.3 %collective-permute-start.8 = (bf16[4,32,1280]{2,1,0:T(8,128)(2,1)S(1)}, bf16[4,32,1280]{2,1,0:T(8,128)(2,1)S(1)}, u32[]{:S(2)}, u32[]{:S(2)}) collective-permute-start(bf16[4,32,1280]{2,1,0:T(8,128)(2,1)S(1)} %pad_maximum_fusion.1), channel_id=1, source_target_pairs={{0,2},{1,3},{2,0},{3,1},{4,6},{5,7},{6,4},{7,5},{8,10},{9,11},{10,... | collective-permute-start | bytes 983048 | tf_op jit(solution)/shard_map/ppermute | solution.py:275
  19.6 5.4 %collective-permute-done.1 = bf16[64,2560]{1,0:T(8,128)(2,1)S(1)} collective-permute-done((bf16[64,2560]{1,0:T(8,128)(2,1)S(1)}, bf16[64,2560]{1,0:T(8,128)(2,1)S(1)}, u32[]{:S(2)}, u32[]{:S(2)}) %collective-permute-start.1) | collective-permute-done | bytes 327712 | tf_op jit(solution)/shard_map/ppermute | solution.py:275
  25.1 4.6 %collective-permute-done.8.rest_3_ = bf16[4,32,1280]{2,1,0:T(8,128)(2,1)S(1)} collective-permute-done((bf16[4,32,1280]{2,1,0:T(8,128)(2,1)S(1)}, bf16[4,32,1280]{2,1,0:T(8,128)(2,1)S(1)}, u32[]{:S(2)}, u32[]{:S(2)}) %collective-permute-start.8) | collective-permute-done | bytes 327712 | tf_op jit(solution)/shard_map/ppermute | solution.py:275
  30.0 1.4 %collective-permute-done.6.rest_2_ = bf16[10,96,128]{2,1,0:T(8,128)(2,1)S(1)} collective-permute-done((bf16[10,96,128]{2,1,0:T(8,128)(2,1)S(1)}, bf16[10,96,128]{2,1,0:T(8,128)(2,1)S(1)}, u32[]{:S(2)}, u32[]{:S(2)}) %collective-permute-start.6) | collective-permute-done | bytes 245792 | tf_op jit(solution)/shard_map/ppermute | solution.py:275
  31.4 0.6 %stack.90.weights = bf16[10,384,128]{2,1,0:T(8,128)(2,1)S(1)} custom-call(s32[4]{0:T(128)S(1)} %pad_add_fusion.scalars, bf16[10,96,128]{2,1,0:T(8,128)(2,1)S(1)} %get-tuple-element.43.rest_0_, bf16[10,96,128]{2,1,0:T(8,128)(2,1)S(1)} %collective-permute-done.5.rest_1_, bf16[10,96,128]{2,1,0:T(8,128)(2,1)S(1)} %collective-permute-done.6.rest_2_, ...), custom_call_target="tpu_custom_call" | custom-call | flops 2000000000 | tf_op jit(solution)/shard_map/stack/pallas_call | solution.py:184
  32.1 1.8 %forward.1 = (bf16[4,32,1280]{2,1,0:T(8,128)(2,1)S(1)}, bf16[4,32,1280]{2,1,0:T(8,128)(2,1)S(1)}, bf16[256,1280]{1,0:T(8,128)(2,1)S(1)}) custom-call(s32[86]{0:T(128)S(1)} %concatenate.19.starts.scalars, bf16[128,2560]{1,0:T(8,128)(2,1)S(1)} %constant_dynamic-update-slice_fusion.near, bf16[128,2560]{1,0:T(8,128)(2,1)S(1)} %collective-permute-done.2.far, ...), custom_call_target="tpu_custom_call" | custom-call | tf_op jit(solution)/shard_map/forward/pallas_call | solution.py:143
  34.1 1.4 %collective-permute-start.12 = (bf16[4,32,1280]{2,1,0:T(8,128)(2,1)S(1)}, bf16[4,32,1280]{2,1,0:T(8,128)(2,1)S(1)}, u32[]{:S(2)}, u32[]{:S(2)}) collective-permute-start(bf16[4,32,1280]{2,1,0:T(8,128)(2,1)S(1)} %get-tuple-element.27), channel_id=1, source_target_pairs={{0,4},{1,5},{2,6},{3,7},{4,0},{5,1},{6,2},{7,3},{8,12},{9,13},{10,... | collective-permute-start | bytes 983048 | tf_op jit(solution)/shard_map/ppermute | solution.py:275
  35.5 1.4 %backward.1 = (f32[10,96,128]{2,1,0:T(8,128)S(1)}, bf16[10,96,128]{2,1,0:T(8,128)(2,1)S(1)}, bf16[10,96,128]{2,1,0:T(8,128)(2,1)S(1)}, bf16[10,96,128]{2,1,0:T(8,128)(2,1)S(1)}) custom-call(s32[86]{0:T(128)S(1)} %concatenate.19.starts.scalars, bf16[128,2560]{1,0:T(8,128)(2,1)S(1)} %constant_dynamic-update-slice_fusion.near, ...), custom_call_target="tpu_custom_call" | custom-call | tf_op jit(solution)/shard_map/backward/pallas_call | solution.py:210
  36.8 3.5 %collective-permute-start.16 = (bf16[10,96,128]{2,1,0:T(8,128)(2,1)S(1)}, bf16[10,96,128]{2,1,0:T(8,128)(2,1)S(1)}, u32[]{:S(2)}, u32[]{:S(2)}) collective-permute-start(bf16[10,96,128]{2,1,0:T(8,128)(2,1)S(1)} %get-tuple-element.35), channel_id=1, source_target_pairs={{0,8},{1,9},{2,10},{3,11},{4,12},{5,13},{6,14},{7,15},{8,0},{9,1},... | collective-permute-start | bytes 737288 | tf_op jit(solution)/shard_map/ppermute | solution.py:275
  40.5 1.6 %collective-permute-start.11 = (bf16[2,32,1280]{2,1,0:T(8,128)(2,1)S(1)}, bf16[2,32,1280]{2,1,0:T(8,128)(2,1)S(1)}, u32[]{:S(2)}, u32[]{:S(2)}) collective-permute-start(bf16[2,32,1280]{2,1,0:T(8,128)(2,1)S(1)} %pad_maximum_fusion.5), channel_id=1, source_target_pairs={{0,2},{1,3},{2,0},{3,1},{4,6},{5,7},{6,4},{7,5},{8,10},{9,11},{10,... | collective-permute-start | bytes 491528 | tf_op jit(solution)/shard_map/ppermute | solution.py:275
  42.1 0.5 collective-permute-start.17
  42.6 7.3 %collective-permute-done.12.rest_0_ = bf16[4,32,1280]{2,1,0:T(8,128)(2,1)S(1)} collective-permute-done((bf16[4,32,1280]{2,1,0:T(8,128)(2,1)S(1)}, bf16[4,32,1280]{2,1,0:T(8,128)(2,1)S(1)}, u32[]{:S(2)}, u32[]{:S(2)}) %collective-permute-start.12) | collective-permute-done | bytes 327712 | tf_op jit(solution)/shard_map/ppermute | solution.py:275
  49.9 0.4 collective-permute-start.13
  50.3 1.3 %collective-permute-start.14 = (bf16[1,32,1280]{2,1,0:T(8,128)(2,1)S(1)}, bf16[1,32,1280]{2,1,0:T(8,128)(2,1)S(1)}, u32[]{:S(2)}, u32[]{:S(2)}) collective-permute-start(bf16[1,32,1280]{2,1,0:T(8,128)(2,1)S(1)} %get-tuple-element.29), channel_id=1, source_target_pairs={{0,2},{1,3},{2,0},{3,1},{4,6},{5,7},{6,4},{7,5},{8,10},{9,11},{10,... | collective-permute-start | bytes 245768 | tf_op jit(solution)/shard_map/ppermute | solution.py:275
  51.5 3.1 %collective-permute-done.13.rest_3_ = bf16[1,32,1280]{2,1,0:T(8,128)(2,1)S(1)} collective-permute-done((bf16[1,32,1280]{2,1,0:T(8,128)(2,1)S(1)}, bf16[1,32,1280]{2,1,0:T(8,128)(2,1)S(1)}, u32[]{:S(2)}, u32[]{:S(2)}) %collective-permute-start.13) | collective-permute-done | bytes 81952 | tf_op jit(solution)/shard_map/ppermute | solution.py:275
  54.9 1.5 %collective-permute-done.14.rest_4_ = bf16[1,32,1280]{2,1,0:T(8,128)(2,1)S(1)} collective-permute-done((bf16[1,32,1280]{2,1,0:T(8,128)(2,1)S(1)}, bf16[1,32,1280]{2,1,0:T(8,128)(2,1)S(1)}, u32[]{:S(2)}, u32[]{:S(2)}) %collective-permute-start.14) | collective-permute-done | bytes 81952 | tf_op jit(solution)/shard_map/ppermute | solution.py:275
  56.5 1.4 %join.1 = bf16[32,10240]{1,0:T(8,128)(2,1)} custom-call(s32[8]{0:T(128)S(1)} %stack.77.starts, bf16[4,32,1280]{2,1,0:T(8,128)(2,1)S(1)} %get-tuple-element.23.rest_0_, bf16[2,32,1280]{2,1,0:T(8,128)(2,1)S(1)} %collective-permute-done.10.rest_1_, bf16[2,32,1280]{2,1,0:T(8,128)(2,1)S(1)} %collective-permute-done.11.rest_2_, ...), custom_call_target="tpu_custom_call" | custom-call | tf_op jit(solution)/shard_map/join/pallas_call | solution.py:92
  57.9 0.9 %sum.2.before = f32[2,10,96,128]{3,2,1,0:T(8,128)} custom-call(s32[1]{0:T(128)} %bitcast.19.half, f32[10,96,128]{2,1,0:T(8,128)S(1)} %get-tuple-element.34.rest_0_, bf16[10,96,128]{2,1,0:T(8,128)(2,1)S(1)} %collective-permute-done.16.rest_1_), custom_call_target="tpu_custom_call" | custom-call | tf_op jit(solution)/shard_map/sum/pallas_call | solution.py:242
  58.8 1.2 %collective-permute-done.17.rest_0_ = bf16[10,96,128]{2,1,0:T(8,128)(2,1)S(1)} collective-permute-done((bf16[10,96,128]{2,1,0:T(8,128)(2,1)S(1)}, bf16[10,96,128]{2,1,0:T(8,128)(2,1)S(1)}, u32[]{:S(2)}, u32[]{:S(2)}) %collective-permute-start.17) | collective-permute-done | bytes 245792 | tf_op jit(solution)/shard_map/ppermute | solution.py:275
  60.0 0.9 %sum.3 = f32[2,10,96,128]{3,2,1,0:T(8,128)} custom-call(s32[1]{0:T(128)S(6)} %sub.5.half, f32[2,10,96,128]{3,2,1,0:T(8,128)} %sum.2.before, bf16[10,96,128]{2,1,0:T(8,128)(2,1)S(1)} %collective-permute-done.17.rest_0_, bf16[10,96,128]{2,1,0:T(8,128)(2,1)S(1)} %collective-permute-done.18.rest_1_), custom_call_target="tpu_custom_call", output_to_operand_aliasing={{}: (1, {})} | custom-call | tf_op jit(solution)/shard_map/sum/pallas_call | solution.py:242
  (57 shorter events, 1.6 us)
Async XLA Ops:
  0.6 13.6 %collective-permute-start = (bf16[32,2560]{1,0:T(8,128)(2,1)}, bf16[32,2560]{1,0:T(8,128)(2,1)S(1)}, u32[]{:S(2)}, u32[]{:S(2)}) collective-permute-start(bf16[32,2560]{1,0:T(8,128)(2,1)} %param.5), channel_id=1, source_target_pairs={{0,4},{1,5},{2,6},{3,7},{4,0},{5,1},{6,2},{7,3},{8,12},{9,13},{10,... | collective-permute-start | bytes 491528 | tf_op jit(solution)/shard_map/ppermute | solution.py:275
  4.8 2.2 %copy-start.5 = (bf16[96,20,128]{2,0,1:T(8,128)(2,1)S(1)}, bf16[96,20,128]{2,0,1:T(8,128)(2,1)}, u32[]{:S(2)}) copy-start(bf16[96,20,128]{2,0,1:T(8,128)(2,1)} %param.6) | copy-start | bytes 1474564
  4.8 11.1 %collective-permute-start.3 = (bf16[2,32,1280]{2,1,0:T(8,128)(2,1)S(1)}, bf16[2,32,1280]{2,1,0:T(8,128)(2,1)S(1)}, u32[]{:S(2)}, u32[]{:S(2)}) collective-permute-start(bf16[2,32,1280]{2,1,0:T(8,128)(2,1)S(1)} %pad_maximum_fusion.3), channel_id=1, source_target_pairs={{0,4},{1,5},{2,6},{3,7},{4,0},{5,1},{6,2},{7,3},{8,12},{9,13},{10,... | collective-permute-start | bytes 491528 | tf_op jit(solution)/shard_map/ppermute | solution.py:275
  4.9 11.7 %collective-permute-start.4 = (bf16[2,32,1280]{2,1,0:T(8,128)(2,1)S(1)}, bf16[2,32,1280]{2,1,0:T(8,128)(2,1)S(1)}, u32[]{:S(2)}, u32[]{:S(2)}) collective-permute-start(bf16[2,32,1280]{2,1,0:T(8,128)(2,1)S(1)} %pad_maximum_fusion.4), channel_id=1, source_target_pairs={{0,4},{1,5},{2,6},{3,7},{4,0},{5,1},{6,2},{7,3},{8,12},{9,13},{10,... | collective-permute-start | bytes 491528 | tf_op jit(solution)/shard_map/ppermute | solution.py:275
  7.0 3.3 %copy-start.4 = (bf16[32,2560]{1,0:T(8,128)(2,1)S(1)}, bf16[32,2560]{1,0:T(8,128)(2,1)}, u32[]{:S(2)}) copy-start(bf16[32,2560]{1,0:T(8,128)(2,1)} %param.5) | copy-start | bytes 491524
  7.7 22.3 %collective-permute-start.7 = (bf16[10,96,128]{2,1,0:T(8,128)(2,1)}, bf16[10,96,128]{2,1,0:T(8,128)(2,1)S(1)}, u32[]{:S(2)}, u32[]{:S(2)}) collective-permute-start(bf16[10,96,128]{2,1,0:T(8,128)(2,1)} %get-tuple-element.20), channel_id=1, source_target_pairs={{0,12},{1,13},{2,14},{3,15},{4,8},{5,9},{6,10},{7,11},{8,4},{9,5},... | collective-permute-start | bytes 737288 | tf_op jit(solution)/shard_map/ppermute | solution.py:275
  10.2 21.2 %collective-permute-start.6 = (bf16[10,96,128]{2,1,0:T(8,128)(2,1)S(1)}, bf16[10,96,128]{2,1,0:T(8,128)(2,1)S(1)}, u32[]{:S(2)}, u32[]{:S(2)}) collective-permute-start(bf16[10,96,128]{2,1,0:T(8,128)(2,1)S(1)} %get-tuple-element.43.rest_0_), channel_id=1, source_target_pairs={{0,8},{1,9},{2,10},{3,11},{4,12},{5,13},{6,14},{7,15},{8,0},{9,1},... | collective-permute-start | bytes 737288 | tf_op jit(solution)/shard_map/ppermute | solution.py:275
  10.3 0.7 %copy-start.6 = (s32[20,3]{0,1:T(4,128)S(1)}, s32[20,3]{0,1:T(4,128)}, u32[]{:S(2)}) copy-start(s32[20,3]{0,1:T(4,128)} %param.8) | copy-start | bytes 724
  11.2 0.7 %copy-start.7 = (s32[20]{0:T(128)S(1)}, s32[20]{0:T(128)}, u32[]{:S(2)}) copy-start(s32[20]{0:T(128)} %param.9) | copy-start | bytes 244
  13.5 0.7 %copy-start = (bf16[4,32,1280]{2,1,0:T(8,128)(2,1)}, bf16[4,32,1280]{2,1,0:T(8,128)(2,1)S(1)}, u32[]{:S(2)}) copy-start(bf16[4,32,1280]{2,1,0:T(8,128)(2,1)S(1)} %cut.1.rest_0_) | copy-start | bytes 983044
  14.3 4.0 %slice-start.1 = ((bf16[4,32,1280]{2,1,0:T(8,128)(2,1)}), bf16[2,32,1280]{2,1,0:T(8,128)(2,1)S(1)}, s32[]{:S(2)}) async-start(bf16[4,32,1280]{2,1,0:T(8,128)(2,1)} %copy-done), calls=%async_computation.1 | async-start | bytes 327680 | tf_op jit(solution)/shard_map/slice | solution.py:261
  14.3 10.7 %collective-permute-start.1 = (bf16[64,2560]{1,0:T(8,128)(2,1)S(1)}, bf16[64,2560]{1,0:T(8,128)(2,1)S(1)}, u32[]{:S(2)}, u32[]{:S(2)}) collective-permute-start(bf16[64,2560]{1,0:T(8,128)(2,1)S(1)} %pad_maximum_fusion), channel_id=1, source_target_pairs={{0,2},{1,3},{2,0},{3,1},{4,6},{5,7},{6,4},{7,5},{8,10},{9,11},{10,... | collective-permute-start | bytes 983048 | tf_op jit(solution)/shard_map/ppermute | solution.py:275
  15.9 0.8 %copy-start.2 = (bf16[2,32,1280]{2,1,0:T(8,128)(2,1)}, bf16[2,32,1280]{2,1,0:T(8,128)(2,1)S(1)}, u32[]{:S(2)}) copy-start(bf16[2,32,1280]{2,1,0:T(8,128)(2,1)S(1)} %collective-permute-done.3.rest_1_) | copy-start | bytes 491524
  16.7 14.7 %collective-permute-start.5 = (bf16[10,96,128]{2,1,0:T(8,128)(2,1)}, bf16[10,96,128]{2,1,0:T(8,128)(2,1)S(1)}, u32[]{:S(2)}, u32[]{:S(2)}) collective-permute-start(bf16[10,96,128]{2,1,0:T(8,128)(2,1)} %get-tuple-element.20), channel_id=1, source_target_pairs={{0,4},{1,5},{2,6},{3,7},{4,0},{5,1},{6,2},{7,3},{8,12},{9,13},{10,... | collective-permute-start | bytes 737288 | tf_op jit(solution)/shard_map/ppermute | solution.py:275
  18.4 11.4 %collective-permute-start.8 = (bf16[4,32,1280]{2,1,0:T(8,128)(2,1)S(1)}, bf16[4,32,1280]{2,1,0:T(8,128)(2,1)S(1)}, u32[]{:S(2)}, u32[]{:S(2)}) collective-permute-start(bf16[4,32,1280]{2,1,0:T(8,128)(2,1)S(1)} %pad_maximum_fusion.1), channel_id=1, source_target_pairs={{0,2},{1,3},{2,0},{3,1},{4,6},{5,7},{6,4},{7,5},{8,10},{9,11},{10,... | collective-permute-start | bytes 983048 | tf_op jit(solution)/shard_map/ppermute | solution.py:275
  25.0 4.7 %slice-start = ((bf16[4,32,1280]{2,1,0:T(8,128)(2,1)}), bf16[1,32,1280]{2,1,0:T(8,128)(2,1)S(1)}, s32[]{:S(2)}) async-start(bf16[4,32,1280]{2,1,0:T(8,128)(2,1)} %copy-done), calls=%async_computation | async-start | bytes 163840 | tf_op jit(solution)/shard_map/slice | solution.py:261
  25.1 4.7 %slice-start.2 = ((bf16[2,32,1280]{2,1,0:T(8,128)(2,1)}), bf16[1,32,1280]{2,1,0:T(8,128)(2,1)S(1)}, s32[]{:S(2)}) async-start(bf16[2,32,1280]{2,1,0:T(8,128)(2,1)} %copy-done.2), calls=%async_computation.2 | async-start | bytes 163840 | tf_op jit(solution)/shard_map/slice | solution.py:261
  25.1 7.0 %collective-permute-start.2 = (bf16[128,2560]{1,0:T(8,128)(2,1)S(1)}, bf16[128,2560]{1,0:T(8,128)(2,1)S(1)}, u32[]{:S(2)}, u32[]{:S(2)}) collective-permute-start(bf16[128,2560]{1,0:T(8,128)(2,1)S(1)} %constant_dynamic-update-slice_fusion.near), channel_id=1, source_target_pairs={{0,1},{1,0},{2,3},{3,2},{4,5},{5,4},{6,7},{7,6},{8,9},{9,8},{10,11... | collective-permute-start | bytes 1966088 | tf_op jit(solution)/shard_map/ppermute | solution.py:275
  29.8 2.2 %collective-permute-start.9 = (bf16[4,32,1280]{2,1,0:T(8,128)(2,1)S(1)}, bf16[4,32,1280]{2,1,0:T(8,128)(2,1)S(1)}, u32[]{:S(2)}, u32[]{:S(2)}) collective-permute-start(bf16[4,32,1280]{2,1,0:T(8,128)(2,1)S(1)} %pad_maximum_fusion.2), channel_id=1, source_target_pairs={{0,1},{1,0},{2,3},{3,2},{4,5},{5,4},{6,7},{7,6},{8,9},{9,8},{10,11... | collective-permute-start | bytes 983048 | tf_op jit(solution)/shard_map/ppermute | solution.py:275
  30.0 2.1 %copy-start.1 = (bf16[4,32,1280]{2,1,0:T(8,128)(2,1)S(1)}, bf16[4,32,1280]{2,1,0:T(8,128)(2,1)}, u32[]{:S(2)}) copy-start(bf16[4,32,1280]{2,1,0:T(8,128)(2,1)} %copy-done) | copy-start | bytes 983044
  30.0 2.1 %copy-start.3 = (bf16[2,32,1280]{2,1,0:T(8,128)(2,1)S(1)}, bf16[2,32,1280]{2,1,0:T(8,128)(2,1)}, u32[]{:S(2)}) copy-start(bf16[2,32,1280]{2,1,0:T(8,128)(2,1)} %copy-done.2) | copy-start | bytes 491524
  34.0 6.5 %collective-permute-start.10 = (bf16[2,32,1280]{2,1,0:T(8,128)(2,1)S(1)}, bf16[2,32,1280]{2,1,0:T(8,128)(2,1)S(1)}, u32[]{:S(2)}, u32[]{:S(2)}) collective-permute-start(bf16[2,32,1280]{2,1,0:T(8,128)(2,1)S(1)} %slice.29), channel_id=1, source_target_pairs={{0,1},{1,0},{2,3},{3,2},{4,5},{5,4},{6,7},{7,6},{8,9},{9,8},{10,11... | collective-permute-start | bytes 491528 | tf_op jit(solution)/shard_map/ppermute | solution.py:275
  34.1 15.8 %collective-permute-start.12 = (bf16[4,32,1280]{2,1,0:T(8,128)(2,1)S(1)}, bf16[4,32,1280]{2,1,0:T(8,128)(2,1)S(1)}, u32[]{:S(2)}, u32[]{:S(2)}) collective-permute-start(bf16[4,32,1280]{2,1,0:T(8,128)(2,1)S(1)} %get-tuple-element.27), channel_id=1, source_target_pairs={{0,4},{1,5},{2,6},{3,7},{4,0},{5,1},{6,2},{7,3},{8,12},{9,13},{10,... | collective-permute-start | bytes 983048 | tf_op jit(solution)/shard_map/ppermute | solution.py:275
  36.8 21.1 %collective-permute-start.16 = (bf16[10,96,128]{2,1,0:T(8,128)(2,1)S(1)}, bf16[10,96,128]{2,1,0:T(8,128)(2,1)S(1)}, u32[]{:S(2)}, u32[]{:S(2)}) collective-permute-start(bf16[10,96,128]{2,1,0:T(8,128)(2,1)S(1)} %get-tuple-element.35), channel_id=1, source_target_pairs={{0,8},{1,9},{2,10},{3,11},{4,12},{5,13},{6,14},{7,15},{8,0},{9,1},... | collective-permute-start | bytes 737288 | tf_op jit(solution)/shard_map/ppermute | solution.py:275
  40.3 18.5 %collective-permute-start.18 = (bf16[10,96,128]{2,1,0:T(8,128)(2,1)S(1)}, bf16[10,96,128]{2,1,0:T(8,128)(2,1)S(1)}, u32[]{:S(2)}, u32[]{:S(2)}) collective-permute-start(bf16[10,96,128]{2,1,0:T(8,128)(2,1)S(1)} %get-tuple-element.37), channel_id=1, source_target_pairs={{0,12},{1,13},{2,14},{3,15},{4,8},{5,9},{6,10},{7,11},{8,4},{9,5},... | collective-permute-start | bytes 737288 | tf_op jit(solution)/shard_map/ppermute | solution.py:275
  40.5 9.7 %collective-permute-start.11 = (bf16[2,32,1280]{2,1,0:T(8,128)(2,1)S(1)}, bf16[2,32,1280]{2,1,0:T(8,128)(2,1)S(1)}, u32[]{:S(2)}, u32[]{:S(2)}) collective-permute-start(bf16[2,32,1280]{2,1,0:T(8,128)(2,1)S(1)} %pad_maximum_fusion.5), channel_id=1, source_target_pairs={{0,2},{1,3},{2,0},{3,1},{4,6},{5,7},{6,4},{7,5},{8,10},{9,11},{10,... | collective-permute-start | bytes 491528 | tf_op jit(solution)/shard_map/ppermute | solution.py:275
  42.1 17.9 %collective-permute-start.17 = (bf16[10,96,128]{2,1,0:T(8,128)(2,1)S(1)}, bf16[10,96,128]{2,1,0:T(8,128)(2,1)S(1)}, u32[]{:S(2)}, u32[]{:S(2)}) collective-permute-start(bf16[10,96,128]{2,1,0:T(8,128)(2,1)S(1)} %get-tuple-element.36), channel_id=1, source_target_pairs={{0,4},{1,5},{2,6},{3,7},{4,0},{5,1},{6,2},{7,3},{8,12},{9,13},{10,... | collective-permute-start | bytes 737288 | tf_op jit(solution)/shard_map/ppermute | solution.py:275
  49.9 4.8 %collective-permute-start.13 = (bf16[1,32,1280]{2,1,0:T(8,128)(2,1)S(1)}, bf16[1,32,1280]{2,1,0:T(8,128)(2,1)S(1)}, u32[]{:S(2)}, u32[]{:S(2)}) collective-permute-start(bf16[1,32,1280]{2,1,0:T(8,128)(2,1)S(1)} %get-tuple-element.28), channel_id=1, source_target_pairs={{0,3},{1,2},{2,1},{3,0},{4,7},{5,6},{6,5},{7,4},{8,11},{9,10},{10,... | collective-permute-start | bytes 245768 | tf_op jit(solution)/shard_map/ppermute | solution.py:275
  50.3 6.2 %collective-permute-start.14 = (bf16[1,32,1280]{2,1,0:T(8,128)(2,1)S(1)}, bf16[1,32,1280]{2,1,0:T(8,128)(2,1)S(1)}, u32[]{:S(2)}, u32[]{:S(2)}) collective-permute-start(bf16[1,32,1280]{2,1,0:T(8,128)(2,1)S(1)} %get-tuple-element.29), channel_id=1, source_target_pairs={{0,2},{1,3},{2,0},{3,1},{4,6},{5,7},{6,4},{7,5},{8,10},{9,11},{10,... | collective-permute-start | bytes 245768 | tf_op jit(solution)/shard_map/ppermute | solution.py:275
  54.6 1.8 %collective-permute-start.15 = (bf16[1,32,1280]{2,1,0:T(8,128)(2,1)S(1)}, bf16[1,32,1280]{2,1,0:T(8,128)(2,1)S(1)}, u32[]{:S(2)}, u32[]{:S(2)}) collective-permute-start(bf16[1,32,1280]{2,1,0:T(8,128)(2,1)S(1)} %get-tuple-element.30), channel_id=1, source_target_pairs={{0,1},{1,0},{2,3},{3,2},{4,5},{5,4},{6,7},{7,6},{8,9},{9,8},{10,11... | collective-permute-start | bytes 245768 | tf_op jit(solution)/shard_map/ppermute | solution.py:275
